TPU v7x, 32 devices: a whole 2x2x4 slice. The times are simulated.
32 devices in a mesh: parts: 2 (over y), src: 4 (over z), tgt: 2 (over x), rep: 2 (over core).
Axes of the slice: x: 2, y: 2, z: 4, core: 2. Of those that a mesh axis runs over, the one named last changes fastest.
Arguments:
- acts: bfloat16 [1024, 4096], P(('parts', 'rep'), 'src'), parts along dimension 0, may hold values from -6 to 6
- enc_w: bfloat16 [4096, 1024], P('src', 'tgt'), may hold values from -0.09375 to 0.09375
- enc_b: float32 [1024], P('tgt'), may hold values from -3 to 3
- dec_w: bfloat16 [2, 2, 512, 4096], P(None, None, 'src', 'tgt'), may hold values from -0.375 to 0.375
- dec_b: float32 [2, 4096], P(None, 'tgt'), may hold values from -2 to 2
- targets: bfloat16 [2, 1024, 4096], P(None, ('parts', 'rep', 'src'), 'tgt'), parts along dimension 1, may hold values from -3 to 3
- active: int32 [8, 8], P(('parts', 'rep')), parts along dimension 0, may hold values from -1 to 7, as said below
Outputs:
- error: bfloat16 [2, 1024, 4096], P(None, ('parts', 'rep', 'src'), 'tgt'), parts along dimension 1
There are 2 independent parts, one for each index of `parts`. A program takes and returns all parts, laid end to end along the dimension named above; an argument that names none is the same for every part. Nothing has to cross between parts.
Inputs may be any that keep to these rules, and one draw needn't show every extreme that they name: `active`: each row lists distinct blocks in ascending order, then -1 in the empty slots. In each aligned group of 2 tiles (the tiles of one token half) a block is listed by at most 2 tiles, and some block by exactly 2.
All inputs are finite; a program needn't handle non-finite values.
Results may differ from a plain program's by a relative error of at most 0.015.
Values may be sent and summed in bfloat16 or wider, within the bound.
No kernel may reach another device: no remote copies, remote signals or barrier semaphores. Data moves between devices by JAX's collectives and lax.ppermute only.
A program may use at most 64 MiB of HBM per device.

v0:
```python
import jax
import jax.numpy as jnp
from jax import lax
from jax.sharding import PartitionSpec as P


def body(acts, enc_w, enc_b, dec_w, dec_b, targets, active):
    src_count = lax.axis_size("src")
    src_index = lax.axis_index("src")
    tgt_index = lax.axis_index("tgt")
    tok_rows = acts.shape[0]
    layers = dec_w.shape[0]
    groups = dec_w.shape[1]
    block = dec_w.shape[2]
    out_cols = dec_w.shape[3]
    tile_count = active.shape[0]
    tile_rows = tok_rows // tile_count
    total_blocks = src_count * groups
    listed = jnp.any(
        active[:, :, None] == jnp.arange(total_blocks, dtype=jnp.int32)[None, None, :], axis=1
    )
    group_flags = lax.dynamic_slice_in_dim(listed, tgt_index * src_count, src_count, 1)
    own_bias = lax.dynamic_slice_in_dim(enc_b.reshape(src_count, block), src_index, 1, 0)[0]
    pre_cols = lax.psum_scatter(
        jnp.einsum("dk,td->kt", enc_w, acts, preferred_element_type=jnp.float32).astype(
            jnp.bfloat16
        ),
        "src",
        scatter_dimension=0,
        tiled=True,
    ).astype(jnp.float32)
    own_flags = lax.dynamic_slice_in_dim(group_flags, src_index, 1, 1)[:, 0]
    live_rows = jnp.repeat(own_flags.astype(jnp.float32), tile_rows)
    codes = (live_rows[:, None] * jnp.maximum(pre_cols.T + own_bias[None, :], 0.0)).astype(
        jnp.bfloat16
    )
    dec_flat = dec_w.reshape(layers, groups * block, out_cols)
    decoded = jnp.einsum(
        "tk,lkd->ltd",
        lax.all_gather(codes, "tgt", axis=1, tiled=True),
        dec_flat,
        preferred_element_type=jnp.float32,
    )
    summed = lax.psum_scatter(
        decoded.astype(jnp.bfloat16), "src", scatter_dimension=1, tiled=True
    ).astype(jnp.float32)
    return (summed + dec_b[:, None, :] - targets.astype(jnp.float32)).astype(jnp.bfloat16)


def solution(mesh):
    in_specs = (
        P(("parts", "rep"), "src"),
        P("src", "tgt"),
        P("tgt"),
        P(None, None, "src", "tgt"),
        P(None, "tgt"),
        P(None, ("parts", "rep", "src"), "tgt"),
        P(("parts", "rep"), None),
    )
    out_specs = P(None, ("parts", "rep", "src"), "tgt")
    return jax.shard_map(body, mesh=mesh, in_specs=in_specs, out_specs=out_specs, check_vma=False)
```

profile of v0, /device:TPU:0, one launch (start us, length us, event | category | flops | bytes accessed | tf_op | source)
XLA Modules:
  0.0 91.3 jit_solution(1792842516460851966)
XLA Ops:
  6.5 0.0 copy-start
  6.5 0.0 copy-start.3
  6.5 0.0 reduce-scatter.7.cloned.1.call-start
  6.5 2.7 %convolution_convert_fusion.1 = bf16[512,256]{1,0:T(8,128)(2,1)} fusion(bf16[1024,512]{1,0:T(8,128)(2,1)} %param.8, bf16[256,1024]{1,0:T(8,128)(2,1)} %param.7), kind=kOutput, calls=%fused_computation.2 | convolution fusion | flops 268566528 | bytes 1835008 | tf_op jit(solution)/shard_map/dk,td->kt/dot_general | solution.py:25
  9.3 0.0 reduce-scatter.7.cloned.1.call-update
  9.3 0.0 reduce-scatter.5.cloned.1.call-start
  9.3 0.0 copy-done.3
  9.3 0.1 fusion.3
  9.4 0.2 fusion.4
  9.6 0.7 dynamic-slice_bitcast_fusion
  10.3 0.1 broadcast_bitcast_fusion
  10.4 21.7 %reduce-scatter.7.cloned.1.call-done = bf16[128,256]{1,0:T(8,128)(2,1)} async-done(((bf16[512,256]{1,0:T(8,128)(2,1)}), bf16[128,256]{1,0:T(8,128)(2,1)}) %reduce-scatter.7.cloned.1.call-update) | async-done | bytes 65552
  32.0 0.9 %copy.11 = bf16[128,256]{0,1:T(8,128)(2,1)S(1)} copy(bf16[128,256]{1,0:T(8,128)(2,1)} %reduce-scatter.7.cloned.1.call-done) | data formatting | bytes 131072
  33.0 0.1 fusion.2
  33.1 5.0 %all_gather.3 = bf16[256,256]{1,0:T(8,128)(2,1)S(1)} all-gather(bf16[256,128]{1,0:T(8,128)(2,1)S(1)} %fusion.2), channel_id=1, replica_groups=mesh['parts'=2,'src'=4,'tgt'=2,'rep'=2] {'tgt'}, dimensions={1}, use_global_device_ids=true | all-gather | bytes 196608 | tf_op jit(solution)/shard_map/all_gather | solution.py:40
  38.1 0.0 copy-done
  38.1 2.1 %fusion = bf16[2,256,2048]{2,1,0:T(8,128)(2,1)} fusion(bf16[2,256,2048]{2,1,0:T(8,128)(2,1)S(1)} %bitcast.17, bf16[256,256]{1,0:T(8,128)(2,1)S(1)} %all_gather.3), kind=kOutput, calls=%fused_computation.1 | convolution fusion | flops 537919488 | bytes 4325376 | tf_op jit(solution)/shard_map/tk,lkd->ltd/dot_general | solution.py:38
  40.1 0.0 copy-start.1
  40.1 0.0 copy-start.2
  40.1 0.0 reduce-scatter.5.cloned.1.call-update
  40.2 42.2 %reduce-scatter.5.cloned.1.call-done = bf16[2,64,2048]{2,1,0:T(8,128)(2,1)} async-done(((bf16[2,256,2048]{2,1,0:T(8,128)(2,1)}), bf16[2,64,2048]{2,1,0:T(8,128)(2,1)}) %reduce-scatter.5.cloned.1.call-update) | async-done | bytes 524304 | tf_op jit(solution)/shard_map/reduce_scatter | solution.py:44
  82.4 0.0 copy-done.1
  82.4 0.0 copy-done.2
  82.4 2.0 %subtract_convert_fusion = bf16[2,64,2048]{2,1,0:T(8,128)(2,1)} fusion(bf16[2,64,2048]{2,1,0:T(8,128)(2,1)S(1)} %copy-done.1, bf16[2,64,2048]{2,1,0:T(8,128)(2,1)} %reduce-scatter.5.cloned.1.call-done, f32[2,2048]{1,0:T(2,128)S(1)} %copy-done.2), kind=kLoop, calls=%fused_computation.3 | loop fusion | flops 1310720 | bytes 1589248 | tf_op jit(solution)/shard_map/convert_element_type | solution.py:47
Async XLA Ops:
  6.5 31.5 %copy-start = (bf16[2,2,128,2048]{3,2,1,0:T(8,128)(2,1)S(1)}, bf16[2,2,128,2048]{3,2,1,0:T(8,128)(2,1)}, u32[]{:S(2)}) copy-start(bf16[2,2,128,2048]{3,2,1,0:T(8,128)(2,1)} %param.10) | copy-start | bytes 6291460
  6.5 2.8 %copy-start.3 = (s32[2,8]{1,0:T(2,128)S(1)}, s32[2,8]{1,0:T(2,128)}, u32[]{:S(2)}) copy-start(s32[2,8]{1,0:T(2,128)} %param.13) | copy-start | bytes 196
  6.5 25.5 %reduce-scatter.7.cloned.1.call-start = ((), (), s32[]{:S(2)}) async-start(), calls=%async_computation.3 | async-start | bytes 327680
  9.3 73.1 %reduce-scatter.5.cloned.1.call-start = ((), (), s32[]{:S(2)}) async-start(), calls=%async_computation.2 | async-start | bytes 2621440 | tf_op jit(solution)/shard_map/reduce_scatter | solution.py:44
  40.1 42.3 %copy-start.1 = (bf16[2,64,2048]{2,1,0:T(8,128)(2,1)S(1)}, bf16[2,64,2048]{2,1,0:T(8,128)(2,1)}, u32[]{:S(2)}) copy-start(bf16[2,64,2048]{2,1,0:T(8,128)(2,1)} %param.12) | copy-start | bytes 1572868
  40.1 42.3 %copy-start.2 = (f32[2,2048]{1,0:T(2,128)S(1)}, f32[2,2048]{1,0:T(2,128)}, u32[]{:S(2)}) copy-start(f32[2,2048]{1,0:T(2,128)} %param.11) | copy-start | bytes 49156
Sparse Core Ops, SparseCore 0:
  9.6 22.3 reduce-scatter.6
  40.3 42.0 reduce-scatter.4
where the time goes:
time: 91.5 us; the launch traced here: 91.3 us
  waiting for transfers between devices  63.9 us (70%)
  between operations  13.4 us (15%)
  blocking collectives  4.96 us (5%)
  matrix products  4.78 us (5%)
  other arithmetic  2.38 us (3%)
  local copies, waits for them, and re-layouts  1.72 us (2%)
    reduce_scatter x1, waiting for transfers between devices, body(): lax.psum_scatter(decoded.astype(jnp.bfloat16), 'src', scatter_dimension=1...  42.2 us
    unnamed x3, waiting for transfers between devices  21.7 us
    all_gather x1, blocking collectives, body(): lax.all_gather(codes, 'tgt', axis=1, tiled=True)  4.96 us
    dot_general x1, matrix products, body(): jnp.einsum('dk,td->kt', enc_w, acts, preferred_element_type=jnp.float32)  2.71 us
    dot_general x1, matrix products, body(): jnp.einsum('tk,lkd->ltd', lax.all_gather(codes, 'tgt', axis=1, tiled=True...  2.07 us
    convert_element_type x1, other arithmetic, body(): (summed + dec_b[:, None, :] - targets.astype(jnp.float32)).astype(jnp.bfl...  2 us
  transfers between devices with their start and end apart: 2, of which 2 were waited for; matrix products, arithmetic and copies ran while one was open for 1% of the time, Pallas kernels for 0%

commit v1 on v0

v1 whole, which is shorter than its diff:
```python
import functools

import jax
import jax.numpy as jnp
from jax import lax
from jax.experimental import pallas as pl
from jax.experimental.pallas import tpu as pltpu
from jax.sharding import PartitionSpec as P

VMEM_BYTES = 32 * 1024 * 1024


def encode_kernel(n, acts_ref, w_ref, *out_refs):
    src = lax.axis_index("src")
    width = w_ref.shape[1] // (n // 2)
    for k in range(n):
        dest = lax.rem(src + k, n)
        rows = acts_ref[:, lax.rem(dest, 2)]
        rows = rows.reshape(rows.shape[0] * rows.shape[1], rows.shape[2])
        columns = pl.ds(pl.multiple_of((dest // 2) * width, width), width)
        out_refs[k][...] = jnp.dot(
            rows, w_ref[:, columns], preferred_element_type=jnp.float32
        ).astype(jnp.bfloat16)


def codes_kernel(n, share, tile_rows, active_ref, bias_ref, *refs):
    term_refs, out_ref = refs[:-1], refs[-1]
    src = lax.axis_index("src")
    tgt = lax.axis_index("tgt")
    parity, half = lax.rem(src, 2), src // 2
    block = out_ref.shape[2] // 2
    pre = term_refs[0][...].astype(jnp.float32)
    for ref in term_refs[1:]:
        pre = pre + ref[...].astype(jnp.float32)
    tiles, slots = active_ref.shape
    for piece in range(2):
        columns = slice(piece * block, (piece + 1) * block)
        bias = bias_ref[pl.ds(half * 2 + piece, 1), :]
        wanted = tgt * n + half * 2 + piece
        flags = []
        for tile in range(tiles):
            flags.append(
                lax.fori_loop(
                    0,
                    slots,
                    lambda i, total: total + (active_ref[tile, i] == wanted).astype(jnp.int32),
                    jnp.int32(0),
                    unroll=slots <= 16,
                )
            )
        for group in range(n // 2):
            tile = ((group * 2 + parity) * share) // tile_rows
            flag = flags[0]
            for i in range(1, tiles):
                flag = jnp.where(tile == i, flags[i], flag)
            live = jnp.where(flag > 0, 1.0, 0.0).astype(jnp.float32)
            rows = slice(group * share, (group + 1) * share)
            value = live * jnp.maximum(pre[rows, columns] + bias, 0.0)
            out_ref[group, :, columns] = value.astype(jnp.bfloat16)


def gather_rows(n, groups, lhs_ref, code_refs, group):
    src = lax.axis_index("src")
    tgt = lax.axis_index("tgt")
    rep = lax.axis_index("rep")
    parity = lax.rem(src, 2)
    block = code_refs[0].shape[2] // 2
    for place in range(2 * groups):
        if place < groups:
            wanted, piece = place, parity
        else:
            side = (place - groups) // (groups // 2)
            owner = rep if side == 0 else 1 - rep
            wanted = owner * (groups // 2) + (place - groups) % (groups // 2)
            piece = 1 - parity
        offset = lax.rem(tgt - wanted + groups, groups)
        columns = pl.ds(pl.multiple_of(piece * block, block), block)
        for k in range(groups):

            @pl.when(offset == k)
            def _():
                lhs_ref[:, place * block : (place + 1) * block] = code_refs[k][group, :, columns]


def product(groups, lhs_ref, own_ref, got_ref, swapped_ref):
    block = own_ref.shape[-2]
    own = own_ref[...].reshape(groups * block, own_ref.shape[-1])
    got = got_ref[...].reshape(groups // 2 * block, own_ref.shape[-1])
    swapped = swapped_ref[...].reshape(groups // 2 * block, own_ref.shape[-1])
    edge, last = groups * block, groups * block * 3 // 2
    total = jnp.dot(lhs_ref[:, :edge], own, preferred_element_type=jnp.float32)
    total += jnp.dot(lhs_ref[:, edge:last], got, preferred_element_type=jnp.float32)
    total += jnp.dot(lhs_ref[:, last:], swapped, preferred_element_type=jnp.float32)
    return total


def send_kernel(n, groups, step, own_ref, got_ref, swapped_ref, *refs):
    code_refs, out_ref, lhs_ref = refs[:-2], refs[-2], refs[-1]

    @pl.when(pl.program_id(0) == 0)
    def _():
        group = lax.rem(lax.axis_index("src") // 2 + step, n // 2)
        gather_rows(n, groups, lhs_ref, code_refs, group)

    out_ref[...] = product(groups, lhs_ref, own_ref, got_ref, swapped_ref).astype(jnp.bfloat16)


def keep_kernel(n, groups, own_ref, got_ref, swapped_ref, bias_ref, target_ref, *refs):
    code_refs, out_ref, lhs_ref = refs[:-2], refs[-2], refs[-1]

    @pl.when(pl.program_id(0) == 0)
    def _():
        gather_rows(n, groups, lhs_ref, code_refs, lax.axis_index("src") // 2)

    total = product(groups, lhs_ref, own_ref, got_ref, swapped_ref)
    out_ref[...] = total + bias_ref[...] - target_ref[0].astype(jnp.float32)


def add_kernel(layers, *refs):
    out_ref = refs[-1]
    per_layer = (len(refs) - 1) // layers
    for layer in range(layers):
        mine = refs[layer * per_layer : (layer + 1) * per_layer]
        total = mine[0][...]
        for ref in mine[1:]:
            total = total + ref[...].astype(jnp.float32)
        out_ref[layer] = total.astype(jnp.bfloat16)


def body(acts, enc_w, enc_b, dec_w, dec_b, targets, active):
    n = lax.axis_size("src")
    rep = lax.axis_index("rep")
    rows, features = acts.shape
    layers, groups, block, cols = dec_w.shape
    share = rows // n
    half = n // 2
    tile_rows = rows // active.shape[0]
    pair = [(i, i ^ 1) for i in range(n)]
    params = pltpu.CompilerParams(vmem_limit_bytes=VMEM_BYTES)
    vmem = pl.BlockSpec(memory_space=pltpu.VMEM)
    smem = pl.BlockSpec(memory_space=pltpu.SMEM)

    got, swapped = [], []
    for layer in range(layers):
        part = lax.dynamic_slice_in_dim(dec_w[layer], rep * (groups // 2), groups // 2, 0)
        got.append(lax.ppermute(part, "src", pair))
        swapped.append(lax.ppermute(got[-1], "rep", [(0, 1), (1, 0)]))

    term_shape = jax.ShapeDtypeStruct((half * share, 2 * block), jnp.bfloat16)
    terms = pl.pallas_call(
        functools.partial(encode_kernel, n),
        out_shape=[term_shape] * n,
        in_specs=[vmem, vmem],
        out_specs=[vmem] * n,
        compiler_params=params,
        cost_estimate=pl.CostEstimate(
            flops=2 * rows * features * groups * block * 0 + 2 * rows * features * enc_w.shape[1],
            bytes_accessed=(acts.size + enc_w.size) * 2,
            transcendentals=0,
        ),
        name="encode",
    )(acts.reshape(half, 2, share, features), enc_w)
    arrived = [terms[0]]
    for k in range(1, n):
        arrived.append(lax.ppermute(terms[k], "src", [(i, (i + k) % n) for i in range(n)]))

    codes = [
        pl.pallas_call(
            functools.partial(codes_kernel, n, share, tile_rows),
            out_shape=jax.ShapeDtypeStruct((half, share, 2 * block), jnp.bfloat16),
            in_specs=[smem, vmem] + [vmem] * n,
            out_specs=vmem,
            compiler_params=params,
            name="codes",
        )(active, enc_b.reshape(n, block), *arrived)
    ]
    for k in range(1, groups):
        codes.append(
            lax.ppermute(codes[0], "tgt", [(i, (i + k) % groups) for i in range(groups)])
        )

    width = min(cols, 512)
    lhs = pltpu.VMEM((share, 2 * groups * block), jnp.bfloat16)
    cost = pl.CostEstimate(
        flops=2 * share * 2 * groups * block * cols,
        bytes_accessed=2 * groups * block * cols * 2,
        transcendentals=0,
    )

    def weight_specs(layer):
        return [
            pl.BlockSpec((1, groups, block, width), lambda j: (layer, 0, 0, j)),
            pl.BlockSpec((groups // 2, block, width), lambda j: (0, 0, j)),
            pl.BlockSpec((groups // 2, block, width), lambda j: (0, 0, j)),
        ]

    block_spec = pl.BlockSpec((share, width), lambda j: (0, j))
    sums = []
    for layer in range(layers):
        received = []
        for step in range(1, half):
            term = pl.pallas_call(
                functools.partial(send_kernel, n, groups, step),
                grid=(cols // width,),
                out_shape=jax.ShapeDtypeStruct((share, cols), jnp.bfloat16),
                in_specs=weight_specs(layer) + [vmem] * groups,
                out_specs=block_spec,
                scratch_shapes=[lhs],
                compiler_params=params,
                cost_estimate=cost,
                name="decode_send",
            )(dec_w, got[layer], swapped[layer], *codes)
            perm = [(i, (i + 2 * step) % n) for i in range(n)]
            received.append(lax.ppermute(term, "src", perm))
        sums.append(received)

    operands = []
    for layer in range(layers):
        kept = pl.pallas_call(
            functools.partial(keep_kernel, n, groups),
            grid=(cols // width,),
            out_shape=jax.ShapeDtypeStruct((share, cols), jnp.float32),
            in_specs=weight_specs(layer)
            + [
                pl.BlockSpec((1, width), lambda j: (0, j)),
                pl.BlockSpec((1, share, width), lambda j, layer=layer: (layer, 0, j)),
            ]
            + [vmem] * groups,
            out_specs=block_spec,
            scratch_shapes=[lhs],
            compiler_params=params,
            cost_estimate=cost,
            name="decode_keep",
        )(dec_w, got[layer], swapped[layer], dec_b[layer : layer + 1], targets, *codes)
        operands += [kept] + sums[layer]

    return pl.pallas_call(
        functools.partial(add_kernel, layers),
        out_shape=jax.ShapeDtypeStruct((layers, share, cols), jnp.bfloat16),
        in_specs=[vmem] * len(operands),
        out_specs=vmem,
        compiler_params=params,
        name="add",
    )(*operands)


def solution(mesh):
    in_specs = (
        P(("parts", "rep"), "src"),
        P("src", "tgt"),
        P("tgt"),
        P(None, None, "src", "tgt"),
        P(None, "tgt"),
        P(None, ("parts", "rep", "src"), "tgt"),
        P(("parts", "rep"), None),
    )
    out_specs = P(None, ("parts", "rep", "src"), "tgt")
    return jax.shard_map(body, mesh=mesh, in_specs=in_specs, out_specs=out_specs, check_vma=False)
```

time: 91.5 us -> 73.9 us (0.81)
  waiting for transfers between devices: 63.9 us -> 46.4 us
  starting transfers between devices: 0.04 us -> 13.5 us
  between operations: 13.4 us -> 0.1 us
  Pallas kernels: 0 us -> 7.13 us
  blocking collectives: 4.96 us -> 0 us
  local copies, waits for them, and re-layouts: 1.72 us -> 6.6 us
  matrix products: 4.78 us -> 0 us
  other arithmetic: 2.38 us -> 0 us
    ppermute x0 -> x10, waiting for transfers between devices: none -> 46.4 us  [the longest x2 22 us: body(): got.append(lax.ppermute(part, 'src', pair))]
    reduce_scatter x1 -> x0, waiting for transfers between devices: 42.2 us -> none  [body(): lax.psum_scatter(decoded.astype(jnp.bfloat16), 'src', scatter_dimension=1...]
    unnamed x3 -> x0, waiting for transfers between devices: 21.7 us -> none
    ppermute x0 -> x10, starting transfers between devices: none -> 13.5 us  [the longest x3 5.72 us: body(): lax.ppermute(terms[k], 'src', [(i, (i + k) % n) for i in range(n)])]
    pallas_call x0 -> x7, Pallas kernels: none -> 7.13 us  [the longest x2 2.64 us: body(): pl.pallas_call(functools.partial(keep_kernel, n, groups), grid=(cols // w...]
    all_gather x1 -> x0, blocking collectives: 4.96 us -> none  [body(): lax.all_gather(codes, 'tgt', axis=1, tiled=True)]
    dot_general x2 -> x0, matrix products: 4.78 us -> none  [the longest x1 2.71 us: body(): jnp.einsum('dk,td->kt', enc_w, acts, preferred_element_type=jnp.float32)]
    slice x0 -> x2, local copies, waits for them, and re-layouts: none -> 3.23 us  [the longest x1 3.22 us: body(): dec_w[layer]]
  transfers between devices with their start and end apart: 2 -> 10, of which waited for: 2 -> 8; matrix products, arithmetic and copies ran while one was open for 1% -> 1% of each run, Pallas kernels for 0% -> 8%
where the time goes in v1:
time: 73.9 us; the launch traced here: 73.7 us
  waiting for transfers between devices  46.4 us (63%)
  starting transfers between devices  13.5 us (18%)
  Pallas kernels  7.13 us (10%)
  local copies, waits for them, and re-layouts  6.6 us (9%)
    ppermute x2, waiting for transfers between devices, body(): got.append(lax.ppermute(part, 'src', pair))  22 us
    ppermute x2, waiting for transfers between devices, body(): received.append(lax.ppermute(term, 'src', perm))  17.6 us
    ppermute x3, starting transfers between devices, body(): lax.ppermute(terms[k], 'src', [(i, (i + k) % n) for i in range(n)])  5.72 us
    ppermute x3, waiting for transfers between devices, body(): lax.ppermute(terms[k], 'src', [(i, (i + k) % n) for i in range(n)])  4.02 us
    slice x1, local copies, waits for them, and re-layouts, body(): dec_w[layer]  3.22 us
    ppermute x2, starting transfers between devices, body(): got.append(lax.ppermute(part, 'src', pair))  3.17 us
    ppermute x2, starting transfers between devices, body(): received.append(lax.ppermute(term, 'src', perm))  3.05 us
    ppermute x1, waiting for transfers between devices, body(): lax.ppermute(codes[0], 'tgt', [(i, (i + k) % groups) for i in range(group...  2.77 us
  transfers between devices with their start and end apart: 10, of which 8 were waited for; matrix products, arithmetic and copies ran while one was open for 1% of the time, Pallas kernels for 8%

profile of v1, /device:TPU:0, one launch (start us, length us, event | category | flops | bytes accessed | tf_op | source)
XLA Modules:
  0.0 73.7 jit_solution(5922485266436759454)
XLA Ops:
  0.0 0.0 copy-start.2
  0.0 3.2 %fusion = (bf16[1,2,128,2048]{3,2,1,0:T(8,128)(2,1)}, bf16[1,2,128,2048]{3,2,1,0:T(8,128)(2,1)}) fusion(bf16[2,2,128,2048]{3,2,1,0:T(8,128)(2,1)} %own_ref.7), kind=kLoop, calls=%fused_computation.2 | loop fusion | bytes 4194304 | tf_op jit(solution)/shard_map/slice | solution.py:145
  3.2 0.0 copy-start.4
  3.2 0.0 copy-start.5
  3.2 0.0 copy-start
  3.2 1.2 %dynamic-slice_bitcast_fusion.1 = bf16[1,128,2048]{2,1,0:T(8,128)(2,1)S(1)} fusion(bf16[1,2,128,2048]{3,2,1,0:T(8,128)(2,1)} %get-tuple-element.14, s32[]{:T(128)S(6)} %select_n.4), kind=kLoop, calls=%fused_computation.1 | loop fusion | bytes 1048580 | tf_op jit(solution)/shard_map/dynamic_slice | solution.py:145
  4.5 3.1 %collective-permute-start = (bf16[1,128,2048]{2,1,0:T(8,128)(2,1)S(1)}, bf16[1,128,2048]{2,1,0:T(8,128)(2,1)S(1)}, u32[]{:S(2)}, u32[]{:S(2)}) collective-permute-start(bf16[1,128,2048]{2,1,0:T(8,128)(2,1)S(1)} %dynamic-slice_bitcast_fusion.1), channel_id=1, source_target_pairs={{0,4},{4,0},{8,12},{12,8},{1,5},{5,1},{9,13},{13,9},{2,6},{6,2},{1... | collective-permute-start | bytes 1572872 | tf_op jit(solution)/shard_map/ppermute | solution.py:146
  7.6 1.1 %dynamic-slice_bitcast_fusion = bf16[1,128,2048]{2,1,0:T(8,128)(2,1)S(1)} fusion(bf16[1,2,128,2048]{3,2,1,0:T(8,128)(2,1)} %get-tuple-element.13, s32[]{:T(128)S(6)} %select_n.4), kind=kLoop, calls=%fused_computation | loop fusion | bytes 1048580 | tf_op jit(solution)/shard_map/dynamic_slice | solution.py:145
  8.6 0.1 collective-permute-start.7
  8.7 11.6 %collective-permute-done.got_ref = bf16[1,128,2048]{2,1,0:T(8,128)(2,1)S(1)} collective-permute-done((bf16[1,128,2048]{2,1,0:T(8,128)(2,1)S(1)}, bf16[1,128,2048]{2,1,0:T(8,128)(2,1)S(1)}, u32[]{:S(2)}, u32[]{:S(2)}) %collective-permute-start) | collective-permute-done | bytes 524320 | tf_op jit(solution)/shard_map/ppermute | solution.py:146
  20.3 0.0 collective-permute-start.1
  20.3 10.4 %collective-permute-done.7.got_ref = bf16[1,128,2048]{2,1,0:T(8,128)(2,1)S(1)} collective-permute-done((bf16[1,128,2048]{2,1,0:T(8,128)(2,1)S(1)}, bf16[1,128,2048]{2,1,0:T(8,128)(2,1)S(1)}, u32[]{:S(2)}, u32[]{:S(2)}) %collective-permute-start.7) | collective-permute-done | bytes 524320 | tf_op jit(solution)/shard_map/ppermute | solution.py:146
  30.7 0.0 collective-permute-start.8
  30.7 0.0 copy-done.2
  30.7 0.0 copy-start.3
  30.7 1.0 %copy-done.3 = bf16[256,1024]{1,0:T(8,128)(2,1)S(1)} copy-done((bf16[256,1024]{1,0:T(8,128)(2,1)S(1)}, bf16[256,1024]{1,0:T(8,128)(2,1)}, u32[]{:S(2)}) %copy-start.3) | copy-done | bytes 524312
  31.8 0.5 encode.1
  32.2 1.8 %collective-permute-start.2 = (bf16[128,256]{1,0:T(8,128)(2,1)S(1)}, bf16[128,256]{1,0:T(8,128)(2,1)S(1)}, u32[]{:S(2)}, u32[]{:S(2)}) collective-permute-start(bf16[128,256]{1,0:T(8,128)(2,1)S(1)} %get-tuple-element.10), channel_id=1, source_target_pairs={{0,4},{4,8},{8,12},{12,0},{1,5},{5,9},{9,13},{13,1},{2,6},{6,10},{... | collective-permute-start | bytes 196616 | tf_op jit(solution)/shard_map/ppermute | solution.py:165
  34.0 2.6 %collective-permute-start.3 = (bf16[128,256]{1,0:T(8,128)(2,1)S(1)}, bf16[128,256]{1,0:T(8,128)(2,1)S(1)}, u32[]{:S(2)}, u32[]{:S(2)}) collective-permute-start(bf16[128,256]{1,0:T(8,128)(2,1)S(1)} %get-tuple-element.11), channel_id=1, source_target_pairs={{0,8},{4,12},{8,0},{12,4},{1,9},{5,13},{9,1},{13,5},{2,10},{6,14},... | collective-permute-start | bytes 196616 | tf_op jit(solution)/shard_map/ppermute | solution.py:165
  36.6 1.3 %collective-permute-start.4 = (bf16[128,256]{1,0:T(8,128)(2,1)S(1)}, bf16[128,256]{1,0:T(8,128)(2,1)S(1)}, u32[]{:S(2)}, u32[]{:S(2)}) collective-permute-start(bf16[128,256]{1,0:T(8,128)(2,1)S(1)} %get-tuple-element.12), channel_id=1, source_target_pairs={{0,12},{4,0},{8,4},{12,8},{1,13},{5,1},{9,5},{13,9},{2,14},{6,2},{... | collective-permute-start | bytes 196616 | tf_op jit(solution)/shard_map/ppermute | solution.py:165
  38.0 1.0 %collective-permute-done.2.refs_1_ = bf16[128,256]{1,0:T(8,128)(2,1)S(1)} collective-permute-done((bf16[128,256]{1,0:T(8,128)(2,1)S(1)}, bf16[128,256]{1,0:T(8,128)(2,1)S(1)}, u32[]{:S(2)}, u32[]{:S(2)}) %collective-permute-start.2) | collective-permute-done | bytes 65568 | tf_op jit(solution)/shard_map/ppermute | solution.py:165
  38.9 2.8 %collective-permute-done.3.refs_2_ = bf16[128,256]{1,0:T(8,128)(2,1)S(1)} collective-permute-done((bf16[128,256]{1,0:T(8,128)(2,1)S(1)}, bf16[128,256]{1,0:T(8,128)(2,1)S(1)}, u32[]{:S(2)}, u32[]{:S(2)}) %collective-permute-start.3) | collective-permute-done | bytes 65568 | tf_op jit(solution)/shard_map/ppermute | solution.py:165
  41.7 0.2 collective-permute-done.4.refs_3_
  42.0 0.0 copy-done.4
  42.0 0.0 copy-done.5
  42.0 0.6 codes.1.refs_0_
  42.6 1.6 %collective-permute-start.5 = (bf16[2,64,256]{2,1,0:T(8,128)(2,1)S(1)}, bf16[2,64,256]{2,1,0:T(8,128)(2,1)S(1)}, u32[]{:S(2)}, u32[]{:S(2)}) collective-permute-start(bf16[2,64,256]{2,1,0:T(8,128)(2,1)S(1)} %codes.1.refs_0_), channel_id=1, source_target_pairs={{0,2},{2,0},{1,3},{3,1},{4,6},{6,4},{5,7},{7,5},{8,10},{10,8},{9,1... | collective-permute-start | bytes 196616 | tf_op jit(solution)/shard_map/ppermute | solution.py:179
  44.2 2.8 %collective-permute-done.5.refs_1_ = bf16[2,64,256]{2,1,0:T(8,128)(2,1)S(1)} collective-permute-done((bf16[2,64,256]{2,1,0:T(8,128)(2,1)S(1)}, bf16[2,64,256]{2,1,0:T(8,128)(2,1)S(1)}, u32[]{:S(2)}, u32[]{:S(2)}) %collective-permute-start.5) | collective-permute-done | bytes 65568 | tf_op jit(solution)/shard_map/ppermute | solution.py:179
  46.9 0.0 collective-permute-done.1.swapped_ref
  46.9 0.0 copy-done
  46.9 1.2 %decode_send.2 = bf16[64,2048]{1,0:T(8,128)(2,1)S(1)} custom-call(bf16[2,2,128,2048]{3,2,1,0:T(8,128)(2,1)S(1)} %copy-done, bf16[1,128,2048]{2,1,0:T(8,128)(2,1)S(1)} %collective-permute-done.got_ref, bf16[1,128,2048]{2,1,0:T(8,128)(2,1)S(1)} %collective-permute-done.1.swapped_ref, bf16[2,64,256]{2,1,0:T(8,128)(2,1)S(1)} %codes.1.refs_0_, ...), custom_call_target="tpu_custom_call" | custom-call | flops 134217728 | bytes 2097152 | tf_op jit(solution)/shard_map/decode_send/pallas_call | solution.py:202
  48.2 0.0 copy-start.6
  48.2 0.0 copy-start.1
  48.2 0.7 collective-permute-start.6
  48.9 0.0 collective-permute-done.8.swapped_ref
  48.9 1.2 %decode_send.3 = bf16[64,2048]{1,0:T(8,128)(2,1)S(1)} custom-call(bf16[2,2,128,2048]{3,2,1,0:T(8,128)(2,1)S(1)} %copy-done, bf16[1,128,2048]{2,1,0:T(8,128)(2,1)S(1)} %collective-permute-done.7.got_ref, bf16[1,128,2048]{2,1,0:T(8,128)(2,1)S(1)} %collective-permute-done.8.swapped_ref, bf16[2,64,256]{2,1,0:T(8,128)(2,1)S(1)} %codes.1.refs_0_, ...), custom_call_target="tpu_custom_call" | custom-call | flops 134217728 | bytes 2097152 | tf_op jit(solution)/shard_map/decode_send/pallas_call | solution.py:202
  50.1 2.4 %collective-permute-start.9 = (bf16[64,2048]{1,0:T(8,128)(2,1)S(1)}, bf16[64,2048]{1,0:T(8,128)(2,1)S(1)}, u32[]{:S(2)}, u32[]{:S(2)}) collective-permute-start(bf16[64,2048]{1,0:T(8,128)(2,1)S(1)} %decode_send.3), channel_id=1, source_target_pairs={{0,8},{4,12},{8,0},{12,4},{1,9},{5,13},{9,1},{13,5},{2,10},{6,14},... | collective-permute-start | bytes 786440 | tf_op jit(solution)/shard_map/ppermute | solution.py:214
  52.5 0.0 copy-done.6
  52.5 0.0 copy-done.1
  52.6 1.3 %decode_keep.2.refs_0_ = f32[64,2048]{1,0:T(8,128)S(1)} custom-call(bf16[2,2,128,2048]{3,2,1,0:T(8,128)(2,1)S(1)} %copy-done, bf16[1,128,2048]{2,1,0:T(8,128)(2,1)S(1)} %collective-permute-done.got_ref, bf16[1,128,2048]{2,1,0:T(8,128)(2,1)S(1)} %collective-permute-done.1.swapped_ref, f32[1,2048]{1,0:T(1,128)S(1)} %get-tuple-element.16.bias_ref, ...), custom_call_target="tpu_custom_call" | custom-call | flops 134217728 | bytes 2097152 | tf_op jit(solution)/shard_map/decode_keep/pallas_call | solution.py:219
  53.9 1.3 %decode_keep.3.refs_2_ = f32[64,2048]{1,0:T(8,128)S(1)} custom-call(bf16[2,2,128,2048]{3,2,1,0:T(8,128)(2,1)S(1)} %copy-done, bf16[1,128,2048]{2,1,0:T(8,128)(2,1)S(1)} %collective-permute-done.7.got_ref, bf16[1,128,2048]{2,1,0:T(8,128)(2,1)S(1)} %collective-permute-done.8.swapped_ref, f32[1,2048]{1,0:T(1,128)S(1)} %get-tuple-element.15.bias_ref, ...), custom_call_target="tpu_custom_call" | custom-call | flops 134217728 | bytes 2097152 | tf_op jit(solution)/shard_map/decode_keep/pallas_call | solution.py:219
  55.2 13.5 %collective-permute-done.6.refs_1_ = bf16[64,2048]{1,0:T(8,128)(2,1)S(1)} collective-permute-done((bf16[64,2048]{1,0:T(8,128)(2,1)S(1)}, bf16[64,2048]{1,0:T(8,128)(2,1)S(1)}, u32[]{:S(2)}, u32[]{:S(2)}) %collective-permute-start.6) | collective-permute-done | bytes 262176 | tf_op jit(solution)/shard_map/ppermute | solution.py:214
  68.7 4.1 %collective-permute-done.9.refs_3_ = bf16[64,2048]{1,0:T(8,128)(2,1)S(1)} collective-permute-done((bf16[64,2048]{1,0:T(8,128)(2,1)S(1)}, bf16[64,2048]{1,0:T(8,128)(2,1)S(1)}, u32[]{:S(2)}, u32[]{:S(2)}) %collective-permute-start.9) | collective-permute-done | bytes 262176 | tf_op jit(solution)/shard_map/ppermute | solution.py:214
  72.8 0.9 %add.6 = bf16[2,64,2048]{2,1,0:T(8,128)(2,1)} custom-call(f32[64,2048]{1,0:T(8,128)S(1)} %decode_keep.2.refs_0_, bf16[64,2048]{1,0:T(8,128)(2,1)S(1)} %collective-permute-done.6.refs_1_, f32[64,2048]{1,0:T(8,128)S(1)} %decode_keep.3.refs_2_, bf16[64,2048]{1,0:T(8,128)(2,1)S(1)} %collective-permute-done.9.refs_3_), custom_call_target="tpu_custom_call" | custom-call | tf_op jit(solution)/shard_map/add/pallas_call | solution.py:237
  (1 shorter events, 0.0 us)
Async XLA Ops:
  0.0 30.7 %copy-start.2 = (bf16[1024,512]{1,0:T(8,128)(2,1)S(1)}, bf16[1024,512]{1,0:T(8,128)(2,1)}, u32[]{:S(2)}) copy-start(bf16[1024,512]{1,0:T(8,128)(2,1)} %w_ref.1) | copy-start | bytes 3145732
  3.2 38.7 %copy-start.4 = (f32[512]{0:T(512)S(1)}, f32[512]{0:T(512)}, u32[]{:S(2)}) copy-start(f32[512]{0:T(512)} %param.9) | copy-start | bytes 6148
  3.2 38.7 %copy-start.5 = (s32[2,8]{1,0:T(2,128)S(1)}, s32[2,8]{1,0:T(2,128)}, u32[]{:S(2)}) copy-start(s32[2,8]{1,0:T(2,128)} %active_ref.1) | copy-start | bytes 196
  3.2 43.7 %copy-start = (bf16[2,2,128,2048]{3,2,1,0:T(8,128)(2,1)S(1)}, bf16[2,2,128,2048]{3,2,1,0:T(8,128)(2,1)}, u32[]{:S(2)}) copy-start(bf16[2,2,128,2048]{3,2,1,0:T(8,128)(2,1)} %own_ref.7) | copy-start | bytes 6291460
  4.5 15.8 %collective-permute-start = (bf16[1,128,2048]{2,1,0:T(8,128)(2,1)S(1)}, bf16[1,128,2048]{2,1,0:T(8,128)(2,1)S(1)}, u32[]{:S(2)}, u32[]{:S(2)}) collective-permute-start(bf16[1,128,2048]{2,1,0:T(8,128)(2,1)S(1)} %dynamic-slice_bitcast_fusion.1), channel_id=1, source_target_pairs={{0,4},{4,0},{8,12},{12,8},{1,5},{5,1},{9,13},{13,9},{2,6},{6,2},{1... | collective-permute-start | bytes 1572872 | tf_op jit(solution)/shard_map/ppermute | solution.py:146
  8.6 22.1 %collective-permute-start.7 = (bf16[1,128,2048]{2,1,0:T(8,128)(2,1)S(1)}, bf16[1,128,2048]{2,1,0:T(8,128)(2,1)S(1)}, u32[]{:S(2)}, u32[]{:S(2)}) collective-permute-start(bf16[1,128,2048]{2,1,0:T(8,128)(2,1)S(1)} %dynamic-slice_bitcast_fusion), channel_id=1, source_target_pairs={{0,4},{4,0},{8,12},{12,8},{1,5},{5,1},{9,13},{13,9},{2,6},{6,2},{1... | collective-permute-start | bytes 1572872 | tf_op jit(solution)/shard_map/ppermute | solution.py:146
  20.3 26.6 %collective-permute-start.1 = (bf16[1,128,2048]{2,1,0:T(8,128)(2,1)S(1)}, bf16[1,128,2048]{2,1,0:T(8,128)(2,1)S(1)}, u32[]{:S(2)}, u32[]{:S(2)}) collective-permute-start(bf16[1,128,2048]{2,1,0:T(8,128)(2,1)S(1)} %collective-permute-done.got_ref), channel_id=1, source_target_pairs={{0,1},{1,0},{2,3},{3,2},{4,5},{5,4},{6,7},{7,6},{8,9},{9,8},{10,11... | collective-permute-start | bytes 1572872 | tf_op jit(solution)/shard_map/ppermute | solution.py:147
  30.7 18.2 %collective-permute-start.8 = (bf16[1,128,2048]{2,1,0:T(8,128)(2,1)S(1)}, bf16[1,128,2048]{2,1,0:T(8,128)(2,1)S(1)}, u32[]{:S(2)}, u32[]{:S(2)}) collective-permute-start(bf16[1,128,2048]{2,1,0:T(8,128)(2,1)S(1)} %collective-permute-done.7.got_ref), channel_id=1, source_target_pairs={{0,1},{1,0},{2,3},{3,2},{4,5},{5,4},{6,7},{7,6},{8,9},{9,8},{10,11... | collective-permute-start | bytes 1572872 | tf_op jit(solution)/shard_map/ppermute | solution.py:147
  30.7 1.0 %copy-start.3 = (bf16[256,1024]{1,0:T(8,128)(2,1)S(1)}, bf16[256,1024]{1,0:T(8,128)(2,1)}, u32[]{:S(2)}) copy-start(bf16[256,1024]{1,0:T(8,128)(2,1)} %param.7) | copy-start | bytes 1572868
  32.2 6.7 %collective-permute-start.2 = (bf16[128,256]{1,0:T(8,128)(2,1)S(1)}, bf16[128,256]{1,0:T(8,128)(2,1)S(1)}, u32[]{:S(2)}, u32[]{:S(2)}) collective-permute-start(bf16[128,256]{1,0:T(8,128)(2,1)S(1)} %get-tuple-element.10), channel_id=1, source_target_pairs={{0,4},{4,8},{8,12},{12,0},{1,5},{5,9},{9,13},{13,1},{2,6},{6,10},{... | collective-permute-start | bytes 196616 | tf_op jit(solution)/shard_map/ppermute | solution.py:165
  34.0 7.7 %collective-permute-start.3 = (bf16[128,256]{1,0:T(8,128)(2,1)S(1)}, bf16[128,256]{1,0:T(8,128)(2,1)S(1)}, u32[]{:S(2)}, u32[]{:S(2)}) collective-permute-start(bf16[128,256]{1,0:T(8,128)(2,1)S(1)} %get-tuple-element.11), channel_id=1, source_target_pairs={{0,8},{4,12},{8,0},{12,4},{1,9},{5,13},{9,1},{13,5},{2,10},{6,14},... | collective-permute-start | bytes 196616 | tf_op jit(solution)/shard_map/ppermute | solution.py:165
  36.6 5.4 %collective-permute-start.4 = (bf16[128,256]{1,0:T(8,128)(2,1)S(1)}, bf16[128,256]{1,0:T(8,128)(2,1)S(1)}, u32[]{:S(2)}, u32[]{:S(2)}) collective-permute-start(bf16[128,256]{1,0:T(8,128)(2,1)S(1)} %get-tuple-element.12), channel_id=1, source_target_pairs={{0,12},{4,0},{8,4},{12,8},{1,13},{5,1},{9,5},{13,9},{2,14},{6,2},{... | collective-permute-start | bytes 196616 | tf_op jit(solution)/shard_map/ppermute | solution.py:165
  42.6 4.3 %collective-permute-start.5 = (bf16[2,64,256]{2,1,0:T(8,128)(2,1)S(1)}, bf16[2,64,256]{2,1,0:T(8,128)(2,1)S(1)}, u32[]{:S(2)}, u32[]{:S(2)}) collective-permute-start(bf16[2,64,256]{2,1,0:T(8,128)(2,1)S(1)} %codes.1.refs_0_), channel_id=1, source_target_pairs={{0,2},{2,0},{1,3},{3,1},{4,6},{6,4},{5,7},{7,5},{8,10},{10,8},{9,1... | collective-permute-start | bytes 196616 | tf_op jit(solution)/shard_map/ppermute | solution.py:179
  48.2 4.3 %copy-start.6 = (f32[2,2048]{1,0:T(2,128)S(1)}, f32[2,2048]{1,0:T(2,128)}, u32[]{:S(2)}) copy-start(f32[2,2048]{1,0:T(2,128)} %param.11) | copy-start | bytes 49156
  48.2 4.3 %copy-start.1 = (bf16[2,64,2048]{2,1,0:T(8,128)(2,1)S(1)}, bf16[2,64,2048]{2,1,0:T(8,128)(2,1)}, u32[]{:S(2)}) copy-start(bf16[2,64,2048]{2,1,0:T(8,128)(2,1)} %target_ref.3) | copy-start | bytes 1572868
  48.2 20.5 %collective-permute-start.6 = (bf16[64,2048]{1,0:T(8,128)(2,1)S(1)}, bf16[64,2048]{1,0:T(8,128)(2,1)S(1)}, u32[]{:S(2)}, u32[]{:S(2)}) collective-permute-start(bf16[64,2048]{1,0:T(8,128)(2,1)S(1)} %decode_send.2), channel_id=1, source_target_pairs={{0,8},{4,12},{8,0},{12,4},{1,9},{5,13},{9,1},{13,5},{2,10},{6,14},... | collective-permute-start | bytes 786440 | tf_op jit(solution)/shard_map/ppermute | solution.py:214
  50.1 22.7 %collective-permute-start.9 = (bf16[64,2048]{1,0:T(8,128)(2,1)S(1)}, bf16[64,2048]{1,0:T(8,128)(2,1)S(1)}, u32[]{:S(2)}, u32[]{:S(2)}) collective-permute-start(bf16[64,2048]{1,0:T(8,128)(2,1)S(1)} %decode_send.3), channel_id=1, source_target_pairs={{0,8},{4,12},{8,0},{12,4},{1,9},{5,13},{9,1},{13,5},{2,10},{6,14},... | collective-permute-start | bytes 786440 | tf_op jit(solution)/shard_map/ppermute | solution.py:214

commit v2 on v0

v2 whole, which is shorter than its diff:
```python
import functools

import jax
import jax.numpy as jnp
from jax import lax
from jax.experimental import pallas as pl
from jax.experimental.pallas import tpu as pltpu
from jax.sharding import PartitionSpec as P

VMEM_BYTES = 32 * 1024 * 1024
ENCODE_VMEM_BYTES = 60 * 1024 * 1024


def encode_kernel(n, acts_hbm, w_hbm, dec_hbm, terms_ref, *refs):
    part_refs, (acts_ref, w_ref, part_sems, acts_sems, w_sems) = refs[:-5], refs[-5:]
    cut = part_refs[0].shape[-1]
    half = n // 2
    width = w_ref.shape[1] // half
    copies_w = []
    for i in range(half):
        columns = slice(i * width, (i + 1) * width)
        copies_w.append(
            pltpu.make_async_copy(w_hbm.at[:, columns], w_ref.at[:, columns], w_sems.at[i])
        )
    copies_acts = [
        pltpu.make_async_copy(acts_hbm.at[:, i], acts_ref.at[i], acts_sems.at[i]) for i in range(2)
    ]
    mine = pl.ds(pl.multiple_of(lax.axis_index("rep") * cut, cut), cut)
    copies_part = [
        pltpu.make_async_copy(dec_hbm.at[i, :, :, mine], ref, part_sems.at[i])
        for i, ref in enumerate(part_refs)
    ]
    copies_acts[0].start()
    copies_w[0].start()
    copies_acts[1].start()
    for copy in copies_w[1:] + copies_part:
        copy.start()
    for i in range(half):
        copies_w[i].wait()
        for parity in range(2):
            if i == 0:
                copies_acts[parity].wait()
            rows = acts_ref[parity]
            rows = rows.reshape(rows.shape[0] * rows.shape[1], rows.shape[2])
            terms_ref[i * 2 + parity] = jnp.dot(
                rows, w_ref[:, i * width : (i + 1) * width], preferred_element_type=jnp.float32
            ).astype(jnp.bfloat16)
    for copy in copies_part:
        copy.wait()


def codes_kernel(n, share, tile_rows, active_ref, bias_ref, terms_ref, out_ref):
    src = lax.axis_index("src")
    tgt = lax.axis_index("tgt")
    parity, half = lax.rem(src, 2), src // 2
    block = out_ref.shape[2] // 2
    pre = terms_ref[0].astype(jnp.float32)
    for i in range(1, n):
        pre = pre + terms_ref[i].astype(jnp.float32)
    tiles, slots = active_ref.shape
    for piece in range(2):
        columns = slice(piece * block, (piece + 1) * block)
        bias = bias_ref[pl.ds(half * 2 + piece, 1), :]
        wanted = tgt * n + half * 2 + piece
        flags = []
        for tile in range(tiles):
            flags.append(
                lax.fori_loop(
                    0,
                    slots,
                    lambda i, total: total + (active_ref[tile, i] == wanted).astype(jnp.int32),
                    jnp.int32(0),
                    unroll=slots <= 16,
                )
            )
        for group in range(n // 2):
            tile = ((group * 2 + parity) * share) // tile_rows
            flag = flags[0]
            for i in range(1, tiles):
                flag = jnp.where(tile == i, flags[i], flag)
            live = jnp.where(flag > 0, 1.0, 0.0).astype(jnp.float32)
            rows = slice(group * share, (group + 1) * share)
            value = live * jnp.maximum(pre[rows, columns] + bias, 0.0)
            out_ref[group, :, columns] = value.astype(jnp.bfloat16)


def decode_kernel(n, groups, own_ref, got_ref, *refs):
    half = n // 2
    code_refs, out_refs, lhs_ref = refs[: 2 * groups], refs[-2 * half - 1 : -1], refs[-1]
    src, tgt = lax.axis_index("src"), lax.axis_index("tgt")
    parity = lax.rem(src, 2)
    share, block = code_refs[0].shape[1], code_refs[0].shape[2] // 2
    depth = groups * block
    for k in range(groups):
        place = lax.rem(tgt - k + groups, groups)
        for side in range(2):
            piece = parity if side == 0 else 1 - parity
            piece = pl.ds(pl.multiple_of(piece * block, block), block)
            columns = pl.ds(pl.multiple_of((side * groups + place) * block, block), block)
            for j in range(half):
                group = lax.rem(src // 2 + j, half)
                for r in range(2):
                    rows = slice((2 * j + r) * share, (2 * j + r + 1) * share)
                    lhs_ref[rows, columns] = code_refs[2 * k + r][group, :, piece]
    own = own_ref[...].reshape(depth, own_ref.shape[2])
    got = got_ref[...].reshape(depth, own_ref.shape[2])
    total = jnp.dot(lhs_ref[:, :depth], own, preferred_element_type=jnp.float32)
    total += jnp.dot(lhs_ref[:, depth:], got, preferred_element_type=jnp.float32)
    for i, ref in enumerate(out_refs):
        ref[...] = total[i * share : (i + 1) * share].astype(ref.dtype)


def add_kernel(layers, bias_ref, target_ref, *refs):
    out_ref = refs[-1]
    each = (len(refs) - 1) // (2 * layers)
    cut = refs[0].shape[1]
    rep = lax.axis_index("rep")
    for layer in range(layers):
        for side in range(2):
            core = rep if side == 0 else 1 - rep
            columns = pl.ds(pl.multiple_of(core * cut, cut), cut)
            total = bias_ref[layer : layer + 1, columns]
            total = total - target_ref[layer, :, columns].astype(jnp.float32)
            first = (layer * 2 + side) * each
            for ref in refs[first : first + each]:
                total = total + ref[...].astype(jnp.float32)
            out_ref[layer, :, columns] = total.astype(jnp.bfloat16)


def body(acts, enc_w, enc_b, dec_w, dec_b, targets, active):
    n = lax.axis_size("src")
    rows, features = acts.shape
    layers, groups, block, cols = dec_w.shape
    share = rows // n
    half = n // 2
    cut = cols // 2
    tile_rows = rows // active.shape[0]
    pair = [(i, i ^ 1) for i in range(n)]
    params = pltpu.CompilerParams(vmem_limit_bytes=VMEM_BYTES)
    vmem = pl.BlockSpec(memory_space=pltpu.VMEM)
    smem = pl.BlockSpec(memory_space=pltpu.SMEM)
    anywhere = pl.BlockSpec(memory_space=pl.ANY)
    cost = pl.CostEstimate(flops=0, bytes_accessed=0, transcendentals=0)

    def shape(*extent, kind=jnp.bfloat16):
        return jax.ShapeDtypeStruct(extent, kind)

    terms, *parts = pl.pallas_call(
        functools.partial(encode_kernel, n),
        out_shape=[shape(n, half * share, 2 * block)] + [shape(groups, block, cut)] * layers,
        in_specs=[anywhere] * 3,
        out_specs=[vmem] * (1 + layers),
        scratch_shapes=[
            pltpu.VMEM((2, half, share, features), jnp.bfloat16),
            pltpu.VMEM(enc_w.shape, jnp.bfloat16),
            pltpu.SemaphoreType.DMA((layers,)),
            pltpu.SemaphoreType.DMA((2,)),
            pltpu.SemaphoreType.DMA((half,)),
        ],
        compiler_params=pltpu.CompilerParams(vmem_limit_bytes=ENCODE_VMEM_BYTES),
        cost_estimate=cost,
        name="encode",
    )(acts.reshape(half, 2, share, features), enc_w, dec_w)
    got = [lax.ppermute(part, "src", pair) for part in parts]
    terms = lax.all_to_all(terms, "src", 0, 0, tiled=True)

    own = pl.pallas_call(
        functools.partial(codes_kernel, n, share, tile_rows),
        out_shape=shape(half, share, 2 * block),
        in_specs=[smem, vmem, vmem],
        out_specs=vmem,
        compiler_params=params,
        cost_estimate=cost,
        name="codes",
    )(active, enc_b.reshape(n, block), terms)
    codes = []
    for k in range(groups):
        for r in range(2):
            perm = [
                (i * 2 + c, (i + k) % groups * 2 + (c ^ r)) for i in range(groups) for c in range(2)
            ]
            codes.append(lax.ppermute(own, ("tgt", "rep"), perm) if k + r else own)

    sums, after = [], []
    for layer in range(layers):
        kinds = [jnp.float32] + [jnp.bfloat16] * (2 * half - 1)
        terms = pl.pallas_call(
            functools.partial(decode_kernel, n, groups),
            out_shape=[shape(share, cut, kind=kind) for kind in kinds],
            in_specs=[vmem] * (2 + 2 * groups) + [anywhere] * len(after),
            out_specs=[vmem] * (2 * half),
            scratch_shapes=[pltpu.VMEM((rows, 2 * groups * block), jnp.bfloat16)],
            compiler_params=params,
            cost_estimate=cost,
            name="decode",
        )(parts[layer], got[layer], *codes, *after)
        after = [terms[0]]
        for r in range(2):
            for j in range(half):
                perm = [
                    (i * 2 + c, (i + 2 * j) % n * 2 + (c ^ r)) for i in range(n) for c in range(2)
                ]
                term = terms[2 * j + r]
                sums.append(lax.ppermute(term, ("src", "rep"), perm) if j + r else term)

    return pl.pallas_call(
        functools.partial(add_kernel, layers),
        out_shape=shape(layers, share, cols),
        in_specs=[vmem] * (2 + len(sums)),
        out_specs=vmem,
        compiler_params=params,
        cost_estimate=cost,
        name="add",
    )(dec_b, targets, *sums)


def solution(mesh):
    in_specs = (
        P(("parts", "rep"), "src"),
        P("src", "tgt"),
        P("tgt"),
        P(None, None, "src", "tgt"),
        P(None, "tgt"),
        P(None, ("parts", "rep", "src"), "tgt"),
        P(("parts", "rep"), None),
    )
    out_specs = P(None, ("parts", "rep", "src"), "tgt")
    return jax.shard_map(body, mesh=mesh, in_specs=in_specs, out_specs=out_specs, check_vma=False)
```

time: 91.5 us -> 58.7 us (0.64)
  waiting for transfers between devices: 63.9 us -> 34 us
  starting transfers between devices: 0.04 us -> 17.6 us
  between operations: 13.4 us -> 0.08 us
  Pallas kernels: 0 us -> 5.73 us
  blocking collectives: 4.96 us -> 0 us
  matrix products: 4.78 us -> 0 us
  other arithmetic: 2.38 us -> 0 us
    reduce_scatter x1 -> x0, waiting for transfers between devices: 42.2 us -> none  [body(): lax.psum_scatter(decoded.astype(jnp.bfloat16), 'src', scatter_dimension=1...]
    ppermute x0 -> x11, waiting for transfers between devices: none -> 22.7 us  [the longest x6 19.3 us: body(): sums.append(lax.ppermute(term, ('src', 'rep'), perm) if j + r else term)]
    unnamed x3 -> x0, waiting for transfers between devices: 21.7 us -> none
    ppermute x0 -> x11, starting transfers between devices: none -> 13.7 us  [the longest x6 6.45 us: body(): sums.append(lax.ppermute(term, ('src', 'rep'), perm) if j + r else term)]
    all_to_all x0 -> x1, waiting for transfers between devices: none -> 11.3 us  [body(): terms = lax.all_to_all(terms, 'src', 0, 0, tiled=True)]
    pallas_call x0 -> x5, Pallas kernels: none -> 5.73 us  [the longest x1 3.18 us: body(): pl.pallas_call(functools.partial(encode_kernel, n), out_shape=[shape(n, h...]
    all_gather x1 -> x0, blocking collectives: 4.96 us -> none  [body(): lax.all_gather(codes, 'tgt', axis=1, tiled=True)]
    dot_general x2 -> x0, matrix products: 4.78 us -> none  [the longest x1 2.71 us: body(): jnp.einsum('dk,td->kt', enc_w, acts, preferred_element_type=jnp.float32)]
  transfers between devices with their start and end apart: 2 -> 12, of which waited for: 2 -> 7; matrix products, arithmetic and copies ran while one was open for 1% -> 0% of each run, Pallas kernels for 0% -> 3%
where the time goes in v2:
time: 58.7 us; the launch traced here: 58.5 us
  waiting for transfers between devices  34 us (58%)
  starting transfers between devices  17.6 us (30%)
  Pallas kernels  5.73 us (10%)
  local copies, waits for them, and re-layouts  1.06 us (2%)
    ppermute x6, waiting for transfers between devices, body(): sums.append(lax.ppermute(term, ('src', 'rep'), perm) if j + r else term)  19.3 us
    all_to_all x1, waiting for transfers between devices, body(): terms = lax.all_to_all(terms, 'src', 0, 0, tiled=True)  11.3 us
    ppermute x6, starting transfers between devices, body(): sums.append(lax.ppermute(term, ('src', 'rep'), perm) if j + r else term)  6.45 us
    ppermute x2, starting transfers between devices, body(): got = [lax.ppermute(part, 'src', pair) for part in parts]  5.12 us
    all_to_all x1, starting transfers between devices, body(): terms = lax.all_to_all(terms, 'src', 0, 0, tiled=True)  3.86 us
    ppermute x3, waiting for transfers between devices, body(): codes.append(lax.ppermute(own, ('tgt', 'rep'), perm) if k + r else own)  3.39 us
    pallas_call x1, Pallas kernels, body(): pl.pallas_call(functools.partial(encode_kernel, n), out_shape=[shape(n, h...  3.18 us
    ppermute x3, starting transfers between devices, body(): codes.append(lax.ppermute(own, ('tgt', 'rep'), perm) if k + r else own)  2.15 us
  transfers between devices with their start and end apart: 12, of which 7 were waited for; matrix products, arithmetic and copies ran while one was open for 0% of the time, Pallas kernels for 3%

profile of v2, /device:TPU:0, one launch (start us, length us, event | category | flops | bytes accessed | tf_op | source)
XLA Modules:
  0.0 58.5 jit_solution(12094571065419828010)
XLA Ops:
  0.0 0.0 copy-start.4
  0.0 0.0 copy-start.5
  0.0 0.0 copy-start.2
  0.0 3.2 %encode.1 = (bf16[4,128,256]{2,1,0:T(8,128)(2,1)}, bf16[2,128,1024]{2,1,0:T(8,128)(2,1)}, bf16[2,128,1024]{2,1,0:T(8,128)(2,1)}) custom-call(bf16[2,2,64,1024]{3,2,1,0:T(8,128)(2,1)} %bitcast.3, bf16[1024,512]{1,0:T(8,128)(2,1)} %w_hbm.1, bf16[2,2,128,2048]{3,2,1,0:T(8,128)(2,1)} %dec_hbm.1), custom_call_target="tpu_custom_call" | custom-call | tf_op jit(solution)/shard_map/encode/pallas_call | solution.py:148
  3.2 0.0 copy-start
  3.2 0.0 copy-start.3
  3.2 3.1 %collective-permute-start = (bf16[2,128,1024]{2,1,0:T(8,128)(2,1)}, bf16[2,128,1024]{2,1,0:T(8,128)(2,1)S(1)}, u32[]{:S(2)}, u32[]{:S(2)}) collective-permute-start(bf16[2,128,1024]{2,1,0:T(8,128)(2,1)} %get-tuple-element.16.own_ref), channel_id=1, source_target_pairs={{0,4},{4,0},{8,12},{12,8},{1,5},{5,1},{9,13},{13,9},{2,6},{6,2},{1... | collective-permute-start | bytes 1572872 | tf_op jit(solution)/shard_map/ppermute | solution.py:164
  6.3 3.9 %all-to-all-start = ((bf16[4,128,256]{2,1,0:T(8,128)(2,1)}), bf16[4,128,256]{2,1,0:T(8,128)(2,1)S(1)}, u32[]{:S(2)}, u32[]{:S(2)}) async-start(bf16[4,128,256]{2,1,0:T(8,128)(2,1)} %get-tuple-element.17), calls=%async_computation | async-start | bytes 524288 | tf_op jit(solution)/shard_map/all_to_all | solution.py:165
  10.2 2.0 %collective-permute-start.7 = (bf16[2,128,1024]{2,1,0:T(8,128)(2,1)}, bf16[2,128,1024]{2,1,0:T(8,128)(2,1)S(1)}, u32[]{:S(2)}, u32[]{:S(2)}) collective-permute-start(bf16[2,128,1024]{2,1,0:T(8,128)(2,1)} %get-tuple-element.22.own_ref), channel_id=1, source_target_pairs={{0,4},{4,0},{8,12},{12,8},{1,5},{5,1},{9,13},{13,9},{2,6},{6,2},{1... | collective-permute-start | bytes 1572872 | tf_op jit(solution)/shard_map/ppermute | solution.py:164
  12.2 11.3 %all-to-all-done.terms_ref = bf16[4,128,256]{2,1,0:T(8,128)(2,1)S(1)} async-done(((bf16[4,128,256]{2,1,0:T(8,128)(2,1)}), bf16[4,128,256]{2,1,0:T(8,128)(2,1)S(1)}, u32[]{:S(2)}, u32[]{:S(2)}) %all-to-all-start) | async-done | bytes 262176 | tf_op jit(solution)/shard_map/all_to_all | solution.py:165
  23.5 0.0 copy-done.4
  23.5 0.0 copy-done.5
  23.5 0.6 %codes.1.refs_0_ = bf16[2,64,256]{2,1,0:T(8,128)(2,1)S(1)} custom-call(s32[2,8]{1,0:T(2,128)S(1)} %copy-done.5, f32[4,128]{1,0:T(4,128)S(1)} %bitcast.2, bf16[4,128,256]{2,1,0:T(8,128)(2,1)S(1)} %all-to-all-done.terms_ref), custom_call_target="tpu_custom_call" | custom-call | tf_op jit(solution)/shard_map/codes/pallas_call | solution.py:167
  24.1 0.1 collective-permute-start.3
  24.2 2.0 %collective-permute-start.2 = (bf16[2,64,256]{2,1,0:T(8,128)(2,1)S(1)}, bf16[2,64,256]{2,1,0:T(8,128)(2,1)S(1)}, u32[]{:S(2)}, u32[]{:S(2)}) collective-permute-start(bf16[2,64,256]{2,1,0:T(8,128)(2,1)S(1)} %codes.1.refs_0_), channel_id=1, source_target_pairs={{0,2},{1,3},{2,0},{3,1},{4,6},{5,7},{6,4},{7,5},{8,10},{9,11},{10,... | collective-permute-start | bytes 196616 | tf_op jit(solution)/shard_map/ppermute | solution.py:182
  26.2 0.0 collective-permute-start.1
  26.3 1.8 %collective-permute-done.3.refs_3_ = bf16[2,64,256]{2,1,0:T(8,128)(2,1)S(1)} collective-permute-done((bf16[2,64,256]{2,1,0:T(8,128)(2,1)S(1)}, bf16[2,64,256]{2,1,0:T(8,128)(2,1)S(1)}, u32[]{:S(2)}, u32[]{:S(2)}) %collective-permute-start.3) | collective-permute-done | bytes 65568 | tf_op jit(solution)/shard_map/ppermute | solution.py:182
  28.1 1.6 %collective-permute-done.2.refs_2_ = bf16[2,64,256]{2,1,0:T(8,128)(2,1)S(1)} collective-permute-done((bf16[2,64,256]{2,1,0:T(8,128)(2,1)S(1)}, bf16[2,64,256]{2,1,0:T(8,128)(2,1)S(1)}, u32[]{:S(2)}, u32[]{:S(2)}) %collective-permute-start.2) | collective-permute-done | bytes 65568 | tf_op jit(solution)/shard_map/ppermute | solution.py:182
  29.7 0.0 collective-permute-done.1.refs_1_
  29.7 0.0 collective-permute-done.got_ref
  29.7 0.0 copy-start.1
  29.7 1.0 %copy-done.1 = bf16[2,128,1024]{2,1,0:T(8,128)(2,1)S(1)} copy-done((bf16[2,128,1024]{2,1,0:T(8,128)(2,1)S(1)}, bf16[2,128,1024]{2,1,0:T(8,128)(2,1)}, u32[]{:S(2)}) %copy-start.1) | copy-done | bytes 524312
  30.7 0.5 decode.2
  31.2 3.3 %collective-permute-start.4 = (bf16[64,1024]{1,0:T(8,128)(2,1)S(1)}, bf16[64,1024]{1,0:T(8,128)(2,1)S(1)}, u32[]{:S(2)}, u32[]{:S(2)}) collective-permute-start(bf16[64,1024]{1,0:T(8,128)(2,1)S(1)} %get-tuple-element.19), channel_id=1, source_target_pairs={{0,8},{1,9},{4,12},{5,13},{8,0},{9,1},{12,4},{13,5},{2,10},{3,11},... | collective-permute-start | bytes 393224 | tf_op jit(solution)/shard_map/ppermute | solution.py:204
  34.5 0.0 collective-permute-start.5
  34.5 0.2 collective-permute-start.6
  34.7 0.0 collective-permute-done.7.got_ref
  34.7 0.0 copy-done
  34.7 0.5 decode.3
  35.2 2.9 %collective-permute-start.8 = (bf16[64,1024]{1,0:T(8,128)(2,1)S(1)}, bf16[64,1024]{1,0:T(8,128)(2,1)S(1)}, u32[]{:S(2)}, u32[]{:S(2)}) collective-permute-start(bf16[64,1024]{1,0:T(8,128)(2,1)S(1)} %get-tuple-element.24), channel_id=1, source_target_pairs={{0,8},{1,9},{4,12},{5,13},{8,0},{9,1},{12,4},{13,5},{2,10},{3,11},... | collective-permute-start | bytes 393224 | tf_op jit(solution)/shard_map/ppermute | solution.py:204
  38.1 0.0 collective-permute-start.9
  38.1 9.0 %collective-permute-done.4.refs_1_ = bf16[64,1024]{1,0:T(8,128)(2,1)S(1)} collective-permute-done((bf16[64,1024]{1,0:T(8,128)(2,1)S(1)}, bf16[64,1024]{1,0:T(8,128)(2,1)S(1)}, u32[]{:S(2)}, u32[]{:S(2)}) %collective-permute-start.4) | collective-permute-done | bytes 131104 | tf_op jit(solution)/shard_map/ppermute | solution.py:204
  47.1 0.0 collective-permute-start.10
  47.1 0.0 collective-permute-done.5.refs_2_
  47.1 1.9 %collective-permute-done.6.refs_3_ = bf16[64,1024]{1,0:T(8,128)(2,1)S(1)} collective-permute-done((bf16[64,1024]{1,0:T(8,128)(2,1)S(1)}, bf16[64,1024]{1,0:T(8,128)(2,1)S(1)}, u32[]{:S(2)}, u32[]{:S(2)}) %collective-permute-start.6) | collective-permute-done | bytes 131104 | tf_op jit(solution)/shard_map/ppermute | solution.py:204
  49.0 6.5 %collective-permute-done.8.refs_5_ = bf16[64,1024]{1,0:T(8,128)(2,1)S(1)} collective-permute-done((bf16[64,1024]{1,0:T(8,128)(2,1)S(1)}, bf16[64,1024]{1,0:T(8,128)(2,1)S(1)}, u32[]{:S(2)}, u32[]{:S(2)}) %collective-permute-start.8) | collective-permute-done | bytes 131104 | tf_op jit(solution)/shard_map/ppermute | solution.py:204
  55.6 0.0 collective-permute-done.9.refs_6_
  55.6 1.9 %collective-permute-done.10.refs_7_ = bf16[64,1024]{1,0:T(8,128)(2,1)S(1)} collective-permute-done((bf16[64,1024]{1,0:T(8,128)(2,1)S(1)}, bf16[64,1024]{1,0:T(8,128)(2,1)S(1)}, u32[]{:S(2)}, u32[]{:S(2)}) %collective-permute-start.10) | collective-permute-done | bytes 131104 | tf_op jit(solution)/shard_map/ppermute | solution.py:204
  57.5 0.0 copy-done.2
  57.5 0.0 copy-done.3
  57.5 1.0 %add.1 = bf16[2,64,2048]{2,1,0:T(8,128)(2,1)} custom-call(f32[2,2048]{1,0:T(2,128)S(1)} %copy-done.3, bf16[2,64,2048]{2,1,0:T(8,128)(2,1)S(1)} %copy-done.2, f32[64,1024]{1,0:T(8,128)S(1)} %get-tuple-element.18.refs_4_.refs_0_, bf16[64,1024]{1,0:T(8,128)(2,1)S(1)} %collective-permute-done.4.refs_1_, bf16[64,1024]{1,0:T(8,128)(2,1)S(1)} %collective-permute-done.5.refs_2_, ...), custom_call_target="tpu_custom_call" | custom-call | tf_op jit(solution)/shard_map/add/pallas_call | solution.py:206
Async XLA Ops:
  0.0 23.5 %copy-start.4 = (f32[512]{0:T(512)S(1)}, f32[512]{0:T(512)}, u32[]{:S(2)}) copy-start(f32[512]{0:T(512)} %param.9) | copy-start | bytes 6148
  0.0 23.5 %copy-start.5 = (s32[2,8]{1,0:T(2,128)S(1)}, s32[2,8]{1,0:T(2,128)}, u32[]{:S(2)}) copy-start(s32[2,8]{1,0:T(2,128)} %active_ref.1) | copy-start | bytes 196
  0.0 57.5 %copy-start.2 = (bf16[2,64,2048]{2,1,0:T(8,128)(2,1)S(1)}, bf16[2,64,2048]{2,1,0:T(8,128)(2,1)}, u32[]{:S(2)}) copy-start(bf16[2,64,2048]{2,1,0:T(8,128)(2,1)} %target_ref.1) | copy-start | bytes 1572868
  3.2 31.5 %copy-start = (bf16[2,128,1024]{2,1,0:T(8,128)(2,1)S(1)}, bf16[2,128,1024]{2,1,0:T(8,128)(2,1)}, u32[]{:S(2)}) copy-start(bf16[2,128,1024]{2,1,0:T(8,128)(2,1)} %get-tuple-element.22.own_ref) | copy-start | bytes 1572868
  3.2 54.3 %copy-start.3 = (f32[2,2048]{1,0:T(2,128)S(1)}, f32[2,2048]{1,0:T(2,128)}, u32[]{:S(2)}) copy-start(f32[2,2048]{1,0:T(2,128)} %bias_ref.1) | copy-start | bytes 49156
  3.2 26.5 %collective-permute-start = (bf16[2,128,1024]{2,1,0:T(8,128)(2,1)}, bf16[2,128,1024]{2,1,0:T(8,128)(2,1)S(1)}, u32[]{:S(2)}, u32[]{:S(2)}) collective-permute-start(bf16[2,128,1024]{2,1,0:T(8,128)(2,1)} %get-tuple-element.16.own_ref), channel_id=1, source_target_pairs={{0,4},{4,0},{8,12},{12,8},{1,5},{5,1},{9,13},{13,9},{2,6},{6,2},{1... | collective-permute-start | bytes 1572872 | tf_op jit(solution)/shard_map/ppermute | solution.py:164
  6.3 17.2 %all-to-all-start = ((bf16[4,128,256]{2,1,0:T(8,128)(2,1)}), bf16[4,128,256]{2,1,0:T(8,128)(2,1)S(1)}, u32[]{:S(2)}, u32[]{:S(2)}) async-start(bf16[4,128,256]{2,1,0:T(8,128)(2,1)} %get-tuple-element.17), calls=%async_computation | async-start | bytes 524288 | tf_op jit(solution)/shard_map/all_to_all | solution.py:165
  10.2 24.6 %collective-permute-start.7 = (bf16[2,128,1024]{2,1,0:T(8,128)(2,1)}, bf16[2,128,1024]{2,1,0:T(8,128)(2,1)S(1)}, u32[]{:S(2)}, u32[]{:S(2)}) collective-permute-start(bf16[2,128,1024]{2,1,0:T(8,128)(2,1)} %get-tuple-element.22.own_ref), channel_id=1, source_target_pairs={{0,4},{4,0},{8,12},{12,8},{1,5},{5,1},{9,13},{13,9},{2,6},{6,2},{1... | collective-permute-start | bytes 1572872 | tf_op jit(solution)/shard_map/ppermute | solution.py:164
  24.1 4.0 %collective-permute-start.3 = (bf16[2,64,256]{2,1,0:T(8,128)(2,1)S(1)}, bf16[2,64,256]{2,1,0:T(8,128)(2,1)S(1)}, u32[]{:S(2)}, u32[]{:S(2)}) collective-permute-start(bf16[2,64,256]{2,1,0:T(8,128)(2,1)S(1)} %codes.1.refs_0_), channel_id=1, source_target_pairs={{0,3},{1,2},{2,1},{3,0},{4,7},{5,6},{6,5},{7,4},{8,11},{9,10},{10,... | collective-permute-start | bytes 196616 | tf_op jit(solution)/shard_map/ppermute | solution.py:182
  24.2 5.5 %collective-permute-start.2 = (bf16[2,64,256]{2,1,0:T(8,128)(2,1)S(1)}, bf16[2,64,256]{2,1,0:T(8,128)(2,1)S(1)}, u32[]{:S(2)}, u32[]{:S(2)}) collective-permute-start(bf16[2,64,256]{2,1,0:T(8,128)(2,1)S(1)} %codes.1.refs_0_), channel_id=1, source_target_pairs={{0,2},{1,3},{2,0},{3,1},{4,6},{5,7},{6,4},{7,5},{8,10},{9,11},{10,... | collective-permute-start | bytes 196616 | tf_op jit(solution)/shard_map/ppermute | solution.py:182
  26.2 3.4 %collective-permute-start.1 = (bf16[2,64,256]{2,1,0:T(8,128)(2,1)S(1)}, bf16[2,64,256]{2,1,0:T(8,128)(2,1)S(1)}, u32[]{:S(2)}, u32[]{:S(2)}) collective-permute-start(bf16[2,64,256]{2,1,0:T(8,128)(2,1)S(1)} %codes.1.refs_0_), channel_id=1, source_target_pairs={{0,1},{1,0},{2,3},{3,2},{4,5},{5,4},{6,7},{7,6},{8,9},{9,8},{10,11... | collective-permute-start | bytes 196616 | tf_op jit(solution)/shard_map/ppermute | solution.py:182
  29.7 1.0 %copy-start.1 = (bf16[2,128,1024]{2,1,0:T(8,128)(2,1)S(1)}, bf16[2,128,1024]{2,1,0:T(8,128)(2,1)}, u32[]{:S(2)}) copy-start(bf16[2,128,1024]{2,1,0:T(8,128)(2,1)} %get-tuple-element.16.own_ref) | copy-start | bytes 1572868
  31.2 15.9 %collective-permute-start.4 = (bf16[64,1024]{1,0:T(8,128)(2,1)S(1)}, bf16[64,1024]{1,0:T(8,128)(2,1)S(1)}, u32[]{:S(2)}, u32[]{:S(2)}) collective-permute-start(bf16[64,1024]{1,0:T(8,128)(2,1)S(1)} %get-tuple-element.19), channel_id=1, source_target_pairs={{0,8},{1,9},{4,12},{5,13},{8,0},{9,1},{12,4},{13,5},{2,10},{3,11},... | collective-permute-start | bytes 393224 | tf_op jit(solution)/shard_map/ppermute | solution.py:204
  34.5 12.6 %collective-permute-start.5 = (bf16[64,1024]{1,0:T(8,128)(2,1)S(1)}, bf16[64,1024]{1,0:T(8,128)(2,1)S(1)}, u32[]{:S(2)}, u32[]{:S(2)}) collective-permute-start(bf16[64,1024]{1,0:T(8,128)(2,1)S(1)} %get-tuple-element.20), channel_id=1, source_target_pairs={{0,1},{1,0},{4,5},{5,4},{8,9},{9,8},{12,13},{13,12},{2,3},{3,2},{6... | collective-permute-start | bytes 393224 | tf_op jit(solution)/shard_map/ppermute | solution.py:204
  34.5 14.5 %collective-permute-start.6 = (bf16[64,1024]{1,0:T(8,128)(2,1)S(1)}, bf16[64,1024]{1,0:T(8,128)(2,1)S(1)}, u32[]{:S(2)}, u32[]{:S(2)}) collective-permute-start(bf16[64,1024]{1,0:T(8,128)(2,1)S(1)} %get-tuple-element.21), channel_id=1, source_target_pairs={{0,9},{1,8},{4,13},{5,12},{8,1},{9,0},{12,5},{13,4},{2,11},{3,10},... | collective-permute-start | bytes 393224 | tf_op jit(solution)/shard_map/ppermute | solution.py:204
  35.2 20.3 %collective-permute-start.8 = (bf16[64,1024]{1,0:T(8,128)(2,1)S(1)}, bf16[64,1024]{1,0:T(8,128)(2,1)S(1)}, u32[]{:S(2)}, u32[]{:S(2)}) collective-permute-start(bf16[64,1024]{1,0:T(8,128)(2,1)S(1)} %get-tuple-element.24), channel_id=1, source_target_pairs={{0,8},{1,9},{4,12},{5,13},{8,0},{9,1},{12,4},{13,5},{2,10},{3,11},... | collective-permute-start | bytes 393224 | tf_op jit(solution)/shard_map/ppermute | solution.py:204
  38.1 17.5 %collective-permute-start.9 = (bf16[64,1024]{1,0:T(8,128)(2,1)S(1)}, bf16[64,1024]{1,0:T(8,128)(2,1)S(1)}, u32[]{:S(2)}, u32[]{:S(2)}) collective-permute-start(bf16[64,1024]{1,0:T(8,128)(2,1)S(1)} %get-tuple-element.25), channel_id=1, source_target_pairs={{0,1},{1,0},{4,5},{5,4},{8,9},{9,8},{12,13},{13,12},{2,3},{3,2},{6... | collective-permute-start | bytes 393224 | tf_op jit(solution)/shard_map/ppermute | solution.py:204
  47.1 10.3 %collective-permute-start.10 = (bf16[64,1024]{1,0:T(8,128)(2,1)S(1)}, bf16[64,1024]{1,0:T(8,128)(2,1)S(1)}, u32[]{:S(2)}, u32[]{:S(2)}) collective-permute-start(bf16[64,1024]{1,0:T(8,128)(2,1)S(1)} %get-tuple-element.26), channel_id=1, source_target_pairs={{0,9},{1,8},{4,13},{5,12},{8,1},{9,0},{12,5},{13,4},{2,11},{3,10},... | collective-permute-start | bytes 393224 | tf_op jit(solution)/shard_map/ppermute | solution.py:204

commit v3 on v2

v3 whole, which is shorter than its diff:
```python
import functools

import jax
import jax.numpy as jnp
from jax import lax
from jax.experimental import pallas as pl
from jax.experimental.pallas import tpu as pltpu
from jax.sharding import PartitionSpec as P

VMEM_BYTES = 32 * 1024 * 1024
ENCODE_VMEM_BYTES = 60 * 1024 * 1024
LANES = 128
SHARES = (4, 4)


def cut_columns(columns):
    tiles = columns // LANES
    pieces, start = [], 0
    for i, eighths in enumerate(SHARES):
        stop = min(tiles, start + -(-tiles * eighths // 8))
        stop = tiles if i == len(SHARES) - 1 else stop
        if stop > start:
            pieces.append((start * LANES, (stop - start) * LANES))
        start = stop
    return pieces


def part_copies(piece, dec_hbm, part_ref, sems):
    layers, groups, _, cols = dec_hbm.shape
    start = pl.multiple_of(lax.axis_index("rep") * (cols // 2) + piece[0], LANES)
    copies = []
    for layer in range(layers):
        for group in range(groups):
            source = dec_hbm.at[layer, group, :, pl.ds(start, piece[1])]
            copies.append(
                pltpu.make_async_copy(
                    source, part_ref.at[layer, group], sems.at[layer * groups + group]
                )
            )
            copies[-1].start()
    return copies


def encode_kernel(
    n, piece, acts_hbm, w_hbm, dec_hbm, terms_ref, part_ref, acts_ref, w_ref, part_sems, acts_sems, w_sems
):
    half = n // 2
    width = w_ref.shape[1] // half
    depth = w_ref.shape[0] // 4
    copies_w, copies_acts = [], []
    for i in range(half):
        columns = slice(i * width, (i + 1) * width)
        for j in range(4):
            rows = slice(j * depth, (j + 1) * depth)
            copies_w.append(
                pltpu.make_async_copy(
                    w_hbm.at[rows, columns], w_ref.at[rows, columns], w_sems.at[i * 4 + j]
                )
            )
    for i in range(2):
        for j in range(half):
            copies_acts.append(
                pltpu.make_async_copy(
                    acts_hbm.at[j, i], acts_ref.at[i, j], acts_sems.at[i * half + j]
                )
            )
    for copy in copies_w[:4] + copies_acts + copies_w[4:]:
        copy.start()
    copies_part = part_copies(piece, dec_hbm, part_ref, part_sems)
    for i in range(half):
        for copy in copies_w[i * 4 : i * 4 + 4]:
            copy.wait()
        for parity in range(2):
            if i == 0:
                for copy in copies_acts[parity * half : (parity + 1) * half]:
                    copy.wait()
            rows = acts_ref[parity]
            rows = rows.reshape(rows.shape[0] * rows.shape[1], rows.shape[2])
            terms_ref[i * 2 + parity] = jnp.dot(
                rows, w_ref[:, i * width : (i + 1) * width], preferred_element_type=jnp.float32
            ).astype(jnp.bfloat16)
    for copy in copies_part:
        copy.wait()


def codes_kernel(n, share, tile_rows, piece, active_ref, bias_ref, terms_ref, *refs):
    copies_part = []
    if piece is None:
        (out_ref,) = refs
    else:
        dec_hbm, out_ref, part_ref, part_sems = refs
        copies_part = part_copies(piece, dec_hbm, part_ref, part_sems)
    src = lax.axis_index("src")
    tgt = lax.axis_index("tgt")
    parity, half = lax.rem(src, 2), src // 2
    block = out_ref.shape[2] // 2
    pre = terms_ref[0].astype(jnp.float32)
    for i in range(1, n):
        pre = pre + terms_ref[i].astype(jnp.float32)
    tiles, slots = active_ref.shape
    for piece in range(2):
        columns = slice(piece * block, (piece + 1) * block)
        bias = bias_ref[pl.ds(half * 2 + piece, 1), :]
        wanted = tgt * n + half * 2 + piece
        flags = []
        for tile in range(tiles):
            flags.append(
                lax.fori_loop(
                    0,
                    slots,
                    lambda i, total: total + (active_ref[tile, i] == wanted).astype(jnp.int32),
                    jnp.int32(0),
                    unroll=slots <= 16,
                )
            )
        for group in range(n // 2):
            tile = ((group * 2 + parity) * share) // tile_rows
            flag = flags[0]
            for i in range(1, tiles):
                flag = jnp.where(tile == i, flags[i], flag)
            live = jnp.where(flag > 0, 1.0, 0.0).astype(jnp.float32)
            rows = slice(group * share, (group + 1) * share)
            value = live * jnp.maximum(pre[rows, columns] + bias, 0.0)
            out_ref[group, :, columns] = value.astype(jnp.bfloat16)
    for copy in copies_part:
        copy.wait()


def decode_kernel(n, piece, later, dec_hbm, got_hbm, *refs):
    half = n // 2
    layers, groups, block, _ = dec_hbm.shape
    code_refs, refs = refs[: 2 * groups], refs[2 * groups :]
    out_refs, refs = refs[-5 - 2 * half - (later is not None) :][: 2 * half], refs[-5 - (later is not None) :]
    own_ref, got_ref, lhs_ref, sems, part_sems = refs[-5:]
    copies = part_copies(piece, dec_hbm, own_ref, sems)
    for layer in range(layers):
        for group in range(groups):
            copies.append(
                pltpu.make_async_copy(
                    got_hbm.at[layer, group],
                    got_ref.at[layer, group],
                    sems.at[(layers + layer) * groups + group],
                )
            )
            copies[-1].start()
    copies_part = []
    if later is not None:
        copies_part = part_copies(later, dec_hbm, refs[0], part_sems)
    src, tgt = lax.axis_index("src"), lax.axis_index("tgt")
    parity = lax.rem(src, 2)
    share = code_refs[0].shape[1]
    depth, width = groups * block, piece[1]
    for k in range(groups):
        place = lax.rem(tgt - k + groups, groups)
        for side in range(2):
            latents = parity if side == 0 else 1 - parity
            latents = pl.ds(pl.multiple_of(latents * block, block), block)
            columns = pl.ds(pl.multiple_of((side * groups + place) * block, block), block)
            for j in range(half):
                group = lax.rem(src // 2 + j, half)
                for r in range(2):
                    rows = slice((2 * j + r) * share, (2 * j + r + 1) * share)
                    lhs_ref[rows, columns] = code_refs[2 * k + r][group, :, latents]
    for copy in copies:
        copy.wait()
    for layer in range(layers):
        own = own_ref[layer].reshape(depth, width)
        got = got_ref[layer].reshape(depth, width)
        total = jnp.dot(lhs_ref[:, :depth], own, preferred_element_type=jnp.float32)
        total += jnp.dot(lhs_ref[:, depth:], got, preferred_element_type=jnp.float32)
        for i, ref in enumerate(out_refs):
            ref[layer] = total[i * share : (i + 1) * share].astype(ref.dtype)
    for copy in copies_part:
        copy.wait()


def add_kernel(n, pieces, bias_ref, target_ref, *refs):
    out_hbm, out_ref, sems = refs[-3:]
    half = n // 2
    layers, _, cols = target_ref.shape
    rep = lax.axis_index("rep")
    copies = []
    for i, (first, width) in enumerate(pieces):
        for side in range(2):
            core = rep if side == 0 else 1 - rep
            columns = pl.ds(pl.multiple_of(core * (cols // 2) + first, LANES), width)
            mine = refs[(2 * i + side) * half : (2 * i + side + 1) * half]
            for layer in range(layers):
                total = bias_ref[layer : layer + 1, columns]
                total = total - target_ref[layer, :, columns].astype(jnp.float32)
                for ref in mine:
                    total = total + ref[layer].astype(jnp.float32)
                out_ref[layer, :, columns] = total.astype(jnp.bfloat16)
                copies.append(
                    pltpu.make_async_copy(
                        out_ref.at[layer, :, columns],
                        out_hbm.at[layer, :, columns],
                        sems.at[(2 * i + side) * layers + layer],
                    )
                )
                copies[-1].start()
    for copy in copies:
        copy.wait()


def body(acts, enc_w, enc_b, dec_w, dec_b, targets, active):
    n = lax.axis_size("src")
    rows, features = acts.shape
    layers, groups, block, cols = dec_w.shape
    share = rows // n
    half = n // 2
    pieces = cut_columns(cols // 2)
    tile_rows = rows // active.shape[0]
    pair = [(i, i ^ 1) for i in range(n)]
    params = pltpu.CompilerParams(vmem_limit_bytes=VMEM_BYTES)
    vmem = pl.BlockSpec(memory_space=pltpu.VMEM)
    smem = pl.BlockSpec(memory_space=pltpu.SMEM)
    anywhere = pl.BlockSpec(memory_space=pl.ANY)
    cost = pl.CostEstimate(flops=0, bytes_accessed=0, transcendentals=0)
    part_sems = pltpu.SemaphoreType.DMA((layers * groups,))

    def shape(*extent, kind=jnp.bfloat16):
        return jax.ShapeDtypeStruct(extent, kind)

    def part_shapes(i):
        return [shape(layers, groups, block, pieces[i][1])] if i < len(pieces) else []

    terms, part = pl.pallas_call(
        functools.partial(encode_kernel, n, pieces[0]),
        out_shape=[shape(n, half * share, 2 * block)] + part_shapes(0),
        in_specs=[anywhere] * 3,
        out_specs=[vmem] * 2,
        scratch_shapes=[
            pltpu.VMEM((2, half, share, features), jnp.bfloat16),
            pltpu.VMEM(enc_w.shape, jnp.bfloat16),
            part_sems,
            pltpu.SemaphoreType.DMA((2 * half,)),
            pltpu.SemaphoreType.DMA((4 * half,)),
        ],
        compiler_params=pltpu.CompilerParams(vmem_limit_bytes=ENCODE_VMEM_BYTES),
        cost_estimate=cost,
        name="encode",
    )(acts.reshape(half, 2, share, features), enc_w, dec_w)
    got = [lax.ppermute(part, "src", pair)]
    terms = lax.all_to_all(terms, "src", 0, 0, tiled=True)

    more = len(pieces) > 1
    own, *part = pl.pallas_call(
        functools.partial(codes_kernel, n, share, tile_rows, pieces[1] if more else None),
        out_shape=[shape(half, share, 2 * block)] + part_shapes(1),
        in_specs=[smem, vmem, vmem] + [anywhere] * more,
        out_specs=[vmem] * (1 + more),
        scratch_shapes=[part_sems] * more,
        compiler_params=params,
        cost_estimate=cost,
        name="codes",
    )(active, enc_b.reshape(n, block), terms, *[dec_w] * more)
    got += [lax.ppermute(value, "src", pair) for value in part]
    codes = []
    for k in range(groups):
        for r in range(2):
            perm = [
                (i * 2 + c, (i + k) % groups * 2 + (c ^ r)) for i in range(groups) for c in range(2)
            ]
            codes.append(lax.ppermute(own, ("tgt", "rep"), perm) if k + r else own)

    sums, after = [], []
    for i, piece in enumerate(pieces):
        later = pieces[i + 2] if i + 2 < len(pieces) else None
        width = piece[1]
        shapes = [shape(layers, share, width)] * (2 * half)
        shapes[0] = shape(layers, share, width, kind=jnp.float32)
        shapes += part_shapes(i + 2)
        terms = pl.pallas_call(
            functools.partial(decode_kernel, n, piece, later),
            out_shape=shapes,
            in_specs=[anywhere] * 2 + [vmem] * (2 * groups) + [anywhere] * len(after),
            out_specs=[vmem] * len(shapes),
            scratch_shapes=[
                pltpu.VMEM((layers, groups, block, width), jnp.bfloat16),
                pltpu.VMEM((layers, groups, block, width), jnp.bfloat16),
                pltpu.VMEM((rows, 2 * groups * block), jnp.bfloat16),
                pltpu.SemaphoreType.DMA((2 * layers * groups,)),
                part_sems,
            ],
            compiler_params=params,
            cost_estimate=cost,
            name="decode",
        )(dec_w, got[i], *codes, *after)
        after = [terms[0]]
        got += [lax.ppermute(value, "src", pair) for value in terms[2 * half :]]
        for r in range(2):
            for j in range(half):
                perm = [
                    (d * 2 + c, (d + 2 * j) % n * 2 + (c ^ r)) for d in range(n) for c in range(2)
                ]
                term = terms[2 * j + r]
                sums.append(lax.ppermute(term, ("src", "rep"), perm) if j + r else term)

    return pl.pallas_call(
        functools.partial(add_kernel, n, pieces),
        out_shape=shape(layers, share, cols),
        in_specs=[vmem] * (2 + len(sums)),
        out_specs=anywhere,
        scratch_shapes=[
            pltpu.VMEM((layers, share, cols), jnp.bfloat16),
            pltpu.SemaphoreType.DMA((2 * len(pieces) * layers,)),
        ],
        compiler_params=params,
        cost_estimate=cost,
        name="add",
    )(dec_b, targets, *sums)


def solution(mesh):
    in_specs = (
        P(("parts", "rep"), "src"),
        P("src", "tgt"),
        P("tgt"),
        P(None, None, "src", "tgt"),
        P(None, "tgt"),
        P(None, ("parts", "rep", "src"), "tgt"),
        P(("parts", "rep"), None),
    )
    out_specs = P(None, ("parts", "rep", "src"), "tgt")
    return jax.shard_map(body, mesh=mesh, in_specs=in_specs, out_specs=out_specs, check_vma=False)
```

time: 58.7 us -> 59.7 us (1.017)
  Pallas kernels: 5.73 us -> 7.71 us
  starting transfers between devices: 17.6 us -> 18.7 us
  local copies, waits for them, and re-layouts: 1.06 us -> 0.02 us
  waiting for transfers between devices: 34 us -> 33 us
    ppermute x2, waiting for transfers between devices: 0.01 us -> 13.3 us  [the longest x1 10.9 us: body(): got += [lax.ppermute(value, 'src', pair) for value in part]]
    ppermute x6, waiting for transfers between devices: 19.3 us -> 9.74 us  [body(): sums.append(lax.ppermute(term, ('src', 'rep'), perm) if j + r else term)]
    all_to_all x1, waiting for transfers between devices: 11.3 us -> 6.25 us  [body(): terms = lax.all_to_all(terms, 'src', 0, 0, tiled=True)]
    all_to_all x1, starting transfers between devices: 3.86 us -> 6.33 us  [body(): terms = lax.all_to_all(terms, 'src', 0, 0, tiled=True)]
    pallas_call x5, Pallas kernels: 5.73 us -> 7.71 us  [the longest x1 3.3 us: body(): pl.pallas_call(functools.partial(encode_kernel, n, pieces[0]), out_shape=...]
    unnamed x12 -> x10, local copies, waits for them, and re-layouts: 1.06 us -> 0.02 us
    ppermute x2, starting transfers between devices: 5.12 us -> 4.26 us  [the longest x1 2.23 us: body(): got += [lax.ppermute(value, 'src', pair) for value in part]]
  transfers between devices with their start and end apart: 12 -> 12, of which waited for: 7 -> 7; matrix products, arithmetic and copies ran while one was open for 0% -> 0% of each run, Pallas kernels for 3% -> 6%
where the time goes in v3:
time: 59.7 us; the launch traced here: 59.5 us
  waiting for transfers between devices  33 us (55%)
  starting transfers between devices  18.7 us (31%)
  Pallas kernels  7.71 us (13%)
    ppermute x1, waiting for transfers between devices, body(): got += [lax.ppermute(value, 'src', pair) for value in part]  10.9 us
    ppermute x6, waiting for transfers between devices, body(): sums.append(lax.ppermute(term, ('src', 'rep'), perm) if j + r else term)  9.74 us
    all_to_all x1, starting transfers between devices, body(): terms = lax.all_to_all(terms, 'src', 0, 0, tiled=True)  6.33 us
    all_to_all x1, waiting for transfers between devices, body(): terms = lax.all_to_all(terms, 'src', 0, 0, tiled=True)  6.25 us
    ppermute x6, starting transfers between devices, body(): sums.append(lax.ppermute(term, ('src', 'rep'), perm) if j + r else term)  6.21 us
    ppermute x3, waiting for transfers between devices, body(): codes.append(lax.ppermute(own, ('tgt', 'rep'), perm) if k + r else own)  3.75 us
    pallas_call x1, Pallas kernels, body(): pl.pallas_call(functools.partial(encode_kernel, n, pieces[0]), out_shape=...  3.3 us
    pallas_call x2, Pallas kernels, body(): pl.pallas_call(functools.partial(decode_kernel, n, piece, later), out_sha...  2.74 us
  transfers between devices with their start and end apart: 12, of which 7 were waited for; matrix products, arithmetic and copies ran while one was open for 0% of the time, Pallas kernels for 6%

profile of v3, /device:TPU:0, one launch (start us, length us, event | category | flops | bytes accessed | tf_op | source)
XLA Modules:
  0.0 59.5 jit_solution(6149417675042377181)
XLA Ops:
  0.0 0.0 copy-start
  0.0 0.0 copy-start.3
  0.0 0.0 copy-start.4
  0.0 3.3 %encode.1 = (bf16[4,128,256]{2,1,0:T(8,128)(2,1)}, bf16[2,2,128,512]{3,2,1,0:T(8,128)(2,1)}) custom-call(bf16[2,2,64,1024]{3,2,1,0:T(8,128)(2,1)} %bitcast.3, bf16[1024,512]{1,0:T(8,128)(2,1)} %w_hbm.1, bf16[2,2,128,2048]{3,2,1,0:T(8,128)(2,1)} %dec_hbm.5), custom_call_target="tpu_custom_call" | custom-call | tf_op jit(solution)/shard_map/encode/pallas_call | solution.py:228
  3.3 6.3 %all-to-all-start = ((bf16[4,128,256]{2,1,0:T(8,128)(2,1)}), bf16[4,128,256]{2,1,0:T(8,128)(2,1)S(1)}, u32[]{:S(2)}, u32[]{:S(2)}) async-start(bf16[4,128,256]{2,1,0:T(8,128)(2,1)} %get-tuple-element.18), calls=%async_computation | async-start | bytes 524288 | tf_op jit(solution)/shard_map/all_to_all | solution.py:245
  9.6 2.0 %collective-permute-start = (bf16[2,2,128,512]{3,2,1,0:T(8,128)(2,1)}, bf16[2,2,128,512]{3,2,1,0:T(8,128)(2,1)S(1)}, u32[]{:S(2)}, u32[]{:S(2)}) collective-permute-start(bf16[2,2,128,512]{3,2,1,0:T(8,128)(2,1)} %get-tuple-element.17), channel_id=1, source_target_pairs={{0,4},{4,0},{8,12},{12,8},{1,5},{5,1},{9,13},{13,9},{2,6},{6,2},{1... | collective-permute-start | bytes 1572872 | tf_op jit(solution)/shard_map/ppermute | solution.py:244
  11.7 6.2 %all-to-all-done.terms_ref = bf16[4,128,256]{2,1,0:T(8,128)(2,1)S(1)} async-done(((bf16[4,128,256]{2,1,0:T(8,128)(2,1)}), bf16[4,128,256]{2,1,0:T(8,128)(2,1)S(1)}, u32[]{:S(2)}, u32[]{:S(2)}) %all-to-all-start) | async-done | bytes 262176 | tf_op jit(solution)/shard_map/all_to_all | solution.py:245
  17.9 0.0 copy-done
  17.9 0.0 copy-done.3
  17.9 0.0 copy-done.4
  17.9 0.7 %codes.1 = (bf16[2,64,256]{2,1,0:T(8,128)(2,1)S(1)}, bf16[2,2,128,512]{3,2,1,0:T(8,128)(2,1)S(1)}) custom-call(s32[2,8]{1,0:T(2,128)S(1)} %copy-done.4, f32[4,128]{1,0:T(4,128)S(1)} %bitcast.2, bf16[4,128,256]{2,1,0:T(8,128)(2,1)S(1)} %all-to-all-done.terms_ref, bf16[2,2,128,2048]{3,2,1,0:T(8,128)(2,1)S(1)} %copy-done), custom_call_target="tpu_custom_call" | custom-call | tf_op jit(solution)/shard_map/codes/pallas_call | solution.py:248
  18.7 2.2 %collective-permute-start.7 = (bf16[2,2,128,512]{3,2,1,0:T(8,128)(2,1)S(1)}, bf16[2,2,128,512]{3,2,1,0:T(8,128)(2,1)S(1)}, u32[]{:S(2)}, u32[]{:S(2)}) collective-permute-start(bf16[2,2,128,512]{3,2,1,0:T(8,128)(2,1)S(1)} %get-tuple-element.24), channel_id=1, source_target_pairs={{0,4},{4,0},{8,12},{12,8},{1,5},{5,1},{9,13},{13,9},{2,6},{6,2},{1... | collective-permute-start | bytes 1572872 | tf_op jit(solution)/shard_map/ppermute | solution.py:258
  20.9 0.0 collective-permute-start.1
  20.9 1.5 %collective-permute-start.2 = (bf16[2,64,256]{2,1,0:T(8,128)(2,1)S(1)}, bf16[2,64,256]{2,1,0:T(8,128)(2,1)S(1)}, u32[]{:S(2)}, u32[]{:S(2)}) collective-permute-start(bf16[2,64,256]{2,1,0:T(8,128)(2,1)S(1)} %get-tuple-element.19.refs_0_), channel_id=1, source_target_pairs={{0,2},{1,3},{2,0},{3,1},{4,6},{5,7},{6,4},{7,5},{8,10},{9,11},{10,... | collective-permute-start | bytes 196616 | tf_op jit(solution)/shard_map/ppermute | solution.py:265
  22.4 0.4 collective-permute-start.3
  22.8 0.0 collective-permute-done.1.refs_1_
  22.8 2.7 %collective-permute-done.2.refs_2_ = bf16[2,64,256]{2,1,0:T(8,128)(2,1)S(1)} collective-permute-done((bf16[2,64,256]{2,1,0:T(8,128)(2,1)S(1)}, bf16[2,64,256]{2,1,0:T(8,128)(2,1)S(1)}, u32[]{:S(2)}, u32[]{:S(2)}) %collective-permute-start.2) | collective-permute-done | bytes 65568 | tf_op jit(solution)/shard_map/ppermute | solution.py:265
  25.5 1.1 %collective-permute-done.3.refs_3_ = bf16[2,64,256]{2,1,0:T(8,128)(2,1)S(1)} collective-permute-done((bf16[2,64,256]{2,1,0:T(8,128)(2,1)S(1)}, bf16[2,64,256]{2,1,0:T(8,128)(2,1)S(1)}, u32[]{:S(2)}, u32[]{:S(2)}) %collective-permute-start.3) | collective-permute-done | bytes 65568 | tf_op jit(solution)/shard_map/ppermute | solution.py:265
  26.5 2.4 %collective-permute-done.got_hbm = bf16[2,2,128,512]{3,2,1,0:T(8,128)(2,1)S(1)} collective-permute-done((bf16[2,2,128,512]{3,2,1,0:T(8,128)(2,1)}, bf16[2,2,128,512]{3,2,1,0:T(8,128)(2,1)S(1)}, u32[]{:S(2)}, u32[]{:S(2)}) %collective-permute-start) | collective-permute-done | bytes 524320 | tf_op jit(solution)/shard_map/ppermute | solution.py:244
  28.9 1.4 %decode.2 = (f32[2,64,512]{2,1,0:T(8,128)S(1)}, bf16[2,64,512]{2,1,0:T(8,128)(2,1)S(1)}, bf16[2,64,512]{2,1,0:T(8,128)(2,1)S(1)}, bf16[2,64,512]{2,1,0:T(8,128)(2,1)S(1)}) custom-call(bf16[2,2,128,2048]{3,2,1,0:T(8,128)(2,1)S(1)} %copy-done, bf16[2,2,128,512]{3,2,1,0:T(8,128)(2,1)S(1)} %collective-permute-done.got_hbm, ...), custom_call_target="tpu_custom_call" | custom-call | tf_op jit(solution)/shard_map/decode/pallas_call | solution.py:274
  30.3 0.0 copy-start.1
  30.3 0.0 copy-start.2
  30.3 2.5 %collective-permute-start.4 = (bf16[2,64,512]{2,1,0:T(8,128)(2,1)S(1)}, bf16[2,64,512]{2,1,0:T(8,128)(2,1)S(1)}, u32[]{:S(2)}, u32[]{:S(2)}) collective-permute-start(bf16[2,64,512]{2,1,0:T(8,128)(2,1)S(1)} %get-tuple-element.21), channel_id=1, source_target_pairs={{0,8},{1,9},{4,12},{5,13},{8,0},{9,1},{12,4},{13,5},{2,10},{3,11},... | collective-permute-start | bytes 393224 | tf_op jit(solution)/shard_map/ppermute | solution.py:298
  32.8 0.0 collective-permute-start.5
  32.8 0.6 %collective-permute-start.6 = (bf16[2,64,512]{2,1,0:T(8,128)(2,1)S(1)}, bf16[2,64,512]{2,1,0:T(8,128)(2,1)S(1)}, u32[]{:S(2)}, u32[]{:S(2)}) collective-permute-start(bf16[2,64,512]{2,1,0:T(8,128)(2,1)S(1)} %get-tuple-element.23), channel_id=1, source_target_pairs={{0,9},{1,8},{4,13},{5,12},{8,1},{9,0},{12,5},{13,4},{2,11},{3,10},... | collective-permute-start | bytes 393224 | tf_op jit(solution)/shard_map/ppermute | solution.py:298
  33.4 10.9 %collective-permute-done.7.got_hbm = bf16[2,2,128,512]{3,2,1,0:T(8,128)(2,1)S(1)} collective-permute-done((bf16[2,2,128,512]{3,2,1,0:T(8,128)(2,1)S(1)}, bf16[2,2,128,512]{3,2,1,0:T(8,128)(2,1)S(1)}, u32[]{:S(2)}, u32[]{:S(2)}) %collective-permute-start.7) | collective-permute-done | bytes 524320 | tf_op jit(solution)/shard_map/ppermute | solution.py:258
  44.3 1.4 %decode.3 = (f32[2,64,512]{2,1,0:T(8,128)S(1)}, bf16[2,64,512]{2,1,0:T(8,128)(2,1)S(1)}, bf16[2,64,512]{2,1,0:T(8,128)(2,1)S(1)}, bf16[2,64,512]{2,1,0:T(8,128)(2,1)S(1)}) custom-call(bf16[2,2,128,2048]{3,2,1,0:T(8,128)(2,1)S(1)} %copy-done, bf16[2,2,128,512]{3,2,1,0:T(8,128)(2,1)S(1)} %collective-permute-done.7.got_hbm, ...), custom_call_target="tpu_custom_call" | custom-call | tf_op jit(solution)/shard_map/decode/pallas_call | solution.py:274
  45.7 0.5 collective-permute-start.8
  46.2 0.0 collective-permute-start.9
  46.2 0.0 collective-permute-done.4.refs_1_
  46.2 2.6 %collective-permute-start.10 = (bf16[2,64,512]{2,1,0:T(8,128)(2,1)S(1)}, bf16[2,64,512]{2,1,0:T(8,128)(2,1)S(1)}, u32[]{:S(2)}, u32[]{:S(2)}) collective-permute-start(bf16[2,64,512]{2,1,0:T(8,128)(2,1)S(1)} %get-tuple-element.28), channel_id=1, source_target_pairs={{0,9},{1,8},{4,13},{5,12},{8,1},{9,0},{12,5},{13,4},{2,11},{3,10},... | collective-permute-start | bytes 393224 | tf_op jit(solution)/shard_map/ppermute | solution.py:298
  48.8 0.0 collective-permute-done.5.refs_2_
  48.8 0.0 collective-permute-done.6.refs_3_
  48.8 8.1 %collective-permute-done.8.refs_5_ = bf16[2,64,512]{2,1,0:T(8,128)(2,1)S(1)} collective-permute-done((bf16[2,64,512]{2,1,0:T(8,128)(2,1)S(1)}, bf16[2,64,512]{2,1,0:T(8,128)(2,1)S(1)}, u32[]{:S(2)}, u32[]{:S(2)}) %collective-permute-start.8) | collective-permute-done | bytes 131104 | tf_op jit(solution)/shard_map/ppermute | solution.py:298
  56.9 0.0 collective-permute-done.9.refs_6_
  56.9 1.6 %collective-permute-done.10.refs_7_ = bf16[2,64,512]{2,1,0:T(8,128)(2,1)S(1)} collective-permute-done((bf16[2,64,512]{2,1,0:T(8,128)(2,1)S(1)}, bf16[2,64,512]{2,1,0:T(8,128)(2,1)S(1)}, u32[]{:S(2)}, u32[]{:S(2)}) %collective-permute-start.10) | collective-permute-done | bytes 131104 | tf_op jit(solution)/shard_map/ppermute | solution.py:298
  58.5 0.0 copy-done.1
  58.5 0.0 copy-done.2
  58.5 0.9 %add.1 = bf16[2,64,2048]{2,1,0:T(8,128)(2,1)} custom-call(f32[2,2048]{1,0:T(2,128)S(1)} %copy-done.2, bf16[2,64,2048]{2,1,0:T(8,128)(2,1)S(1)} %copy-done.1, f32[2,64,512]{2,1,0:T(8,128)S(1)} %get-tuple-element.20.refs_4_.refs_0_, bf16[2,64,512]{2,1,0:T(8,128)(2,1)S(1)} %collective-permute-done.4.refs_1_, ...), custom_call_target="tpu_custom_call" | custom-call | tf_op jit(solution)/shard_map/add/pallas_call | solution.py:300
Async XLA Ops:
  0.0 17.9 %copy-start = (bf16[2,2,128,2048]{3,2,1,0:T(8,128)(2,1)S(1)}, bf16[2,2,128,2048]{3,2,1,0:T(8,128)(2,1)}, u32[]{:S(2)}) copy-start(bf16[2,2,128,2048]{3,2,1,0:T(8,128)(2,1)} %dec_hbm.5) | copy-start | bytes 6291460
  0.0 17.9 %copy-start.3 = (f32[512]{0:T(512)S(1)}, f32[512]{0:T(512)}, u32[]{:S(2)}) copy-start(f32[512]{0:T(512)} %param.9) | copy-start | bytes 6148
  0.0 17.9 %copy-start.4 = (s32[2,8]{1,0:T(2,128)S(1)}, s32[2,8]{1,0:T(2,128)}, u32[]{:S(2)}) copy-start(s32[2,8]{1,0:T(2,128)} %active_ref.1) | copy-start | bytes 196
  3.3 14.6 %all-to-all-start = ((bf16[4,128,256]{2,1,0:T(8,128)(2,1)}), bf16[4,128,256]{2,1,0:T(8,128)(2,1)S(1)}, u32[]{:S(2)}, u32[]{:S(2)}) async-start(bf16[4,128,256]{2,1,0:T(8,128)(2,1)} %get-tuple-element.18), calls=%async_computation | async-start | bytes 524288 | tf_op jit(solution)/shard_map/all_to_all | solution.py:245
  9.6 19.3 %collective-permute-start = (bf16[2,2,128,512]{3,2,1,0:T(8,128)(2,1)}, bf16[2,2,128,512]{3,2,1,0:T(8,128)(2,1)S(1)}, u32[]{:S(2)}, u32[]{:S(2)}) collective-permute-start(bf16[2,2,128,512]{3,2,1,0:T(8,128)(2,1)} %get-tuple-element.17), channel_id=1, source_target_pairs={{0,4},{4,0},{8,12},{12,8},{1,5},{5,1},{9,13},{13,9},{2,6},{6,2},{1... | collective-permute-start | bytes 1572872 | tf_op jit(solution)/shard_map/ppermute | solution.py:244
  18.7 25.6 %collective-permute-start.7 = (bf16[2,2,128,512]{3,2,1,0:T(8,128)(2,1)S(1)}, bf16[2,2,128,512]{3,2,1,0:T(8,128)(2,1)S(1)}, u32[]{:S(2)}, u32[]{:S(2)}) collective-permute-start(bf16[2,2,128,512]{3,2,1,0:T(8,128)(2,1)S(1)} %get-tuple-element.24), channel_id=1, source_target_pairs={{0,4},{4,0},{8,12},{12,8},{1,5},{5,1},{9,13},{13,9},{2,6},{6,2},{1... | collective-permute-start | bytes 1572872 | tf_op jit(solution)/shard_map/ppermute | solution.py:258
  20.9 1.9 %collective-permute-start.1 = (bf16[2,64,256]{2,1,0:T(8,128)(2,1)S(1)}, bf16[2,64,256]{2,1,0:T(8,128)(2,1)S(1)}, u32[]{:S(2)}, u32[]{:S(2)}) collective-permute-start(bf16[2,64,256]{2,1,0:T(8,128)(2,1)S(1)} %get-tuple-element.19.refs_0_), channel_id=1, source_target_pairs={{0,1},{1,0},{2,3},{3,2},{4,5},{5,4},{6,7},{7,6},{8,9},{9,8},{10,11... | collective-permute-start | bytes 196616 | tf_op jit(solution)/shard_map/ppermute | solution.py:265
  20.9 4.5 %collective-permute-start.2 = (bf16[2,64,256]{2,1,0:T(8,128)(2,1)S(1)}, bf16[2,64,256]{2,1,0:T(8,128)(2,1)S(1)}, u32[]{:S(2)}, u32[]{:S(2)}) collective-permute-start(bf16[2,64,256]{2,1,0:T(8,128)(2,1)S(1)} %get-tuple-element.19.refs_0_), channel_id=1, source_target_pairs={{0,2},{1,3},{2,0},{3,1},{4,6},{5,7},{6,4},{7,5},{8,10},{9,11},{10,... | collective-permute-start | bytes 196616 | tf_op jit(solution)/shard_map/ppermute | solution.py:265
  22.4 4.1 %collective-permute-start.3 = (bf16[2,64,256]{2,1,0:T(8,128)(2,1)S(1)}, bf16[2,64,256]{2,1,0:T(8,128)(2,1)S(1)}, u32[]{:S(2)}, u32[]{:S(2)}) collective-permute-start(bf16[2,64,256]{2,1,0:T(8,128)(2,1)S(1)} %get-tuple-element.19.refs_0_), channel_id=1, source_target_pairs={{0,3},{1,2},{2,1},{3,0},{4,7},{5,6},{6,5},{7,4},{8,11},{9,10},{10,... | collective-permute-start | bytes 196616 | tf_op jit(solution)/shard_map/ppermute | solution.py:265
  30.3 28.2 %copy-start.1 = (bf16[2,64,2048]{2,1,0:T(8,128)(2,1)S(1)}, bf16[2,64,2048]{2,1,0:T(8,128)(2,1)}, u32[]{:S(2)}) copy-start(bf16[2,64,2048]{2,1,0:T(8,128)(2,1)} %target_ref.1) | copy-start | bytes 1572868
  30.3 28.2 %copy-start.2 = (f32[2,2048]{1,0:T(2,128)S(1)}, f32[2,2048]{1,0:T(2,128)}, u32[]{:S(2)}) copy-start(f32[2,2048]{1,0:T(2,128)} %bias_ref.1) | copy-start | bytes 49156
  30.3 15.9 %collective-permute-start.4 = (bf16[2,64,512]{2,1,0:T(8,128)(2,1)S(1)}, bf16[2,64,512]{2,1,0:T(8,128)(2,1)S(1)}, u32[]{:S(2)}, u32[]{:S(2)}) collective-permute-start(bf16[2,64,512]{2,1,0:T(8,128)(2,1)S(1)} %get-tuple-element.21), channel_id=1, source_target_pairs={{0,8},{1,9},{4,12},{5,13},{8,0},{9,1},{12,4},{13,5},{2,10},{3,11},... | collective-permute-start | bytes 393224 | tf_op jit(solution)/shard_map/ppermute | solution.py:298
  32.8 16.0 %collective-permute-start.5 = (bf16[2,64,512]{2,1,0:T(8,128)(2,1)S(1)}, bf16[2,64,512]{2,1,0:T(8,128)(2,1)S(1)}, u32[]{:S(2)}, u32[]{:S(2)}) collective-permute-start(bf16[2,64,512]{2,1,0:T(8,128)(2,1)S(1)} %get-tuple-element.22), channel_id=1, source_target_pairs={{0,1},{1,0},{4,5},{5,4},{8,9},{9,8},{12,13},{13,12},{2,3},{3,2},{6... | collective-permute-start | bytes 393224 | tf_op jit(solution)/shard_map/ppermute | solution.py:298
  32.8 16.0 %collective-permute-start.6 = (bf16[2,64,512]{2,1,0:T(8,128)(2,1)S(1)}, bf16[2,64,512]{2,1,0:T(8,128)(2,1)S(1)}, u32[]{:S(2)}, u32[]{:S(2)}) collective-permute-start(bf16[2,64,512]{2,1,0:T(8,128)(2,1)S(1)} %get-tuple-element.23), channel_id=1, source_target_pairs={{0,9},{1,8},{4,13},{5,12},{8,1},{9,0},{12,5},{13,4},{2,11},{3,10},... | collective-permute-start | bytes 393224 | tf_op jit(solution)/shard_map/ppermute | solution.py:298
  45.7 11.2 %collective-permute-start.8 = (bf16[2,64,512]{2,1,0:T(8,128)(2,1)S(1)}, bf16[2,64,512]{2,1,0:T(8,128)(2,1)S(1)}, u32[]{:S(2)}, u32[]{:S(2)}) collective-permute-start(bf16[2,64,512]{2,1,0:T(8,128)(2,1)S(1)} %get-tuple-element.26), channel_id=1, source_target_pairs={{0,8},{1,9},{4,12},{5,13},{8,0},{9,1},{12,4},{13,5},{2,10},{3,11},... | collective-permute-start | bytes 393224 | tf_op jit(solution)/shard_map/ppermute | solution.py:298
  46.2 10.7 %collective-permute-start.9 = (bf16[2,64,512]{2,1,0:T(8,128)(2,1)S(1)}, bf16[2,64,512]{2,1,0:T(8,128)(2,1)S(1)}, u32[]{:S(2)}, u32[]{:S(2)}) collective-permute-start(bf16[2,64,512]{2,1,0:T(8,128)(2,1)S(1)} %get-tuple-element.27), channel_id=1, source_target_pairs={{0,1},{1,0},{4,5},{5,4},{8,9},{9,8},{12,13},{13,12},{2,3},{3,2},{6... | collective-permute-start | bytes 393224 | tf_op jit(solution)/shard_map/ppermute | solution.py:298
  46.2 12.3 %collective-permute-start.10 = (bf16[2,64,512]{2,1,0:T(8,128)(2,1)S(1)}, bf16[2,64,512]{2,1,0:T(8,128)(2,1)S(1)}, u32[]{:S(2)}, u32[]{:S(2)}) collective-permute-start(bf16[2,64,512]{2,1,0:T(8,128)(2,1)S(1)} %get-tuple-element.28), channel_id=1, source_target_pairs={{0,9},{1,8},{4,13},{5,12},{8,1},{9,0},{12,5},{13,4},{2,11},{3,10},... | collective-permute-start | bytes 393224 | tf_op jit(solution)/shard_map/ppermute | solution.py:298

commit v4 on v3

v4 whole, which is shorter than its diff:
```python
import functools

import jax
import jax.numpy as jnp
from jax import lax
from jax.experimental import pallas as pl
from jax.experimental.pallas import tpu as pltpu
from jax.sharding import PartitionSpec as P

VMEM_BYTES = 32 * 1024 * 1024
LANES = 128
SHARES = (4, 4)


def cut_columns(columns):
    tiles = columns // LANES
    pieces, start = [], 0
    for i, eighths in enumerate(SHARES):
        stop = min(tiles, start + -(-tiles * eighths // 8))
        stop = tiles if i == len(SHARES) - 1 else stop
        if stop > start:
            pieces.append((start * LANES, (stop - start) * LANES))
        start = stop
    return pieces


def part_copies(piece, dec_hbm, part_ref, sems):
    layers, groups, _, cols = dec_hbm.shape
    start = pl.multiple_of(lax.axis_index("rep") * (cols // 2) + piece[0], LANES)
    copies = []
    for layer in range(layers):
        for group in range(groups):
            source = dec_hbm.at[layer, group, :, pl.ds(start, piece[1])]
            copies.append(
                pltpu.make_async_copy(
                    source, part_ref.at[layer, group], sems.at[layer * groups + group]
                )
            )
            copies[-1].start()
    return copies


def encode_kernel(n, pieces, acts_hbm, w_hbm, dec_hbm, *refs):
    term_refs, part_refs, refs = refs[:n], refs[n : n + len(pieces)], refs[n + len(pieces) :]
    acts_ref, w_ref, part_sems, acts_sems, w_sems = refs
    half = n // 2
    width = w_ref.shape[1] // half
    depth = w_ref.shape[0] // 8
    copies = []
    for i in range(2):
        for j in range(half):
            copies.append(
                pltpu.make_async_copy(
                    acts_hbm.at[j, i], acts_ref.at[i, j], acts_sems.at[i * half + j]
                )
            )
    for i in range(8):
        rows = slice(i * depth, (i + 1) * depth)
        copies.append(pltpu.make_async_copy(w_hbm.at[rows], w_ref.at[rows], w_sems.at[i]))
    for copy in copies:
        copy.start()
    for copy in copies:
        copy.wait()
    copies_part = []
    for i, piece in enumerate(pieces):
        copies_part += part_copies(piece, dec_hbm, part_refs[i], part_sems.at[i])
    src = lax.axis_index("src")
    for k in range(n):
        dest = lax.rem(src + k, n)
        rows = acts_ref[lax.rem(dest, 2)]
        rows = rows.reshape(rows.shape[0] * rows.shape[1], rows.shape[2])
        columns = pl.ds(pl.multiple_of((dest // 2) * width, width), width)
        term_refs[k][...] = jnp.dot(
            rows, w_ref[:, columns], preferred_element_type=jnp.float32
        ).astype(jnp.bfloat16)
    for copy in copies_part:
        copy.wait()


def codes_kernel(n, share, tile_rows, active_ref, bias_ref, *refs):
    term_refs, out_ref = refs[:n], refs[n + (len(refs) - n - 1) // 2]
    src = lax.axis_index("src")
    tgt = lax.axis_index("tgt")
    parity, half = lax.rem(src, 2), src // 2
    block = out_ref.shape[2] // 2
    pre = term_refs[0][...].astype(jnp.float32)
    for ref in term_refs[1:]:
        pre = pre + ref[...].astype(jnp.float32)
    tiles, slots = active_ref.shape
    for piece in range(2):
        columns = slice(piece * block, (piece + 1) * block)
        bias = bias_ref[pl.ds(half * 2 + piece, 1), :]
        wanted = tgt * n + half * 2 + piece
        flags = []
        for tile in range(tiles):
            flags.append(
                lax.fori_loop(
                    0,
                    slots,
                    lambda i, total: total + (active_ref[tile, i] == wanted).astype(jnp.int32),
                    jnp.int32(0),
                    unroll=slots <= 16,
                )
            )
        for group in range(n // 2):
            tile = ((group * 2 + parity) * share) // tile_rows
            flag = flags[0]
            for i in range(1, tiles):
                flag = jnp.where(tile == i, flags[i], flag)
            live = jnp.where(flag > 0, 1.0, 0.0).astype(jnp.float32)
            rows = slice(group * share, (group + 1) * share)
            value = live * jnp.maximum(pre[rows, columns] + bias, 0.0)
            out_ref[group, :, columns] = value.astype(jnp.bfloat16)


def decode_kernel(n, own_ref, got_ref, *refs):
    half = n // 2
    layers, groups, block, width = own_ref.shape
    code_refs, out_refs, lhs_ref = refs[: 2 * groups], refs[-2 * half - 1 : -1], refs[-1]
    src, tgt = lax.axis_index("src"), lax.axis_index("tgt")
    parity = lax.rem(src, 2)
    share = code_refs[0].shape[1]
    depth = groups * block
    for k in range(groups):
        place = lax.rem(tgt - k + groups, groups)
        for side in range(2):
            latents = parity if side == 0 else 1 - parity
            latents = pl.ds(pl.multiple_of(latents * block, block), block)
            columns = pl.ds(pl.multiple_of((side * groups + place) * block, block), block)
            for j in range(half):
                group = lax.rem(src // 2 + j, half)
                for r in range(2):
                    rows = slice((2 * j + r) * share, (2 * j + r + 1) * share)
                    lhs_ref[rows, columns] = code_refs[2 * k + r][group, :, latents]
    for layer in range(layers):
        own = own_ref[layer].reshape(depth, width)
        got = got_ref[layer].reshape(depth, width)
        total = jnp.dot(lhs_ref[:, :depth], own, preferred_element_type=jnp.float32)
        total += jnp.dot(lhs_ref[:, depth:], got, preferred_element_type=jnp.float32)
        for i, ref in enumerate(out_refs):
            ref[layer] = total[i * share : (i + 1) * share].astype(ref.dtype)


def add_kernel(n, pieces, bias_ref, target_ref, *refs):
    out_hbm, out_ref, sems = refs[-3:]
    half = n // 2
    layers, _, cols = target_ref.shape
    rep = lax.axis_index("rep")
    copies = []
    for i, (first, width) in enumerate(pieces):
        for side in range(2):
            core = rep if side == 0 else 1 - rep
            columns = pl.ds(pl.multiple_of(core * (cols // 2) + first, LANES), width)
            mine = refs[(2 * i + side) * half : (2 * i + side + 1) * half]
            for layer in range(layers):
                total = bias_ref[layer : layer + 1, columns]
                total = total - target_ref[layer, :, columns].astype(jnp.float32)
                for ref in mine:
                    total = total + ref[layer].astype(jnp.float32)
                out_ref[layer, :, columns] = total.astype(jnp.bfloat16)
                copies.append(
                    pltpu.make_async_copy(
                        out_ref.at[layer, :, columns],
                        out_hbm.at[layer, :, columns],
                        sems.at[(2 * i + side) * layers + layer],
                    )
                )
                copies[-1].start()
    for copy in copies:
        copy.wait()


def body(acts, enc_w, enc_b, dec_w, dec_b, targets, active):
    n = lax.axis_size("src")
    rows, features = acts.shape
    layers, groups, block, cols = dec_w.shape
    share = rows // n
    half = n // 2
    pieces = cut_columns(cols // 2)
    tile_rows = rows // active.shape[0]
    pair = [(i, i ^ 1) for i in range(n)]
    params = pltpu.CompilerParams(vmem_limit_bytes=VMEM_BYTES)
    vmem = pl.BlockSpec(memory_space=pltpu.VMEM)
    smem = pl.BlockSpec(memory_space=pltpu.SMEM)
    anywhere = pl.BlockSpec(memory_space=pl.ANY)
    cost = pl.CostEstimate(flops=0, bytes_accessed=0, transcendentals=0)

    acts, enc_w, dec_w = (
        pltpu.with_memory_space_constraint(value, pltpu.HBM)
        for value in (acts.reshape(half, 2, share, features), enc_w, dec_w)
    )

    def shape(*extent, kind=jnp.bfloat16):
        return jax.ShapeDtypeStruct(extent, kind)

    results = pl.pallas_call(
        functools.partial(encode_kernel, n, pieces),
        out_shape=[shape(half * share, 2 * block)] * n
        + [shape(layers, groups, block, width) for _, width in pieces],
        in_specs=[anywhere] * 3,
        out_specs=[vmem] * (n + len(pieces)),
        scratch_shapes=[
            pltpu.VMEM((2, half, share, features), jnp.bfloat16),
            pltpu.VMEM(enc_w.shape, jnp.bfloat16),
            pltpu.SemaphoreType.DMA((len(pieces), layers * groups)),
            pltpu.SemaphoreType.DMA((2 * half,)),
            pltpu.SemaphoreType.DMA((8,)),
        ],
        compiler_params=params,
        cost_estimate=cost,
        name="encode",
    )(acts, enc_w, dec_w)
    terms, parts = list(results[:n]), results[n:]
    for k in range(1, n):
        terms[k] = lax.ppermute(terms[k], "src", [(i, (i + k) % n) for i in range(n)])
    own, *late = pl.pallas_call(
        functools.partial(codes_kernel, n, share, tile_rows),
        out_shape=[shape(half, share, 2 * block)]
        + [jax.ShapeDtypeStruct(part.shape, part.dtype) for part in parts[1:]],
        in_specs=[smem] + [vmem] * (1 + n) + [anywhere] * (len(parts) - 1),
        out_specs=[vmem] + [anywhere] * (len(parts) - 1),
        input_output_aliases={2 + n + i: 1 + i for i in range(len(parts) - 1)},
        compiler_params=params,
        cost_estimate=cost,
        name="codes",
    )(active, enc_b.reshape(n, block), *terms, *parts[1:])
    parts = [parts[0], *late]
    got = [lax.ppermute(part, "src", pair) for part in parts]
    codes = []
    for k in range(groups):
        for r in range(2):
            perm = [
                (i * 2 + c, (i + k) % groups * 2 + (c ^ r)) for i in range(groups) for c in range(2)
            ]
            codes.append(lax.ppermute(own, ("tgt", "rep"), perm) if k + r else own)

    sums, after = [], []
    for i, piece in enumerate(pieces):
        shapes = [shape(layers, share, piece[1])] * (2 * half)
        shapes[0] = shape(layers, share, piece[1], kind=jnp.float32)
        terms = pl.pallas_call(
            functools.partial(decode_kernel, n),
            out_shape=shapes,
            in_specs=[vmem] * (2 + 2 * groups) + [anywhere] * len(after),
            out_specs=[vmem] * len(shapes),
            scratch_shapes=[pltpu.VMEM((rows, 2 * groups * block), jnp.bfloat16)],
            compiler_params=params,
            cost_estimate=cost,
            name="decode",
        )(parts[i], got[i], *codes, *after)
        after = [terms[0]]
        for r in range(2):
            for j in range(half):
                perm = [
                    (d * 2 + c, (d + 2 * j) % n * 2 + (c ^ r)) for d in range(n) for c in range(2)
                ]
                term = terms[2 * j + r]
                sums.append(lax.ppermute(term, ("src", "rep"), perm) if j + r else term)

    return pl.pallas_call(
        functools.partial(add_kernel, n, pieces),
        out_shape=shape(layers, share, cols),
        in_specs=[vmem] * (2 + len(sums)),
        out_specs=anywhere,
        scratch_shapes=[
            pltpu.VMEM((layers, share, cols), jnp.bfloat16),
            pltpu.SemaphoreType.DMA((2 * len(pieces) * layers,)),
        ],
        compiler_params=params,
        cost_estimate=cost,
        name="add",
    )(dec_b, targets, *sums)


def solution(mesh):
    in_specs = (
        P(("parts", "rep"), "src"),
        P("src", "tgt"),
        P("tgt"),
        P(None, None, "src", "tgt"),
        P(None, "tgt"),
        P(None, ("parts", "rep", "src"), "tgt"),
        P(("parts", "rep"), None),
    )
    out_specs = P(None, ("parts", "rep", "src"), "tgt")
    return jax.shard_map(body, mesh=mesh, in_specs=in_specs, out_specs=out_specs, check_vma=False)
```

time: 59.7 us -> 58.4 us (0.978)
  Pallas kernels: 7.71 us -> 5.74 us
  starting transfers between devices: 18.7 us -> 19.4 us
    all_to_all x1 -> x0, starting transfers between devices: 6.33 us -> none  [body(): terms = lax.all_to_all(terms, 'src', 0, 0, tiled=True)]
    all_to_all x1 -> x0, waiting for transfers between devices: 6.25 us -> none  [body(): terms = lax.all_to_all(terms, 'src', 0, 0, tiled=True)]
    ppermute x6, waiting for transfers between devices: 9.74 us -> 16 us  [body(): sums.append(lax.ppermute(term, ('src', 'rep'), perm) if j + r else term)]
    ppermute x2 -> x5, starting transfers between devices: 4.26 us -> 10.2 us  [the longest x3 5.51 us: body(): lax.ppermute(terms[k], 'src', [(i, (i + k) % n) for i in range(n)])]
    pallas_call x4, Pallas kernels: 6.78 us -> 4.81 us  [the longest x1 3.25 us: body(): pl.pallas_call(functools.partial(encode_kernel, n, pieces), out_shape=[sh...]
    ppermute x6, starting transfers between devices: 6.21 us -> 7.33 us  [body(): sums.append(lax.ppermute(term, ('src', 'rep'), perm) if j + r else term)]
    ppermute x2 -> x5, waiting for transfers between devices: 13.3 us -> 13.3 us  [the longest x3 11.1 us: body(): lax.ppermute(terms[k], 'src', [(i, (i + k) % n) for i in range(n)])]
  transfers between devices with their start and end apart: 12 -> 14, of which waited for: 7 -> 8; matrix products, arithmetic and copies ran while one was open for 0% -> 0% of each run, Pallas kernels for 6% -> 3%
where the time goes in v4:
time: 58.4 us; the launch traced here: 58.3 us
  waiting for transfers between devices  33.1 us (57%)
  starting transfers between devices  19.4 us (33%)
  Pallas kernels  5.74 us (10%)
    ppermute x6, waiting for transfers between devices, body(): sums.append(lax.ppermute(term, ('src', 'rep'), perm) if j + r else term)  16 us
    ppermute x3, waiting for transfers between devices, body(): lax.ppermute(terms[k], 'src', [(i, (i + k) % n) for i in range(n)])  11.1 us
    ppermute x6, starting transfers between devices, body(): sums.append(lax.ppermute(term, ('src', 'rep'), perm) if j + r else term)  7.33 us
    ppermute x3, starting transfers between devices, body(): lax.ppermute(terms[k], 'src', [(i, (i + k) % n) for i in range(n)])  5.51 us
    ppermute x2, starting transfers between devices, body(): got = [lax.ppermute(part, 'src', pair) for part in parts]  4.67 us
    ppermute x3, waiting for transfers between devices, body(): codes.append(lax.ppermute(own, ('tgt', 'rep'), perm) if k + r else own)  3.76 us
    pallas_call x1, Pallas kernels, body(): pl.pallas_call(functools.partial(encode_kernel, n, pieces), out_shape=[sh...  3.25 us
    ppermute x2, waiting for transfers between devices, body(): got = [lax.ppermute(part, 'src', pair) for part in parts]  2.2 us
  transfers between devices with their start and end apart: 14, of which 8 were waited for; matrix products, arithmetic and copies ran while one was open for 0% of the time, Pallas kernels for 3%

profile of v4, /device:TPU:0, one launch (start us, length us, event | category | flops | bytes accessed | tf_op | source)
XLA Modules:
  0.0 58.3 jit_solution(6834003482279712996)
XLA Ops:
  0.0 0.0 copy-start.3
  0.0 0.0 copy-start.2
  0.0 3.3 %encode.1 = (bf16[128,256]{1,0:T(8,128)(2,1)S(1)}, bf16[128,256]{1,0:T(8,128)(2,1)S(1)}, bf16[128,256]{1,0:T(8,128)(2,1)S(1)}, bf16[128,256]{1,0:T(8,128)(2,1)S(...) custom-call(bf16[2,2,64,1024]{3,2,1,0:T(8,128)(2,1)} %bitcast.3, bf16[1024,512]{1,0:T(8,128)(2,1)} %w_hbm.1, ...), custom_call_target="tpu_custom_call" | custom-call | tf_op jit(solution)/shard_map/encode/pallas_call | solution.py:196
  3.3 0.0 copy-start
  3.3 0.0 copy-start.1
  3.3 3.1 %collective-permute-start = (bf16[2,2,128,512]{3,2,1,0:T(8,128)(2,1)S(1)}, bf16[2,2,128,512]{3,2,1,0:T(8,128)(2,1)S(1)}, u32[]{:S(2)}, u32[]{:S(2)}) collective-permute-start(bf16[2,2,128,512]{3,2,1,0:T(8,128)(2,1)S(1)} %get-tuple-element.21.own_ref), channel_id=1, source_target_pairs={{0,4},{4,0},{8,12},{12,8},{1,5},{5,1},{9,13},{13,9},{2,6},{6,2},{1... | collective-permute-start | bytes 1572872 | tf_op jit(solution)/shard_map/ppermute | solution.py:228
  6.4 0.1 collective-permute-start.1
  6.4 3.0 %collective-permute-start.2 = (bf16[128,256]{1,0:T(8,128)(2,1)S(1)}, bf16[128,256]{1,0:T(8,128)(2,1)S(1)}, u32[]{:S(2)}, u32[]{:S(2)}) collective-permute-start(bf16[128,256]{1,0:T(8,128)(2,1)S(1)} %get-tuple-element.24), channel_id=1, source_target_pairs={{0,8},{4,12},{8,0},{12,4},{1,9},{5,13},{9,1},{13,5},{2,10},{6,14},... | collective-permute-start | bytes 196616 | tf_op jit(solution)/shard_map/ppermute | solution.py:215
  9.4 2.5 %collective-permute-start.3 = (bf16[128,256]{1,0:T(8,128)(2,1)S(1)}, bf16[128,256]{1,0:T(8,128)(2,1)S(1)}, u32[]{:S(2)}, u32[]{:S(2)}) collective-permute-start(bf16[128,256]{1,0:T(8,128)(2,1)S(1)} %get-tuple-element.25), channel_id=1, source_target_pairs={{0,12},{4,0},{8,4},{12,8},{1,13},{5,1},{9,5},{13,9},{2,14},{6,2},{... | collective-permute-start | bytes 196616 | tf_op jit(solution)/shard_map/ppermute | solution.py:215
  11.9 11.1 %collective-permute-done.1.refs_1_ = bf16[128,256]{1,0:T(8,128)(2,1)S(1)} collective-permute-done((bf16[128,256]{1,0:T(8,128)(2,1)S(1)}, bf16[128,256]{1,0:T(8,128)(2,1)S(1)}, u32[]{:S(2)}, u32[]{:S(2)}) %collective-permute-start.1) | collective-permute-done | bytes 65568 | tf_op jit(solution)/shard_map/ppermute | solution.py:215
  23.0 0.0 collective-permute-done.2.refs_2_
  23.0 0.0 collective-permute-done.3.refs_3_
  23.0 0.0 copy-done.3
  23.0 0.0 copy-done.2
  23.0 0.6 %codes.1 = (bf16[2,64,256]{2,1,0:T(8,128)(2,1)S(1)}, bf16[2,2,128,512]{3,2,1,0:T(8,128)(2,1)S(1)}) custom-call(s32[2,8]{1,0:T(2,128)S(1)} %copy-done.3, f32[4,128]{1,0:T(4,128)S(1)} %bitcast.2, bf16[128,256]{1,0:T(8,128)(2,1)S(1)} %get-tuple-element.22.refs_0_, bf16[128,256]{1,0:T(8,128)(2,1)S(1)} %collective-permute-done.1.refs_1_, ...), custom_call_target="tpu_custom_call", output_to_operand_aliasing={{1}: (6, {})} | custom-call | tf_op jit(solution)/shard_map/codes/pallas_call | solution.py:216
  23.7 1.6 %collective-permute-start.10 = (bf16[2,2,128,512]{3,2,1,0:T(8,128)(2,1)S(1)}, bf16[2,2,128,512]{3,2,1,0:T(8,128)(2,1)S(1)}, u32[]{:S(2)}, u32[]{:S(2)}) collective-permute-start(bf16[2,2,128,512]{3,2,1,0:T(8,128)(2,1)S(1)} %get-tuple-element.32.own_ref), channel_id=1, source_target_pairs={{0,4},{4,0},{8,12},{12,8},{1,5},{5,1},{9,13},{13,9},{2,6},{6,2},{1... | collective-permute-start | bytes 1572872 | tf_op jit(solution)/shard_map/ppermute | solution.py:228
  25.3 0.0 collective-permute-start.4
  25.3 1.5 %collective-permute-start.5 = (bf16[2,64,256]{2,1,0:T(8,128)(2,1)S(1)}, bf16[2,64,256]{2,1,0:T(8,128)(2,1)S(1)}, u32[]{:S(2)}, u32[]{:S(2)}) collective-permute-start(bf16[2,64,256]{2,1,0:T(8,128)(2,1)S(1)} %get-tuple-element.27.refs_0_), channel_id=1, source_target_pairs={{0,2},{1,3},{2,0},{3,1},{4,6},{5,7},{6,4},{7,5},{8,10},{9,11},{10,... | collective-permute-start | bytes 196616 | tf_op jit(solution)/shard_map/ppermute | solution.py:235
  26.8 0.4 collective-permute-start.6
  27.1 0.0 collective-permute-done.4.refs_1_
  27.1 2.7 %collective-permute-done.5.refs_2_ = bf16[2,64,256]{2,1,0:T(8,128)(2,1)S(1)} collective-permute-done((bf16[2,64,256]{2,1,0:T(8,128)(2,1)S(1)}, bf16[2,64,256]{2,1,0:T(8,128)(2,1)S(1)}, u32[]{:S(2)}, u32[]{:S(2)}) %collective-permute-start.5) | collective-permute-done | bytes 65568 | tf_op jit(solution)/shard_map/ppermute | solution.py:235
  29.8 1.1 %collective-permute-done.6.refs_3_ = bf16[2,64,256]{2,1,0:T(8,128)(2,1)S(1)} collective-permute-done((bf16[2,64,256]{2,1,0:T(8,128)(2,1)S(1)}, bf16[2,64,256]{2,1,0:T(8,128)(2,1)S(1)}, u32[]{:S(2)}, u32[]{:S(2)}) %collective-permute-start.6) | collective-permute-done | bytes 65568 | tf_op jit(solution)/shard_map/ppermute | solution.py:235
  30.9 0.0 collective-permute-done.got_ref
  30.9 0.5 decode.2
  31.4 2.4 %collective-permute-start.7 = (bf16[2,64,512]{2,1,0:T(8,128)(2,1)S(1)}, bf16[2,64,512]{2,1,0:T(8,128)(2,1)S(1)}, u32[]{:S(2)}, u32[]{:S(2)}) collective-permute-start(bf16[2,64,512]{2,1,0:T(8,128)(2,1)S(1)} %get-tuple-element.29), channel_id=1, source_target_pairs={{0,8},{1,9},{4,12},{5,13},{8,0},{9,1},{12,4},{13,5},{2,10},{3,11},... | collective-permute-start | bytes 393224 | tf_op jit(solution)/shard_map/ppermute | solution.py:258
  33.7 0.1 collective-permute-start.8
  33.9 0.6 %collective-permute-start.9 = (bf16[2,64,512]{2,1,0:T(8,128)(2,1)S(1)}, bf16[2,64,512]{2,1,0:T(8,128)(2,1)S(1)}, u32[]{:S(2)}, u32[]{:S(2)}) collective-permute-start(bf16[2,64,512]{2,1,0:T(8,128)(2,1)S(1)} %get-tuple-element.31), channel_id=1, source_target_pairs={{0,9},{1,8},{4,13},{5,12},{8,1},{9,0},{12,5},{13,4},{2,11},{3,10},... | collective-permute-start | bytes 393224 | tf_op jit(solution)/shard_map/ppermute | solution.py:258
  34.5 2.2 %collective-permute-done.10.got_ref = bf16[2,2,128,512]{3,2,1,0:T(8,128)(2,1)S(1)} collective-permute-done((bf16[2,2,128,512]{3,2,1,0:T(8,128)(2,1)S(1)}, bf16[2,2,128,512]{3,2,1,0:T(8,128)(2,1)S(1)}, u32[]{:S(2)}, u32[]{:S(2)}) %collective-permute-start.10) | collective-permute-done | bytes 524320 | tf_op jit(solution)/shard_map/ppermute | solution.py:228
  36.7 0.5 decode.3
  37.1 4.2 %collective-permute-start.11 = (bf16[2,64,512]{2,1,0:T(8,128)(2,1)S(1)}, bf16[2,64,512]{2,1,0:T(8,128)(2,1)S(1)}, u32[]{:S(2)}, u32[]{:S(2)}) collective-permute-start(bf16[2,64,512]{2,1,0:T(8,128)(2,1)S(1)} %get-tuple-element.34), channel_id=1, source_target_pairs={{0,8},{1,9},{4,12},{5,13},{8,0},{9,1},{12,4},{13,5},{2,10},{3,11},... | collective-permute-start | bytes 393224 | tf_op jit(solution)/shard_map/ppermute | solution.py:258
  41.4 0.0 collective-permute-start.12
  41.4 5.7 %collective-permute-done.7.refs_1_ = bf16[2,64,512]{2,1,0:T(8,128)(2,1)S(1)} collective-permute-done((bf16[2,64,512]{2,1,0:T(8,128)(2,1)S(1)}, bf16[2,64,512]{2,1,0:T(8,128)(2,1)S(1)}, u32[]{:S(2)}, u32[]{:S(2)}) %collective-permute-start.7) | collective-permute-done | bytes 131104 | tf_op jit(solution)/shard_map/ppermute | solution.py:258
  47.1 0.0 collective-permute-start.13
  47.1 0.0 collective-permute-done.8.refs_2_
  47.1 1.9 %collective-permute-done.9.refs_3_ = bf16[2,64,512]{2,1,0:T(8,128)(2,1)S(1)} collective-permute-done((bf16[2,64,512]{2,1,0:T(8,128)(2,1)S(1)}, bf16[2,64,512]{2,1,0:T(8,128)(2,1)S(1)}, u32[]{:S(2)}, u32[]{:S(2)}) %collective-permute-start.9) | collective-permute-done | bytes 131104 | tf_op jit(solution)/shard_map/ppermute | solution.py:258
  48.9 6.6 %collective-permute-done.11.refs_5_ = bf16[2,64,512]{2,1,0:T(8,128)(2,1)S(1)} collective-permute-done((bf16[2,64,512]{2,1,0:T(8,128)(2,1)S(1)}, bf16[2,64,512]{2,1,0:T(8,128)(2,1)S(1)}, u32[]{:S(2)}, u32[]{:S(2)}) %collective-permute-start.11) | collective-permute-done | bytes 131104 | tf_op jit(solution)/shard_map/ppermute | solution.py:258
  55.5 0.0 collective-permute-done.12.refs_6_
  55.5 1.9 %collective-permute-done.13.refs_7_ = bf16[2,64,512]{2,1,0:T(8,128)(2,1)S(1)} collective-permute-done((bf16[2,64,512]{2,1,0:T(8,128)(2,1)S(1)}, bf16[2,64,512]{2,1,0:T(8,128)(2,1)S(1)}, u32[]{:S(2)}, u32[]{:S(2)}) %collective-permute-start.13) | collective-permute-done | bytes 131104 | tf_op jit(solution)/shard_map/ppermute | solution.py:258
  57.3 0.0 copy-done
  57.4 0.0 copy-done.1
  57.4 0.9 %add.1 = bf16[2,64,2048]{2,1,0:T(8,128)(2,1)} custom-call(f32[2,2048]{1,0:T(2,128)S(1)} %copy-done.1, bf16[2,64,2048]{2,1,0:T(8,128)(2,1)S(1)} %copy-done, f32[2,64,512]{2,1,0:T(8,128)S(1)} %get-tuple-element.28.refs_4_.refs_0_, bf16[2,64,512]{2,1,0:T(8,128)(2,1)S(1)} %collective-permute-done.7.refs_1_, ...), custom_call_target="tpu_custom_call" | custom-call | tf_op jit(solution)/shard_map/add/pallas_call | solution.py:260
Async XLA Ops:
  0.0 23.0 %copy-start.3 = (s32[2,8]{1,0:T(2,128)S(1)}, s32[2,8]{1,0:T(2,128)}, u32[]{:S(2)}) copy-start(s32[2,8]{1,0:T(2,128)} %active_ref.1) | copy-start | bytes 196
  0.0 23.0 %copy-start.2 = (f32[512]{0:T(512)S(1)}, f32[512]{0:T(512)}, u32[]{:S(2)}) copy-start(f32[512]{0:T(512)} %param.9) | copy-start | bytes 6148
  3.3 54.1 %copy-start = (bf16[2,64,2048]{2,1,0:T(8,128)(2,1)S(1)}, bf16[2,64,2048]{2,1,0:T(8,128)(2,1)}, u32[]{:S(2)}) copy-start(bf16[2,64,2048]{2,1,0:T(8,128)(2,1)} %target_ref.1) | copy-start | bytes 1572868
  3.3 54.1 %copy-start.1 = (f32[2,2048]{1,0:T(2,128)S(1)}, f32[2,2048]{1,0:T(2,128)}, u32[]{:S(2)}) copy-start(f32[2,2048]{1,0:T(2,128)} %bias_ref.1) | copy-start | bytes 49156
  3.3 27.6 %collective-permute-start = (bf16[2,2,128,512]{3,2,1,0:T(8,128)(2,1)S(1)}, bf16[2,2,128,512]{3,2,1,0:T(8,128)(2,1)S(1)}, u32[]{:S(2)}, u32[]{:S(2)}) collective-permute-start(bf16[2,2,128,512]{3,2,1,0:T(8,128)(2,1)S(1)} %get-tuple-element.21.own_ref), channel_id=1, source_target_pairs={{0,4},{4,0},{8,12},{12,8},{1,5},{5,1},{9,13},{13,9},{2,6},{6,2},{1... | collective-permute-start | bytes 1572872 | tf_op jit(solution)/shard_map/ppermute | solution.py:228
  6.4 16.6 %collective-permute-start.1 = (bf16[128,256]{1,0:T(8,128)(2,1)S(1)}, bf16[128,256]{1,0:T(8,128)(2,1)S(1)}, u32[]{:S(2)}, u32[]{:S(2)}) collective-permute-start(bf16[128,256]{1,0:T(8,128)(2,1)S(1)} %get-tuple-element.23), channel_id=1, source_target_pairs={{0,4},{4,8},{8,12},{12,0},{1,5},{5,9},{9,13},{13,1},{2,6},{6,10},{... | collective-permute-start | bytes 196616 | tf_op jit(solution)/shard_map/ppermute | solution.py:215
  6.4 16.6 %collective-permute-start.2 = (bf16[128,256]{1,0:T(8,128)(2,1)S(1)}, bf16[128,256]{1,0:T(8,128)(2,1)S(1)}, u32[]{:S(2)}, u32[]{:S(2)}) collective-permute-start(bf16[128,256]{1,0:T(8,128)(2,1)S(1)} %get-tuple-element.24), channel_id=1, source_target_pairs={{0,8},{4,12},{8,0},{12,4},{1,9},{5,13},{9,1},{13,5},{2,10},{6,14},... | collective-permute-start | bytes 196616 | tf_op jit(solution)/shard_map/ppermute | solution.py:215
  9.4 13.6 %collective-permute-start.3 = (bf16[128,256]{1,0:T(8,128)(2,1)S(1)}, bf16[128,256]{1,0:T(8,128)(2,1)S(1)}, u32[]{:S(2)}, u32[]{:S(2)}) collective-permute-start(bf16[128,256]{1,0:T(8,128)(2,1)S(1)} %get-tuple-element.25), channel_id=1, source_target_pairs={{0,12},{4,0},{8,4},{12,8},{1,13},{5,1},{9,5},{13,9},{2,14},{6,2},{... | collective-permute-start | bytes 196616 | tf_op jit(solution)/shard_map/ppermute | solution.py:215
  23.7 13.0 %collective-permute-start.10 = (bf16[2,2,128,512]{3,2,1,0:T(8,128)(2,1)S(1)}, bf16[2,2,128,512]{3,2,1,0:T(8,128)(2,1)S(1)}, u32[]{:S(2)}, u32[]{:S(2)}) collective-permute-start(bf16[2,2,128,512]{3,2,1,0:T(8,128)(2,1)S(1)} %get-tuple-element.32.own_ref), channel_id=1, source_target_pairs={{0,4},{4,0},{8,12},{12,8},{1,5},{5,1},{9,13},{13,9},{2,6},{6,2},{1... | collective-permute-start | bytes 1572872 | tf_op jit(solution)/shard_map/ppermute | solution.py:228
  25.3 1.9 %collective-permute-start.4 = (bf16[2,64,256]{2,1,0:T(8,128)(2,1)S(1)}, bf16[2,64,256]{2,1,0:T(8,128)(2,1)S(1)}, u32[]{:S(2)}, u32[]{:S(2)}) collective-permute-start(bf16[2,64,256]{2,1,0:T(8,128)(2,1)S(1)} %get-tuple-element.27.refs_0_), channel_id=1, source_target_pairs={{0,1},{1,0},{2,3},{3,2},{4,5},{5,4},{6,7},{7,6},{8,9},{9,8},{10,11... | collective-permute-start | bytes 196616 | tf_op jit(solution)/shard_map/ppermute | solution.py:235
  25.3 4.5 %collective-permute-start.5 = (bf16[2,64,256]{2,1,0:T(8,128)(2,1)S(1)}, bf16[2,64,256]{2,1,0:T(8,128)(2,1)S(1)}, u32[]{:S(2)}, u32[]{:S(2)}) collective-permute-start(bf16[2,64,256]{2,1,0:T(8,128)(2,1)S(1)} %get-tuple-element.27.refs_0_), channel_id=1, source_target_pairs={{0,2},{1,3},{2,0},{3,1},{4,6},{5,7},{6,4},{7,5},{8,10},{9,11},{10,... | collective-permute-start | bytes 196616 | tf_op jit(solution)/shard_map/ppermute | solution.py:235
  26.8 4.1 %collective-permute-start.6 = (bf16[2,64,256]{2,1,0:T(8,128)(2,1)S(1)}, bf16[2,64,256]{2,1,0:T(8,128)(2,1)S(1)}, u32[]{:S(2)}, u32[]{:S(2)}) collective-permute-start(bf16[2,64,256]{2,1,0:T(8,128)(2,1)S(1)} %get-tuple-element.27.refs_0_), channel_id=1, source_target_pairs={{0,3},{1,2},{2,1},{3,0},{4,7},{5,6},{6,5},{7,4},{8,11},{9,10},{10,... | collective-permute-start | bytes 196616 | tf_op jit(solution)/shard_map/ppermute | solution.py:235
  31.4 15.7 %collective-permute-start.7 = (bf16[2,64,512]{2,1,0:T(8,128)(2,1)S(1)}, bf16[2,64,512]{2,1,0:T(8,128)(2,1)S(1)}, u32[]{:S(2)}, u32[]{:S(2)}) collective-permute-start(bf16[2,64,512]{2,1,0:T(8,128)(2,1)S(1)} %get-tuple-element.29), channel_id=1, source_target_pairs={{0,8},{1,9},{4,12},{5,13},{8,0},{9,1},{12,4},{13,5},{2,10},{3,11},... | collective-permute-start | bytes 393224 | tf_op jit(solution)/shard_map/ppermute | solution.py:258
  33.7 13.3 %collective-permute-start.8 = (bf16[2,64,512]{2,1,0:T(8,128)(2,1)S(1)}, bf16[2,64,512]{2,1,0:T(8,128)(2,1)S(1)}, u32[]{:S(2)}, u32[]{:S(2)}) collective-permute-start(bf16[2,64,512]{2,1,0:T(8,128)(2,1)S(1)} %get-tuple-element.30), channel_id=1, source_target_pairs={{0,1},{1,0},{4,5},{5,4},{8,9},{9,8},{12,13},{13,12},{2,3},{3,2},{6... | collective-permute-start | bytes 393224 | tf_op jit(solution)/shard_map/ppermute | solution.py:258
  33.9 15.1 %collective-permute-start.9 = (bf16[2,64,512]{2,1,0:T(8,128)(2,1)S(1)}, bf16[2,64,512]{2,1,0:T(8,128)(2,1)S(1)}, u32[]{:S(2)}, u32[]{:S(2)}) collective-permute-start(bf16[2,64,512]{2,1,0:T(8,128)(2,1)S(1)} %get-tuple-element.31), channel_id=1, source_target_pairs={{0,9},{1,8},{4,13},{5,12},{8,1},{9,0},{12,5},{13,4},{2,11},{3,10},... | collective-permute-start | bytes 393224 | tf_op jit(solution)/shard_map/ppermute | solution.py:258
  37.1 18.3 %collective-permute-start.11 = (bf16[2,64,512]{2,1,0:T(8,128)(2,1)S(1)}, bf16[2,64,512]{2,1,0:T(8,128)(2,1)S(1)}, u32[]{:S(2)}, u32[]{:S(2)}) collective-permute-start(bf16[2,64,512]{2,1,0:T(8,128)(2,1)S(1)} %get-tuple-element.34), channel_id=1, source_target_pairs={{0,8},{1,9},{4,12},{5,13},{8,0},{9,1},{12,4},{13,5},{2,10},{3,11},... | collective-permute-start | bytes 393224 | tf_op jit(solution)/shard_map/ppermute | solution.py:258
  41.4 14.1 %collective-permute-start.12 = (bf16[2,64,512]{2,1,0:T(8,128)(2,1)S(1)}, bf16[2,64,512]{2,1,0:T(8,128)(2,1)S(1)}, u32[]{:S(2)}, u32[]{:S(2)}) collective-permute-start(bf16[2,64,512]{2,1,0:T(8,128)(2,1)S(1)} %get-tuple-element.35), channel_id=1, source_target_pairs={{0,1},{1,0},{4,5},{5,4},{8,9},{9,8},{12,13},{13,12},{2,3},{3,2},{6... | collective-permute-start | bytes 393224 | tf_op jit(solution)/shard_map/ppermute | solution.py:258
  47.1 10.3 %collective-permute-start.13 = (bf16[2,64,512]{2,1,0:T(8,128)(2,1)S(1)}, bf16[2,64,512]{2,1,0:T(8,128)(2,1)S(1)}, u32[]{:S(2)}, u32[]{:S(2)}) collective-permute-start(bf16[2,64,512]{2,1,0:T(8,128)(2,1)S(1)} %get-tuple-element.36), channel_id=1, source_target_pairs={{0,9},{1,8},{4,13},{5,12},{8,1},{9,0},{12,5},{13,4},{2,11},{3,10},... | collective-permute-start | bytes 393224 | tf_op jit(solution)/shard_map/ppermute | solution.py:258

commit v5 on v4

--- a/solution.py
+++ b/solution.py
@@ -9,7 +9,7 @@
 
 VMEM_BYTES = 32 * 1024 * 1024
 LANES = 128
-SHARES = (4, 4)
+SHARES = (5, 3)
 
 
 def cut_columns(columns):
@@ -24,24 +24,20 @@
     return pieces
 
 
-def part_copies(piece, dec_hbm, part_ref, sems):
-    layers, groups, _, cols = dec_hbm.shape
+def part_copies(piece, layer, dec_hbm, part_ref, sems):
+    groups, cols = dec_hbm.shape[1], dec_hbm.shape[3]
     start = pl.multiple_of(lax.axis_index("rep") * (cols // 2) + piece[0], LANES)
     copies = []
-    for layer in range(layers):
-        for group in range(groups):
-            source = dec_hbm.at[layer, group, :, pl.ds(start, piece[1])]
-            copies.append(
-                pltpu.make_async_copy(
-                    source, part_ref.at[layer, group], sems.at[layer * groups + group]
-                )
-            )
-            copies[-1].start()
+    for group in range(groups):
+        source = dec_hbm.at[layer, group, :, pl.ds(start, piece[1])]
+        copies.append(pltpu.make_async_copy(source, part_ref.at[group], sems.at[group]))
+        copies[-1].start()
     return copies
 
 
 def encode_kernel(n, pieces, acts_hbm, w_hbm, dec_hbm, *refs):
-    term_refs, part_refs, refs = refs[:n], refs[n : n + len(pieces)], refs[n + len(pieces) :]
+    layers = dec_hbm.shape[0]
+    term_refs, part_refs, refs = refs[:n], refs[n:-5], refs[-5:]
     acts_ref, w_ref, part_sems, acts_sems, w_sems = refs
     half = n // 2
     width = w_ref.shape[1] // half
@@ -63,7 +59,9 @@
         copy.wait()
     copies_part = []
     for i, piece in enumerate(pieces):
-        copies_part += part_copies(piece, dec_hbm, part_refs[i], part_sems.at[i])
+        for layer in range(layers):
+            ref = part_refs[layer] if i == 0 else part_refs[layers + i - 1].at[layer]
+            copies_part += part_copies(piece, layer, dec_hbm, ref, part_sems.at[i, layer])
     src = lax.axis_index("src")
     for k in range(n):
         dest = lax.rem(src + k, n)
@@ -78,7 +76,7 @@
 
 
 def codes_kernel(n, share, tile_rows, active_ref, bias_ref, *refs):
-    term_refs, out_ref = refs[:n], refs[n + (len(refs) - n - 1) // 2]
+    term_refs, out_ref = refs[:n], refs[n]
     src = lax.axis_index("src")
     tgt = lax.axis_index("tgt")
     parity, half = lax.rem(src, 2), src // 2
@@ -113,9 +111,11 @@
             out_ref[group, :, columns] = value.astype(jnp.bfloat16)
 
 
-def decode_kernel(n, own_ref, got_ref, *refs):
-    half = n // 2
-    layers, groups, block, width = own_ref.shape
+def decode_kernel(n, layers, *refs):
+    half = n // 2
+    count = 1 if len(refs[0].shape) == 4 else layers
+    own_refs, got_refs, refs = refs[:count], refs[count : 2 * count], refs[2 * count :]
+    groups, block, width = own_refs[0].shape[-3:]
     code_refs, out_refs, lhs_ref = refs[: 2 * groups], refs[-2 * half - 1 : -1], refs[-1]
     src, tgt = lax.axis_index("src"), lax.axis_index("tgt")
     parity = lax.rem(src, 2)
@@ -133,8 +133,8 @@
                     rows = slice((2 * j + r) * share, (2 * j + r + 1) * share)
                     lhs_ref[rows, columns] = code_refs[2 * k + r][group, :, latents]
     for layer in range(layers):
-        own = own_ref[layer].reshape(depth, width)
-        got = got_ref[layer].reshape(depth, width)
+        own = (own_refs[layer][...] if count > 1 else own_refs[0][layer]).reshape(depth, width)
+        got = (got_refs[layer][...] if count > 1 else got_refs[0][layer]).reshape(depth, width)
         total = jnp.dot(lhs_ref[:, :depth], own, preferred_element_type=jnp.float32)
         total += jnp.dot(lhs_ref[:, depth:], got, preferred_element_type=jnp.float32)
         for i, ref in enumerate(out_refs):
@@ -196,13 +196,14 @@
     results = pl.pallas_call(
         functools.partial(encode_kernel, n, pieces),
         out_shape=[shape(half * share, 2 * block)] * n
-        + [shape(layers, groups, block, width) for _, width in pieces],
+        + [shape(groups, block, pieces[0][1])] * layers
+        + [shape(layers, groups, block, width) for _, width in pieces[1:]],
         in_specs=[anywhere] * 3,
-        out_specs=[vmem] * (n + len(pieces)),
+        out_specs=[vmem] * (n + layers + len(pieces) - 1),
         scratch_shapes=[
             pltpu.VMEM((2, half, share, features), jnp.bfloat16),
             pltpu.VMEM(enc_w.shape, jnp.bfloat16),
-            pltpu.SemaphoreType.DMA((len(pieces), layers * groups)),
+            pltpu.SemaphoreType.DMA((len(pieces), layers, groups)),
             pltpu.SemaphoreType.DMA((2 * half,)),
             pltpu.SemaphoreType.DMA((8,)),
         ],
@@ -213,19 +214,16 @@
     terms, parts = list(results[:n]), results[n:]
     for k in range(1, n):
         terms[k] = lax.ppermute(terms[k], "src", [(i, (i + k) % n) for i in range(n)])
-    own, *late = pl.pallas_call(
+    early, late = parts[:layers], parts[layers:]
+    own = pl.pallas_call(
         functools.partial(codes_kernel, n, share, tile_rows),
-        out_shape=[shape(half, share, 2 * block)]
-        + [jax.ShapeDtypeStruct(part.shape, part.dtype) for part in parts[1:]],
-        in_specs=[smem] + [vmem] * (1 + n) + [anywhere] * (len(parts) - 1),
-        out_specs=[vmem] + [anywhere] * (len(parts) - 1),
-        input_output_aliases={2 + n + i: 1 + i for i in range(len(parts) - 1)},
+        out_shape=shape(half, share, 2 * block),
+        in_specs=[smem] + [vmem] * (1 + n),
+        out_specs=vmem,
         compiler_params=params,
         cost_estimate=cost,
         name="codes",
-    )(active, enc_b.reshape(n, block), *terms, *parts[1:])
-    parts = [parts[0], *late]
-    got = [lax.ppermute(part, "src", pair) for part in parts]
+    )(active, enc_b.reshape(n, block), *terms)
     codes = []
     for k in range(groups):
         for r in range(2):
@@ -234,20 +232,35 @@
             ]
             codes.append(lax.ppermute(own, ("tgt", "rep"), perm) if k + r else own)
 
+    def hold(value, after):
+        return pl.pallas_call(
+            lambda *refs: None,
+            out_shape=jax.ShapeDtypeStruct(value.shape, value.dtype),
+            in_specs=[anywhere] * 2,
+            out_specs=anywhere,
+            input_output_aliases={0: 0},
+            compiler_params=params,
+            cost_estimate=cost,
+            name="hold",
+        )(value, after)
+
+    parts = [early] + [[hold(part, codes[1])] for part in late]
+    got = [[lax.ppermute(part, "src", pair) for part in piece] for piece in parts]
+
     sums, after = [], []
     for i, piece in enumerate(pieces):
         shapes = [shape(layers, share, piece[1])] * (2 * half)
         shapes[0] = shape(layers, share, piece[1], kind=jnp.float32)
         terms = pl.pallas_call(
-            functools.partial(decode_kernel, n),
+            functools.partial(decode_kernel, n, layers),
             out_shape=shapes,
-            in_specs=[vmem] * (2 + 2 * groups) + [anywhere] * len(after),
+            in_specs=[vmem] * (2 * len(parts[i]) + 2 * groups) + [anywhere] * len(after),
             out_specs=[vmem] * len(shapes),
             scratch_shapes=[pltpu.VMEM((rows, 2 * groups * block), jnp.bfloat16)],
             compiler_params=params,
             cost_estimate=cost,
             name="decode",
-        )(parts[i], got[i], *codes, *after)
+        )(*parts[i], *got[i], *codes, *after)
         after = [terms[0]]
         for r in range(2):
             for j in range(half):

time: 58.4 us -> 54.8 us (0.938)
  starting transfers between devices: 19.4 us -> 15.4 us
    ppermute x2 -> x3, waiting for transfers between devices: 2.2 us -> 13.4 us  [body(): lax.ppermute(part, 'src', pair)]
    ppermute x3, waiting for transfers between devices: 11.1 us -> 2.05 us  [body(): lax.ppermute(terms[k], 'src', [(i, (i + k) % n) for i in range(n)])]
    ppermute x6, waiting for transfers between devices: 16 us -> 11.8 us  [body(): sums.append(lax.ppermute(term, ('src', 'rep'), perm) if j + r else term)]
    ppermute x6, starting transfers between devices: 7.33 us -> 3.94 us  [body(): sums.append(lax.ppermute(term, ('src', 'rep'), perm) if j + r else term)]
    ppermute x2 -> x3, starting transfers between devices: 4.67 us -> 2.91 us  [body(): lax.ppermute(part, 'src', pair)]
    ppermute x3, waiting for transfers between devices: 3.76 us -> 5.51 us  [body(): codes.append(lax.ppermute(own, ('tgt', 'rep'), perm) if k + r else own)]
    ppermute x3, starting transfers between devices: 5.51 us -> 7 us  [body(): lax.ppermute(terms[k], 'src', [(i, (i + k) % n) for i in range(n)])]
  transfers between devices with their start and end apart: 14 -> 15, of which waited for: 8 -> 10; matrix products, arithmetic and copies ran while one was open for 0% -> 0% of each run, Pallas kernels for 3% -> 3%
where the time goes in v5:
time: 54.8 us; the launch traced here: 54.2 us
  waiting for transfers between devices  32.8 us (60%)
  starting transfers between devices  15.4 us (28%)
  Pallas kernels  5.93 us (11%)
    ppermute x3, waiting for transfers between devices, body(): lax.ppermute(part, 'src', pair)  13.4 us
    ppermute x6, waiting for transfers between devices, body(): sums.append(lax.ppermute(term, ('src', 'rep'), perm) if j + r else term)  11.8 us
    ppermute x3, starting transfers between devices, body(): lax.ppermute(terms[k], 'src', [(i, (i + k) % n) for i in range(n)])  7 us
    ppermute x3, waiting for transfers between devices, body(): codes.append(lax.ppermute(own, ('tgt', 'rep'), perm) if k + r else own)  5.51 us
    ppermute x6, starting transfers between devices, body(): sums.append(lax.ppermute(term, ('src', 'rep'), perm) if j + r else term)  3.94 us
    pallas_call x1, Pallas kernels, body(): pl.pallas_call(functools.partial(encode_kernel, n, pieces), out_shape=[sh...  3.27 us
    ppermute x3, starting transfers between devices, body(): lax.ppermute(part, 'src', pair)  2.91 us
    ppermute x3, waiting for transfers between devices, body(): lax.ppermute(terms[k], 'src', [(i, (i + k) % n) for i in range(n)])  2.05 us
  transfers between devices with their start and end apart: 15, of which 10 were waited for; matrix products, arithmetic and copies ran while one was open for 0% of the time, Pallas kernels for 3%

profile of v5, /device:TPU:0, one launch (start us, length us, event | category | flops | bytes accessed | tf_op | source)
XLA Modules:
  0.0 54.2 jit_solution(8910110608485363141)
XLA Ops:
  0.0 0.0 copy-start.3
  0.0 0.0 copy-start.2
  0.0 3.3 %encode.1 = (bf16[128,256]{1,0:T(8,128)(2,1)S(1)}, bf16[128,256]{1,0:T(8,128)(2,1)S(1)}, bf16[128,256]{1,0:T(8,128)(2,1)S(1)}, bf16[128,256]{1,0:T(8,128)(2,1)S(...) custom-call(bf16[2,2,64,1024]{3,2,1,0:T(8,128)(2,1)} %bitcast.3, ...), custom_call_target="tpu_custom_call" | custom-call | tf_op jit(solution)/shard_map/encode/pallas_call | solution.py:196
  3.3 0.0 copy-start
  3.3 0.0 copy-start.1
  3.3 3.1 %collective-permute-start.2 = (bf16[128,256]{1,0:T(8,128)(2,1)S(1)}, bf16[128,256]{1,0:T(8,128)(2,1)S(1)}, u32[]{:S(2)}, u32[]{:S(2)}) collective-permute-start(bf16[128,256]{1,0:T(8,128)(2,1)S(1)} %get-tuple-element.23), channel_id=1, source_target_pairs={{0,4},{4,8},{8,12},{12,0},{1,5},{5,9},{9,13},{13,1},{2,6},{6,10},{... | collective-permute-start | bytes 196616 | tf_op jit(solution)/shard_map/ppermute | solution.py:216
  6.4 2.6 %collective-permute-start.3 = (bf16[128,256]{1,0:T(8,128)(2,1)S(1)}, bf16[128,256]{1,0:T(8,128)(2,1)S(1)}, u32[]{:S(2)}, u32[]{:S(2)}) collective-permute-start(bf16[128,256]{1,0:T(8,128)(2,1)S(1)} %get-tuple-element.24), channel_id=1, source_target_pairs={{0,8},{4,12},{8,0},{12,4},{1,9},{5,13},{9,1},{13,5},{2,10},{6,14},... | collective-permute-start | bytes 196616 | tf_op jit(solution)/shard_map/ppermute | solution.py:216
  9.0 1.3 %collective-permute-start.4 = (bf16[128,256]{1,0:T(8,128)(2,1)S(1)}, bf16[128,256]{1,0:T(8,128)(2,1)S(1)}, u32[]{:S(2)}, u32[]{:S(2)}) collective-permute-start(bf16[128,256]{1,0:T(8,128)(2,1)S(1)} %get-tuple-element.25), channel_id=1, source_target_pairs={{0,12},{4,0},{8,4},{12,8},{1,13},{5,1},{9,5},{13,9},{2,14},{6,2},{... | collective-permute-start | bytes 196616 | tf_op jit(solution)/shard_map/ppermute | solution.py:216
  10.3 0.7 %collective-permute-start = (bf16[2,128,640]{2,1,0:T(8,128)(2,1)S(1)}, bf16[2,128,640]{2,1,0:T(8,128)(2,1)S(1)}, u32[]{:S(2)}, u32[]{:S(2)}) collective-permute-start(bf16[2,128,640]{2,1,0:T(8,128)(2,1)S(1)} %get-tuple-element.20.refs_0_), channel_id=1, source_target_pairs={{0,4},{4,0},{8,12},{12,8},{1,5},{5,1},{9,13},{13,9},{2,6},{6,2},{1... | collective-permute-start | bytes 983048 | tf_op jit(solution)/shard_map/ppermute | solution.py:248
  11.0 1.3 %collective-permute-start.1 = (bf16[2,128,640]{2,1,0:T(8,128)(2,1)S(1)}, bf16[2,128,640]{2,1,0:T(8,128)(2,1)S(1)}, u32[]{:S(2)}, u32[]{:S(2)}) collective-permute-start(bf16[2,128,640]{2,1,0:T(8,128)(2,1)S(1)} %get-tuple-element.21.refs_1_), channel_id=1, source_target_pairs={{0,4},{4,0},{8,12},{12,8},{1,5},{5,1},{9,13},{13,9},{2,6},{6,2},{1... | collective-permute-start | bytes 983048 | tf_op jit(solution)/shard_map/ppermute | solution.py:248
  12.3 0.0 collective-permute-done.2.refs_1_
  12.3 1.1 %collective-permute-done.3.refs_2_ = bf16[128,256]{1,0:T(8,128)(2,1)S(1)} collective-permute-done((bf16[128,256]{1,0:T(8,128)(2,1)S(1)}, bf16[128,256]{1,0:T(8,128)(2,1)S(1)}, u32[]{:S(2)}, u32[]{:S(2)}) %collective-permute-start.3) | collective-permute-done | bytes 65568 | tf_op jit(solution)/shard_map/ppermute | solution.py:216
  13.5 0.9 %collective-permute-done.4.refs_3_ = bf16[128,256]{1,0:T(8,128)(2,1)S(1)} collective-permute-done((bf16[128,256]{1,0:T(8,128)(2,1)S(1)}, bf16[128,256]{1,0:T(8,128)(2,1)S(1)}, u32[]{:S(2)}, u32[]{:S(2)}) %collective-permute-start.4) | collective-permute-done | bytes 65568 | tf_op jit(solution)/shard_map/ppermute | solution.py:216
  14.4 0.0 copy-done.3
  14.4 0.0 copy-done.2
  14.4 0.6 %codes.1.refs_4_.refs_2_ = bf16[2,64,256]{2,1,0:T(8,128)(2,1)S(1)} custom-call(s32[2,8]{1,0:T(2,128)S(1)} %copy-done.3, f32[4,128]{1,0:T(4,128)S(1)} %bitcast.2, bf16[128,256]{1,0:T(8,128)(2,1)S(1)} %get-tuple-element.22.refs_0_, bf16[128,256]{1,0:T(8,128)(2,1)S(1)} %collective-permute-done.2.refs_1_, bf16[128,256]{1,0:T(8,128)(2,1)S(1)} %collective-permute-done.3.refs_2_, ...), custom_call_target="tpu_custom_call" | custom-call | tf_op jit(solution)/shard_map/codes/pallas_call | solution.py:218
  15.0 0.1 collective-permute-start.5
  15.1 1.2 %collective-permute-done.5.refs_5_.refs_1_.refs_3_ = bf16[2,64,256]{2,1,0:T(8,128)(2,1)S(1)} collective-permute-done((bf16[2,64,256]{2,1,0:T(8,128)(2,1)S(1)}, bf16[2,64,256]{2,1,0:T(8,128)(2,1)S(1)}, u32[]{:S(2)}, u32[]{:S(2)}) %collective-permute-start.5) | collective-permute-done | bytes 65568 | tf_op jit(solution)/shard_map/ppermute | solution.py:233
  16.3 0.9 %collective-permute-start.11 = (bf16[2,2,128,384]{3,2,1,0:T(8,128)(2,1)S(1)}, bf16[2,2,128,384]{3,2,1,0:T(8,128)(2,1)S(1)}, u32[]{:S(2)}, u32[]{:S(2)}) collective-permute-start(bf16[2,2,128,384]{3,2,1,0:T(8,128)(2,1)S(1)} %hold.1.refs_0_), channel_id=1, source_target_pairs={{0,4},{4,0},{8,12},{12,8},{1,5},{5,1},{9,13},{13,9},{2,6},{6,2},{1... | collective-permute-start | bytes 1179656 | tf_op jit(solution)/shard_map/ppermute | solution.py:248
  17.2 1.0 %collective-permute-start.7 = (bf16[2,64,256]{2,1,0:T(8,128)(2,1)S(1)}, bf16[2,64,256]{2,1,0:T(8,128)(2,1)S(1)}, u32[]{:S(2)}, u32[]{:S(2)}) collective-permute-start(bf16[2,64,256]{2,1,0:T(8,128)(2,1)S(1)} %codes.1.refs_4_.refs_2_), channel_id=1, source_target_pairs={{0,3},{1,2},{2,1},{3,0},{4,7},{5,6},{6,5},{7,4},{8,11},{9,10},{10,... | collective-permute-start | bytes 196616 | tf_op jit(solution)/shard_map/ppermute | solution.py:233
  18.2 0.6 %collective-permute-start.6 = (bf16[2,64,256]{2,1,0:T(8,128)(2,1)S(1)}, bf16[2,64,256]{2,1,0:T(8,128)(2,1)S(1)}, u32[]{:S(2)}, u32[]{:S(2)}) collective-permute-start(bf16[2,64,256]{2,1,0:T(8,128)(2,1)S(1)} %codes.1.refs_4_.refs_2_), channel_id=1, source_target_pairs={{0,2},{1,3},{2,0},{3,1},{4,6},{5,7},{6,4},{7,5},{8,10},{9,11},{10,... | collective-permute-start | bytes 196616 | tf_op jit(solution)/shard_map/ppermute | solution.py:233
  18.8 2.8 %collective-permute-done.7.refs_7_.refs_5_ = bf16[2,64,256]{2,1,0:T(8,128)(2,1)S(1)} collective-permute-done((bf16[2,64,256]{2,1,0:T(8,128)(2,1)S(1)}, bf16[2,64,256]{2,1,0:T(8,128)(2,1)S(1)}, u32[]{:S(2)}, u32[]{:S(2)}) %collective-permute-start.7) | collective-permute-done | bytes 65568 | tf_op jit(solution)/shard_map/ppermute | solution.py:233
  21.6 1.5 %collective-permute-done.6.refs_6_.refs_4_ = bf16[2,64,256]{2,1,0:T(8,128)(2,1)S(1)} collective-permute-done((bf16[2,64,256]{2,1,0:T(8,128)(2,1)S(1)}, bf16[2,64,256]{2,1,0:T(8,128)(2,1)S(1)}, u32[]{:S(2)}, u32[]{:S(2)}) %collective-permute-start.6) | collective-permute-done | bytes 65568 | tf_op jit(solution)/shard_map/ppermute | solution.py:233
  23.0 0.0 collective-permute-done.refs_2_
  23.0 5.4 %collective-permute-done.1.refs_3_ = bf16[2,128,640]{2,1,0:T(8,128)(2,1)S(1)} collective-permute-done((bf16[2,128,640]{2,1,0:T(8,128)(2,1)S(1)}, bf16[2,128,640]{2,1,0:T(8,128)(2,1)S(1)}, u32[]{:S(2)}, u32[]{:S(2)}) %collective-permute-start.1) | collective-permute-done | bytes 327712 | tf_op jit(solution)/shard_map/ppermute | solution.py:248
  28.4 0.6 %decode.2 = (f32[2,64,640]{2,1,0:T(8,128)S(1)}, bf16[2,64,640]{2,1,0:T(8,128)(2,1)S(1)}, bf16[2,64,640]{2,1,0:T(8,128)(2,1)S(1)}, bf16[2,64,640]{2,1,0:T(8,128)(2,1)S(1)}) custom-call(bf16[2,128,640]{2,1,0:T(8,128)(2,1)S(1)} %get-tuple-element.20.refs_0_, bf16[2,128,640]{2,1,0:T(8,128)(2,1)S(1)} %get-tuple-element.21.refs_1_, ...), custom_call_target="tpu_custom_call" | custom-call | tf_op jit(solution)/shard_map/decode/pallas_call | solution.py:254
  29.1 0.9 %collective-permute-start.8 = (bf16[2,64,640]{2,1,0:T(8,128)(2,1)S(1)}, bf16[2,64,640]{2,1,0:T(8,128)(2,1)S(1)}, u32[]{:S(2)}, u32[]{:S(2)}) collective-permute-start(bf16[2,64,640]{2,1,0:T(8,128)(2,1)S(1)} %get-tuple-element.27), channel_id=1, source_target_pairs={{0,8},{1,9},{4,12},{5,13},{8,0},{9,1},{12,4},{13,5},{2,10},{3,11},... | collective-permute-start | bytes 491528 | tf_op jit(solution)/shard_map/ppermute | solution.py:271
  30.0 0.0 collective-permute-start.9
  30.0 2.2 %collective-permute-start.10 = (bf16[2,64,640]{2,1,0:T(8,128)(2,1)S(1)}, bf16[2,64,640]{2,1,0:T(8,128)(2,1)S(1)}, u32[]{:S(2)}, u32[]{:S(2)}) collective-permute-start(bf16[2,64,640]{2,1,0:T(8,128)(2,1)S(1)} %get-tuple-element.29), channel_id=1, source_target_pairs={{0,9},{1,8},{4,13},{5,12},{8,1},{9,0},{12,5},{13,4},{2,11},{3,10},... | collective-permute-start | bytes 491528 | tf_op jit(solution)/shard_map/ppermute | solution.py:271
  32.2 8.0 %collective-permute-done.11.refs_1_ = bf16[2,2,128,384]{3,2,1,0:T(8,128)(2,1)S(1)} collective-permute-done((bf16[2,2,128,384]{3,2,1,0:T(8,128)(2,1)S(1)}, bf16[2,2,128,384]{3,2,1,0:T(8,128)(2,1)S(1)}, u32[]{:S(2)}, u32[]{:S(2)}) %collective-permute-start.11) | collective-permute-done | bytes 393248 | tf_op jit(solution)/shard_map/ppermute | solution.py:248
  40.2 0.5 decode.3
  40.7 0.8 %collective-permute-start.12 = (bf16[2,64,384]{2,1,0:T(8,128)(2,1)S(1)}, bf16[2,64,384]{2,1,0:T(8,128)(2,1)S(1)}, u32[]{:S(2)}, u32[]{:S(2)}) collective-permute-start(bf16[2,64,384]{2,1,0:T(8,128)(2,1)S(1)} %get-tuple-element.32), channel_id=1, source_target_pairs={{0,8},{1,9},{4,12},{5,13},{8,0},{9,1},{12,4},{13,5},{2,10},{3,11},... | collective-permute-start | bytes 294920 | tf_op jit(solution)/shard_map/ppermute | solution.py:271
  41.5 0.0 collective-permute-start.13
  41.5 3.4 %collective-permute-done.8.refs_1_ = bf16[2,64,640]{2,1,0:T(8,128)(2,1)S(1)} collective-permute-done((bf16[2,64,640]{2,1,0:T(8,128)(2,1)S(1)}, bf16[2,64,640]{2,1,0:T(8,128)(2,1)S(1)}, u32[]{:S(2)}, u32[]{:S(2)}) %collective-permute-start.8) | collective-permute-done | bytes 163872 | tf_op jit(solution)/shard_map/ppermute | solution.py:271
  44.9 0.0 collective-permute-start.14
  44.9 0.0 collective-permute-done.9.refs_2_
  44.9 1.7 %collective-permute-done.10.refs_3_ = bf16[2,64,640]{2,1,0:T(8,128)(2,1)S(1)} collective-permute-done((bf16[2,64,640]{2,1,0:T(8,128)(2,1)S(1)}, bf16[2,64,640]{2,1,0:T(8,128)(2,1)S(1)}, u32[]{:S(2)}, u32[]{:S(2)}) %collective-permute-start.10) | collective-permute-done | bytes 163872 | tf_op jit(solution)/shard_map/ppermute | solution.py:271
  46.6 6.7 %collective-permute-done.12.refs_5_ = bf16[2,64,384]{2,1,0:T(8,128)(2,1)S(1)} collective-permute-done((bf16[2,64,384]{2,1,0:T(8,128)(2,1)S(1)}, bf16[2,64,384]{2,1,0:T(8,128)(2,1)S(1)}, u32[]{:S(2)}, u32[]{:S(2)}) %collective-permute-start.12) | collective-permute-done | bytes 98336 | tf_op jit(solution)/shard_map/ppermute | solution.py:271
  53.3 0.0 collective-permute-done.13.refs_6_
  53.3 0.0 collective-permute-done.14.refs_7_
  53.3 0.0 copy-done
  53.3 0.0 copy-done.1
  53.3 0.9 %add.1 = bf16[2,64,2048]{2,1,0:T(8,128)(2,1)} custom-call(f32[2,2048]{1,0:T(2,128)S(1)} %copy-done.1, bf16[2,64,2048]{2,1,0:T(8,128)(2,1)S(1)} %copy-done, f32[2,64,640]{2,1,0:T(8,128)S(1)} %get-tuple-element.26.refs_6_.refs_0_, bf16[2,64,640]{2,1,0:T(8,128)(2,1)S(1)} %collective-permute-done.8.refs_1_, ...), custom_call_target="tpu_custom_call" | custom-call | tf_op jit(solution)/shard_map/add/pallas_call | solution.py:273
  (1 shorter events, 0.0 us)
Async XLA Ops:
  0.0 14.4 %copy-start.3 = (s32[2,8]{1,0:T(2,128)S(1)}, s32[2,8]{1,0:T(2,128)}, u32[]{:S(2)}) copy-start(s32[2,8]{1,0:T(2,128)} %active_ref.1) | copy-start | bytes 196
  0.0 14.4 %copy-start.2 = (f32[512]{0:T(512)S(1)}, f32[512]{0:T(512)}, u32[]{:S(2)}) copy-start(f32[512]{0:T(512)} %param.9) | copy-start | bytes 6148
  3.3 50.0 %copy-start = (bf16[2,64,2048]{2,1,0:T(8,128)(2,1)S(1)}, bf16[2,64,2048]{2,1,0:T(8,128)(2,1)}, u32[]{:S(2)}) copy-start(bf16[2,64,2048]{2,1,0:T(8,128)(2,1)} %target_ref.1) | copy-start | bytes 1572868
  3.3 50.0 %copy-start.1 = (f32[2,2048]{1,0:T(2,128)S(1)}, f32[2,2048]{1,0:T(2,128)}, u32[]{:S(2)}) copy-start(f32[2,2048]{1,0:T(2,128)} %bias_ref.1) | copy-start | bytes 49156
  3.3 9.0 %collective-permute-start.2 = (bf16[128,256]{1,0:T(8,128)(2,1)S(1)}, bf16[128,256]{1,0:T(8,128)(2,1)S(1)}, u32[]{:S(2)}, u32[]{:S(2)}) collective-permute-start(bf16[128,256]{1,0:T(8,128)(2,1)S(1)} %get-tuple-element.23), channel_id=1, source_target_pairs={{0,4},{4,8},{8,12},{12,0},{1,5},{5,9},{9,13},{13,1},{2,6},{6,10},{... | collective-permute-start | bytes 196616 | tf_op jit(solution)/shard_map/ppermute | solution.py:216
  6.4 7.1 %collective-permute-start.3 = (bf16[128,256]{1,0:T(8,128)(2,1)S(1)}, bf16[128,256]{1,0:T(8,128)(2,1)S(1)}, u32[]{:S(2)}, u32[]{:S(2)}) collective-permute-start(bf16[128,256]{1,0:T(8,128)(2,1)S(1)} %get-tuple-element.24), channel_id=1, source_target_pairs={{0,8},{4,12},{8,0},{12,4},{1,9},{5,13},{9,1},{13,5},{2,10},{6,14},... | collective-permute-start | bytes 196616 | tf_op jit(solution)/shard_map/ppermute | solution.py:216
  9.0 5.4 %collective-permute-start.4 = (bf16[128,256]{1,0:T(8,128)(2,1)S(1)}, bf16[128,256]{1,0:T(8,128)(2,1)S(1)}, u32[]{:S(2)}, u32[]{:S(2)}) collective-permute-start(bf16[128,256]{1,0:T(8,128)(2,1)S(1)} %get-tuple-element.25), channel_id=1, source_target_pairs={{0,12},{4,0},{8,4},{12,8},{1,13},{5,1},{9,5},{13,9},{2,14},{6,2},{... | collective-permute-start | bytes 196616 | tf_op jit(solution)/shard_map/ppermute | solution.py:216
  10.3 12.7 %collective-permute-start = (bf16[2,128,640]{2,1,0:T(8,128)(2,1)S(1)}, bf16[2,128,640]{2,1,0:T(8,128)(2,1)S(1)}, u32[]{:S(2)}, u32[]{:S(2)}) collective-permute-start(bf16[2,128,640]{2,1,0:T(8,128)(2,1)S(1)} %get-tuple-element.20.refs_0_), channel_id=1, source_target_pairs={{0,4},{4,0},{8,12},{12,8},{1,5},{5,1},{9,13},{13,9},{2,6},{6,2},{1... | collective-permute-start | bytes 983048 | tf_op jit(solution)/shard_map/ppermute | solution.py:248
  11.0 17.4 %collective-permute-start.1 = (bf16[2,128,640]{2,1,0:T(8,128)(2,1)S(1)}, bf16[2,128,640]{2,1,0:T(8,128)(2,1)S(1)}, u32[]{:S(2)}, u32[]{:S(2)}) collective-permute-start(bf16[2,128,640]{2,1,0:T(8,128)(2,1)S(1)} %get-tuple-element.21.refs_1_), channel_id=1, source_target_pairs={{0,4},{4,0},{8,12},{12,8},{1,5},{5,1},{9,13},{13,9},{2,6},{6,2},{1... | collective-permute-start | bytes 983048 | tf_op jit(solution)/shard_map/ppermute | solution.py:248
  15.0 1.3 %collective-permute-start.5 = (bf16[2,64,256]{2,1,0:T(8,128)(2,1)S(1)}, bf16[2,64,256]{2,1,0:T(8,128)(2,1)S(1)}, u32[]{:S(2)}, u32[]{:S(2)}) collective-permute-start(bf16[2,64,256]{2,1,0:T(8,128)(2,1)S(1)} %codes.1.refs_4_.refs_2_), channel_id=1, source_target_pairs={{0,1},{1,0},{2,3},{3,2},{4,5},{5,4},{6,7},{7,6},{8,9},{9,8},{10,11... | collective-permute-start | bytes 196616 | tf_op jit(solution)/shard_map/ppermute | solution.py:233
  16.3 23.8 %collective-permute-start.11 = (bf16[2,2,128,384]{3,2,1,0:T(8,128)(2,1)S(1)}, bf16[2,2,128,384]{3,2,1,0:T(8,128)(2,1)S(1)}, u32[]{:S(2)}, u32[]{:S(2)}) collective-permute-start(bf16[2,2,128,384]{3,2,1,0:T(8,128)(2,1)S(1)} %hold.1.refs_0_), channel_id=1, source_target_pairs={{0,4},{4,0},{8,12},{12,8},{1,5},{5,1},{9,13},{13,9},{2,6},{6,2},{1... | collective-permute-start | bytes 1179656 | tf_op jit(solution)/shard_map/ppermute | solution.py:248
  17.2 4.3 %collective-permute-start.7 = (bf16[2,64,256]{2,1,0:T(8,128)(2,1)S(1)}, bf16[2,64,256]{2,1,0:T(8,128)(2,1)S(1)}, u32[]{:S(2)}, u32[]{:S(2)}) collective-permute-start(bf16[2,64,256]{2,1,0:T(8,128)(2,1)S(1)} %codes.1.refs_4_.refs_2_), channel_id=1, source_target_pairs={{0,3},{1,2},{2,1},{3,0},{4,7},{5,6},{6,5},{7,4},{8,11},{9,10},{10,... | collective-permute-start | bytes 196616 | tf_op jit(solution)/shard_map/ppermute | solution.py:233
  18.2 4.8 %collective-permute-start.6 = (bf16[2,64,256]{2,1,0:T(8,128)(2,1)S(1)}, bf16[2,64,256]{2,1,0:T(8,128)(2,1)S(1)}, u32[]{:S(2)}, u32[]{:S(2)}) collective-permute-start(bf16[2,64,256]{2,1,0:T(8,128)(2,1)S(1)} %codes.1.refs_4_.refs_2_), channel_id=1, source_target_pairs={{0,2},{1,3},{2,0},{3,1},{4,6},{5,7},{6,4},{7,5},{8,10},{9,11},{10,... | collective-permute-start | bytes 196616 | tf_op jit(solution)/shard_map/ppermute | solution.py:233
  29.1 15.9 %collective-permute-start.8 = (bf16[2,64,640]{2,1,0:T(8,128)(2,1)S(1)}, bf16[2,64,640]{2,1,0:T(8,128)(2,1)S(1)}, u32[]{:S(2)}, u32[]{:S(2)}) collective-permute-start(bf16[2,64,640]{2,1,0:T(8,128)(2,1)S(1)} %get-tuple-element.27), channel_id=1, source_target_pairs={{0,8},{1,9},{4,12},{5,13},{8,0},{9,1},{12,4},{13,5},{2,10},{3,11},... | collective-permute-start | bytes 491528 | tf_op jit(solution)/shard_map/ppermute | solution.py:271
  30.0 14.9 %collective-permute-start.9 = (bf16[2,64,640]{2,1,0:T(8,128)(2,1)S(1)}, bf16[2,64,640]{2,1,0:T(8,128)(2,1)S(1)}, u32[]{:S(2)}, u32[]{:S(2)}) collective-permute-start(bf16[2,64,640]{2,1,0:T(8,128)(2,1)S(1)} %get-tuple-element.28), channel_id=1, source_target_pairs={{0,1},{1,0},{4,5},{5,4},{8,9},{9,8},{12,13},{13,12},{2,3},{3,2},{6... | collective-permute-start | bytes 491528 | tf_op jit(solution)/shard_map/ppermute | solution.py:271
  30.0 16.6 %collective-permute-start.10 = (bf16[2,64,640]{2,1,0:T(8,128)(2,1)S(1)}, bf16[2,64,640]{2,1,0:T(8,128)(2,1)S(1)}, u32[]{:S(2)}, u32[]{:S(2)}) collective-permute-start(bf16[2,64,640]{2,1,0:T(8,128)(2,1)S(1)} %get-tuple-element.29), channel_id=1, source_target_pairs={{0,9},{1,8},{4,13},{5,12},{8,1},{9,0},{12,5},{13,4},{2,11},{3,10},... | collective-permute-start | bytes 491528 | tf_op jit(solution)/shard_map/ppermute | solution.py:271
  40.7 12.6 %collective-permute-start.12 = (bf16[2,64,384]{2,1,0:T(8,128)(2,1)S(1)}, bf16[2,64,384]{2,1,0:T(8,128)(2,1)S(1)}, u32[]{:S(2)}, u32[]{:S(2)}) collective-permute-start(bf16[2,64,384]{2,1,0:T(8,128)(2,1)S(1)} %get-tuple-element.32), channel_id=1, source_target_pairs={{0,8},{1,9},{4,12},{5,13},{8,0},{9,1},{12,4},{13,5},{2,10},{3,11},... | collective-permute-start | bytes 294920 | tf_op jit(solution)/shard_map/ppermute | solution.py:271
  41.5 11.8 %collective-permute-start.13 = (bf16[2,64,384]{2,1,0:T(8,128)(2,1)S(1)}, bf16[2,64,384]{2,1,0:T(8,128)(2,1)S(1)}, u32[]{:S(2)}, u32[]{:S(2)}) collective-permute-start(bf16[2,64,384]{2,1,0:T(8,128)(2,1)S(1)} %get-tuple-element.33), channel_id=1, source_target_pairs={{0,1},{1,0},{4,5},{5,4},{8,9},{9,8},{12,13},{13,12},{2,3},{3,2},{6... | collective-permute-start | bytes 294920 | tf_op jit(solution)/shard_map/ppermute | solution.py:271
  44.9 8.4 %collective-permute-start.14 = (bf16[2,64,384]{2,1,0:T(8,128)(2,1)S(1)}, bf16[2,64,384]{2,1,0:T(8,128)(2,1)S(1)}, u32[]{:S(2)}, u32[]{:S(2)}) collective-permute-start(bf16[2,64,384]{2,1,0:T(8,128)(2,1)S(1)} %get-tuple-element.34), channel_id=1, source_target_pairs={{0,9},{1,8},{4,13},{5,12},{8,1},{9,0},{12,5},{13,4},{2,11},{3,10},... | collective-permute-start | bytes 294920 | tf_op jit(solution)/shard_map/ppermute | solution.py:271

commit v6 on v5

--- a/solution.py
+++ b/solution.py
@@ -9,34 +9,33 @@
 
 VMEM_BYTES = 32 * 1024 * 1024
 LANES = 128
-SHARES = (5, 3)
-
-
-def cut_columns(columns):
+FIRST = 7
+
+
+def cut_pieces(layers, columns):
     tiles = columns // LANES
-    pieces, start = [], 0
-    for i, eighths in enumerate(SHARES):
-        stop = min(tiles, start + -(-tiles * eighths // 8))
-        stop = tiles if i == len(SHARES) - 1 else stop
-        if stop > start:
-            pieces.append((start * LANES, (stop - start) * LANES))
-        start = stop
+    first = -(-tiles * FIRST // 8)
+    pieces = [((layer,), 0, first * LANES) for layer in range(layers)]
+    if first < tiles:
+        pieces.append((tuple(range(layers)), first * LANES, (tiles - first) * LANES))
     return pieces
 
 
-def part_copies(piece, layer, dec_hbm, part_ref, sems):
+def part_copies(piece, dec_hbm, part_ref, sems):
+    layers, first, width = piece
     groups, cols = dec_hbm.shape[1], dec_hbm.shape[3]
-    start = pl.multiple_of(lax.axis_index("rep") * (cols // 2) + piece[0], LANES)
+    start = pl.multiple_of(lax.axis_index("rep") * (cols // 2) + first, LANES)
     copies = []
-    for group in range(groups):
-        source = dec_hbm.at[layer, group, :, pl.ds(start, piece[1])]
-        copies.append(pltpu.make_async_copy(source, part_ref.at[group], sems.at[group]))
-        copies[-1].start()
+    for i, layer in enumerate(layers):
+        for group in range(groups):
+            source = dec_hbm.at[layer, group, :, pl.ds(start, width)]
+            sem = sems.at[i * groups + group]
+            copies.append(pltpu.make_async_copy(source, part_ref.at[i, group], sem))
+            copies[-1].start()
     return copies
 
 
 def encode_kernel(n, pieces, acts_hbm, w_hbm, dec_hbm, *refs):
-    layers = dec_hbm.shape[0]
     term_refs, part_refs, refs = refs[:n], refs[n:-5], refs[-5:]
     acts_ref, w_ref, part_sems, acts_sems, w_sems = refs
     half = n // 2
@@ -59,9 +58,7 @@
         copy.wait()
     copies_part = []
     for i, piece in enumerate(pieces):
-        for layer in range(layers):
-            ref = part_refs[layer] if i == 0 else part_refs[layers + i - 1].at[layer]
-            copies_part += part_copies(piece, layer, dec_hbm, ref, part_sems.at[i, layer])
+        copies_part += part_copies(piece, dec_hbm, part_refs[i], part_sems.at[i])
     src = lax.axis_index("src")
     for k in range(n):
         dest = lax.rem(src + k, n)
@@ -111,11 +108,9 @@
             out_ref[group, :, columns] = value.astype(jnp.bfloat16)
 
 
-def decode_kernel(n, layers, *refs):
+def decode_kernel(n, own_ref, got_ref, *refs):
     half = n // 2
-    count = 1 if len(refs[0].shape) == 4 else layers
-    own_refs, got_refs, refs = refs[:count], refs[count : 2 * count], refs[2 * count :]
-    groups, block, width = own_refs[0].shape[-3:]
+    layers, groups, block, width = own_ref.shape
     code_refs, out_refs, lhs_ref = refs[: 2 * groups], refs[-2 * half - 1 : -1], refs[-1]
     src, tgt = lax.axis_index("src"), lax.axis_index("tgt")
     parity = lax.rem(src, 2)
@@ -133,36 +128,36 @@
                     rows = slice((2 * j + r) * share, (2 * j + r + 1) * share)
                     lhs_ref[rows, columns] = code_refs[2 * k + r][group, :, latents]
     for layer in range(layers):
-        own = (own_refs[layer][...] if count > 1 else own_refs[0][layer]).reshape(depth, width)
-        got = (got_refs[layer][...] if count > 1 else got_refs[0][layer]).reshape(depth, width)
+        own = own_ref[layer].reshape(depth, width)
+        got = got_ref[layer].reshape(depth, width)
         total = jnp.dot(lhs_ref[:, :depth], own, preferred_element_type=jnp.float32)
         total += jnp.dot(lhs_ref[:, depth:], got, preferred_element_type=jnp.float32)
         for i, ref in enumerate(out_refs):
             ref[layer] = total[i * share : (i + 1) * share].astype(ref.dtype)
 
 
-def add_kernel(n, pieces, bias_ref, target_ref, *refs):
+def add_kernel(n, pieces, chained, bias_ref, target_ref, *refs):
     out_hbm, out_ref, sems = refs[-3:]
     half = n // 2
-    layers, _, cols = target_ref.shape
+    cols = target_ref.shape[2]
     rep = lax.axis_index("rep")
     copies = []
-    for i, (first, width) in enumerate(pieces):
+    for i, (layers, first, width) in enumerate(pieces):
         for side in range(2):
             core = rep if side == 0 else 1 - rep
             columns = pl.ds(pl.multiple_of(core * (cols // 2) + first, LANES), width)
             mine = refs[(2 * i + side) * half : (2 * i + side + 1) * half]
-            for layer in range(layers):
+            for j, layer in enumerate(layers):
                 total = bias_ref[layer : layer + 1, columns]
                 total = total - target_ref[layer, :, columns].astype(jnp.float32)
                 for ref in mine:
-                    total = total + ref[layer].astype(jnp.float32)
+                    total = total + ref[j].astype(jnp.float32)
                 out_ref[layer, :, columns] = total.astype(jnp.bfloat16)
                 copies.append(
                     pltpu.make_async_copy(
                         out_ref.at[layer, :, columns],
                         out_hbm.at[layer, :, columns],
-                        sems.at[(2 * i + side) * layers + layer],
+                        sems.at[len(copies)],
                     )
                 )
                 copies[-1].start()
@@ -176,7 +171,7 @@
     layers, groups, block, cols = dec_w.shape
     share = rows // n
     half = n // 2
-    pieces = cut_columns(cols // 2)
+    pieces = cut_pieces(layers, cols // 2)
     tile_rows = rows // active.shape[0]
     pair = [(i, i ^ 1) for i in range(n)]
     params = pltpu.CompilerParams(vmem_limit_bytes=VMEM_BYTES)
@@ -196,14 +191,13 @@
     results = pl.pallas_call(
         functools.partial(encode_kernel, n, pieces),
         out_shape=[shape(half * share, 2 * block)] * n
-        + [shape(groups, block, pieces[0][1])] * layers
-        + [shape(layers, groups, block, width) for _, width in pieces[1:]],
+        + [shape(len(which), groups, block, width) for which, _, width in pieces],
         in_specs=[anywhere] * 3,
-        out_specs=[vmem] * (n + layers + len(pieces) - 1),
+        out_specs=[vmem] * (n + len(pieces)),
         scratch_shapes=[
             pltpu.VMEM((2, half, share, features), jnp.bfloat16),
             pltpu.VMEM(enc_w.shape, jnp.bfloat16),
-            pltpu.SemaphoreType.DMA((len(pieces), layers, groups)),
+            pltpu.SemaphoreType.DMA((len(pieces), layers * groups)),
             pltpu.SemaphoreType.DMA((2 * half,)),
             pltpu.SemaphoreType.DMA((8,)),
         ],
@@ -211,10 +205,9 @@
         cost_estimate=cost,
         name="encode",
     )(acts, enc_w, dec_w)
-    terms, parts = list(results[:n]), results[n:]
+    terms, parts = list(results[:n]), list(results[n:])
     for k in range(1, n):
         terms[k] = lax.ppermute(terms[k], "src", [(i, (i + k) % n) for i in range(n)])
-    early, late = parts[:layers], parts[layers:]
     own = pl.pallas_call(
         functools.partial(codes_kernel, n, share, tile_rows),
         out_shape=shape(half, share, 2 * block),
@@ -244,45 +237,57 @@
             name="hold",
         )(value, after)
 
-    parts = [early] + [[hold(part, codes[1])] for part in late]
-    got = [[lax.ppermute(part, "src", pair) for part in piece] for piece in parts]
-
-    sums, after = [], []
-    for i, piece in enumerate(pieces):
-        shapes = [shape(layers, share, piece[1])] * (2 * half)
-        shapes[0] = shape(layers, share, piece[1], kind=jnp.float32)
+    def add(some, out):
+        chained = [] if out is None else [out]
+        operands = [value for i in some for value in sums[i]]
+        return pl.pallas_call(
+            functools.partial(add_kernel, n, [pieces[i] for i in some], len(chained)),
+            out_shape=shape(layers, share, cols),
+            in_specs=[vmem] * (2 + len(operands)) + [anywhere] * len(chained),
+            out_specs=anywhere,
+            scratch_shapes=[
+                pltpu.VMEM((layers, share, cols), jnp.bfloat16),
+                pltpu.SemaphoreType.DMA((2 * len(some) * layers,)),
+            ],
+            input_output_aliases={2 + len(operands): 0} if chained else {},
+            compiler_params=params,
+            cost_estimate=cost,
+            name="add",
+        )(dec_b, targets, *operands, *chained)
+
+    parts[1:layers] = [hold(part, codes[1]) for part in parts[1:layers]]
+    got = [lax.ppermute(part, "src", pair) for part in parts[:layers]]
+    sums, after, out = [], [], None
+    for i, (which, _, width) in enumerate(pieces):
+        if i == layers:
+            out = add([0], None)
+            after.append(out)
+        shapes = [shape(len(which), share, width)] * (2 * half)
+        shapes[0] = shape(len(which), share, width, kind=jnp.float32)
         terms = pl.pallas_call(
-            functools.partial(decode_kernel, n, layers),
+            functools.partial(decode_kernel, n),
             out_shape=shapes,
-            in_specs=[vmem] * (2 * len(parts[i]) + 2 * groups) + [anywhere] * len(after),
+            in_specs=[vmem] * (2 + 2 * groups) + [anywhere] * len(after),
             out_specs=[vmem] * len(shapes),
             scratch_shapes=[pltpu.VMEM((rows, 2 * groups * block), jnp.bfloat16)],
             compiler_params=params,
             cost_estimate=cost,
             name="decode",
-        )(*parts[i], *got[i], *codes, *after)
+        )(parts[i], got[i], *codes, *after)
         after = [terms[0]]
+        if i == 0:
+            for part in parts[layers:]:
+                got.append(lax.ppermute(hold(part, terms[0]), "src", pair))
+        sums.append([])
         for r in range(2):
             for j in range(half):
                 perm = [
                     (d * 2 + c, (d + 2 * j) % n * 2 + (c ^ r)) for d in range(n) for c in range(2)
                 ]
                 term = terms[2 * j + r]
-                sums.append(lax.ppermute(term, ("src", "rep"), perm) if j + r else term)
-
-    return pl.pallas_call(
-        functools.partial(add_kernel, n, pieces),
-        out_shape=shape(layers, share, cols),
-        in_specs=[vmem] * (2 + len(sums)),
-        out_specs=anywhere,
-        scratch_shapes=[
-            pltpu.VMEM((layers, share, cols), jnp.bfloat16),
-            pltpu.SemaphoreType.DMA((2 * len(pieces) * layers,)),
-        ],
-        compiler_params=params,
-        cost_estimate=cost,
-        name="add",
-    )(dec_b, targets, *sums)
+                sums[i].append(lax.ppermute(term, ("src", "rep"), perm) if j + r else term)
+    rest = range(0 if out is None else 1, len(pieces))
+    return add(list(rest), out)
 
 
 def solution(mesh):

time: 54.8 us -> 58 us (1.058)
  starting transfers between devices: 15.4 us -> 17.4 us
  local copies, waits for them, and re-layouts: 0.02 us -> 1.06 us
  Pallas kernels: 5.93 us -> 6.8 us
    ppermute x9 -> x12, starting transfers between devices: 6.85 us -> 8.8 us  [the longest x9 5.93 us: body(): sums[i].append(lax.ppermute(term, ('src', 'rep'), perm) if j + r else term)]
    ppermute x9 -> x12, waiting for transfers between devices: 25.2 us -> 23.6 us  [the longest x9 11.9 us: body(): sums[i].append(lax.ppermute(term, ('src', 'rep'), perm) if j + r else term)]
    ppermute x3, waiting for transfers between devices: 2.05 us -> 3.39 us  [body(): lax.ppermute(terms[k], 'src', [(i, (i + k) % n) for i in range(n)])]
    unnamed x8 -> x11, local copies, waits for them, and re-layouts: 0.02 us -> 1.06 us
    pallas_call x3 -> x5, Pallas kernels: 2.03 us -> 2.89 us  [the longest x2 1.62 us: add(): pl.pallas_call(functools.partial(add_kernel, n, [pieces[i] for i in some]...]
  transfers between devices with their start and end apart: 15 -> 18, of which waited for: 10 -> 9; matrix products, arithmetic and copies ran while one was open for 0% -> 0% of each run, Pallas kernels for 3% -> 5%
where the time goes in v6:
time: 58 us; the launch traced here: 57.8 us
  waiting for transfers between devices  32.4 us (56%)
  starting transfers between devices  17.4 us (30%)
  Pallas kernels  6.8 us (12%)
  local copies, waits for them, and re-layouts  1.06 us (2%)
    ppermute x9, waiting for transfers between devices, body(): sums[i].append(lax.ppermute(term, ('src', 'rep'), perm) if j + r else term)  11.9 us
    ppermute x2, waiting for transfers between devices, body(): got = [lax.ppermute(part, 'src', pair) for part in parts[:layers]]  11.7 us
    ppermute x3, starting transfers between devices, body(): lax.ppermute(terms[k], 'src', [(i, (i + k) % n) for i in range(n)])  7 us
    ppermute x9, starting transfers between devices, body(): sums[i].append(lax.ppermute(term, ('src', 'rep'), perm) if j + r else term)  5.93 us
    ppermute x3, waiting for transfers between devices, body(): codes.append(lax.ppermute(own, ('tgt', 'rep'), perm) if k + r else own)  5.42 us
    ppermute x3, waiting for transfers between devices, body(): lax.ppermute(terms[k], 'src', [(i, (i + k) % n) for i in range(n)])  3.39 us
    pallas_call x1, Pallas kernels, body(): pl.pallas_call(functools.partial(encode_kernel, n, pieces), out_shape=[sh...  3.29 us
    pallas_call x2, Pallas kernels, add(): pl.pallas_call(functools.partial(add_kernel, n, [pieces[i] for i in some]...  1.62 us
  transfers between devices with their start and end apart: 18, of which 9 were waited for; matrix products, arithmetic and copies ran while one was open for 0% of the time, Pallas kernels for 5%

profile of v6, /device:TPU:0, one launch (start us, length us, event | category | flops | bytes accessed | tf_op | source)
XLA Modules:
  0.0 57.8 jit_solution(4686896613733044284)
XLA Ops:
  0.0 3.3 %encode.1 = (bf16[128,256]{1,0:T(8,128)(2,1)S(1)}, bf16[128,256]{1,0:T(8,128)(2,1)S(1)}, bf16[128,256]{1,0:T(8,128)(2,1)S(1)}, bf16[128,256]{1,0:T(8,128)(2,1)S(...) custom-call(bf16[2,2,64,1024]{3,2,1,0:T(8,128)(2,1)} %bitcast.3, ...), custom_call_target="tpu_custom_call" | custom-call | tf_op jit(solution)/shard_map/encode/pallas_call | solution.py:191
  3.3 3.1 %collective-permute-start = (bf16[128,256]{1,0:T(8,128)(2,1)S(1)}, bf16[128,256]{1,0:T(8,128)(2,1)S(1)}, u32[]{:S(2)}, u32[]{:S(2)}) collective-permute-start(bf16[128,256]{1,0:T(8,128)(2,1)S(1)} %get-tuple-element.26), channel_id=1, source_target_pairs={{0,4},{4,8},{8,12},{12,0},{1,5},{5,9},{9,13},{13,1},{2,6},{6,10},{... | collective-permute-start | bytes 196616 | tf_op jit(solution)/shard_map/ppermute | solution.py:210
  6.4 2.6 %collective-permute-start.1 = (bf16[128,256]{1,0:T(8,128)(2,1)S(1)}, bf16[128,256]{1,0:T(8,128)(2,1)S(1)}, u32[]{:S(2)}, u32[]{:S(2)}) collective-permute-start(bf16[128,256]{1,0:T(8,128)(2,1)S(1)} %get-tuple-element.27), channel_id=1, source_target_pairs={{0,8},{4,12},{8,0},{12,4},{1,9},{5,13},{9,1},{13,5},{2,10},{6,14},... | collective-permute-start | bytes 196616 | tf_op jit(solution)/shard_map/ppermute | solution.py:210
  9.0 1.3 %collective-permute-start.2 = (bf16[128,256]{1,0:T(8,128)(2,1)S(1)}, bf16[128,256]{1,0:T(8,128)(2,1)S(1)}, u32[]{:S(2)}, u32[]{:S(2)}) collective-permute-start(bf16[128,256]{1,0:T(8,128)(2,1)S(1)} %get-tuple-element.28), channel_id=1, source_target_pairs={{0,12},{4,0},{8,4},{12,8},{1,13},{5,1},{9,5},{13,9},{2,14},{6,2},{... | collective-permute-start | bytes 196616 | tf_op jit(solution)/shard_map/ppermute | solution.py:210
  10.3 0.7 %collective-permute-start.7 = (bf16[1,2,128,896]{3,2,1,0:T(8,128)(2,1)S(1)}, bf16[1,2,128,896]{3,2,1,0:T(8,128)(2,1)S(1)}, u32[]{:S(2)}, u32[]{:S(2)}) collective-permute-start(bf16[1,2,128,896]{3,2,1,0:T(8,128)(2,1)S(1)} %get-tuple-element.29.own_ref), channel_id=1, source_target_pairs={{0,4},{4,0},{8,12},{12,8},{1,5},{5,1},{9,13},{13,9},{2,6},{6,2},{1... | collective-permute-start | bytes 1376264 | tf_op jit(solution)/shard_map/ppermute | solution.py:259
  11.0 0.0 collective-permute-done.refs_1_
  11.0 2.5 %collective-permute-done.1.refs_2_ = bf16[128,256]{1,0:T(8,128)(2,1)S(1)} collective-permute-done((bf16[128,256]{1,0:T(8,128)(2,1)S(1)}, bf16[128,256]{1,0:T(8,128)(2,1)S(1)}, u32[]{:S(2)}, u32[]{:S(2)}) %collective-permute-start.1) | collective-permute-done | bytes 65568 | tf_op jit(solution)/shard_map/ppermute | solution.py:210
  13.4 0.9 %collective-permute-done.2.refs_3_ = bf16[128,256]{1,0:T(8,128)(2,1)S(1)} collective-permute-done((bf16[128,256]{1,0:T(8,128)(2,1)S(1)}, bf16[128,256]{1,0:T(8,128)(2,1)S(1)}, u32[]{:S(2)}, u32[]{:S(2)}) %collective-permute-start.2) | collective-permute-done | bytes 65568 | tf_op jit(solution)/shard_map/ppermute | solution.py:210
  14.4 0.0 copy-done.3
  14.4 0.0 copy-done.4
  14.4 0.6 %codes.1.refs_0_ = bf16[2,64,256]{2,1,0:T(8,128)(2,1)S(1)} custom-call(s32[2,8]{1,0:T(2,128)S(1)} %copy-done.4, f32[4,128]{1,0:T(4,128)S(1)} %bitcast.2, bf16[128,256]{1,0:T(8,128)(2,1)S(1)} %get-tuple-element.25.refs_0_, bf16[128,256]{1,0:T(8,128)(2,1)S(1)} %collective-permute-done.refs_1_, bf16[128,256]{1,0:T(8,128)(2,1)S(1)} %collective-permute-done.1.refs_2_, ...), custom_call_target="tpu_custom_call" | custom-call | tf_op jit(solution)/shard_map/codes/pallas_call | solution.py:211
  15.0 0.1 collective-permute-start.3
  15.1 1.2 %collective-permute-done.3.refs_1_ = bf16[2,64,256]{2,1,0:T(8,128)(2,1)S(1)} collective-permute-done((bf16[2,64,256]{2,1,0:T(8,128)(2,1)S(1)}, bf16[2,64,256]{2,1,0:T(8,128)(2,1)S(1)}, u32[]{:S(2)}, u32[]{:S(2)}) %collective-permute-start.3) | collective-permute-done | bytes 65568 | tf_op jit(solution)/shard_map/ppermute | solution.py:226
  16.3 0.9 %collective-permute-start.4 = (bf16[1,2,128,896]{3,2,1,0:T(8,128)(2,1)S(1)}, bf16[1,2,128,896]{3,2,1,0:T(8,128)(2,1)S(1)}, u32[]{:S(2)}, u32[]{:S(2)}) collective-permute-start(bf16[1,2,128,896]{3,2,1,0:T(8,128)(2,1)S(1)} %hold.2.own_ref), channel_id=1, source_target_pairs={{0,4},{4,0},{8,12},{12,8},{1,5},{5,1},{9,13},{13,9},{2,6},{6,2},{1... | collective-permute-start | bytes 1376264 | tf_op jit(solution)/shard_map/ppermute | solution.py:259
  17.2 1.5 %collective-permute-start.5 = (bf16[2,64,256]{2,1,0:T(8,128)(2,1)S(1)}, bf16[2,64,256]{2,1,0:T(8,128)(2,1)S(1)}, u32[]{:S(2)}, u32[]{:S(2)}) collective-permute-start(bf16[2,64,256]{2,1,0:T(8,128)(2,1)S(1)} %codes.1.refs_0_), channel_id=1, source_target_pairs={{0,2},{1,3},{2,0},{3,1},{4,6},{5,7},{6,4},{7,5},{8,10},{9,11},{10,... | collective-permute-start | bytes 196616 | tf_op jit(solution)/shard_map/ppermute | solution.py:226
  18.7 0.0 collective-permute-start.6
  18.7 2.8 %collective-permute-done.5.refs_2_ = bf16[2,64,256]{2,1,0:T(8,128)(2,1)S(1)} collective-permute-done((bf16[2,64,256]{2,1,0:T(8,128)(2,1)S(1)}, bf16[2,64,256]{2,1,0:T(8,128)(2,1)S(1)}, u32[]{:S(2)}, u32[]{:S(2)}) %collective-permute-start.5) | collective-permute-done | bytes 65568 | tf_op jit(solution)/shard_map/ppermute | solution.py:226
  21.5 1.4 %collective-permute-done.6.refs_3_ = bf16[2,64,256]{2,1,0:T(8,128)(2,1)S(1)} collective-permute-done((bf16[2,64,256]{2,1,0:T(8,128)(2,1)S(1)}, bf16[2,64,256]{2,1,0:T(8,128)(2,1)S(1)}, u32[]{:S(2)}, u32[]{:S(2)}) %collective-permute-start.6) | collective-permute-done | bytes 65568 | tf_op jit(solution)/shard_map/ppermute | solution.py:226
  22.9 1.3 %collective-permute-done.7.got_ref = bf16[1,2,128,896]{3,2,1,0:T(8,128)(2,1)S(1)} collective-permute-done((bf16[1,2,128,896]{3,2,1,0:T(8,128)(2,1)S(1)}, bf16[1,2,128,896]{3,2,1,0:T(8,128)(2,1)S(1)}, u32[]{:S(2)}, u32[]{:S(2)}) %collective-permute-start.7) | collective-permute-done | bytes 458784 | tf_op jit(solution)/shard_map/ppermute | solution.py:259
  24.2 0.5 decode.3
  24.7 1.2 %collective-permute-start.12 = (bf16[1,64,896]{2,1,0:T(8,128)(2,1)S(1)}, bf16[1,64,896]{2,1,0:T(8,128)(2,1)S(1)}, u32[]{:S(2)}, u32[]{:S(2)}) collective-permute-start(bf16[1,64,896]{2,1,0:T(8,128)(2,1)S(1)} %get-tuple-element.36), channel_id=1, source_target_pairs={{0,8},{1,9},{4,12},{5,13},{8,0},{9,1},{12,4},{13,5},{2,10},{3,11},... | collective-permute-start | bytes 344072 | tf_op jit(solution)/shard_map/ppermute | solution.py:288
  25.9 0.0 collective-permute-start.13
  25.9 1.3 %collective-permute-start.11 = (bf16[2,2,128,128]{3,2,1,0:T(8,128)(2,1)S(1)}, bf16[2,2,128,128]{3,2,1,0:T(8,128)(2,1)S(1)}, u32[]{:S(2)}, u32[]{:S(2)}) collective-permute-start(bf16[2,2,128,128]{3,2,1,0:T(8,128)(2,1)S(1)} %hold.3), channel_id=1, source_target_pairs={{0,4},{4,0},{8,12},{12,8},{1,5},{5,1},{9,13},{13,9},{2,6},{6,2},{1... | collective-permute-start | bytes 393224 | tf_op jit(solution)/shard_map/ppermute | solution.py:280
  27.2 1.4 %collective-permute-start.14 = (bf16[1,64,896]{2,1,0:T(8,128)(2,1)S(1)}, bf16[1,64,896]{2,1,0:T(8,128)(2,1)S(1)}, u32[]{:S(2)}, u32[]{:S(2)}) collective-permute-start(bf16[1,64,896]{2,1,0:T(8,128)(2,1)S(1)} %get-tuple-element.38), channel_id=1, source_target_pairs={{0,9},{1,8},{4,13},{5,12},{8,1},{9,0},{12,5},{13,4},{2,11},{3,10},... | collective-permute-start | bytes 344072 | tf_op jit(solution)/shard_map/ppermute | solution.py:288
  28.6 10.4 %collective-permute-done.4.got_ref = bf16[1,2,128,896]{3,2,1,0:T(8,128)(2,1)S(1)} collective-permute-done((bf16[1,2,128,896]{3,2,1,0:T(8,128)(2,1)S(1)}, bf16[1,2,128,896]{3,2,1,0:T(8,128)(2,1)S(1)}, u32[]{:S(2)}, u32[]{:S(2)}) %collective-permute-start.4) | collective-permute-done | bytes 458784 | tf_op jit(solution)/shard_map/ppermute | solution.py:259
  39.0 0.5 decode.4
  39.4 0.1 collective-permute-start.10
  39.5 0.0 collective-permute-done.12.refs_1_
  39.5 0.9 %collective-permute-start.8 = (bf16[1,64,896]{2,1,0:T(8,128)(2,1)S(1)}, bf16[1,64,896]{2,1,0:T(8,128)(2,1)S(1)}, u32[]{:S(2)}, u32[]{:S(2)}) collective-permute-start(bf16[1,64,896]{2,1,0:T(8,128)(2,1)S(1)} %get-tuple-element.32), channel_id=1, source_target_pairs={{0,8},{1,9},{4,12},{5,13},{8,0},{9,1},{12,4},{13,5},{2,10},{3,11},... | collective-permute-start | bytes 344072 | tf_op jit(solution)/shard_map/ppermute | solution.py:288
  40.4 0.0 collective-permute-done.13.refs_2_
  40.5 1.8 %collective-permute-start.9 = (bf16[1,64,896]{2,1,0:T(8,128)(2,1)S(1)}, bf16[1,64,896]{2,1,0:T(8,128)(2,1)S(1)}, u32[]{:S(2)}, u32[]{:S(2)}) collective-permute-start(bf16[1,64,896]{2,1,0:T(8,128)(2,1)S(1)} %get-tuple-element.33), channel_id=1, source_target_pairs={{0,1},{1,0},{4,5},{5,4},{8,9},{9,8},{12,13},{13,12},{2,3},{3,2},{6... | collective-permute-start | bytes 344072 | tf_op jit(solution)/shard_map/ppermute | solution.py:288
  42.3 0.0 collective-permute-done.14.refs_3_
  42.3 0.0 copy-done.1
  42.3 0.8 %add.2.refs_5_.refs_8_ = bf16[2,64,2048]{2,1,0:T(8,128)(2,1)} custom-call(f32[2,2048]{1,0:T(2,128)S(1)} %copy-done.2, bf16[2,64,2048]{2,1,0:T(8,128)(2,1)S(1)} %copy-done.1, f32[1,64,896]{2,1,0:T(8,128)S(1)} %get-tuple-element.30.refs_4_.refs_1_.refs_0_, bf16[1,64,896]{2,1,0:T(8,128)(2,1)S(1)} %collective-permute-done.12.refs_1_, ...), custom_call_target="tpu_custom_call" | custom-call | tf_op jit(solution)/shard_map/add/pallas_call | solution.py:243
  43.1 0.0 collective-permute-done.11.got_ref
  43.1 0.0 copy-start
  43.1 1.0 %copy-done = bf16[2,64,2048]{2,1,0:T(8,128)(2,1)S(1)} copy-done((bf16[2,64,2048]{2,1,0:T(8,128)(2,1)S(1)}, bf16[2,64,2048]{2,1,0:T(8,128)(2,1)}, u32[]{:S(2)}) %copy-start) | copy-done | bytes 524312
  44.1 0.3 decode.5
  44.5 0.4 collective-permute-start.15
  44.9 0.1 collective-permute-start.16
  45.0 7.7 %collective-permute-done.15.refs_5_ = bf16[2,64,128]{2,1,0:T(8,128)(2,1)S(1)} collective-permute-done((bf16[2,64,128]{2,1,0:T(8,128)(2,1)S(1)}, bf16[2,64,128]{2,1,0:T(8,128)(2,1)S(1)}, u32[]{:S(2)}, u32[]{:S(2)}) %collective-permute-start.15) | collective-permute-done | bytes 32800 | tf_op jit(solution)/shard_map/ppermute | solution.py:288
  52.7 0.0 collective-permute-start.17
  52.7 0.0 collective-permute-done.16.refs_6_
  52.7 4.2 %collective-permute-done.17.refs_7_ = bf16[2,64,128]{2,1,0:T(8,128)(2,1)S(1)} collective-permute-done((bf16[2,64,128]{2,1,0:T(8,128)(2,1)S(1)}, bf16[2,64,128]{2,1,0:T(8,128)(2,1)S(1)}, u32[]{:S(2)}, u32[]{:S(2)}) %collective-permute-start.17) | collective-permute-done | bytes 32800 | tf_op jit(solution)/shard_map/ppermute | solution.py:288
  56.9 0.0 collective-permute-done.10.refs_3_
  56.9 0.0 collective-permute-done.8.refs_1_
  56.9 0.0 collective-permute-done.9.refs_2_
  56.9 0.8 %add.3 = bf16[2,64,2048]{2,1,0:T(8,128)(2,1)} custom-call(f32[2,2048]{1,0:T(2,128)S(1)} %copy-done.2, bf16[2,64,2048]{2,1,0:T(8,128)(2,1)S(1)} %copy-done.1, f32[1,64,896]{2,1,0:T(8,128)S(1)} %get-tuple-element.31.refs_4_.refs_0_, bf16[1,64,896]{2,1,0:T(8,128)(2,1)S(1)} %collective-permute-done.8.refs_1_, ...), custom_call_target="tpu_custom_call", output_to_operand_aliasing={{}: (10, {})} | custom-call | tf_op jit(solution)/shard_map/add/pallas_call | solution.py:243
  (8 shorter events, 0.0 us)
Async XLA Ops:
  0.0 14.4 %copy-start.3 = (f32[512]{0:T(512)S(1)}, f32[512]{0:T(512)}, u32[]{:S(2)}) copy-start(f32[512]{0:T(512)} %param.9) | copy-start | bytes 6148
  0.0 14.4 %copy-start.4 = (s32[2,8]{1,0:T(2,128)S(1)}, s32[2,8]{1,0:T(2,128)}, u32[]{:S(2)}) copy-start(s32[2,8]{1,0:T(2,128)} %active_ref.1) | copy-start | bytes 196
  3.3 7.7 %collective-permute-start = (bf16[128,256]{1,0:T(8,128)(2,1)S(1)}, bf16[128,256]{1,0:T(8,128)(2,1)S(1)}, u32[]{:S(2)}, u32[]{:S(2)}) collective-permute-start(bf16[128,256]{1,0:T(8,128)(2,1)S(1)} %get-tuple-element.26), channel_id=1, source_target_pairs={{0,4},{4,8},{8,12},{12,0},{1,5},{5,9},{9,13},{13,1},{2,6},{6,10},{... | collective-permute-start | bytes 196616 | tf_op jit(solution)/shard_map/ppermute | solution.py:210
  6.4 7.1 %collective-permute-start.1 = (bf16[128,256]{1,0:T(8,128)(2,1)S(1)}, bf16[128,256]{1,0:T(8,128)(2,1)S(1)}, u32[]{:S(2)}, u32[]{:S(2)}) collective-permute-start(bf16[128,256]{1,0:T(8,128)(2,1)S(1)} %get-tuple-element.27), channel_id=1, source_target_pairs={{0,8},{4,12},{8,0},{12,4},{1,9},{5,13},{9,1},{13,5},{2,10},{6,14},... | collective-permute-start | bytes 196616 | tf_op jit(solution)/shard_map/ppermute | solution.py:210
  9.0 5.4 %collective-permute-start.2 = (bf16[128,256]{1,0:T(8,128)(2,1)S(1)}, bf16[128,256]{1,0:T(8,128)(2,1)S(1)}, u32[]{:S(2)}, u32[]{:S(2)}) collective-permute-start(bf16[128,256]{1,0:T(8,128)(2,1)S(1)} %get-tuple-element.28), channel_id=1, source_target_pairs={{0,12},{4,0},{8,4},{12,8},{1,13},{5,1},{9,5},{13,9},{2,14},{6,2},{... | collective-permute-start | bytes 196616 | tf_op jit(solution)/shard_map/ppermute | solution.py:210
  10.3 13.9 %collective-permute-start.7 = (bf16[1,2,128,896]{3,2,1,0:T(8,128)(2,1)S(1)}, bf16[1,2,128,896]{3,2,1,0:T(8,128)(2,1)S(1)}, u32[]{:S(2)}, u32[]{:S(2)}) collective-permute-start(bf16[1,2,128,896]{3,2,1,0:T(8,128)(2,1)S(1)} %get-tuple-element.29.own_ref), channel_id=1, source_target_pairs={{0,4},{4,0},{8,12},{12,8},{1,5},{5,1},{9,13},{13,9},{2,6},{6,2},{1... | collective-permute-start | bytes 1376264 | tf_op jit(solution)/shard_map/ppermute | solution.py:259
  15.0 1.3 %collective-permute-start.3 = (bf16[2,64,256]{2,1,0:T(8,128)(2,1)S(1)}, bf16[2,64,256]{2,1,0:T(8,128)(2,1)S(1)}, u32[]{:S(2)}, u32[]{:S(2)}) collective-permute-start(bf16[2,64,256]{2,1,0:T(8,128)(2,1)S(1)} %codes.1.refs_0_), channel_id=1, source_target_pairs={{0,1},{1,0},{2,3},{3,2},{4,5},{5,4},{6,7},{7,6},{8,9},{9,8},{10,11... | collective-permute-start | bytes 196616 | tf_op jit(solution)/shard_map/ppermute | solution.py:226
  16.3 25.9 %copy-start.1 = (bf16[2,64,2048]{2,1,0:T(8,128)(2,1)S(1)}, bf16[2,64,2048]{2,1,0:T(8,128)(2,1)}, u32[]{:S(2)}) copy-start(bf16[2,64,2048]{2,1,0:T(8,128)(2,1)} %target_ref.3) | copy-start | bytes 1572868
  16.3 25.9 %copy-start.2 = (f32[2,2048]{1,0:T(2,128)S(1)}, f32[2,2048]{1,0:T(2,128)}, u32[]{:S(2)}) copy-start(f32[2,2048]{1,0:T(2,128)} %bias_ref.3) | copy-start | bytes 49156
  16.3 22.6 %collective-permute-start.4 = (bf16[1,2,128,896]{3,2,1,0:T(8,128)(2,1)S(1)}, bf16[1,2,128,896]{3,2,1,0:T(8,128)(2,1)S(1)}, u32[]{:S(2)}, u32[]{:S(2)}) collective-permute-start(bf16[1,2,128,896]{3,2,1,0:T(8,128)(2,1)S(1)} %hold.2.own_ref), channel_id=1, source_target_pairs={{0,4},{4,0},{8,12},{12,8},{1,5},{5,1},{9,13},{13,9},{2,6},{6,2},{1... | collective-permute-start | bytes 1376264 | tf_op jit(solution)/shard_map/ppermute | solution.py:259
  17.2 4.3 %collective-permute-start.5 = (bf16[2,64,256]{2,1,0:T(8,128)(2,1)S(1)}, bf16[2,64,256]{2,1,0:T(8,128)(2,1)S(1)}, u32[]{:S(2)}, u32[]{:S(2)}) collective-permute-start(bf16[2,64,256]{2,1,0:T(8,128)(2,1)S(1)} %codes.1.refs_0_), channel_id=1, source_target_pairs={{0,2},{1,3},{2,0},{3,1},{4,6},{5,7},{6,4},{7,5},{8,10},{9,11},{10,... | collective-permute-start | bytes 196616 | tf_op jit(solution)/shard_map/ppermute | solution.py:226
  18.7 4.2 %collective-permute-start.6 = (bf16[2,64,256]{2,1,0:T(8,128)(2,1)S(1)}, bf16[2,64,256]{2,1,0:T(8,128)(2,1)S(1)}, u32[]{:S(2)}, u32[]{:S(2)}) collective-permute-start(bf16[2,64,256]{2,1,0:T(8,128)(2,1)S(1)} %codes.1.refs_0_), channel_id=1, source_target_pairs={{0,3},{1,2},{2,1},{3,0},{4,7},{5,6},{6,5},{7,4},{8,11},{9,10},{10,... | collective-permute-start | bytes 196616 | tf_op jit(solution)/shard_map/ppermute | solution.py:226
  24.7 14.8 %collective-permute-start.12 = (bf16[1,64,896]{2,1,0:T(8,128)(2,1)S(1)}, bf16[1,64,896]{2,1,0:T(8,128)(2,1)S(1)}, u32[]{:S(2)}, u32[]{:S(2)}) collective-permute-start(bf16[1,64,896]{2,1,0:T(8,128)(2,1)S(1)} %get-tuple-element.36), channel_id=1, source_target_pairs={{0,8},{1,9},{4,12},{5,13},{8,0},{9,1},{12,4},{13,5},{2,10},{3,11},... | collective-permute-start | bytes 344072 | tf_op jit(solution)/shard_map/ppermute | solution.py:288
  25.9 14.6 %collective-permute-start.13 = (bf16[1,64,896]{2,1,0:T(8,128)(2,1)S(1)}, bf16[1,64,896]{2,1,0:T(8,128)(2,1)S(1)}, u32[]{:S(2)}, u32[]{:S(2)}) collective-permute-start(bf16[1,64,896]{2,1,0:T(8,128)(2,1)S(1)} %get-tuple-element.37), channel_id=1, source_target_pairs={{0,1},{1,0},{4,5},{5,4},{8,9},{9,8},{12,13},{13,12},{2,3},{3,2},{6... | collective-permute-start | bytes 344072 | tf_op jit(solution)/shard_map/ppermute | solution.py:288
  25.9 17.2 %collective-permute-start.11 = (bf16[2,2,128,128]{3,2,1,0:T(8,128)(2,1)S(1)}, bf16[2,2,128,128]{3,2,1,0:T(8,128)(2,1)S(1)}, u32[]{:S(2)}, u32[]{:S(2)}) collective-permute-start(bf16[2,2,128,128]{3,2,1,0:T(8,128)(2,1)S(1)} %hold.3), channel_id=1, source_target_pairs={{0,4},{4,0},{8,12},{12,8},{1,5},{5,1},{9,13},{13,9},{2,6},{6,2},{1... | collective-permute-start | bytes 393224 | tf_op jit(solution)/shard_map/ppermute | solution.py:280
  27.2 15.1 %collective-permute-start.14 = (bf16[1,64,896]{2,1,0:T(8,128)(2,1)S(1)}, bf16[1,64,896]{2,1,0:T(8,128)(2,1)S(1)}, u32[]{:S(2)}, u32[]{:S(2)}) collective-permute-start(bf16[1,64,896]{2,1,0:T(8,128)(2,1)S(1)} %get-tuple-element.38), channel_id=1, source_target_pairs={{0,9},{1,8},{4,13},{5,12},{8,1},{9,0},{12,5},{13,4},{2,11},{3,10},... | collective-permute-start | bytes 344072 | tf_op jit(solution)/shard_map/ppermute | solution.py:288
  39.4 17.5 %collective-permute-start.10 = (bf16[1,64,896]{2,1,0:T(8,128)(2,1)S(1)}, bf16[1,64,896]{2,1,0:T(8,128)(2,1)S(1)}, u32[]{:S(2)}, u32[]{:S(2)}) collective-permute-start(bf16[1,64,896]{2,1,0:T(8,128)(2,1)S(1)} %get-tuple-element.34), channel_id=1, source_target_pairs={{0,9},{1,8},{4,13},{5,12},{8,1},{9,0},{12,5},{13,4},{2,11},{3,10},... | collective-permute-start | bytes 344072 | tf_op jit(solution)/shard_map/ppermute | solution.py:288
  39.5 17.4 %collective-permute-start.8 = (bf16[1,64,896]{2,1,0:T(8,128)(2,1)S(1)}, bf16[1,64,896]{2,1,0:T(8,128)(2,1)S(1)}, u32[]{:S(2)}, u32[]{:S(2)}) collective-permute-start(bf16[1,64,896]{2,1,0:T(8,128)(2,1)S(1)} %get-tuple-element.32), channel_id=1, source_target_pairs={{0,8},{1,9},{4,12},{5,13},{8,0},{9,1},{12,4},{13,5},{2,10},{3,11},... | collective-permute-start | bytes 344072 | tf_op jit(solution)/shard_map/ppermute | solution.py:288
  40.5 16.5 %collective-permute-start.9 = (bf16[1,64,896]{2,1,0:T(8,128)(2,1)S(1)}, bf16[1,64,896]{2,1,0:T(8,128)(2,1)S(1)}, u32[]{:S(2)}, u32[]{:S(2)}) collective-permute-start(bf16[1,64,896]{2,1,0:T(8,128)(2,1)S(1)} %get-tuple-element.33), channel_id=1, source_target_pairs={{0,1},{1,0},{4,5},{5,4},{8,9},{9,8},{12,13},{13,12},{2,3},{3,2},{6... | collective-permute-start | bytes 344072 | tf_op jit(solution)/shard_map/ppermute | solution.py:288
  43.1 1.0 %copy-start = (bf16[2,64,2048]{2,1,0:T(8,128)(2,1)S(1)}, bf16[2,64,2048]{2,1,0:T(8,128)(2,1)}, u32[]{:S(2)}) copy-start(bf16[2,64,2048]{2,1,0:T(8,128)(2,1)} %add.2.refs_5_.refs_8_) | copy-start | bytes 1572868
  44.5 8.2 %collective-permute-start.15 = (bf16[2,64,128]{2,1,0:T(8,128)(2,1)S(1)}, bf16[2,64,128]{2,1,0:T(8,128)(2,1)S(1)}, u32[]{:S(2)}, u32[]{:S(2)}) collective-permute-start(bf16[2,64,128]{2,1,0:T(8,128)(2,1)S(1)} %get-tuple-element.40), channel_id=1, source_target_pairs={{0,8},{1,9},{4,12},{5,13},{8,0},{9,1},{12,4},{13,5},{2,10},{3,11},... | collective-permute-start | bytes 98312 | tf_op jit(solution)/shard_map/ppermute | solution.py:288
  44.9 7.8 %collective-permute-start.16 = (bf16[2,64,128]{2,1,0:T(8,128)(2,1)S(1)}, bf16[2,64,128]{2,1,0:T(8,128)(2,1)S(1)}, u32[]{:S(2)}, u32[]{:S(2)}) collective-permute-start(bf16[2,64,128]{2,1,0:T(8,128)(2,1)S(1)} %get-tuple-element.41), channel_id=1, source_target_pairs={{0,1},{1,0},{4,5},{5,4},{8,9},{9,8},{12,13},{13,12},{2,3},{3,2},{6... | collective-permute-start | bytes 98312 | tf_op jit(solution)/shard_map/ppermute | solution.py:288
  52.7 4.3 %collective-permute-start.17 = (bf16[2,64,128]{2,1,0:T(8,128)(2,1)S(1)}, bf16[2,64,128]{2,1,0:T(8,128)(2,1)S(1)}, u32[]{:S(2)}, u32[]{:S(2)}) collective-permute-start(bf16[2,64,128]{2,1,0:T(8,128)(2,1)S(1)} %get-tuple-element.42), channel_id=1, source_target_pairs={{0,9},{1,8},{4,13},{5,12},{8,1},{9,0},{12,5},{13,4},{2,11},{3,10},... | collective-permute-start | bytes 98312 | tf_op jit(solution)/shard_map/ppermute | solution.py:288

commit v7 on v6

--- a/solution.py
+++ b/solution.py
@@ -9,16 +9,18 @@
 
 VMEM_BYTES = 32 * 1024 * 1024
 LANES = 128
-FIRST = 7
+FIRST = 4
 
 
 def cut_pieces(layers, columns):
     tiles = columns // LANES
     first = -(-tiles * FIRST // 8)
-    pieces = [((layer,), 0, first * LANES) for layer in range(layers)]
-    if first < tiles:
-        pieces.append((tuple(range(layers)), first * LANES, (tiles - first) * LANES))
-    return pieces
+    every = tuple(range(layers))
+    return [
+        (every, start * LANES, (stop - start) * LANES)
+        for start, stop in ((0, first), (first, tiles))
+        if stop > start
+    ]
 
 
 def part_copies(piece, dec_hbm, part_ref, sems):
@@ -58,6 +60,8 @@
         copy.wait()
     copies_part = []
     for i, piece in enumerate(pieces):
+        if i == 0:
+            piece = ((lax.axis_index("parts"),), *piece[1:])
         copies_part += part_copies(piece, dec_hbm, part_refs[i], part_sems.at[i])
     src = lax.axis_index("src")
     for k in range(n):
@@ -72,8 +76,9 @@
         copy.wait()
 
 
-def codes_kernel(n, share, tile_rows, active_ref, bias_ref, *refs):
-    term_refs, out_ref = refs[:n], refs[n]
+def codes_kernel(n, share, tile_rows, piece, active_ref, bias_ref, *refs):
+    term_refs, (dec_hbm, out_ref, part_ref, part_sems) = refs[:n], refs[n:]
+    copies_part = part_copies(piece, dec_hbm, part_ref, part_sems)
     src = lax.axis_index("src")
     tgt = lax.axis_index("tgt")
     parity, half = lax.rem(src, 2), src // 2
@@ -106,11 +111,14 @@
             rows = slice(group * share, (group + 1) * share)
             value = live * jnp.maximum(pre[rows, columns] + bias, 0.0)
             out_ref[group, :, columns] = value.astype(jnp.bfloat16)
-
-
-def decode_kernel(n, own_ref, got_ref, *refs):
+    for copy in copies_part:
+        copy.wait()
+
+
+def decode_kernel(n, shared, own_ref, *refs):
     half = n // 2
     layers, groups, block, width = own_ref.shape
+    got_refs, refs = refs[: 1 + shared], refs[1 + shared :]
     code_refs, out_refs, lhs_ref = refs[: 2 * groups], refs[-2 * half - 1 : -1], refs[-1]
     src, tgt = lax.axis_index("src"), lax.axis_index("tgt")
     parity = lax.rem(src, 2)
@@ -127,16 +135,17 @@
                 for r in range(2):
                     rows = slice((2 * j + r) * share, (2 * j + r + 1) * share)
                     lhs_ref[rows, columns] = code_refs[2 * k + r][group, :, latents]
-    for layer in range(layers):
+    for i in range(layers):
+        layer = lax.rem(lax.axis_index("parts") + i, layers) if shared else i
         own = own_ref[layer].reshape(depth, width)
-        got = got_ref[layer].reshape(depth, width)
+        got = (got_refs[i][0] if shared else got_refs[0][i]).reshape(depth, width)
         total = jnp.dot(lhs_ref[:, :depth], own, preferred_element_type=jnp.float32)
         total += jnp.dot(lhs_ref[:, depth:], got, preferred_element_type=jnp.float32)
-        for i, ref in enumerate(out_refs):
-            ref[layer] = total[i * share : (i + 1) * share].astype(ref.dtype)
-
-
-def add_kernel(n, pieces, chained, bias_ref, target_ref, *refs):
+        for j, ref in enumerate(out_refs):
+            ref[layer] = total[j * share : (j + 1) * share].astype(ref.dtype)
+
+
+def add_kernel(n, pieces, bias_ref, target_ref, *refs):
     out_hbm, out_ref, sems = refs[-3:]
     half = n // 2
     cols = target_ref.shape[2]
@@ -191,7 +200,10 @@
     results = pl.pallas_call(
         functools.partial(encode_kernel, n, pieces),
         out_shape=[shape(half * share, 2 * block)] * n
-        + [shape(len(which), groups, block, width) for which, _, width in pieces],
+        + [
+            shape(1 if i == 0 else layers, groups, block, width)
+            for i, (_, _, width) in enumerate(pieces)
+        ],
         in_specs=[anywhere] * 3,
         out_specs=[vmem] * (n + len(pieces)),
         scratch_shapes=[
@@ -208,15 +220,19 @@
     terms, parts = list(results[:n]), list(results[n:])
     for k in range(1, n):
         terms[k] = lax.ppermute(terms[k], "src", [(i, (i + k) % n) for i in range(n)])
-    own = pl.pallas_call(
-        functools.partial(codes_kernel, n, share, tile_rows),
-        out_shape=shape(half, share, 2 * block),
-        in_specs=[smem] + [vmem] * (1 + n),
-        out_specs=vmem,
+    own, own_part = pl.pallas_call(
+        functools.partial(codes_kernel, n, share, tile_rows, pieces[0]),
+        out_shape=[
+            shape(half, share, 2 * block),
+            shape(layers, groups, block, pieces[0][2]),
+        ],
+        in_specs=[smem] + [vmem] * (1 + n) + [anywhere],
+        out_specs=[vmem] * 2,
+        scratch_shapes=[pltpu.SemaphoreType.DMA((layers * groups,))],
         compiler_params=params,
         cost_estimate=cost,
         name="codes",
-    )(active, enc_b.reshape(n, block), *terms)
+    )(active, enc_b.reshape(n, block), *terms, dec_w)
     codes = []
     for k in range(groups):
         for r in range(2):
@@ -237,57 +253,47 @@
             name="hold",
         )(value, after)
 
-    def add(some, out):
-        chained = [] if out is None else [out]
-        operands = [value for i in some for value in sums[i]]
-        return pl.pallas_call(
-            functools.partial(add_kernel, n, [pieces[i] for i in some], len(chained)),
-            out_shape=shape(layers, share, cols),
-            in_specs=[vmem] * (2 + len(operands)) + [anywhere] * len(chained),
-            out_specs=anywhere,
-            scratch_shapes=[
-                pltpu.VMEM((layers, share, cols), jnp.bfloat16),
-                pltpu.SemaphoreType.DMA((2 * len(some) * layers,)),
-            ],
-            input_output_aliases={2 + len(operands): 0} if chained else {},
-            compiler_params=params,
-            cost_estimate=cost,
-            name="add",
-        )(dec_b, targets, *operands, *chained)
-
-    parts[1:layers] = [hold(part, codes[1]) for part in parts[1:layers]]
-    got = [lax.ppermute(part, "src", pair) for part in parts[:layers]]
-    sums, after, out = [], [], None
-    for i, (which, _, width) in enumerate(pieces):
-        if i == layers:
-            out = add([0], None)
-            after.append(out)
-        shapes = [shape(len(which), share, width)] * (2 * half)
-        shapes[0] = shape(len(which), share, width, kind=jnp.float32)
+    got = [[lax.ppermute(parts[0], "src", pair)]]
+    got[0].append(lax.ppermute(got[0][0], "parts", [(0, 1), (1, 0)]))
+    for part in parts[1:]:
+        got.append([lax.ppermute(hold(part, codes[1]), "src", pair)])
+    parts[0] = own_part
+    sums, after = [], []
+    for i, (_, _, width) in enumerate(pieces):
+        shapes = [shape(layers, share, width)] * (2 * half)
+        shapes[0] = shape(layers, share, width, kind=jnp.float32)
         terms = pl.pallas_call(
-            functools.partial(decode_kernel, n),
+            functools.partial(decode_kernel, n, i == 0),
             out_shape=shapes,
-            in_specs=[vmem] * (2 + 2 * groups) + [anywhere] * len(after),
+            in_specs=[vmem] * (1 + len(got[i]) + 2 * groups) + [anywhere] * len(after),
             out_specs=[vmem] * len(shapes),
             scratch_shapes=[pltpu.VMEM((rows, 2 * groups * block), jnp.bfloat16)],
             compiler_params=params,
             cost_estimate=cost,
             name="decode",
-        )(parts[i], got[i], *codes, *after)
+        )(parts[i], *got[i], *codes, *after)
         after = [terms[0]]
-        if i == 0:
-            for part in parts[layers:]:
-                got.append(lax.ppermute(hold(part, terms[0]), "src", pair))
-        sums.append([])
         for r in range(2):
             for j in range(half):
                 perm = [
                     (d * 2 + c, (d + 2 * j) % n * 2 + (c ^ r)) for d in range(n) for c in range(2)
                 ]
                 term = terms[2 * j + r]
-                sums[i].append(lax.ppermute(term, ("src", "rep"), perm) if j + r else term)
-    rest = range(0 if out is None else 1, len(pieces))
-    return add(list(rest), out)
+                sums.append(lax.ppermute(term, ("src", "rep"), perm) if j + r else term)
+
+    return pl.pallas_call(
+        functools.partial(add_kernel, n, pieces),
+        out_shape=shape(layers, share, cols),
+        in_specs=[vmem] * (2 + len(sums)),
+        out_specs=anywhere,
+        scratch_shapes=[
+            pltpu.VMEM((layers, share, cols), jnp.bfloat16),
+            pltpu.SemaphoreType.DMA((2 * len(pieces) * layers,)),
+        ],
+        compiler_params=params,
+        cost_estimate=cost,
+        name="add",
+    )(dec_b, targets, *sums)
 
 
 def solution(mesh):

time: 58 us -> 53.4 us (0.921)
  starting transfers between devices: 17.4 us -> 15.5 us
  waiting for transfers between devices: 32.4 us -> 30.7 us
  local copies, waits for them, and re-layouts: 1.06 us -> 0.06 us
    ppermute x12 -> x9, starting transfers between devices: 8.8 us -> 6.9 us  [the longest x6 3.84 us: body(): sums.append(lax.ppermute(term, ('src', 'rep'), perm) if j + r else term)]
    ppermute x12 -> x9, waiting for transfers between devices: 23.6 us -> 21.9 us  [the longest x6 17.7 us: body(): sums.append(lax.ppermute(term, ('src', 'rep'), perm) if j + r else term)]
    unnamed x11 -> x9, local copies, waits for them, and re-layouts: 1.06 us -> 0.06 us
    pallas_call x6 -> x4, Pallas kernels: 3.51 us -> 3.54 us  [the longest x1 1.69 us: body(): pl.pallas_call(functools.partial(codes_kernel, n, share, tile_rows, piece...]
  transfers between devices with their start and end apart: 18 -> 15, of which waited for: 9 -> 12; matrix products, arithmetic and copies ran while one was open for 0% -> 0% of each run, Pallas kernels for 5% -> 5%
where the time goes in v7:
time: 53.4 us; the launch traced here: 53 us
  waiting for transfers between devices  30.7 us (57%)
  starting transfers between devices  15.5 us (29%)
  Pallas kernels  6.72 us (13%)
    ppermute x6, waiting for transfers between devices, body(): sums.append(lax.ppermute(term, ('src', 'rep'), perm) if j + r else term)  17.7 us
    ppermute x3, starting transfers between devices, body(): lax.ppermute(terms[k], 'src', [(i, (i + k) % n) for i in range(n)])  7 us
    ppermute x3, waiting for transfers between devices, body(): codes.append(lax.ppermute(own, ('tgt', 'rep'), perm) if k + r else own)  5.45 us
    ppermute x6, starting transfers between devices, body(): sums.append(lax.ppermute(term, ('src', 'rep'), perm) if j + r else term)  3.84 us
    ppermute x3, waiting for transfers between devices, body(): lax.ppermute(terms[k], 'src', [(i, (i + k) % n) for i in range(n)])  3.39 us
    pallas_call x1, Pallas kernels, body(): pl.pallas_call(functools.partial(encode_kernel, n, pieces), out_shape=[sh...  3.17 us
    ppermute x1, waiting for transfers between devices, body(): got.append([lax.ppermute(hold(part, codes[1]), 'src', pair)])  3.11 us
    pallas_call x1, Pallas kernels, body(): pl.pallas_call(functools.partial(codes_kernel, n, share, tile_rows, piece...  1.69 us
  transfers between devices with their start and end apart: 15, of which 12 were waited for; matrix products, arithmetic and copies ran while one was open for 0% of the time, Pallas kernels for 5%

profile of v7, /device:TPU:0, one launch (start us, length us, event | category | flops | bytes accessed | tf_op | source)
XLA Modules:
  0.0 53.0 jit_solution(8980760331613962064)
XLA Ops:
  0.0 0.0 copy-start.3
  0.0 0.0 copy-start.2
  0.0 3.2 %encode.1 = (bf16[128,256]{1,0:T(8,128)(2,1)S(1)}, bf16[128,256]{1,0:T(8,128)(2,1)S(1)}, bf16[128,256]{1,0:T(8,128)(2,1)S(1)}, bf16[128,256]{1,0:T(8,128)(2,1)S(...) custom-call(bf16[2,2,64,1024]{3,2,1,0:T(8,128)(2,1)} %bitcast.3, bf16[1024,512]{1,0:T(8,128)(2,1)} %w_hbm.1, ...), custom_call_target="tpu_custom_call" | custom-call | tf_op jit(solution)/shard_map/encode/pallas_call | solution.py:200
  3.2 3.1 %collective-permute-start = (bf16[128,256]{1,0:T(8,128)(2,1)S(1)}, bf16[128,256]{1,0:T(8,128)(2,1)S(1)}, u32[]{:S(2)}, u32[]{:S(2)}) collective-permute-start(bf16[128,256]{1,0:T(8,128)(2,1)S(1)} %get-tuple-element.22), channel_id=1, source_target_pairs={{0,4},{4,8},{8,12},{12,0},{1,5},{5,9},{9,13},{13,1},{2,6},{6,10},{... | collective-permute-start | bytes 196616 | tf_op jit(solution)/shard_map/ppermute | solution.py:222
  6.3 2.6 %collective-permute-start.1 = (bf16[128,256]{1,0:T(8,128)(2,1)S(1)}, bf16[128,256]{1,0:T(8,128)(2,1)S(1)}, u32[]{:S(2)}, u32[]{:S(2)}) collective-permute-start(bf16[128,256]{1,0:T(8,128)(2,1)S(1)} %get-tuple-element.23), channel_id=1, source_target_pairs={{0,8},{4,12},{8,0},{12,4},{1,9},{5,13},{9,1},{13,5},{2,10},{6,14},... | collective-permute-start | bytes 196616 | tf_op jit(solution)/shard_map/ppermute | solution.py:222
  8.8 1.3 %collective-permute-start.2 = (bf16[128,256]{1,0:T(8,128)(2,1)S(1)}, bf16[128,256]{1,0:T(8,128)(2,1)S(1)}, u32[]{:S(2)}, u32[]{:S(2)}) collective-permute-start(bf16[128,256]{1,0:T(8,128)(2,1)S(1)} %get-tuple-element.24), channel_id=1, source_target_pairs={{0,12},{4,0},{8,4},{12,8},{1,13},{5,1},{9,5},{13,9},{2,14},{6,2},{... | collective-permute-start | bytes 196616 | tf_op jit(solution)/shard_map/ppermute | solution.py:222
  10.2 0.7 %collective-permute-start.3 = (bf16[1,2,128,512]{3,2,1,0:T(8,128)(2,1)S(1)}, bf16[1,2,128,512]{3,2,1,0:T(8,128)(2,1)S(1)}, u32[]{:S(2)}, u32[]{:S(2)}) collective-permute-start(bf16[1,2,128,512]{3,2,1,0:T(8,128)(2,1)S(1)} %get-tuple-element.26), channel_id=1, source_target_pairs={{0,4},{4,0},{8,12},{12,8},{1,5},{5,1},{9,13},{13,9},{2,6},{6,2},{1... | collective-permute-start | bytes 786440 | tf_op jit(solution)/shard_map/ppermute | solution.py:256
  10.9 0.0 collective-permute-done.refs_1_
  10.9 2.5 %collective-permute-done.1.refs_2_ = bf16[128,256]{1,0:T(8,128)(2,1)S(1)} collective-permute-done((bf16[128,256]{1,0:T(8,128)(2,1)S(1)}, bf16[128,256]{1,0:T(8,128)(2,1)S(1)}, u32[]{:S(2)}, u32[]{:S(2)}) %collective-permute-start.1) | collective-permute-done | bytes 65568 | tf_op jit(solution)/shard_map/ppermute | solution.py:222
  13.3 0.9 %collective-permute-done.2.refs_3_ = bf16[128,256]{1,0:T(8,128)(2,1)S(1)} collective-permute-done((bf16[128,256]{1,0:T(8,128)(2,1)S(1)}, bf16[128,256]{1,0:T(8,128)(2,1)S(1)}, u32[]{:S(2)}, u32[]{:S(2)}) %collective-permute-start.2) | collective-permute-done | bytes 65568 | tf_op jit(solution)/shard_map/ppermute | solution.py:222
  14.3 0.0 copy-done.3
  14.3 0.0 copy-done.2
  14.3 1.7 %codes.1 = (bf16[2,64,256]{2,1,0:T(8,128)(2,1)S(1)}, bf16[2,2,128,512]{3,2,1,0:T(8,128)(2,1)S(1)}) custom-call(s32[2,8]{1,0:T(2,128)S(1)} %copy-done.3, f32[4,128]{1,0:T(4,128)S(1)} %bitcast.2, bf16[128,256]{1,0:T(8,128)(2,1)S(1)} %get-tuple-element.21.refs_0_, bf16[128,256]{1,0:T(8,128)(2,1)S(1)} %collective-permute-done.refs_1_, ...), custom_call_target="tpu_custom_call" | custom-call | tf_op jit(solution)/shard_map/codes/pallas_call | solution.py:223
  16.0 0.1 collective-permute-start.5
  16.1 0.0 copy-start
  16.1 0.0 copy-start.1
  16.1 1.2 %collective-permute-done.5.refs_3_.refs_1_.refs_2_ = bf16[2,64,256]{2,1,0:T(8,128)(2,1)S(1)} collective-permute-done((bf16[2,64,256]{2,1,0:T(8,128)(2,1)S(1)}, bf16[2,64,256]{2,1,0:T(8,128)(2,1)S(1)}, u32[]{:S(2)}, u32[]{:S(2)}) %collective-permute-start.5) | collective-permute-done | bytes 65568 | tf_op jit(solution)/shard_map/ppermute | solution.py:242
  17.3 0.9 %collective-permute-start.11 = (bf16[2,2,128,512]{3,2,1,0:T(8,128)(2,1)S(1)}, bf16[2,2,128,512]{3,2,1,0:T(8,128)(2,1)S(1)}, u32[]{:S(2)}, u32[]{:S(2)}) collective-permute-start(bf16[2,2,128,512]{3,2,1,0:T(8,128)(2,1)S(1)} %hold.1), channel_id=1, source_target_pairs={{0,4},{4,0},{8,12},{12,8},{1,5},{5,1},{9,13},{13,9},{2,6},{6,2},{1... | collective-permute-start | bytes 1572872 | tf_op jit(solution)/shard_map/ppermute | solution.py:259
  18.2 0.9 %collective-permute-done.3.refs_0_ = bf16[1,2,128,512]{3,2,1,0:T(8,128)(2,1)S(1)} collective-permute-done((bf16[1,2,128,512]{3,2,1,0:T(8,128)(2,1)S(1)}, bf16[1,2,128,512]{3,2,1,0:T(8,128)(2,1)S(1)}, u32[]{:S(2)}, u32[]{:S(2)}) %collective-permute-start.3) | collective-permute-done | bytes 262176 | tf_op jit(solution)/shard_map/ppermute | solution.py:256
  19.0 1.5 %collective-permute-start.4 = (bf16[1,2,128,512]{3,2,1,0:T(8,128)(2,1)S(1)}, bf16[1,2,128,512]{3,2,1,0:T(8,128)(2,1)S(1)}, u32[]{:S(2)}, u32[]{:S(2)}) collective-permute-start(bf16[1,2,128,512]{3,2,1,0:T(8,128)(2,1)S(1)} %collective-permute-done.3.refs_0_), channel_id=1, source_target_pairs={{0,16},{16,0},{1,17},{17,1},{2,18},{18,2},{3,19},{19,3},{4,20},{20... | collective-permute-start | bytes 786440 | tf_op jit(solution)/shard_map/ppermute | solution.py:257
  20.5 0.0 collective-permute-start.7
  20.5 1.5 %collective-permute-start.6 = (bf16[2,64,256]{2,1,0:T(8,128)(2,1)S(1)}, bf16[2,64,256]{2,1,0:T(8,128)(2,1)S(1)}, u32[]{:S(2)}, u32[]{:S(2)}) collective-permute-start(bf16[2,64,256]{2,1,0:T(8,128)(2,1)S(1)} %get-tuple-element.27.refs_2_.refs_1_), channel_id=1, source_target_pairs={{0,2},{1,3},{2,0},{3,1},{4,6},{5,7},{6,4},{7,5},{8,10},{9,11},{10,... | collective-permute-start | bytes 196616 | tf_op jit(solution)/shard_map/ppermute | solution.py:242
  22.0 2.8 %collective-permute-done.7.refs_5_.refs_4_ = bf16[2,64,256]{2,1,0:T(8,128)(2,1)S(1)} collective-permute-done((bf16[2,64,256]{2,1,0:T(8,128)(2,1)S(1)}, bf16[2,64,256]{2,1,0:T(8,128)(2,1)S(1)}, u32[]{:S(2)}, u32[]{:S(2)}) %collective-permute-start.7) | collective-permute-done | bytes 65568 | tf_op jit(solution)/shard_map/ppermute | solution.py:242
  24.9 1.4 %collective-permute-done.6.refs_4_.refs_3_ = bf16[2,64,256]{2,1,0:T(8,128)(2,1)S(1)} collective-permute-done((bf16[2,64,256]{2,1,0:T(8,128)(2,1)S(1)}, bf16[2,64,256]{2,1,0:T(8,128)(2,1)S(1)}, u32[]{:S(2)}, u32[]{:S(2)}) %collective-permute-start.6) | collective-permute-done | bytes 65568 | tf_op jit(solution)/shard_map/ppermute | solution.py:242
  26.3 0.2 collective-permute-done.4.refs_1_
  26.5 0.5 decode.2
  27.0 2.3 %collective-permute-start.8 = (bf16[2,64,512]{2,1,0:T(8,128)(2,1)S(1)}, bf16[2,64,512]{2,1,0:T(8,128)(2,1)S(1)}, u32[]{:S(2)}, u32[]{:S(2)}) collective-permute-start(bf16[2,64,512]{2,1,0:T(8,128)(2,1)S(1)} %get-tuple-element.29), channel_id=1, source_target_pairs={{0,8},{1,9},{4,12},{5,13},{8,0},{9,1},{12,4},{13,5},{2,10},{3,11},... | collective-permute-start | bytes 393224 | tf_op jit(solution)/shard_map/ppermute | solution.py:282
  29.2 0.0 collective-permute-start.9
  29.2 0.8 %collective-permute-start.10 = (bf16[2,64,512]{2,1,0:T(8,128)(2,1)S(1)}, bf16[2,64,512]{2,1,0:T(8,128)(2,1)S(1)}, u32[]{:S(2)}, u32[]{:S(2)}) collective-permute-start(bf16[2,64,512]{2,1,0:T(8,128)(2,1)S(1)} %get-tuple-element.31), channel_id=1, source_target_pairs={{0,9},{1,8},{4,13},{5,12},{8,1},{9,0},{12,5},{13,4},{2,11},{3,10},... | collective-permute-start | bytes 393224 | tf_op jit(solution)/shard_map/ppermute | solution.py:282
  30.1 3.1 %collective-permute-done.11.refs_0_ = bf16[2,2,128,512]{3,2,1,0:T(8,128)(2,1)S(1)} collective-permute-done((bf16[2,2,128,512]{3,2,1,0:T(8,128)(2,1)S(1)}, bf16[2,2,128,512]{3,2,1,0:T(8,128)(2,1)S(1)}, u32[]{:S(2)}, u32[]{:S(2)}) %collective-permute-start.11) | collective-permute-done | bytes 524320 | tf_op jit(solution)/shard_map/ppermute | solution.py:259
  33.2 0.5 decode.3
  33.7 0.7 %collective-permute-start.12 = (bf16[2,64,512]{2,1,0:T(8,128)(2,1)S(1)}, bf16[2,64,512]{2,1,0:T(8,128)(2,1)S(1)}, u32[]{:S(2)}, u32[]{:S(2)}) collective-permute-start(bf16[2,64,512]{2,1,0:T(8,128)(2,1)S(1)} %get-tuple-element.34), channel_id=1, source_target_pairs={{0,8},{1,9},{4,12},{5,13},{8,0},{9,1},{12,4},{13,5},{2,10},{3,11},... | collective-permute-start | bytes 393224 | tf_op jit(solution)/shard_map/ppermute | solution.py:282
  34.4 0.0 collective-permute-start.13
  34.4 8.1 %collective-permute-done.8.refs_1_ = bf16[2,64,512]{2,1,0:T(8,128)(2,1)S(1)} collective-permute-done((bf16[2,64,512]{2,1,0:T(8,128)(2,1)S(1)}, bf16[2,64,512]{2,1,0:T(8,128)(2,1)S(1)}, u32[]{:S(2)}, u32[]{:S(2)}) %collective-permute-start.8) | collective-permute-done | bytes 131104 | tf_op jit(solution)/shard_map/ppermute | solution.py:282
  42.5 0.0 collective-permute-start.14
  42.5 0.0 collective-permute-done.9.refs_2_
  42.5 1.2 %collective-permute-done.10.refs_3_ = bf16[2,64,512]{2,1,0:T(8,128)(2,1)S(1)} collective-permute-done((bf16[2,64,512]{2,1,0:T(8,128)(2,1)S(1)}, bf16[2,64,512]{2,1,0:T(8,128)(2,1)S(1)}, u32[]{:S(2)}, u32[]{:S(2)}) %collective-permute-start.10) | collective-permute-done | bytes 131104 | tf_op jit(solution)/shard_map/ppermute | solution.py:282
  43.7 7.3 %collective-permute-done.12.refs_5_ = bf16[2,64,512]{2,1,0:T(8,128)(2,1)S(1)} collective-permute-done((bf16[2,64,512]{2,1,0:T(8,128)(2,1)S(1)}, bf16[2,64,512]{2,1,0:T(8,128)(2,1)S(1)}, u32[]{:S(2)}, u32[]{:S(2)}) %collective-permute-start.12) | collective-permute-done | bytes 131104 | tf_op jit(solution)/shard_map/ppermute | solution.py:282
  51.0 0.0 collective-permute-done.13.refs_6_
  51.0 1.2 %collective-permute-done.14.refs_7_ = bf16[2,64,512]{2,1,0:T(8,128)(2,1)S(1)} collective-permute-done((bf16[2,64,512]{2,1,0:T(8,128)(2,1)S(1)}, bf16[2,64,512]{2,1,0:T(8,128)(2,1)S(1)}, u32[]{:S(2)}, u32[]{:S(2)}) %collective-permute-start.14) | collective-permute-done | bytes 131104 | tf_op jit(solution)/shard_map/ppermute | solution.py:282
  52.1 0.0 copy-done
  52.1 0.0 copy-done.1
  52.1 0.9 %add.1 = bf16[2,64,2048]{2,1,0:T(8,128)(2,1)} custom-call(f32[2,2048]{1,0:T(2,128)S(1)} %copy-done.1, bf16[2,64,2048]{2,1,0:T(8,128)(2,1)S(1)} %copy-done, f32[2,64,512]{2,1,0:T(8,128)S(1)} %get-tuple-element.28.refs_5_.refs_0_, bf16[2,64,512]{2,1,0:T(8,128)(2,1)S(1)} %collective-permute-done.8.refs_1_, ...), custom_call_target="tpu_custom_call" | custom-call | tf_op jit(solution)/shard_map/add/pallas_call | solution.py:284
  (2 shorter events, 0.0 us)
Async XLA Ops:
  0.0 14.3 %copy-start.3 = (s32[2,8]{1,0:T(2,128)S(1)}, s32[2,8]{1,0:T(2,128)}, u32[]{:S(2)}) copy-start(s32[2,8]{1,0:T(2,128)} %active_ref.1) | copy-start | bytes 196
  0.0 14.3 %copy-start.2 = (f32[512]{0:T(512)S(1)}, f32[512]{0:T(512)}, u32[]{:S(2)}) copy-start(f32[512]{0:T(512)} %param.9) | copy-start | bytes 6148
  3.2 7.7 %collective-permute-start = (bf16[128,256]{1,0:T(8,128)(2,1)S(1)}, bf16[128,256]{1,0:T(8,128)(2,1)S(1)}, u32[]{:S(2)}, u32[]{:S(2)}) collective-permute-start(bf16[128,256]{1,0:T(8,128)(2,1)S(1)} %get-tuple-element.22), channel_id=1, source_target_pairs={{0,4},{4,8},{8,12},{12,0},{1,5},{5,9},{9,13},{13,1},{2,6},{6,10},{... | collective-permute-start | bytes 196616 | tf_op jit(solution)/shard_map/ppermute | solution.py:222
  6.3 7.1 %collective-permute-start.1 = (bf16[128,256]{1,0:T(8,128)(2,1)S(1)}, bf16[128,256]{1,0:T(8,128)(2,1)S(1)}, u32[]{:S(2)}, u32[]{:S(2)}) collective-permute-start(bf16[128,256]{1,0:T(8,128)(2,1)S(1)} %get-tuple-element.23), channel_id=1, source_target_pairs={{0,8},{4,12},{8,0},{12,4},{1,9},{5,13},{9,1},{13,5},{2,10},{6,14},... | collective-permute-start | bytes 196616 | tf_op jit(solution)/shard_map/ppermute | solution.py:222
  8.8 5.4 %collective-permute-start.2 = (bf16[128,256]{1,0:T(8,128)(2,1)S(1)}, bf16[128,256]{1,0:T(8,128)(2,1)S(1)}, u32[]{:S(2)}, u32[]{:S(2)}) collective-permute-start(bf16[128,256]{1,0:T(8,128)(2,1)S(1)} %get-tuple-element.24), channel_id=1, source_target_pairs={{0,12},{4,0},{8,4},{12,8},{1,13},{5,1},{9,5},{13,9},{2,14},{6,2},{... | collective-permute-start | bytes 196616 | tf_op jit(solution)/shard_map/ppermute | solution.py:222
  10.2 8.8 %collective-permute-start.3 = (bf16[1,2,128,512]{3,2,1,0:T(8,128)(2,1)S(1)}, bf16[1,2,128,512]{3,2,1,0:T(8,128)(2,1)S(1)}, u32[]{:S(2)}, u32[]{:S(2)}) collective-permute-start(bf16[1,2,128,512]{3,2,1,0:T(8,128)(2,1)S(1)} %get-tuple-element.26), channel_id=1, source_target_pairs={{0,4},{4,0},{8,12},{12,8},{1,5},{5,1},{9,13},{13,9},{2,6},{6,2},{1... | collective-permute-start | bytes 786440 | tf_op jit(solution)/shard_map/ppermute | solution.py:256
  16.0 1.3 %collective-permute-start.5 = (bf16[2,64,256]{2,1,0:T(8,128)(2,1)S(1)}, bf16[2,64,256]{2,1,0:T(8,128)(2,1)S(1)}, u32[]{:S(2)}, u32[]{:S(2)}) collective-permute-start(bf16[2,64,256]{2,1,0:T(8,128)(2,1)S(1)} %get-tuple-element.27.refs_2_.refs_1_), channel_id=1, source_target_pairs={{0,1},{1,0},{2,3},{3,2},{4,5},{5,4},{6,7},{7,6},{8,9},{9,8},{10,11... | collective-permute-start | bytes 196616 | tf_op jit(solution)/shard_map/ppermute | solution.py:242
  16.1 36.0 %copy-start = (bf16[2,64,2048]{2,1,0:T(8,128)(2,1)S(1)}, bf16[2,64,2048]{2,1,0:T(8,128)(2,1)}, u32[]{:S(2)}) copy-start(bf16[2,64,2048]{2,1,0:T(8,128)(2,1)} %target_ref.1) | copy-start | bytes 1572868
  16.1 36.0 %copy-start.1 = (f32[2,2048]{1,0:T(2,128)S(1)}, f32[2,2048]{1,0:T(2,128)}, u32[]{:S(2)}) copy-start(f32[2,2048]{1,0:T(2,128)} %bias_ref.1) | copy-start | bytes 49156
  17.3 15.9 %collective-permute-start.11 = (bf16[2,2,128,512]{3,2,1,0:T(8,128)(2,1)S(1)}, bf16[2,2,128,512]{3,2,1,0:T(8,128)(2,1)S(1)}, u32[]{:S(2)}, u32[]{:S(2)}) collective-permute-start(bf16[2,2,128,512]{3,2,1,0:T(8,128)(2,1)S(1)} %hold.1), channel_id=1, source_target_pairs={{0,4},{4,0},{8,12},{12,8},{1,5},{5,1},{9,13},{13,9},{2,6},{6,2},{1... | collective-permute-start | bytes 1572872 | tf_op jit(solution)/shard_map/ppermute | solution.py:259
  19.0 7.5 %collective-permute-start.4 = (bf16[1,2,128,512]{3,2,1,0:T(8,128)(2,1)S(1)}, bf16[1,2,128,512]{3,2,1,0:T(8,128)(2,1)S(1)}, u32[]{:S(2)}, u32[]{:S(2)}) collective-permute-start(bf16[1,2,128,512]{3,2,1,0:T(8,128)(2,1)S(1)} %collective-permute-done.3.refs_0_), channel_id=1, source_target_pairs={{0,16},{16,0},{1,17},{17,1},{2,18},{18,2},{3,19},{19,3},{4,20},{20... | collective-permute-start | bytes 786440 | tf_op jit(solution)/shard_map/ppermute | solution.py:257
  20.5 4.4 %collective-permute-start.7 = (bf16[2,64,256]{2,1,0:T(8,128)(2,1)S(1)}, bf16[2,64,256]{2,1,0:T(8,128)(2,1)S(1)}, u32[]{:S(2)}, u32[]{:S(2)}) collective-permute-start(bf16[2,64,256]{2,1,0:T(8,128)(2,1)S(1)} %get-tuple-element.27.refs_2_.refs_1_), channel_id=1, source_target_pairs={{0,3},{1,2},{2,1},{3,0},{4,7},{5,6},{6,5},{7,4},{8,11},{9,10},{10,... | collective-permute-start | bytes 196616 | tf_op jit(solution)/shard_map/ppermute | solution.py:242
  20.5 5.8 %collective-permute-start.6 = (bf16[2,64,256]{2,1,0:T(8,128)(2,1)S(1)}, bf16[2,64,256]{2,1,0:T(8,128)(2,1)S(1)}, u32[]{:S(2)}, u32[]{:S(2)}) collective-permute-start(bf16[2,64,256]{2,1,0:T(8,128)(2,1)S(1)} %get-tuple-element.27.refs_2_.refs_1_), channel_id=1, source_target_pairs={{0,2},{1,3},{2,0},{3,1},{4,6},{5,7},{6,4},{7,5},{8,10},{9,11},{10,... | collective-permute-start | bytes 196616 | tf_op jit(solution)/shard_map/ppermute | solution.py:242
  27.0 15.6 %collective-permute-start.8 = (bf16[2,64,512]{2,1,0:T(8,128)(2,1)S(1)}, bf16[2,64,512]{2,1,0:T(8,128)(2,1)S(1)}, u32[]{:S(2)}, u32[]{:S(2)}) collective-permute-start(bf16[2,64,512]{2,1,0:T(8,128)(2,1)S(1)} %get-tuple-element.29), channel_id=1, source_target_pairs={{0,8},{1,9},{4,12},{5,13},{8,0},{9,1},{12,4},{13,5},{2,10},{3,11},... | collective-permute-start | bytes 393224 | tf_op jit(solution)/shard_map/ppermute | solution.py:282
  29.2 13.3 %collective-permute-start.9 = (bf16[2,64,512]{2,1,0:T(8,128)(2,1)S(1)}, bf16[2,64,512]{2,1,0:T(8,128)(2,1)S(1)}, u32[]{:S(2)}, u32[]{:S(2)}) collective-permute-start(bf16[2,64,512]{2,1,0:T(8,128)(2,1)S(1)} %get-tuple-element.30), channel_id=1, source_target_pairs={{0,1},{1,0},{4,5},{5,4},{8,9},{9,8},{12,13},{13,12},{2,3},{3,2},{6... | collective-permute-start | bytes 393224 | tf_op jit(solution)/shard_map/ppermute | solution.py:282
  29.2 14.4 %collective-permute-start.10 = (bf16[2,64,512]{2,1,0:T(8,128)(2,1)S(1)}, bf16[2,64,512]{2,1,0:T(8,128)(2,1)S(1)}, u32[]{:S(2)}, u32[]{:S(2)}) collective-permute-start(bf16[2,64,512]{2,1,0:T(8,128)(2,1)S(1)} %get-tuple-element.31), channel_id=1, source_target_pairs={{0,9},{1,8},{4,13},{5,12},{8,1},{9,0},{12,5},{13,4},{2,11},{3,10},... | collective-permute-start | bytes 393224 | tf_op jit(solution)/shard_map/ppermute | solution.py:282
  33.7 17.3 %collective-permute-start.12 = (bf16[2,64,512]{2,1,0:T(8,128)(2,1)S(1)}, bf16[2,64,512]{2,1,0:T(8,128)(2,1)S(1)}, u32[]{:S(2)}, u32[]{:S(2)}) collective-permute-start(bf16[2,64,512]{2,1,0:T(8,128)(2,1)S(1)} %get-tuple-element.34), channel_id=1, source_target_pairs={{0,8},{1,9},{4,12},{5,13},{8,0},{9,1},{12,4},{13,5},{2,10},{3,11},... | collective-permute-start | bytes 393224 | tf_op jit(solution)/shard_map/ppermute | solution.py:282
  34.4 16.6 %collective-permute-start.13 = (bf16[2,64,512]{2,1,0:T(8,128)(2,1)S(1)}, bf16[2,64,512]{2,1,0:T(8,128)(2,1)S(1)}, u32[]{:S(2)}, u32[]{:S(2)}) collective-permute-start(bf16[2,64,512]{2,1,0:T(8,128)(2,1)S(1)} %get-tuple-element.35), channel_id=1, source_target_pairs={{0,1},{1,0},{4,5},{5,4},{8,9},{9,8},{12,13},{13,12},{2,3},{3,2},{6... | collective-permute-start | bytes 393224 | tf_op jit(solution)/shard_map/ppermute | solution.py:282
  42.5 9.6 %collective-permute-start.14 = (bf16[2,64,512]{2,1,0:T(8,128)(2,1)S(1)}, bf16[2,64,512]{2,1,0:T(8,128)(2,1)S(1)}, u32[]{:S(2)}, u32[]{:S(2)}) collective-permute-start(bf16[2,64,512]{2,1,0:T(8,128)(2,1)S(1)} %get-tuple-element.36), channel_id=1, source_target_pairs={{0,9},{1,8},{4,13},{5,12},{8,1},{9,0},{12,5},{13,4},{2,11},{3,10},... | collective-permute-start | bytes 393224 | tf_op jit(solution)/shard_map/ppermute | solution.py:282

commit v8 on v6

--- a/solution.py
+++ b/solution.py
@@ -9,15 +9,17 @@
 
 VMEM_BYTES = 32 * 1024 * 1024
 LANES = 128
-FIRST = 7
+SHARES = (3, 3, 2)
 
 
 def cut_pieces(layers, columns):
     tiles = columns // LANES
-    first = -(-tiles * FIRST // 8)
-    pieces = [((layer,), 0, first * LANES) for layer in range(layers)]
-    if first < tiles:
-        pieces.append((tuple(range(layers)), first * LANES, (tiles - first) * LANES))
+    pieces, start = [], 0
+    for i, eighths in enumerate(SHARES):
+        stop = tiles if i + 1 == len(SHARES) else min(tiles, start + -(-tiles * eighths // 8))
+        if stop > start:
+            pieces.append((tuple(range(layers)), start * LANES, (stop - start) * LANES))
+        start = stop
     return pieces
 
 
@@ -58,6 +60,8 @@
         copy.wait()
     copies_part = []
     for i, piece in enumerate(pieces):
+        if i == 0:
+            piece = ((lax.axis_index("parts"),), *piece[1:])
         copies_part += part_copies(piece, dec_hbm, part_refs[i], part_sems.at[i])
     src = lax.axis_index("src")
     for k in range(n):
@@ -108,9 +112,11 @@
             out_ref[group, :, columns] = value.astype(jnp.bfloat16)
 
 
-def decode_kernel(n, own_ref, got_ref, *refs):
+def decode_kernel(n, piece, shared, dec_ref, *refs):
     half = n // 2
-    layers, groups, block, width = own_ref.shape
+    layers, groups, block, cols = dec_ref.shape
+    _, first, width = piece
+    got_refs, refs = refs[: 1 + shared], refs[1 + shared :]
     code_refs, out_refs, lhs_ref = refs[: 2 * groups], refs[-2 * half - 1 : -1], refs[-1]
     src, tgt = lax.axis_index("src"), lax.axis_index("tgt")
     parity = lax.rem(src, 2)
@@ -127,16 +133,18 @@
                 for r in range(2):
                     rows = slice((2 * j + r) * share, (2 * j + r + 1) * share)
                     lhs_ref[rows, columns] = code_refs[2 * k + r][group, :, latents]
-    for layer in range(layers):
-        own = own_ref[layer].reshape(depth, width)
-        got = got_ref[layer].reshape(depth, width)
+    start = pl.multiple_of(lax.axis_index("rep") * (cols // 2) + first, LANES)
+    for i in range(layers):
+        layer = lax.rem(lax.axis_index("parts") + i, layers) if shared else i
+        own = dec_ref[layer, :, :, pl.ds(start, width)].reshape(depth, width)
+        got = (got_refs[i][0] if shared else got_refs[0][i]).reshape(depth, width)
         total = jnp.dot(lhs_ref[:, :depth], own, preferred_element_type=jnp.float32)
         total += jnp.dot(lhs_ref[:, depth:], got, preferred_element_type=jnp.float32)
-        for i, ref in enumerate(out_refs):
-            ref[layer] = total[i * share : (i + 1) * share].astype(ref.dtype)
-
-
-def add_kernel(n, pieces, chained, bias_ref, target_ref, *refs):
+        for j, ref in enumerate(out_refs):
+            ref[layer] = total[j * share : (j + 1) * share].astype(ref.dtype)
+
+
+def add_kernel(n, pieces, bias_ref, target_ref, *refs):
     out_hbm, out_ref, sems = refs[-3:]
     half = n // 2
     cols = target_ref.shape[2]
@@ -180,6 +188,7 @@
     anywhere = pl.BlockSpec(memory_space=pl.ANY)
     cost = pl.CostEstimate(flops=0, bytes_accessed=0, transcendentals=0)
 
+    dec_rows = dec_w
     acts, enc_w, dec_w = (
         pltpu.with_memory_space_constraint(value, pltpu.HBM)
         for value in (acts.reshape(half, 2, share, features), enc_w, dec_w)
@@ -191,7 +200,10 @@
     results = pl.pallas_call(
         functools.partial(encode_kernel, n, pieces),
         out_shape=[shape(half * share, 2 * block)] * n
-        + [shape(len(which), groups, block, width) for which, _, width in pieces],
+        + [
+            shape(1 if i == 0 else layers, groups, block, width)
+            for i, (_, _, width) in enumerate(pieces)
+        ],
         in_specs=[anywhere] * 3,
         out_specs=[vmem] * (n + len(pieces)),
         scratch_shapes=[
@@ -237,47 +249,48 @@
             name="hold",
         )(value, after)
 
-    def add(some, out):
-        chained = [] if out is None else [out]
+    got = [[lax.ppermute(parts[0], "src", pair)]]
+    got[0].append(lax.ppermute(got[0][0], "parts", [(0, 1), (1, 0)]))
+    if len(pieces) > 1:
+        got.append([lax.ppermute(hold(parts[1], own), "src", pair)])
+    def add(some, begun):
         operands = [value for i in some for value in sums[i]]
         return pl.pallas_call(
-            functools.partial(add_kernel, n, [pieces[i] for i in some], len(chained)),
+            functools.partial(add_kernel, n, [pieces[i] for i in some]),
             out_shape=shape(layers, share, cols),
-            in_specs=[vmem] * (2 + len(operands)) + [anywhere] * len(chained),
+            in_specs=[vmem] * (2 + len(operands)) + [anywhere] * len(begun),
             out_specs=anywhere,
             scratch_shapes=[
                 pltpu.VMEM((layers, share, cols), jnp.bfloat16),
                 pltpu.SemaphoreType.DMA((2 * len(some) * layers,)),
             ],
-            input_output_aliases={2 + len(operands): 0} if chained else {},
+            input_output_aliases={2 + len(operands): 0} if begun else {},
             compiler_params=params,
             cost_estimate=cost,
             name="add",
-        )(dec_b, targets, *operands, *chained)
-
-    parts[1:layers] = [hold(part, codes[1]) for part in parts[1:layers]]
-    got = [lax.ppermute(part, "src", pair) for part in parts[:layers]]
-    sums, after, out = [], [], None
-    for i, (which, _, width) in enumerate(pieces):
-        if i == layers:
-            out = add([0], None)
-            after.append(out)
-        shapes = [shape(len(which), share, width)] * (2 * half)
-        shapes[0] = shape(len(which), share, width, kind=jnp.float32)
+        )(dec_b, targets, *operands, *begun)
+
+    sums, after, begun = [], [], []
+    for i, (_, _, width) in enumerate(pieces):
+        if i == 2:
+            begun = [add([0], [])]
+            after.append(begun[0])
+        shapes = [shape(layers, share, width)] * (2 * half)
+        shapes[0] = shape(layers, share, width, kind=jnp.float32)
         terms = pl.pallas_call(
-            functools.partial(decode_kernel, n),
+            functools.partial(decode_kernel, n, pieces[i], i == 0),
             out_shape=shapes,
-            in_specs=[vmem] * (2 + 2 * groups) + [anywhere] * len(after),
+            in_specs=[vmem] * (1 + len(got[i]) + 2 * groups) + [anywhere] * len(after),
             out_specs=[vmem] * len(shapes),
             scratch_shapes=[pltpu.VMEM((rows, 2 * groups * block), jnp.bfloat16)],
             compiler_params=params,
             cost_estimate=cost,
             name="decode",
-        )(parts[i], got[i], *codes, *after)
+        )(dec_rows, *got[i], *codes, *after)
         after = [terms[0]]
         if i == 0:
-            for part in parts[layers:]:
-                got.append(lax.ppermute(hold(part, terms[0]), "src", pair))
+            for part in parts[2:]:
+                got.append([lax.ppermute(hold(part, own), "src", pair)])
         sums.append([])
         for r in range(2):
             for j in range(half):
@@ -286,8 +299,8 @@
                 ]
                 term = terms[2 * j + r]
                 sums[i].append(lax.ppermute(term, ("src", "rep"), perm) if j + r else term)
-    rest = range(0 if out is None else 1, len(pieces))
-    return add(list(rest), out)
+
+    return add(list(range(len(begun), len(pieces))), begun)
 
 
 def solution(mesh):

time: 58 us -> 53.8 us (0.928)
  waiting for transfers between devices: 32.4 us -> 24.1 us
  starting transfers between devices: 17.4 us -> 21.6 us
    ppermute x3 -> x4, waiting for transfers between devices: 11.7 us -> 2.61 us  [the longest x1 2.61 us: body(): got = [[lax.ppermute(parts[0], 'src', pair)]]]
    ppermute x9, waiting for transfers between devices: 11.9 us -> 14.9 us  [body(): sums[i].append(lax.ppermute(term, ('src', 'rep'), perm) if j + r else term)]
    ppermute x9, starting transfers between devices: 5.93 us -> 8.85 us  [body(): sums[i].append(lax.ppermute(term, ('src', 'rep'), perm) if j + r else term)]
    ppermute x3, waiting for transfers between devices: 5.42 us -> 3.16 us  [body(): codes.append(lax.ppermute(own, ('tgt', 'rep'), perm) if k + r else own)]
    ppermute x3, starting transfers between devices: 1.56 us -> 2.44 us  [body(): codes.append(lax.ppermute(own, ('tgt', 'rep'), perm) if k + r else own)]
    ppermute x3 -> x4, starting transfers between devices: 2.87 us -> 3.24 us  [the longest x1 1.55 us: body(): got[0].append(lax.ppermute(got[0][0], 'parts', [(0, 1), (1, 0)]))]
  transfers between devices with their start and end apart: 18 -> 19, of which waited for: 9 -> 10; matrix products, arithmetic and copies ran while one was open for 0% -> 0% of each run, Pallas kernels for 5% -> 5%
where the time goes in v8:
time: 53.8 us; the launch traced here: 53.6 us
  waiting for transfers between devices  24.1 us (45%)
  starting transfers between devices  21.6 us (40%)
  Pallas kernels  6.81 us (13%)
  local copies, waits for them, and re-layouts  1.06 us (2%)
    ppermute x9, waiting for transfers between devices, body(): sums[i].append(lax.ppermute(term, ('src', 'rep'), perm) if j + r else term)  14.9 us
    ppermute x9, starting transfers between devices, body(): sums[i].append(lax.ppermute(term, ('src', 'rep'), perm) if j + r else term)  8.85 us
    ppermute x3, starting transfers between devices, body(): lax.ppermute(terms[k], 'src', [(i, (i + k) % n) for i in range(n)])  7.02 us
    ppermute x3, waiting for transfers between devices, body(): lax.ppermute(terms[k], 'src', [(i, (i + k) % n) for i in range(n)])  3.38 us
    pallas_call x1, Pallas kernels, body(): pl.pallas_call(functools.partial(encode_kernel, n, pieces), out_shape=[sh...  3.31 us
    ppermute x3, waiting for transfers between devices, body(): codes.append(lax.ppermute(own, ('tgt', 'rep'), perm) if k + r else own)  3.16 us
    ppermute x1, waiting for transfers between devices, body(): got = [[lax.ppermute(parts[0], 'src', pair)]]  2.61 us
    ppermute x3, starting transfers between devices, body(): codes.append(lax.ppermute(own, ('tgt', 'rep'), perm) if k + r else own)  2.44 us
  transfers between devices with their start and end apart: 19, of which 10 were waited for; matrix products, arithmetic and copies ran while one was open for 0% of the time, Pallas kernels for 5%

profile of v8, /device:TPU:0, one launch (start us, length us, event | category | flops | bytes accessed | tf_op | source)
XLA Modules:
  0.0 53.6 jit_solution(7804430980744714921)
XLA Ops:
  0.0 3.3 %encode.1 = (bf16[128,256]{1,0:T(8,128)(2,1)S(1)}, bf16[128,256]{1,0:T(8,128)(2,1)S(1)}, bf16[128,256]{1,0:T(8,128)(2,1)S(1)}, bf16[128,256]{1,0:T(8,128)(2,1)S(...) custom-call(bf16[2,2,64,1024]{3,2,1,0:T(8,128)(2,1)} %bitcast.3, ...), custom_call_target="tpu_custom_call" | custom-call | tf_op jit(solution)/shard_map/encode/pallas_call | solution.py:200
  3.3 3.1 %collective-permute-start = (bf16[128,256]{1,0:T(8,128)(2,1)S(1)}, bf16[128,256]{1,0:T(8,128)(2,1)S(1)}, u32[]{:S(2)}, u32[]{:S(2)}) collective-permute-start(bf16[128,256]{1,0:T(8,128)(2,1)S(1)} %get-tuple-element.26), channel_id=1, source_target_pairs={{0,4},{4,8},{8,12},{12,0},{1,5},{5,9},{9,13},{13,1},{2,6},{6,10},{... | collective-permute-start | bytes 196616 | tf_op jit(solution)/shard_map/ppermute | solution.py:222
  6.4 2.6 %collective-permute-start.1 = (bf16[128,256]{1,0:T(8,128)(2,1)S(1)}, bf16[128,256]{1,0:T(8,128)(2,1)S(1)}, u32[]{:S(2)}, u32[]{:S(2)}) collective-permute-start(bf16[128,256]{1,0:T(8,128)(2,1)S(1)} %get-tuple-element.27), channel_id=1, source_target_pairs={{0,8},{4,12},{8,0},{12,4},{1,9},{5,13},{9,1},{13,5},{2,10},{6,14},... | collective-permute-start | bytes 196616 | tf_op jit(solution)/shard_map/ppermute | solution.py:222
  9.0 1.3 %collective-permute-start.2 = (bf16[128,256]{1,0:T(8,128)(2,1)S(1)}, bf16[128,256]{1,0:T(8,128)(2,1)S(1)}, u32[]{:S(2)}, u32[]{:S(2)}) collective-permute-start(bf16[128,256]{1,0:T(8,128)(2,1)S(1)} %get-tuple-element.28), channel_id=1, source_target_pairs={{0,12},{4,0},{8,4},{12,8},{1,13},{5,1},{9,5},{13,9},{2,14},{6,2},{... | collective-permute-start | bytes 196616 | tf_op jit(solution)/shard_map/ppermute | solution.py:222
  10.3 0.7 %collective-permute-start.7 = (bf16[1,2,128,384]{3,2,1,0:T(8,128)(2,1)S(1)}, bf16[1,2,128,384]{3,2,1,0:T(8,128)(2,1)S(1)}, u32[]{:S(2)}, u32[]{:S(2)}) collective-permute-start(bf16[1,2,128,384]{3,2,1,0:T(8,128)(2,1)S(1)} %get-tuple-element.29), channel_id=1, source_target_pairs={{0,4},{4,0},{8,12},{12,8},{1,5},{5,1},{9,13},{13,9},{2,6},{6,2},{1... | collective-permute-start | bytes 589832 | tf_op jit(solution)/shard_map/ppermute | solution.py:252
  11.0 0.0 collective-permute-done.refs_1_
  11.0 2.5 %collective-permute-done.1.refs_2_ = bf16[128,256]{1,0:T(8,128)(2,1)S(1)} collective-permute-done((bf16[128,256]{1,0:T(8,128)(2,1)S(1)}, bf16[128,256]{1,0:T(8,128)(2,1)S(1)}, u32[]{:S(2)}, u32[]{:S(2)}) %collective-permute-start.1) | collective-permute-done | bytes 65568 | tf_op jit(solution)/shard_map/ppermute | solution.py:222
  13.5 0.9 %collective-permute-done.2.refs_3_ = bf16[128,256]{1,0:T(8,128)(2,1)S(1)} collective-permute-done((bf16[128,256]{1,0:T(8,128)(2,1)S(1)}, bf16[128,256]{1,0:T(8,128)(2,1)S(1)}, u32[]{:S(2)}, u32[]{:S(2)}) %collective-permute-start.2) | collective-permute-done | bytes 65568 | tf_op jit(solution)/shard_map/ppermute | solution.py:222
  14.4 0.6 %codes.1.refs_1_.refs_2_ = bf16[2,64,256]{2,1,0:T(8,128)(2,1)S(1)} custom-call(s32[2,8]{1,0:T(2,128)S(1)} %copy-done.5, f32[4,128]{1,0:T(4,128)S(1)} %bitcast.2, bf16[128,256]{1,0:T(8,128)(2,1)S(1)} %get-tuple-element.25.refs_0_, bf16[128,256]{1,0:T(8,128)(2,1)S(1)} %collective-permute-done.refs_1_, bf16[128,256]{1,0:T(8,128)(2,1)S(1)} %collective-permute-done.1.refs_2_, ...), custom_call_target="tpu_custom_call" | custom-call | tf_op jit(solution)/shard_map/codes/pallas_call | solution.py:223
  15.1 1.0 %collective-permute-start.3 = (bf16[2,2,128,384]{3,2,1,0:T(8,128)(2,1)S(1)}, bf16[2,2,128,384]{3,2,1,0:T(8,128)(2,1)S(1)}, u32[]{:S(2)}, u32[]{:S(2)}) collective-permute-start(bf16[2,2,128,384]{3,2,1,0:T(8,128)(2,1)S(1)} %hold.2), channel_id=1, source_target_pairs={{0,4},{4,0},{8,12},{12,8},{1,5},{5,1},{9,13},{13,9},{2,6},{6,2},{1... | collective-permute-start | bytes 1179656 | tf_op jit(solution)/shard_map/ppermute | solution.py:255
  16.0 2.6 %collective-permute-done.7.refs_0_ = bf16[1,2,128,384]{3,2,1,0:T(8,128)(2,1)S(1)} collective-permute-done((bf16[1,2,128,384]{3,2,1,0:T(8,128)(2,1)S(1)}, bf16[1,2,128,384]{3,2,1,0:T(8,128)(2,1)S(1)}, u32[]{:S(2)}, u32[]{:S(2)}) %collective-permute-start.7) | collective-permute-done | bytes 196640 | tf_op jit(solution)/shard_map/ppermute | solution.py:252
  18.6 1.5 %collective-permute-start.8 = (bf16[1,2,128,384]{3,2,1,0:T(8,128)(2,1)S(1)}, bf16[1,2,128,384]{3,2,1,0:T(8,128)(2,1)S(1)}, u32[]{:S(2)}, u32[]{:S(2)}) collective-permute-start(bf16[1,2,128,384]{3,2,1,0:T(8,128)(2,1)S(1)} %collective-permute-done.7.refs_0_), channel_id=1, source_target_pairs={{0,16},{16,0},{1,17},{17,1},{2,18},{18,2},{3,19},{19,3},{4,20},{20... | collective-permute-start | bytes 589832 | tf_op jit(solution)/shard_map/ppermute | solution.py:253
  20.2 0.0 collective-permute-start.4
  20.2 0.1 collective-permute-start.12
  20.2 1.5 %collective-permute-start.5 = (bf16[2,64,256]{2,1,0:T(8,128)(2,1)S(1)}, bf16[2,64,256]{2,1,0:T(8,128)(2,1)S(1)}, u32[]{:S(2)}, u32[]{:S(2)}) collective-permute-start(bf16[2,64,256]{2,1,0:T(8,128)(2,1)S(1)} %codes.1.refs_1_.refs_2_), channel_id=1, source_target_pairs={{0,2},{1,3},{2,0},{3,1},{4,6},{5,7},{6,4},{7,5},{8,10},{9,11},{10,... | collective-permute-start | bytes 196616 | tf_op jit(solution)/shard_map/ppermute | solution.py:238
  21.7 0.0 collective-permute-done.4.refs_3_.refs_2_
  21.7 1.0 %collective-permute-start.6 = (bf16[2,64,256]{2,1,0:T(8,128)(2,1)S(1)}, bf16[2,64,256]{2,1,0:T(8,128)(2,1)S(1)}, u32[]{:S(2)}, u32[]{:S(2)}) collective-permute-start(bf16[2,64,256]{2,1,0:T(8,128)(2,1)S(1)} %codes.1.refs_1_.refs_2_), channel_id=1, source_target_pairs={{0,3},{1,2},{2,1},{3,0},{4,7},{5,6},{6,5},{7,4},{8,11},{9,10},{10,... | collective-permute-start | bytes 196616 | tf_op jit(solution)/shard_map/ppermute | solution.py:238
  22.7 2.0 %collective-permute-done.5.refs_4_.refs_3_ = bf16[2,64,256]{2,1,0:T(8,128)(2,1)S(1)} collective-permute-done((bf16[2,64,256]{2,1,0:T(8,128)(2,1)S(1)}, bf16[2,64,256]{2,1,0:T(8,128)(2,1)S(1)}, u32[]{:S(2)}, u32[]{:S(2)}) %collective-permute-start.5) | collective-permute-done | bytes 65568 | tf_op jit(solution)/shard_map/ppermute | solution.py:238
  24.7 1.2 %collective-permute-done.6.refs_5_.refs_4_ = bf16[2,64,256]{2,1,0:T(8,128)(2,1)S(1)} collective-permute-done((bf16[2,64,256]{2,1,0:T(8,128)(2,1)S(1)}, bf16[2,64,256]{2,1,0:T(8,128)(2,1)S(1)}, u32[]{:S(2)}, u32[]{:S(2)}) %collective-permute-start.6) | collective-permute-done | bytes 65568 | tf_op jit(solution)/shard_map/ppermute | solution.py:238
  25.8 0.0 collective-permute-done.8.refs_1_
  25.8 0.5 decode.3
  26.3 0.0 copy-start.2
  26.3 0.0 copy-start.3
  26.4 2.5 %collective-permute-start.13 = (bf16[2,64,384]{2,1,0:T(8,128)(2,1)S(1)}, bf16[2,64,384]{2,1,0:T(8,128)(2,1)S(1)}, u32[]{:S(2)}, u32[]{:S(2)}) collective-permute-start(bf16[2,64,384]{2,1,0:T(8,128)(2,1)S(1)} %get-tuple-element.36), channel_id=1, source_target_pairs={{0,8},{1,9},{4,12},{5,13},{8,0},{9,1},{12,4},{13,5},{2,10},{3,11},... | collective-permute-start | bytes 294920 | tf_op jit(solution)/shard_map/ppermute | solution.py:301
  28.8 0.0 collective-permute-start.14
  28.9 0.6 %collective-permute-start.15 = (bf16[2,64,384]{2,1,0:T(8,128)(2,1)S(1)}, bf16[2,64,384]{2,1,0:T(8,128)(2,1)S(1)}, u32[]{:S(2)}, u32[]{:S(2)}) collective-permute-start(bf16[2,64,384]{2,1,0:T(8,128)(2,1)S(1)} %get-tuple-element.38), channel_id=1, source_target_pairs={{0,9},{1,8},{4,13},{5,12},{8,1},{9,0},{12,5},{13,4},{2,11},{3,10},... | collective-permute-start | bytes 294920 | tf_op jit(solution)/shard_map/ppermute | solution.py:301
  29.5 0.0 collective-permute-done.3.refs_0_
  29.5 0.5 decode.4
  30.0 2.5 %collective-permute-start.9 = (bf16[2,64,384]{2,1,0:T(8,128)(2,1)S(1)}, bf16[2,64,384]{2,1,0:T(8,128)(2,1)S(1)}, u32[]{:S(2)}, u32[]{:S(2)}) collective-permute-start(bf16[2,64,384]{2,1,0:T(8,128)(2,1)S(1)} %get-tuple-element.32), channel_id=1, source_target_pairs={{0,8},{1,9},{4,12},{5,13},{8,0},{9,1},{12,4},{13,5},{2,10},{3,11},... | collective-permute-start | bytes 294920 | tf_op jit(solution)/shard_map/ppermute | solution.py:301
  32.5 6.9 %collective-permute-done.13.refs_1_ = bf16[2,64,384]{2,1,0:T(8,128)(2,1)S(1)} collective-permute-done((bf16[2,64,384]{2,1,0:T(8,128)(2,1)S(1)}, bf16[2,64,384]{2,1,0:T(8,128)(2,1)S(1)}, u32[]{:S(2)}, u32[]{:S(2)}) %collective-permute-start.13) | collective-permute-done | bytes 98336 | tf_op jit(solution)/shard_map/ppermute | solution.py:301
  39.3 0.0 collective-permute-start.10
  39.3 0.0 collective-permute-done.14.refs_2_
  39.3 0.0 collective-permute-start.11
  39.3 1.0 %collective-permute-done.15.refs_3_ = bf16[2,64,384]{2,1,0:T(8,128)(2,1)S(1)} collective-permute-done((bf16[2,64,384]{2,1,0:T(8,128)(2,1)S(1)}, bf16[2,64,384]{2,1,0:T(8,128)(2,1)S(1)}, u32[]{:S(2)}, u32[]{:S(2)}) %collective-permute-start.15) | collective-permute-done | bytes 98336 | tf_op jit(solution)/shard_map/ppermute | solution.py:301
  40.3 0.7 %add.2.refs_6_.refs_8_ = bf16[2,64,2048]{2,1,0:T(8,128)(2,1)} custom-call(f32[2,2048]{1,0:T(2,128)S(1)} %copy-done.3, bf16[2,64,2048]{2,1,0:T(8,128)(2,1)S(1)} %copy-done.2, f32[2,64,384]{2,1,0:T(8,128)S(1)} %get-tuple-element.30.refs_5_.refs_0_, bf16[2,64,384]{2,1,0:T(8,128)(2,1)S(1)} %collective-permute-done.13.refs_1_, ...), custom_call_target="tpu_custom_call" | custom-call | tf_op jit(solution)/shard_map/add/pallas_call | solution.py:258
  41.1 0.0 collective-permute-done.12.refs_0_
  41.1 0.0 copy-start.1
  41.1 1.0 %copy-done.1 = bf16[2,64,2048]{2,1,0:T(8,128)(2,1)S(1)} copy-done((bf16[2,64,2048]{2,1,0:T(8,128)(2,1)S(1)}, bf16[2,64,2048]{2,1,0:T(8,128)(2,1)}, u32[]{:S(2)}) %copy-start.1) | copy-done | bytes 524312
  42.1 0.3 decode.5
  42.5 2.1 %collective-permute-start.16 = (bf16[2,64,256]{2,1,0:T(8,128)(2,1)S(1)}, bf16[2,64,256]{2,1,0:T(8,128)(2,1)S(1)}, u32[]{:S(2)}, u32[]{:S(2)}) collective-permute-start(bf16[2,64,256]{2,1,0:T(8,128)(2,1)S(1)} %get-tuple-element.40), channel_id=1, source_target_pairs={{0,8},{1,9},{4,12},{5,13},{8,0},{9,1},{12,4},{13,5},{2,10},{3,11},... | collective-permute-start | bytes 196616 | tf_op jit(solution)/shard_map/ppermute | solution.py:301
  44.6 0.0 collective-permute-start.17
  44.6 0.0 collective-permute-done.9.refs_1_
  44.6 1.1 %collective-permute-start.18 = (bf16[2,64,256]{2,1,0:T(8,128)(2,1)S(1)}, bf16[2,64,256]{2,1,0:T(8,128)(2,1)S(1)}, u32[]{:S(2)}, u32[]{:S(2)}) collective-permute-start(bf16[2,64,256]{2,1,0:T(8,128)(2,1)S(1)} %get-tuple-element.42), channel_id=1, source_target_pairs={{0,9},{1,8},{4,13},{5,12},{8,1},{9,0},{12,5},{13,4},{2,11},{3,10},... | collective-permute-start | bytes 196616 | tf_op jit(solution)/shard_map/ppermute | solution.py:301
  45.7 0.0 collective-permute-done.10.refs_2_
  45.7 1.5 %collective-permute-done.11.refs_3_ = bf16[2,64,384]{2,1,0:T(8,128)(2,1)S(1)} collective-permute-done((bf16[2,64,384]{2,1,0:T(8,128)(2,1)S(1)}, bf16[2,64,384]{2,1,0:T(8,128)(2,1)S(1)}, u32[]{:S(2)}, u32[]{:S(2)}) %collective-permute-start.11) | collective-permute-done | bytes 98336 | tf_op jit(solution)/shard_map/ppermute | solution.py:301
  47.2 4.2 %collective-permute-done.16.refs_5_ = bf16[2,64,256]{2,1,0:T(8,128)(2,1)S(1)} collective-permute-done((bf16[2,64,256]{2,1,0:T(8,128)(2,1)S(1)}, bf16[2,64,256]{2,1,0:T(8,128)(2,1)S(1)}, u32[]{:S(2)}, u32[]{:S(2)}) %collective-permute-start.16) | collective-permute-done | bytes 65568 | tf_op jit(solution)/shard_map/ppermute | solution.py:301
  51.4 1.4 %collective-permute-done.18.refs_7_ = bf16[2,64,256]{2,1,0:T(8,128)(2,1)S(1)} collective-permute-done((bf16[2,64,256]{2,1,0:T(8,128)(2,1)S(1)}, bf16[2,64,256]{2,1,0:T(8,128)(2,1)S(1)}, u32[]{:S(2)}, u32[]{:S(2)}) %collective-permute-start.18) | collective-permute-done | bytes 65568 | tf_op jit(solution)/shard_map/ppermute | solution.py:301
  52.8 0.8 %add.3 = bf16[2,64,2048]{2,1,0:T(8,128)(2,1)} custom-call(f32[2,2048]{1,0:T(2,128)S(1)} %copy-done.3, bf16[2,64,2048]{2,1,0:T(8,128)(2,1)S(1)} %copy-done.2, f32[2,64,384]{2,1,0:T(8,128)S(1)} %get-tuple-element.31.refs_5_.refs_0_, bf16[2,64,384]{2,1,0:T(8,128)(2,1)S(1)} %collective-permute-done.9.refs_1_, ...), custom_call_target="tpu_custom_call", output_to_operand_aliasing={{}: (10, {})} | custom-call | tf_op jit(solution)/shard_map/add/pallas_call | solution.py:258
  (11 shorter events, 0.0 us)
Async XLA Ops:
  0.0 14.4 %copy-start.5 = (s32[2,8]{1,0:T(2,128)S(1)}, s32[2,8]{1,0:T(2,128)}, u32[]{:S(2)}) copy-start(s32[2,8]{1,0:T(2,128)} %active_ref.1) | copy-start | bytes 196
  0.0 14.4 %copy-start.4 = (f32[512]{0:T(512)S(1)}, f32[512]{0:T(512)}, u32[]{:S(2)}) copy-start(f32[512]{0:T(512)} %param.9) | copy-start | bytes 6148
  0.0 25.8 %copy-start = (bf16[2,2,128,2048]{3,2,1,0:T(8,128)(2,1)S(1)}, bf16[2,2,128,2048]{3,2,1,0:T(8,128)(2,1)}, u32[]{:S(2)}) copy-start(bf16[2,2,128,2048]{3,2,1,0:T(8,128)(2,1)} %dec_ref.5) | copy-start | bytes 6291460
  3.3 7.7 %collective-permute-start = (bf16[128,256]{1,0:T(8,128)(2,1)S(1)}, bf16[128,256]{1,0:T(8,128)(2,1)S(1)}, u32[]{:S(2)}, u32[]{:S(2)}) collective-permute-start(bf16[128,256]{1,0:T(8,128)(2,1)S(1)} %get-tuple-element.26), channel_id=1, source_target_pairs={{0,4},{4,8},{8,12},{12,0},{1,5},{5,9},{9,13},{13,1},{2,6},{6,10},{... | collective-permute-start | bytes 196616 | tf_op jit(solution)/shard_map/ppermute | solution.py:222
  6.4 7.1 %collective-permute-start.1 = (bf16[128,256]{1,0:T(8,128)(2,1)S(1)}, bf16[128,256]{1,0:T(8,128)(2,1)S(1)}, u32[]{:S(2)}, u32[]{:S(2)}) collective-permute-start(bf16[128,256]{1,0:T(8,128)(2,1)S(1)} %get-tuple-element.27), channel_id=1, source_target_pairs={{0,8},{4,12},{8,0},{12,4},{1,9},{5,13},{9,1},{13,5},{2,10},{6,14},... | collective-permute-start | bytes 196616 | tf_op jit(solution)/shard_map/ppermute | solution.py:222
  9.0 5.4 %collective-permute-start.2 = (bf16[128,256]{1,0:T(8,128)(2,1)S(1)}, bf16[128,256]{1,0:T(8,128)(2,1)S(1)}, u32[]{:S(2)}, u32[]{:S(2)}) collective-permute-start(bf16[128,256]{1,0:T(8,128)(2,1)S(1)} %get-tuple-element.28), channel_id=1, source_target_pairs={{0,12},{4,0},{8,4},{12,8},{1,13},{5,1},{9,5},{13,9},{2,14},{6,2},{... | collective-permute-start | bytes 196616 | tf_op jit(solution)/shard_map/ppermute | solution.py:222
  10.3 8.3 %collective-permute-start.7 = (bf16[1,2,128,384]{3,2,1,0:T(8,128)(2,1)S(1)}, bf16[1,2,128,384]{3,2,1,0:T(8,128)(2,1)S(1)}, u32[]{:S(2)}, u32[]{:S(2)}) collective-permute-start(bf16[1,2,128,384]{3,2,1,0:T(8,128)(2,1)S(1)} %get-tuple-element.29), channel_id=1, source_target_pairs={{0,4},{4,0},{8,12},{12,8},{1,5},{5,1},{9,13},{13,9},{2,6},{6,2},{1... | collective-permute-start | bytes 589832 | tf_op jit(solution)/shard_map/ppermute | solution.py:252
  15.1 14.4 %collective-permute-start.3 = (bf16[2,2,128,384]{3,2,1,0:T(8,128)(2,1)S(1)}, bf16[2,2,128,384]{3,2,1,0:T(8,128)(2,1)S(1)}, u32[]{:S(2)}, u32[]{:S(2)}) collective-permute-start(bf16[2,2,128,384]{3,2,1,0:T(8,128)(2,1)S(1)} %hold.2), channel_id=1, source_target_pairs={{0,4},{4,0},{8,12},{12,8},{1,5},{5,1},{9,13},{13,9},{2,6},{6,2},{1... | collective-permute-start | bytes 1179656 | tf_op jit(solution)/shard_map/ppermute | solution.py:255
  18.6 7.2 %collective-permute-start.8 = (bf16[1,2,128,384]{3,2,1,0:T(8,128)(2,1)S(1)}, bf16[1,2,128,384]{3,2,1,0:T(8,128)(2,1)S(1)}, u32[]{:S(2)}, u32[]{:S(2)}) collective-permute-start(bf16[1,2,128,384]{3,2,1,0:T(8,128)(2,1)S(1)} %collective-permute-done.7.refs_0_), channel_id=1, source_target_pairs={{0,16},{16,0},{1,17},{17,1},{2,18},{18,2},{3,19},{19,3},{4,20},{20... | collective-permute-start | bytes 589832 | tf_op jit(solution)/shard_map/ppermute | solution.py:253
  20.2 1.5 %collective-permute-start.4 = (bf16[2,64,256]{2,1,0:T(8,128)(2,1)S(1)}, bf16[2,64,256]{2,1,0:T(8,128)(2,1)S(1)}, u32[]{:S(2)}, u32[]{:S(2)}) collective-permute-start(bf16[2,64,256]{2,1,0:T(8,128)(2,1)S(1)} %codes.1.refs_1_.refs_2_), channel_id=1, source_target_pairs={{0,1},{1,0},{2,3},{3,2},{4,5},{5,4},{6,7},{7,6},{8,9},{9,8},{10,11... | collective-permute-start | bytes 196616 | tf_op jit(solution)/shard_map/ppermute | solution.py:238
  20.2 20.9 %collective-permute-start.12 = (bf16[2,2,128,256]{3,2,1,0:T(8,128)(2,1)S(1)}, bf16[2,2,128,256]{3,2,1,0:T(8,128)(2,1)S(1)}, u32[]{:S(2)}, u32[]{:S(2)}) collective-permute-start(bf16[2,2,128,256]{3,2,1,0:T(8,128)(2,1)S(1)} %hold.3), channel_id=1, source_target_pairs={{0,4},{4,0},{8,12},{12,8},{1,5},{5,1},{9,13},{13,9},{2,6},{6,2},{1... | collective-permute-start | bytes 786440 | tf_op jit(solution)/shard_map/ppermute | solution.py:293
  20.2 4.4 %collective-permute-start.5 = (bf16[2,64,256]{2,1,0:T(8,128)(2,1)S(1)}, bf16[2,64,256]{2,1,0:T(8,128)(2,1)S(1)}, u32[]{:S(2)}, u32[]{:S(2)}) collective-permute-start(bf16[2,64,256]{2,1,0:T(8,128)(2,1)S(1)} %codes.1.refs_1_.refs_2_), channel_id=1, source_target_pairs={{0,2},{1,3},{2,0},{3,1},{4,6},{5,7},{6,4},{7,5},{8,10},{9,11},{10,... | collective-permute-start | bytes 196616 | tf_op jit(solution)/shard_map/ppermute | solution.py:238
  21.7 4.1 %collective-permute-start.6 = (bf16[2,64,256]{2,1,0:T(8,128)(2,1)S(1)}, bf16[2,64,256]{2,1,0:T(8,128)(2,1)S(1)}, u32[]{:S(2)}, u32[]{:S(2)}) collective-permute-start(bf16[2,64,256]{2,1,0:T(8,128)(2,1)S(1)} %codes.1.refs_1_.refs_2_), channel_id=1, source_target_pairs={{0,3},{1,2},{2,1},{3,0},{4,7},{5,6},{6,5},{7,4},{8,11},{9,10},{10,... | collective-permute-start | bytes 196616 | tf_op jit(solution)/shard_map/ppermute | solution.py:238
  26.3 14.0 %copy-start.2 = (bf16[2,64,2048]{2,1,0:T(8,128)(2,1)S(1)}, bf16[2,64,2048]{2,1,0:T(8,128)(2,1)}, u32[]{:S(2)}) copy-start(bf16[2,64,2048]{2,1,0:T(8,128)(2,1)} %target_ref.3) | copy-start | bytes 1572868
  26.3 14.0 %copy-start.3 = (f32[2,2048]{1,0:T(2,128)S(1)}, f32[2,2048]{1,0:T(2,128)}, u32[]{:S(2)}) copy-start(f32[2,2048]{1,0:T(2,128)} %bias_ref.3) | copy-start | bytes 49156
  26.4 13.0 %collective-permute-start.13 = (bf16[2,64,384]{2,1,0:T(8,128)(2,1)S(1)}, bf16[2,64,384]{2,1,0:T(8,128)(2,1)S(1)}, u32[]{:S(2)}, u32[]{:S(2)}) collective-permute-start(bf16[2,64,384]{2,1,0:T(8,128)(2,1)S(1)} %get-tuple-element.36), channel_id=1, source_target_pairs={{0,8},{1,9},{4,12},{5,13},{8,0},{9,1},{12,4},{13,5},{2,10},{3,11},... | collective-permute-start | bytes 294920 | tf_op jit(solution)/shard_map/ppermute | solution.py:301
  28.8 10.5 %collective-permute-start.14 = (bf16[2,64,384]{2,1,0:T(8,128)(2,1)S(1)}, bf16[2,64,384]{2,1,0:T(8,128)(2,1)S(1)}, u32[]{:S(2)}, u32[]{:S(2)}) collective-permute-start(bf16[2,64,384]{2,1,0:T(8,128)(2,1)S(1)} %get-tuple-element.37), channel_id=1, source_target_pairs={{0,1},{1,0},{4,5},{5,4},{8,9},{9,8},{12,13},{13,12},{2,3},{3,2},{6... | collective-permute-start | bytes 294920 | tf_op jit(solution)/shard_map/ppermute | solution.py:301
  28.9 11.5 %collective-permute-start.15 = (bf16[2,64,384]{2,1,0:T(8,128)(2,1)S(1)}, bf16[2,64,384]{2,1,0:T(8,128)(2,1)S(1)}, u32[]{:S(2)}, u32[]{:S(2)}) collective-permute-start(bf16[2,64,384]{2,1,0:T(8,128)(2,1)S(1)} %get-tuple-element.38), channel_id=1, source_target_pairs={{0,9},{1,8},{4,13},{5,12},{8,1},{9,0},{12,5},{13,4},{2,11},{3,10},... | collective-permute-start | bytes 294920 | tf_op jit(solution)/shard_map/ppermute | solution.py:301
  30.0 14.6 %collective-permute-start.9 = (bf16[2,64,384]{2,1,0:T(8,128)(2,1)S(1)}, bf16[2,64,384]{2,1,0:T(8,128)(2,1)S(1)}, u32[]{:S(2)}, u32[]{:S(2)}) collective-permute-start(bf16[2,64,384]{2,1,0:T(8,128)(2,1)S(1)} %get-tuple-element.32), channel_id=1, source_target_pairs={{0,8},{1,9},{4,12},{5,13},{8,0},{9,1},{12,4},{13,5},{2,10},{3,11},... | collective-permute-start | bytes 294920 | tf_op jit(solution)/shard_map/ppermute | solution.py:301
  39.3 6.4 %collective-permute-start.10 = (bf16[2,64,384]{2,1,0:T(8,128)(2,1)S(1)}, bf16[2,64,384]{2,1,0:T(8,128)(2,1)S(1)}, u32[]{:S(2)}, u32[]{:S(2)}) collective-permute-start(bf16[2,64,384]{2,1,0:T(8,128)(2,1)S(1)} %get-tuple-element.33), channel_id=1, source_target_pairs={{0,1},{1,0},{4,5},{5,4},{8,9},{9,8},{12,13},{13,12},{2,3},{3,2},{6... | collective-permute-start | bytes 294920 | tf_op jit(solution)/shard_map/ppermute | solution.py:301
  39.3 7.9 %collective-permute-start.11 = (bf16[2,64,384]{2,1,0:T(8,128)(2,1)S(1)}, bf16[2,64,384]{2,1,0:T(8,128)(2,1)S(1)}, u32[]{:S(2)}, u32[]{:S(2)}) collective-permute-start(bf16[2,64,384]{2,1,0:T(8,128)(2,1)S(1)} %get-tuple-element.34), channel_id=1, source_target_pairs={{0,9},{1,8},{4,13},{5,12},{8,1},{9,0},{12,5},{13,4},{2,11},{3,10},... | collective-permute-start | bytes 294920 | tf_op jit(solution)/shard_map/ppermute | solution.py:301
  41.1 1.0 %copy-start.1 = (bf16[2,64,2048]{2,1,0:T(8,128)(2,1)S(1)}, bf16[2,64,2048]{2,1,0:T(8,128)(2,1)}, u32[]{:S(2)}) copy-start(bf16[2,64,2048]{2,1,0:T(8,128)(2,1)} %add.2.refs_6_.refs_8_) | copy-start | bytes 1572868
  42.5 8.9 %collective-permute-start.16 = (bf16[2,64,256]{2,1,0:T(8,128)(2,1)S(1)}, bf16[2,64,256]{2,1,0:T(8,128)(2,1)S(1)}, u32[]{:S(2)}, u32[]{:S(2)}) collective-permute-start(bf16[2,64,256]{2,1,0:T(8,128)(2,1)S(1)} %get-tuple-element.40), channel_id=1, source_target_pairs={{0,8},{1,9},{4,12},{5,13},{8,0},{9,1},{12,4},{13,5},{2,10},{3,11},... | collective-permute-start | bytes 196616 | tf_op jit(solution)/shard_map/ppermute | solution.py:301
  44.6 6.8 %collective-permute-start.17 = (bf16[2,64,256]{2,1,0:T(8,128)(2,1)S(1)}, bf16[2,64,256]{2,1,0:T(8,128)(2,1)S(1)}, u32[]{:S(2)}, u32[]{:S(2)}) collective-permute-start(bf16[2,64,256]{2,1,0:T(8,128)(2,1)S(1)} %get-tuple-element.41), channel_id=1, source_target_pairs={{0,1},{1,0},{4,5},{5,4},{8,9},{9,8},{12,13},{13,12},{2,3},{3,2},{6... | collective-permute-start | bytes 196616 | tf_op jit(solution)/shard_map/ppermute | solution.py:301
  44.6 8.2 %collective-permute-start.18 = (bf16[2,64,256]{2,1,0:T(8,128)(2,1)S(1)}, bf16[2,64,256]{2,1,0:T(8,128)(2,1)S(1)}, u32[]{:S(2)}, u32[]{:S(2)}) collective-permute-start(bf16[2,64,256]{2,1,0:T(8,128)(2,1)S(1)} %get-tuple-element.42), channel_id=1, source_target_pairs={{0,9},{1,8},{4,13},{5,12},{8,1},{9,0},{12,5},{13,4},{2,11},{3,10},... | collective-permute-start | bytes 196616 | tf_op jit(solution)/shard_map/ppermute | solution.py:301

commit v9 on v8

--- a/solution.py
+++ b/solution.py
@@ -117,22 +117,22 @@
     layers, groups, block, cols = dec_ref.shape
     _, first, width = piece
     got_refs, refs = refs[: 1 + shared], refs[1 + shared :]
-    code_refs, out_refs, lhs_ref = refs[: 2 * groups], refs[-2 * half - 1 : -1], refs[-1]
-    src, tgt = lax.axis_index("src"), lax.axis_index("tgt")
+    codes_ref, out_refs, lhs_ref = refs[0], refs[-2 * half - 1 : -1], refs[-1]
+    src = lax.axis_index("src")
     parity = lax.rem(src, 2)
-    share = code_refs[0].shape[1]
+    share = codes_ref.shape[2]
     depth = groups * block
-    for k in range(groups):
-        place = lax.rem(tgt - k + groups, groups)
-        for side in range(2):
-            latents = parity if side == 0 else 1 - parity
-            latents = pl.ds(pl.multiple_of(latents * block, block), block)
-            columns = pl.ds(pl.multiple_of((side * groups + place) * block, block), block)
-            for j in range(half):
-                group = lax.rem(src // 2 + j, half)
-                for r in range(2):
+    for place in range(groups):
+        for r in range(2):
+            origin = place * 2 + lax.rem(lax.axis_index("rep") + r, 2)
+            for side in range(2):
+                latents = parity if side == 0 else 1 - parity
+                latents = pl.ds(pl.multiple_of(latents * block, block), block)
+                columns = slice((side * groups + place) * block, (side * groups + place + 1) * block)
+                for j in range(half):
+                    group = lax.rem(src // 2 + j, half)
                     rows = slice((2 * j + r) * share, (2 * j + r + 1) * share)
-                    lhs_ref[rows, columns] = code_refs[2 * k + r][group, :, latents]
+                    lhs_ref[rows, columns] = codes_ref[origin, group, :, latents]
     start = pl.multiple_of(lax.axis_index("rep") * (cols // 2) + first, LANES)
     for i in range(layers):
         layer = lax.rem(lax.axis_index("parts") + i, layers) if shared else i
@@ -229,13 +229,7 @@
         cost_estimate=cost,
         name="codes",
     )(active, enc_b.reshape(n, block), *terms)
-    codes = []
-    for k in range(groups):
-        for r in range(2):
-            perm = [
-                (i * 2 + c, (i + k) % groups * 2 + (c ^ r)) for i in range(groups) for c in range(2)
-            ]
-            codes.append(lax.ppermute(own, ("tgt", "rep"), perm) if k + r else own)
+    codes = lax.all_gather(own, ("tgt", "rep"), axis=0, tiled=False)
 
     def hold(value, after):
         return pl.pallas_call(
@@ -280,13 +274,13 @@
         terms = pl.pallas_call(
             functools.partial(decode_kernel, n, pieces[i], i == 0),
             out_shape=shapes,
-            in_specs=[vmem] * (1 + len(got[i]) + 2 * groups) + [anywhere] * len(after),
+            in_specs=[vmem] * (1 + len(got[i]) + 1) + [anywhere] * len(after),
             out_specs=[vmem] * len(shapes),
             scratch_shapes=[pltpu.VMEM((rows, 2 * groups * block), jnp.bfloat16)],
             compiler_params=params,
             cost_estimate=cost,
             name="decode",
-        )(dec_rows, *got[i], *codes, *after)
+        )(dec_rows, *got[i], codes, *after)
         after = [terms[0]]
         if i == 0:
             for part in parts[2:]:

time: 53.8 us -> 53.9 us (level)
  blocking collectives: 0 us -> 5.77 us
  waiting for transfers between devices: 24.1 us -> 21.1 us
  starting transfers between devices: 21.6 us -> 19 us
    all_gather x0 -> x1, blocking collectives: none -> 5.77 us  [body(): codes = lax.all_gather(own, ('tgt', 'rep'), axis=0, tiled=False)]
    ppermute x3 -> x0, waiting for transfers between devices: 3.16 us -> none  [body(): codes.append(lax.ppermute(own, ('tgt', 'rep'), perm) if k + r else own)]
    ppermute x3 -> x0, starting transfers between devices: 2.44 us -> none  [body(): codes.append(lax.ppermute(own, ('tgt', 'rep'), perm) if k + r else own)]
  transfers between devices with their start and end apart: 19 -> 16, of which waited for: 10 -> 8; matrix products, arithmetic and copies ran while one was open for 0% -> 0% of each run, Pallas kernels for 5% -> 5%
where the time goes in v9:
time: 53.9 us; the launch traced here: 53.7 us
  waiting for transfers between devices  21.1 us (39%)
  starting transfers between devices  19 us (35%)
  Pallas kernels  6.74 us (13%)
  blocking collectives  5.77 us (11%)
  local copies, waits for them, and re-layouts  1.06 us (2%)
    ppermute x9, waiting for transfers between devices, body(): sums[i].append(lax.ppermute(term, ('src', 'rep'), perm) if j + r else term)  15.1 us
    ppermute x9, starting transfers between devices, body(): sums[i].append(lax.ppermute(term, ('src', 'rep'), perm) if j + r else term)  8.73 us
    ppermute x3, starting transfers between devices, body(): lax.ppermute(terms[k], 'src', [(i, (i + k) % n) for i in range(n)])  7.02 us
    all_gather x1, blocking collectives, body(): codes = lax.all_gather(own, ('tgt', 'rep'), axis=0, tiled=False)  5.77 us
    ppermute x3, waiting for transfers between devices, body(): lax.ppermute(terms[k], 'src', [(i, (i + k) % n) for i in range(n)])  3.38 us
    pallas_call x1, Pallas kernels, body(): pl.pallas_call(functools.partial(encode_kernel, n, pieces), out_shape=[sh...  3.31 us
    ppermute x1, waiting for transfers between devices, body(): got = [[lax.ppermute(parts[0], 'src', pair)]]  2.61 us
    pallas_call x2, Pallas kernels, add(): pl.pallas_call(functools.partial(add_kernel, n, [pieces[i] for i in some]...  1.57 us
  transfers between devices with their start and end apart: 16, of which 8 were waited for; matrix products, arithmetic and copies ran while one was open for 0% of the time, Pallas kernels for 5%

profile of v9, /device:TPU:0, one launch (start us, length us, event | category | flops | bytes accessed | tf_op | source)
XLA Modules:
  0.0 53.7 jit_solution(15422431622729866408)
XLA Ops:
  0.0 3.3 %encode.1 = (bf16[128,256]{1,0:T(8,128)(2,1)S(1)}, bf16[128,256]{1,0:T(8,128)(2,1)S(1)}, bf16[128,256]{1,0:T(8,128)(2,1)S(1)}, bf16[128,256]{1,0:T(8,128)(2,1)S(...) custom-call(bf16[2,2,64,1024]{3,2,1,0:T(8,128)(2,1)} %bitcast.7, ...), custom_call_target="tpu_custom_call" | custom-call | tf_op jit(solution)/shard_map/encode/pallas_call | solution.py:200
  3.3 3.1 %collective-permute-start = (bf16[128,256]{1,0:T(8,128)(2,1)S(1)}, bf16[128,256]{1,0:T(8,128)(2,1)S(1)}, u32[]{:S(2)}, u32[]{:S(2)}) collective-permute-start(bf16[128,256]{1,0:T(8,128)(2,1)S(1)} %get-tuple-element.26), channel_id=1, source_target_pairs={{0,4},{4,8},{8,12},{12,0},{1,5},{5,9},{9,13},{13,1},{2,6},{6,10},{... | collective-permute-start | bytes 196616 | tf_op jit(solution)/shard_map/ppermute | solution.py:222
  6.4 2.6 %collective-permute-start.1 = (bf16[128,256]{1,0:T(8,128)(2,1)S(1)}, bf16[128,256]{1,0:T(8,128)(2,1)S(1)}, u32[]{:S(2)}, u32[]{:S(2)}) collective-permute-start(bf16[128,256]{1,0:T(8,128)(2,1)S(1)} %get-tuple-element.27), channel_id=1, source_target_pairs={{0,8},{4,12},{8,0},{12,4},{1,9},{5,13},{9,1},{13,5},{2,10},{6,14},... | collective-permute-start | bytes 196616 | tf_op jit(solution)/shard_map/ppermute | solution.py:222
  9.0 1.3 %collective-permute-start.2 = (bf16[128,256]{1,0:T(8,128)(2,1)S(1)}, bf16[128,256]{1,0:T(8,128)(2,1)S(1)}, u32[]{:S(2)}, u32[]{:S(2)}) collective-permute-start(bf16[128,256]{1,0:T(8,128)(2,1)S(1)} %get-tuple-element.28), channel_id=1, source_target_pairs={{0,12},{4,0},{8,4},{12,8},{1,13},{5,1},{9,5},{13,9},{2,14},{6,2},{... | collective-permute-start | bytes 196616 | tf_op jit(solution)/shard_map/ppermute | solution.py:222
  10.3 0.7 %collective-permute-start.4 = (bf16[1,2,128,384]{3,2,1,0:T(8,128)(2,1)S(1)}, bf16[1,2,128,384]{3,2,1,0:T(8,128)(2,1)S(1)}, u32[]{:S(2)}, u32[]{:S(2)}) collective-permute-start(bf16[1,2,128,384]{3,2,1,0:T(8,128)(2,1)S(1)} %get-tuple-element.29), channel_id=1, source_target_pairs={{0,4},{4,0},{8,12},{12,8},{1,5},{5,1},{9,13},{13,9},{2,6},{6,2},{1... | collective-permute-start | bytes 589832 | tf_op jit(solution)/shard_map/ppermute | solution.py:246
  11.0 0.0 collective-permute-done.refs_1_
  11.0 2.5 %collective-permute-done.1.refs_2_ = bf16[128,256]{1,0:T(8,128)(2,1)S(1)} collective-permute-done((bf16[128,256]{1,0:T(8,128)(2,1)S(1)}, bf16[128,256]{1,0:T(8,128)(2,1)S(1)}, u32[]{:S(2)}, u32[]{:S(2)}) %collective-permute-start.1) | collective-permute-done | bytes 65568 | tf_op jit(solution)/shard_map/ppermute | solution.py:222
  13.5 0.9 %collective-permute-done.2.refs_3_ = bf16[128,256]{1,0:T(8,128)(2,1)S(1)} collective-permute-done((bf16[128,256]{1,0:T(8,128)(2,1)S(1)}, bf16[128,256]{1,0:T(8,128)(2,1)S(1)}, u32[]{:S(2)}, u32[]{:S(2)}) %collective-permute-start.2) | collective-permute-done | bytes 65568 | tf_op jit(solution)/shard_map/ppermute | solution.py:222
  14.4 0.0 copy-done.5
  14.4 0.0 copy-done.4
  14.4 0.6 %codes.1.refs_1_ = bf16[2,64,256]{2,1,0:T(8,128)(2,1)S(1)} custom-call(s32[2,8]{1,0:T(2,128)S(1)} %copy-done.5, f32[4,128]{1,0:T(4,128)S(1)} %bitcast.6, bf16[128,256]{1,0:T(8,128)(2,1)S(1)} %get-tuple-element.25.refs_0_, bf16[128,256]{1,0:T(8,128)(2,1)S(1)} %collective-permute-done.refs_1_, bf16[128,256]{1,0:T(8,128)(2,1)S(1)} %collective-permute-done.1.refs_2_, ...), custom_call_target="tpu_custom_call" | custom-call | tf_op jit(solution)/shard_map/codes/pallas_call | solution.py:223
  15.1 1.0 %collective-permute-start.3 = (bf16[2,2,128,384]{3,2,1,0:T(8,128)(2,1)S(1)}, bf16[2,2,128,384]{3,2,1,0:T(8,128)(2,1)S(1)}, u32[]{:S(2)}, u32[]{:S(2)}) collective-permute-start(bf16[2,2,128,384]{3,2,1,0:T(8,128)(2,1)S(1)} %hold.2), channel_id=1, source_target_pairs={{0,4},{4,0},{8,12},{12,8},{1,5},{5,1},{9,13},{13,9},{2,6},{6,2},{1... | collective-permute-start | bytes 1179656 | tf_op jit(solution)/shard_map/ppermute | solution.py:249
  16.0 2.6 %collective-permute-done.4.refs_0_ = bf16[1,2,128,384]{3,2,1,0:T(8,128)(2,1)S(1)} collective-permute-done((bf16[1,2,128,384]{3,2,1,0:T(8,128)(2,1)S(1)}, bf16[1,2,128,384]{3,2,1,0:T(8,128)(2,1)S(1)}, u32[]{:S(2)}, u32[]{:S(2)}) %collective-permute-start.4) | collective-permute-done | bytes 196640 | tf_op jit(solution)/shard_map/ppermute | solution.py:246
  18.6 1.5 %collective-permute-start.5 = (bf16[1,2,128,384]{3,2,1,0:T(8,128)(2,1)S(1)}, bf16[1,2,128,384]{3,2,1,0:T(8,128)(2,1)S(1)}, u32[]{:S(2)}, u32[]{:S(2)}) collective-permute-start(bf16[1,2,128,384]{3,2,1,0:T(8,128)(2,1)S(1)} %collective-permute-done.4.refs_0_), channel_id=1, source_target_pairs={{0,16},{16,0},{1,17},{17,1},{2,18},{18,2},{3,19},{19,3},{4,20},{20... | collective-permute-start | bytes 589832 | tf_op jit(solution)/shard_map/ppermute | solution.py:247
  20.2 0.1 collective-permute-start.9
  20.2 5.8 %all-gather = bf16[8,64,256]{2,1,0:T(8,128)(2,1)S(1)} all-gather(bf16[2,64,256]{2,1,0:T(8,128)(2,1)S(1)} %codes.1.refs_1_), channel_id=2, replica_groups=mesh['parts'=2,'src'=4,'tgt'=2,'rep'=2] {'tgt','rep'}, dimensions={0}, use_global_device_ids=true | all-gather | bytes 327680 | tf_op jit(solution)/shard_map/all_gather | solution.py:232
  26.0 0.0 collective-permute-done.5.refs_1_
  26.0 0.0 copy-done
  26.0 0.5 decode.3
  26.5 0.0 copy-start.2
  26.5 0.0 copy-start.3
  26.5 2.3 %collective-permute-start.10 = (bf16[2,64,384]{2,1,0:T(8,128)(2,1)S(1)}, bf16[2,64,384]{2,1,0:T(8,128)(2,1)S(1)}, u32[]{:S(2)}, u32[]{:S(2)}) collective-permute-start(bf16[2,64,384]{2,1,0:T(8,128)(2,1)S(1)} %get-tuple-element.36), channel_id=1, source_target_pairs={{0,8},{1,9},{4,12},{5,13},{8,0},{9,1},{12,4},{13,5},{2,10},{3,11},... | collective-permute-start | bytes 294920 | tf_op jit(solution)/shard_map/ppermute | solution.py:295
  28.8 0.1 collective-permute-start.11
  28.9 0.7 %collective-permute-start.12 = (bf16[2,64,384]{2,1,0:T(8,128)(2,1)S(1)}, bf16[2,64,384]{2,1,0:T(8,128)(2,1)S(1)}, u32[]{:S(2)}, u32[]{:S(2)}) collective-permute-start(bf16[2,64,384]{2,1,0:T(8,128)(2,1)S(1)} %get-tuple-element.38), channel_id=1, source_target_pairs={{0,9},{1,8},{4,13},{5,12},{8,1},{9,0},{12,5},{13,4},{2,11},{3,10},... | collective-permute-start | bytes 294920 | tf_op jit(solution)/shard_map/ppermute | solution.py:295
  29.6 0.0 collective-permute-done.3.refs_0_
  29.6 0.4 decode.4
  30.1 2.3 %collective-permute-start.6 = (bf16[2,64,384]{2,1,0:T(8,128)(2,1)S(1)}, bf16[2,64,384]{2,1,0:T(8,128)(2,1)S(1)}, u32[]{:S(2)}, u32[]{:S(2)}) collective-permute-start(bf16[2,64,384]{2,1,0:T(8,128)(2,1)S(1)} %get-tuple-element.32), channel_id=1, source_target_pairs={{0,8},{1,9},{4,12},{5,13},{8,0},{9,1},{12,4},{13,5},{2,10},{3,11},... | collective-permute-start | bytes 294920 | tf_op jit(solution)/shard_map/ppermute | solution.py:295
  32.4 7.0 %collective-permute-done.10.refs_1_ = bf16[2,64,384]{2,1,0:T(8,128)(2,1)S(1)} collective-permute-done((bf16[2,64,384]{2,1,0:T(8,128)(2,1)S(1)}, bf16[2,64,384]{2,1,0:T(8,128)(2,1)S(1)}, u32[]{:S(2)}, u32[]{:S(2)}) %collective-permute-start.10) | collective-permute-done | bytes 98336 | tf_op jit(solution)/shard_map/ppermute | solution.py:295
  39.4 0.0 collective-permute-start.7
  39.4 0.0 collective-permute-done.11.refs_2_
  39.4 0.0 collective-permute-start.8
  39.4 0.9 %collective-permute-done.12.refs_3_ = bf16[2,64,384]{2,1,0:T(8,128)(2,1)S(1)} collective-permute-done((bf16[2,64,384]{2,1,0:T(8,128)(2,1)S(1)}, bf16[2,64,384]{2,1,0:T(8,128)(2,1)S(1)}, u32[]{:S(2)}, u32[]{:S(2)}) %collective-permute-start.12) | collective-permute-done | bytes 98336 | tf_op jit(solution)/shard_map/ppermute | solution.py:295
  40.4 0.0 copy-done.3
  40.4 0.7 %add.2.refs_3_.refs_8_ = bf16[2,64,2048]{2,1,0:T(8,128)(2,1)} custom-call(f32[2,2048]{1,0:T(2,128)S(1)} %copy-done.3, bf16[2,64,2048]{2,1,0:T(8,128)(2,1)S(1)} %copy-done.2, f32[2,64,384]{2,1,0:T(8,128)S(1)} %get-tuple-element.30.refs_2_.refs_0_, bf16[2,64,384]{2,1,0:T(8,128)(2,1)S(1)} %collective-permute-done.10.refs_1_, ...), custom_call_target="tpu_custom_call" | custom-call | tf_op jit(solution)/shard_map/add/pallas_call | solution.py:252
  41.1 0.0 collective-permute-done.9.refs_0_
  41.2 0.0 copy-start.1
  41.2 1.0 %copy-done.1 = bf16[2,64,2048]{2,1,0:T(8,128)(2,1)S(1)} copy-done((bf16[2,64,2048]{2,1,0:T(8,128)(2,1)S(1)}, bf16[2,64,2048]{2,1,0:T(8,128)(2,1)}, u32[]{:S(2)}) %copy-start.1) | copy-done | bytes 524312
  42.2 0.3 decode.5
  42.5 2.2 %collective-permute-start.13 = (bf16[2,64,256]{2,1,0:T(8,128)(2,1)S(1)}, bf16[2,64,256]{2,1,0:T(8,128)(2,1)S(1)}, u32[]{:S(2)}, u32[]{:S(2)}) collective-permute-start(bf16[2,64,256]{2,1,0:T(8,128)(2,1)S(1)} %get-tuple-element.40), channel_id=1, source_target_pairs={{0,8},{1,9},{4,12},{5,13},{8,0},{9,1},{12,4},{13,5},{2,10},{3,11},... | collective-permute-start | bytes 196616 | tf_op jit(solution)/shard_map/ppermute | solution.py:295
  44.7 0.0 collective-permute-start.14
  44.7 0.0 collective-permute-done.6.refs_1_
  44.7 1.1 %collective-permute-start.15 = (bf16[2,64,256]{2,1,0:T(8,128)(2,1)S(1)}, bf16[2,64,256]{2,1,0:T(8,128)(2,1)S(1)}, u32[]{:S(2)}, u32[]{:S(2)}) collective-permute-start(bf16[2,64,256]{2,1,0:T(8,128)(2,1)S(1)} %get-tuple-element.42), channel_id=1, source_target_pairs={{0,9},{1,8},{4,13},{5,12},{8,1},{9,0},{12,5},{13,4},{2,11},{3,10},... | collective-permute-start | bytes 196616 | tf_op jit(solution)/shard_map/ppermute | solution.py:295
  45.8 0.0 collective-permute-done.7.refs_2_
  45.8 1.5 %collective-permute-done.8.refs_3_ = bf16[2,64,384]{2,1,0:T(8,128)(2,1)S(1)} collective-permute-done((bf16[2,64,384]{2,1,0:T(8,128)(2,1)S(1)}, bf16[2,64,384]{2,1,0:T(8,128)(2,1)S(1)}, u32[]{:S(2)}, u32[]{:S(2)}) %collective-permute-start.8) | collective-permute-done | bytes 98336 | tf_op jit(solution)/shard_map/ppermute | solution.py:295
  47.3 4.2 %collective-permute-done.13.refs_5_ = bf16[2,64,256]{2,1,0:T(8,128)(2,1)S(1)} collective-permute-done((bf16[2,64,256]{2,1,0:T(8,128)(2,1)S(1)}, bf16[2,64,256]{2,1,0:T(8,128)(2,1)S(1)}, u32[]{:S(2)}, u32[]{:S(2)}) %collective-permute-start.13) | collective-permute-done | bytes 65568 | tf_op jit(solution)/shard_map/ppermute | solution.py:295
  51.5 0.0 collective-permute-done.14.refs_6_
  51.5 1.4 %collective-permute-done.15.refs_7_ = bf16[2,64,256]{2,1,0:T(8,128)(2,1)S(1)} collective-permute-done((bf16[2,64,256]{2,1,0:T(8,128)(2,1)S(1)}, bf16[2,64,256]{2,1,0:T(8,128)(2,1)S(1)}, u32[]{:S(2)}, u32[]{:S(2)}) %collective-permute-start.15) | collective-permute-done | bytes 65568 | tf_op jit(solution)/shard_map/ppermute | solution.py:295
  52.9 0.8 %add.3 = bf16[2,64,2048]{2,1,0:T(8,128)(2,1)} custom-call(f32[2,2048]{1,0:T(2,128)S(1)} %copy-done.3, bf16[2,64,2048]{2,1,0:T(8,128)(2,1)S(1)} %copy-done.2, f32[2,64,384]{2,1,0:T(8,128)S(1)} %get-tuple-element.31.refs_2_.refs_0_, bf16[2,64,384]{2,1,0:T(8,128)(2,1)S(1)} %collective-permute-done.6.refs_1_, ...), custom_call_target="tpu_custom_call", output_to_operand_aliasing={{}: (10, {})} | custom-call | tf_op jit(solution)/shard_map/add/pallas_call | solution.py:252
  (6 shorter events, 0.0 us)
Async XLA Ops:
  0.0 14.4 %copy-start.5 = (s32[2,8]{1,0:T(2,128)S(1)}, s32[2,8]{1,0:T(2,128)}, u32[]{:S(2)}) copy-start(s32[2,8]{1,0:T(2,128)} %active_ref.1) | copy-start | bytes 196
  0.0 14.4 %copy-start.4 = (f32[512]{0:T(512)S(1)}, f32[512]{0:T(512)}, u32[]{:S(2)}) copy-start(f32[512]{0:T(512)} %param.9) | copy-start | bytes 6148
  0.0 26.0 %copy-start = (bf16[2,2,128,2048]{3,2,1,0:T(8,128)(2,1)S(1)}, bf16[2,2,128,2048]{3,2,1,0:T(8,128)(2,1)}, u32[]{:S(2)}) copy-start(bf16[2,2,128,2048]{3,2,1,0:T(8,128)(2,1)} %dec_ref.5) | copy-start | bytes 6291460
  3.3 7.7 %collective-permute-start = (bf16[128,256]{1,0:T(8,128)(2,1)S(1)}, bf16[128,256]{1,0:T(8,128)(2,1)S(1)}, u32[]{:S(2)}, u32[]{:S(2)}) collective-permute-start(bf16[128,256]{1,0:T(8,128)(2,1)S(1)} %get-tuple-element.26), channel_id=1, source_target_pairs={{0,4},{4,8},{8,12},{12,0},{1,5},{5,9},{9,13},{13,1},{2,6},{6,10},{... | collective-permute-start | bytes 196616 | tf_op jit(solution)/shard_map/ppermute | solution.py:222
  6.4 7.1 %collective-permute-start.1 = (bf16[128,256]{1,0:T(8,128)(2,1)S(1)}, bf16[128,256]{1,0:T(8,128)(2,1)S(1)}, u32[]{:S(2)}, u32[]{:S(2)}) collective-permute-start(bf16[128,256]{1,0:T(8,128)(2,1)S(1)} %get-tuple-element.27), channel_id=1, source_target_pairs={{0,8},{4,12},{8,0},{12,4},{1,9},{5,13},{9,1},{13,5},{2,10},{6,14},... | collective-permute-start | bytes 196616 | tf_op jit(solution)/shard_map/ppermute | solution.py:222
  9.0 5.4 %collective-permute-start.2 = (bf16[128,256]{1,0:T(8,128)(2,1)S(1)}, bf16[128,256]{1,0:T(8,128)(2,1)S(1)}, u32[]{:S(2)}, u32[]{:S(2)}) collective-permute-start(bf16[128,256]{1,0:T(8,128)(2,1)S(1)} %get-tuple-element.28), channel_id=1, source_target_pairs={{0,12},{4,0},{8,4},{12,8},{1,13},{5,1},{9,5},{13,9},{2,14},{6,2},{... | collective-permute-start | bytes 196616 | tf_op jit(solution)/shard_map/ppermute | solution.py:222
  10.3 8.3 %collective-permute-start.4 = (bf16[1,2,128,384]{3,2,1,0:T(8,128)(2,1)S(1)}, bf16[1,2,128,384]{3,2,1,0:T(8,128)(2,1)S(1)}, u32[]{:S(2)}, u32[]{:S(2)}) collective-permute-start(bf16[1,2,128,384]{3,2,1,0:T(8,128)(2,1)S(1)} %get-tuple-element.29), channel_id=1, source_target_pairs={{0,4},{4,0},{8,12},{12,8},{1,5},{5,1},{9,13},{13,9},{2,6},{6,2},{1... | collective-permute-start | bytes 589832 | tf_op jit(solution)/shard_map/ppermute | solution.py:246
  15.1 14.5 %collective-permute-start.3 = (bf16[2,2,128,384]{3,2,1,0:T(8,128)(2,1)S(1)}, bf16[2,2,128,384]{3,2,1,0:T(8,128)(2,1)S(1)}, u32[]{:S(2)}, u32[]{:S(2)}) collective-permute-start(bf16[2,2,128,384]{3,2,1,0:T(8,128)(2,1)S(1)} %hold.2), channel_id=1, source_target_pairs={{0,4},{4,0},{8,12},{12,8},{1,5},{5,1},{9,13},{13,9},{2,6},{6,2},{1... | collective-permute-start | bytes 1179656 | tf_op jit(solution)/shard_map/ppermute | solution.py:249
  18.6 7.4 %collective-permute-start.5 = (bf16[1,2,128,384]{3,2,1,0:T(8,128)(2,1)S(1)}, bf16[1,2,128,384]{3,2,1,0:T(8,128)(2,1)S(1)}, u32[]{:S(2)}, u32[]{:S(2)}) collective-permute-start(bf16[1,2,128,384]{3,2,1,0:T(8,128)(2,1)S(1)} %collective-permute-done.4.refs_0_), channel_id=1, source_target_pairs={{0,16},{16,0},{1,17},{17,1},{2,18},{18,2},{3,19},{19,3},{4,20},{20... | collective-permute-start | bytes 589832 | tf_op jit(solution)/shard_map/ppermute | solution.py:247
  20.2 21.0 %collective-permute-start.9 = (bf16[2,2,128,256]{3,2,1,0:T(8,128)(2,1)S(1)}, bf16[2,2,128,256]{3,2,1,0:T(8,128)(2,1)S(1)}, u32[]{:S(2)}, u32[]{:S(2)}) collective-permute-start(bf16[2,2,128,256]{3,2,1,0:T(8,128)(2,1)S(1)} %hold.3), channel_id=1, source_target_pairs={{0,4},{4,0},{8,12},{12,8},{1,5},{5,1},{9,13},{13,9},{2,6},{6,2},{1... | collective-permute-start | bytes 786440 | tf_op jit(solution)/shard_map/ppermute | solution.py:287
  26.5 13.9 %copy-start.2 = (bf16[2,64,2048]{2,1,0:T(8,128)(2,1)S(1)}, bf16[2,64,2048]{2,1,0:T(8,128)(2,1)}, u32[]{:S(2)}) copy-start(bf16[2,64,2048]{2,1,0:T(8,128)(2,1)} %target_ref.3) | copy-start | bytes 1572868
  26.5 13.9 %copy-start.3 = (f32[2,2048]{1,0:T(2,128)S(1)}, f32[2,2048]{1,0:T(2,128)}, u32[]{:S(2)}) copy-start(f32[2,2048]{1,0:T(2,128)} %bias_ref.3) | copy-start | bytes 49156
  26.5 12.9 %collective-permute-start.10 = (bf16[2,64,384]{2,1,0:T(8,128)(2,1)S(1)}, bf16[2,64,384]{2,1,0:T(8,128)(2,1)S(1)}, u32[]{:S(2)}, u32[]{:S(2)}) collective-permute-start(bf16[2,64,384]{2,1,0:T(8,128)(2,1)S(1)} %get-tuple-element.36), channel_id=1, source_target_pairs={{0,8},{1,9},{4,12},{5,13},{8,0},{9,1},{12,4},{13,5},{2,10},{3,11},... | collective-permute-start | bytes 294920 | tf_op jit(solution)/shard_map/ppermute | solution.py:295
  28.8 10.6 %collective-permute-start.11 = (bf16[2,64,384]{2,1,0:T(8,128)(2,1)S(1)}, bf16[2,64,384]{2,1,0:T(8,128)(2,1)S(1)}, u32[]{:S(2)}, u32[]{:S(2)}) collective-permute-start(bf16[2,64,384]{2,1,0:T(8,128)(2,1)S(1)} %get-tuple-element.37), channel_id=1, source_target_pairs={{0,1},{1,0},{4,5},{5,4},{8,9},{9,8},{12,13},{13,12},{2,3},{3,2},{6... | collective-permute-start | bytes 294920 | tf_op jit(solution)/shard_map/ppermute | solution.py:295
  28.9 11.5 %collective-permute-start.12 = (bf16[2,64,384]{2,1,0:T(8,128)(2,1)S(1)}, bf16[2,64,384]{2,1,0:T(8,128)(2,1)S(1)}, u32[]{:S(2)}, u32[]{:S(2)}) collective-permute-start(bf16[2,64,384]{2,1,0:T(8,128)(2,1)S(1)} %get-tuple-element.38), channel_id=1, source_target_pairs={{0,9},{1,8},{4,13},{5,12},{8,1},{9,0},{12,5},{13,4},{2,11},{3,10},... | collective-permute-start | bytes 294920 | tf_op jit(solution)/shard_map/ppermute | solution.py:295
  30.1 14.6 %collective-permute-start.6 = (bf16[2,64,384]{2,1,0:T(8,128)(2,1)S(1)}, bf16[2,64,384]{2,1,0:T(8,128)(2,1)S(1)}, u32[]{:S(2)}, u32[]{:S(2)}) collective-permute-start(bf16[2,64,384]{2,1,0:T(8,128)(2,1)S(1)} %get-tuple-element.32), channel_id=1, source_target_pairs={{0,8},{1,9},{4,12},{5,13},{8,0},{9,1},{12,4},{13,5},{2,10},{3,11},... | collective-permute-start | bytes 294920 | tf_op jit(solution)/shard_map/ppermute | solution.py:295
  39.4 6.4 %collective-permute-start.7 = (bf16[2,64,384]{2,1,0:T(8,128)(2,1)S(1)}, bf16[2,64,384]{2,1,0:T(8,128)(2,1)S(1)}, u32[]{:S(2)}, u32[]{:S(2)}) collective-permute-start(bf16[2,64,384]{2,1,0:T(8,128)(2,1)S(1)} %get-tuple-element.33), channel_id=1, source_target_pairs={{0,1},{1,0},{4,5},{5,4},{8,9},{9,8},{12,13},{13,12},{2,3},{3,2},{6... | collective-permute-start | bytes 294920 | tf_op jit(solution)/shard_map/ppermute | solution.py:295
  39.4 7.8 %collective-permute-start.8 = (bf16[2,64,384]{2,1,0:T(8,128)(2,1)S(1)}, bf16[2,64,384]{2,1,0:T(8,128)(2,1)S(1)}, u32[]{:S(2)}, u32[]{:S(2)}) collective-permute-start(bf16[2,64,384]{2,1,0:T(8,128)(2,1)S(1)} %get-tuple-element.34), channel_id=1, source_target_pairs={{0,9},{1,8},{4,13},{5,12},{8,1},{9,0},{12,5},{13,4},{2,11},{3,10},... | collective-permute-start | bytes 294920 | tf_op jit(solution)/shard_map/ppermute | solution.py:295
  41.2 1.0 %copy-start.1 = (bf16[2,64,2048]{2,1,0:T(8,128)(2,1)S(1)}, bf16[2,64,2048]{2,1,0:T(8,128)(2,1)}, u32[]{:S(2)}) copy-start(bf16[2,64,2048]{2,1,0:T(8,128)(2,1)} %add.2.refs_3_.refs_8_) | copy-start | bytes 1572868
  42.5 9.0 %collective-permute-start.13 = (bf16[2,64,256]{2,1,0:T(8,128)(2,1)S(1)}, bf16[2,64,256]{2,1,0:T(8,128)(2,1)S(1)}, u32[]{:S(2)}, u32[]{:S(2)}) collective-permute-start(bf16[2,64,256]{2,1,0:T(8,128)(2,1)S(1)} %get-tuple-element.40), channel_id=1, source_target_pairs={{0,8},{1,9},{4,12},{5,13},{8,0},{9,1},{12,4},{13,5},{2,10},{3,11},... | collective-permute-start | bytes 196616 | tf_op jit(solution)/shard_map/ppermute | solution.py:295
  44.7 6.8 %collective-permute-start.14 = (bf16[2,64,256]{2,1,0:T(8,128)(2,1)S(1)}, bf16[2,64,256]{2,1,0:T(8,128)(2,1)S(1)}, u32[]{:S(2)}, u32[]{:S(2)}) collective-permute-start(bf16[2,64,256]{2,1,0:T(8,128)(2,1)S(1)} %get-tuple-element.41), channel_id=1, source_target_pairs={{0,1},{1,0},{4,5},{5,4},{8,9},{9,8},{12,13},{13,12},{2,3},{3,2},{6... | collective-permute-start | bytes 196616 | tf_op jit(solution)/shard_map/ppermute | solution.py:295
  44.7 8.2 %collective-permute-start.15 = (bf16[2,64,256]{2,1,0:T(8,128)(2,1)S(1)}, bf16[2,64,256]{2,1,0:T(8,128)(2,1)S(1)}, u32[]{:S(2)}, u32[]{:S(2)}) collective-permute-start(bf16[2,64,256]{2,1,0:T(8,128)(2,1)S(1)} %get-tuple-element.42), channel_id=1, source_target_pairs={{0,9},{1,8},{4,13},{5,12},{8,1},{9,0},{12,5},{13,4},{2,11},{3,10},... | collective-permute-start | bytes 196616 | tf_op jit(solution)/shard_map/ppermute | solution.py:295

commit v10 on v8

--- a/solution.py
+++ b/solution.py
@@ -9,7 +9,7 @@
 
 VMEM_BYTES = 32 * 1024 * 1024
 LANES = 128
-SHARES = (3, 3, 2)
+SHARES = (4, 4)
 
 
 def cut_pieces(layers, columns):
@@ -21,6 +21,10 @@
             pieces.append((tuple(range(layers)), start * LANES, (stop - start) * LANES))
         start = stop
     return pieces
+
+
+def peer(index, k, n):
+    return index ^ k if n & (n - 1) == 0 else (index + k) % n
 
 
 def part_copies(piece, dec_hbm, part_ref, sems):
@@ -65,7 +69,7 @@
         copies_part += part_copies(piece, dec_hbm, part_refs[i], part_sems.at[i])
     src = lax.axis_index("src")
     for k in range(n):
-        dest = lax.rem(src + k, n)
+        dest = peer(src, k, n)
         rows = acts_ref[lax.rem(dest, 2)]
         rows = rows.reshape(rows.shape[0] * rows.shape[1], rows.shape[2])
         columns = pl.ds(pl.multiple_of((dest // 2) * width, width), width)
@@ -219,7 +223,7 @@
     )(acts, enc_w, dec_w)
     terms, parts = list(results[:n]), list(results[n:])
     for k in range(1, n):
-        terms[k] = lax.ppermute(terms[k], "src", [(i, (i + k) % n) for i in range(n)])
+        terms[k] = lax.ppermute(terms[k], "src", [(i, peer(i, k, n)) for i in range(n)])
     own = pl.pallas_call(
         functools.partial(codes_kernel, n, share, tile_rows),
         out_shape=shape(half, share, 2 * block),
@@ -252,7 +256,7 @@
     got = [[lax.ppermute(parts[0], "src", pair)]]
     got[0].append(lax.ppermute(got[0][0], "parts", [(0, 1), (1, 0)]))
     if len(pieces) > 1:
-        got.append([lax.ppermute(hold(parts[1], own), "src", pair)])
+        got.append([lax.ppermute(hold(parts[1], codes[1]), "src", pair)])
     def add(some, begun):
         operands = [value for i in some for value in sums[i]]
         return pl.pallas_call(

time: 53.8 us -> 53 us (0.985)
  waiting for transfers between devices: 24.1 us -> 33.5 us
  starting transfers between devices: 21.6 us -> 13 us
  local copies, waits for them, and re-layouts: 1.06 us -> 0.02 us
  Pallas kernels: 6.81 us -> 5.79 us
    ppermute x5 -> x4, waiting for transfers between devices: 3.39 us -> 9.96 us  [the longest x3 5.91 us: body(): lax.ppermute(terms[k], 'src', [(i, peer(i, k, n)) for i in range(n)])]
    ppermute x9 -> x6, starting transfers between devices: 8.85 us -> 3.25 us  [body(): sums[i].append(lax.ppermute(term, ('src', 'rep'), perm) if j + r else term)]
    ppermute x5 -> x4, starting transfers between devices: 8.03 us -> 5.68 us  [the longest x3 5.67 us: body(): lax.ppermute(terms[k], 'src', [(i, peer(i, k, n)) for i in range(n)])]
    ppermute x3, waiting for transfers between devices: 3.16 us -> 5.51 us  [body(): codes.append(lax.ppermute(own, ('tgt', 'rep'), perm) if k + r else own)]
    ppermute x9 -> x6, waiting for transfers between devices: 14.9 us -> 17 us  [body(): sums[i].append(lax.ppermute(term, ('src', 'rep'), perm) if j + r else term)]
    ppermute x1, waiting for transfers between devices: 2.61 us -> 0.8 us  [body(): got = [[lax.ppermute(parts[0], 'src', pair)]]]
    unnamed x12 -> x10, local copies, waits for them, and re-layouts: 1.06 us -> 0.02 us
    ppermute x3, starting transfers between devices: 2.44 us -> 1.6 us  [body(): codes.append(lax.ppermute(own, ('tgt', 'rep'), perm) if k + r else own)]
  transfers between devices with their start and end apart: 19 -> 15, of which waited for: 10 -> 12; matrix products, arithmetic and copies ran while one was open for 0% -> 0% of each run, Pallas kernels for 5% -> 3%
where the time goes in v10:
time: 53 us; the launch traced here: 52.3 us
  waiting for transfers between devices  33.5 us (63%)
  starting transfers between devices  13 us (25%)
  Pallas kernels  5.79 us (11%)
    ppermute x6, waiting for transfers between devices, body(): sums[i].append(lax.ppermute(term, ('src', 'rep'), perm) if j + r else term)  17 us
    ppermute x3, waiting for transfers between devices, body(): lax.ppermute(terms[k], 'src', [(i, peer(i, k, n)) for i in range(n)])  5.91 us
    ppermute x3, starting transfers between devices, body(): lax.ppermute(terms[k], 'src', [(i, peer(i, k, n)) for i in range(n)])  5.67 us
    ppermute x3, waiting for transfers between devices, body(): codes.append(lax.ppermute(own, ('tgt', 'rep'), perm) if k + r else own)  5.51 us
    ppermute x1, waiting for transfers between devices, body(): got.append([lax.ppermute(hold(parts[1], codes[1]), 'src', pair)])  4.05 us
    pallas_call x1, Pallas kernels, body(): pl.pallas_call(functools.partial(encode_kernel, n, pieces), out_shape=[sh...  3.3 us
    ppermute x6, starting transfers between devices, body(): sums[i].append(lax.ppermute(term, ('src', 'rep'), perm) if j + r else term)  3.25 us
    ppermute x3, starting transfers between devices, body(): codes.append(lax.ppermute(own, ('tgt', 'rep'), perm) if k + r else own)  1.6 us
  transfers between devices with their start and end apart: 15, of which 12 were waited for; matrix products, arithmetic and copies ran while one was open for 0% of the time, Pallas kernels for 3%

profile of v10, /device:TPU:0, one launch (start us, length us, event | category | flops | bytes accessed | tf_op | source)
XLA Modules:
  0.0 52.3 jit_solution(16696806778095023796)
XLA Ops:
  0.0 0.0 copy-start.4
  0.0 0.0 copy-start.3
  0.0 0.0 copy-start
  0.0 3.3 %encode.1 = (bf16[128,256]{1,0:T(8,128)(2,1)S(1)}, bf16[128,256]{1,0:T(8,128)(2,1)S(1)}, bf16[128,256]{1,0:T(8,128)(2,1)S(1)}, bf16[128,256]{1,0:T(8,128)(2,1)S(...) custom-call(bf16[2,2,64,1024]{3,2,1,0:T(8,128)(2,1)} %bitcast.3, bf16[1024,512]{1,0:T(8,128)(2,1)} %w_hbm.1, ...), custom_call_target="tpu_custom_call" | custom-call | tf_op jit(solution)/shard_map/encode/pallas_call | solution.py:204
  3.3 3.1 %collective-permute-start.2 = (bf16[128,256]{1,0:T(8,128)(2,1)S(1)}, bf16[128,256]{1,0:T(8,128)(2,1)S(1)}, u32[]{:S(2)}, u32[]{:S(2)}) collective-permute-start(bf16[128,256]{1,0:T(8,128)(2,1)S(1)} %get-tuple-element.21), channel_id=1, source_target_pairs={{0,4},{4,0},{8,12},{12,8},{1,5},{5,1},{9,13},{13,9},{2,6},{6,2},{1... | collective-permute-start | bytes 196616 | tf_op jit(solution)/shard_map/ppermute | solution.py:226
  6.4 2.6 %collective-permute-start.3 = (bf16[128,256]{1,0:T(8,128)(2,1)S(1)}, bf16[128,256]{1,0:T(8,128)(2,1)S(1)}, u32[]{:S(2)}, u32[]{:S(2)}) collective-permute-start(bf16[128,256]{1,0:T(8,128)(2,1)S(1)} %get-tuple-element.22), channel_id=1, source_target_pairs={{0,8},{4,12},{8,0},{12,4},{1,9},{5,13},{9,1},{13,5},{2,10},{6,14},... | collective-permute-start | bytes 196616 | tf_op jit(solution)/shard_map/ppermute | solution.py:226
  9.0 0.0 collective-permute-start.4
  9.0 0.9 %collective-permute-start = (bf16[1,2,128,512]{3,2,1,0:T(8,128)(2,1)S(1)}, bf16[1,2,128,512]{3,2,1,0:T(8,128)(2,1)S(1)}, u32[]{:S(2)}, u32[]{:S(2)}) collective-permute-start(bf16[1,2,128,512]{3,2,1,0:T(8,128)(2,1)S(1)} %get-tuple-element.19), channel_id=1, source_target_pairs={{0,4},{4,0},{8,12},{12,8},{1,5},{5,1},{9,13},{13,9},{2,6},{6,2},{1... | collective-permute-start | bytes 786440 | tf_op jit(solution)/shard_map/ppermute | solution.py:256
  9.9 0.0 collective-permute-done.2.refs_1_
  9.9 3.8 %collective-permute-done.3.refs_2_ = bf16[128,256]{1,0:T(8,128)(2,1)S(1)} collective-permute-done((bf16[128,256]{1,0:T(8,128)(2,1)S(1)}, bf16[128,256]{1,0:T(8,128)(2,1)S(1)}, u32[]{:S(2)}, u32[]{:S(2)}) %collective-permute-start.3) | collective-permute-done | bytes 65568 | tf_op jit(solution)/shard_map/ppermute | solution.py:226
  13.7 2.1 %collective-permute-done.4.refs_3_ = bf16[128,256]{1,0:T(8,128)(2,1)S(1)} collective-permute-done((bf16[128,256]{1,0:T(8,128)(2,1)S(1)}, bf16[128,256]{1,0:T(8,128)(2,1)S(1)}, u32[]{:S(2)}, u32[]{:S(2)}) %collective-permute-start.4) | collective-permute-done | bytes 65568 | tf_op jit(solution)/shard_map/ppermute | solution.py:226
  15.8 0.0 copy-done.4
  15.8 0.0 copy-done.3
  15.8 0.6 %codes.1.refs_2_.refs_1_ = bf16[2,64,256]{2,1,0:T(8,128)(2,1)S(1)} custom-call(s32[2,8]{1,0:T(2,128)S(1)} %copy-done.4, f32[4,128]{1,0:T(4,128)S(1)} %bitcast.2, bf16[128,256]{1,0:T(8,128)(2,1)S(1)} %get-tuple-element.20.refs_0_, bf16[128,256]{1,0:T(8,128)(2,1)S(1)} %collective-permute-done.2.refs_1_, bf16[128,256]{1,0:T(8,128)(2,1)S(1)} %collective-permute-done.3.refs_2_, ...), custom_call_target="tpu_custom_call" | custom-call | tf_op jit(solution)/shard_map/codes/pallas_call | solution.py:227
  16.5 0.1 collective-permute-start.5
  16.5 1.2 %collective-permute-done.5.refs_3_.refs_1_.refs_2_ = bf16[2,64,256]{2,1,0:T(8,128)(2,1)S(1)} collective-permute-done((bf16[2,64,256]{2,1,0:T(8,128)(2,1)S(1)}, bf16[2,64,256]{2,1,0:T(8,128)(2,1)S(1)}, u32[]{:S(2)}, u32[]{:S(2)}) %collective-permute-start.5) | collective-permute-done | bytes 65568 | tf_op jit(solution)/shard_map/ppermute | solution.py:242
  17.8 0.0 collective-permute-start.11
  17.8 0.8 %collective-permute-done.refs_0_ = bf16[1,2,128,512]{3,2,1,0:T(8,128)(2,1)S(1)} collective-permute-done((bf16[1,2,128,512]{3,2,1,0:T(8,128)(2,1)S(1)}, bf16[1,2,128,512]{3,2,1,0:T(8,128)(2,1)S(1)}, u32[]{:S(2)}, u32[]{:S(2)}) %collective-permute-start) | collective-permute-done | bytes 262176 | tf_op jit(solution)/shard_map/ppermute | solution.py:256
  18.6 1.5 %collective-permute-start.1 = (bf16[1,2,128,512]{3,2,1,0:T(8,128)(2,1)S(1)}, bf16[1,2,128,512]{3,2,1,0:T(8,128)(2,1)S(1)}, u32[]{:S(2)}, u32[]{:S(2)}) collective-permute-start(bf16[1,2,128,512]{3,2,1,0:T(8,128)(2,1)S(1)} %collective-permute-done.refs_0_), channel_id=1, source_target_pairs={{0,16},{16,0},{1,17},{17,1},{2,18},{18,2},{3,19},{19,3},{4,20},{20... | collective-permute-start | bytes 786440 | tf_op jit(solution)/shard_map/ppermute | solution.py:257
  20.1 0.2 collective-permute-start.7
  20.3 1.3 %collective-permute-start.6 = (bf16[2,64,256]{2,1,0:T(8,128)(2,1)S(1)}, bf16[2,64,256]{2,1,0:T(8,128)(2,1)S(1)}, u32[]{:S(2)}, u32[]{:S(2)}) collective-permute-start(bf16[2,64,256]{2,1,0:T(8,128)(2,1)S(1)} %codes.1.refs_2_.refs_1_), channel_id=1, source_target_pairs={{0,2},{1,3},{2,0},{3,1},{4,6},{5,7},{6,4},{7,5},{8,10},{9,11},{10,... | collective-permute-start | bytes 196616 | tf_op jit(solution)/shard_map/ppermute | solution.py:242
  21.6 2.8 %collective-permute-done.7.refs_5_.refs_4_ = bf16[2,64,256]{2,1,0:T(8,128)(2,1)S(1)} collective-permute-done((bf16[2,64,256]{2,1,0:T(8,128)(2,1)S(1)}, bf16[2,64,256]{2,1,0:T(8,128)(2,1)S(1)}, u32[]{:S(2)}, u32[]{:S(2)}) %collective-permute-start.7) | collective-permute-done | bytes 65568 | tf_op jit(solution)/shard_map/ppermute | solution.py:242
  24.4 1.5 %collective-permute-done.6.refs_4_.refs_3_ = bf16[2,64,256]{2,1,0:T(8,128)(2,1)S(1)} collective-permute-done((bf16[2,64,256]{2,1,0:T(8,128)(2,1)S(1)}, bf16[2,64,256]{2,1,0:T(8,128)(2,1)S(1)}, u32[]{:S(2)}, u32[]{:S(2)}) %collective-permute-start.6) | collective-permute-done | bytes 65568 | tf_op jit(solution)/shard_map/ppermute | solution.py:242
  25.9 0.3 collective-permute-done.1.refs_1_
  26.2 0.0 copy-done
  26.2 0.5 decode.2
  26.6 0.0 copy-start.1
  26.6 0.0 copy-start.2
  26.6 1.7 %collective-permute-start.8 = (bf16[2,64,512]{2,1,0:T(8,128)(2,1)S(1)}, bf16[2,64,512]{2,1,0:T(8,128)(2,1)S(1)}, u32[]{:S(2)}, u32[]{:S(2)}) collective-permute-start(bf16[2,64,512]{2,1,0:T(8,128)(2,1)S(1)} %get-tuple-element.25), channel_id=1, source_target_pairs={{0,8},{1,9},{4,12},{5,13},{8,0},{9,1},{12,4},{13,5},{2,10},{3,11},... | collective-permute-start | bytes 393224 | tf_op jit(solution)/shard_map/ppermute | solution.py:305
  28.4 0.0 collective-permute-start.9
  28.4 1.4 %collective-permute-start.10 = (bf16[2,64,512]{2,1,0:T(8,128)(2,1)S(1)}, bf16[2,64,512]{2,1,0:T(8,128)(2,1)S(1)}, u32[]{:S(2)}, u32[]{:S(2)}) collective-permute-start(bf16[2,64,512]{2,1,0:T(8,128)(2,1)S(1)} %get-tuple-element.27), channel_id=1, source_target_pairs={{0,9},{1,8},{4,13},{5,12},{8,1},{9,0},{12,5},{13,4},{2,11},{3,10},... | collective-permute-start | bytes 393224 | tf_op jit(solution)/shard_map/ppermute | solution.py:305
  29.8 4.1 %collective-permute-done.11.refs_0_ = bf16[2,2,128,512]{3,2,1,0:T(8,128)(2,1)S(1)} collective-permute-done((bf16[2,2,128,512]{3,2,1,0:T(8,128)(2,1)S(1)}, bf16[2,2,128,512]{3,2,1,0:T(8,128)(2,1)S(1)}, u32[]{:S(2)}, u32[]{:S(2)}) %collective-permute-start.11) | collective-permute-done | bytes 524320 | tf_op jit(solution)/shard_map/ppermute | solution.py:259
  33.8 0.5 decode.3
  34.3 0.1 collective-permute-start.12
  34.4 0.1 collective-permute-start.13
  34.5 8.0 %collective-permute-done.8.refs_1_ = bf16[2,64,512]{2,1,0:T(8,128)(2,1)S(1)} collective-permute-done((bf16[2,64,512]{2,1,0:T(8,128)(2,1)S(1)}, bf16[2,64,512]{2,1,0:T(8,128)(2,1)S(1)}, u32[]{:S(2)}, u32[]{:S(2)}) %collective-permute-start.8) | collective-permute-done | bytes 131104 | tf_op jit(solution)/shard_map/ppermute | solution.py:305
  42.4 0.0 collective-permute-start.14
  42.4 0.0 collective-permute-done.9.refs_2_
  42.4 0.5 %collective-permute-done.10.refs_3_ = bf16[2,64,512]{2,1,0:T(8,128)(2,1)S(1)} collective-permute-done((bf16[2,64,512]{2,1,0:T(8,128)(2,1)S(1)}, bf16[2,64,512]{2,1,0:T(8,128)(2,1)S(1)}, u32[]{:S(2)}, u32[]{:S(2)}) %collective-permute-start.10) | collective-permute-done | bytes 131104 | tf_op jit(solution)/shard_map/ppermute | solution.py:305
  43.0 7.9 %collective-permute-done.12.refs_5_ = bf16[2,64,512]{2,1,0:T(8,128)(2,1)S(1)} collective-permute-done((bf16[2,64,512]{2,1,0:T(8,128)(2,1)S(1)}, bf16[2,64,512]{2,1,0:T(8,128)(2,1)S(1)}, u32[]{:S(2)}, u32[]{:S(2)}) %collective-permute-start.12) | collective-permute-done | bytes 131104 | tf_op jit(solution)/shard_map/ppermute | solution.py:305
  50.9 0.0 collective-permute-done.13.refs_6_
  50.9 0.6 %collective-permute-done.14.refs_7_ = bf16[2,64,512]{2,1,0:T(8,128)(2,1)S(1)} collective-permute-done((bf16[2,64,512]{2,1,0:T(8,128)(2,1)S(1)}, bf16[2,64,512]{2,1,0:T(8,128)(2,1)S(1)}, u32[]{:S(2)}, u32[]{:S(2)}) %collective-permute-start.14) | collective-permute-done | bytes 131104 | tf_op jit(solution)/shard_map/ppermute | solution.py:305
  51.4 0.0 copy-done.1
  51.4 0.0 copy-done.2
  51.4 0.9 %add.1 = bf16[2,64,2048]{2,1,0:T(8,128)(2,1)} custom-call(f32[2,2048]{1,0:T(2,128)S(1)} %copy-done.2, bf16[2,64,2048]{2,1,0:T(8,128)(2,1)S(1)} %copy-done.1, f32[2,64,512]{2,1,0:T(8,128)S(1)} %get-tuple-element.24.refs_5_.refs_0_, bf16[2,64,512]{2,1,0:T(8,128)(2,1)S(1)} %collective-permute-done.8.refs_1_, ...), custom_call_target="tpu_custom_call" | custom-call | tf_op jit(solution)/shard_map/add/pallas_call | solution.py:262
  (1 shorter events, 0.0 us)
Async XLA Ops:
  0.0 15.8 %copy-start.4 = (s32[2,8]{1,0:T(2,128)S(1)}, s32[2,8]{1,0:T(2,128)}, u32[]{:S(2)}) copy-start(s32[2,8]{1,0:T(2,128)} %active_ref.1) | copy-start | bytes 196
  0.0 15.8 %copy-start.3 = (f32[512]{0:T(512)S(1)}, f32[512]{0:T(512)}, u32[]{:S(2)}) copy-start(f32[512]{0:T(512)} %param.9) | copy-start | bytes 6148
  0.0 26.1 %copy-start = (bf16[2,2,128,2048]{3,2,1,0:T(8,128)(2,1)S(1)}, bf16[2,2,128,2048]{3,2,1,0:T(8,128)(2,1)}, u32[]{:S(2)}) copy-start(bf16[2,2,128,2048]{3,2,1,0:T(8,128)(2,1)} %dec_ref.3) | copy-start | bytes 6291460
  3.3 6.6 %collective-permute-start.2 = (bf16[128,256]{1,0:T(8,128)(2,1)S(1)}, bf16[128,256]{1,0:T(8,128)(2,1)S(1)}, u32[]{:S(2)}, u32[]{:S(2)}) collective-permute-start(bf16[128,256]{1,0:T(8,128)(2,1)S(1)} %get-tuple-element.21), channel_id=1, source_target_pairs={{0,4},{4,0},{8,12},{12,8},{1,5},{5,1},{9,13},{13,9},{2,6},{6,2},{1... | collective-permute-start | bytes 196616 | tf_op jit(solution)/shard_map/ppermute | solution.py:226
  6.4 7.3 %collective-permute-start.3 = (bf16[128,256]{1,0:T(8,128)(2,1)S(1)}, bf16[128,256]{1,0:T(8,128)(2,1)S(1)}, u32[]{:S(2)}, u32[]{:S(2)}) collective-permute-start(bf16[128,256]{1,0:T(8,128)(2,1)S(1)} %get-tuple-element.22), channel_id=1, source_target_pairs={{0,8},{4,12},{8,0},{12,4},{1,9},{5,13},{9,1},{13,5},{2,10},{6,14},... | collective-permute-start | bytes 196616 | tf_op jit(solution)/shard_map/ppermute | solution.py:226
  9.0 6.8 %collective-permute-start.4 = (bf16[128,256]{1,0:T(8,128)(2,1)S(1)}, bf16[128,256]{1,0:T(8,128)(2,1)S(1)}, u32[]{:S(2)}, u32[]{:S(2)}) collective-permute-start(bf16[128,256]{1,0:T(8,128)(2,1)S(1)} %get-tuple-element.23), channel_id=1, source_target_pairs={{0,12},{4,8},{8,4},{12,0},{1,13},{5,9},{9,5},{13,1},{2,14},{6,10},... | collective-permute-start | bytes 196616 | tf_op jit(solution)/shard_map/ppermute | solution.py:226
  9.0 9.6 %collective-permute-start = (bf16[1,2,128,512]{3,2,1,0:T(8,128)(2,1)S(1)}, bf16[1,2,128,512]{3,2,1,0:T(8,128)(2,1)S(1)}, u32[]{:S(2)}, u32[]{:S(2)}) collective-permute-start(bf16[1,2,128,512]{3,2,1,0:T(8,128)(2,1)S(1)} %get-tuple-element.19), channel_id=1, source_target_pairs={{0,4},{4,0},{8,12},{12,8},{1,5},{5,1},{9,13},{13,9},{2,6},{6,2},{1... | collective-permute-start | bytes 786440 | tf_op jit(solution)/shard_map/ppermute | solution.py:256
  16.5 1.3 %collective-permute-start.5 = (bf16[2,64,256]{2,1,0:T(8,128)(2,1)S(1)}, bf16[2,64,256]{2,1,0:T(8,128)(2,1)S(1)}, u32[]{:S(2)}, u32[]{:S(2)}) collective-permute-start(bf16[2,64,256]{2,1,0:T(8,128)(2,1)S(1)} %codes.1.refs_2_.refs_1_), channel_id=1, source_target_pairs={{0,1},{1,0},{2,3},{3,2},{4,5},{5,4},{6,7},{7,6},{8,9},{9,8},{10,11... | collective-permute-start | bytes 196616 | tf_op jit(solution)/shard_map/ppermute | solution.py:242
  17.8 16.0 %collective-permute-start.11 = (bf16[2,2,128,512]{3,2,1,0:T(8,128)(2,1)S(1)}, bf16[2,2,128,512]{3,2,1,0:T(8,128)(2,1)S(1)}, u32[]{:S(2)}, u32[]{:S(2)}) collective-permute-start(bf16[2,2,128,512]{3,2,1,0:T(8,128)(2,1)S(1)} %hold.1), channel_id=1, source_target_pairs={{0,4},{4,0},{8,12},{12,8},{1,5},{5,1},{9,13},{13,9},{2,6},{6,2},{1... | collective-permute-start | bytes 1572872 | tf_op jit(solution)/shard_map/ppermute | solution.py:259
  18.6 7.6 %collective-permute-start.1 = (bf16[1,2,128,512]{3,2,1,0:T(8,128)(2,1)S(1)}, bf16[1,2,128,512]{3,2,1,0:T(8,128)(2,1)S(1)}, u32[]{:S(2)}, u32[]{:S(2)}) collective-permute-start(bf16[1,2,128,512]{3,2,1,0:T(8,128)(2,1)S(1)} %collective-permute-done.refs_0_), channel_id=1, source_target_pairs={{0,16},{16,0},{1,17},{17,1},{2,18},{18,2},{3,19},{19,3},{4,20},{20... | collective-permute-start | bytes 786440 | tf_op jit(solution)/shard_map/ppermute | solution.py:257
  20.1 4.3 %collective-permute-start.7 = (bf16[2,64,256]{2,1,0:T(8,128)(2,1)S(1)}, bf16[2,64,256]{2,1,0:T(8,128)(2,1)S(1)}, u32[]{:S(2)}, u32[]{:S(2)}) collective-permute-start(bf16[2,64,256]{2,1,0:T(8,128)(2,1)S(1)} %codes.1.refs_2_.refs_1_), channel_id=1, source_target_pairs={{0,3},{1,2},{2,1},{3,0},{4,7},{5,6},{6,5},{7,4},{8,11},{9,10},{10,... | collective-permute-start | bytes 196616 | tf_op jit(solution)/shard_map/ppermute | solution.py:242
  20.3 5.6 %collective-permute-start.6 = (bf16[2,64,256]{2,1,0:T(8,128)(2,1)S(1)}, bf16[2,64,256]{2,1,0:T(8,128)(2,1)S(1)}, u32[]{:S(2)}, u32[]{:S(2)}) collective-permute-start(bf16[2,64,256]{2,1,0:T(8,128)(2,1)S(1)} %codes.1.refs_2_.refs_1_), channel_id=1, source_target_pairs={{0,2},{1,3},{2,0},{3,1},{4,6},{5,7},{6,4},{7,5},{8,10},{9,11},{10,... | collective-permute-start | bytes 196616 | tf_op jit(solution)/shard_map/ppermute | solution.py:242
  26.6 24.8 %copy-start.1 = (bf16[2,64,2048]{2,1,0:T(8,128)(2,1)S(1)}, bf16[2,64,2048]{2,1,0:T(8,128)(2,1)}, u32[]{:S(2)}) copy-start(bf16[2,64,2048]{2,1,0:T(8,128)(2,1)} %target_ref.1) | copy-start | bytes 1572868
  26.6 24.8 %copy-start.2 = (f32[2,2048]{1,0:T(2,128)S(1)}, f32[2,2048]{1,0:T(2,128)}, u32[]{:S(2)}) copy-start(f32[2,2048]{1,0:T(2,128)} %bias_ref.1) | copy-start | bytes 49156
  26.6 15.8 %collective-permute-start.8 = (bf16[2,64,512]{2,1,0:T(8,128)(2,1)S(1)}, bf16[2,64,512]{2,1,0:T(8,128)(2,1)S(1)}, u32[]{:S(2)}, u32[]{:S(2)}) collective-permute-start(bf16[2,64,512]{2,1,0:T(8,128)(2,1)S(1)} %get-tuple-element.25), channel_id=1, source_target_pairs={{0,8},{1,9},{4,12},{5,13},{8,0},{9,1},{12,4},{13,5},{2,10},{3,11},... | collective-permute-start | bytes 393224 | tf_op jit(solution)/shard_map/ppermute | solution.py:305
  28.4 14.1 %collective-permute-start.9 = (bf16[2,64,512]{2,1,0:T(8,128)(2,1)S(1)}, bf16[2,64,512]{2,1,0:T(8,128)(2,1)S(1)}, u32[]{:S(2)}, u32[]{:S(2)}) collective-permute-start(bf16[2,64,512]{2,1,0:T(8,128)(2,1)S(1)} %get-tuple-element.26), channel_id=1, source_target_pairs={{0,1},{1,0},{4,5},{5,4},{8,9},{9,8},{12,13},{13,12},{2,3},{3,2},{6... | collective-permute-start | bytes 393224 | tf_op jit(solution)/shard_map/ppermute | solution.py:305
  28.4 14.6 %collective-permute-start.10 = (bf16[2,64,512]{2,1,0:T(8,128)(2,1)S(1)}, bf16[2,64,512]{2,1,0:T(8,128)(2,1)S(1)}, u32[]{:S(2)}, u32[]{:S(2)}) collective-permute-start(bf16[2,64,512]{2,1,0:T(8,128)(2,1)S(1)} %get-tuple-element.27), channel_id=1, source_target_pairs={{0,9},{1,8},{4,13},{5,12},{8,1},{9,0},{12,5},{13,4},{2,11},{3,10},... | collective-permute-start | bytes 393224 | tf_op jit(solution)/shard_map/ppermute | solution.py:305
  34.3 16.6 %collective-permute-start.12 = (bf16[2,64,512]{2,1,0:T(8,128)(2,1)S(1)}, bf16[2,64,512]{2,1,0:T(8,128)(2,1)S(1)}, u32[]{:S(2)}, u32[]{:S(2)}) collective-permute-start(bf16[2,64,512]{2,1,0:T(8,128)(2,1)S(1)} %get-tuple-element.30), channel_id=1, source_target_pairs={{0,8},{1,9},{4,12},{5,13},{8,0},{9,1},{12,4},{13,5},{2,10},{3,11},... | collective-permute-start | bytes 393224 | tf_op jit(solution)/shard_map/ppermute | solution.py:305
  34.4 16.5 %collective-permute-start.13 = (bf16[2,64,512]{2,1,0:T(8,128)(2,1)S(1)}, bf16[2,64,512]{2,1,0:T(8,128)(2,1)S(1)}, u32[]{:S(2)}, u32[]{:S(2)}) collective-permute-start(bf16[2,64,512]{2,1,0:T(8,128)(2,1)S(1)} %get-tuple-element.31), channel_id=1, source_target_pairs={{0,1},{1,0},{4,5},{5,4},{8,9},{9,8},{12,13},{13,12},{2,3},{3,2},{6... | collective-permute-start | bytes 393224 | tf_op jit(solution)/shard_map/ppermute | solution.py:305
  42.4 9.0 %collective-permute-start.14 = (bf16[2,64,512]{2,1,0:T(8,128)(2,1)S(1)}, bf16[2,64,512]{2,1,0:T(8,128)(2,1)S(1)}, u32[]{:S(2)}, u32[]{:S(2)}) collective-permute-start(bf16[2,64,512]{2,1,0:T(8,128)(2,1)S(1)} %get-tuple-element.32), channel_id=1, source_target_pairs={{0,9},{1,8},{4,13},{5,12},{8,1},{9,0},{12,5},{13,4},{2,11},{3,10},... | collective-permute-start | bytes 393224 | tf_op jit(solution)/shard_map/ppermute | solution.py:305

commit v11 on v10

--- a/solution.py
+++ b/solution.py
@@ -232,7 +232,7 @@
         compiler_params=params,
         cost_estimate=cost,
         name="codes",
-    )(active, enc_b.reshape(n, block), *terms)
+    )(active, enc_b.reshape(n, block), terms[0], *reversed(terms[1:]))
     codes = []
     for k in range(groups):
         for r in range(2):

time: 53 us -> 53.8 us (1.015)
  starting transfers between devices: 13 us -> 17.1 us
  waiting for transfers between devices: 33.5 us -> 30.4 us
    ppermute x1, waiting for transfers between devices: 4.05 us -> 0.21 us  [body(): got.append([lax.ppermute(hold(parts[1], codes[1]), 'src', pair)])]
    ppermute x6, waiting for transfers between devices: 17 us -> 19.5 us  [body(): sums[i].append(lax.ppermute(term, ('src', 'rep'), perm) if j + r else term)]
    ppermute x6, starting transfers between devices: 3.25 us -> 5.03 us  [body(): sums[i].append(lax.ppermute(term, ('src', 'rep'), perm) if j + r else term)]
    ppermute x3, waiting for transfers between devices: 5.91 us -> 4.14 us  [body(): lax.ppermute(terms[k], 'src', [(i, peer(i, k, n)) for i in range(n)])]
    ppermute x1, starting transfers between devices: 0.01 us -> 1.62 us  [body(): got.append([lax.ppermute(hold(parts[1], codes[1]), 'src', pair)])]
where the time goes in v11:
time: 53.8 us; the launch traced here: 53.4 us
  waiting for transfers between devices  30.4 us (57%)
  starting transfers between devices  17.1 us (32%)
  Pallas kernels  5.78 us (11%)
    ppermute x6, waiting for transfers between devices, body(): sums[i].append(lax.ppermute(term, ('src', 'rep'), perm) if j + r else term)  19.5 us
    ppermute x3, starting transfers between devices, body(): lax.ppermute(terms[k], 'src', [(i, peer(i, k, n)) for i in range(n)])  5.75 us
    ppermute x3, waiting for transfers between devices, body(): codes.append(lax.ppermute(own, ('tgt', 'rep'), perm) if k + r else own)  5.52 us
    ppermute x6, starting transfers between devices, body(): sums[i].append(lax.ppermute(term, ('src', 'rep'), perm) if j + r else term)  5.03 us
    ppermute x3, waiting for transfers between devices, body(): lax.ppermute(terms[k], 'src', [(i, peer(i, k, n)) for i in range(n)])  4.14 us
    pallas_call x1, Pallas kernels, body(): pl.pallas_call(functools.partial(encode_kernel, n, pieces), out_shape=[sh...  3.3 us
    ppermute x1, starting transfers between devices, body(): got[0].append(lax.ppermute(got[0][0], 'parts', [(0, 1), (1, 0)]))  1.72 us
    ppermute x1, starting transfers between devices, body(): got.append([lax.ppermute(hold(parts[1], codes[1]), 'src', pair)])  1.62 us
  transfers between devices with their start and end apart: 15, of which 12 were waited for; matrix products, arithmetic and copies ran while one was open for 0% of the time, Pallas kernels for 3%

profile of v11, /device:TPU:0, one launch (start us, length us, event | category | flops | bytes accessed | tf_op | source)
XLA Modules:
  0.0 53.4 jit_solution(13947165003197414994)
XLA Ops:
  0.0 0.0 copy-start.4
  0.0 0.0 copy-start.3
  0.0 0.0 copy-start
  0.0 3.3 %encode.1 = (bf16[128,256]{1,0:T(8,128)(2,1)S(1)}, bf16[128,256]{1,0:T(8,128)(2,1)S(1)}, bf16[128,256]{1,0:T(8,128)(2,1)S(1)}, bf16[128,256]{1,0:T(8,128)(2,1)S(...) custom-call(bf16[2,2,64,1024]{3,2,1,0:T(8,128)(2,1)} %bitcast.3, bf16[1024,512]{1,0:T(8,128)(2,1)} %w_hbm.1, ...), custom_call_target="tpu_custom_call" | custom-call | tf_op jit(solution)/shard_map/encode/pallas_call | solution.py:204
  3.3 5.1 %collective-permute-start.2 = (bf16[128,256]{1,0:T(8,128)(2,1)S(1)}, bf16[128,256]{1,0:T(8,128)(2,1)S(1)}, u32[]{:S(2)}, u32[]{:S(2)}) collective-permute-start(bf16[128,256]{1,0:T(8,128)(2,1)S(1)} %get-tuple-element.21), channel_id=1, source_target_pairs={{0,12},{4,8},{8,4},{12,0},{1,13},{5,9},{9,5},{13,1},{2,14},{6,10},... | collective-permute-start | bytes 196616 | tf_op jit(solution)/shard_map/ppermute | solution.py:226
  8.4 0.0 collective-permute-start.3
  8.4 0.6 %collective-permute-start.4 = (bf16[128,256]{1,0:T(8,128)(2,1)S(1)}, bf16[128,256]{1,0:T(8,128)(2,1)S(1)}, u32[]{:S(2)}, u32[]{:S(2)}) collective-permute-start(bf16[128,256]{1,0:T(8,128)(2,1)S(1)} %get-tuple-element.23), channel_id=1, source_target_pairs={{0,4},{4,0},{8,12},{12,8},{1,5},{5,1},{9,13},{13,9},{2,6},{6,2},{1... | collective-permute-start | bytes 196616 | tf_op jit(solution)/shard_map/ppermute | solution.py:226
  9.1 1.4 %collective-permute-start = (bf16[1,2,128,512]{3,2,1,0:T(8,128)(2,1)S(1)}, bf16[1,2,128,512]{3,2,1,0:T(8,128)(2,1)S(1)}, u32[]{:S(2)}, u32[]{:S(2)}) collective-permute-start(bf16[1,2,128,512]{3,2,1,0:T(8,128)(2,1)S(1)} %get-tuple-element.19), channel_id=1, source_target_pairs={{0,4},{4,0},{8,12},{12,8},{1,5},{5,1},{9,13},{13,9},{2,6},{6,2},{1... | collective-permute-start | bytes 786440 | tf_op jit(solution)/shard_map/ppermute | solution.py:256
  10.4 0.6 %collective-permute-done.2.refs_1_ = bf16[128,256]{1,0:T(8,128)(2,1)S(1)} collective-permute-done((bf16[128,256]{1,0:T(8,128)(2,1)S(1)}, bf16[128,256]{1,0:T(8,128)(2,1)S(1)}, u32[]{:S(2)}, u32[]{:S(2)}) %collective-permute-start.2) | collective-permute-done | bytes 65568 | tf_op jit(solution)/shard_map/ppermute | solution.py:226
  11.0 3.1 %collective-permute-done.3.refs_2_ = bf16[128,256]{1,0:T(8,128)(2,1)S(1)} collective-permute-done((bf16[128,256]{1,0:T(8,128)(2,1)S(1)}, bf16[128,256]{1,0:T(8,128)(2,1)S(1)}, u32[]{:S(2)}, u32[]{:S(2)}) %collective-permute-start.3) | collective-permute-done | bytes 65568 | tf_op jit(solution)/shard_map/ppermute | solution.py:226
  14.1 0.5 collective-permute-done.4.refs_3_
  14.6 0.0 copy-done.4
  14.6 0.0 copy-done.3
  14.6 0.6 %codes.1.refs_2_.refs_1_ = bf16[2,64,256]{2,1,0:T(8,128)(2,1)S(1)} custom-call(s32[2,8]{1,0:T(2,128)S(1)} %copy-done.4, f32[4,128]{1,0:T(4,128)S(1)} %bitcast.2, bf16[128,256]{1,0:T(8,128)(2,1)S(1)} %get-tuple-element.20.refs_0_, bf16[128,256]{1,0:T(8,128)(2,1)S(1)} %collective-permute-done.2.refs_1_, bf16[128,256]{1,0:T(8,128)(2,1)S(1)} %collective-permute-done.3.refs_2_, ...), custom_call_target="tpu_custom_call" | custom-call | tf_op jit(solution)/shard_map/codes/pallas_call | solution.py:227
  15.2 0.1 collective-permute-start.5
  15.3 1.2 %collective-permute-done.5.refs_3_.refs_1_.refs_2_ = bf16[2,64,256]{2,1,0:T(8,128)(2,1)S(1)} collective-permute-done((bf16[2,64,256]{2,1,0:T(8,128)(2,1)S(1)}, bf16[2,64,256]{2,1,0:T(8,128)(2,1)S(1)}, u32[]{:S(2)}, u32[]{:S(2)}) %collective-permute-start.5) | collective-permute-done | bytes 65568 | tf_op jit(solution)/shard_map/ppermute | solution.py:242
  16.6 1.6 %collective-permute-start.11 = (bf16[2,2,128,512]{3,2,1,0:T(8,128)(2,1)S(1)}, bf16[2,2,128,512]{3,2,1,0:T(8,128)(2,1)S(1)}, u32[]{:S(2)}, u32[]{:S(2)}) collective-permute-start(bf16[2,2,128,512]{3,2,1,0:T(8,128)(2,1)S(1)} %hold.1), channel_id=1, source_target_pairs={{0,4},{4,0},{8,12},{12,8},{1,5},{5,1},{9,13},{13,9},{2,6},{6,2},{1... | collective-permute-start | bytes 1572872 | tf_op jit(solution)/shard_map/ppermute | solution.py:259
  18.2 1.0 %collective-permute-done.refs_0_ = bf16[1,2,128,512]{3,2,1,0:T(8,128)(2,1)S(1)} collective-permute-done((bf16[1,2,128,512]{3,2,1,0:T(8,128)(2,1)S(1)}, bf16[1,2,128,512]{3,2,1,0:T(8,128)(2,1)S(1)}, u32[]{:S(2)}, u32[]{:S(2)}) %collective-permute-start) | collective-permute-done | bytes 262176 | tf_op jit(solution)/shard_map/ppermute | solution.py:256
  19.2 1.7 %collective-permute-start.1 = (bf16[1,2,128,512]{3,2,1,0:T(8,128)(2,1)S(1)}, bf16[1,2,128,512]{3,2,1,0:T(8,128)(2,1)S(1)}, u32[]{:S(2)}, u32[]{:S(2)}) collective-permute-start(bf16[1,2,128,512]{3,2,1,0:T(8,128)(2,1)S(1)} %collective-permute-done.refs_0_), channel_id=1, source_target_pairs={{0,16},{16,0},{1,17},{17,1},{2,18},{18,2},{3,19},{19,3},{4,20},{20... | collective-permute-start | bytes 786440 | tf_op jit(solution)/shard_map/ppermute | solution.py:257
  20.9 0.0 collective-permute-start.7
  20.9 1.5 %collective-permute-start.6 = (bf16[2,64,256]{2,1,0:T(8,128)(2,1)S(1)}, bf16[2,64,256]{2,1,0:T(8,128)(2,1)S(1)}, u32[]{:S(2)}, u32[]{:S(2)}) collective-permute-start(bf16[2,64,256]{2,1,0:T(8,128)(2,1)S(1)} %codes.1.refs_2_.refs_1_), channel_id=1, source_target_pairs={{0,2},{1,3},{2,0},{3,1},{4,6},{5,7},{6,4},{7,5},{8,10},{9,11},{10,... | collective-permute-start | bytes 196616 | tf_op jit(solution)/shard_map/ppermute | solution.py:242
  22.4 2.8 %collective-permute-done.7.refs_5_.refs_4_ = bf16[2,64,256]{2,1,0:T(8,128)(2,1)S(1)} collective-permute-done((bf16[2,64,256]{2,1,0:T(8,128)(2,1)S(1)}, bf16[2,64,256]{2,1,0:T(8,128)(2,1)S(1)}, u32[]{:S(2)}, u32[]{:S(2)}) %collective-permute-start.7) | collective-permute-done | bytes 65568 | tf_op jit(solution)/shard_map/ppermute | solution.py:242
  25.3 1.4 %collective-permute-done.6.refs_4_.refs_3_ = bf16[2,64,256]{2,1,0:T(8,128)(2,1)S(1)} collective-permute-done((bf16[2,64,256]{2,1,0:T(8,128)(2,1)S(1)}, bf16[2,64,256]{2,1,0:T(8,128)(2,1)S(1)}, u32[]{:S(2)}, u32[]{:S(2)}) %collective-permute-start.6) | collective-permute-done | bytes 65568 | tf_op jit(solution)/shard_map/ppermute | solution.py:242
  26.7 0.0 collective-permute-done.1.refs_1_
  26.7 0.0 copy-done
  26.7 0.5 decode.2
  27.2 0.0 copy-start.1
  27.2 0.0 copy-start.2
  27.2 1.1 %collective-permute-start.8 = (bf16[2,64,512]{2,1,0:T(8,128)(2,1)S(1)}, bf16[2,64,512]{2,1,0:T(8,128)(2,1)S(1)}, u32[]{:S(2)}, u32[]{:S(2)}) collective-permute-start(bf16[2,64,512]{2,1,0:T(8,128)(2,1)S(1)} %get-tuple-element.25), channel_id=1, source_target_pairs={{0,8},{1,9},{4,12},{5,13},{8,0},{9,1},{12,4},{13,5},{2,10},{3,11},... | collective-permute-start | bytes 393224 | tf_op jit(solution)/shard_map/ppermute | solution.py:305
  28.4 0.0 collective-permute-start.9
  28.4 2.0 %collective-permute-start.10 = (bf16[2,64,512]{2,1,0:T(8,128)(2,1)S(1)}, bf16[2,64,512]{2,1,0:T(8,128)(2,1)S(1)}, u32[]{:S(2)}, u32[]{:S(2)}) collective-permute-start(bf16[2,64,512]{2,1,0:T(8,128)(2,1)S(1)} %get-tuple-element.27), channel_id=1, source_target_pairs={{0,9},{1,8},{4,13},{5,12},{8,1},{9,0},{12,5},{13,4},{2,11},{3,10},... | collective-permute-start | bytes 393224 | tf_op jit(solution)/shard_map/ppermute | solution.py:305
  30.3 0.2 collective-permute-done.11.refs_0_
  30.5 0.5 decode.3
  31.0 1.9 %collective-permute-start.12 = (bf16[2,64,512]{2,1,0:T(8,128)(2,1)S(1)}, bf16[2,64,512]{2,1,0:T(8,128)(2,1)S(1)}, u32[]{:S(2)}, u32[]{:S(2)}) collective-permute-start(bf16[2,64,512]{2,1,0:T(8,128)(2,1)S(1)} %get-tuple-element.30), channel_id=1, source_target_pairs={{0,8},{1,9},{4,12},{5,13},{8,0},{9,1},{12,4},{13,5},{2,10},{3,11},... | collective-permute-start | bytes 393224 | tf_op jit(solution)/shard_map/ppermute | solution.py:305
  32.9 0.0 collective-permute-start.13
  33.0 10.0 %collective-permute-done.8.refs_1_ = bf16[2,64,512]{2,1,0:T(8,128)(2,1)S(1)} collective-permute-done((bf16[2,64,512]{2,1,0:T(8,128)(2,1)S(1)}, bf16[2,64,512]{2,1,0:T(8,128)(2,1)S(1)}, u32[]{:S(2)}, u32[]{:S(2)}) %collective-permute-start.8) | collective-permute-done | bytes 131104 | tf_op jit(solution)/shard_map/ppermute | solution.py:305
  42.9 0.0 collective-permute-start.14
  42.9 0.0 collective-permute-done.9.refs_2_
  42.9 1.1 %collective-permute-done.10.refs_3_ = bf16[2,64,512]{2,1,0:T(8,128)(2,1)S(1)} collective-permute-done((bf16[2,64,512]{2,1,0:T(8,128)(2,1)S(1)}, bf16[2,64,512]{2,1,0:T(8,128)(2,1)S(1)}, u32[]{:S(2)}, u32[]{:S(2)}) %collective-permute-start.10) | collective-permute-done | bytes 131104 | tf_op jit(solution)/shard_map/ppermute | solution.py:305
  44.1 7.3 %collective-permute-done.12.refs_5_ = bf16[2,64,512]{2,1,0:T(8,128)(2,1)S(1)} collective-permute-done((bf16[2,64,512]{2,1,0:T(8,128)(2,1)S(1)}, bf16[2,64,512]{2,1,0:T(8,128)(2,1)S(1)}, u32[]{:S(2)}, u32[]{:S(2)}) %collective-permute-start.12) | collective-permute-done | bytes 131104 | tf_op jit(solution)/shard_map/ppermute | solution.py:305
  51.4 0.0 collective-permute-done.13.refs_6_
  51.4 1.1 %collective-permute-done.14.refs_7_ = bf16[2,64,512]{2,1,0:T(8,128)(2,1)S(1)} collective-permute-done((bf16[2,64,512]{2,1,0:T(8,128)(2,1)S(1)}, bf16[2,64,512]{2,1,0:T(8,128)(2,1)S(1)}, u32[]{:S(2)}, u32[]{:S(2)}) %collective-permute-start.14) | collective-permute-done | bytes 131104 | tf_op jit(solution)/shard_map/ppermute | solution.py:305
  52.5 0.0 copy-done.1
  52.5 0.0 copy-done.2
  52.5 0.9 %add.1 = bf16[2,64,2048]{2,1,0:T(8,128)(2,1)} custom-call(f32[2,2048]{1,0:T(2,128)S(1)} %copy-done.2, bf16[2,64,2048]{2,1,0:T(8,128)(2,1)S(1)} %copy-done.1, f32[2,64,512]{2,1,0:T(8,128)S(1)} %get-tuple-element.24.refs_5_.refs_0_, bf16[2,64,512]{2,1,0:T(8,128)(2,1)S(1)} %collective-permute-done.8.refs_1_, ...), custom_call_target="tpu_custom_call" | custom-call | tf_op jit(solution)/shard_map/add/pallas_call | solution.py:262
  (1 shorter events, 0.0 us)
Async XLA Ops:
  0.0 14.6 %copy-start.4 = (s32[2,8]{1,0:T(2,128)S(1)}, s32[2,8]{1,0:T(2,128)}, u32[]{:S(2)}) copy-start(s32[2,8]{1,0:T(2,128)} %active_ref.1) | copy-start | bytes 196
  0.0 14.6 %copy-start.3 = (f32[512]{0:T(512)S(1)}, f32[512]{0:T(512)}, u32[]{:S(2)}) copy-start(f32[512]{0:T(512)} %param.9) | copy-start | bytes 6148
  0.0 26.7 %copy-start = (bf16[2,2,128,2048]{3,2,1,0:T(8,128)(2,1)S(1)}, bf16[2,2,128,2048]{3,2,1,0:T(8,128)(2,1)}, u32[]{:S(2)}) copy-start(bf16[2,2,128,2048]{3,2,1,0:T(8,128)(2,1)} %dec_ref.3) | copy-start | bytes 6291460
  3.3 7.7 %collective-permute-start.2 = (bf16[128,256]{1,0:T(8,128)(2,1)S(1)}, bf16[128,256]{1,0:T(8,128)(2,1)S(1)}, u32[]{:S(2)}, u32[]{:S(2)}) collective-permute-start(bf16[128,256]{1,0:T(8,128)(2,1)S(1)} %get-tuple-element.21), channel_id=1, source_target_pairs={{0,12},{4,8},{8,4},{12,0},{1,13},{5,9},{9,5},{13,1},{2,14},{6,10},... | collective-permute-start | bytes 196616 | tf_op jit(solution)/shard_map/ppermute | solution.py:226
  8.4 5.7 %collective-permute-start.3 = (bf16[128,256]{1,0:T(8,128)(2,1)S(1)}, bf16[128,256]{1,0:T(8,128)(2,1)S(1)}, u32[]{:S(2)}, u32[]{:S(2)}) collective-permute-start(bf16[128,256]{1,0:T(8,128)(2,1)S(1)} %get-tuple-element.22), channel_id=1, source_target_pairs={{0,8},{4,12},{8,0},{12,4},{1,9},{5,13},{9,1},{13,5},{2,10},{6,14},... | collective-permute-start | bytes 196616 | tf_op jit(solution)/shard_map/ppermute | solution.py:226
  8.4 6.2 %collective-permute-start.4 = (bf16[128,256]{1,0:T(8,128)(2,1)S(1)}, bf16[128,256]{1,0:T(8,128)(2,1)S(1)}, u32[]{:S(2)}, u32[]{:S(2)}) collective-permute-start(bf16[128,256]{1,0:T(8,128)(2,1)S(1)} %get-tuple-element.23), channel_id=1, source_target_pairs={{0,4},{4,0},{8,12},{12,8},{1,5},{5,1},{9,13},{13,9},{2,6},{6,2},{1... | collective-permute-start | bytes 196616 | tf_op jit(solution)/shard_map/ppermute | solution.py:226
  9.1 10.1 %collective-permute-start = (bf16[1,2,128,512]{3,2,1,0:T(8,128)(2,1)S(1)}, bf16[1,2,128,512]{3,2,1,0:T(8,128)(2,1)S(1)}, u32[]{:S(2)}, u32[]{:S(2)}) collective-permute-start(bf16[1,2,128,512]{3,2,1,0:T(8,128)(2,1)S(1)} %get-tuple-element.19), channel_id=1, source_target_pairs={{0,4},{4,0},{8,12},{12,8},{1,5},{5,1},{9,13},{13,9},{2,6},{6,2},{1... | collective-permute-start | bytes 786440 | tf_op jit(solution)/shard_map/ppermute | solution.py:256
  15.2 1.3 %collective-permute-start.5 = (bf16[2,64,256]{2,1,0:T(8,128)(2,1)S(1)}, bf16[2,64,256]{2,1,0:T(8,128)(2,1)S(1)}, u32[]{:S(2)}, u32[]{:S(2)}) collective-permute-start(bf16[2,64,256]{2,1,0:T(8,128)(2,1)S(1)} %codes.1.refs_2_.refs_1_), channel_id=1, source_target_pairs={{0,1},{1,0},{2,3},{3,2},{4,5},{5,4},{6,7},{7,6},{8,9},{9,8},{10,11... | collective-permute-start | bytes 196616 | tf_op jit(solution)/shard_map/ppermute | solution.py:242
  16.6 14.0 %collective-permute-start.11 = (bf16[2,2,128,512]{3,2,1,0:T(8,128)(2,1)S(1)}, bf16[2,2,128,512]{3,2,1,0:T(8,128)(2,1)S(1)}, u32[]{:S(2)}, u32[]{:S(2)}) collective-permute-start(bf16[2,2,128,512]{3,2,1,0:T(8,128)(2,1)S(1)} %hold.1), channel_id=1, source_target_pairs={{0,4},{4,0},{8,12},{12,8},{1,5},{5,1},{9,13},{13,9},{2,6},{6,2},{1... | collective-permute-start | bytes 1572872 | tf_op jit(solution)/shard_map/ppermute | solution.py:259
  19.2 7.5 %collective-permute-start.1 = (bf16[1,2,128,512]{3,2,1,0:T(8,128)(2,1)S(1)}, bf16[1,2,128,512]{3,2,1,0:T(8,128)(2,1)S(1)}, u32[]{:S(2)}, u32[]{:S(2)}) collective-permute-start(bf16[1,2,128,512]{3,2,1,0:T(8,128)(2,1)S(1)} %collective-permute-done.refs_0_), channel_id=1, source_target_pairs={{0,16},{16,0},{1,17},{17,1},{2,18},{18,2},{3,19},{19,3},{4,20},{20... | collective-permute-start | bytes 786440 | tf_op jit(solution)/shard_map/ppermute | solution.py:257
  20.9 4.4 %collective-permute-start.7 = (bf16[2,64,256]{2,1,0:T(8,128)(2,1)S(1)}, bf16[2,64,256]{2,1,0:T(8,128)(2,1)S(1)}, u32[]{:S(2)}, u32[]{:S(2)}) collective-permute-start(bf16[2,64,256]{2,1,0:T(8,128)(2,1)S(1)} %codes.1.refs_2_.refs_1_), channel_id=1, source_target_pairs={{0,3},{1,2},{2,1},{3,0},{4,7},{5,6},{6,5},{7,4},{8,11},{9,10},{10,... | collective-permute-start | bytes 196616 | tf_op jit(solution)/shard_map/ppermute | solution.py:242
  20.9 5.8 %collective-permute-start.6 = (bf16[2,64,256]{2,1,0:T(8,128)(2,1)S(1)}, bf16[2,64,256]{2,1,0:T(8,128)(2,1)S(1)}, u32[]{:S(2)}, u32[]{:S(2)}) collective-permute-start(bf16[2,64,256]{2,1,0:T(8,128)(2,1)S(1)} %codes.1.refs_2_.refs_1_), channel_id=1, source_target_pairs={{0,2},{1,3},{2,0},{3,1},{4,6},{5,7},{6,4},{7,5},{8,10},{9,11},{10,... | collective-permute-start | bytes 196616 | tf_op jit(solution)/shard_map/ppermute | solution.py:242
  27.2 25.3 %copy-start.1 = (bf16[2,64,2048]{2,1,0:T(8,128)(2,1)S(1)}, bf16[2,64,2048]{2,1,0:T(8,128)(2,1)}, u32[]{:S(2)}) copy-start(bf16[2,64,2048]{2,1,0:T(8,128)(2,1)} %target_ref.1) | copy-start | bytes 1572868
  27.2 25.3 %copy-start.2 = (f32[2,2048]{1,0:T(2,128)S(1)}, f32[2,2048]{1,0:T(2,128)}, u32[]{:S(2)}) copy-start(f32[2,2048]{1,0:T(2,128)} %bias_ref.1) | copy-start | bytes 49156
  27.2 15.7 %collective-permute-start.8 = (bf16[2,64,512]{2,1,0:T(8,128)(2,1)S(1)}, bf16[2,64,512]{2,1,0:T(8,128)(2,1)S(1)}, u32[]{:S(2)}, u32[]{:S(2)}) collective-permute-start(bf16[2,64,512]{2,1,0:T(8,128)(2,1)S(1)} %get-tuple-element.25), channel_id=1, source_target_pairs={{0,8},{1,9},{4,12},{5,13},{8,0},{9,1},{12,4},{13,5},{2,10},{3,11},... | collective-permute-start | bytes 393224 | tf_op jit(solution)/shard_map/ppermute | solution.py:305
  28.4 14.6 %collective-permute-start.9 = (bf16[2,64,512]{2,1,0:T(8,128)(2,1)S(1)}, bf16[2,64,512]{2,1,0:T(8,128)(2,1)S(1)}, u32[]{:S(2)}, u32[]{:S(2)}) collective-permute-start(bf16[2,64,512]{2,1,0:T(8,128)(2,1)S(1)} %get-tuple-element.26), channel_id=1, source_target_pairs={{0,1},{1,0},{4,5},{5,4},{8,9},{9,8},{12,13},{13,12},{2,3},{3,2},{6... | collective-permute-start | bytes 393224 | tf_op jit(solution)/shard_map/ppermute | solution.py:305
  28.4 15.7 %collective-permute-start.10 = (bf16[2,64,512]{2,1,0:T(8,128)(2,1)S(1)}, bf16[2,64,512]{2,1,0:T(8,128)(2,1)S(1)}, u32[]{:S(2)}, u32[]{:S(2)}) collective-permute-start(bf16[2,64,512]{2,1,0:T(8,128)(2,1)S(1)} %get-tuple-element.27), channel_id=1, source_target_pairs={{0,9},{1,8},{4,13},{5,12},{8,1},{9,0},{12,5},{13,4},{2,11},{3,10},... | collective-permute-start | bytes 393224 | tf_op jit(solution)/shard_map/ppermute | solution.py:305
  31.0 20.3 %collective-permute-start.12 = (bf16[2,64,512]{2,1,0:T(8,128)(2,1)S(1)}, bf16[2,64,512]{2,1,0:T(8,128)(2,1)S(1)}, u32[]{:S(2)}, u32[]{:S(2)}) collective-permute-start(bf16[2,64,512]{2,1,0:T(8,128)(2,1)S(1)} %get-tuple-element.30), channel_id=1, source_target_pairs={{0,8},{1,9},{4,12},{5,13},{8,0},{9,1},{12,4},{13,5},{2,10},{3,11},... | collective-permute-start | bytes 393224 | tf_op jit(solution)/shard_map/ppermute | solution.py:305
  32.9 18.4 %collective-permute-start.13 = (bf16[2,64,512]{2,1,0:T(8,128)(2,1)S(1)}, bf16[2,64,512]{2,1,0:T(8,128)(2,1)S(1)}, u32[]{:S(2)}, u32[]{:S(2)}) collective-permute-start(bf16[2,64,512]{2,1,0:T(8,128)(2,1)S(1)} %get-tuple-element.31), channel_id=1, source_target_pairs={{0,1},{1,0},{4,5},{5,4},{8,9},{9,8},{12,13},{13,12},{2,3},{3,2},{6... | collective-permute-start | bytes 393224 | tf_op jit(solution)/shard_map/ppermute | solution.py:305
  42.9 9.6 %collective-permute-start.14 = (bf16[2,64,512]{2,1,0:T(8,128)(2,1)S(1)}, bf16[2,64,512]{2,1,0:T(8,128)(2,1)S(1)}, u32[]{:S(2)}, u32[]{:S(2)}) collective-permute-start(bf16[2,64,512]{2,1,0:T(8,128)(2,1)S(1)} %get-tuple-element.32), channel_id=1, source_target_pairs={{0,9},{1,8},{4,13},{5,12},{8,1},{9,0},{12,5},{13,4},{2,11},{3,10},... | collective-permute-start | bytes 393224 | tf_op jit(solution)/shard_map/ppermute | solution.py:305

commit v12 on v9

v12 whole, which is shorter than its diff:
```python
import functools

import jax
import jax.numpy as jnp
from jax import lax
from jax.experimental import pallas as pl
from jax.experimental.pallas import tpu as pltpu
from jax.sharding import PartitionSpec as P

VMEM_BYTES = 32 * 1024 * 1024
LANES = 128
PIECES = ((0, 0, False), (0, 1, False), (1, 0, True), (1, 1, False))


def cut_pieces(columns):
    tiles = columns // LANES
    middle = -(-tiles // 2) * LANES
    bounds = ((0, middle), (middle, columns))
    return [
        (offset, bounds[side][0], bounds[side][1] - bounds[side][0], across)
        for offset, side, across in PIECES
    ]


def layer_of(piece, layers):
    return lax.rem(lax.axis_index("parts") + piece[0], layers)


def peer(index, k, n):
    return index ^ k if n & (n - 1) == 0 else (index + k) % n


def part_copies(piece, dec_hbm, part_ref, sems):
    layers, groups, _, cols = dec_hbm.shape
    start = pl.multiple_of(lax.axis_index("rep") * (cols // 2) + piece[1], LANES)
    layer = layer_of(piece, layers)
    copies = []
    for group in range(groups):
        source = dec_hbm.at[layer, group, :, pl.ds(start, piece[2])]
        copies.append(pltpu.make_async_copy(source, part_ref.at[group], sems.at[group]))
        copies[-1].start()
    return copies


def encode_kernel(n, pieces, acts_hbm, w_hbm, dec_hbm, *refs):
    term_refs, part_refs, refs = refs[:n], refs[n:-5], refs[-5:]
    acts_ref, w_ref, part_sems, acts_sems, w_sems = refs
    half = n // 2
    width = w_ref.shape[1] // half
    depth = w_ref.shape[0] // 8
    copies = []
    for i in range(2):
        for j in range(half):
            copies.append(
                pltpu.make_async_copy(
                    acts_hbm.at[j, i], acts_ref.at[i, j], acts_sems.at[i * half + j]
                )
            )
    for i in range(8):
        rows = slice(i * depth, (i + 1) * depth)
        copies.append(pltpu.make_async_copy(w_hbm.at[rows], w_ref.at[rows], w_sems.at[i]))
    for copy in copies:
        copy.start()
    for copy in copies:
        copy.wait()
    copies_part = []
    for i, ref in enumerate(part_refs):
        copies_part += part_copies(pieces[i], dec_hbm, ref, part_sems.at[i])
    src = lax.axis_index("src")
    for k in range(n):
        dest = peer(src, k, n)
        rows = acts_ref[lax.rem(dest, 2)]
        rows = rows.reshape(rows.shape[0] * rows.shape[1], rows.shape[2])
        columns = pl.ds(pl.multiple_of((dest // 2) * width, width), width)
        term_refs[k][...] = jnp.dot(
            rows, w_ref[:, columns], preferred_element_type=jnp.float32
        ).astype(jnp.bfloat16)
    for copy in copies_part:
        copy.wait()


def codes_kernel(n, share, tile_rows, active_ref, bias_ref, *refs):
    term_refs, out_ref = refs[:n], refs[n]
    src = lax.axis_index("src")
    tgt = lax.axis_index("tgt")
    parity, half = lax.rem(src, 2), src // 2
    block = out_ref.shape[2] // 2
    pre = term_refs[0][...].astype(jnp.float32)
    for ref in term_refs[1:]:
        pre = pre + ref[...].astype(jnp.float32)
    tiles, slots = active_ref.shape
    for piece in range(2):
        columns = slice(piece * block, (piece + 1) * block)
        bias = bias_ref[pl.ds(half * 2 + piece, 1), :]
        wanted = tgt * n + half * 2 + piece
        flags = []
        for tile in range(tiles):
            flags.append(
                lax.fori_loop(
                    0,
                    slots,
                    lambda i, total: total + (active_ref[tile, i] == wanted).astype(jnp.int32),
                    jnp.int32(0),
                    unroll=slots <= 16,
                )
            )
        for group in range(n // 2):
            tile = ((group * 2 + parity) * share) // tile_rows
            flag = flags[0]
            for i in range(1, tiles):
                flag = jnp.where(tile == i, flags[i], flag)
            live = jnp.where(flag > 0, 1.0, 0.0).astype(jnp.float32)
            rows = slice(group * share, (group + 1) * share)
            value = live * jnp.maximum(pre[rows, columns] + bias, 0.0)
            out_ref[group, :, columns] = value.astype(jnp.bfloat16)


def decode_kernel(n, piece, dec_ref, got_ref, codes_ref, *refs):
    half = n // 2
    layers, groups, block, cols = dec_ref.shape
    _, first, width, _ = piece
    out_refs, lhs_ref = refs[-2 * half - 1 : -1], refs[-1]
    src, rep = lax.axis_index("src"), lax.axis_index("rep")
    parity = lax.rem(src, 2)
    share = codes_ref.shape[2]
    depth = groups * block
    for place in range(groups):
        for r in range(2):
            origin = place * 2 + lax.rem(rep + r, 2)
            for side in range(2):
                latents = parity if side == 0 else 1 - parity
                latents = pl.ds(pl.multiple_of(latents * block, block), block)
                columns = slice((side * groups + place) * block, (side * groups + place + 1) * block)
                for j in range(half):
                    group = lax.rem(src // 2 + j, half)
                    rows = slice((2 * j + r) * share, (2 * j + r + 1) * share)
                    lhs_ref[rows, columns] = codes_ref[origin, group, :, latents]
    start = pl.multiple_of(rep * (cols // 2) + first, LANES)
    own = dec_ref[layer_of(piece, layers), :, :, pl.ds(start, width)].reshape(depth, width)
    got = got_ref[...].reshape(depth, width)
    total = jnp.dot(lhs_ref[:, :depth], own, preferred_element_type=jnp.float32)
    total += jnp.dot(lhs_ref[:, depth:], got, preferred_element_type=jnp.float32)
    for i, ref in enumerate(out_refs):
        ref[...] = total[i * share : (i + 1) * share].astype(ref.dtype)


def add_kernel(n, pieces, bias_ref, target_ref, *refs):
    out_hbm, out_ref, sems = refs[-3:]
    half = n // 2
    layers, _, cols = target_ref.shape
    rep = lax.axis_index("rep")
    copies = []
    for i, piece in enumerate(pieces):
        _, first, width, _ = piece
        layer = layer_of(piece, layers)
        for side in range(2):
            core = rep if side == 0 else 1 - rep
            columns = pl.ds(pl.multiple_of(core * (cols // 2) + first, LANES), width)
            total = bias_ref[0:1, columns]
            for other in range(1, layers):
                total = jnp.where(layer == other, bias_ref[other : other + 1, columns], total)
            total = total - target_ref[layer, :, columns].astype(jnp.float32)
            for ref in refs[(2 * i + side) * half : (2 * i + side + 1) * half]:
                total = total + ref[...].astype(jnp.float32)
            place = 2 * i + side
            out_ref[place, :, :width] = total.astype(jnp.bfloat16)
            copies.append(
                pltpu.make_async_copy(
                    out_ref.at[place, :, :width], out_hbm.at[layer, :, columns], sems.at[place]
                )
            )
            copies[-1].start()
    for copy in copies:
        copy.wait()


def body(acts, enc_w, enc_b, dec_w, dec_b, targets, active):
    n = lax.axis_size("src")
    rows, features = acts.shape
    layers, groups, block, cols = dec_w.shape
    share = rows // n
    half = n // 2
    pieces = cut_pieces(cols // 2)
    fetched = [piece for piece in pieces if not piece[3]]
    tile_rows = rows // active.shape[0]
    pair = [(i, i ^ 1) for i in range(n)]
    params = pltpu.CompilerParams(vmem_limit_bytes=VMEM_BYTES)
    vmem = pl.BlockSpec(memory_space=pltpu.VMEM)
    smem = pl.BlockSpec(memory_space=pltpu.SMEM)
    anywhere = pl.BlockSpec(memory_space=pl.ANY)
    cost = pl.CostEstimate(flops=0, bytes_accessed=0, transcendentals=0)

    dec_rows = dec_w
    acts, enc_w, dec_w = (
        pltpu.with_memory_space_constraint(value, pltpu.HBM)
        for value in (acts.reshape(half, 2, share, features), enc_w, dec_w)
    )

    def shape(*extent, kind=jnp.bfloat16):
        return jax.ShapeDtypeStruct(extent, kind)

    results = pl.pallas_call(
        functools.partial(encode_kernel, n, fetched),
        out_shape=[shape(half * share, 2 * block)] * n
        + [shape(groups, block, piece[2]) for piece in fetched],
        in_specs=[anywhere] * 3,
        out_specs=[vmem] * (n + len(fetched)),
        scratch_shapes=[
            pltpu.VMEM((2, half, share, features), jnp.bfloat16),
            pltpu.VMEM(enc_w.shape, jnp.bfloat16),
            pltpu.SemaphoreType.DMA((len(fetched), groups)),
            pltpu.SemaphoreType.DMA((2 * half,)),
            pltpu.SemaphoreType.DMA((8,)),
        ],
        compiler_params=params,
        cost_estimate=cost,
        name="encode",
    )(acts, enc_w, dec_w)
    terms, parts = list(results[:n]), list(results[n:])
    for k in range(1, n):
        terms[k] = lax.ppermute(terms[k], "src", [(i, peer(i, k, n)) for i in range(n)])
    own = pl.pallas_call(
        functools.partial(codes_kernel, n, share, tile_rows),
        out_shape=shape(half, share, 2 * block),
        in_specs=[smem] + [vmem] * (1 + n),
        out_specs=vmem,
        compiler_params=params,
        cost_estimate=cost,
        name="codes",
    )(active, enc_b.reshape(n, block), *terms)
    codes = lax.all_gather(own, ("tgt", "rep"), axis=0, tiled=False)

    def hold(value, after):
        return pl.pallas_call(
            lambda *refs: None,
            out_shape=jax.ShapeDtypeStruct(value.shape, value.dtype),
            in_specs=[anywhere] * 2,
            out_specs=anywhere,
            input_output_aliases={0: 0},
            compiler_params=params,
            cost_estimate=cost,
            name="hold",
        )(value, after)

    got = []
    for i, piece in enumerate(pieces):
        if piece[3]:
            first = next(j for j in range(i) if pieces[j][1] == piece[1])
            value = hold(got[first], codes)
            got.append(lax.ppermute(value, "parts", [(0, 1), (1, 0)]))
        else:
            value = parts.pop(0)
            if i > 0:
                value = hold(value, own)
            got.append(lax.ppermute(value, "src", pair))

    def add(some, begun):
        operands = [value for i in some for value in sums[i]]
        widest = max(piece[2] for piece in pieces)
        return pl.pallas_call(
            functools.partial(add_kernel, n, [pieces[i] for i in some]),
            out_shape=shape(layers, share, cols),
            in_specs=[vmem] * (2 + len(operands)) + [anywhere] * len(begun),
            out_specs=anywhere,
            scratch_shapes=[
                pltpu.VMEM((2 * len(some), share, widest), jnp.bfloat16),
                pltpu.SemaphoreType.DMA((2 * len(some),)),
            ],
            input_output_aliases={2 + len(operands): 0} if begun else {},
            compiler_params=params,
            cost_estimate=cost,
            name="add",
        )(dec_b, targets, *operands, *begun)

    sums, after, begun = [], [], []
    for i, piece in enumerate(pieces):
        if i == 3:
            begun = [add(list(range(2)), [])]
            after.append(begun[0])
        shapes = [shape(share, piece[2])] * (2 * half)
        shapes[0] = shape(share, piece[2], kind=jnp.float32)
        terms = pl.pallas_call(
            functools.partial(decode_kernel, n, piece),
            out_shape=shapes,
            in_specs=[vmem] * 3 + [anywhere] * len(after),
            out_specs=[vmem] * len(shapes),
            scratch_shapes=[pltpu.VMEM((rows, 2 * groups * block), jnp.bfloat16)],
            compiler_params=params,
            cost_estimate=cost,
            name="decode",
        )(dec_rows, got[i], codes, *after)
        after = [terms[0]]
        sums.append([None] * (2 * half))
        for j in [*range(1, half), 0]:
            for r in range(2):
                perm = [
                    (d * 2 + c, (d + 2 * j) % n * 2 + (c ^ r)) for d in range(n) for c in range(2)
                ]
                term = terms[2 * j + r]
                sums[i][r * half + j] = (
                    lax.ppermute(term, ("src", "rep"), perm) if j + r else term
                )

    return add(list(range(2, len(pieces))), begun)


def solution(mesh):
    in_specs = (
        P(("parts", "rep"), "src"),
        P("src", "tgt"),
        P("tgt"),
        P(None, None, "src", "tgt"),
        P(None, "tgt"),
        P(None, ("parts", "rep", "src"), "tgt"),
        P(("parts", "rep"), None),
    )
    out_specs = P(None, ("parts", "rep", "src"), "tgt")
    return jax.shard_map(body, mesh=mesh, in_specs=in_specs, out_specs=out_specs, check_vma=False)
```

time: 53.9 us -> 62.5 us (1.16)
  starting transfers between devices: 19 us -> 24.1 us
  waiting for transfers between devices: 21.1 us -> 24.5 us
    ppermute x16 -> x19, starting transfers between devices: 19 us -> 24.1 us  [the longest x12 12.9 us: body(): lax.ppermute(term, ('src', 'rep'), perm)]
    ppermute x16 -> x19, waiting for transfers between devices: 21.1 us -> 24.5 us  [the longest x12 16.2 us: body(): lax.ppermute(term, ('src', 'rep'), perm)]
    pallas_call x4 -> x5, Pallas kernels: 4.53 us -> 4.53 us  [the longest x1 3.28 us: body(): pl.pallas_call(functools.partial(encode_kernel, n, fetched), out_shape=[s...]
  transfers between devices with their start and end apart: 16 -> 19, of which waited for: 8 -> 7; matrix products, arithmetic and copies ran while one was open for 0% -> 0% of each run, Pallas kernels for 5% -> 4%
where the time goes in v12:
time: 62.5 us; the launch traced here: 62.3 us
  waiting for transfers between devices  24.5 us (39%)
  starting transfers between devices  24.1 us (39%)
  Pallas kernels  6.73 us (11%)
  blocking collectives  5.79 us (9%)
  local copies, waits for them, and re-layouts  1.06 us (2%)
    ppermute x12, waiting for transfers between devices, body(): lax.ppermute(term, ('src', 'rep'), perm)  16.2 us
    ppermute x12, starting transfers between devices, body(): lax.ppermute(term, ('src', 'rep'), perm)  12.9 us
    ppermute x3, waiting for transfers between devices, body(): lax.ppermute(terms[k], 'src', [(i, peer(i, k, n)) for i in range(n)])  8.3 us
    all_gather x1, blocking collectives, body(): codes = lax.all_gather(own, ('tgt', 'rep'), axis=0, tiled=False)  5.79 us
    ppermute x3, starting transfers between devices, body(): got.append(lax.ppermute(value, 'src', pair))  5.17 us
    ppermute x3, starting transfers between devices, body(): lax.ppermute(terms[k], 'src', [(i, peer(i, k, n)) for i in range(n)])  4.39 us
    pallas_call x1, Pallas kernels, body(): pl.pallas_call(functools.partial(encode_kernel, n, fetched), out_shape=[s...  3.28 us
    ppermute x1, starting transfers between devices, body(): got.append(lax.ppermute(value, 'parts', [(0, 1), (1, 0)]))  1.58 us
  transfers between devices with their start and end apart: 19, of which 7 were waited for; matrix products, arithmetic and copies ran while one was open for 0% of the time, Pallas kernels for 4%

profile of v12, /device:TPU:0, one launch (start us, length us, event | category | flops | bytes accessed | tf_op | source)
XLA Modules:
  0.0 62.3 jit_solution(13103669165205786160)
XLA Ops:
  0.0 3.3 %encode.1 = (bf16[128,256]{1,0:T(8,128)(2,1)S(1)}, bf16[128,256]{1,0:T(8,128)(2,1)S(1)}, bf16[128,256]{1,0:T(8,128)(2,1)S(1)}, bf16[128,256]{1,0:T(8,128)(2,1)S(...) custom-call(bf16[2,2,64,1024]{3,2,1,0:T(8,128)(2,1)} %bitcast.9, ...), custom_call_target="tpu_custom_call" | custom-call | tf_op jit(solution)/shard_map/encode/pallas_call | solution.py:202
  3.3 3.1 %collective-permute-start = (bf16[2,128,512]{2,1,0:T(8,128)(2,1)S(1)}, bf16[2,128,512]{2,1,0:T(8,128)(2,1)S(1)}, u32[]{:S(2)}, u32[]{:S(2)}) collective-permute-start(bf16[2,128,512]{2,1,0:T(8,128)(2,1)S(1)} %get-tuple-element.28), channel_id=1, source_target_pairs={{0,4},{4,0},{8,12},{12,8},{1,5},{5,1},{9,13},{13,9},{2,6},{6,2},{1... | collective-permute-start | bytes 786440 | tf_op jit(solution)/shard_map/ppermute | solution.py:255
  6.4 0.1 collective-permute-start.1
  6.5 2.9 %collective-permute-start.2 = (bf16[128,256]{1,0:T(8,128)(2,1)S(1)}, bf16[128,256]{1,0:T(8,128)(2,1)S(1)}, u32[]{:S(2)}, u32[]{:S(2)}) collective-permute-start(bf16[128,256]{1,0:T(8,128)(2,1)S(1)} %get-tuple-element.31), channel_id=1, source_target_pairs={{0,8},{4,12},{8,0},{12,4},{1,9},{5,13},{9,1},{13,5},{2,10},{6,14},... | collective-permute-start | bytes 196616 | tf_op jit(solution)/shard_map/ppermute | solution.py:221
  9.4 1.4 %collective-permute-start.3 = (bf16[128,256]{1,0:T(8,128)(2,1)S(1)}, bf16[128,256]{1,0:T(8,128)(2,1)S(1)}, u32[]{:S(2)}, u32[]{:S(2)}) collective-permute-start(bf16[128,256]{1,0:T(8,128)(2,1)S(1)} %get-tuple-element.32), channel_id=1, source_target_pairs={{0,12},{4,8},{8,4},{12,0},{1,13},{5,9},{9,5},{13,1},{2,14},{6,10},... | collective-permute-start | bytes 196616 | tf_op jit(solution)/shard_map/ppermute | solution.py:221
  10.8 4.7 %collective-permute-done.1.refs_1_ = bf16[128,256]{1,0:T(8,128)(2,1)S(1)} collective-permute-done((bf16[128,256]{1,0:T(8,128)(2,1)S(1)}, bf16[128,256]{1,0:T(8,128)(2,1)S(1)}, u32[]{:S(2)}, u32[]{:S(2)}) %collective-permute-start.1) | collective-permute-done | bytes 65568 | tf_op jit(solution)/shard_map/ppermute | solution.py:221
  15.5 0.0 collective-permute-done.2.refs_2_
  15.5 3.6 %collective-permute-done.3.refs_3_ = bf16[128,256]{1,0:T(8,128)(2,1)S(1)} collective-permute-done((bf16[128,256]{1,0:T(8,128)(2,1)S(1)}, bf16[128,256]{1,0:T(8,128)(2,1)S(1)}, u32[]{:S(2)}, u32[]{:S(2)}) %collective-permute-start.3) | collective-permute-done | bytes 65568 | tf_op jit(solution)/shard_map/ppermute | solution.py:221
  19.1 0.6 %codes.1.refs_1_ = bf16[2,64,256]{2,1,0:T(8,128)(2,1)S(1)} custom-call(s32[2,8]{1,0:T(2,128)S(1)} %copy-done.5, f32[4,128]{1,0:T(4,128)S(1)} %bitcast.8, bf16[128,256]{1,0:T(8,128)(2,1)S(1)} %get-tuple-element.29.refs_0_, bf16[128,256]{1,0:T(8,128)(2,1)S(1)} %collective-permute-done.1.refs_1_, bf16[128,256]{1,0:T(8,128)(2,1)S(1)} %collective-permute-done.2.refs_2_, ...), custom_call_target="tpu_custom_call" | custom-call | tf_op jit(solution)/shard_map/codes/pallas_call | solution.py:222
  19.7 0.1 collective-permute-start.5
  19.8 5.8 %all-gather = bf16[8,64,256]{2,1,0:T(8,128)(2,1)S(1)} all-gather(bf16[2,64,256]{2,1,0:T(8,128)(2,1)S(1)} %codes.1.refs_1_), channel_id=2, replica_groups=mesh['parts'=2,'src'=4,'tgt'=2,'rep'=2] {'tgt','rep'}, dimensions={0}, use_global_device_ids=true | all-gather | bytes 327680 | tf_op jit(solution)/shard_map/all_gather | solution.py:231
  25.6 0.0 collective-permute-done.refs_0_.got_ref
  25.6 0.3 decode.4
  25.9 1.6 %collective-permute-start.4 = (bf16[2,128,512]{2,1,0:T(8,128)(2,1)S(1)}, bf16[2,128,512]{2,1,0:T(8,128)(2,1)S(1)}, u32[]{:S(2)}, u32[]{:S(2)}) collective-permute-start(bf16[2,128,512]{2,1,0:T(8,128)(2,1)S(1)} %hold.3), channel_id=1, source_target_pairs={{0,16},{16,0},{1,17},{17,1},{2,18},{18,2},{3,19},{19,3},{4,20},{20... | collective-permute-start | bytes 786440 | tf_op jit(solution)/shard_map/ppermute | solution.py:250
  27.5 2.0 %collective-permute-start.9 = (bf16[2,128,512]{2,1,0:T(8,128)(2,1)S(1)}, bf16[2,128,512]{2,1,0:T(8,128)(2,1)S(1)}, u32[]{:S(2)}, u32[]{:S(2)}) collective-permute-start(bf16[2,128,512]{2,1,0:T(8,128)(2,1)S(1)} %hold.5), channel_id=1, source_target_pairs={{0,4},{4,0},{8,12},{12,8},{1,5},{5,1},{9,13},{13,9},{2,6},{6,2},{1... | collective-permute-start | bytes 786440 | tf_op jit(solution)/shard_map/ppermute | solution.py:255
  29.5 0.2 collective-permute-start.10
  29.7 0.0 collective-permute-start.11
  29.7 0.0 collective-permute-done.5.got_ref
  29.7 2.9 %collective-permute-start.12 = (bf16[64,512]{1,0:T(8,128)(2,1)S(1)}, bf16[64,512]{1,0:T(8,128)(2,1)S(1)}, u32[]{:S(2)}, u32[]{:S(2)}) collective-permute-start(bf16[64,512]{1,0:T(8,128)(2,1)S(1)} %get-tuple-element.43), channel_id=1, source_target_pairs={{0,9},{1,8},{4,13},{5,12},{8,1},{9,0},{12,5},{13,4},{2,11},{3,10},... | collective-permute-start | bytes 196616 | tf_op jit(solution)/shard_map/ppermute | solution.py:301
  32.6 0.3 decode.5
  32.9 4.5 %collective-permute-done.10.refs_1_ = bf16[64,512]{1,0:T(8,128)(2,1)S(1)} collective-permute-done((bf16[64,512]{1,0:T(8,128)(2,1)S(1)}, bf16[64,512]{1,0:T(8,128)(2,1)S(1)}, u32[]{:S(2)}, u32[]{:S(2)}) %collective-permute-start.10) | collective-permute-done | bytes 65568 | tf_op jit(solution)/shard_map/ppermute | solution.py:301
  37.4 3.4 %collective-permute-start.13 = (bf16[64,512]{1,0:T(8,128)(2,1)S(1)}, bf16[64,512]{1,0:T(8,128)(2,1)S(1)}, u32[]{:S(2)}, u32[]{:S(2)}) collective-permute-start(bf16[64,512]{1,0:T(8,128)(2,1)S(1)} %get-tuple-element.44), channel_id=1, source_target_pairs={{0,8},{1,9},{4,12},{5,13},{8,0},{9,1},{12,4},{13,5},{2,10},{3,11},... | collective-permute-start | bytes 196616 | tf_op jit(solution)/shard_map/ppermute | solution.py:301
  40.8 0.0 collective-permute-done.11.refs_2_
  40.8 0.0 collective-permute-start.14
  40.8 0.0 collective-permute-done.4.got_ref
  40.8 0.1 collective-permute-start.15
  41.0 0.3 decode.6
  41.3 0.0 collective-permute-done.12.refs_3_
  41.3 3.0 %collective-permute-start.6 = (bf16[64,512]{1,0:T(8,128)(2,1)S(1)}, bf16[64,512]{1,0:T(8,128)(2,1)S(1)}, u32[]{:S(2)}, u32[]{:S(2)}) collective-permute-start(bf16[64,512]{1,0:T(8,128)(2,1)S(1)} %get-tuple-element.37), channel_id=1, source_target_pairs={{0,8},{1,9},{4,12},{5,13},{8,0},{9,1},{12,4},{13,5},{2,10},{3,11},... | collective-permute-start | bytes 196616 | tf_op jit(solution)/shard_map/ppermute | solution.py:301
  44.2 0.0 collective-permute-done.13.refs_5_
  44.2 0.0 collective-permute-done.14.refs_6_
  44.3 4.4 %collective-permute-done.15.refs_7_ = bf16[64,512]{1,0:T(8,128)(2,1)S(1)} collective-permute-done((bf16[64,512]{1,0:T(8,128)(2,1)S(1)}, bf16[64,512]{1,0:T(8,128)(2,1)S(1)}, u32[]{:S(2)}, u32[]{:S(2)}) %collective-permute-start.15) | collective-permute-done | bytes 65568 | tf_op jit(solution)/shard_map/ppermute | solution.py:301
  48.6 0.8 %add.2.refs_1_.refs_8_ = bf16[2,64,2048]{2,1,0:T(8,128)(2,1)} custom-call(f32[2,2048]{1,0:T(2,128)S(1)} %copy-done.3, bf16[2,64,2048]{2,1,0:T(8,128)(2,1)S(1)} %copy-done.2, f32[64,512]{1,0:T(8,128)S(1)} %get-tuple-element.34.refs_0_, bf16[64,512]{1,0:T(8,128)(2,1)S(1)} %collective-permute-done.10.refs_1_, ...), custom_call_target="tpu_custom_call" | custom-call | tf_op jit(solution)/shard_map/add/pallas_call | solution.py:260
  49.4 0.2 collective-permute-start.7
  49.6 0.0 collective-permute-start.8
  49.6 0.0 collective-permute-done.9.got_ref
  49.6 1.0 %copy-done.1 = bf16[2,64,2048]{2,1,0:T(8,128)(2,1)S(1)} copy-done((bf16[2,64,2048]{2,1,0:T(8,128)(2,1)S(1)}, bf16[2,64,2048]{2,1,0:T(8,128)(2,1)}, u32[]{:S(2)}) %copy-start.1) | copy-done | bytes 524312
  50.7 0.3 decode.7
  51.0 3.0 %collective-permute-start.16 = (bf16[64,512]{1,0:T(8,128)(2,1)S(1)}, bf16[64,512]{1,0:T(8,128)(2,1)S(1)}, u32[]{:S(2)}, u32[]{:S(2)}) collective-permute-start(bf16[64,512]{1,0:T(8,128)(2,1)S(1)} %get-tuple-element.48), channel_id=1, source_target_pairs={{0,8},{1,9},{4,12},{5,13},{8,0},{9,1},{12,4},{13,5},{2,10},{3,11},... | collective-permute-start | bytes 196616 | tf_op jit(solution)/shard_map/ppermute | solution.py:301
  54.0 0.0 collective-permute-start.17
  54.0 0.0 collective-permute-done.6.refs_1_
  54.0 0.2 collective-permute-start.18
  54.2 0.0 collective-permute-done.7.refs_2_
  54.2 1.7 %collective-permute-done.8.refs_3_ = bf16[64,512]{1,0:T(8,128)(2,1)S(1)} collective-permute-done((bf16[64,512]{1,0:T(8,128)(2,1)S(1)}, bf16[64,512]{1,0:T(8,128)(2,1)S(1)}, u32[]{:S(2)}, u32[]{:S(2)}) %collective-permute-start.8) | collective-permute-done | bytes 65568 | tf_op jit(solution)/shard_map/ppermute | solution.py:301
  55.9 4.3 %collective-permute-done.16.refs_5_ = bf16[64,512]{1,0:T(8,128)(2,1)S(1)} collective-permute-done((bf16[64,512]{1,0:T(8,128)(2,1)S(1)}, bf16[64,512]{1,0:T(8,128)(2,1)S(1)}, u32[]{:S(2)}, u32[]{:S(2)}) %collective-permute-start.16) | collective-permute-done | bytes 65568 | tf_op jit(solution)/shard_map/ppermute | solution.py:301
  60.2 0.0 collective-permute-done.17.refs_6_
  60.2 1.3 %collective-permute-done.18.refs_7_ = bf16[64,512]{1,0:T(8,128)(2,1)S(1)} collective-permute-done((bf16[64,512]{1,0:T(8,128)(2,1)S(1)}, bf16[64,512]{1,0:T(8,128)(2,1)S(1)}, u32[]{:S(2)}, u32[]{:S(2)}) %collective-permute-start.18) | collective-permute-done | bytes 65568 | tf_op jit(solution)/shard_map/ppermute | solution.py:301
  61.5 0.8 %add.3 = bf16[2,64,2048]{2,1,0:T(8,128)(2,1)} custom-call(f32[2,2048]{1,0:T(2,128)S(1)} %copy-done.3, bf16[2,64,2048]{2,1,0:T(8,128)(2,1)S(1)} %copy-done.2, f32[64,512]{1,0:T(8,128)S(1)} %get-tuple-element.36.refs_0_, bf16[64,512]{1,0:T(8,128)(2,1)S(1)} %collective-permute-done.6.refs_1_, ...), custom_call_target="tpu_custom_call", output_to_operand_aliasing={{}: (10, {})} | custom-call | tf_op jit(solution)/shard_map/add/pallas_call | solution.py:260
  (14 shorter events, 0.0 us)
Async XLA Ops:
  0.0 19.1 %copy-start.5 = (s32[2,8]{1,0:T(2,128)S(1)}, s32[2,8]{1,0:T(2,128)}, u32[]{:S(2)}) copy-start(s32[2,8]{1,0:T(2,128)} %active_ref.1) | copy-start | bytes 196
  0.0 19.1 %copy-start.4 = (f32[512]{0:T(512)S(1)}, f32[512]{0:T(512)}, u32[]{:S(2)}) copy-start(f32[512]{0:T(512)} %param.9) | copy-start | bytes 6148
  0.0 25.6 %copy-start = (bf16[2,2,128,2048]{3,2,1,0:T(8,128)(2,1)S(1)}, bf16[2,2,128,2048]{3,2,1,0:T(8,128)(2,1)}, u32[]{:S(2)}) copy-start(bf16[2,2,128,2048]{3,2,1,0:T(8,128)(2,1)} %dec_ref.7) | copy-start | bytes 6291460
  3.3 22.3 %collective-permute-start = (bf16[2,128,512]{2,1,0:T(8,128)(2,1)S(1)}, bf16[2,128,512]{2,1,0:T(8,128)(2,1)S(1)}, u32[]{:S(2)}, u32[]{:S(2)}) collective-permute-start(bf16[2,128,512]{2,1,0:T(8,128)(2,1)S(1)} %get-tuple-element.28), channel_id=1, source_target_pairs={{0,4},{4,0},{8,12},{12,8},{1,5},{5,1},{9,13},{13,9},{2,6},{6,2},{1... | collective-permute-start | bytes 786440 | tf_op jit(solution)/shard_map/ppermute | solution.py:255
  6.4 9.1 %collective-permute-start.1 = (bf16[128,256]{1,0:T(8,128)(2,1)S(1)}, bf16[128,256]{1,0:T(8,128)(2,1)S(1)}, u32[]{:S(2)}, u32[]{:S(2)}) collective-permute-start(bf16[128,256]{1,0:T(8,128)(2,1)S(1)} %get-tuple-element.30), channel_id=1, source_target_pairs={{0,4},{4,0},{8,12},{12,8},{1,5},{5,1},{9,13},{13,9},{2,6},{6,2},{1... | collective-permute-start | bytes 196616 | tf_op jit(solution)/shard_map/ppermute | solution.py:221
  6.5 9.0 %collective-permute-start.2 = (bf16[128,256]{1,0:T(8,128)(2,1)S(1)}, bf16[128,256]{1,0:T(8,128)(2,1)S(1)}, u32[]{:S(2)}, u32[]{:S(2)}) collective-permute-start(bf16[128,256]{1,0:T(8,128)(2,1)S(1)} %get-tuple-element.31), channel_id=1, source_target_pairs={{0,8},{4,12},{8,0},{12,4},{1,9},{5,13},{9,1},{13,5},{2,10},{6,14},... | collective-permute-start | bytes 196616 | tf_op jit(solution)/shard_map/ppermute | solution.py:221
  9.4 9.7 %collective-permute-start.3 = (bf16[128,256]{1,0:T(8,128)(2,1)S(1)}, bf16[128,256]{1,0:T(8,128)(2,1)S(1)}, u32[]{:S(2)}, u32[]{:S(2)}) collective-permute-start(bf16[128,256]{1,0:T(8,128)(2,1)S(1)} %get-tuple-element.32), channel_id=1, source_target_pairs={{0,12},{4,8},{8,4},{12,0},{1,13},{5,9},{9,5},{13,1},{2,14},{6,10},... | collective-permute-start | bytes 196616 | tf_op jit(solution)/shard_map/ppermute | solution.py:221
  19.7 9.9 %collective-permute-start.5 = (bf16[2,128,512]{2,1,0:T(8,128)(2,1)S(1)}, bf16[2,128,512]{2,1,0:T(8,128)(2,1)S(1)}, u32[]{:S(2)}, u32[]{:S(2)}) collective-permute-start(bf16[2,128,512]{2,1,0:T(8,128)(2,1)S(1)} %hold.4), channel_id=1, source_target_pairs={{0,4},{4,0},{8,12},{12,8},{1,5},{5,1},{9,13},{13,9},{2,6},{6,2},{1... | collective-permute-start | bytes 786440 | tf_op jit(solution)/shard_map/ppermute | solution.py:255
  25.9 14.9 %collective-permute-start.4 = (bf16[2,128,512]{2,1,0:T(8,128)(2,1)S(1)}, bf16[2,128,512]{2,1,0:T(8,128)(2,1)S(1)}, u32[]{:S(2)}, u32[]{:S(2)}) collective-permute-start(bf16[2,128,512]{2,1,0:T(8,128)(2,1)S(1)} %hold.3), channel_id=1, source_target_pairs={{0,16},{16,0},{1,17},{17,1},{2,18},{18,2},{3,19},{19,3},{4,20},{20... | collective-permute-start | bytes 786440 | tf_op jit(solution)/shard_map/ppermute | solution.py:250
  27.5 22.1 %collective-permute-start.9 = (bf16[2,128,512]{2,1,0:T(8,128)(2,1)S(1)}, bf16[2,128,512]{2,1,0:T(8,128)(2,1)S(1)}, u32[]{:S(2)}, u32[]{:S(2)}) collective-permute-start(bf16[2,128,512]{2,1,0:T(8,128)(2,1)S(1)} %hold.5), channel_id=1, source_target_pairs={{0,4},{4,0},{8,12},{12,8},{1,5},{5,1},{9,13},{13,9},{2,6},{6,2},{1... | collective-permute-start | bytes 786440 | tf_op jit(solution)/shard_map/ppermute | solution.py:255
  29.5 7.9 %collective-permute-start.10 = (bf16[64,512]{1,0:T(8,128)(2,1)S(1)}, bf16[64,512]{1,0:T(8,128)(2,1)S(1)}, u32[]{:S(2)}, u32[]{:S(2)}) collective-permute-start(bf16[64,512]{1,0:T(8,128)(2,1)S(1)} %get-tuple-element.41), channel_id=1, source_target_pairs={{0,8},{1,9},{4,12},{5,13},{8,0},{9,1},{12,4},{13,5},{2,10},{3,11},... | collective-permute-start | bytes 196616 | tf_op jit(solution)/shard_map/ppermute | solution.py:301
  29.7 11.1 %collective-permute-start.11 = (bf16[64,512]{1,0:T(8,128)(2,1)S(1)}, bf16[64,512]{1,0:T(8,128)(2,1)S(1)}, u32[]{:S(2)}, u32[]{:S(2)}) collective-permute-start(bf16[64,512]{1,0:T(8,128)(2,1)S(1)} %get-tuple-element.42), channel_id=1, source_target_pairs={{0,1},{1,0},{4,5},{5,4},{8,9},{9,8},{12,13},{13,12},{2,3},{3,2},{6... | collective-permute-start | bytes 196616 | tf_op jit(solution)/shard_map/ppermute | solution.py:301
  29.7 11.6 %collective-permute-start.12 = (bf16[64,512]{1,0:T(8,128)(2,1)S(1)}, bf16[64,512]{1,0:T(8,128)(2,1)S(1)}, u32[]{:S(2)}, u32[]{:S(2)}) collective-permute-start(bf16[64,512]{1,0:T(8,128)(2,1)S(1)} %get-tuple-element.43), channel_id=1, source_target_pairs={{0,9},{1,8},{4,13},{5,12},{8,1},{9,0},{12,5},{13,4},{2,11},{3,10},... | collective-permute-start | bytes 196616 | tf_op jit(solution)/shard_map/ppermute | solution.py:301
  32.6 16.1 %copy-start.2 = (bf16[2,64,2048]{2,1,0:T(8,128)(2,1)S(1)}, bf16[2,64,2048]{2,1,0:T(8,128)(2,1)}, u32[]{:S(2)}) copy-start(bf16[2,64,2048]{2,1,0:T(8,128)(2,1)} %target_ref.3) | copy-start | bytes 1572868
  32.6 16.1 %copy-start.3 = (f32[2,2048]{1,0:T(2,128)S(1)}, f32[2,2048]{1,0:T(2,128)}, u32[]{:S(2)}) copy-start(f32[2,2048]{1,0:T(2,128)} %bias_ref.3) | copy-start | bytes 49156
  37.4 6.8 %collective-permute-start.13 = (bf16[64,512]{1,0:T(8,128)(2,1)S(1)}, bf16[64,512]{1,0:T(8,128)(2,1)S(1)}, u32[]{:S(2)}, u32[]{:S(2)}) collective-permute-start(bf16[64,512]{1,0:T(8,128)(2,1)S(1)} %get-tuple-element.44), channel_id=1, source_target_pairs={{0,8},{1,9},{4,12},{5,13},{8,0},{9,1},{12,4},{13,5},{2,10},{3,11},... | collective-permute-start | bytes 196616 | tf_op jit(solution)/shard_map/ppermute | solution.py:301
  40.8 3.4 %collective-permute-start.14 = (bf16[64,512]{1,0:T(8,128)(2,1)S(1)}, bf16[64,512]{1,0:T(8,128)(2,1)S(1)}, u32[]{:S(2)}, u32[]{:S(2)}) collective-permute-start(bf16[64,512]{1,0:T(8,128)(2,1)S(1)} %get-tuple-element.45), channel_id=1, source_target_pairs={{0,1},{1,0},{4,5},{5,4},{8,9},{9,8},{12,13},{13,12},{2,3},{3,2},{6... | collective-permute-start | bytes 196616 | tf_op jit(solution)/shard_map/ppermute | solution.py:301
  40.8 7.8 %collective-permute-start.15 = (bf16[64,512]{1,0:T(8,128)(2,1)S(1)}, bf16[64,512]{1,0:T(8,128)(2,1)S(1)}, u32[]{:S(2)}, u32[]{:S(2)}) collective-permute-start(bf16[64,512]{1,0:T(8,128)(2,1)S(1)} %get-tuple-element.46), channel_id=1, source_target_pairs={{0,9},{1,8},{4,13},{5,12},{8,1},{9,0},{12,5},{13,4},{2,11},{3,10},... | collective-permute-start | bytes 196616 | tf_op jit(solution)/shard_map/ppermute | solution.py:301
  41.3 12.7 %collective-permute-start.6 = (bf16[64,512]{1,0:T(8,128)(2,1)S(1)}, bf16[64,512]{1,0:T(8,128)(2,1)S(1)}, u32[]{:S(2)}, u32[]{:S(2)}) collective-permute-start(bf16[64,512]{1,0:T(8,128)(2,1)S(1)} %get-tuple-element.37), channel_id=1, source_target_pairs={{0,8},{1,9},{4,12},{5,13},{8,0},{9,1},{12,4},{13,5},{2,10},{3,11},... | collective-permute-start | bytes 196616 | tf_op jit(solution)/shard_map/ppermute | solution.py:301
  49.4 4.8 %collective-permute-start.7 = (bf16[64,512]{1,0:T(8,128)(2,1)S(1)}, bf16[64,512]{1,0:T(8,128)(2,1)S(1)}, u32[]{:S(2)}, u32[]{:S(2)}) collective-permute-start(bf16[64,512]{1,0:T(8,128)(2,1)S(1)} %get-tuple-element.38), channel_id=1, source_target_pairs={{0,1},{1,0},{4,5},{5,4},{8,9},{9,8},{12,13},{13,12},{2,3},{3,2},{6... | collective-permute-start | bytes 196616 | tf_op jit(solution)/shard_map/ppermute | solution.py:301
  49.6 6.2 %collective-permute-start.8 = (bf16[64,512]{1,0:T(8,128)(2,1)S(1)}, bf16[64,512]{1,0:T(8,128)(2,1)S(1)}, u32[]{:S(2)}, u32[]{:S(2)}) collective-permute-start(bf16[64,512]{1,0:T(8,128)(2,1)S(1)} %get-tuple-element.39), channel_id=1, source_target_pairs={{0,9},{1,8},{4,13},{5,12},{8,1},{9,0},{12,5},{13,4},{2,11},{3,10},... | collective-permute-start | bytes 196616 | tf_op jit(solution)/shard_map/ppermute | solution.py:301
  49.6 1.0 %copy-start.1 = (bf16[2,64,2048]{2,1,0:T(8,128)(2,1)S(1)}, bf16[2,64,2048]{2,1,0:T(8,128)(2,1)}, u32[]{:S(2)}) copy-start(bf16[2,64,2048]{2,1,0:T(8,128)(2,1)} %add.2.refs_1_.refs_8_) | copy-start | bytes 1572868
  51.0 9.2 %collective-permute-start.16 = (bf16[64,512]{1,0:T(8,128)(2,1)S(1)}, bf16[64,512]{1,0:T(8,128)(2,1)S(1)}, u32[]{:S(2)}, u32[]{:S(2)}) collective-permute-start(bf16[64,512]{1,0:T(8,128)(2,1)S(1)} %get-tuple-element.48), channel_id=1, source_target_pairs={{0,8},{1,9},{4,12},{5,13},{8,0},{9,1},{12,4},{13,5},{2,10},{3,11},... | collective-permute-start | bytes 196616 | tf_op jit(solution)/shard_map/ppermute | solution.py:301
  54.0 6.2 %collective-permute-start.17 = (bf16[64,512]{1,0:T(8,128)(2,1)S(1)}, bf16[64,512]{1,0:T(8,128)(2,1)S(1)}, u32[]{:S(2)}, u32[]{:S(2)}) collective-permute-start(bf16[64,512]{1,0:T(8,128)(2,1)S(1)} %get-tuple-element.49), channel_id=1, source_target_pairs={{0,1},{1,0},{4,5},{5,4},{8,9},{9,8},{12,13},{13,12},{2,3},{3,2},{6... | collective-permute-start | bytes 196616 | tf_op jit(solution)/shard_map/ppermute | solution.py:301
  54.0 7.5 %collective-permute-start.18 = (bf16[64,512]{1,0:T(8,128)(2,1)S(1)}, bf16[64,512]{1,0:T(8,128)(2,1)S(1)}, u32[]{:S(2)}, u32[]{:S(2)}) collective-permute-start(bf16[64,512]{1,0:T(8,128)(2,1)S(1)} %get-tuple-element.50), channel_id=1, source_target_pairs={{0,9},{1,8},{4,13},{5,12},{8,1},{9,0},{12,5},{13,4},{2,11},{3,10},... | collective-permute-start | bytes 196616 | tf_op jit(solution)/shard_map/ppermute | solution.py:301

commit v13 on v10

--- a/solution.py
+++ b/solution.py
@@ -9,7 +9,7 @@
 
 VMEM_BYTES = 32 * 1024 * 1024
 LANES = 128
-SHARES = (4, 4)
+SHARES = (3, 5)
 
 
 def cut_pieces(layers, columns):
@@ -116,16 +116,13 @@
             out_ref[group, :, columns] = value.astype(jnp.bfloat16)
 
 
-def decode_kernel(n, piece, shared, dec_ref, *refs):
+def gather_kernel(n, *refs):
     half = n // 2
-    layers, groups, block, cols = dec_ref.shape
-    _, first, width = piece
-    got_refs, refs = refs[: 1 + shared], refs[1 + shared :]
-    code_refs, out_refs, lhs_ref = refs[: 2 * groups], refs[-2 * half - 1 : -1], refs[-1]
+    code_refs, out_ref = refs[:-1], refs[-1]
+    groups = len(code_refs) // 2
     src, tgt = lax.axis_index("src"), lax.axis_index("tgt")
     parity = lax.rem(src, 2)
-    share = code_refs[0].shape[1]
-    depth = groups * block
+    share, block = code_refs[0].shape[1], code_refs[0].shape[2] // 2
     for k in range(groups):
         place = lax.rem(tgt - k + groups, groups)
         for side in range(2):
@@ -136,7 +133,15 @@
                 group = lax.rem(src // 2 + j, half)
                 for r in range(2):
                     rows = slice((2 * j + r) * share, (2 * j + r + 1) * share)
-                    lhs_ref[rows, columns] = code_refs[2 * k + r][group, :, latents]
+                    out_ref[rows, columns] = code_refs[2 * k + r][group, :, latents]
+
+
+def decode_kernel(n, piece, shared, dec_ref, lhs_ref, *refs):
+    layers, groups, block, cols = dec_ref.shape
+    _, first, width = piece
+    got_refs, out_refs = refs[: 1 + shared], refs[-2 * (n // 2) :]
+    depth = groups * block
+    share = lhs_ref.shape[0] // len(out_refs)
     start = pl.multiple_of(lax.axis_index("rep") * (cols // 2) + first, LANES)
     for i in range(layers):
         layer = lax.rem(lax.axis_index("parts") + i, layers) if shared else i
@@ -190,7 +195,12 @@
     vmem = pl.BlockSpec(memory_space=pltpu.VMEM)
     smem = pl.BlockSpec(memory_space=pltpu.SMEM)
     anywhere = pl.BlockSpec(memory_space=pl.ANY)
-    cost = pl.CostEstimate(flops=0, bytes_accessed=0, transcendentals=0)
+    def weight(billions):
+        return pl.CostEstimate(
+            flops=int(billions * 1e9), bytes_accessed=0, transcendentals=0
+        )
+
+    cost = weight(0)
 
     dec_rows = dec_w
     acts, enc_w, dec_w = (
@@ -230,7 +240,7 @@
         in_specs=[smem] + [vmem] * (1 + n),
         out_specs=vmem,
         compiler_params=params,
-        cost_estimate=cost,
+        cost_estimate=weight(20),
         name="codes",
     )(active, enc_b.reshape(n, block), *terms)
     codes = []
@@ -240,6 +250,16 @@
                 (i * 2 + c, (i + k) % groups * 2 + (c ^ r)) for i in range(groups) for c in range(2)
             ]
             codes.append(lax.ppermute(own, ("tgt", "rep"), perm) if k + r else own)
+
+    lhs = pl.pallas_call(
+        functools.partial(gather_kernel, n),
+        out_shape=shape(rows, 2 * groups * block),
+        in_specs=[vmem] * len(codes),
+        out_specs=vmem,
+        compiler_params=params,
+        cost_estimate=weight(20),
+        name="gather",
+    )(*codes)
 
     def hold(value, after):
         return pl.pallas_call(
@@ -256,8 +276,8 @@
     got = [[lax.ppermute(parts[0], "src", pair)]]
     got[0].append(lax.ppermute(got[0][0], "parts", [(0, 1), (1, 0)]))
     if len(pieces) > 1:
-        got.append([lax.ppermute(hold(parts[1], codes[1]), "src", pair)])
-    def add(some, begun):
+        got.append([lax.ppermute(hold(parts[1], own), "src", pair)])
+    def add(some, begun, billions):
         operands = [value for i in some for value in sums[i]]
         return pl.pallas_call(
             functools.partial(add_kernel, n, [pieces[i] for i in some]),
@@ -270,27 +290,23 @@
             ],
             input_output_aliases={2 + len(operands): 0} if begun else {},
             compiler_params=params,
-            cost_estimate=cost,
+            cost_estimate=weight(billions),
             name="add",
         )(dec_b, targets, *operands, *begun)
 
     sums, after, begun = [], [], []
     for i, (_, _, width) in enumerate(pieces):
-        if i == 2:
-            begun = [add([0], [])]
-            after.append(begun[0])
         shapes = [shape(layers, share, width)] * (2 * half)
         shapes[0] = shape(layers, share, width, kind=jnp.float32)
         terms = pl.pallas_call(
             functools.partial(decode_kernel, n, pieces[i], i == 0),
             out_shape=shapes,
-            in_specs=[vmem] * (1 + len(got[i]) + 2 * groups) + [anywhere] * len(after),
+            in_specs=[vmem] * (2 + len(got[i])) + [anywhere] * len(after),
             out_specs=[vmem] * len(shapes),
-            scratch_shapes=[pltpu.VMEM((rows, 2 * groups * block), jnp.bfloat16)],
             compiler_params=params,
-            cost_estimate=cost,
+            cost_estimate=weight(0),
             name="decode",
-        )(dec_rows, *got[i], *codes, *after)
+        )(dec_rows, lhs, *got[i], *after)
         after = [terms[0]]
         if i == 0:
             for part in parts[2:]:
@@ -304,7 +320,9 @@
                 term = terms[2 * j + r]
                 sums[i].append(lax.ppermute(term, ("src", "rep"), perm) if j + r else term)
 
-    return add(list(range(len(begun), len(pieces))), begun)
+    for i in range(len(pieces) - 1):
+        begun = [add([i], begun, 20)]
+    return add([len(pieces) - 1], begun, 0)
 
 
 def solution(mesh):

time: 53 us -> 57.1 us (1.077)
  starting transfers between devices: 13 us -> 16.3 us
  Pallas kernels: 5.79 us -> 6.44 us
  waiting for transfers between devices: 33.5 us -> 34.1 us
    ppermute x1, waiting for transfers between devices: 4.05 us -> 10.4 us  [body(): got.append([lax.ppermute(hold(parts[1], own), 'src', pair)])]
    ppermute x6, waiting for transfers between devices: 17 us -> 12.2 us  [body(): sums[i].append(lax.ppermute(term, ('src', 'rep'), perm) if j + r else term)]
    ppermute x3, waiting for transfers between devices: 5.51 us -> 2.14 us  [body(): codes.append(lax.ppermute(own, ('tgt', 'rep'), perm) if k + r else own)]
    ppermute x1, waiting for transfers between devices: 0.25 us -> 3.44 us  [body(): got[0].append(lax.ppermute(got[0][0], 'parts', [(0, 1), (1, 0)]))]
    ppermute x6, starting transfers between devices: 3.25 us -> 6.19 us  [body(): sums[i].append(lax.ppermute(term, ('src', 'rep'), perm) if j + r else term)]
    ppermute x1, waiting for transfers between devices: 0.8 us -> 0.01 us  [body(): got = [[lax.ppermute(parts[0], 'src', pair)]]]
    pallas_call x1 -> x2, Pallas kernels: 0.92 us -> 1.57 us  [add(): pl.pallas_call(functools.partial(add_kernel, n, [pieces[i] for i in some]...]
  transfers between devices with their start and end apart: 15 -> 15, of which waited for: 12 -> 8; matrix products, arithmetic and copies ran while one was open for 0% -> 0% of each run, Pallas kernels for 3% -> 4%
where the time goes in v13:
time: 57.1 us; the launch traced here: 56.9 us
  waiting for transfers between devices  34.1 us (60%)
  starting transfers between devices  16.3 us (29%)
  Pallas kernels  6.44 us (11%)
    ppermute x6, waiting for transfers between devices, body(): sums[i].append(lax.ppermute(term, ('src', 'rep'), perm) if j + r else term)  12.2 us
    ppermute x1, waiting for transfers between devices, body(): got.append([lax.ppermute(hold(parts[1], own), 'src', pair)])  10.4 us
    ppermute x6, starting transfers between devices, body(): sums[i].append(lax.ppermute(term, ('src', 'rep'), perm) if j + r else term)  6.19 us
    ppermute x3, waiting for transfers between devices, body(): lax.ppermute(terms[k], 'src', [(i, peer(i, k, n)) for i in range(n)])  5.92 us
    ppermute x3, starting transfers between devices, body(): lax.ppermute(terms[k], 'src', [(i, peer(i, k, n)) for i in range(n)])  5.68 us
    ppermute x1, waiting for transfers between devices, body(): got[0].append(lax.ppermute(got[0][0], 'parts', [(0, 1), (1, 0)]))  3.44 us
    pallas_call x1, Pallas kernels, body(): pl.pallas_call(functools.partial(encode_kernel, n, pieces), out_shape=[sh...  3.19 us
    ppermute x3, waiting for transfers between devices, body(): codes.append(lax.ppermute(own, ('tgt', 'rep'), perm) if k + r else own)  2.14 us
  transfers between devices with their start and end apart: 15, of which 8 were waited for; matrix products, arithmetic and copies ran while one was open for 0% of the time, Pallas kernels for 4%

profile of v13, /device:TPU:0, one launch (start us, length us, event | category | flops | bytes accessed | tf_op | source)
XLA Modules:
  0.0 56.9 jit_solution(12267815896574976154)
XLA Ops:
  0.0 0.0 copy-start.4
  0.0 0.0 copy-start.3
  0.0 3.2 %encode.1 = (bf16[128,256]{1,0:T(8,128)(2,1)S(1)}, bf16[128,256]{1,0:T(8,128)(2,1)S(1)}, bf16[128,256]{1,0:T(8,128)(2,1)S(1)}, bf16[128,256]{1,0:T(8,128)(2,1)S(...) custom-call(bf16[2,2,64,1024]{3,2,1,0:T(8,128)(2,1)} %bitcast.3, bf16[1024,512]{1,0:T(8,128)(2,1)} %w_hbm.1, ...), custom_call_target="tpu_custom_call" | custom-call | tf_op jit(solution)/shard_map/encode/pallas_call | solution.py:214
  3.2 3.1 %collective-permute-start = (bf16[128,256]{1,0:T(8,128)(2,1)S(1)}, bf16[128,256]{1,0:T(8,128)(2,1)S(1)}, u32[]{:S(2)}, u32[]{:S(2)}) collective-permute-start(bf16[128,256]{1,0:T(8,128)(2,1)S(1)} %get-tuple-element.20), channel_id=1, source_target_pairs={{0,4},{4,0},{8,12},{12,8},{1,5},{5,1},{9,13},{13,9},{2,6},{6,2},{1... | collective-permute-start | bytes 196616 | tf_op jit(solution)/shard_map/ppermute | solution.py:236
  6.3 2.6 %collective-permute-start.1 = (bf16[128,256]{1,0:T(8,128)(2,1)S(1)}, bf16[128,256]{1,0:T(8,128)(2,1)S(1)}, u32[]{:S(2)}, u32[]{:S(2)}) collective-permute-start(bf16[128,256]{1,0:T(8,128)(2,1)S(1)} %get-tuple-element.21), channel_id=1, source_target_pairs={{0,8},{4,12},{8,0},{12,4},{1,9},{5,13},{9,1},{13,5},{2,10},{6,14},... | collective-permute-start | bytes 196616 | tf_op jit(solution)/shard_map/ppermute | solution.py:236
  8.9 0.0 collective-permute-start.2
  8.9 0.9 %collective-permute-start.7 = (bf16[1,2,128,384]{3,2,1,0:T(8,128)(2,1)S(1)}, bf16[1,2,128,384]{3,2,1,0:T(8,128)(2,1)S(1)}, u32[]{:S(2)}, u32[]{:S(2)}) collective-permute-start(bf16[1,2,128,384]{3,2,1,0:T(8,128)(2,1)S(1)} %get-tuple-element.24), channel_id=1, source_target_pairs={{0,4},{4,0},{8,12},{12,8},{1,5},{5,1},{9,13},{13,9},{2,6},{6,2},{1... | collective-permute-start | bytes 589832 | tf_op jit(solution)/shard_map/ppermute | solution.py:276
  9.8 0.0 collective-permute-done.refs_1_
  9.8 3.8 %collective-permute-done.1.refs_2_ = bf16[128,256]{1,0:T(8,128)(2,1)S(1)} collective-permute-done((bf16[128,256]{1,0:T(8,128)(2,1)S(1)}, bf16[128,256]{1,0:T(8,128)(2,1)S(1)}, u32[]{:S(2)}, u32[]{:S(2)}) %collective-permute-start.1) | collective-permute-done | bytes 65568 | tf_op jit(solution)/shard_map/ppermute | solution.py:236
  13.6 2.1 %collective-permute-done.2.refs_3_ = bf16[128,256]{1,0:T(8,128)(2,1)S(1)} collective-permute-done((bf16[128,256]{1,0:T(8,128)(2,1)S(1)}, bf16[128,256]{1,0:T(8,128)(2,1)S(1)}, u32[]{:S(2)}, u32[]{:S(2)}) %collective-permute-start.2) | collective-permute-done | bytes 65568 | tf_op jit(solution)/shard_map/ppermute | solution.py:236
  15.7 0.0 copy-done.4
  15.7 0.0 copy-done.3
  15.7 0.6 %codes.1.refs_0_.refs_1_ = bf16[2,64,256]{2,1,0:T(8,128)(2,1)S(1)} custom-call(s32[2,8]{1,0:T(2,128)S(1)} %copy-done.4, f32[4,128]{1,0:T(4,128)S(1)} %bitcast.2, bf16[128,256]{1,0:T(8,128)(2,1)S(1)} %get-tuple-element.19.refs_0_, bf16[128,256]{1,0:T(8,128)(2,1)S(1)} %collective-permute-done.refs_1_, bf16[128,256]{1,0:T(8,128)(2,1)S(1)} %collective-permute-done.1.refs_2_, ...), custom_call_target="tpu_custom_call" | custom-call | flops 20000000000 | tf_op jit(solution)/shard_map/codes/pallas_call | solution.py:237
  16.4 0.1 collective-permute-start.3
  16.4 1.6 %collective-permute-start.4 = (bf16[2,64,256]{2,1,0:T(8,128)(2,1)S(1)}, bf16[2,64,256]{2,1,0:T(8,128)(2,1)S(1)}, u32[]{:S(2)}, u32[]{:S(2)}) collective-permute-start(bf16[2,64,256]{2,1,0:T(8,128)(2,1)S(1)} %codes.1.refs_0_.refs_1_), channel_id=1, source_target_pairs={{0,2},{1,3},{2,0},{3,1},{4,6},{5,7},{6,4},{7,5},{8,10},{9,11},{10,... | collective-permute-start | bytes 196616 | tf_op jit(solution)/shard_map/ppermute | solution.py:252
  18.0 0.3 collective-permute-start.5
  18.3 0.0 copy-start
  18.3 0.0 collective-permute-start.6
  18.3 0.0 collective-permute-done.7.refs_0_
  18.3 1.6 %collective-permute-start.8 = (bf16[1,2,128,384]{3,2,1,0:T(8,128)(2,1)S(1)}, bf16[1,2,128,384]{3,2,1,0:T(8,128)(2,1)S(1)}, u32[]{:S(2)}, u32[]{:S(2)}) collective-permute-start(bf16[1,2,128,384]{3,2,1,0:T(8,128)(2,1)S(1)} %collective-permute-done.7.refs_0_), channel_id=1, source_target_pairs={{0,16},{16,0},{1,17},{17,1},{2,18},{18,2},{3,19},{19,3},{4,20},{20... | collective-permute-start | bytes 589832 | tf_op jit(solution)/shard_map/ppermute | solution.py:277
  19.9 0.0 collective-permute-done.3.refs_1_
  19.9 1.1 %collective-permute-done.4.refs_2_ = bf16[2,64,256]{2,1,0:T(8,128)(2,1)S(1)} collective-permute-done((bf16[2,64,256]{2,1,0:T(8,128)(2,1)S(1)}, bf16[2,64,256]{2,1,0:T(8,128)(2,1)S(1)}, u32[]{:S(2)}, u32[]{:S(2)}) %collective-permute-start.4) | collective-permute-done | bytes 65568 | tf_op jit(solution)/shard_map/ppermute | solution.py:252
  20.9 1.1 %collective-permute-done.5.refs_3_ = bf16[2,64,256]{2,1,0:T(8,128)(2,1)S(1)} collective-permute-done((bf16[2,64,256]{2,1,0:T(8,128)(2,1)S(1)}, bf16[2,64,256]{2,1,0:T(8,128)(2,1)S(1)}, u32[]{:S(2)}, u32[]{:S(2)}) %collective-permute-start.5) | collective-permute-done | bytes 65568 | tf_op jit(solution)/shard_map/ppermute | solution.py:252
  22.1 3.4 %collective-permute-done.8.refs_1_ = bf16[1,2,128,384]{3,2,1,0:T(8,128)(2,1)S(1)} collective-permute-done((bf16[1,2,128,384]{3,2,1,0:T(8,128)(2,1)S(1)}, bf16[1,2,128,384]{3,2,1,0:T(8,128)(2,1)S(1)}, u32[]{:S(2)}, u32[]{:S(2)}) %collective-permute-start.8) | collective-permute-done | bytes 196640 | tf_op jit(solution)/shard_map/ppermute | solution.py:277
  25.5 0.0 copy-done
  25.5 0.4 decode.2
  26.0 0.0 copy-start.1
  26.0 0.0 copy-start.2
  26.0 1.7 %collective-permute-start.12 = (bf16[2,64,384]{2,1,0:T(8,128)(2,1)S(1)}, bf16[2,64,384]{2,1,0:T(8,128)(2,1)S(1)}, u32[]{:S(2)}, u32[]{:S(2)}) collective-permute-start(bf16[2,64,384]{2,1,0:T(8,128)(2,1)S(1)} %get-tuple-element.30), channel_id=1, source_target_pairs={{0,8},{1,9},{4,12},{5,13},{8,0},{9,1},{12,4},{13,5},{2,10},{3,11},... | collective-permute-start | bytes 294920 | tf_op jit(solution)/shard_map/ppermute | solution.py:321
  27.6 0.0 collective-permute-start.13
  27.7 1.4 %collective-permute-start.14 = (bf16[2,64,384]{2,1,0:T(8,128)(2,1)S(1)}, bf16[2,64,384]{2,1,0:T(8,128)(2,1)S(1)}, u32[]{:S(2)}, u32[]{:S(2)}) collective-permute-start(bf16[2,64,384]{2,1,0:T(8,128)(2,1)S(1)} %get-tuple-element.32), channel_id=1, source_target_pairs={{0,9},{1,8},{4,13},{5,12},{8,1},{9,0},{12,5},{13,4},{2,11},{3,10},... | collective-permute-start | bytes 294920 | tf_op jit(solution)/shard_map/ppermute | solution.py:321
  29.1 10.4 %collective-permute-done.6.refs_0_ = bf16[2,2,128,640]{3,2,1,0:T(8,128)(2,1)S(1)} collective-permute-done((bf16[2,2,128,640]{3,2,1,0:T(8,128)(2,1)S(1)}, bf16[2,2,128,640]{3,2,1,0:T(8,128)(2,1)S(1)}, u32[]{:S(2)}, u32[]{:S(2)}) %collective-permute-start.6) | collective-permute-done | bytes 655392 | tf_op jit(solution)/shard_map/ppermute | solution.py:279
  39.5 0.6 %decode.3 = (f32[2,64,640]{2,1,0:T(8,128)S(1)}, bf16[2,64,640]{2,1,0:T(8,128)(2,1)S(1)}, bf16[2,64,640]{2,1,0:T(8,128)(2,1)S(1)}, bf16[2,64,640]{2,1,0:T(8,128)(2,1)S(1)}) custom-call(bf16[2,2,128,2048]{3,2,1,0:T(8,128)(2,1)S(1)} %copy-done, bf16[256,512]{1,0:T(8,128)(2,1)S(1)} %gather.1.lhs_ref, ...), custom_call_target="tpu_custom_call" | custom-call | tf_op jit(solution)/shard_map/decode/pallas_call | solution.py:301
  40.1 0.1 collective-permute-start.9
  40.2 0.1 collective-permute-start.10
  40.2 0.0 collective-permute-done.12.refs_1_
  40.2 2.9 %collective-permute-start.11 = (bf16[2,64,640]{2,1,0:T(8,128)(2,1)S(1)}, bf16[2,64,640]{2,1,0:T(8,128)(2,1)S(1)}, u32[]{:S(2)}, u32[]{:S(2)}) collective-permute-start(bf16[2,64,640]{2,1,0:T(8,128)(2,1)S(1)} %get-tuple-element.29), channel_id=1, source_target_pairs={{0,9},{1,8},{4,13},{5,12},{8,1},{9,0},{12,5},{13,4},{2,11},{3,10},... | collective-permute-start | bytes 491528 | tf_op jit(solution)/shard_map/ppermute | solution.py:321
  43.2 0.0 collective-permute-done.13.refs_2_
  43.2 0.0 collective-permute-done.14.refs_3_
  43.2 0.0 copy-done.1
  43.2 0.0 copy-done.2
  43.2 0.7 %add.2.refs_4_ = bf16[2,64,2048]{2,1,0:T(8,128)(2,1)} custom-call(f32[2,2048]{1,0:T(2,128)S(1)} %copy-done.2, bf16[2,64,2048]{2,1,0:T(8,128)(2,1)S(1)} %copy-done.1, f32[2,64,384]{2,1,0:T(8,128)S(1)} %get-tuple-element.25.refs_1_.refs_0_, bf16[2,64,384]{2,1,0:T(8,128)(2,1)S(1)} %collective-permute-done.12.refs_1_, ...), custom_call_target="tpu_custom_call" | custom-call | flops 20000000000 | tf_op jit(solution)/shard_map/add/pallas_call | solution.py:282
  44.0 8.8 %collective-permute-done.9.refs_1_ = bf16[2,64,640]{2,1,0:T(8,128)(2,1)S(1)} collective-permute-done((bf16[2,64,640]{2,1,0:T(8,128)(2,1)S(1)}, bf16[2,64,640]{2,1,0:T(8,128)(2,1)S(1)}, u32[]{:S(2)}, u32[]{:S(2)}) %collective-permute-start.9) | collective-permute-done | bytes 163872 | tf_op jit(solution)/shard_map/ppermute | solution.py:321
  52.8 0.0 collective-permute-done.10.refs_2_
  52.8 3.3 %collective-permute-done.11.refs_3_ = bf16[2,64,640]{2,1,0:T(8,128)(2,1)S(1)} collective-permute-done((bf16[2,64,640]{2,1,0:T(8,128)(2,1)S(1)}, bf16[2,64,640]{2,1,0:T(8,128)(2,1)S(1)}, u32[]{:S(2)}, u32[]{:S(2)}) %collective-permute-start.11) | collective-permute-done | bytes 163872 | tf_op jit(solution)/shard_map/ppermute | solution.py:321
  56.1 0.8 %add.3 = bf16[2,64,2048]{2,1,0:T(8,128)(2,1)} custom-call(f32[2,2048]{1,0:T(2,128)S(1)} %copy-done.2, bf16[2,64,2048]{2,1,0:T(8,128)(2,1)S(1)} %copy-done.1, f32[2,64,640]{2,1,0:T(8,128)S(1)} %get-tuple-element.26.refs_0_, bf16[2,64,640]{2,1,0:T(8,128)(2,1)S(1)} %collective-permute-done.9.refs_1_, ...), custom_call_target="tpu_custom_call", output_to_operand_aliasing={{}: (6, {})} | custom-call | tf_op jit(solution)/shard_map/add/pallas_call | solution.py:282
  (2 shorter events, 0.0 us)
Async XLA Ops:
  0.0 15.7 %copy-start.4 = (s32[2,8]{1,0:T(2,128)S(1)}, s32[2,8]{1,0:T(2,128)}, u32[]{:S(2)}) copy-start(s32[2,8]{1,0:T(2,128)} %active_ref.1) | copy-start | bytes 196
  0.0 15.7 %copy-start.3 = (f32[512]{0:T(512)S(1)}, f32[512]{0:T(512)}, u32[]{:S(2)}) copy-start(f32[512]{0:T(512)} %param.9) | copy-start | bytes 6148
  3.2 6.6 %collective-permute-start = (bf16[128,256]{1,0:T(8,128)(2,1)S(1)}, bf16[128,256]{1,0:T(8,128)(2,1)S(1)}, u32[]{:S(2)}, u32[]{:S(2)}) collective-permute-start(bf16[128,256]{1,0:T(8,128)(2,1)S(1)} %get-tuple-element.20), channel_id=1, source_target_pairs={{0,4},{4,0},{8,12},{12,8},{1,5},{5,1},{9,13},{13,9},{2,6},{6,2},{1... | collective-permute-start | bytes 196616 | tf_op jit(solution)/shard_map/ppermute | solution.py:236
  6.3 7.3 %collective-permute-start.1 = (bf16[128,256]{1,0:T(8,128)(2,1)S(1)}, bf16[128,256]{1,0:T(8,128)(2,1)S(1)}, u32[]{:S(2)}, u32[]{:S(2)}) collective-permute-start(bf16[128,256]{1,0:T(8,128)(2,1)S(1)} %get-tuple-element.21), channel_id=1, source_target_pairs={{0,8},{4,12},{8,0},{12,4},{1,9},{5,13},{9,1},{13,5},{2,10},{6,14},... | collective-permute-start | bytes 196616 | tf_op jit(solution)/shard_map/ppermute | solution.py:236
  8.9 6.8 %collective-permute-start.2 = (bf16[128,256]{1,0:T(8,128)(2,1)S(1)}, bf16[128,256]{1,0:T(8,128)(2,1)S(1)}, u32[]{:S(2)}, u32[]{:S(2)}) collective-permute-start(bf16[128,256]{1,0:T(8,128)(2,1)S(1)} %get-tuple-element.22), channel_id=1, source_target_pairs={{0,12},{4,8},{8,4},{12,0},{1,13},{5,9},{9,5},{13,1},{2,14},{6,10},... | collective-permute-start | bytes 196616 | tf_op jit(solution)/shard_map/ppermute | solution.py:236
  8.9 9.4 %collective-permute-start.7 = (bf16[1,2,128,384]{3,2,1,0:T(8,128)(2,1)S(1)}, bf16[1,2,128,384]{3,2,1,0:T(8,128)(2,1)S(1)}, u32[]{:S(2)}, u32[]{:S(2)}) collective-permute-start(bf16[1,2,128,384]{3,2,1,0:T(8,128)(2,1)S(1)} %get-tuple-element.24), channel_id=1, source_target_pairs={{0,4},{4,0},{8,12},{12,8},{1,5},{5,1},{9,13},{13,9},{2,6},{6,2},{1... | collective-permute-start | bytes 589832 | tf_op jit(solution)/shard_map/ppermute | solution.py:276
  16.4 3.5 %collective-permute-start.3 = (bf16[2,64,256]{2,1,0:T(8,128)(2,1)S(1)}, bf16[2,64,256]{2,1,0:T(8,128)(2,1)S(1)}, u32[]{:S(2)}, u32[]{:S(2)}) collective-permute-start(bf16[2,64,256]{2,1,0:T(8,128)(2,1)S(1)} %codes.1.refs_0_.refs_1_), channel_id=1, source_target_pairs={{0,1},{1,0},{2,3},{3,2},{4,5},{5,4},{6,7},{7,6},{8,9},{9,8},{10,11... | collective-permute-start | bytes 196616 | tf_op jit(solution)/shard_map/ppermute | solution.py:252
  16.4 4.5 %collective-permute-start.4 = (bf16[2,64,256]{2,1,0:T(8,128)(2,1)S(1)}, bf16[2,64,256]{2,1,0:T(8,128)(2,1)S(1)}, u32[]{:S(2)}, u32[]{:S(2)}) collective-permute-start(bf16[2,64,256]{2,1,0:T(8,128)(2,1)S(1)} %codes.1.refs_0_.refs_1_), channel_id=1, source_target_pairs={{0,2},{1,3},{2,0},{3,1},{4,6},{5,7},{6,4},{7,5},{8,10},{9,11},{10,... | collective-permute-start | bytes 196616 | tf_op jit(solution)/shard_map/ppermute | solution.py:252
  18.0 4.0 %collective-permute-start.5 = (bf16[2,64,256]{2,1,0:T(8,128)(2,1)S(1)}, bf16[2,64,256]{2,1,0:T(8,128)(2,1)S(1)}, u32[]{:S(2)}, u32[]{:S(2)}) collective-permute-start(bf16[2,64,256]{2,1,0:T(8,128)(2,1)S(1)} %codes.1.refs_0_.refs_1_), channel_id=1, source_target_pairs={{0,3},{1,2},{2,1},{3,0},{4,7},{5,6},{6,5},{7,4},{8,11},{9,10},{10,... | collective-permute-start | bytes 196616 | tf_op jit(solution)/shard_map/ppermute | solution.py:252
  18.3 7.2 %copy-start = (bf16[2,2,128,2048]{3,2,1,0:T(8,128)(2,1)S(1)}, bf16[2,2,128,2048]{3,2,1,0:T(8,128)(2,1)}, u32[]{:S(2)}) copy-start(bf16[2,2,128,2048]{3,2,1,0:T(8,128)(2,1)} %dec_ref.3) | copy-start | bytes 6291460
  18.3 21.2 %collective-permute-start.6 = (bf16[2,2,128,640]{3,2,1,0:T(8,128)(2,1)S(1)}, bf16[2,2,128,640]{3,2,1,0:T(8,128)(2,1)S(1)}, u32[]{:S(2)}, u32[]{:S(2)}) collective-permute-start(bf16[2,2,128,640]{3,2,1,0:T(8,128)(2,1)S(1)} %hold.1), channel_id=1, source_target_pairs={{0,4},{4,0},{8,12},{12,8},{1,5},{5,1},{9,13},{13,9},{2,6},{6,2},{1... | collective-permute-start | bytes 1966088 | tf_op jit(solution)/shard_map/ppermute | solution.py:279
  18.3 7.2 %collective-permute-start.8 = (bf16[1,2,128,384]{3,2,1,0:T(8,128)(2,1)S(1)}, bf16[1,2,128,384]{3,2,1,0:T(8,128)(2,1)S(1)}, u32[]{:S(2)}, u32[]{:S(2)}) collective-permute-start(bf16[1,2,128,384]{3,2,1,0:T(8,128)(2,1)S(1)} %collective-permute-done.7.refs_0_), channel_id=1, source_target_pairs={{0,16},{16,0},{1,17},{17,1},{2,18},{18,2},{3,19},{19,3},{4,20},{20... | collective-permute-start | bytes 589832 | tf_op jit(solution)/shard_map/ppermute | solution.py:277
  26.0 17.2 %copy-start.1 = (bf16[2,64,2048]{2,1,0:T(8,128)(2,1)S(1)}, bf16[2,64,2048]{2,1,0:T(8,128)(2,1)}, u32[]{:S(2)}) copy-start(bf16[2,64,2048]{2,1,0:T(8,128)(2,1)} %target_ref.3) | copy-start | bytes 1572868
  26.0 17.2 %copy-start.2 = (f32[2,2048]{1,0:T(2,128)S(1)}, f32[2,2048]{1,0:T(2,128)}, u32[]{:S(2)}) copy-start(f32[2,2048]{1,0:T(2,128)} %bias_ref.3) | copy-start | bytes 49156
  26.0 14.3 %collective-permute-start.12 = (bf16[2,64,384]{2,1,0:T(8,128)(2,1)S(1)}, bf16[2,64,384]{2,1,0:T(8,128)(2,1)S(1)}, u32[]{:S(2)}, u32[]{:S(2)}) collective-permute-start(bf16[2,64,384]{2,1,0:T(8,128)(2,1)S(1)} %get-tuple-element.30), channel_id=1, source_target_pairs={{0,8},{1,9},{4,12},{5,13},{8,0},{9,1},{12,4},{13,5},{2,10},{3,11},... | collective-permute-start | bytes 294920 | tf_op jit(solution)/shard_map/ppermute | solution.py:321
  27.6 15.5 %collective-permute-start.13 = (bf16[2,64,384]{2,1,0:T(8,128)(2,1)S(1)}, bf16[2,64,384]{2,1,0:T(8,128)(2,1)S(1)}, u32[]{:S(2)}, u32[]{:S(2)}) collective-permute-start(bf16[2,64,384]{2,1,0:T(8,128)(2,1)S(1)} %get-tuple-element.31), channel_id=1, source_target_pairs={{0,1},{1,0},{4,5},{5,4},{8,9},{9,8},{12,13},{13,12},{2,3},{3,2},{6... | collective-permute-start | bytes 294920 | tf_op jit(solution)/shard_map/ppermute | solution.py:321
  27.7 15.5 %collective-permute-start.14 = (bf16[2,64,384]{2,1,0:T(8,128)(2,1)S(1)}, bf16[2,64,384]{2,1,0:T(8,128)(2,1)S(1)}, u32[]{:S(2)}, u32[]{:S(2)}) collective-permute-start(bf16[2,64,384]{2,1,0:T(8,128)(2,1)S(1)} %get-tuple-element.32), channel_id=1, source_target_pairs={{0,9},{1,8},{4,13},{5,12},{8,1},{9,0},{12,5},{13,4},{2,11},{3,10},... | collective-permute-start | bytes 294920 | tf_op jit(solution)/shard_map/ppermute | solution.py:321
  40.1 12.7 %collective-permute-start.9 = (bf16[2,64,640]{2,1,0:T(8,128)(2,1)S(1)}, bf16[2,64,640]{2,1,0:T(8,128)(2,1)S(1)}, u32[]{:S(2)}, u32[]{:S(2)}) collective-permute-start(bf16[2,64,640]{2,1,0:T(8,128)(2,1)S(1)} %get-tuple-element.27), channel_id=1, source_target_pairs={{0,8},{1,9},{4,12},{5,13},{8,0},{9,1},{12,4},{13,5},{2,10},{3,11},... | collective-permute-start | bytes 491528 | tf_op jit(solution)/shard_map/ppermute | solution.py:321
  40.2 12.6 %collective-permute-start.10 = (bf16[2,64,640]{2,1,0:T(8,128)(2,1)S(1)}, bf16[2,64,640]{2,1,0:T(8,128)(2,1)S(1)}, u32[]{:S(2)}, u32[]{:S(2)}) collective-permute-start(bf16[2,64,640]{2,1,0:T(8,128)(2,1)S(1)} %get-tuple-element.28), channel_id=1, source_target_pairs={{0,1},{1,0},{4,5},{5,4},{8,9},{9,8},{12,13},{13,12},{2,3},{3,2},{6... | collective-permute-start | bytes 491528 | tf_op jit(solution)/shard_map/ppermute | solution.py:321
  40.2 15.9 %collective-permute-start.11 = (bf16[2,64,640]{2,1,0:T(8,128)(2,1)S(1)}, bf16[2,64,640]{2,1,0:T(8,128)(2,1)S(1)}, u32[]{:S(2)}, u32[]{:S(2)}) collective-permute-start(bf16[2,64,640]{2,1,0:T(8,128)(2,1)S(1)} %get-tuple-element.29), channel_id=1, source_target_pairs={{0,9},{1,8},{4,13},{5,12},{8,1},{9,0},{12,5},{13,4},{2,11},{3,10},... | collective-permute-start | bytes 491528 | tf_op jit(solution)/shard_map/ppermute | solution.py:321

commit v14 on v13

--- a/solution.py
+++ b/solution.py
@@ -9,18 +9,20 @@
 
 VMEM_BYTES = 32 * 1024 * 1024
 LANES = 128
-SHARES = (3, 5)
-
-
-def cut_pieces(layers, columns):
-    tiles = columns // LANES
-    pieces, start = [], 0
-    for i, eighths in enumerate(SHARES):
-        stop = tiles if i + 1 == len(SHARES) else min(tiles, start + -(-tiles * eighths // 8))
-        if stop > start:
-            pieces.append((tuple(range(layers)), start * LANES, (stop - start) * LANES))
-        start = stop
-    return pieces
+PIECES = (((0,), 0, False), ((1,), 0, True), ((0, 1), 1, False))
+
+
+def cut_pieces(columns):
+    middle = -(-(columns // LANES) // 2) * LANES
+    bounds = ((0, middle), (middle, columns))
+    return [
+        (layers, bounds[side][0], bounds[side][1] - bounds[side][0], across)
+        for layers, side, across in PIECES
+    ]
+
+
+def layer_of(offset, layers):
+    return lax.rem(lax.axis_index("parts") + offset, layers)
 
 
 def peer(index, k, n):
@@ -28,13 +30,13 @@
 
 
 def part_copies(piece, dec_hbm, part_ref, sems):
-    layers, first, width = piece
-    groups, cols = dec_hbm.shape[1], dec_hbm.shape[3]
+    offsets, first, width, _ = piece
+    layers, groups, _, cols = dec_hbm.shape
     start = pl.multiple_of(lax.axis_index("rep") * (cols // 2) + first, LANES)
     copies = []
-    for i, layer in enumerate(layers):
+    for i, offset in enumerate(offsets):
         for group in range(groups):
-            source = dec_hbm.at[layer, group, :, pl.ds(start, width)]
+            source = dec_hbm.at[layer_of(offset, layers), group, :, pl.ds(start, width)]
             sem = sems.at[i * groups + group]
             copies.append(pltpu.make_async_copy(source, part_ref.at[i, group], sem))
             copies[-1].start()
@@ -64,8 +66,6 @@
         copy.wait()
     copies_part = []
     for i, piece in enumerate(pieces):
-        if i == 0:
-            piece = ((lax.axis_index("parts"),), *piece[1:])
         copies_part += part_copies(piece, dec_hbm, part_refs[i], part_sems.at[i])
     src = lax.axis_index("src")
     for k in range(n):
@@ -136,45 +136,45 @@
                     out_ref[rows, columns] = code_refs[2 * k + r][group, :, latents]
 
 
-def decode_kernel(n, piece, shared, dec_ref, lhs_ref, *refs):
+def decode_kernel(n, piece, dec_ref, lhs_ref, got_ref, *refs):
+    offsets, first, width, _ = piece
     layers, groups, block, cols = dec_ref.shape
-    _, first, width = piece
-    got_refs, out_refs = refs[: 1 + shared], refs[-2 * (n // 2) :]
+    out_refs = refs[-2 * (n // 2) :]
     depth = groups * block
     share = lhs_ref.shape[0] // len(out_refs)
     start = pl.multiple_of(lax.axis_index("rep") * (cols // 2) + first, LANES)
-    for i in range(layers):
-        layer = lax.rem(lax.axis_index("parts") + i, layers) if shared else i
-        own = dec_ref[layer, :, :, pl.ds(start, width)].reshape(depth, width)
-        got = (got_refs[i][0] if shared else got_refs[0][i]).reshape(depth, width)
+    for i, offset in enumerate(offsets):
+        own = dec_ref[layer_of(offset, layers), :, :, pl.ds(start, width)].reshape(depth, width)
+        got = got_ref[i].reshape(depth, width)
         total = jnp.dot(lhs_ref[:, :depth], own, preferred_element_type=jnp.float32)
         total += jnp.dot(lhs_ref[:, depth:], got, preferred_element_type=jnp.float32)
         for j, ref in enumerate(out_refs):
-            ref[layer] = total[j * share : (j + 1) * share].astype(ref.dtype)
+            ref[i] = total[j * share : (j + 1) * share].astype(ref.dtype)
 
 
 def add_kernel(n, pieces, bias_ref, target_ref, *refs):
     out_hbm, out_ref, sems = refs[-3:]
     half = n // 2
-    cols = target_ref.shape[2]
+    layers, _, cols = target_ref.shape
     rep = lax.axis_index("rep")
     copies = []
-    for i, (layers, first, width) in enumerate(pieces):
+    for i, (offsets, first, width, _) in enumerate(pieces):
         for side in range(2):
             core = rep if side == 0 else 1 - rep
             columns = pl.ds(pl.multiple_of(core * (cols // 2) + first, LANES), width)
-            mine = refs[(2 * i + side) * half : (2 * i + side + 1) * half]
-            for j, layer in enumerate(layers):
-                total = bias_ref[layer : layer + 1, columns]
+            for j, offset in enumerate(offsets):
+                layer = layer_of(offset, layers)
+                total = bias_ref[0:1, columns]
+                for other in range(1, layers):
+                    total = jnp.where(layer == other, bias_ref[other : other + 1, columns], total)
                 total = total - target_ref[layer, :, columns].astype(jnp.float32)
-                for ref in mine:
+                for ref in refs[(2 * i + side) * half : (2 * i + side + 1) * half]:
                     total = total + ref[j].astype(jnp.float32)
-                out_ref[layer, :, columns] = total.astype(jnp.bfloat16)
+                place = len(copies)
+                out_ref[place, :, :width] = total.astype(jnp.bfloat16)
                 copies.append(
                     pltpu.make_async_copy(
-                        out_ref.at[layer, :, columns],
-                        out_hbm.at[layer, :, columns],
-                        sems.at[len(copies)],
+                        out_ref.at[place, :, :width], out_hbm.at[layer, :, columns], sems.at[place]
                     )
                 )
                 copies[-1].start()
@@ -188,7 +188,8 @@
     layers, groups, block, cols = dec_w.shape
     share = rows // n
     half = n // 2
-    pieces = cut_pieces(layers, cols // 2)
+    pieces = cut_pieces(cols // 2)
+    fetched = [piece for piece in pieces if not piece[3]]
     tile_rows = rows // active.shape[0]
     pair = [(i, i ^ 1) for i in range(n)]
     params = pltpu.CompilerParams(vmem_limit_bytes=VMEM_BYTES)
@@ -212,18 +213,15 @@
         return jax.ShapeDtypeStruct(extent, kind)
 
     results = pl.pallas_call(
-        functools.partial(encode_kernel, n, pieces),
+        functools.partial(encode_kernel, n, fetched),
         out_shape=[shape(half * share, 2 * block)] * n
-        + [
-            shape(1 if i == 0 else layers, groups, block, width)
-            for i, (_, _, width) in enumerate(pieces)
-        ],
+        + [shape(len(offsets), groups, block, width) for offsets, _, width, _ in fetched],
         in_specs=[anywhere] * 3,
-        out_specs=[vmem] * (n + len(pieces)),
+        out_specs=[vmem] * (n + len(fetched)),
         scratch_shapes=[
             pltpu.VMEM((2, half, share, features), jnp.bfloat16),
             pltpu.VMEM(enc_w.shape, jnp.bfloat16),
-            pltpu.SemaphoreType.DMA((len(pieces), layers * groups)),
+            pltpu.SemaphoreType.DMA((len(fetched), layers * groups)),
             pltpu.SemaphoreType.DMA((2 * half,)),
             pltpu.SemaphoreType.DMA((8,)),
         ],
@@ -273,20 +271,22 @@
             name="hold",
         )(value, after)
 
-    got = [[lax.ppermute(parts[0], "src", pair)]]
-    got[0].append(lax.ppermute(got[0][0], "parts", [(0, 1), (1, 0)]))
-    if len(pieces) > 1:
-        got.append([lax.ppermute(hold(parts[1], own), "src", pair)])
+    got = [lax.ppermute(parts[0], "src", pair)]
+    got.append(lax.ppermute(got[0], "parts", [(0, 1), (1, 0)]))
+    got.append(lax.ppermute(hold(parts[1], own), "src", pair))
+
     def add(some, begun, billions):
         operands = [value for i in some for value in sums[i]]
+        count = 2 * sum(len(pieces[i][0]) for i in some)
+        widest = max(piece[2] for piece in pieces)
         return pl.pallas_call(
             functools.partial(add_kernel, n, [pieces[i] for i in some]),
             out_shape=shape(layers, share, cols),
             in_specs=[vmem] * (2 + len(operands)) + [anywhere] * len(begun),
             out_specs=anywhere,
             scratch_shapes=[
-                pltpu.VMEM((layers, share, cols), jnp.bfloat16),
-                pltpu.SemaphoreType.DMA((2 * len(some) * layers,)),
+                pltpu.VMEM((count, share, widest), jnp.bfloat16),
+                pltpu.SemaphoreType.DMA((count,)),
             ],
             input_output_aliases={2 + len(operands): 0} if begun else {},
             compiler_params=params,
@@ -294,35 +294,35 @@
             name="add",
         )(dec_b, targets, *operands, *begun)
 
-    sums, after, begun = [], [], []
-    for i, (_, _, width) in enumerate(pieces):
-        shapes = [shape(layers, share, width)] * (2 * half)
-        shapes[0] = shape(layers, share, width, kind=jnp.float32)
+    sums, after = [], []
+    for i, piece in enumerate(pieces):
+        offsets, _, width, _ = piece
+        shapes = [shape(len(offsets), share, width)] * (2 * half)
+        shapes[0] = shape(len(offsets), share, width, kind=jnp.float32)
         terms = pl.pallas_call(
-            functools.partial(decode_kernel, n, pieces[i], i == 0),
+            functools.partial(decode_kernel, n, piece),
             out_shape=shapes,
-            in_specs=[vmem] * (2 + len(got[i])) + [anywhere] * len(after),
+            in_specs=[vmem] * 3 + [anywhere] * len(after),
             out_specs=[vmem] * len(shapes),
             compiler_params=params,
             cost_estimate=weight(0),
             name="decode",
-        )(dec_rows, lhs, *got[i], *after)
+        )(dec_rows, lhs, got[i], *after)
         after = [terms[0]]
-        if i == 0:
-            for part in parts[2:]:
-                got.append([lax.ppermute(hold(part, own), "src", pair)])
-        sums.append([])
-        for r in range(2):
-            for j in range(half):
+        sums.append([None] * (2 * half))
+        for j in [*range(1, half), 0]:
+            for r in range(2):
                 perm = [
                     (d * 2 + c, (d + 2 * j) % n * 2 + (c ^ r)) for d in range(n) for c in range(2)
                 ]
                 term = terms[2 * j + r]
-                sums[i].append(lax.ppermute(term, ("src", "rep"), perm) if j + r else term)
-
-    for i in range(len(pieces) - 1):
-        begun = [add([i], begun, 20)]
-    return add([len(pieces) - 1], begun, 0)
+                sums[i][r * half + j] = (
+                    lax.ppermute(term, ("src", "rep"), perm) if j + r else term
+                )
+
+    begun = []
+    begun = [add([0, 1], begun, 20)]
+    return add([2], begun, 0)
 
 
 def solution(mesh):

time: 57.1 us -> 54.4 us (0.953)
  waiting for transfers between devices: 34.1 us -> 29.7 us
  starting transfers between devices: 16.3 us -> 17.9 us
    ppermute x9 -> x12, waiting for transfers between devices: 26 us -> 21.6 us  [the longest x9 15.7 us: body(): lax.ppermute(term, ('src', 'rep'), perm)]
    ppermute x9 -> x12, starting transfers between devices: 8.67 us -> 10.3 us  [the longest x9 7.88 us: body(): lax.ppermute(term, ('src', 'rep'), perm)]
    pallas_call x3 -> x4, Pallas kernels: 4.2 us -> 4.2 us  [the longest x1 3.18 us: body(): pl.pallas_call(functools.partial(encode_kernel, n, fetched), out_shape=[s...]
  transfers between devices with their start and end apart: 15 -> 18, of which waited for: 8 -> 11; matrix products, arithmetic and copies ran while one was open for 0% -> 0% of each run, Pallas kernels for 4% -> 5%
where the time goes in v14:
time: 54.4 us; the launch traced here: 54.2 us
  waiting for transfers between devices  29.7 us (55%)
  starting transfers between devices  17.9 us (33%)
  Pallas kernels  6.45 us (12%)
    ppermute x9, waiting for transfers between devices, body(): lax.ppermute(term, ('src', 'rep'), perm)  15.7 us
    ppermute x9, starting transfers between devices, body(): lax.ppermute(term, ('src', 'rep'), perm)  7.88 us
    ppermute x3, waiting for transfers between devices, body(): lax.ppermute(terms[k], 'src', [(i, peer(i, k, n)) for i in range(n)])  5.92 us
    ppermute x3, starting transfers between devices, body(): lax.ppermute(terms[k], 'src', [(i, peer(i, k, n)) for i in range(n)])  5.68 us
    ppermute x1, waiting for transfers between devices, body(): got.append(lax.ppermute(hold(parts[1], own), 'src', pair))  4.61 us
    pallas_call x1, Pallas kernels, body(): pl.pallas_call(functools.partial(encode_kernel, n, fetched), out_shape=[s...  3.18 us
    ppermute x3, waiting for transfers between devices, body(): codes.append(lax.ppermute(own, ('tgt', 'rep'), perm) if k + r else own)  2.22 us
    ppermute x3, starting transfers between devices, body(): codes.append(lax.ppermute(own, ('tgt', 'rep'), perm) if k + r else own)  1.92 us
  transfers between devices with their start and end apart: 18, of which 11 were waited for; matrix products, arithmetic and copies ran while one was open for 0% of the time, Pallas kernels for 5%

profile of v14, /device:TPU:0, one launch (start us, length us, event | category | flops | bytes accessed | tf_op | source)
XLA Modules:
  0.0 54.2 jit_solution(17108676356521829073)
XLA Ops:
  0.0 3.2 %encode.1 = (bf16[128,256]{1,0:T(8,128)(2,1)S(1)}, bf16[128,256]{1,0:T(8,128)(2,1)S(1)}, bf16[128,256]{1,0:T(8,128)(2,1)S(1)}, bf16[128,256]{1,0:T(8,128)(2,1)S(...) custom-call(bf16[2,2,64,1024]{3,2,1,0:T(8,128)(2,1)} %bitcast.3, bf16[1024,512]{1,0:T(8,128)(2,1)} %w_hbm.1, ...), custom_call_target="tpu_custom_call" | custom-call | tf_op jit(solution)/shard_map/encode/pallas_call | solution.py:215
  3.2 3.1 %collective-permute-start = (bf16[128,256]{1,0:T(8,128)(2,1)S(1)}, bf16[128,256]{1,0:T(8,128)(2,1)S(1)}, u32[]{:S(2)}, u32[]{:S(2)}) collective-permute-start(bf16[128,256]{1,0:T(8,128)(2,1)S(1)} %get-tuple-element.24), channel_id=1, source_target_pairs={{0,4},{4,0},{8,12},{12,8},{1,5},{5,1},{9,13},{13,9},{2,6},{6,2},{1... | collective-permute-start | bytes 196616 | tf_op jit(solution)/shard_map/ppermute | solution.py:234
  6.3 2.6 %collective-permute-start.1 = (bf16[128,256]{1,0:T(8,128)(2,1)S(1)}, bf16[128,256]{1,0:T(8,128)(2,1)S(1)}, u32[]{:S(2)}, u32[]{:S(2)}) collective-permute-start(bf16[128,256]{1,0:T(8,128)(2,1)S(1)} %get-tuple-element.25), channel_id=1, source_target_pairs={{0,8},{4,12},{8,0},{12,4},{1,9},{5,13},{9,1},{13,5},{2,10},{6,14},... | collective-permute-start | bytes 196616 | tf_op jit(solution)/shard_map/ppermute | solution.py:234
  8.9 0.0 collective-permute-start.2
  8.9 0.9 %collective-permute-start.7 = (bf16[1,2,128,512]{3,2,1,0:T(8,128)(2,1)S(1)}, bf16[1,2,128,512]{3,2,1,0:T(8,128)(2,1)S(1)}, u32[]{:S(2)}, u32[]{:S(2)}) collective-permute-start(bf16[1,2,128,512]{3,2,1,0:T(8,128)(2,1)S(1)} %get-tuple-element.28), channel_id=1, source_target_pairs={{0,4},{4,0},{8,12},{12,8},{1,5},{5,1},{9,13},{13,9},{2,6},{6,2},{1... | collective-permute-start | bytes 786440 | tf_op jit(solution)/shard_map/ppermute | solution.py:274
  9.8 0.0 collective-permute-done.refs_1_
  9.8 3.8 %collective-permute-done.1.refs_2_ = bf16[128,256]{1,0:T(8,128)(2,1)S(1)} collective-permute-done((bf16[128,256]{1,0:T(8,128)(2,1)S(1)}, bf16[128,256]{1,0:T(8,128)(2,1)S(1)}, u32[]{:S(2)}, u32[]{:S(2)}) %collective-permute-start.1) | collective-permute-done | bytes 65568 | tf_op jit(solution)/shard_map/ppermute | solution.py:234
  13.6 2.1 %collective-permute-done.2.refs_3_ = bf16[128,256]{1,0:T(8,128)(2,1)S(1)} collective-permute-done((bf16[128,256]{1,0:T(8,128)(2,1)S(1)}, bf16[128,256]{1,0:T(8,128)(2,1)S(1)}, u32[]{:S(2)}, u32[]{:S(2)}) %collective-permute-start.2) | collective-permute-done | bytes 65568 | tf_op jit(solution)/shard_map/ppermute | solution.py:234
  15.7 0.0 copy-done.3
  15.7 0.6 %codes.1.refs_0_.refs_1_ = bf16[2,64,256]{2,1,0:T(8,128)(2,1)S(1)} custom-call(s32[2,8]{1,0:T(2,128)S(1)} %copy-done.4, f32[4,128]{1,0:T(4,128)S(1)} %bitcast.2, bf16[128,256]{1,0:T(8,128)(2,1)S(1)} %get-tuple-element.23.refs_0_, bf16[128,256]{1,0:T(8,128)(2,1)S(1)} %collective-permute-done.refs_1_, bf16[128,256]{1,0:T(8,128)(2,1)S(1)} %collective-permute-done.1.refs_2_, ...), custom_call_target="tpu_custom_call" | custom-call | flops 20000000000 | tf_op jit(solution)/shard_map/codes/pallas_call | solution.py:235
  16.3 0.1 collective-permute-start.5
  16.4 1.6 %collective-permute-start.4 = (bf16[2,64,256]{2,1,0:T(8,128)(2,1)S(1)}, bf16[2,64,256]{2,1,0:T(8,128)(2,1)S(1)}, u32[]{:S(2)}, u32[]{:S(2)}) collective-permute-start(bf16[2,64,256]{2,1,0:T(8,128)(2,1)S(1)} %codes.1.refs_0_.refs_1_), channel_id=1, source_target_pairs={{0,2},{1,3},{2,0},{3,1},{4,6},{5,7},{6,4},{7,5},{8,10},{9,11},{10,... | collective-permute-start | bytes 196616 | tf_op jit(solution)/shard_map/ppermute | solution.py:250
  18.0 0.3 collective-permute-start.3
  18.3 0.0 collective-permute-start.6
  18.3 0.2 collective-permute-done.7.got_ref
  18.5 1.5 %collective-permute-start.8 = (bf16[1,2,128,512]{3,2,1,0:T(8,128)(2,1)S(1)}, bf16[1,2,128,512]{3,2,1,0:T(8,128)(2,1)S(1)}, u32[]{:S(2)}, u32[]{:S(2)}) collective-permute-start(bf16[1,2,128,512]{3,2,1,0:T(8,128)(2,1)S(1)} %collective-permute-done.7.got_ref), channel_id=1, source_target_pairs={{0,16},{16,0},{1,17},{17,1},{2,18},{18,2},{3,19},{19,3},{4,20},{20... | collective-permute-start | bytes 786440 | tf_op jit(solution)/shard_map/ppermute | solution.py:275
  20.0 0.8 %collective-permute-done.5.refs_3_ = bf16[2,64,256]{2,1,0:T(8,128)(2,1)S(1)} collective-permute-done((bf16[2,64,256]{2,1,0:T(8,128)(2,1)S(1)}, bf16[2,64,256]{2,1,0:T(8,128)(2,1)S(1)}, u32[]{:S(2)}, u32[]{:S(2)}) %collective-permute-start.5) | collective-permute-done | bytes 65568 | tf_op jit(solution)/shard_map/ppermute | solution.py:250
  20.7 1.4 %collective-permute-done.4.refs_2_ = bf16[2,64,256]{2,1,0:T(8,128)(2,1)S(1)} collective-permute-done((bf16[2,64,256]{2,1,0:T(8,128)(2,1)S(1)}, bf16[2,64,256]{2,1,0:T(8,128)(2,1)S(1)}, u32[]{:S(2)}, u32[]{:S(2)}) %collective-permute-start.4) | collective-permute-done | bytes 65568 | tf_op jit(solution)/shard_map/ppermute | solution.py:250
  22.2 0.0 collective-permute-done.3.refs_1_
  22.3 0.0 copy-done
  22.3 0.3 decode.3
  22.6 0.9 %collective-permute-start.12 = (bf16[1,64,512]{2,1,0:T(8,128)(2,1)S(1)}, bf16[1,64,512]{2,1,0:T(8,128)(2,1)S(1)}, u32[]{:S(2)}, u32[]{:S(2)}) collective-permute-start(bf16[1,64,512]{2,1,0:T(8,128)(2,1)S(1)} %get-tuple-element.35), channel_id=1, source_target_pairs={{0,8},{1,9},{4,12},{5,13},{8,0},{9,1},{12,4},{13,5},{2,10},{3,11},... | collective-permute-start | bytes 196616 | tf_op jit(solution)/shard_map/ppermute | solution.py:320
  23.5 0.0 collective-permute-start.13
  23.5 2.2 %collective-permute-start.14 = (bf16[1,64,512]{2,1,0:T(8,128)(2,1)S(1)}, bf16[1,64,512]{2,1,0:T(8,128)(2,1)S(1)}, u32[]{:S(2)}, u32[]{:S(2)}) collective-permute-start(bf16[1,64,512]{2,1,0:T(8,128)(2,1)S(1)} %get-tuple-element.37), channel_id=1, source_target_pairs={{0,9},{1,8},{4,13},{5,12},{8,1},{9,0},{12,5},{13,4},{2,11},{3,10},... | collective-permute-start | bytes 196616 | tf_op jit(solution)/shard_map/ppermute | solution.py:320
  25.7 1.1 %collective-permute-done.8.got_ref = bf16[1,2,128,512]{3,2,1,0:T(8,128)(2,1)S(1)} collective-permute-done((bf16[1,2,128,512]{3,2,1,0:T(8,128)(2,1)S(1)}, bf16[1,2,128,512]{3,2,1,0:T(8,128)(2,1)S(1)}, u32[]{:S(2)}, u32[]{:S(2)}) %collective-permute-start.8) | collective-permute-done | bytes 262176 | tf_op jit(solution)/shard_map/ppermute | solution.py:275
  26.8 0.3 decode.4
  27.1 0.0 copy-start.1
  27.1 0.0 copy-start.2
  27.1 1.7 %collective-permute-start.15 = (bf16[1,64,512]{2,1,0:T(8,128)(2,1)S(1)}, bf16[1,64,512]{2,1,0:T(8,128)(2,1)S(1)}, u32[]{:S(2)}, u32[]{:S(2)}) collective-permute-start(bf16[1,64,512]{2,1,0:T(8,128)(2,1)S(1)} %get-tuple-element.38), channel_id=1, source_target_pairs={{0,8},{1,9},{4,12},{5,13},{8,0},{9,1},{12,4},{13,5},{2,10},{3,11},... | collective-permute-start | bytes 196616 | tf_op jit(solution)/shard_map/ppermute | solution.py:320
  28.8 3.1 %collective-permute-done.12.refs_1_ = bf16[1,64,512]{2,1,0:T(8,128)(2,1)S(1)} collective-permute-done((bf16[1,64,512]{2,1,0:T(8,128)(2,1)S(1)}, bf16[1,64,512]{2,1,0:T(8,128)(2,1)S(1)}, u32[]{:S(2)}, u32[]{:S(2)}) %collective-permute-start.12) | collective-permute-done | bytes 65568 | tf_op jit(solution)/shard_map/ppermute | solution.py:320
  31.9 0.0 collective-permute-start.16
  31.9 4.6 %collective-permute-done.6.got_ref = bf16[2,2,128,512]{3,2,1,0:T(8,128)(2,1)S(1)} collective-permute-done((bf16[2,2,128,512]{3,2,1,0:T(8,128)(2,1)S(1)}, bf16[2,2,128,512]{3,2,1,0:T(8,128)(2,1)S(1)}, u32[]{:S(2)}, u32[]{:S(2)}) %collective-permute-start.6) | collective-permute-done | bytes 524320 | tf_op jit(solution)/shard_map/ppermute | solution.py:276
  36.5 0.0 collective-permute-start.17
  36.5 0.4 decode.5
  37.0 0.0 collective-permute-done.13.refs_2_
  37.0 2.0 %collective-permute-start.9 = (bf16[2,64,512]{2,1,0:T(8,128)(2,1)S(1)}, bf16[2,64,512]{2,1,0:T(8,128)(2,1)S(1)}, u32[]{:S(2)}, u32[]{:S(2)}) collective-permute-start(bf16[2,64,512]{2,1,0:T(8,128)(2,1)S(1)} %get-tuple-element.32), channel_id=1, source_target_pairs={{0,8},{1,9},{4,12},{5,13},{8,0},{9,1},{12,4},{13,5},{2,10},{3,11},... | collective-permute-start | bytes 393224 | tf_op jit(solution)/shard_map/ppermute | solution.py:320
  39.0 0.0 collective-permute-done.14.refs_3_
  39.0 0.8 %collective-permute-start.10 = (bf16[2,64,512]{2,1,0:T(8,128)(2,1)S(1)}, bf16[2,64,512]{2,1,0:T(8,128)(2,1)S(1)}, u32[]{:S(2)}, u32[]{:S(2)}) collective-permute-start(bf16[2,64,512]{2,1,0:T(8,128)(2,1)S(1)} %get-tuple-element.33), channel_id=1, source_target_pairs={{0,1},{1,0},{4,5},{5,4},{8,9},{9,8},{12,13},{13,12},{2,3},{3,2},{6... | collective-permute-start | bytes 393224 | tf_op jit(solution)/shard_map/ppermute | solution.py:320
  39.8 0.0 collective-permute-done.15.refs_5_
  39.8 0.3 collective-permute-start.11
  40.1 0.0 collective-permute-done.16.refs_6_
  40.1 7.8 %collective-permute-done.17.refs_7_ = bf16[1,64,512]{2,1,0:T(8,128)(2,1)S(1)} collective-permute-done((bf16[1,64,512]{2,1,0:T(8,128)(2,1)S(1)}, bf16[1,64,512]{2,1,0:T(8,128)(2,1)S(1)}, u32[]{:S(2)}, u32[]{:S(2)}) %collective-permute-start.17) | collective-permute-done | bytes 65568 | tf_op jit(solution)/shard_map/ppermute | solution.py:320
  47.9 0.0 copy-done.1
  47.9 0.8 %add.2.refs_4_ = bf16[2,64,2048]{2,1,0:T(8,128)(2,1)} custom-call(f32[2,2048]{1,0:T(2,128)S(1)} %copy-done.2, bf16[2,64,2048]{2,1,0:T(8,128)(2,1)S(1)} %copy-done.1, f32[1,64,512]{2,1,0:T(8,128)S(1)} %get-tuple-element.29.refs_0_, bf16[1,64,512]{2,1,0:T(8,128)(2,1)S(1)} %collective-permute-done.12.refs_1_, ...), custom_call_target="tpu_custom_call" | custom-call | flops 20000000000 | tf_op jit(solution)/shard_map/add/pallas_call | solution.py:282
  48.6 1.9 %collective-permute-done.9.refs_1_ = bf16[2,64,512]{2,1,0:T(8,128)(2,1)S(1)} collective-permute-done((bf16[2,64,512]{2,1,0:T(8,128)(2,1)S(1)}, bf16[2,64,512]{2,1,0:T(8,128)(2,1)S(1)}, u32[]{:S(2)}, u32[]{:S(2)}) %collective-permute-start.9) | collective-permute-done | bytes 131104 | tf_op jit(solution)/shard_map/ppermute | solution.py:320
  50.6 0.0 collective-permute-done.10.refs_2_
  50.6 2.8 %collective-permute-done.11.refs_3_ = bf16[2,64,512]{2,1,0:T(8,128)(2,1)S(1)} collective-permute-done((bf16[2,64,512]{2,1,0:T(8,128)(2,1)S(1)}, bf16[2,64,512]{2,1,0:T(8,128)(2,1)S(1)}, u32[]{:S(2)}, u32[]{:S(2)}) %collective-permute-start.11) | collective-permute-done | bytes 131104 | tf_op jit(solution)/shard_map/ppermute | solution.py:320
  53.4 0.8 %add.3 = bf16[2,64,2048]{2,1,0:T(8,128)(2,1)} custom-call(f32[2,2048]{1,0:T(2,128)S(1)} %copy-done.2, bf16[2,64,2048]{2,1,0:T(8,128)(2,1)S(1)} %copy-done.1, f32[2,64,512]{2,1,0:T(8,128)S(1)} %get-tuple-element.31.refs_0_, bf16[2,64,512]{2,1,0:T(8,128)(2,1)S(1)} %collective-permute-done.9.refs_1_, ...), custom_call_target="tpu_custom_call", output_to_operand_aliasing={{}: (6, {})} | custom-call | tf_op jit(solution)/shard_map/add/pallas_call | solution.py:282
  (7 shorter events, 0.1 us)
Async XLA Ops:
  0.0 15.7 %copy-start.4 = (s32[2,8]{1,0:T(2,128)S(1)}, s32[2,8]{1,0:T(2,128)}, u32[]{:S(2)}) copy-start(s32[2,8]{1,0:T(2,128)} %active_ref.1) | copy-start | bytes 196
  0.0 15.7 %copy-start.3 = (f32[512]{0:T(512)S(1)}, f32[512]{0:T(512)}, u32[]{:S(2)}) copy-start(f32[512]{0:T(512)} %param.9) | copy-start | bytes 6148
  3.2 6.6 %collective-permute-start = (bf16[128,256]{1,0:T(8,128)(2,1)S(1)}, bf16[128,256]{1,0:T(8,128)(2,1)S(1)}, u32[]{:S(2)}, u32[]{:S(2)}) collective-permute-start(bf16[128,256]{1,0:T(8,128)(2,1)S(1)} %get-tuple-element.24), channel_id=1, source_target_pairs={{0,4},{4,0},{8,12},{12,8},{1,5},{5,1},{9,13},{13,9},{2,6},{6,2},{1... | collective-permute-start | bytes 196616 | tf_op jit(solution)/shard_map/ppermute | solution.py:234
  6.3 7.3 %collective-permute-start.1 = (bf16[128,256]{1,0:T(8,128)(2,1)S(1)}, bf16[128,256]{1,0:T(8,128)(2,1)S(1)}, u32[]{:S(2)}, u32[]{:S(2)}) collective-permute-start(bf16[128,256]{1,0:T(8,128)(2,1)S(1)} %get-tuple-element.25), channel_id=1, source_target_pairs={{0,8},{4,12},{8,0},{12,4},{1,9},{5,13},{9,1},{13,5},{2,10},{6,14},... | collective-permute-start | bytes 196616 | tf_op jit(solution)/shard_map/ppermute | solution.py:234
  8.9 6.8 %collective-permute-start.2 = (bf16[128,256]{1,0:T(8,128)(2,1)S(1)}, bf16[128,256]{1,0:T(8,128)(2,1)S(1)}, u32[]{:S(2)}, u32[]{:S(2)}) collective-permute-start(bf16[128,256]{1,0:T(8,128)(2,1)S(1)} %get-tuple-element.26), channel_id=1, source_target_pairs={{0,12},{4,8},{8,4},{12,0},{1,13},{5,9},{9,5},{13,1},{2,14},{6,10},... | collective-permute-start | bytes 196616 | tf_op jit(solution)/shard_map/ppermute | solution.py:234
  8.9 9.6 %collective-permute-start.7 = (bf16[1,2,128,512]{3,2,1,0:T(8,128)(2,1)S(1)}, bf16[1,2,128,512]{3,2,1,0:T(8,128)(2,1)S(1)}, u32[]{:S(2)}, u32[]{:S(2)}) collective-permute-start(bf16[1,2,128,512]{3,2,1,0:T(8,128)(2,1)S(1)} %get-tuple-element.28), channel_id=1, source_target_pairs={{0,4},{4,0},{8,12},{12,8},{1,5},{5,1},{9,13},{13,9},{2,6},{6,2},{1... | collective-permute-start | bytes 786440 | tf_op jit(solution)/shard_map/ppermute | solution.py:274
  16.3 4.4 %collective-permute-start.5 = (bf16[2,64,256]{2,1,0:T(8,128)(2,1)S(1)}, bf16[2,64,256]{2,1,0:T(8,128)(2,1)S(1)}, u32[]{:S(2)}, u32[]{:S(2)}) collective-permute-start(bf16[2,64,256]{2,1,0:T(8,128)(2,1)S(1)} %codes.1.refs_0_.refs_1_), channel_id=1, source_target_pairs={{0,3},{1,2},{2,1},{3,0},{4,7},{5,6},{6,5},{7,4},{8,11},{9,10},{10,... | collective-permute-start | bytes 196616 | tf_op jit(solution)/shard_map/ppermute | solution.py:250
  16.4 5.8 %collective-permute-start.4 = (bf16[2,64,256]{2,1,0:T(8,128)(2,1)S(1)}, bf16[2,64,256]{2,1,0:T(8,128)(2,1)S(1)}, u32[]{:S(2)}, u32[]{:S(2)}) collective-permute-start(bf16[2,64,256]{2,1,0:T(8,128)(2,1)S(1)} %codes.1.refs_0_.refs_1_), channel_id=1, source_target_pairs={{0,2},{1,3},{2,0},{3,1},{4,6},{5,7},{6,4},{7,5},{8,10},{9,11},{10,... | collective-permute-start | bytes 196616 | tf_op jit(solution)/shard_map/ppermute | solution.py:250
  18.0 4.2 %collective-permute-start.3 = (bf16[2,64,256]{2,1,0:T(8,128)(2,1)S(1)}, bf16[2,64,256]{2,1,0:T(8,128)(2,1)S(1)}, u32[]{:S(2)}, u32[]{:S(2)}) collective-permute-start(bf16[2,64,256]{2,1,0:T(8,128)(2,1)S(1)} %codes.1.refs_0_.refs_1_), channel_id=1, source_target_pairs={{0,1},{1,0},{2,3},{3,2},{4,5},{5,4},{6,7},{7,6},{8,9},{9,8},{10,11... | collective-permute-start | bytes 196616 | tf_op jit(solution)/shard_map/ppermute | solution.py:250
  18.3 4.0 %copy-start = (bf16[2,2,128,2048]{3,2,1,0:T(8,128)(2,1)S(1)}, bf16[2,2,128,2048]{3,2,1,0:T(8,128)(2,1)}, u32[]{:S(2)}) copy-start(bf16[2,2,128,2048]{3,2,1,0:T(8,128)(2,1)} %dec_ref.5) | copy-start | bytes 6291460
  18.3 18.3 %collective-permute-start.6 = (bf16[2,2,128,512]{3,2,1,0:T(8,128)(2,1)S(1)}, bf16[2,2,128,512]{3,2,1,0:T(8,128)(2,1)S(1)}, u32[]{:S(2)}, u32[]{:S(2)}) collective-permute-start(bf16[2,2,128,512]{3,2,1,0:T(8,128)(2,1)S(1)} %hold.1), channel_id=1, source_target_pairs={{0,4},{4,0},{8,12},{12,8},{1,5},{5,1},{9,13},{13,9},{2,6},{6,2},{1... | collective-permute-start | bytes 1572872 | tf_op jit(solution)/shard_map/ppermute | solution.py:276
  18.5 8.3 %collective-permute-start.8 = (bf16[1,2,128,512]{3,2,1,0:T(8,128)(2,1)S(1)}, bf16[1,2,128,512]{3,2,1,0:T(8,128)(2,1)S(1)}, u32[]{:S(2)}, u32[]{:S(2)}) collective-permute-start(bf16[1,2,128,512]{3,2,1,0:T(8,128)(2,1)S(1)} %collective-permute-done.7.got_ref), channel_id=1, source_target_pairs={{0,16},{16,0},{1,17},{17,1},{2,18},{18,2},{3,19},{19,3},{4,20},{20... | collective-permute-start | bytes 786440 | tf_op jit(solution)/shard_map/ppermute | solution.py:275
  22.6 9.3 %collective-permute-start.12 = (bf16[1,64,512]{2,1,0:T(8,128)(2,1)S(1)}, bf16[1,64,512]{2,1,0:T(8,128)(2,1)S(1)}, u32[]{:S(2)}, u32[]{:S(2)}) collective-permute-start(bf16[1,64,512]{2,1,0:T(8,128)(2,1)S(1)} %get-tuple-element.35), channel_id=1, source_target_pairs={{0,8},{1,9},{4,12},{5,13},{8,0},{9,1},{12,4},{13,5},{2,10},{3,11},... | collective-permute-start | bytes 196616 | tf_op jit(solution)/shard_map/ppermute | solution.py:320
  23.5 13.5 %collective-permute-start.13 = (bf16[1,64,512]{2,1,0:T(8,128)(2,1)S(1)}, bf16[1,64,512]{2,1,0:T(8,128)(2,1)S(1)}, u32[]{:S(2)}, u32[]{:S(2)}) collective-permute-start(bf16[1,64,512]{2,1,0:T(8,128)(2,1)S(1)} %get-tuple-element.36), channel_id=1, source_target_pairs={{0,1},{1,0},{4,5},{5,4},{8,9},{9,8},{12,13},{13,12},{2,3},{3,2},{6... | collective-permute-start | bytes 196616 | tf_op jit(solution)/shard_map/ppermute | solution.py:320
  23.5 15.5 %collective-permute-start.14 = (bf16[1,64,512]{2,1,0:T(8,128)(2,1)S(1)}, bf16[1,64,512]{2,1,0:T(8,128)(2,1)S(1)}, u32[]{:S(2)}, u32[]{:S(2)}) collective-permute-start(bf16[1,64,512]{2,1,0:T(8,128)(2,1)S(1)} %get-tuple-element.37), channel_id=1, source_target_pairs={{0,9},{1,8},{4,13},{5,12},{8,1},{9,0},{12,5},{13,4},{2,11},{3,10},... | collective-permute-start | bytes 196616 | tf_op jit(solution)/shard_map/ppermute | solution.py:320
  27.1 20.8 %copy-start.1 = (bf16[2,64,2048]{2,1,0:T(8,128)(2,1)S(1)}, bf16[2,64,2048]{2,1,0:T(8,128)(2,1)}, u32[]{:S(2)}) copy-start(bf16[2,64,2048]{2,1,0:T(8,128)(2,1)} %target_ref.3) | copy-start | bytes 1572868
  27.1 20.8 %copy-start.2 = (f32[2,2048]{1,0:T(2,128)S(1)}, f32[2,2048]{1,0:T(2,128)}, u32[]{:S(2)}) copy-start(f32[2,2048]{1,0:T(2,128)} %bias_ref.3) | copy-start | bytes 49156
  27.1 12.7 %collective-permute-start.15 = (bf16[1,64,512]{2,1,0:T(8,128)(2,1)S(1)}, bf16[1,64,512]{2,1,0:T(8,128)(2,1)S(1)}, u32[]{:S(2)}, u32[]{:S(2)}) collective-permute-start(bf16[1,64,512]{2,1,0:T(8,128)(2,1)S(1)} %get-tuple-element.38), channel_id=1, source_target_pairs={{0,8},{1,9},{4,12},{5,13},{8,0},{9,1},{12,4},{13,5},{2,10},{3,11},... | collective-permute-start | bytes 196616 | tf_op jit(solution)/shard_map/ppermute | solution.py:320
  31.9 8.2 %collective-permute-start.16 = (bf16[1,64,512]{2,1,0:T(8,128)(2,1)S(1)}, bf16[1,64,512]{2,1,0:T(8,128)(2,1)S(1)}, u32[]{:S(2)}, u32[]{:S(2)}) collective-permute-start(bf16[1,64,512]{2,1,0:T(8,128)(2,1)S(1)} %get-tuple-element.39), channel_id=1, source_target_pairs={{0,1},{1,0},{4,5},{5,4},{8,9},{9,8},{12,13},{13,12},{2,3},{3,2},{6... | collective-permute-start | bytes 196616 | tf_op jit(solution)/shard_map/ppermute | solution.py:320
  36.5 11.3 %collective-permute-start.17 = (bf16[1,64,512]{2,1,0:T(8,128)(2,1)S(1)}, bf16[1,64,512]{2,1,0:T(8,128)(2,1)S(1)}, u32[]{:S(2)}, u32[]{:S(2)}) collective-permute-start(bf16[1,64,512]{2,1,0:T(8,128)(2,1)S(1)} %get-tuple-element.40), channel_id=1, source_target_pairs={{0,9},{1,8},{4,13},{5,12},{8,1},{9,0},{12,5},{13,4},{2,11},{3,10},... | collective-permute-start | bytes 196616 | tf_op jit(solution)/shard_map/ppermute | solution.py:320
  37.0 13.6 %collective-permute-start.9 = (bf16[2,64,512]{2,1,0:T(8,128)(2,1)S(1)}, bf16[2,64,512]{2,1,0:T(8,128)(2,1)S(1)}, u32[]{:S(2)}, u32[]{:S(2)}) collective-permute-start(bf16[2,64,512]{2,1,0:T(8,128)(2,1)S(1)} %get-tuple-element.32), channel_id=1, source_target_pairs={{0,8},{1,9},{4,12},{5,13},{8,0},{9,1},{12,4},{13,5},{2,10},{3,11},... | collective-permute-start | bytes 393224 | tf_op jit(solution)/shard_map/ppermute | solution.py:320
  39.0 11.6 %collective-permute-start.10 = (bf16[2,64,512]{2,1,0:T(8,128)(2,1)S(1)}, bf16[2,64,512]{2,1,0:T(8,128)(2,1)S(1)}, u32[]{:S(2)}, u32[]{:S(2)}) collective-permute-start(bf16[2,64,512]{2,1,0:T(8,128)(2,1)S(1)} %get-tuple-element.33), channel_id=1, source_target_pairs={{0,1},{1,0},{4,5},{5,4},{8,9},{9,8},{12,13},{13,12},{2,3},{3,2},{6... | collective-permute-start | bytes 393224 | tf_op jit(solution)/shard_map/ppermute | solution.py:320
  39.8 13.6 %collective-permute-start.11 = (bf16[2,64,512]{2,1,0:T(8,128)(2,1)S(1)}, bf16[2,64,512]{2,1,0:T(8,128)(2,1)S(1)}, u32[]{:S(2)}, u32[]{:S(2)}) collective-permute-start(bf16[2,64,512]{2,1,0:T(8,128)(2,1)S(1)} %get-tuple-element.34), channel_id=1, source_target_pairs={{0,9},{1,8},{4,13},{5,12},{8,1},{9,0},{12,5},{13,4},{2,11},{3,10},... | collective-permute-start | bytes 393224 | tf_op jit(solution)/shard_map/ppermute | solution.py:320

commit v15 on v14

--- a/solution.py
+++ b/solution.py
@@ -9,11 +9,12 @@
 
 VMEM_BYTES = 32 * 1024 * 1024
 LANES = 128
+FIRST = 5
 PIECES = (((0,), 0, False), ((1,), 0, True), ((0, 1), 1, False))
 
 
 def cut_pieces(columns):
-    middle = -(-(columns // LANES) // 2) * LANES
+    middle = columns // LANES * FIRST // 8 * LANES
     bounds = ((0, middle), (middle, columns))
     return [
         (layers, bounds[side][0], bounds[side][1] - bounds[side][0], across)
@@ -168,7 +169,9 @@
                 for other in range(1, layers):
                     total = jnp.where(layer == other, bias_ref[other : other + 1, columns], total)
                 total = total - target_ref[layer, :, columns].astype(jnp.float32)
-                for ref in refs[(2 * i + side) * half : (2 * i + side + 1) * half]:
+                mine = refs[2 * half * i : 2 * half * (i + 1)]
+                first_sum = side * (half - 1)
+                for ref in (*mine[first_sum : first_sum + half - 1], mine[-1 - side]):
                     total = total + ref[j].astype(jnp.float32)
                 place = len(copies)
                 out_ref[place, :, :width] = total.astype(jnp.bfloat16)
@@ -309,16 +312,11 @@
             name="decode",
         )(dec_rows, lhs, got[i], *after)
         after = [terms[0]]
-        sums.append([None] * (2 * half))
-        for j in [*range(1, half), 0]:
-            for r in range(2):
-                perm = [
-                    (d * 2 + c, (d + 2 * j) % n * 2 + (c ^ r)) for d in range(n) for c in range(2)
-                ]
-                term = terms[2 * j + r]
-                sums[i][r * half + j] = (
-                    lax.ppermute(term, ("src", "rep"), perm) if j + r else term
-                )
+        sums.append([])
+        for r, j in [(r, j) for r in range(2) for j in range(1, half)] + [(1, 0)]:
+            perm = [(d * 2 + c, (d + 2 * j) % n * 2 + (c ^ r)) for d in range(n) for c in range(2)]
+            sums[i].append(lax.ppermute(terms[2 * j + r], ("src", "rep"), perm))
+        sums[i].append(terms[0])
 
     begun = []
     begun = [add([0, 1], begun, 20)]

time: 54.4 us -> 49.5 us (0.910)
  waiting for transfers between devices: 29.7 us -> 21.7 us
  starting transfers between devices: 17.9 us -> 20.9 us
    ppermute x9, waiting for transfers between devices: 15.7 us -> 9.54 us  [body(): sums[i].append(lax.ppermute(terms[2 * j + r], ('src', 'rep'), perm))]
    ppermute x1, waiting for transfers between devices: 4.61 us -> 1.29 us  [body(): got.append(lax.ppermute(hold(parts[1], own), 'src', pair))]
    ppermute x9, starting transfers between devices: 7.88 us -> 10.9 us  [body(): sums[i].append(lax.ppermute(terms[2 * j + r], ('src', 'rep'), perm))]
    ppermute x1, waiting for transfers between devices: 1.09 us -> 2.53 us  [body(): got.append(lax.ppermute(got[0], 'parts', [(0, 1), (1, 0)]))]
    ppermute x3, waiting for transfers between devices: 2.22 us -> 0.81 us  [body(): codes.append(lax.ppermute(own, ('tgt', 'rep'), perm) if k + r else own)]
    ppermute x1, waiting for transfers between devices: 0.19 us -> 1.6 us  [body(): got = [lax.ppermute(parts[0], 'src', pair)]]
  transfers between devices with their start and end apart: 18 -> 18, of which waited for: 11 -> 10; matrix products, arithmetic and copies ran while one was open for 0% -> 0% of each run, Pallas kernels for 5% -> 5%
where the time goes in v15:
time: 49.5 us; the launch traced here: 49.3 us
  waiting for transfers between devices  21.7 us (44%)
  starting transfers between devices  20.9 us (42%)
  Pallas kernels  6.57 us (13%)
    ppermute x9, starting transfers between devices, body(): sums[i].append(lax.ppermute(terms[2 * j + r], ('src', 'rep'), perm))  10.9 us
    ppermute x9, waiting for transfers between devices, body(): sums[i].append(lax.ppermute(terms[2 * j + r], ('src', 'rep'), perm))  9.54 us
    ppermute x3, waiting for transfers between devices, body(): lax.ppermute(terms[k], 'src', [(i, peer(i, k, n)) for i in range(n)])  5.92 us
    ppermute x3, starting transfers between devices, body(): lax.ppermute(terms[k], 'src', [(i, peer(i, k, n)) for i in range(n)])  5.68 us
    pallas_call x1, Pallas kernels, body(): pl.pallas_call(functools.partial(encode_kernel, n, fetched), out_shape=[s...  3.16 us
    ppermute x1, waiting for transfers between devices, body(): got.append(lax.ppermute(got[0], 'parts', [(0, 1), (1, 0)]))  2.53 us
    ppermute x3, starting transfers between devices, body(): codes.append(lax.ppermute(own, ('tgt', 'rep'), perm) if k + r else own)  1.92 us
    ppermute x1, waiting for transfers between devices, body(): got = [lax.ppermute(parts[0], 'src', pair)]  1.6 us
  transfers between devices with their start and end apart: 18, of which 10 were waited for; matrix products, arithmetic and copies ran while one was open for 0% of the time, Pallas kernels for 5%

profile of v15, /device:TPU:0, one launch (start us, length us, event | category | flops | bytes accessed | tf_op | source)
XLA Modules:
  0.0 49.3 jit_solution(13208512151218800650)
XLA Ops:
  0.0 3.2 %encode.1 = (bf16[128,256]{1,0:T(8,128)(2,1)S(1)}, bf16[128,256]{1,0:T(8,128)(2,1)S(1)}, bf16[128,256]{1,0:T(8,128)(2,1)S(1)}, bf16[128,256]{1,0:T(8,128)(2,1)S(...) custom-call(bf16[2,2,64,1024]{3,2,1,0:T(8,128)(2,1)} %bitcast.3, bf16[1024,512]{1,0:T(8,128)(2,1)} %w_hbm.1, ...), custom_call_target="tpu_custom_call" | custom-call | tf_op jit(solution)/shard_map/encode/pallas_call | solution.py:218
  3.2 3.1 %collective-permute-start = (bf16[128,256]{1,0:T(8,128)(2,1)S(1)}, bf16[128,256]{1,0:T(8,128)(2,1)S(1)}, u32[]{:S(2)}, u32[]{:S(2)}) collective-permute-start(bf16[128,256]{1,0:T(8,128)(2,1)S(1)} %get-tuple-element.24), channel_id=1, source_target_pairs={{0,4},{4,0},{8,12},{12,8},{1,5},{5,1},{9,13},{13,9},{2,6},{6,2},{1... | collective-permute-start | bytes 196616 | tf_op jit(solution)/shard_map/ppermute | solution.py:237
  6.3 2.6 %collective-permute-start.1 = (bf16[128,256]{1,0:T(8,128)(2,1)S(1)}, bf16[128,256]{1,0:T(8,128)(2,1)S(1)}, u32[]{:S(2)}, u32[]{:S(2)}) collective-permute-start(bf16[128,256]{1,0:T(8,128)(2,1)S(1)} %get-tuple-element.25), channel_id=1, source_target_pairs={{0,8},{4,12},{8,0},{12,4},{1,9},{5,13},{9,1},{13,5},{2,10},{6,14},... | collective-permute-start | bytes 196616 | tf_op jit(solution)/shard_map/ppermute | solution.py:237
  8.8 0.0 collective-permute-start.2
  8.8 0.9 %collective-permute-start.7 = (bf16[1,2,128,640]{3,2,1,0:T(8,128)(2,1)S(1)}, bf16[1,2,128,640]{3,2,1,0:T(8,128)(2,1)S(1)}, u32[]{:S(2)}, u32[]{:S(2)}) collective-permute-start(bf16[1,2,128,640]{3,2,1,0:T(8,128)(2,1)S(1)} %get-tuple-element.28), channel_id=1, source_target_pairs={{0,4},{4,0},{8,12},{12,8},{1,5},{5,1},{9,13},{13,9},{2,6},{6,2},{1... | collective-permute-start | bytes 983048 | tf_op jit(solution)/shard_map/ppermute | solution.py:277
  9.8 0.0 collective-permute-done.refs_1_
  9.8 3.8 %collective-permute-done.1.refs_2_ = bf16[128,256]{1,0:T(8,128)(2,1)S(1)} collective-permute-done((bf16[128,256]{1,0:T(8,128)(2,1)S(1)}, bf16[128,256]{1,0:T(8,128)(2,1)S(1)}, u32[]{:S(2)}, u32[]{:S(2)}) %collective-permute-start.1) | collective-permute-done | bytes 65568 | tf_op jit(solution)/shard_map/ppermute | solution.py:237
  13.5 2.1 %collective-permute-done.2.refs_3_ = bf16[128,256]{1,0:T(8,128)(2,1)S(1)} collective-permute-done((bf16[128,256]{1,0:T(8,128)(2,1)S(1)}, bf16[128,256]{1,0:T(8,128)(2,1)S(1)}, u32[]{:S(2)}, u32[]{:S(2)}) %collective-permute-start.2) | collective-permute-done | bytes 65568 | tf_op jit(solution)/shard_map/ppermute | solution.py:237
  15.7 0.0 copy-done.4
  15.7 0.0 copy-done.3
  15.7 0.6 %codes.1.refs_0_.refs_1_ = bf16[2,64,256]{2,1,0:T(8,128)(2,1)S(1)} custom-call(s32[2,8]{1,0:T(2,128)S(1)} %copy-done.4, f32[4,128]{1,0:T(4,128)S(1)} %bitcast.2, bf16[128,256]{1,0:T(8,128)(2,1)S(1)} %get-tuple-element.23.refs_0_, bf16[128,256]{1,0:T(8,128)(2,1)S(1)} %collective-permute-done.refs_1_, bf16[128,256]{1,0:T(8,128)(2,1)S(1)} %collective-permute-done.1.refs_2_, ...), custom_call_target="tpu_custom_call" | custom-call | flops 20000000000 | tf_op jit(solution)/shard_map/codes/pallas_call | solution.py:238
  16.3 0.1 collective-permute-start.5
  16.4 1.6 %collective-permute-start.4 = (bf16[2,64,256]{2,1,0:T(8,128)(2,1)S(1)}, bf16[2,64,256]{2,1,0:T(8,128)(2,1)S(1)}, u32[]{:S(2)}, u32[]{:S(2)}) collective-permute-start(bf16[2,64,256]{2,1,0:T(8,128)(2,1)S(1)} %codes.1.refs_0_.refs_1_), channel_id=1, source_target_pairs={{0,2},{1,3},{2,0},{3,1},{4,6},{5,7},{6,4},{7,5},{8,10},{9,11},{10,... | collective-permute-start | bytes 196616 | tf_op jit(solution)/shard_map/ppermute | solution.py:253
  17.9 0.3 collective-permute-start.3
  18.2 0.0 collective-permute-start.6
  18.2 1.6 %collective-permute-done.7.got_ref = bf16[1,2,128,640]{3,2,1,0:T(8,128)(2,1)S(1)} collective-permute-done((bf16[1,2,128,640]{3,2,1,0:T(8,128)(2,1)S(1)}, bf16[1,2,128,640]{3,2,1,0:T(8,128)(2,1)S(1)}, u32[]{:S(2)}, u32[]{:S(2)}) %collective-permute-start.7) | collective-permute-done | bytes 327712 | tf_op jit(solution)/shard_map/ppermute | solution.py:277
  19.8 1.5 %collective-permute-start.8 = (bf16[1,2,128,640]{3,2,1,0:T(8,128)(2,1)S(1)}, bf16[1,2,128,640]{3,2,1,0:T(8,128)(2,1)S(1)}, u32[]{:S(2)}, u32[]{:S(2)}) collective-permute-start(bf16[1,2,128,640]{3,2,1,0:T(8,128)(2,1)S(1)} %collective-permute-done.7.got_ref), channel_id=1, source_target_pairs={{0,16},{16,0},{1,17},{17,1},{2,18},{18,2},{3,19},{19,3},{4,20},{20... | collective-permute-start | bytes 983048 | tf_op jit(solution)/shard_map/ppermute | solution.py:278
  21.4 0.0 collective-permute-done.5.refs_3_
  21.4 0.8 %collective-permute-done.4.refs_2_ = bf16[2,64,256]{2,1,0:T(8,128)(2,1)S(1)} collective-permute-done((bf16[2,64,256]{2,1,0:T(8,128)(2,1)S(1)}, bf16[2,64,256]{2,1,0:T(8,128)(2,1)S(1)}, u32[]{:S(2)}, u32[]{:S(2)}) %collective-permute-start.4) | collective-permute-done | bytes 65568 | tf_op jit(solution)/shard_map/ppermute | solution.py:253
  22.2 0.0 collective-permute-done.3.refs_1_
  22.2 0.4 decode.3
  22.6 0.9 %collective-permute-start.12 = (bf16[1,64,640]{2,1,0:T(8,128)(2,1)S(1)}, bf16[1,64,640]{2,1,0:T(8,128)(2,1)S(1)}, u32[]{:S(2)}, u32[]{:S(2)}) collective-permute-start(bf16[1,64,640]{2,1,0:T(8,128)(2,1)S(1)} %get-tuple-element.35), channel_id=1, source_target_pairs={{0,8},{1,9},{4,12},{5,13},{8,0},{9,1},{12,4},{13,5},{2,10},{3,11},... | collective-permute-start | bytes 245768 | tf_op jit(solution)/shard_map/ppermute | solution.py:318
  23.6 1.4 %collective-permute-start.13 = (bf16[1,64,640]{2,1,0:T(8,128)(2,1)S(1)}, bf16[1,64,640]{2,1,0:T(8,128)(2,1)S(1)}, u32[]{:S(2)}, u32[]{:S(2)}) collective-permute-start(bf16[1,64,640]{2,1,0:T(8,128)(2,1)S(1)} %get-tuple-element.36), channel_id=1, source_target_pairs={{0,9},{1,8},{4,13},{5,12},{8,1},{9,0},{12,5},{13,4},{2,11},{3,10},... | collective-permute-start | bytes 245768 | tf_op jit(solution)/shard_map/ppermute | solution.py:318
  25.0 0.7 %collective-permute-start.14 = (bf16[1,64,640]{2,1,0:T(8,128)(2,1)S(1)}, bf16[1,64,640]{2,1,0:T(8,128)(2,1)S(1)}, u32[]{:S(2)}, u32[]{:S(2)}) collective-permute-start(bf16[1,64,640]{2,1,0:T(8,128)(2,1)S(1)} %get-tuple-element.37), channel_id=1, source_target_pairs={{0,1},{1,0},{4,5},{5,4},{8,9},{9,8},{12,13},{13,12},{2,3},{3,2},{6... | collective-permute-start | bytes 245768 | tf_op jit(solution)/shard_map/ppermute | solution.py:318
  25.7 2.5 %collective-permute-done.8.got_ref = bf16[1,2,128,640]{3,2,1,0:T(8,128)(2,1)S(1)} collective-permute-done((bf16[1,2,128,640]{3,2,1,0:T(8,128)(2,1)S(1)}, bf16[1,2,128,640]{3,2,1,0:T(8,128)(2,1)S(1)}, u32[]{:S(2)}, u32[]{:S(2)}) %collective-permute-start.8) | collective-permute-done | bytes 327712 | tf_op jit(solution)/shard_map/ppermute | solution.py:278
  28.3 0.4 decode.4
  28.6 0.0 copy-start.1
  28.6 0.0 copy-start.2
  28.7 1.6 %collective-permute-start.15 = (bf16[1,64,640]{2,1,0:T(8,128)(2,1)S(1)}, bf16[1,64,640]{2,1,0:T(8,128)(2,1)S(1)}, u32[]{:S(2)}, u32[]{:S(2)}) collective-permute-start(bf16[1,64,640]{2,1,0:T(8,128)(2,1)S(1)} %get-tuple-element.38), channel_id=1, source_target_pairs={{0,8},{1,9},{4,12},{5,13},{8,0},{9,1},{12,4},{13,5},{2,10},{3,11},... | collective-permute-start | bytes 245768 | tf_op jit(solution)/shard_map/ppermute | solution.py:318
  30.2 0.0 collective-permute-done.12.refs_0_
  30.2 1.5 %collective-permute-start.16 = (bf16[1,64,640]{2,1,0:T(8,128)(2,1)S(1)}, bf16[1,64,640]{2,1,0:T(8,128)(2,1)S(1)}, u32[]{:S(2)}, u32[]{:S(2)}) collective-permute-start(bf16[1,64,640]{2,1,0:T(8,128)(2,1)S(1)} %get-tuple-element.39), channel_id=1, source_target_pairs={{0,9},{1,8},{4,13},{5,12},{8,1},{9,0},{12,5},{13,4},{2,11},{3,10},... | collective-permute-start | bytes 245768 | tf_op jit(solution)/shard_map/ppermute | solution.py:318
  31.7 1.3 %collective-permute-done.6.got_ref = bf16[2,2,128,384]{3,2,1,0:T(8,128)(2,1)S(1)} collective-permute-done((bf16[2,2,128,384]{3,2,1,0:T(8,128)(2,1)S(1)}, bf16[2,2,128,384]{3,2,1,0:T(8,128)(2,1)S(1)}, u32[]{:S(2)}, u32[]{:S(2)}) %collective-permute-start.6) | collective-permute-done | bytes 393248 | tf_op jit(solution)/shard_map/ppermute | solution.py:279
  33.0 0.0 collective-permute-start.17
  33.0 0.4 decode.5
  33.5 0.0 collective-permute-done.13.refs_1_
  33.5 0.4 collective-permute-start.9
  33.9 0.0 collective-permute-done.14.refs_2_
  33.9 4.3 %collective-permute-start.10 = (bf16[2,64,384]{2,1,0:T(8,128)(2,1)S(1)}, bf16[2,64,384]{2,1,0:T(8,128)(2,1)S(1)}, u32[]{:S(2)}, u32[]{:S(2)}) collective-permute-start(bf16[2,64,384]{2,1,0:T(8,128)(2,1)S(1)} %get-tuple-element.32), channel_id=1, source_target_pairs={{0,9},{1,8},{4,13},{5,12},{8,1},{9,0},{12,5},{13,4},{2,11},{3,10},... | collective-permute-start | bytes 294920 | tf_op jit(solution)/shard_map/ppermute | solution.py:318
  38.2 3.7 %collective-permute-done.15.refs_4_ = bf16[1,64,640]{2,1,0:T(8,128)(2,1)S(1)} collective-permute-done((bf16[1,64,640]{2,1,0:T(8,128)(2,1)S(1)}, bf16[1,64,640]{2,1,0:T(8,128)(2,1)S(1)}, u32[]{:S(2)}, u32[]{:S(2)}) %collective-permute-start.15) | collective-permute-done | bytes 81952 | tf_op jit(solution)/shard_map/ppermute | solution.py:318
  41.9 0.0 collective-permute-start.11
  41.9 2.4 %collective-permute-done.16.refs_5_ = bf16[1,64,640]{2,1,0:T(8,128)(2,1)S(1)} collective-permute-done((bf16[1,64,640]{2,1,0:T(8,128)(2,1)S(1)}, bf16[1,64,640]{2,1,0:T(8,128)(2,1)S(1)}, u32[]{:S(2)}, u32[]{:S(2)}) %collective-permute-start.16) | collective-permute-done | bytes 81952 | tf_op jit(solution)/shard_map/ppermute | solution.py:318
  44.4 0.0 collective-permute-done.17.refs_6_
  44.4 0.0 copy-done.2
  44.4 0.8 %add.2.refs_4_ = bf16[2,64,2048]{2,1,0:T(8,128)(2,1)} custom-call(f32[2,2048]{1,0:T(2,128)S(1)} %copy-done.2, bf16[2,64,2048]{2,1,0:T(8,128)(2,1)S(1)} %copy-done.1, bf16[1,64,640]{2,1,0:T(8,128)(2,1)S(1)} %collective-permute-done.12.refs_0_, bf16[1,64,640]{2,1,0:T(8,128)(2,1)S(1)} %collective-permute-done.13.refs_1_, ...), custom_call_target="tpu_custom_call" | custom-call | flops 20000000000 | tf_op jit(solution)/shard_map/add/pallas_call | solution.py:285
  45.2 1.6 %collective-permute-done.9.refs_0_ = bf16[2,64,384]{2,1,0:T(8,128)(2,1)S(1)} collective-permute-done((bf16[2,64,384]{2,1,0:T(8,128)(2,1)S(1)}, bf16[2,64,384]{2,1,0:T(8,128)(2,1)S(1)}, u32[]{:S(2)}, u32[]{:S(2)}) %collective-permute-start.9) | collective-permute-done | bytes 98336 | tf_op jit(solution)/shard_map/ppermute | solution.py:318
  46.8 1.7 %collective-permute-done.10.refs_1_ = bf16[2,64,384]{2,1,0:T(8,128)(2,1)S(1)} collective-permute-done((bf16[2,64,384]{2,1,0:T(8,128)(2,1)S(1)}, bf16[2,64,384]{2,1,0:T(8,128)(2,1)S(1)}, u32[]{:S(2)}, u32[]{:S(2)}) %collective-permute-start.10) | collective-permute-done | bytes 98336 | tf_op jit(solution)/shard_map/ppermute | solution.py:318
  48.6 0.0 collective-permute-done.11.refs_2_
  48.6 0.8 %add.3 = bf16[2,64,2048]{2,1,0:T(8,128)(2,1)} custom-call(f32[2,2048]{1,0:T(2,128)S(1)} %copy-done.2, bf16[2,64,2048]{2,1,0:T(8,128)(2,1)S(1)} %copy-done.1, bf16[2,64,384]{2,1,0:T(8,128)(2,1)S(1)} %collective-permute-done.9.refs_0_, bf16[2,64,384]{2,1,0:T(8,128)(2,1)S(1)} %collective-permute-done.10.refs_1_, ...), custom_call_target="tpu_custom_call", output_to_operand_aliasing={{}: (6, {})} | custom-call | tf_op jit(solution)/shard_map/add/pallas_call | solution.py:285
  (7 shorter events, 0.1 us)
Async XLA Ops:
  0.0 15.7 %copy-start.4 = (s32[2,8]{1,0:T(2,128)S(1)}, s32[2,8]{1,0:T(2,128)}, u32[]{:S(2)}) copy-start(s32[2,8]{1,0:T(2,128)} %active_ref.1) | copy-start | bytes 196
  0.0 15.7 %copy-start.3 = (f32[512]{0:T(512)S(1)}, f32[512]{0:T(512)}, u32[]{:S(2)}) copy-start(f32[512]{0:T(512)} %param.9) | copy-start | bytes 6148
  3.2 6.6 %collective-permute-start = (bf16[128,256]{1,0:T(8,128)(2,1)S(1)}, bf16[128,256]{1,0:T(8,128)(2,1)S(1)}, u32[]{:S(2)}, u32[]{:S(2)}) collective-permute-start(bf16[128,256]{1,0:T(8,128)(2,1)S(1)} %get-tuple-element.24), channel_id=1, source_target_pairs={{0,4},{4,0},{8,12},{12,8},{1,5},{5,1},{9,13},{13,9},{2,6},{6,2},{1... | collective-permute-start | bytes 196616 | tf_op jit(solution)/shard_map/ppermute | solution.py:237
  6.3 7.3 %collective-permute-start.1 = (bf16[128,256]{1,0:T(8,128)(2,1)S(1)}, bf16[128,256]{1,0:T(8,128)(2,1)S(1)}, u32[]{:S(2)}, u32[]{:S(2)}) collective-permute-start(bf16[128,256]{1,0:T(8,128)(2,1)S(1)} %get-tuple-element.25), channel_id=1, source_target_pairs={{0,8},{4,12},{8,0},{12,4},{1,9},{5,13},{9,1},{13,5},{2,10},{6,14},... | collective-permute-start | bytes 196616 | tf_op jit(solution)/shard_map/ppermute | solution.py:237
  8.8 6.8 %collective-permute-start.2 = (bf16[128,256]{1,0:T(8,128)(2,1)S(1)}, bf16[128,256]{1,0:T(8,128)(2,1)S(1)}, u32[]{:S(2)}, u32[]{:S(2)}) collective-permute-start(bf16[128,256]{1,0:T(8,128)(2,1)S(1)} %get-tuple-element.26), channel_id=1, source_target_pairs={{0,12},{4,8},{8,4},{12,0},{1,13},{5,9},{9,5},{13,1},{2,14},{6,10},... | collective-permute-start | bytes 196616 | tf_op jit(solution)/shard_map/ppermute | solution.py:237
  8.8 11.0 %collective-permute-start.7 = (bf16[1,2,128,640]{3,2,1,0:T(8,128)(2,1)S(1)}, bf16[1,2,128,640]{3,2,1,0:T(8,128)(2,1)S(1)}, u32[]{:S(2)}, u32[]{:S(2)}) collective-permute-start(bf16[1,2,128,640]{3,2,1,0:T(8,128)(2,1)S(1)} %get-tuple-element.28), channel_id=1, source_target_pairs={{0,4},{4,0},{8,12},{12,8},{1,5},{5,1},{9,13},{13,9},{2,6},{6,2},{1... | collective-permute-start | bytes 983048 | tf_op jit(solution)/shard_map/ppermute | solution.py:277
  16.3 5.1 %collective-permute-start.5 = (bf16[2,64,256]{2,1,0:T(8,128)(2,1)S(1)}, bf16[2,64,256]{2,1,0:T(8,128)(2,1)S(1)}, u32[]{:S(2)}, u32[]{:S(2)}) collective-permute-start(bf16[2,64,256]{2,1,0:T(8,128)(2,1)S(1)} %codes.1.refs_0_.refs_1_), channel_id=1, source_target_pairs={{0,3},{1,2},{2,1},{3,0},{4,7},{5,6},{6,5},{7,4},{8,11},{9,10},{10,... | collective-permute-start | bytes 196616 | tf_op jit(solution)/shard_map/ppermute | solution.py:253
  16.4 5.8 %collective-permute-start.4 = (bf16[2,64,256]{2,1,0:T(8,128)(2,1)S(1)}, bf16[2,64,256]{2,1,0:T(8,128)(2,1)S(1)}, u32[]{:S(2)}, u32[]{:S(2)}) collective-permute-start(bf16[2,64,256]{2,1,0:T(8,128)(2,1)S(1)} %codes.1.refs_0_.refs_1_), channel_id=1, source_target_pairs={{0,2},{1,3},{2,0},{3,1},{4,6},{5,7},{6,4},{7,5},{8,10},{9,11},{10,... | collective-permute-start | bytes 196616 | tf_op jit(solution)/shard_map/ppermute | solution.py:253
  17.9 4.2 %collective-permute-start.3 = (bf16[2,64,256]{2,1,0:T(8,128)(2,1)S(1)}, bf16[2,64,256]{2,1,0:T(8,128)(2,1)S(1)}, u32[]{:S(2)}, u32[]{:S(2)}) collective-permute-start(bf16[2,64,256]{2,1,0:T(8,128)(2,1)S(1)} %codes.1.refs_0_.refs_1_), channel_id=1, source_target_pairs={{0,1},{1,0},{2,3},{3,2},{4,5},{5,4},{6,7},{7,6},{8,9},{9,8},{10,11... | collective-permute-start | bytes 196616 | tf_op jit(solution)/shard_map/ppermute | solution.py:253
  18.2 4.0 %copy-start = (bf16[2,2,128,2048]{3,2,1,0:T(8,128)(2,1)S(1)}, bf16[2,2,128,2048]{3,2,1,0:T(8,128)(2,1)}, u32[]{:S(2)}) copy-start(bf16[2,2,128,2048]{3,2,1,0:T(8,128)(2,1)} %dec_ref.5) | copy-start | bytes 6291460
  18.2 14.8 %collective-permute-start.6 = (bf16[2,2,128,384]{3,2,1,0:T(8,128)(2,1)S(1)}, bf16[2,2,128,384]{3,2,1,0:T(8,128)(2,1)S(1)}, u32[]{:S(2)}, u32[]{:S(2)}) collective-permute-start(bf16[2,2,128,384]{3,2,1,0:T(8,128)(2,1)S(1)} %hold.1), channel_id=1, source_target_pairs={{0,4},{4,0},{8,12},{12,8},{1,5},{5,1},{9,13},{13,9},{2,6},{6,2},{1... | collective-permute-start | bytes 1179656 | tf_op jit(solution)/shard_map/ppermute | solution.py:279
  19.8 8.4 %collective-permute-start.8 = (bf16[1,2,128,640]{3,2,1,0:T(8,128)(2,1)S(1)}, bf16[1,2,128,640]{3,2,1,0:T(8,128)(2,1)S(1)}, u32[]{:S(2)}, u32[]{:S(2)}) collective-permute-start(bf16[1,2,128,640]{3,2,1,0:T(8,128)(2,1)S(1)} %collective-permute-done.7.got_ref), channel_id=1, source_target_pairs={{0,16},{16,0},{1,17},{17,1},{2,18},{18,2},{3,19},{19,3},{4,20},{20... | collective-permute-start | bytes 983048 | tf_op jit(solution)/shard_map/ppermute | solution.py:278
  22.6 7.6 %collective-permute-start.12 = (bf16[1,64,640]{2,1,0:T(8,128)(2,1)S(1)}, bf16[1,64,640]{2,1,0:T(8,128)(2,1)S(1)}, u32[]{:S(2)}, u32[]{:S(2)}) collective-permute-start(bf16[1,64,640]{2,1,0:T(8,128)(2,1)S(1)} %get-tuple-element.35), channel_id=1, source_target_pairs={{0,8},{1,9},{4,12},{5,13},{8,0},{9,1},{12,4},{13,5},{2,10},{3,11},... | collective-permute-start | bytes 245768 | tf_op jit(solution)/shard_map/ppermute | solution.py:318
  23.6 9.9 %collective-permute-start.13 = (bf16[1,64,640]{2,1,0:T(8,128)(2,1)S(1)}, bf16[1,64,640]{2,1,0:T(8,128)(2,1)S(1)}, u32[]{:S(2)}, u32[]{:S(2)}) collective-permute-start(bf16[1,64,640]{2,1,0:T(8,128)(2,1)S(1)} %get-tuple-element.36), channel_id=1, source_target_pairs={{0,9},{1,8},{4,13},{5,12},{8,1},{9,0},{12,5},{13,4},{2,11},{3,10},... | collective-permute-start | bytes 245768 | tf_op jit(solution)/shard_map/ppermute | solution.py:318
  25.0 8.9 %collective-permute-start.14 = (bf16[1,64,640]{2,1,0:T(8,128)(2,1)S(1)}, bf16[1,64,640]{2,1,0:T(8,128)(2,1)S(1)}, u32[]{:S(2)}, u32[]{:S(2)}) collective-permute-start(bf16[1,64,640]{2,1,0:T(8,128)(2,1)S(1)} %get-tuple-element.37), channel_id=1, source_target_pairs={{0,1},{1,0},{4,5},{5,4},{8,9},{9,8},{12,13},{13,12},{2,3},{3,2},{6... | collective-permute-start | bytes 245768 | tf_op jit(solution)/shard_map/ppermute | solution.py:318
  28.6 15.7 %copy-start.1 = (bf16[2,64,2048]{2,1,0:T(8,128)(2,1)S(1)}, bf16[2,64,2048]{2,1,0:T(8,128)(2,1)}, u32[]{:S(2)}) copy-start(bf16[2,64,2048]{2,1,0:T(8,128)(2,1)} %target_ref.3) | copy-start | bytes 1572868
  28.6 15.7 %copy-start.2 = (f32[2,2048]{1,0:T(2,128)S(1)}, f32[2,2048]{1,0:T(2,128)}, u32[]{:S(2)}) copy-start(f32[2,2048]{1,0:T(2,128)} %bias_ref.3) | copy-start | bytes 49156
  28.7 13.3 %collective-permute-start.15 = (bf16[1,64,640]{2,1,0:T(8,128)(2,1)S(1)}, bf16[1,64,640]{2,1,0:T(8,128)(2,1)S(1)}, u32[]{:S(2)}, u32[]{:S(2)}) collective-permute-start(bf16[1,64,640]{2,1,0:T(8,128)(2,1)S(1)} %get-tuple-element.38), channel_id=1, source_target_pairs={{0,8},{1,9},{4,12},{5,13},{8,0},{9,1},{12,4},{13,5},{2,10},{3,11},... | collective-permute-start | bytes 245768 | tf_op jit(solution)/shard_map/ppermute | solution.py:318
  30.2 14.1 %collective-permute-start.16 = (bf16[1,64,640]{2,1,0:T(8,128)(2,1)S(1)}, bf16[1,64,640]{2,1,0:T(8,128)(2,1)S(1)}, u32[]{:S(2)}, u32[]{:S(2)}) collective-permute-start(bf16[1,64,640]{2,1,0:T(8,128)(2,1)S(1)} %get-tuple-element.39), channel_id=1, source_target_pairs={{0,9},{1,8},{4,13},{5,12},{8,1},{9,0},{12,5},{13,4},{2,11},{3,10},... | collective-permute-start | bytes 245768 | tf_op jit(solution)/shard_map/ppermute | solution.py:318
  33.0 11.3 %collective-permute-start.17 = (bf16[1,64,640]{2,1,0:T(8,128)(2,1)S(1)}, bf16[1,64,640]{2,1,0:T(8,128)(2,1)S(1)}, u32[]{:S(2)}, u32[]{:S(2)}) collective-permute-start(bf16[1,64,640]{2,1,0:T(8,128)(2,1)S(1)} %get-tuple-element.40), channel_id=1, source_target_pairs={{0,1},{1,0},{4,5},{5,4},{8,9},{9,8},{12,13},{13,12},{2,3},{3,2},{6... | collective-permute-start | bytes 245768 | tf_op jit(solution)/shard_map/ppermute | solution.py:318
  33.5 13.4 %collective-permute-start.9 = (bf16[2,64,384]{2,1,0:T(8,128)(2,1)S(1)}, bf16[2,64,384]{2,1,0:T(8,128)(2,1)S(1)}, u32[]{:S(2)}, u32[]{:S(2)}) collective-permute-start(bf16[2,64,384]{2,1,0:T(8,128)(2,1)S(1)} %get-tuple-element.31), channel_id=1, source_target_pairs={{0,8},{1,9},{4,12},{5,13},{8,0},{9,1},{12,4},{13,5},{2,10},{3,11},... | collective-permute-start | bytes 294920 | tf_op jit(solution)/shard_map/ppermute | solution.py:318
  33.9 14.7 %collective-permute-start.10 = (bf16[2,64,384]{2,1,0:T(8,128)(2,1)S(1)}, bf16[2,64,384]{2,1,0:T(8,128)(2,1)S(1)}, u32[]{:S(2)}, u32[]{:S(2)}) collective-permute-start(bf16[2,64,384]{2,1,0:T(8,128)(2,1)S(1)} %get-tuple-element.32), channel_id=1, source_target_pairs={{0,9},{1,8},{4,13},{5,12},{8,1},{9,0},{12,5},{13,4},{2,11},{3,10},... | collective-permute-start | bytes 294920 | tf_op jit(solution)/shard_map/ppermute | solution.py:318
  41.9 6.7 %collective-permute-start.11 = (bf16[2,64,384]{2,1,0:T(8,128)(2,1)S(1)}, bf16[2,64,384]{2,1,0:T(8,128)(2,1)S(1)}, u32[]{:S(2)}, u32[]{:S(2)}) collective-permute-start(bf16[2,64,384]{2,1,0:T(8,128)(2,1)S(1)} %get-tuple-element.33), channel_id=1, source_target_pairs={{0,1},{1,0},{4,5},{5,4},{8,9},{9,8},{12,13},{13,12},{2,3},{3,2},{6... | collective-permute-start | bytes 294920 | tf_op jit(solution)/shard_map/ppermute | solution.py:318

commit v16 on v15

--- a/solution.py
+++ b/solution.py
@@ -81,6 +81,11 @@
         copy.wait()
 
 
+def part_kernel(piece, before_ref, dec_hbm, after_ref, part_ref, sems):
+    for copy in part_copies(piece, dec_hbm, part_ref, sems):
+        copy.wait()
+
+
 def codes_kernel(n, share, tile_rows, active_ref, bias_ref, *refs):
     term_refs, out_ref = refs[:n], refs[n]
     src = lax.axis_index("src")
@@ -216,15 +221,15 @@
         return jax.ShapeDtypeStruct(extent, kind)
 
     results = pl.pallas_call(
-        functools.partial(encode_kernel, n, fetched),
+        functools.partial(encode_kernel, n, fetched[:1]),
         out_shape=[shape(half * share, 2 * block)] * n
-        + [shape(len(offsets), groups, block, width) for offsets, _, width, _ in fetched],
+        + [shape(len(offsets), groups, block, width) for offsets, _, width, _ in fetched[:1]],
         in_specs=[anywhere] * 3,
-        out_specs=[vmem] * (n + len(fetched)),
+        out_specs=[vmem] * (n + 1),
         scratch_shapes=[
             pltpu.VMEM((2, half, share, features), jnp.bfloat16),
             pltpu.VMEM(enc_w.shape, jnp.bfloat16),
-            pltpu.SemaphoreType.DMA((len(fetched), layers * groups)),
+            pltpu.SemaphoreType.DMA((1, layers * groups)),
             pltpu.SemaphoreType.DMA((2 * half,)),
             pltpu.SemaphoreType.DMA((8,)),
         ],
@@ -235,6 +240,7 @@
     terms, parts = list(results[:n]), list(results[n:])
     for k in range(1, n):
         terms[k] = lax.ppermute(terms[k], "src", [(i, peer(i, k, n)) for i in range(n)])
+    order = [0, half, *(k for k in range(1, n) if k != half)]
     own = pl.pallas_call(
         functools.partial(codes_kernel, n, share, tile_rows),
         out_shape=shape(half, share, 2 * block),
@@ -243,7 +249,7 @@
         compiler_params=params,
         cost_estimate=weight(20),
         name="codes",
-    )(active, enc_b.reshape(n, block), *terms)
+    )(active, enc_b.reshape(n, block), *[terms[k] for k in order])
     codes = []
     for k in range(groups):
         for r in range(2):
@@ -262,21 +268,20 @@
         name="gather",
     )(*codes)
 
-    def hold(value, after):
-        return pl.pallas_call(
-            lambda *refs: None,
-            out_shape=jax.ShapeDtypeStruct(value.shape, value.dtype),
-            in_specs=[anywhere] * 2,
-            out_specs=anywhere,
-            input_output_aliases={0: 0},
-            compiler_params=params,
-            cost_estimate=cost,
-            name="hold",
-        )(value, after)
+    part = pl.pallas_call(
+        functools.partial(part_kernel, fetched[1]),
+        out_shape=shape(len(fetched[1][0]), groups, block, fetched[1][2]),
+        in_specs=[anywhere] * 3,
+        out_specs=vmem,
+        scratch_shapes=[pltpu.SemaphoreType.DMA((layers * groups,))],
+        compiler_params=params,
+        cost_estimate=weight(0),
+        name="part",
+    )(parts[0], dec_w, own)
 
     got = [lax.ppermute(parts[0], "src", pair)]
     got.append(lax.ppermute(got[0], "parts", [(0, 1), (1, 0)]))
-    got.append(lax.ppermute(hold(parts[1], own), "src", pair))
+    got.append(lax.ppermute(part, "src", pair))
 
     def add(some, begun, billions):
         operands = [value for i in some for value in sums[i]]

time: 49.5 us -> 50.2 us (1.014)
  starting transfers between devices: 20.9 us -> 19.3 us
  waiting for transfers between devices: 21.7 us -> 23.2 us
  Pallas kernels: 6.57 us -> 7.41 us
    ppermute x9, starting transfers between devices: 10.9 us -> 9.1 us  [body(): sums[i].append(lax.ppermute(terms[2 * j + r], ('src', 'rep'), perm))]
    ppermute x9, waiting for transfers between devices: 9.54 us -> 11.1 us  [body(): sums[i].append(lax.ppermute(terms[2 * j + r], ('src', 'rep'), perm))]
    ppermute x1, waiting for transfers between devices: 1.6 us -> 0.43 us  [body(): got = [lax.ppermute(parts[0], 'src', pair)]]
    ppermute x1, waiting for transfers between devices: 2.53 us -> 3.59 us  [body(): got.append(lax.ppermute(got[0], 'parts', [(0, 1), (1, 0)]))]
    pallas_call x2, Pallas kernels: 3.16 us -> 4 us  [the longest x1 2.93 us: body(): pl.pallas_call(functools.partial(encode_kernel, n, fetched[:1]), out_shap...]
  transfers between devices with their start and end apart: 18 -> 18, of which waited for: 10 -> 11; matrix products, arithmetic and copies ran while one was open for 0% -> 0% of each run, Pallas kernels for 5% -> 7%
where the time goes in v16:
time: 50.2 us; the launch traced here: 50 us
  waiting for transfers between devices  23.2 us (46%)
  starting transfers between devices  19.3 us (38%)
  Pallas kernels  7.41 us (15%)
    ppermute x9, waiting for transfers between devices, body(): sums[i].append(lax.ppermute(terms[2 * j + r], ('src', 'rep'), perm))  11.1 us
    ppermute x9, starting transfers between devices, body(): sums[i].append(lax.ppermute(terms[2 * j + r], ('src', 'rep'), perm))  9.1 us
    ppermute x3, waiting for transfers between devices, body(): lax.ppermute(terms[k], 'src', [(i, peer(i, k, n)) for i in range(n)])  5.92 us
    ppermute x3, starting transfers between devices, body(): lax.ppermute(terms[k], 'src', [(i, peer(i, k, n)) for i in range(n)])  5.68 us
    ppermute x1, waiting for transfers between devices, body(): got.append(lax.ppermute(got[0], 'parts', [(0, 1), (1, 0)]))  3.59 us
    pallas_call x1, Pallas kernels, body(): pl.pallas_call(functools.partial(encode_kernel, n, fetched[:1]), out_shap...  2.93 us
    ppermute x3, starting transfers between devices, body(): codes.append(lax.ppermute(own, ('tgt', 'rep'), perm) if k + r else own)  1.92 us
    ppermute x1, starting transfers between devices, body(): got.append(lax.ppermute(got[0], 'parts', [(0, 1), (1, 0)]))  1.6 us
  transfers between devices with their start and end apart: 18, of which 11 were waited for; matrix products, arithmetic and copies ran while one was open for 0% of the time, Pallas kernels for 7%

profile of v16, /device:TPU:0, one launch (start us, length us, event | category | flops | bytes accessed | tf_op | source)
XLA Modules:
  0.0 50.0 jit_solution(16212862539421942681)
XLA Ops:
  0.0 2.9 %encode.1 = (bf16[128,256]{1,0:T(8,128)(2,1)S(1)}, bf16[128,256]{1,0:T(8,128)(2,1)S(1)}, bf16[128,256]{1,0:T(8,128)(2,1)S(1)}, bf16[128,256]{1,0:T(8,128)(2,1)S(1)}, bf16[1,2,128,640]{3,2,1,0:T(8,128)(2,1)S(1)}) custom-call(bf16[2,2,64,1024]{3,2,1,0:T(8,128)(2,1)} %bitcast.3, bf16[1024,512]{1,0:T(8,128)(2,1)} %w_hbm.1, bf16[2,2,128,2048]{3,2,1,0:T(8,128)(2,1)} %dec_ref.5), custom_call_target="tpu_custom_call" | custom-call | tf_op jit(solution)/shard_map/encode/pallas_call | solution.py:223
  2.9 4.1 %collective-permute-start = (bf16[128,256]{1,0:T(8,128)(2,1)S(1)}, bf16[128,256]{1,0:T(8,128)(2,1)S(1)}, u32[]{:S(2)}, u32[]{:S(2)}) collective-permute-start(bf16[128,256]{1,0:T(8,128)(2,1)S(1)} %get-tuple-element.23), channel_id=1, source_target_pairs={{0,8},{4,12},{8,0},{12,4},{1,9},{5,13},{9,1},{13,5},{2,10},{6,14},... | collective-permute-start | bytes 196616 | tf_op jit(solution)/shard_map/ppermute | solution.py:242
  7.0 1.6 %collective-permute-start.1 = (bf16[128,256]{1,0:T(8,128)(2,1)S(1)}, bf16[128,256]{1,0:T(8,128)(2,1)S(1)}, u32[]{:S(2)}, u32[]{:S(2)}) collective-permute-start(bf16[128,256]{1,0:T(8,128)(2,1)S(1)} %get-tuple-element.24), channel_id=1, source_target_pairs={{0,4},{4,0},{8,12},{12,8},{1,5},{5,1},{9,13},{13,9},{2,6},{6,2},{1... | collective-permute-start | bytes 196616 | tf_op jit(solution)/shard_map/ppermute | solution.py:242
  8.6 0.0 collective-permute-start.2
  8.6 0.9 %collective-permute-start.7 = (bf16[1,2,128,640]{3,2,1,0:T(8,128)(2,1)S(1)}, bf16[1,2,128,640]{3,2,1,0:T(8,128)(2,1)S(1)}, u32[]{:S(2)}, u32[]{:S(2)}) collective-permute-start(bf16[1,2,128,640]{3,2,1,0:T(8,128)(2,1)S(1)} %get-tuple-element.26.before_ref), channel_id=1, source_target_pairs={{0,4},{4,0},{8,12},{12,8},{1,5},{5,1},{9,13},{13,9},{2,6},{6,2},{1... | collective-permute-start | bytes 983048 | tf_op jit(solution)/shard_map/ppermute | solution.py:282
  9.5 0.6 %collective-permute-done.refs_1_ = bf16[128,256]{1,0:T(8,128)(2,1)S(1)} collective-permute-done((bf16[128,256]{1,0:T(8,128)(2,1)S(1)}, bf16[128,256]{1,0:T(8,128)(2,1)S(1)}, u32[]{:S(2)}, u32[]{:S(2)}) %collective-permute-start) | collective-permute-done | bytes 65568 | tf_op jit(solution)/shard_map/ppermute | solution.py:242
  10.1 1.9 %collective-permute-done.1.refs_2_ = bf16[128,256]{1,0:T(8,128)(2,1)S(1)} collective-permute-done((bf16[128,256]{1,0:T(8,128)(2,1)S(1)}, bf16[128,256]{1,0:T(8,128)(2,1)S(1)}, u32[]{:S(2)}, u32[]{:S(2)}) %collective-permute-start.1) | collective-permute-done | bytes 65568 | tf_op jit(solution)/shard_map/ppermute | solution.py:242
  12.0 3.5 %collective-permute-done.2.refs_3_ = bf16[128,256]{1,0:T(8,128)(2,1)S(1)} collective-permute-done((bf16[128,256]{1,0:T(8,128)(2,1)S(1)}, bf16[128,256]{1,0:T(8,128)(2,1)S(1)}, u32[]{:S(2)}, u32[]{:S(2)}) %collective-permute-start.2) | collective-permute-done | bytes 65568 | tf_op jit(solution)/shard_map/ppermute | solution.py:242
  15.5 0.0 copy-done.3
  15.5 0.6 %codes.1.refs_0_.after_ref = bf16[2,64,256]{2,1,0:T(8,128)(2,1)S(1)} custom-call(s32[2,8]{1,0:T(2,128)S(1)} %copy-done.4, f32[4,128]{1,0:T(4,128)S(1)} %bitcast.2, bf16[128,256]{1,0:T(8,128)(2,1)S(1)} %get-tuple-element.22.refs_0_, bf16[128,256]{1,0:T(8,128)(2,1)S(1)} %collective-permute-done.refs_1_, bf16[128,256]{1,0:T(8,128)(2,1)S(1)} %collective-permute-done.1.refs_2_, ...), custom_call_target="tpu_custom_call" | custom-call | flops 20000000000 | tf_op jit(solution)/shard_map/codes/pallas_call | solution.py:244
  16.1 0.1 collective-permute-start.5
  16.2 1.6 %collective-permute-start.4 = (bf16[2,64,256]{2,1,0:T(8,128)(2,1)S(1)}, bf16[2,64,256]{2,1,0:T(8,128)(2,1)S(1)}, u32[]{:S(2)}, u32[]{:S(2)}) collective-permute-start(bf16[2,64,256]{2,1,0:T(8,128)(2,1)S(1)} %codes.1.refs_0_.after_ref), channel_id=1, source_target_pairs={{0,2},{1,3},{2,0},{3,1},{4,6},{5,7},{6,4},{7,5},{8,10},{9,11},{10,... | collective-permute-start | bytes 196616 | tf_op jit(solution)/shard_map/ppermute | solution.py:259
  17.7 0.3 collective-permute-start.3
  18.0 1.1 %part.1 = bf16[2,2,128,384]{3,2,1,0:T(8,128)(2,1)S(1)} custom-call(bf16[1,2,128,640]{3,2,1,0:T(8,128)(2,1)S(1)} %get-tuple-element.26.before_ref, bf16[2,2,128,2048]{3,2,1,0:T(8,128)(2,1)} %dec_ref.5, bf16[2,64,256]{2,1,0:T(8,128)(2,1)S(1)} %codes.1.refs_0_.after_ref), custom_call_target="tpu_custom_call" | custom-call | tf_op jit(solution)/shard_map/part/pallas_call | solution.py:271
  19.1 0.0 copy-start
  19.1 0.1 collective-permute-start.6
  19.2 0.4 collective-permute-done.7.got_ref
  19.6 1.6 %collective-permute-start.8 = (bf16[1,2,128,640]{3,2,1,0:T(8,128)(2,1)S(1)}, bf16[1,2,128,640]{3,2,1,0:T(8,128)(2,1)S(1)}, u32[]{:S(2)}, u32[]{:S(2)}) collective-permute-start(bf16[1,2,128,640]{3,2,1,0:T(8,128)(2,1)S(1)} %collective-permute-done.7.got_ref), channel_id=1, source_target_pairs={{0,16},{16,0},{1,17},{17,1},{2,18},{18,2},{3,19},{19,3},{4,20},{20... | collective-permute-start | bytes 983048 | tf_op jit(solution)/shard_map/ppermute | solution.py:283
  21.2 0.0 collective-permute-done.5.refs_3_
  21.2 0.7 %collective-permute-done.4.refs_2_ = bf16[2,64,256]{2,1,0:T(8,128)(2,1)S(1)} collective-permute-done((bf16[2,64,256]{2,1,0:T(8,128)(2,1)S(1)}, bf16[2,64,256]{2,1,0:T(8,128)(2,1)S(1)}, u32[]{:S(2)}, u32[]{:S(2)}) %collective-permute-start.4) | collective-permute-done | bytes 65568 | tf_op jit(solution)/shard_map/ppermute | solution.py:259
  21.9 0.0 collective-permute-done.3.refs_1_
  22.0 0.4 decode.3
  22.4 0.9 %collective-permute-start.12 = (bf16[1,64,640]{2,1,0:T(8,128)(2,1)S(1)}, bf16[1,64,640]{2,1,0:T(8,128)(2,1)S(1)}, u32[]{:S(2)}, u32[]{:S(2)}) collective-permute-start(bf16[1,64,640]{2,1,0:T(8,128)(2,1)S(1)} %get-tuple-element.33), channel_id=1, source_target_pairs={{0,8},{1,9},{4,12},{5,13},{8,0},{9,1},{12,4},{13,5},{2,10},{3,11},... | collective-permute-start | bytes 245768 | tf_op jit(solution)/shard_map/ppermute | solution.py:323
  23.3 1.4 %collective-permute-start.13 = (bf16[1,64,640]{2,1,0:T(8,128)(2,1)S(1)}, bf16[1,64,640]{2,1,0:T(8,128)(2,1)S(1)}, u32[]{:S(2)}, u32[]{:S(2)}) collective-permute-start(bf16[1,64,640]{2,1,0:T(8,128)(2,1)S(1)} %get-tuple-element.34), channel_id=1, source_target_pairs={{0,9},{1,8},{4,13},{5,12},{8,1},{9,0},{12,5},{13,4},{2,11},{3,10},... | collective-permute-start | bytes 245768 | tf_op jit(solution)/shard_map/ppermute | solution.py:323
  24.8 0.7 %collective-permute-start.14 = (bf16[1,64,640]{2,1,0:T(8,128)(2,1)S(1)}, bf16[1,64,640]{2,1,0:T(8,128)(2,1)S(1)}, u32[]{:S(2)}, u32[]{:S(2)}) collective-permute-start(bf16[1,64,640]{2,1,0:T(8,128)(2,1)S(1)} %get-tuple-element.35), channel_id=1, source_target_pairs={{0,1},{1,0},{4,5},{5,4},{8,9},{9,8},{12,13},{13,12},{2,3},{3,2},{6... | collective-permute-start | bytes 245768 | tf_op jit(solution)/shard_map/ppermute | solution.py:323
  25.5 3.6 %collective-permute-done.8.got_ref = bf16[1,2,128,640]{3,2,1,0:T(8,128)(2,1)S(1)} collective-permute-done((bf16[1,2,128,640]{3,2,1,0:T(8,128)(2,1)S(1)}, bf16[1,2,128,640]{3,2,1,0:T(8,128)(2,1)S(1)}, u32[]{:S(2)}, u32[]{:S(2)}) %collective-permute-start.8) | collective-permute-done | bytes 327712 | tf_op jit(solution)/shard_map/ppermute | solution.py:283
  29.1 0.4 decode.4
  29.5 0.0 copy-start.1
  29.5 0.0 copy-start.2
  29.5 1.7 %collective-permute-start.15 = (bf16[1,64,640]{2,1,0:T(8,128)(2,1)S(1)}, bf16[1,64,640]{2,1,0:T(8,128)(2,1)S(1)}, u32[]{:S(2)}, u32[]{:S(2)}) collective-permute-start(bf16[1,64,640]{2,1,0:T(8,128)(2,1)S(1)} %get-tuple-element.36), channel_id=1, source_target_pairs={{0,8},{1,9},{4,12},{5,13},{8,0},{9,1},{12,4},{13,5},{2,10},{3,11},... | collective-permute-start | bytes 245768 | tf_op jit(solution)/shard_map/ppermute | solution.py:323
  31.1 0.0 collective-permute-done.12.refs_0_
  31.1 1.5 %collective-permute-start.16 = (bf16[1,64,640]{2,1,0:T(8,128)(2,1)S(1)}, bf16[1,64,640]{2,1,0:T(8,128)(2,1)S(1)}, u32[]{:S(2)}, u32[]{:S(2)}) collective-permute-start(bf16[1,64,640]{2,1,0:T(8,128)(2,1)S(1)} %get-tuple-element.37), channel_id=1, source_target_pairs={{0,9},{1,8},{4,13},{5,12},{8,1},{9,0},{12,5},{13,4},{2,11},{3,10},... | collective-permute-start | bytes 245768 | tf_op jit(solution)/shard_map/ppermute | solution.py:323
  32.7 1.4 %collective-permute-done.6.got_ref = bf16[2,2,128,384]{3,2,1,0:T(8,128)(2,1)S(1)} collective-permute-done((bf16[2,2,128,384]{3,2,1,0:T(8,128)(2,1)S(1)}, bf16[2,2,128,384]{3,2,1,0:T(8,128)(2,1)S(1)}, u32[]{:S(2)}, u32[]{:S(2)}) %collective-permute-start.6) | collective-permute-done | bytes 393248 | tf_op jit(solution)/shard_map/ppermute | solution.py:284
  34.0 0.0 collective-permute-start.17
  34.0 0.4 decode.5
  34.4 0.0 collective-permute-done.13.refs_1_
  34.5 0.3 collective-permute-start.9
  34.8 0.0 collective-permute-done.14.refs_2_
  34.8 2.5 %collective-permute-start.10 = (bf16[2,64,384]{2,1,0:T(8,128)(2,1)S(1)}, bf16[2,64,384]{2,1,0:T(8,128)(2,1)S(1)}, u32[]{:S(2)}, u32[]{:S(2)}) collective-permute-start(bf16[2,64,384]{2,1,0:T(8,128)(2,1)S(1)} %get-tuple-element.30), channel_id=1, source_target_pairs={{0,9},{1,8},{4,13},{5,12},{8,1},{9,0},{12,5},{13,4},{2,11},{3,10},... | collective-permute-start | bytes 294920 | tf_op jit(solution)/shard_map/ppermute | solution.py:323
  37.3 6.2 %collective-permute-done.15.refs_4_ = bf16[1,64,640]{2,1,0:T(8,128)(2,1)S(1)} collective-permute-done((bf16[1,64,640]{2,1,0:T(8,128)(2,1)S(1)}, bf16[1,64,640]{2,1,0:T(8,128)(2,1)S(1)}, u32[]{:S(2)}, u32[]{:S(2)}) %collective-permute-start.15) | collective-permute-done | bytes 81952 | tf_op jit(solution)/shard_map/ppermute | solution.py:323
  43.5 0.0 collective-permute-start.11
  43.5 1.6 %collective-permute-done.16.refs_5_ = bf16[1,64,640]{2,1,0:T(8,128)(2,1)S(1)} collective-permute-done((bf16[1,64,640]{2,1,0:T(8,128)(2,1)S(1)}, bf16[1,64,640]{2,1,0:T(8,128)(2,1)S(1)}, u32[]{:S(2)}, u32[]{:S(2)}) %collective-permute-start.16) | collective-permute-done | bytes 81952 | tf_op jit(solution)/shard_map/ppermute | solution.py:323
  45.0 0.0 collective-permute-done.17.refs_6_
  45.0 0.8 %add.2.refs_4_ = bf16[2,64,2048]{2,1,0:T(8,128)(2,1)} custom-call(f32[2,2048]{1,0:T(2,128)S(1)} %copy-done.2, bf16[2,64,2048]{2,1,0:T(8,128)(2,1)S(1)} %copy-done.1, bf16[1,64,640]{2,1,0:T(8,128)(2,1)S(1)} %collective-permute-done.12.refs_0_, bf16[1,64,640]{2,1,0:T(8,128)(2,1)S(1)} %collective-permute-done.13.refs_1_, ...), custom_call_target="tpu_custom_call" | custom-call | flops 20000000000 | tf_op jit(solution)/shard_map/add/pallas_call | solution.py:290
  45.9 1.5 %collective-permute-done.9.refs_0_ = bf16[2,64,384]{2,1,0:T(8,128)(2,1)S(1)} collective-permute-done((bf16[2,64,384]{2,1,0:T(8,128)(2,1)S(1)}, bf16[2,64,384]{2,1,0:T(8,128)(2,1)S(1)}, u32[]{:S(2)}, u32[]{:S(2)}) %collective-permute-start.9) | collective-permute-done | bytes 98336 | tf_op jit(solution)/shard_map/ppermute | solution.py:323
  47.3 1.9 %collective-permute-done.10.refs_1_ = bf16[2,64,384]{2,1,0:T(8,128)(2,1)S(1)} collective-permute-done((bf16[2,64,384]{2,1,0:T(8,128)(2,1)S(1)}, bf16[2,64,384]{2,1,0:T(8,128)(2,1)S(1)}, u32[]{:S(2)}, u32[]{:S(2)}) %collective-permute-start.10) | collective-permute-done | bytes 98336 | tf_op jit(solution)/shard_map/ppermute | solution.py:323
  49.2 0.0 collective-permute-done.11.refs_2_
  49.2 0.8 %add.3 = bf16[2,64,2048]{2,1,0:T(8,128)(2,1)} custom-call(f32[2,2048]{1,0:T(2,128)S(1)} %copy-done.2, bf16[2,64,2048]{2,1,0:T(8,128)(2,1)S(1)} %copy-done.1, bf16[2,64,384]{2,1,0:T(8,128)(2,1)S(1)} %collective-permute-done.9.refs_0_, bf16[2,64,384]{2,1,0:T(8,128)(2,1)S(1)} %collective-permute-done.10.refs_1_, ...), custom_call_target="tpu_custom_call", output_to_operand_aliasing={{}: (6, {})} | custom-call | tf_op jit(solution)/shard_map/add/pallas_call | solution.py:290
  (7 shorter events, 0.1 us)
Async XLA Ops:
  0.0 15.4 %copy-start.4 = (s32[2,8]{1,0:T(2,128)S(1)}, s32[2,8]{1,0:T(2,128)}, u32[]{:S(2)}) copy-start(s32[2,8]{1,0:T(2,128)} %active_ref.1) | copy-start | bytes 196
  0.0 15.5 %copy-start.3 = (f32[512]{0:T(512)S(1)}, f32[512]{0:T(512)}, u32[]{:S(2)}) copy-start(f32[512]{0:T(512)} %param.9) | copy-start | bytes 6148
  2.9 7.1 %collective-permute-start = (bf16[128,256]{1,0:T(8,128)(2,1)S(1)}, bf16[128,256]{1,0:T(8,128)(2,1)S(1)}, u32[]{:S(2)}, u32[]{:S(2)}) collective-permute-start(bf16[128,256]{1,0:T(8,128)(2,1)S(1)} %get-tuple-element.23), channel_id=1, source_target_pairs={{0,8},{4,12},{8,0},{12,4},{1,9},{5,13},{9,1},{13,5},{2,10},{6,14},... | collective-permute-start | bytes 196616 | tf_op jit(solution)/shard_map/ppermute | solution.py:242
  7.0 5.0 %collective-permute-start.1 = (bf16[128,256]{1,0:T(8,128)(2,1)S(1)}, bf16[128,256]{1,0:T(8,128)(2,1)S(1)}, u32[]{:S(2)}, u32[]{:S(2)}) collective-permute-start(bf16[128,256]{1,0:T(8,128)(2,1)S(1)} %get-tuple-element.24), channel_id=1, source_target_pairs={{0,4},{4,0},{8,12},{12,8},{1,5},{5,1},{9,13},{13,9},{2,6},{6,2},{1... | collective-permute-start | bytes 196616 | tf_op jit(solution)/shard_map/ppermute | solution.py:242
  8.6 6.8 %collective-permute-start.2 = (bf16[128,256]{1,0:T(8,128)(2,1)S(1)}, bf16[128,256]{1,0:T(8,128)(2,1)S(1)}, u32[]{:S(2)}, u32[]{:S(2)}) collective-permute-start(bf16[128,256]{1,0:T(8,128)(2,1)S(1)} %get-tuple-element.25), channel_id=1, source_target_pairs={{0,12},{4,8},{8,4},{12,0},{1,13},{5,9},{9,5},{13,1},{2,14},{6,10},... | collective-permute-start | bytes 196616 | tf_op jit(solution)/shard_map/ppermute | solution.py:242
  8.6 11.0 %collective-permute-start.7 = (bf16[1,2,128,640]{3,2,1,0:T(8,128)(2,1)S(1)}, bf16[1,2,128,640]{3,2,1,0:T(8,128)(2,1)S(1)}, u32[]{:S(2)}, u32[]{:S(2)}) collective-permute-start(bf16[1,2,128,640]{3,2,1,0:T(8,128)(2,1)S(1)} %get-tuple-element.26.before_ref), channel_id=1, source_target_pairs={{0,4},{4,0},{8,12},{12,8},{1,5},{5,1},{9,13},{13,9},{2,6},{6,2},{1... | collective-permute-start | bytes 983048 | tf_op jit(solution)/shard_map/ppermute | solution.py:282
  16.1 5.1 %collective-permute-start.5 = (bf16[2,64,256]{2,1,0:T(8,128)(2,1)S(1)}, bf16[2,64,256]{2,1,0:T(8,128)(2,1)S(1)}, u32[]{:S(2)}, u32[]{:S(2)}) collective-permute-start(bf16[2,64,256]{2,1,0:T(8,128)(2,1)S(1)} %codes.1.refs_0_.after_ref), channel_id=1, source_target_pairs={{0,3},{1,2},{2,1},{3,0},{4,7},{5,6},{6,5},{7,4},{8,11},{9,10},{10,... | collective-permute-start | bytes 196616 | tf_op jit(solution)/shard_map/ppermute | solution.py:259
  16.2 5.8 %collective-permute-start.4 = (bf16[2,64,256]{2,1,0:T(8,128)(2,1)S(1)}, bf16[2,64,256]{2,1,0:T(8,128)(2,1)S(1)}, u32[]{:S(2)}, u32[]{:S(2)}) collective-permute-start(bf16[2,64,256]{2,1,0:T(8,128)(2,1)S(1)} %codes.1.refs_0_.after_ref), channel_id=1, source_target_pairs={{0,2},{1,3},{2,0},{3,1},{4,6},{5,7},{6,4},{7,5},{8,10},{9,11},{10,... | collective-permute-start | bytes 196616 | tf_op jit(solution)/shard_map/ppermute | solution.py:259
  17.7 4.2 %collective-permute-start.3 = (bf16[2,64,256]{2,1,0:T(8,128)(2,1)S(1)}, bf16[2,64,256]{2,1,0:T(8,128)(2,1)S(1)}, u32[]{:S(2)}, u32[]{:S(2)}) collective-permute-start(bf16[2,64,256]{2,1,0:T(8,128)(2,1)S(1)} %codes.1.refs_0_.after_ref), channel_id=1, source_target_pairs={{0,1},{1,0},{2,3},{3,2},{4,5},{5,4},{6,7},{7,6},{8,9},{9,8},{10,11... | collective-permute-start | bytes 196616 | tf_op jit(solution)/shard_map/ppermute | solution.py:259
  19.1 2.9 %copy-start = (bf16[2,2,128,2048]{3,2,1,0:T(8,128)(2,1)S(1)}, bf16[2,2,128,2048]{3,2,1,0:T(8,128)(2,1)}, u32[]{:S(2)}) copy-start(bf16[2,2,128,2048]{3,2,1,0:T(8,128)(2,1)} %dec_ref.5) | copy-start | bytes 6291460
  19.1 14.9 %collective-permute-start.6 = (bf16[2,2,128,384]{3,2,1,0:T(8,128)(2,1)S(1)}, bf16[2,2,128,384]{3,2,1,0:T(8,128)(2,1)S(1)}, u32[]{:S(2)}, u32[]{:S(2)}) collective-permute-start(bf16[2,2,128,384]{3,2,1,0:T(8,128)(2,1)S(1)} %part.1), channel_id=1, source_target_pairs={{0,4},{4,0},{8,12},{12,8},{1,5},{5,1},{9,13},{13,9},{2,6},{6,2},{1... | collective-permute-start | bytes 1179656 | tf_op jit(solution)/shard_map/ppermute | solution.py:284
  19.6 9.5 %collective-permute-start.8 = (bf16[1,2,128,640]{3,2,1,0:T(8,128)(2,1)S(1)}, bf16[1,2,128,640]{3,2,1,0:T(8,128)(2,1)S(1)}, u32[]{:S(2)}, u32[]{:S(2)}) collective-permute-start(bf16[1,2,128,640]{3,2,1,0:T(8,128)(2,1)S(1)} %collective-permute-done.7.got_ref), channel_id=1, source_target_pairs={{0,16},{16,0},{1,17},{17,1},{2,18},{18,2},{3,19},{19,3},{4,20},{20... | collective-permute-start | bytes 983048 | tf_op jit(solution)/shard_map/ppermute | solution.py:283
  22.4 8.8 %collective-permute-start.12 = (bf16[1,64,640]{2,1,0:T(8,128)(2,1)S(1)}, bf16[1,64,640]{2,1,0:T(8,128)(2,1)S(1)}, u32[]{:S(2)}, u32[]{:S(2)}) collective-permute-start(bf16[1,64,640]{2,1,0:T(8,128)(2,1)S(1)} %get-tuple-element.33), channel_id=1, source_target_pairs={{0,8},{1,9},{4,12},{5,13},{8,0},{9,1},{12,4},{13,5},{2,10},{3,11},... | collective-permute-start | bytes 245768 | tf_op jit(solution)/shard_map/ppermute | solution.py:323
  23.3 11.1 %collective-permute-start.13 = (bf16[1,64,640]{2,1,0:T(8,128)(2,1)S(1)}, bf16[1,64,640]{2,1,0:T(8,128)(2,1)S(1)}, u32[]{:S(2)}, u32[]{:S(2)}) collective-permute-start(bf16[1,64,640]{2,1,0:T(8,128)(2,1)S(1)} %get-tuple-element.34), channel_id=1, source_target_pairs={{0,9},{1,8},{4,13},{5,12},{8,1},{9,0},{12,5},{13,4},{2,11},{3,10},... | collective-permute-start | bytes 245768 | tf_op jit(solution)/shard_map/ppermute | solution.py:323
  24.8 10.0 %collective-permute-start.14 = (bf16[1,64,640]{2,1,0:T(8,128)(2,1)S(1)}, bf16[1,64,640]{2,1,0:T(8,128)(2,1)S(1)}, u32[]{:S(2)}, u32[]{:S(2)}) collective-permute-start(bf16[1,64,640]{2,1,0:T(8,128)(2,1)S(1)} %get-tuple-element.35), channel_id=1, source_target_pairs={{0,1},{1,0},{4,5},{5,4},{8,9},{9,8},{12,13},{13,12},{2,3},{3,2},{6... | collective-permute-start | bytes 245768 | tf_op jit(solution)/shard_map/ppermute | solution.py:323
  29.5 15.6 %copy-start.1 = (bf16[2,64,2048]{2,1,0:T(8,128)(2,1)S(1)}, bf16[2,64,2048]{2,1,0:T(8,128)(2,1)}, u32[]{:S(2)}) copy-start(bf16[2,64,2048]{2,1,0:T(8,128)(2,1)} %target_ref.3) | copy-start | bytes 1572868
  29.5 15.6 %copy-start.2 = (f32[2,2048]{1,0:T(2,128)S(1)}, f32[2,2048]{1,0:T(2,128)}, u32[]{:S(2)}) copy-start(f32[2,2048]{1,0:T(2,128)} %bias_ref.3) | copy-start | bytes 49156
  29.5 14.0 %collective-permute-start.15 = (bf16[1,64,640]{2,1,0:T(8,128)(2,1)S(1)}, bf16[1,64,640]{2,1,0:T(8,128)(2,1)S(1)}, u32[]{:S(2)}, u32[]{:S(2)}) collective-permute-start(bf16[1,64,640]{2,1,0:T(8,128)(2,1)S(1)} %get-tuple-element.36), channel_id=1, source_target_pairs={{0,8},{1,9},{4,12},{5,13},{8,0},{9,1},{12,4},{13,5},{2,10},{3,11},... | collective-permute-start | bytes 245768 | tf_op jit(solution)/shard_map/ppermute | solution.py:323
  31.1 13.9 %collective-permute-start.16 = (bf16[1,64,640]{2,1,0:T(8,128)(2,1)S(1)}, bf16[1,64,640]{2,1,0:T(8,128)(2,1)S(1)}, u32[]{:S(2)}, u32[]{:S(2)}) collective-permute-start(bf16[1,64,640]{2,1,0:T(8,128)(2,1)S(1)} %get-tuple-element.37), channel_id=1, source_target_pairs={{0,9},{1,8},{4,13},{5,12},{8,1},{9,0},{12,5},{13,4},{2,11},{3,10},... | collective-permute-start | bytes 245768 | tf_op jit(solution)/shard_map/ppermute | solution.py:323
  34.0 11.0 %collective-permute-start.17 = (bf16[1,64,640]{2,1,0:T(8,128)(2,1)S(1)}, bf16[1,64,640]{2,1,0:T(8,128)(2,1)S(1)}, u32[]{:S(2)}, u32[]{:S(2)}) collective-permute-start(bf16[1,64,640]{2,1,0:T(8,128)(2,1)S(1)} %get-tuple-element.38), channel_id=1, source_target_pairs={{0,1},{1,0},{4,5},{5,4},{8,9},{9,8},{12,13},{13,12},{2,3},{3,2},{6... | collective-permute-start | bytes 245768 | tf_op jit(solution)/shard_map/ppermute | solution.py:323
  34.5 12.9 %collective-permute-start.9 = (bf16[2,64,384]{2,1,0:T(8,128)(2,1)S(1)}, bf16[2,64,384]{2,1,0:T(8,128)(2,1)S(1)}, u32[]{:S(2)}, u32[]{:S(2)}) collective-permute-start(bf16[2,64,384]{2,1,0:T(8,128)(2,1)S(1)} %get-tuple-element.29), channel_id=1, source_target_pairs={{0,8},{1,9},{4,12},{5,13},{8,0},{9,1},{12,4},{13,5},{2,10},{3,11},... | collective-permute-start | bytes 294920 | tf_op jit(solution)/shard_map/ppermute | solution.py:323
  34.8 14.4 %collective-permute-start.10 = (bf16[2,64,384]{2,1,0:T(8,128)(2,1)S(1)}, bf16[2,64,384]{2,1,0:T(8,128)(2,1)S(1)}, u32[]{:S(2)}, u32[]{:S(2)}) collective-permute-start(bf16[2,64,384]{2,1,0:T(8,128)(2,1)S(1)} %get-tuple-element.30), channel_id=1, source_target_pairs={{0,9},{1,8},{4,13},{5,12},{8,1},{9,0},{12,5},{13,4},{2,11},{3,10},... | collective-permute-start | bytes 294920 | tf_op jit(solution)/shard_map/ppermute | solution.py:323
  43.5 5.8 %collective-permute-start.11 = (bf16[2,64,384]{2,1,0:T(8,128)(2,1)S(1)}, bf16[2,64,384]{2,1,0:T(8,128)(2,1)S(1)}, u32[]{:S(2)}, u32[]{:S(2)}) collective-permute-start(bf16[2,64,384]{2,1,0:T(8,128)(2,1)S(1)} %get-tuple-element.31), channel_id=1, source_target_pairs={{0,1},{1,0},{4,5},{5,4},{8,9},{9,8},{12,13},{13,12},{2,3},{3,2},{6... | collective-permute-start | bytes 294920 | tf_op jit(solution)/shard_map/ppermute | solution.py:323

commit v17 on v16

--- a/solution.py
+++ b/solution.py
@@ -9,16 +9,16 @@
 
 VMEM_BYTES = 32 * 1024 * 1024
 LANES = 128
-FIRST = 5
-PIECES = (((0,), 0, False), ((1,), 0, True), ((0, 1), 1, False))
+FIRST = 4
+PIECES = (((0,), 0), ((1,), 0), ((0, 1), 1))
 
 
 def cut_pieces(columns):
     middle = columns // LANES * FIRST // 8 * LANES
     bounds = ((0, middle), (middle, columns))
     return [
-        (layers, bounds[side][0], bounds[side][1] - bounds[side][0], across)
-        for layers, side, across in PIECES
+        (layers, bounds[side][0], bounds[side][1] - bounds[side][0])
+        for layers, side in PIECES
     ]
 
 
@@ -31,7 +31,7 @@
 
 
 def part_copies(piece, dec_hbm, part_ref, sems):
-    offsets, first, width, _ = piece
+    offsets, first, width = piece
     layers, groups, _, cols = dec_hbm.shape
     start = pl.multiple_of(lax.axis_index("rep") * (cols // 2) + first, LANES)
     copies = []
@@ -142,8 +142,8 @@
                     out_ref[rows, columns] = code_refs[2 * k + r][group, :, latents]
 
 
-def decode_kernel(n, piece, dec_ref, lhs_ref, got_ref, *refs):
-    offsets, first, width, _ = piece
+def decode_kernel(n, piece, dec_ref, lhs_ref, *refs):
+    offsets, first, width = piece
     layers, groups, block, cols = dec_ref.shape
     out_refs = refs[-2 * (n // 2) :]
     depth = groups * block
@@ -151,7 +151,7 @@
     start = pl.multiple_of(lax.axis_index("rep") * (cols // 2) + first, LANES)
     for i, offset in enumerate(offsets):
         own = dec_ref[layer_of(offset, layers), :, :, pl.ds(start, width)].reshape(depth, width)
-        got = got_ref[i].reshape(depth, width)
+        got = refs[i][0].reshape(depth, width)
         total = jnp.dot(lhs_ref[:, :depth], own, preferred_element_type=jnp.float32)
         total += jnp.dot(lhs_ref[:, depth:], got, preferred_element_type=jnp.float32)
         for j, ref in enumerate(out_refs):
@@ -164,7 +164,7 @@
     layers, _, cols = target_ref.shape
     rep = lax.axis_index("rep")
     copies = []
-    for i, (offsets, first, width, _) in enumerate(pieces):
+    for i, (offsets, first, width) in enumerate(pieces):
         for side in range(2):
             core = rep if side == 0 else 1 - rep
             columns = pl.ds(pl.multiple_of(core * (cols // 2) + first, LANES), width)
@@ -197,7 +197,7 @@
     share = rows // n
     half = n // 2
     pieces = cut_pieces(cols // 2)
-    fetched = [piece for piece in pieces if not piece[3]]
+    fetched = [((0,), *pieces[i][1:]) for i in (0, 2)]
     tile_rows = rows // active.shape[0]
     pair = [(i, i ^ 1) for i in range(n)]
     params = pltpu.CompilerParams(vmem_limit_bytes=VMEM_BYTES)
@@ -223,7 +223,7 @@
     results = pl.pallas_call(
         functools.partial(encode_kernel, n, fetched[:1]),
         out_shape=[shape(half * share, 2 * block)] * n
-        + [shape(len(offsets), groups, block, width) for offsets, _, width, _ in fetched[:1]],
+        + [shape(len(offsets), groups, block, width) for offsets, _, width in fetched[:1]],
         in_specs=[anywhere] * 3,
         out_specs=[vmem] * (n + 1),
         scratch_shapes=[
@@ -279,14 +279,27 @@
         name="part",
     )(parts[0], dec_w, own)
 
-    got = [lax.ppermute(parts[0], "src", pair)]
-    got.append(lax.ppermute(got[0], "parts", [(0, 1), (1, 0)]))
-    got.append(lax.ppermute(part, "src", pair))
+    def hold(value, after):
+        return pl.pallas_call(
+            lambda *refs: None,
+            out_shape=jax.ShapeDtypeStruct(value.shape, value.dtype),
+            in_specs=[anywhere] * 2,
+            out_specs=anywhere,
+            input_output_aliases={0: 0},
+            compiler_params=params,
+            cost_estimate=cost,
+            name="hold",
+        )(value, after)
+
+    swap = [(0, 1), (1, 0)]
+    got = [[lax.ppermute(parts[0], "src", pair)]]
+    got.append([lax.ppermute(got[0][0], "parts", swap)])
+    got.append([lax.ppermute(part, "src", pair)])
 
     def add(some, begun, billions):
         operands = [value for i in some for value in sums[i]]
         count = 2 * sum(len(pieces[i][0]) for i in some)
-        widest = max(piece[2] for piece in pieces)
+        widest = max(width for _, _, width in pieces)
         return pl.pallas_call(
             functools.partial(add_kernel, n, [pieces[i] for i in some]),
             out_shape=shape(layers, share, cols),
@@ -304,19 +317,21 @@
 
     sums, after = [], []
     for i, piece in enumerate(pieces):
-        offsets, _, width, _ = piece
+        offsets, _, width = piece
         shapes = [shape(len(offsets), share, width)] * (2 * half)
         shapes[0] = shape(len(offsets), share, width, kind=jnp.float32)
         terms = pl.pallas_call(
             functools.partial(decode_kernel, n, piece),
             out_shape=shapes,
-            in_specs=[vmem] * 3 + [anywhere] * len(after),
+            in_specs=[vmem] * (2 + len(got[i])) + [anywhere] * len(after),
             out_specs=[vmem] * len(shapes),
             compiler_params=params,
-            cost_estimate=weight(0),
+            cost_estimate=weight((0, 20, 0)[i]),
             name="decode",
-        )(dec_rows, lhs, got[i], *after)
+        )(dec_rows, lhs, *got[i], *after)
         after = [terms[0]]
+        if i == 0:
+            got[2].append(lax.ppermute(hold(got[2][0], terms[0]), "parts", swap))
         sums.append([])
         for r, j in [(r, j) for r in range(2) for j in range(1, half)] + [(1, 0)]:
             perm = [(d * 2 + c, (d + 2 * j) % n * 2 + (c ^ r)) for d in range(n) for c in range(2)]

time: 50.2 us -> 52.8 us (1.052)
  waiting for transfers between devices: 23.2 us -> 25.9 us
    ppermute x3 -> x4, waiting for transfers between devices: 5.38 us -> 7.85 us  [the longest x1 4.26 us: body(): got[2].append(lax.ppermute(hold(got[2][0], terms[0]), 'parts', swap))]
    ppermute x3 -> x4, starting transfers between devices: 2.57 us -> 4.15 us  [the longest x1 1.6 us: body(): got[2].append(lax.ppermute(hold(got[2][0], terms[0]), 'parts', swap))]
    ppermute x9, starting transfers between devices: 9.1 us -> 7.53 us  [body(): sums[i].append(lax.ppermute(terms[2 * j + r], ('src', 'rep'), perm))]
  transfers between devices with their start and end apart: 18 -> 19, of which waited for: 11 -> 8; matrix products, arithmetic and copies ran while one was open for 0% -> 0% of each run, Pallas kernels for 7% -> 7%
where the time goes in v17:
time: 52.8 us; the launch traced here: 52.6 us
  waiting for transfers between devices  25.9 us (49%)
  starting transfers between devices  19.3 us (37%)
  Pallas kernels  7.18 us (14%)
    ppermute x9, waiting for transfers between devices, body(): sums[i].append(lax.ppermute(terms[2 * j + r], ('src', 'rep'), perm))  10.9 us
    ppermute x9, starting transfers between devices, body(): sums[i].append(lax.ppermute(terms[2 * j + r], ('src', 'rep'), perm))  7.53 us
    ppermute x3, waiting for transfers between devices, body(): lax.ppermute(terms[k], 'src', [(i, peer(i, k, n)) for i in range(n)])  5.92 us
    ppermute x3, starting transfers between devices, body(): lax.ppermute(terms[k], 'src', [(i, peer(i, k, n)) for i in range(n)])  5.68 us
    ppermute x1, waiting for transfers between devices, body(): got[2].append(lax.ppermute(hold(got[2][0], terms[0]), 'parts', swap))  4.26 us
    ppermute x1, waiting for transfers between devices, body(): got.append([lax.ppermute(part, 'src', pair)])  3.58 us
    pallas_call x1, Pallas kernels, body(): pl.pallas_call(functools.partial(encode_kernel, n, fetched[:1]), out_shap...  2.9 us
    ppermute x3, starting transfers between devices, body(): codes.append(lax.ppermute(own, ('tgt', 'rep'), perm) if k + r else own)  1.92 us
  transfers between devices with their start and end apart: 19, of which 8 were waited for; matrix products, arithmetic and copies ran while one was open for 0% of the time, Pallas kernels for 7%

profile of v17, /device:TPU:0, one launch (start us, length us, event | category | flops | bytes accessed | tf_op | source)
XLA Modules:
  0.0 52.6 jit_solution(10178372013071150874)
XLA Ops:
  0.0 2.9 %encode.1 = (bf16[128,256]{1,0:T(8,128)(2,1)S(1)}, bf16[128,256]{1,0:T(8,128)(2,1)S(1)}, bf16[128,256]{1,0:T(8,128)(2,1)S(1)}, bf16[128,256]{1,0:T(8,128)(2,1)S(1)}, bf16[1,2,128,512]{3,2,1,0:T(8,128)(2,1)S(1)}) custom-call(bf16[2,2,64,1024]{3,2,1,0:T(8,128)(2,1)} %bitcast.3, bf16[1024,512]{1,0:T(8,128)(2,1)} %w_hbm.1, bf16[2,2,128,2048]{3,2,1,0:T(8,128)(2,1)} %dec_ref.5), custom_call_target="tpu_custom_call" | custom-call | tf_op jit(solution)/shard_map/encode/pallas_call | solution.py:223
  2.9 4.1 %collective-permute-start = (bf16[128,256]{1,0:T(8,128)(2,1)S(1)}, bf16[128,256]{1,0:T(8,128)(2,1)S(1)}, u32[]{:S(2)}, u32[]{:S(2)}) collective-permute-start(bf16[128,256]{1,0:T(8,128)(2,1)S(1)} %get-tuple-element.23), channel_id=1, source_target_pairs={{0,8},{4,12},{8,0},{12,4},{1,9},{5,13},{9,1},{13,5},{2,10},{6,14},... | collective-permute-start | bytes 196616 | tf_op jit(solution)/shard_map/ppermute | solution.py:242
  7.0 1.6 %collective-permute-start.1 = (bf16[128,256]{1,0:T(8,128)(2,1)S(1)}, bf16[128,256]{1,0:T(8,128)(2,1)S(1)}, u32[]{:S(2)}, u32[]{:S(2)}) collective-permute-start(bf16[128,256]{1,0:T(8,128)(2,1)S(1)} %get-tuple-element.24), channel_id=1, source_target_pairs={{0,4},{4,0},{8,12},{12,8},{1,5},{5,1},{9,13},{13,9},{2,6},{6,2},{1... | collective-permute-start | bytes 196616 | tf_op jit(solution)/shard_map/ppermute | solution.py:242
  8.6 0.0 collective-permute-start.2
  8.6 0.9 %collective-permute-start.7 = (bf16[1,2,128,512]{3,2,1,0:T(8,128)(2,1)S(1)}, bf16[1,2,128,512]{3,2,1,0:T(8,128)(2,1)S(1)}, u32[]{:S(2)}, u32[]{:S(2)}) collective-permute-start(bf16[1,2,128,512]{3,2,1,0:T(8,128)(2,1)S(1)} %get-tuple-element.26.before_ref), channel_id=1, source_target_pairs={{0,4},{4,0},{8,12},{12,8},{1,5},{5,1},{9,13},{13,9},{2,6},{6,2},{1... | collective-permute-start | bytes 786440 | tf_op jit(solution)/shard_map/ppermute | solution.py:295
  9.5 0.6 %collective-permute-done.refs_1_ = bf16[128,256]{1,0:T(8,128)(2,1)S(1)} collective-permute-done((bf16[128,256]{1,0:T(8,128)(2,1)S(1)}, bf16[128,256]{1,0:T(8,128)(2,1)S(1)}, u32[]{:S(2)}, u32[]{:S(2)}) %collective-permute-start) | collective-permute-done | bytes 65568 | tf_op jit(solution)/shard_map/ppermute | solution.py:242
  10.1 1.9 %collective-permute-done.1.refs_2_ = bf16[128,256]{1,0:T(8,128)(2,1)S(1)} collective-permute-done((bf16[128,256]{1,0:T(8,128)(2,1)S(1)}, bf16[128,256]{1,0:T(8,128)(2,1)S(1)}, u32[]{:S(2)}, u32[]{:S(2)}) %collective-permute-start.1) | collective-permute-done | bytes 65568 | tf_op jit(solution)/shard_map/ppermute | solution.py:242
  12.0 3.5 %collective-permute-done.2.refs_3_ = bf16[128,256]{1,0:T(8,128)(2,1)S(1)} collective-permute-done((bf16[128,256]{1,0:T(8,128)(2,1)S(1)}, bf16[128,256]{1,0:T(8,128)(2,1)S(1)}, u32[]{:S(2)}, u32[]{:S(2)}) %collective-permute-start.2) | collective-permute-done | bytes 65568 | tf_op jit(solution)/shard_map/ppermute | solution.py:242
  15.4 0.6 %codes.1.refs_0_.after_ref = bf16[2,64,256]{2,1,0:T(8,128)(2,1)S(1)} custom-call(s32[2,8]{1,0:T(2,128)S(1)} %copy-done.4, f32[4,128]{1,0:T(4,128)S(1)} %bitcast.2, bf16[128,256]{1,0:T(8,128)(2,1)S(1)} %get-tuple-element.22.refs_0_, bf16[128,256]{1,0:T(8,128)(2,1)S(1)} %collective-permute-done.refs_1_, bf16[128,256]{1,0:T(8,128)(2,1)S(1)} %collective-permute-done.1.refs_2_, ...), custom_call_target="tpu_custom_call" | custom-call | flops 20000000000 | tf_op jit(solution)/shard_map/codes/pallas_call | solution.py:244
  16.1 0.1 collective-permute-start.5
  16.1 1.6 %collective-permute-start.4 = (bf16[2,64,256]{2,1,0:T(8,128)(2,1)S(1)}, bf16[2,64,256]{2,1,0:T(8,128)(2,1)S(1)}, u32[]{:S(2)}, u32[]{:S(2)}) collective-permute-start(bf16[2,64,256]{2,1,0:T(8,128)(2,1)S(1)} %codes.1.refs_0_.after_ref), channel_id=1, source_target_pairs={{0,2},{1,3},{2,0},{3,1},{4,6},{5,7},{6,4},{7,5},{8,10},{9,11},{10,... | collective-permute-start | bytes 196616 | tf_op jit(solution)/shard_map/ppermute | solution.py:259
  17.7 0.3 collective-permute-start.3
  18.0 1.0 %part.1 = bf16[1,2,128,512]{3,2,1,0:T(8,128)(2,1)S(1)} custom-call(bf16[1,2,128,512]{3,2,1,0:T(8,128)(2,1)S(1)} %get-tuple-element.26.before_ref, bf16[2,2,128,2048]{3,2,1,0:T(8,128)(2,1)} %dec_ref.5, bf16[2,64,256]{2,1,0:T(8,128)(2,1)S(1)} %codes.1.refs_0_.after_ref), custom_call_target="tpu_custom_call" | custom-call | tf_op jit(solution)/shard_map/part/pallas_call | solution.py:271
  19.0 0.0 copy-start
  19.0 0.1 collective-permute-start.6
  19.1 0.0 collective-permute-done.7.refs_0_
  19.1 1.6 %collective-permute-start.9 = (bf16[1,2,128,512]{3,2,1,0:T(8,128)(2,1)S(1)}, bf16[1,2,128,512]{3,2,1,0:T(8,128)(2,1)S(1)}, u32[]{:S(2)}, u32[]{:S(2)}) collective-permute-start(bf16[1,2,128,512]{3,2,1,0:T(8,128)(2,1)S(1)} %collective-permute-done.7.refs_0_), channel_id=1, source_target_pairs={{0,16},{16,0},{1,17},{17,1},{2,18},{18,2},{3,19},{19,3},{4,20},{20... | collective-permute-start | bytes 786440 | tf_op jit(solution)/shard_map/ppermute | solution.py:296
  20.7 0.0 collective-permute-done.5.refs_3_
  20.7 1.2 %collective-permute-done.4.refs_2_ = bf16[2,64,256]{2,1,0:T(8,128)(2,1)S(1)} collective-permute-done((bf16[2,64,256]{2,1,0:T(8,128)(2,1)S(1)}, bf16[2,64,256]{2,1,0:T(8,128)(2,1)S(1)}, u32[]{:S(2)}, u32[]{:S(2)}) %collective-permute-start.4) | collective-permute-done | bytes 65568 | tf_op jit(solution)/shard_map/ppermute | solution.py:259
  21.9 0.0 collective-permute-done.3.refs_1_
  22.0 0.3 decode.3
  22.3 0.7 %collective-permute-start.13 = (bf16[1,64,512]{2,1,0:T(8,128)(2,1)S(1)}, bf16[1,64,512]{2,1,0:T(8,128)(2,1)S(1)}, u32[]{:S(2)}, u32[]{:S(2)}) collective-permute-start(bf16[1,64,512]{2,1,0:T(8,128)(2,1)S(1)} %get-tuple-element.33), channel_id=1, source_target_pairs={{0,8},{1,9},{4,12},{5,13},{8,0},{9,1},{12,4},{13,5},{2,10},{3,11},... | collective-permute-start | bytes 196616 | tf_op jit(solution)/shard_map/ppermute | solution.py:338
  23.0 1.7 %collective-permute-start.14 = (bf16[1,64,512]{2,1,0:T(8,128)(2,1)S(1)}, bf16[1,64,512]{2,1,0:T(8,128)(2,1)S(1)}, u32[]{:S(2)}, u32[]{:S(2)}) collective-permute-start(bf16[1,64,512]{2,1,0:T(8,128)(2,1)S(1)} %get-tuple-element.34), channel_id=1, source_target_pairs={{0,9},{1,8},{4,13},{5,12},{8,1},{9,0},{12,5},{13,4},{2,11},{3,10},... | collective-permute-start | bytes 196616 | tf_op jit(solution)/shard_map/ppermute | solution.py:338
  24.7 0.7 %collective-permute-start.15 = (bf16[1,64,512]{2,1,0:T(8,128)(2,1)S(1)}, bf16[1,64,512]{2,1,0:T(8,128)(2,1)S(1)}, u32[]{:S(2)}, u32[]{:S(2)}) collective-permute-start(bf16[1,64,512]{2,1,0:T(8,128)(2,1)S(1)} %get-tuple-element.35), channel_id=1, source_target_pairs={{0,1},{1,0},{4,5},{5,4},{8,9},{9,8},{12,13},{13,12},{2,3},{3,2},{6... | collective-permute-start | bytes 196616 | tf_op jit(solution)/shard_map/ppermute | solution.py:338
  25.4 3.6 %collective-permute-done.6.refs_0_ = bf16[1,2,128,512]{3,2,1,0:T(8,128)(2,1)S(1)} collective-permute-done((bf16[1,2,128,512]{3,2,1,0:T(8,128)(2,1)S(1)}, bf16[1,2,128,512]{3,2,1,0:T(8,128)(2,1)S(1)}, u32[]{:S(2)}, u32[]{:S(2)}) %collective-permute-start.6) | collective-permute-done | bytes 262176 | tf_op jit(solution)/shard_map/ppermute | solution.py:297
  29.0 1.6 %collective-permute-start.8 = (bf16[1,2,128,512]{3,2,1,0:T(8,128)(2,1)S(1)}, bf16[1,2,128,512]{3,2,1,0:T(8,128)(2,1)S(1)}, u32[]{:S(2)}, u32[]{:S(2)}) collective-permute-start(bf16[1,2,128,512]{3,2,1,0:T(8,128)(2,1)S(1)} %hold.1), channel_id=1, source_target_pairs={{0,16},{16,0},{1,17},{17,1},{2,18},{18,2},{3,19},{19,3},{4,20},{20... | collective-permute-start | bytes 786440 | tf_op jit(solution)/shard_map/ppermute | solution.py:334
  30.6 0.0 collective-permute-done.9.refs_0_
  30.6 0.3 decode.4
  30.9 0.0 copy-start.1
  30.9 0.0 copy-start.2
  30.9 0.2 collective-permute-start.16
  31.2 0.0 collective-permute-done.13.refs_0_
  31.2 1.1 %collective-permute-start.17 = (bf16[1,64,512]{2,1,0:T(8,128)(2,1)S(1)}, bf16[1,64,512]{2,1,0:T(8,128)(2,1)S(1)}, u32[]{:S(2)}, u32[]{:S(2)}) collective-permute-start(bf16[1,64,512]{2,1,0:T(8,128)(2,1)S(1)} %get-tuple-element.37), channel_id=1, source_target_pairs={{0,9},{1,8},{4,13},{5,12},{8,1},{9,0},{12,5},{13,4},{2,11},{3,10},... | collective-permute-start | bytes 196616 | tf_op jit(solution)/shard_map/ppermute | solution.py:338
  32.3 4.3 %collective-permute-done.8.refs_1_ = bf16[1,2,128,512]{3,2,1,0:T(8,128)(2,1)S(1)} collective-permute-done((bf16[1,2,128,512]{3,2,1,0:T(8,128)(2,1)S(1)}, bf16[1,2,128,512]{3,2,1,0:T(8,128)(2,1)S(1)}, u32[]{:S(2)}, u32[]{:S(2)}) %collective-permute-start.8) | collective-permute-done | bytes 262176 | tf_op jit(solution)/shard_map/ppermute | solution.py:334
  36.5 0.0 collective-permute-start.18
  36.6 0.4 decode.5
  37.0 0.0 collective-permute-done.14.refs_1_
  37.0 0.1 collective-permute-start.10
  37.1 0.0 collective-permute-done.15.refs_2_
  37.1 2.8 %collective-permute-start.11 = (bf16[2,64,512]{2,1,0:T(8,128)(2,1)S(1)}, bf16[2,64,512]{2,1,0:T(8,128)(2,1)S(1)}, u32[]{:S(2)}, u32[]{:S(2)}) collective-permute-start(bf16[2,64,512]{2,1,0:T(8,128)(2,1)S(1)} %get-tuple-element.30), channel_id=1, source_target_pairs={{0,9},{1,8},{4,13},{5,12},{8,1},{9,0},{12,5},{13,4},{2,11},{3,10},... | collective-permute-start | bytes 393224 | tf_op jit(solution)/shard_map/ppermute | solution.py:338
  39.8 0.0 collective-permute-done.16.refs_4_
  39.8 0.3 collective-permute-start.12
  40.1 0.0 collective-permute-done.17.refs_5_
  40.1 0.0 collective-permute-done.18.refs_6_
  40.1 0.8 %add.2.refs_4_ = bf16[2,64,2048]{2,1,0:T(8,128)(2,1)} custom-call(f32[2,2048]{1,0:T(2,128)S(1)} %copy-done.2, bf16[2,64,2048]{2,1,0:T(8,128)(2,1)S(1)} %copy-done.1, bf16[1,64,512]{2,1,0:T(8,128)(2,1)S(1)} %collective-permute-done.13.refs_0_, bf16[1,64,512]{2,1,0:T(8,128)(2,1)S(1)} %collective-permute-done.14.refs_1_, ...), custom_call_target="tpu_custom_call" | custom-call | flops 20000000000 | tf_op jit(solution)/shard_map/add/pallas_call | solution.py:303
  40.9 8.2 %collective-permute-done.10.refs_0_ = bf16[2,64,512]{2,1,0:T(8,128)(2,1)S(1)} collective-permute-done((bf16[2,64,512]{2,1,0:T(8,128)(2,1)S(1)}, bf16[2,64,512]{2,1,0:T(8,128)(2,1)S(1)}, u32[]{:S(2)}, u32[]{:S(2)}) %collective-permute-start.10) | collective-permute-done | bytes 131104 | tf_op jit(solution)/shard_map/ppermute | solution.py:338
  49.1 2.7 %collective-permute-done.11.refs_1_ = bf16[2,64,512]{2,1,0:T(8,128)(2,1)S(1)} collective-permute-done((bf16[2,64,512]{2,1,0:T(8,128)(2,1)S(1)}, bf16[2,64,512]{2,1,0:T(8,128)(2,1)S(1)}, u32[]{:S(2)}, u32[]{:S(2)}) %collective-permute-start.11) | collective-permute-done | bytes 131104 | tf_op jit(solution)/shard_map/ppermute | solution.py:338
  51.8 0.8 %add.3 = bf16[2,64,2048]{2,1,0:T(8,128)(2,1)} custom-call(f32[2,2048]{1,0:T(2,128)S(1)} %copy-done.2, bf16[2,64,2048]{2,1,0:T(8,128)(2,1)S(1)} %copy-done.1, bf16[2,64,512]{2,1,0:T(8,128)(2,1)S(1)} %collective-permute-done.10.refs_0_, bf16[2,64,512]{2,1,0:T(8,128)(2,1)S(1)} %collective-permute-done.11.refs_1_, ...), custom_call_target="tpu_custom_call", output_to_operand_aliasing={{}: (6, {})} | custom-call | tf_op jit(solution)/shard_map/add/pallas_call | solution.py:303
  (11 shorter events, 0.1 us)
Async XLA Ops:
  0.0 15.4 %copy-start.4 = (s32[2,8]{1,0:T(2,128)S(1)}, s32[2,8]{1,0:T(2,128)}, u32[]{:S(2)}) copy-start(s32[2,8]{1,0:T(2,128)} %active_ref.1) | copy-start | bytes 196
  0.0 15.4 %copy-start.3 = (f32[512]{0:T(512)S(1)}, f32[512]{0:T(512)}, u32[]{:S(2)}) copy-start(f32[512]{0:T(512)} %param.9) | copy-start | bytes 6148
  2.9 7.1 %collective-permute-start = (bf16[128,256]{1,0:T(8,128)(2,1)S(1)}, bf16[128,256]{1,0:T(8,128)(2,1)S(1)}, u32[]{:S(2)}, u32[]{:S(2)}) collective-permute-start(bf16[128,256]{1,0:T(8,128)(2,1)S(1)} %get-tuple-element.23), channel_id=1, source_target_pairs={{0,8},{4,12},{8,0},{12,4},{1,9},{5,13},{9,1},{13,5},{2,10},{6,14},... | collective-permute-start | bytes 196616 | tf_op jit(solution)/shard_map/ppermute | solution.py:242
  7.0 5.0 %collective-permute-start.1 = (bf16[128,256]{1,0:T(8,128)(2,1)S(1)}, bf16[128,256]{1,0:T(8,128)(2,1)S(1)}, u32[]{:S(2)}, u32[]{:S(2)}) collective-permute-start(bf16[128,256]{1,0:T(8,128)(2,1)S(1)} %get-tuple-element.24), channel_id=1, source_target_pairs={{0,4},{4,0},{8,12},{12,8},{1,5},{5,1},{9,13},{13,9},{2,6},{6,2},{1... | collective-permute-start | bytes 196616 | tf_op jit(solution)/shard_map/ppermute | solution.py:242
  8.6 6.8 %collective-permute-start.2 = (bf16[128,256]{1,0:T(8,128)(2,1)S(1)}, bf16[128,256]{1,0:T(8,128)(2,1)S(1)}, u32[]{:S(2)}, u32[]{:S(2)}) collective-permute-start(bf16[128,256]{1,0:T(8,128)(2,1)S(1)} %get-tuple-element.25), channel_id=1, source_target_pairs={{0,12},{4,8},{8,4},{12,0},{1,13},{5,9},{9,5},{13,1},{2,14},{6,10},... | collective-permute-start | bytes 196616 | tf_op jit(solution)/shard_map/ppermute | solution.py:242
  8.6 10.5 %collective-permute-start.7 = (bf16[1,2,128,512]{3,2,1,0:T(8,128)(2,1)S(1)}, bf16[1,2,128,512]{3,2,1,0:T(8,128)(2,1)S(1)}, u32[]{:S(2)}, u32[]{:S(2)}) collective-permute-start(bf16[1,2,128,512]{3,2,1,0:T(8,128)(2,1)S(1)} %get-tuple-element.26.before_ref), channel_id=1, source_target_pairs={{0,4},{4,0},{8,12},{12,8},{1,5},{5,1},{9,13},{13,9},{2,6},{6,2},{1... | collective-permute-start | bytes 786440 | tf_op jit(solution)/shard_map/ppermute | solution.py:295
  16.1 4.6 %collective-permute-start.5 = (bf16[2,64,256]{2,1,0:T(8,128)(2,1)S(1)}, bf16[2,64,256]{2,1,0:T(8,128)(2,1)S(1)}, u32[]{:S(2)}, u32[]{:S(2)}) collective-permute-start(bf16[2,64,256]{2,1,0:T(8,128)(2,1)S(1)} %codes.1.refs_0_.after_ref), channel_id=1, source_target_pairs={{0,3},{1,2},{2,1},{3,0},{4,7},{5,6},{6,5},{7,4},{8,11},{9,10},{10,... | collective-permute-start | bytes 196616 | tf_op jit(solution)/shard_map/ppermute | solution.py:259
  16.1 5.8 %collective-permute-start.4 = (bf16[2,64,256]{2,1,0:T(8,128)(2,1)S(1)}, bf16[2,64,256]{2,1,0:T(8,128)(2,1)S(1)}, u32[]{:S(2)}, u32[]{:S(2)}) collective-permute-start(bf16[2,64,256]{2,1,0:T(8,128)(2,1)S(1)} %codes.1.refs_0_.after_ref), channel_id=1, source_target_pairs={{0,2},{1,3},{2,0},{3,1},{4,6},{5,7},{6,4},{7,5},{8,10},{9,11},{10,... | collective-permute-start | bytes 196616 | tf_op jit(solution)/shard_map/ppermute | solution.py:259
  17.7 4.2 %collective-permute-start.3 = (bf16[2,64,256]{2,1,0:T(8,128)(2,1)S(1)}, bf16[2,64,256]{2,1,0:T(8,128)(2,1)S(1)}, u32[]{:S(2)}, u32[]{:S(2)}) collective-permute-start(bf16[2,64,256]{2,1,0:T(8,128)(2,1)S(1)} %codes.1.refs_0_.after_ref), channel_id=1, source_target_pairs={{0,1},{1,0},{2,3},{3,2},{4,5},{5,4},{6,7},{7,6},{8,9},{9,8},{10,11... | collective-permute-start | bytes 196616 | tf_op jit(solution)/shard_map/ppermute | solution.py:259
  19.0 3.0 %copy-start = (bf16[2,2,128,2048]{3,2,1,0:T(8,128)(2,1)S(1)}, bf16[2,2,128,2048]{3,2,1,0:T(8,128)(2,1)}, u32[]{:S(2)}) copy-start(bf16[2,2,128,2048]{3,2,1,0:T(8,128)(2,1)} %dec_ref.5) | copy-start | bytes 6291460
  19.0 10.0 %collective-permute-start.6 = (bf16[1,2,128,512]{3,2,1,0:T(8,128)(2,1)S(1)}, bf16[1,2,128,512]{3,2,1,0:T(8,128)(2,1)S(1)}, u32[]{:S(2)}, u32[]{:S(2)}) collective-permute-start(bf16[1,2,128,512]{3,2,1,0:T(8,128)(2,1)S(1)} %part.1), channel_id=1, source_target_pairs={{0,4},{4,0},{8,12},{12,8},{1,5},{5,1},{9,13},{13,9},{2,6},{6,2},{1... | collective-permute-start | bytes 786440 | tf_op jit(solution)/shard_map/ppermute | solution.py:297
  19.1 11.5 %collective-permute-start.9 = (bf16[1,2,128,512]{3,2,1,0:T(8,128)(2,1)S(1)}, bf16[1,2,128,512]{3,2,1,0:T(8,128)(2,1)S(1)}, u32[]{:S(2)}, u32[]{:S(2)}) collective-permute-start(bf16[1,2,128,512]{3,2,1,0:T(8,128)(2,1)S(1)} %collective-permute-done.7.refs_0_), channel_id=1, source_target_pairs={{0,16},{16,0},{1,17},{17,1},{2,18},{18,2},{3,19},{19,3},{4,20},{20... | collective-permute-start | bytes 786440 | tf_op jit(solution)/shard_map/ppermute | solution.py:296
  22.3 8.9 %collective-permute-start.13 = (bf16[1,64,512]{2,1,0:T(8,128)(2,1)S(1)}, bf16[1,64,512]{2,1,0:T(8,128)(2,1)S(1)}, u32[]{:S(2)}, u32[]{:S(2)}) collective-permute-start(bf16[1,64,512]{2,1,0:T(8,128)(2,1)S(1)} %get-tuple-element.33), channel_id=1, source_target_pairs={{0,8},{1,9},{4,12},{5,13},{8,0},{9,1},{12,4},{13,5},{2,10},{3,11},... | collective-permute-start | bytes 196616 | tf_op jit(solution)/shard_map/ppermute | solution.py:338
  23.0 14.0 %collective-permute-start.14 = (bf16[1,64,512]{2,1,0:T(8,128)(2,1)S(1)}, bf16[1,64,512]{2,1,0:T(8,128)(2,1)S(1)}, u32[]{:S(2)}, u32[]{:S(2)}) collective-permute-start(bf16[1,64,512]{2,1,0:T(8,128)(2,1)S(1)} %get-tuple-element.34), channel_id=1, source_target_pairs={{0,9},{1,8},{4,13},{5,12},{8,1},{9,0},{12,5},{13,4},{2,11},{3,10},... | collective-permute-start | bytes 196616 | tf_op jit(solution)/shard_map/ppermute | solution.py:338
  24.7 12.4 %collective-permute-start.15 = (bf16[1,64,512]{2,1,0:T(8,128)(2,1)S(1)}, bf16[1,64,512]{2,1,0:T(8,128)(2,1)S(1)}, u32[]{:S(2)}, u32[]{:S(2)}) collective-permute-start(bf16[1,64,512]{2,1,0:T(8,128)(2,1)S(1)} %get-tuple-element.35), channel_id=1, source_target_pairs={{0,1},{1,0},{4,5},{5,4},{8,9},{9,8},{12,13},{13,12},{2,3},{3,2},{6... | collective-permute-start | bytes 196616 | tf_op jit(solution)/shard_map/ppermute | solution.py:338
  29.0 7.5 %collective-permute-start.8 = (bf16[1,2,128,512]{3,2,1,0:T(8,128)(2,1)S(1)}, bf16[1,2,128,512]{3,2,1,0:T(8,128)(2,1)S(1)}, u32[]{:S(2)}, u32[]{:S(2)}) collective-permute-start(bf16[1,2,128,512]{3,2,1,0:T(8,128)(2,1)S(1)} %hold.1), channel_id=1, source_target_pairs={{0,16},{16,0},{1,17},{17,1},{2,18},{18,2},{3,19},{19,3},{4,20},{20... | collective-permute-start | bytes 786440 | tf_op jit(solution)/shard_map/ppermute | solution.py:334
  30.9 9.2 %copy-start.1 = (bf16[2,64,2048]{2,1,0:T(8,128)(2,1)S(1)}, bf16[2,64,2048]{2,1,0:T(8,128)(2,1)}, u32[]{:S(2)}) copy-start(bf16[2,64,2048]{2,1,0:T(8,128)(2,1)} %target_ref.3) | copy-start | bytes 1572868
  30.9 9.2 %copy-start.2 = (f32[2,2048]{1,0:T(2,128)S(1)}, f32[2,2048]{1,0:T(2,128)}, u32[]{:S(2)}) copy-start(f32[2,2048]{1,0:T(2,128)} %bias_ref.3) | copy-start | bytes 49156
  30.9 8.9 %collective-permute-start.16 = (bf16[1,64,512]{2,1,0:T(8,128)(2,1)S(1)}, bf16[1,64,512]{2,1,0:T(8,128)(2,1)S(1)}, u32[]{:S(2)}, u32[]{:S(2)}) collective-permute-start(bf16[1,64,512]{2,1,0:T(8,128)(2,1)S(1)} %get-tuple-element.36), channel_id=1, source_target_pairs={{0,8},{1,9},{4,12},{5,13},{8,0},{9,1},{12,4},{13,5},{2,10},{3,11},... | collective-permute-start | bytes 196616 | tf_op jit(solution)/shard_map/ppermute | solution.py:338
  31.2 9.0 %collective-permute-start.17 = (bf16[1,64,512]{2,1,0:T(8,128)(2,1)S(1)}, bf16[1,64,512]{2,1,0:T(8,128)(2,1)S(1)}, u32[]{:S(2)}, u32[]{:S(2)}) collective-permute-start(bf16[1,64,512]{2,1,0:T(8,128)(2,1)S(1)} %get-tuple-element.37), channel_id=1, source_target_pairs={{0,9},{1,8},{4,13},{5,12},{8,1},{9,0},{12,5},{13,4},{2,11},{3,10},... | collective-permute-start | bytes 196616 | tf_op jit(solution)/shard_map/ppermute | solution.py:338
  36.5 3.6 %collective-permute-start.18 = (bf16[1,64,512]{2,1,0:T(8,128)(2,1)S(1)}, bf16[1,64,512]{2,1,0:T(8,128)(2,1)S(1)}, u32[]{:S(2)}, u32[]{:S(2)}) collective-permute-start(bf16[1,64,512]{2,1,0:T(8,128)(2,1)S(1)} %get-tuple-element.38), channel_id=1, source_target_pairs={{0,1},{1,0},{4,5},{5,4},{8,9},{9,8},{12,13},{13,12},{2,3},{3,2},{6... | collective-permute-start | bytes 196616 | tf_op jit(solution)/shard_map/ppermute | solution.py:338
  37.0 12.1 %collective-permute-start.10 = (bf16[2,64,512]{2,1,0:T(8,128)(2,1)S(1)}, bf16[2,64,512]{2,1,0:T(8,128)(2,1)S(1)}, u32[]{:S(2)}, u32[]{:S(2)}) collective-permute-start(bf16[2,64,512]{2,1,0:T(8,128)(2,1)S(1)} %get-tuple-element.29), channel_id=1, source_target_pairs={{0,8},{1,9},{4,12},{5,13},{8,0},{9,1},{12,4},{13,5},{2,10},{3,11},... | collective-permute-start | bytes 393224 | tf_op jit(solution)/shard_map/ppermute | solution.py:338
  37.1 14.7 %collective-permute-start.11 = (bf16[2,64,512]{2,1,0:T(8,128)(2,1)S(1)}, bf16[2,64,512]{2,1,0:T(8,128)(2,1)S(1)}, u32[]{:S(2)}, u32[]{:S(2)}) collective-permute-start(bf16[2,64,512]{2,1,0:T(8,128)(2,1)S(1)} %get-tuple-element.30), channel_id=1, source_target_pairs={{0,9},{1,8},{4,13},{5,12},{8,1},{9,0},{12,5},{13,4},{2,11},{3,10},... | collective-permute-start | bytes 393224 | tf_op jit(solution)/shard_map/ppermute | solution.py:338
  39.8 12.0 %collective-permute-start.12 = (bf16[2,64,512]{2,1,0:T(8,128)(2,1)S(1)}, bf16[2,64,512]{2,1,0:T(8,128)(2,1)S(1)}, u32[]{:S(2)}, u32[]{:S(2)}) collective-permute-start(bf16[2,64,512]{2,1,0:T(8,128)(2,1)S(1)} %get-tuple-element.31), channel_id=1, source_target_pairs={{0,1},{1,0},{4,5},{5,4},{8,9},{9,8},{12,13},{13,12},{2,3},{3,2},{6... | collective-permute-start | bytes 393224 | tf_op jit(solution)/shard_map/ppermute | solution.py:338

commit v18 on v15

--- a/solution.py
+++ b/solution.py
@@ -235,6 +235,7 @@
     terms, parts = list(results[:n]), list(results[n:])
     for k in range(1, n):
         terms[k] = lax.ppermute(terms[k], "src", [(i, peer(i, k, n)) for i in range(n)])
+    order = [0, half, *(k for k in range(1, n) if k != half)]
     own = pl.pallas_call(
         functools.partial(codes_kernel, n, share, tile_rows),
         out_shape=shape(half, share, 2 * block),
@@ -243,15 +244,12 @@
         compiler_params=params,
         cost_estimate=weight(20),
         name="codes",
-    )(active, enc_b.reshape(n, block), *terms)
+    )(active, enc_b.reshape(n, block), *[terms[k] for k in order])
     codes = []
     for k in range(groups):
-        for r in range(2):
-            perm = [
-                (i * 2 + c, (i + k) % groups * 2 + (c ^ r)) for i in range(groups) for c in range(2)
-            ]
-            codes.append(lax.ppermute(own, ("tgt", "rep"), perm) if k + r else own)
-
+        perm = [(i, (i + k) % groups) for i in range(groups)]
+        codes.append(lax.ppermute(own, "tgt", perm) if k else own)
+        codes.append(lax.ppermute(codes[-1], "rep", [(0, 1), (1, 0)]))
     lhs = pl.pallas_call(
         functools.partial(gather_kernel, n),
         out_shape=shape(rows, 2 * groups * block),

time: 49.5 us -> 51.9 us (1.048)
  waiting for transfers between devices: 21.7 us -> 26 us
  starting transfers between devices: 20.9 us -> 19 us
    ppermute x1, waiting for transfers between devices: 2.53 us -> 5.05 us  [body(): got.append(lax.ppermute(got[0], 'parts', [(0, 1), (1, 0)]))]
    ppermute x3, waiting for transfers between devices: 0.81 us -> 2.78 us  [the longest x1 2.78 us: body(): codes.append(lax.ppermute(own, 'tgt', perm) if k else own)]
    ppermute x1, waiting for transfers between devices: 1.6 us -> 0.01 us  [body(): got = [lax.ppermute(parts[0], 'src', pair)]]
    ppermute x9, starting transfers between devices: 10.9 us -> 9.33 us  [body(): sums[i].append(lax.ppermute(terms[2 * j + r], ('src', 'rep'), perm))]
    ppermute x9, waiting for transfers between devices: 9.54 us -> 11.1 us  [body(): sums[i].append(lax.ppermute(terms[2 * j + r], ('src', 'rep'), perm))]
where the time goes in v18:
time: 51.9 us; the launch traced here: 51.8 us
  waiting for transfers between devices  26 us (50%)
  starting transfers between devices  19 us (37%)
  Pallas kernels  6.57 us (13%)
    ppermute x9, waiting for transfers between devices, body(): sums[i].append(lax.ppermute(terms[2 * j + r], ('src', 'rep'), perm))  11.1 us
    ppermute x9, starting transfers between devices, body(): sums[i].append(lax.ppermute(terms[2 * j + r], ('src', 'rep'), perm))  9.33 us
    ppermute x3, waiting for transfers between devices, body(): lax.ppermute(terms[k], 'src', [(i, peer(i, k, n)) for i in range(n)])  5.92 us
    ppermute x3, starting transfers between devices, body(): lax.ppermute(terms[k], 'src', [(i, peer(i, k, n)) for i in range(n)])  5.68 us
    ppermute x1, waiting for transfers between devices, body(): got.append(lax.ppermute(got[0], 'parts', [(0, 1), (1, 0)]))  5.05 us
    pallas_call x1, Pallas kernels, body(): pl.pallas_call(functools.partial(encode_kernel, n, fetched), out_shape=[s...  3.16 us
    ppermute x1, waiting for transfers between devices, body(): codes.append(lax.ppermute(own, 'tgt', perm) if k else own)  2.78 us
    pallas_call x2, Pallas kernels, add(): pl.pallas_call(functools.partial(add_kernel, n, [pieces[i] for i in some]...  1.58 us
  transfers between devices with their start and end apart: 18, of which 10 were waited for; matrix products, arithmetic and copies ran while one was open for 0% of the time, Pallas kernels for 5%

profile of v18, /device:TPU:0, one launch (start us, length us, event | category | flops | bytes accessed | tf_op | source)
XLA Modules:
  0.0 51.8 jit_solution(2002407653810892794)
XLA Ops:
  0.0 3.2 %encode.1 = (bf16[128,256]{1,0:T(8,128)(2,1)S(1)}, bf16[128,256]{1,0:T(8,128)(2,1)S(1)}, bf16[128,256]{1,0:T(8,128)(2,1)S(1)}, bf16[128,256]{1,0:T(8,128)(2,1)S(...) custom-call(bf16[2,2,64,1024]{3,2,1,0:T(8,128)(2,1)} %bitcast.3, bf16[1024,512]{1,0:T(8,128)(2,1)} %w_hbm.1, ...), custom_call_target="tpu_custom_call" | custom-call | tf_op jit(solution)/shard_map/encode/pallas_call | solution.py:218
  3.2 4.1 %collective-permute-start = (bf16[128,256]{1,0:T(8,128)(2,1)S(1)}, bf16[128,256]{1,0:T(8,128)(2,1)S(1)}, u32[]{:S(2)}, u32[]{:S(2)}) collective-permute-start(bf16[128,256]{1,0:T(8,128)(2,1)S(1)} %get-tuple-element.24), channel_id=1, source_target_pairs={{0,8},{4,12},{8,0},{12,4},{1,9},{5,13},{9,1},{13,5},{2,10},{6,14},... | collective-permute-start | bytes 196616 | tf_op jit(solution)/shard_map/ppermute | solution.py:237
  7.3 1.6 %collective-permute-start.1 = (bf16[128,256]{1,0:T(8,128)(2,1)S(1)}, bf16[128,256]{1,0:T(8,128)(2,1)S(1)}, u32[]{:S(2)}, u32[]{:S(2)}) collective-permute-start(bf16[128,256]{1,0:T(8,128)(2,1)S(1)} %get-tuple-element.25), channel_id=1, source_target_pairs={{0,4},{4,0},{8,12},{12,8},{1,5},{5,1},{9,13},{13,9},{2,6},{6,2},{1... | collective-permute-start | bytes 196616 | tf_op jit(solution)/shard_map/ppermute | solution.py:237
  8.8 0.0 collective-permute-start.2
  8.8 0.9 %collective-permute-start.7 = (bf16[1,2,128,640]{3,2,1,0:T(8,128)(2,1)S(1)}, bf16[1,2,128,640]{3,2,1,0:T(8,128)(2,1)S(1)}, u32[]{:S(2)}, u32[]{:S(2)}) collective-permute-start(bf16[1,2,128,640]{3,2,1,0:T(8,128)(2,1)S(1)} %get-tuple-element.28), channel_id=1, source_target_pairs={{0,4},{4,0},{8,12},{12,8},{1,5},{5,1},{9,13},{13,9},{2,6},{6,2},{1... | collective-permute-start | bytes 983048 | tf_op jit(solution)/shard_map/ppermute | solution.py:275
  9.8 0.6 %collective-permute-done.refs_1_ = bf16[128,256]{1,0:T(8,128)(2,1)S(1)} collective-permute-done((bf16[128,256]{1,0:T(8,128)(2,1)S(1)}, bf16[128,256]{1,0:T(8,128)(2,1)S(1)}, u32[]{:S(2)}, u32[]{:S(2)}) %collective-permute-start) | collective-permute-done | bytes 65568 | tf_op jit(solution)/shard_map/ppermute | solution.py:237
  10.3 1.9 %collective-permute-done.1.refs_2_ = bf16[128,256]{1,0:T(8,128)(2,1)S(1)} collective-permute-done((bf16[128,256]{1,0:T(8,128)(2,1)S(1)}, bf16[128,256]{1,0:T(8,128)(2,1)S(1)}, u32[]{:S(2)}, u32[]{:S(2)}) %collective-permute-start.1) | collective-permute-done | bytes 65568 | tf_op jit(solution)/shard_map/ppermute | solution.py:237
  12.2 3.5 %collective-permute-done.2.refs_3_ = bf16[128,256]{1,0:T(8,128)(2,1)S(1)} collective-permute-done((bf16[128,256]{1,0:T(8,128)(2,1)S(1)}, bf16[128,256]{1,0:T(8,128)(2,1)S(1)}, u32[]{:S(2)}, u32[]{:S(2)}) %collective-permute-start.2) | collective-permute-done | bytes 65568 | tf_op jit(solution)/shard_map/ppermute | solution.py:237
  15.7 0.0 copy-done.4
  15.7 0.0 copy-done.3
  15.7 0.6 %codes.1.refs_0_.refs_1_ = bf16[2,64,256]{2,1,0:T(8,128)(2,1)S(1)} custom-call(s32[2,8]{1,0:T(2,128)S(1)} %copy-done.4, f32[4,128]{1,0:T(4,128)S(1)} %bitcast.2, bf16[128,256]{1,0:T(8,128)(2,1)S(1)} %get-tuple-element.23.refs_0_, bf16[128,256]{1,0:T(8,128)(2,1)S(1)} %collective-permute-done.refs_1_, bf16[128,256]{1,0:T(8,128)(2,1)S(1)} %collective-permute-done.1.refs_2_, ...), custom_call_target="tpu_custom_call" | custom-call | flops 20000000000 | tf_op jit(solution)/shard_map/codes/pallas_call | solution.py:239
  16.3 1.6 %collective-permute-start.4 = (bf16[2,64,256]{2,1,0:T(8,128)(2,1)S(1)}, bf16[2,64,256]{2,1,0:T(8,128)(2,1)S(1)}, u32[]{:S(2)}, u32[]{:S(2)}) collective-permute-start(bf16[2,64,256]{2,1,0:T(8,128)(2,1)S(1)} %codes.1.refs_0_.refs_1_), channel_id=1, source_target_pairs={{0,2},{2,0},{1,3},{3,1},{4,6},{6,4},{5,7},{7,5},{8,10},{10,8},{9,1... | collective-permute-start | bytes 196616 | tf_op jit(solution)/shard_map/ppermute | solution.py:251
  17.9 0.0 collective-permute-start.3
  17.9 2.8 %collective-permute-done.4.refs_2_ = bf16[2,64,256]{2,1,0:T(8,128)(2,1)S(1)} collective-permute-done((bf16[2,64,256]{2,1,0:T(8,128)(2,1)S(1)}, bf16[2,64,256]{2,1,0:T(8,128)(2,1)S(1)}, u32[]{:S(2)}, u32[]{:S(2)}) %collective-permute-start.4) | collective-permute-done | bytes 65568 | tf_op jit(solution)/shard_map/ppermute | solution.py:251
  20.6 0.0 collective-permute-start.5
  20.6 0.0 collective-permute-start.6
  20.7 0.0 collective-permute-done.7.got_ref
  20.7 1.6 %collective-permute-start.8 = (bf16[1,2,128,640]{3,2,1,0:T(8,128)(2,1)S(1)}, bf16[1,2,128,640]{3,2,1,0:T(8,128)(2,1)S(1)}, u32[]{:S(2)}, u32[]{:S(2)}) collective-permute-start(bf16[1,2,128,640]{3,2,1,0:T(8,128)(2,1)S(1)} %collective-permute-done.7.got_ref), channel_id=1, source_target_pairs={{0,16},{16,0},{1,17},{17,1},{2,18},{18,2},{3,19},{19,3},{4,20},{20... | collective-permute-start | bytes 983048 | tf_op jit(solution)/shard_map/ppermute | solution.py:276
  22.2 0.0 collective-permute-done.3.refs_1_
  22.2 0.0 collective-permute-done.5.refs_3_
  22.3 0.0 copy-done
  22.3 0.4 decode.3
  22.7 1.9 %collective-permute-start.12 = (bf16[1,64,640]{2,1,0:T(8,128)(2,1)S(1)}, bf16[1,64,640]{2,1,0:T(8,128)(2,1)S(1)}, u32[]{:S(2)}, u32[]{:S(2)}) collective-permute-start(bf16[1,64,640]{2,1,0:T(8,128)(2,1)S(1)} %get-tuple-element.35), channel_id=1, source_target_pairs={{0,8},{1,9},{4,12},{5,13},{8,0},{9,1},{12,4},{13,5},{2,10},{3,11},... | collective-permute-start | bytes 245768 | tf_op jit(solution)/shard_map/ppermute | solution.py:316
  24.6 0.8 %collective-permute-start.13 = (bf16[1,64,640]{2,1,0:T(8,128)(2,1)S(1)}, bf16[1,64,640]{2,1,0:T(8,128)(2,1)S(1)}, u32[]{:S(2)}, u32[]{:S(2)}) collective-permute-start(bf16[1,64,640]{2,1,0:T(8,128)(2,1)S(1)} %get-tuple-element.36), channel_id=1, source_target_pairs={{0,9},{1,8},{4,13},{5,12},{8,1},{9,0},{12,5},{13,4},{2,11},{3,10},... | collective-permute-start | bytes 245768 | tf_op jit(solution)/shard_map/ppermute | solution.py:316
  25.4 0.3 collective-permute-start.14
  25.8 5.0 %collective-permute-done.8.got_ref = bf16[1,2,128,640]{3,2,1,0:T(8,128)(2,1)S(1)} collective-permute-done((bf16[1,2,128,640]{3,2,1,0:T(8,128)(2,1)S(1)}, bf16[1,2,128,640]{3,2,1,0:T(8,128)(2,1)S(1)}, u32[]{:S(2)}, u32[]{:S(2)}) %collective-permute-start.8) | collective-permute-done | bytes 327712 | tf_op jit(solution)/shard_map/ppermute | solution.py:276
  30.8 0.4 decode.4
  31.2 0.0 copy-start.1
  31.2 0.0 copy-start.2
  31.2 1.7 %collective-permute-start.15 = (bf16[1,64,640]{2,1,0:T(8,128)(2,1)S(1)}, bf16[1,64,640]{2,1,0:T(8,128)(2,1)S(1)}, u32[]{:S(2)}, u32[]{:S(2)}) collective-permute-start(bf16[1,64,640]{2,1,0:T(8,128)(2,1)S(1)} %get-tuple-element.38), channel_id=1, source_target_pairs={{0,8},{1,9},{4,12},{5,13},{8,0},{9,1},{12,4},{13,5},{2,10},{3,11},... | collective-permute-start | bytes 245768 | tf_op jit(solution)/shard_map/ppermute | solution.py:316
  32.9 0.0 collective-permute-done.12.refs_0_
  32.9 1.7 %collective-permute-start.16 = (bf16[1,64,640]{2,1,0:T(8,128)(2,1)S(1)}, bf16[1,64,640]{2,1,0:T(8,128)(2,1)S(1)}, u32[]{:S(2)}, u32[]{:S(2)}) collective-permute-start(bf16[1,64,640]{2,1,0:T(8,128)(2,1)S(1)} %get-tuple-element.39), channel_id=1, source_target_pairs={{0,9},{1,8},{4,13},{5,12},{8,1},{9,0},{12,5},{13,4},{2,11},{3,10},... | collective-permute-start | bytes 245768 | tf_op jit(solution)/shard_map/ppermute | solution.py:316
  34.6 1.1 %collective-permute-done.6.got_ref = bf16[2,2,128,384]{3,2,1,0:T(8,128)(2,1)S(1)} collective-permute-done((bf16[2,2,128,384]{3,2,1,0:T(8,128)(2,1)S(1)}, bf16[2,2,128,384]{3,2,1,0:T(8,128)(2,1)S(1)}, u32[]{:S(2)}, u32[]{:S(2)}) %collective-permute-start.6) | collective-permute-done | bytes 393248 | tf_op jit(solution)/shard_map/ppermute | solution.py:277
  35.8 0.0 collective-permute-start.17
  35.8 0.4 decode.5
  36.2 0.0 collective-permute-done.13.refs_1_
  36.2 0.6 %collective-permute-start.9 = (bf16[2,64,384]{2,1,0:T(8,128)(2,1)S(1)}, bf16[2,64,384]{2,1,0:T(8,128)(2,1)S(1)}, u32[]{:S(2)}, u32[]{:S(2)}) collective-permute-start(bf16[2,64,384]{2,1,0:T(8,128)(2,1)S(1)} %get-tuple-element.31), channel_id=1, source_target_pairs={{0,8},{1,9},{4,12},{5,13},{8,0},{9,1},{12,4},{13,5},{2,10},{3,11},... | collective-permute-start | bytes 294920 | tf_op jit(solution)/shard_map/ppermute | solution.py:316
  36.8 0.0 collective-permute-done.14.refs_2_
  36.8 2.3 %collective-permute-start.10 = (bf16[2,64,384]{2,1,0:T(8,128)(2,1)S(1)}, bf16[2,64,384]{2,1,0:T(8,128)(2,1)S(1)}, u32[]{:S(2)}, u32[]{:S(2)}) collective-permute-start(bf16[2,64,384]{2,1,0:T(8,128)(2,1)S(1)} %get-tuple-element.32), channel_id=1, source_target_pairs={{0,9},{1,8},{4,13},{5,12},{8,1},{9,0},{12,5},{13,4},{2,11},{3,10},... | collective-permute-start | bytes 294920 | tf_op jit(solution)/shard_map/ppermute | solution.py:316
  39.1 6.2 %collective-permute-done.15.refs_4_ = bf16[1,64,640]{2,1,0:T(8,128)(2,1)S(1)} collective-permute-done((bf16[1,64,640]{2,1,0:T(8,128)(2,1)S(1)}, bf16[1,64,640]{2,1,0:T(8,128)(2,1)S(1)}, u32[]{:S(2)}, u32[]{:S(2)}) %collective-permute-start.15) | collective-permute-done | bytes 81952 | tf_op jit(solution)/shard_map/ppermute | solution.py:316
  45.2 0.0 collective-permute-start.11
  45.2 1.6 %collective-permute-done.16.refs_5_ = bf16[1,64,640]{2,1,0:T(8,128)(2,1)S(1)} collective-permute-done((bf16[1,64,640]{2,1,0:T(8,128)(2,1)S(1)}, bf16[1,64,640]{2,1,0:T(8,128)(2,1)S(1)}, u32[]{:S(2)}, u32[]{:S(2)}) %collective-permute-start.16) | collective-permute-done | bytes 81952 | tf_op jit(solution)/shard_map/ppermute | solution.py:316
  46.8 0.0 collective-permute-done.17.refs_6_
  46.8 0.8 %add.2.refs_4_ = bf16[2,64,2048]{2,1,0:T(8,128)(2,1)} custom-call(f32[2,2048]{1,0:T(2,128)S(1)} %copy-done.2, bf16[2,64,2048]{2,1,0:T(8,128)(2,1)S(1)} %copy-done.1, bf16[1,64,640]{2,1,0:T(8,128)(2,1)S(1)} %collective-permute-done.12.refs_0_, bf16[1,64,640]{2,1,0:T(8,128)(2,1)S(1)} %collective-permute-done.13.refs_1_, ...), custom_call_target="tpu_custom_call" | custom-call | flops 20000000000 | tf_op jit(solution)/shard_map/add/pallas_call | solution.py:283
  47.6 1.5 %collective-permute-done.9.refs_0_ = bf16[2,64,384]{2,1,0:T(8,128)(2,1)S(1)} collective-permute-done((bf16[2,64,384]{2,1,0:T(8,128)(2,1)S(1)}, bf16[2,64,384]{2,1,0:T(8,128)(2,1)S(1)}, u32[]{:S(2)}, u32[]{:S(2)}) %collective-permute-start.9) | collective-permute-done | bytes 98336 | tf_op jit(solution)/shard_map/ppermute | solution.py:316
  49.1 1.9 %collective-permute-done.10.refs_1_ = bf16[2,64,384]{2,1,0:T(8,128)(2,1)S(1)} collective-permute-done((bf16[2,64,384]{2,1,0:T(8,128)(2,1)S(1)}, bf16[2,64,384]{2,1,0:T(8,128)(2,1)S(1)}, u32[]{:S(2)}, u32[]{:S(2)}) %collective-permute-start.10) | collective-permute-done | bytes 98336 | tf_op jit(solution)/shard_map/ppermute | solution.py:316
  51.0 0.0 collective-permute-done.11.refs_2_
  51.0 0.8 %add.3 = bf16[2,64,2048]{2,1,0:T(8,128)(2,1)} custom-call(f32[2,2048]{1,0:T(2,128)S(1)} %copy-done.2, bf16[2,64,2048]{2,1,0:T(8,128)(2,1)S(1)} %copy-done.1, bf16[2,64,384]{2,1,0:T(8,128)(2,1)S(1)} %collective-permute-done.9.refs_0_, bf16[2,64,384]{2,1,0:T(8,128)(2,1)S(1)} %collective-permute-done.10.refs_1_, ...), custom_call_target="tpu_custom_call", output_to_operand_aliasing={{}: (6, {})} | custom-call | tf_op jit(solution)/shard_map/add/pallas_call | solution.py:283
  (7 shorter events, 0.1 us)
Async XLA Ops:
  0.0 15.7 %copy-start.4 = (s32[2,8]{1,0:T(2,128)S(1)}, s32[2,8]{1,0:T(2,128)}, u32[]{:S(2)}) copy-start(s32[2,8]{1,0:T(2,128)} %active_ref.1) | copy-start | bytes 196
  0.0 15.7 %copy-start.3 = (f32[512]{0:T(512)S(1)}, f32[512]{0:T(512)}, u32[]{:S(2)}) copy-start(f32[512]{0:T(512)} %param.9) | copy-start | bytes 6148
  3.2 7.1 %collective-permute-start = (bf16[128,256]{1,0:T(8,128)(2,1)S(1)}, bf16[128,256]{1,0:T(8,128)(2,1)S(1)}, u32[]{:S(2)}, u32[]{:S(2)}) collective-permute-start(bf16[128,256]{1,0:T(8,128)(2,1)S(1)} %get-tuple-element.24), channel_id=1, source_target_pairs={{0,8},{4,12},{8,0},{12,4},{1,9},{5,13},{9,1},{13,5},{2,10},{6,14},... | collective-permute-start | bytes 196616 | tf_op jit(solution)/shard_map/ppermute | solution.py:237
  7.3 5.0 %collective-permute-start.1 = (bf16[128,256]{1,0:T(8,128)(2,1)S(1)}, bf16[128,256]{1,0:T(8,128)(2,1)S(1)}, u32[]{:S(2)}, u32[]{:S(2)}) collective-permute-start(bf16[128,256]{1,0:T(8,128)(2,1)S(1)} %get-tuple-element.25), channel_id=1, source_target_pairs={{0,4},{4,0},{8,12},{12,8},{1,5},{5,1},{9,13},{13,9},{2,6},{6,2},{1... | collective-permute-start | bytes 196616 | tf_op jit(solution)/shard_map/ppermute | solution.py:237
  8.8 6.8 %collective-permute-start.2 = (bf16[128,256]{1,0:T(8,128)(2,1)S(1)}, bf16[128,256]{1,0:T(8,128)(2,1)S(1)}, u32[]{:S(2)}, u32[]{:S(2)}) collective-permute-start(bf16[128,256]{1,0:T(8,128)(2,1)S(1)} %get-tuple-element.26), channel_id=1, source_target_pairs={{0,12},{4,8},{8,4},{12,0},{1,13},{5,9},{9,5},{13,1},{2,14},{6,10},... | collective-permute-start | bytes 196616 | tf_op jit(solution)/shard_map/ppermute | solution.py:237
  8.8 11.8 %collective-permute-start.7 = (bf16[1,2,128,640]{3,2,1,0:T(8,128)(2,1)S(1)}, bf16[1,2,128,640]{3,2,1,0:T(8,128)(2,1)S(1)}, u32[]{:S(2)}, u32[]{:S(2)}) collective-permute-start(bf16[1,2,128,640]{3,2,1,0:T(8,128)(2,1)S(1)} %get-tuple-element.28), channel_id=1, source_target_pairs={{0,4},{4,0},{8,12},{12,8},{1,5},{5,1},{9,13},{13,9},{2,6},{6,2},{1... | collective-permute-start | bytes 983048 | tf_op jit(solution)/shard_map/ppermute | solution.py:275
  16.3 4.3 %collective-permute-start.4 = (bf16[2,64,256]{2,1,0:T(8,128)(2,1)S(1)}, bf16[2,64,256]{2,1,0:T(8,128)(2,1)S(1)}, u32[]{:S(2)}, u32[]{:S(2)}) collective-permute-start(bf16[2,64,256]{2,1,0:T(8,128)(2,1)S(1)} %codes.1.refs_0_.refs_1_), channel_id=1, source_target_pairs={{0,2},{2,0},{1,3},{3,1},{4,6},{6,4},{5,7},{7,5},{8,10},{10,8},{9,1... | collective-permute-start | bytes 196616 | tf_op jit(solution)/shard_map/ppermute | solution.py:251
  17.9 4.4 %collective-permute-start.3 = (bf16[2,64,256]{2,1,0:T(8,128)(2,1)S(1)}, bf16[2,64,256]{2,1,0:T(8,128)(2,1)S(1)}, u32[]{:S(2)}, u32[]{:S(2)}) collective-permute-start(bf16[2,64,256]{2,1,0:T(8,128)(2,1)S(1)} %codes.1.refs_0_.refs_1_), channel_id=1, source_target_pairs={{0,1},{1,0},{2,3},{3,2},{4,5},{5,4},{6,7},{7,6},{8,9},{9,8},{10,11... | collective-permute-start | bytes 196616 | tf_op jit(solution)/shard_map/ppermute | solution.py:252
  20.6 1.6 %collective-permute-start.5 = (bf16[2,64,256]{2,1,0:T(8,128)(2,1)S(1)}, bf16[2,64,256]{2,1,0:T(8,128)(2,1)S(1)}, u32[]{:S(2)}, u32[]{:S(2)}) collective-permute-start(bf16[2,64,256]{2,1,0:T(8,128)(2,1)S(1)} %collective-permute-done.4.refs_2_), channel_id=1, source_target_pairs={{0,1},{1,0},{2,3},{3,2},{4,5},{5,4},{6,7},{7,6},{8,9},{9,8},{10,11... | collective-permute-start | bytes 196616 | tf_op jit(solution)/shard_map/ppermute | solution.py:252
  20.6 1.7 %copy-start = (bf16[2,2,128,2048]{3,2,1,0:T(8,128)(2,1)S(1)}, bf16[2,2,128,2048]{3,2,1,0:T(8,128)(2,1)}, u32[]{:S(2)}) copy-start(bf16[2,2,128,2048]{3,2,1,0:T(8,128)(2,1)} %dec_ref.5) | copy-start | bytes 6291460
  20.6 15.1 %collective-permute-start.6 = (bf16[2,2,128,384]{3,2,1,0:T(8,128)(2,1)S(1)}, bf16[2,2,128,384]{3,2,1,0:T(8,128)(2,1)S(1)}, u32[]{:S(2)}, u32[]{:S(2)}) collective-permute-start(bf16[2,2,128,384]{3,2,1,0:T(8,128)(2,1)S(1)} %hold.1), channel_id=1, source_target_pairs={{0,4},{4,0},{8,12},{12,8},{1,5},{5,1},{9,13},{13,9},{2,6},{6,2},{1... | collective-permute-start | bytes 1179656 | tf_op jit(solution)/shard_map/ppermute | solution.py:277
  20.7 10.2 %collective-permute-start.8 = (bf16[1,2,128,640]{3,2,1,0:T(8,128)(2,1)S(1)}, bf16[1,2,128,640]{3,2,1,0:T(8,128)(2,1)S(1)}, u32[]{:S(2)}, u32[]{:S(2)}) collective-permute-start(bf16[1,2,128,640]{3,2,1,0:T(8,128)(2,1)S(1)} %collective-permute-done.7.got_ref), channel_id=1, source_target_pairs={{0,16},{16,0},{1,17},{17,1},{2,18},{18,2},{3,19},{19,3},{4,20},{20... | collective-permute-start | bytes 983048 | tf_op jit(solution)/shard_map/ppermute | solution.py:276
  22.7 10.2 %collective-permute-start.12 = (bf16[1,64,640]{2,1,0:T(8,128)(2,1)S(1)}, bf16[1,64,640]{2,1,0:T(8,128)(2,1)S(1)}, u32[]{:S(2)}, u32[]{:S(2)}) collective-permute-start(bf16[1,64,640]{2,1,0:T(8,128)(2,1)S(1)} %get-tuple-element.35), channel_id=1, source_target_pairs={{0,8},{1,9},{4,12},{5,13},{8,0},{9,1},{12,4},{13,5},{2,10},{3,11},... | collective-permute-start | bytes 245768 | tf_op jit(solution)/shard_map/ppermute | solution.py:316
  24.6 11.6 %collective-permute-start.13 = (bf16[1,64,640]{2,1,0:T(8,128)(2,1)S(1)}, bf16[1,64,640]{2,1,0:T(8,128)(2,1)S(1)}, u32[]{:S(2)}, u32[]{:S(2)}) collective-permute-start(bf16[1,64,640]{2,1,0:T(8,128)(2,1)S(1)} %get-tuple-element.36), channel_id=1, source_target_pairs={{0,9},{1,8},{4,13},{5,12},{8,1},{9,0},{12,5},{13,4},{2,11},{3,10},... | collective-permute-start | bytes 245768 | tf_op jit(solution)/shard_map/ppermute | solution.py:316
  25.4 11.3 %collective-permute-start.14 = (bf16[1,64,640]{2,1,0:T(8,128)(2,1)S(1)}, bf16[1,64,640]{2,1,0:T(8,128)(2,1)S(1)}, u32[]{:S(2)}, u32[]{:S(2)}) collective-permute-start(bf16[1,64,640]{2,1,0:T(8,128)(2,1)S(1)} %get-tuple-element.37), channel_id=1, source_target_pairs={{0,1},{1,0},{4,5},{5,4},{8,9},{9,8},{12,13},{13,12},{2,3},{3,2},{6... | collective-permute-start | bytes 245768 | tf_op jit(solution)/shard_map/ppermute | solution.py:316
  31.2 15.6 %copy-start.1 = (bf16[2,64,2048]{2,1,0:T(8,128)(2,1)S(1)}, bf16[2,64,2048]{2,1,0:T(8,128)(2,1)}, u32[]{:S(2)}) copy-start(bf16[2,64,2048]{2,1,0:T(8,128)(2,1)} %target_ref.3) | copy-start | bytes 1572868
  31.2 15.6 %copy-start.2 = (f32[2,2048]{1,0:T(2,128)S(1)}, f32[2,2048]{1,0:T(2,128)}, u32[]{:S(2)}) copy-start(f32[2,2048]{1,0:T(2,128)} %bias_ref.3) | copy-start | bytes 49156
  31.2 14.0 %collective-permute-start.15 = (bf16[1,64,640]{2,1,0:T(8,128)(2,1)S(1)}, bf16[1,64,640]{2,1,0:T(8,128)(2,1)S(1)}, u32[]{:S(2)}, u32[]{:S(2)}) collective-permute-start(bf16[1,64,640]{2,1,0:T(8,128)(2,1)S(1)} %get-tuple-element.38), channel_id=1, source_target_pairs={{0,8},{1,9},{4,12},{5,13},{8,0},{9,1},{12,4},{13,5},{2,10},{3,11},... | collective-permute-start | bytes 245768 | tf_op jit(solution)/shard_map/ppermute | solution.py:316
  32.9 13.9 %collective-permute-start.16 = (bf16[1,64,640]{2,1,0:T(8,128)(2,1)S(1)}, bf16[1,64,640]{2,1,0:T(8,128)(2,1)S(1)}, u32[]{:S(2)}, u32[]{:S(2)}) collective-permute-start(bf16[1,64,640]{2,1,0:T(8,128)(2,1)S(1)} %get-tuple-element.39), channel_id=1, source_target_pairs={{0,9},{1,8},{4,13},{5,12},{8,1},{9,0},{12,5},{13,4},{2,11},{3,10},... | collective-permute-start | bytes 245768 | tf_op jit(solution)/shard_map/ppermute | solution.py:316
  35.8 11.0 %collective-permute-start.17 = (bf16[1,64,640]{2,1,0:T(8,128)(2,1)S(1)}, bf16[1,64,640]{2,1,0:T(8,128)(2,1)S(1)}, u32[]{:S(2)}, u32[]{:S(2)}) collective-permute-start(bf16[1,64,640]{2,1,0:T(8,128)(2,1)S(1)} %get-tuple-element.40), channel_id=1, source_target_pairs={{0,1},{1,0},{4,5},{5,4},{8,9},{9,8},{12,13},{13,12},{2,3},{3,2},{6... | collective-permute-start | bytes 245768 | tf_op jit(solution)/shard_map/ppermute | solution.py:316
  36.2 12.9 %collective-permute-start.9 = (bf16[2,64,384]{2,1,0:T(8,128)(2,1)S(1)}, bf16[2,64,384]{2,1,0:T(8,128)(2,1)S(1)}, u32[]{:S(2)}, u32[]{:S(2)}) collective-permute-start(bf16[2,64,384]{2,1,0:T(8,128)(2,1)S(1)} %get-tuple-element.31), channel_id=1, source_target_pairs={{0,8},{1,9},{4,12},{5,13},{8,0},{9,1},{12,4},{13,5},{2,10},{3,11},... | collective-permute-start | bytes 294920 | tf_op jit(solution)/shard_map/ppermute | solution.py:316
  36.8 14.2 %collective-permute-start.10 = (bf16[2,64,384]{2,1,0:T(8,128)(2,1)S(1)}, bf16[2,64,384]{2,1,0:T(8,128)(2,1)S(1)}, u32[]{:S(2)}, u32[]{:S(2)}) collective-permute-start(bf16[2,64,384]{2,1,0:T(8,128)(2,1)S(1)} %get-tuple-element.32), channel_id=1, source_target_pairs={{0,9},{1,8},{4,13},{5,12},{8,1},{9,0},{12,5},{13,4},{2,11},{3,10},... | collective-permute-start | bytes 294920 | tf_op jit(solution)/shard_map/ppermute | solution.py:316
  45.2 5.8 %collective-permute-start.11 = (bf16[2,64,384]{2,1,0:T(8,128)(2,1)S(1)}, bf16[2,64,384]{2,1,0:T(8,128)(2,1)S(1)}, u32[]{:S(2)}, u32[]{:S(2)}) collective-permute-start(bf16[2,64,384]{2,1,0:T(8,128)(2,1)S(1)} %get-tuple-element.33), channel_id=1, source_target_pairs={{0,1},{1,0},{4,5},{5,4},{8,9},{9,8},{12,13},{13,12},{2,3},{3,2},{6... | collective-permute-start | bytes 294920 | tf_op jit(solution)/shard_map/ppermute | solution.py:316

commit v19 on v15

--- a/solution.py
+++ b/solution.py
@@ -9,7 +9,7 @@
 
 VMEM_BYTES = 32 * 1024 * 1024
 LANES = 128
-FIRST = 5
+FIRST = 6
 PIECES = (((0,), 0, False), ((1,), 0, True), ((0, 1), 1, False))
 
 

time: 49.5 us -> 48.5 us (0.980)
  the two profiles are of different devices: /device:TPU:0 before, /device:TPU:9 now
where the time goes in v19:
time: 48.5 us; the launch traced here: 48.4 us
  starting transfers between devices  33.3 us (69%)
  waiting for transfers between devices  8.52 us (18%)
  Pallas kernels  6.4 us (13%)
    ppermute x9, starting transfers between devices, body(): sums[i].append(lax.ppermute(terms[2 * j + r], ('src', 'rep'), perm))  22.5 us
    ppermute x3, waiting for transfers between devices, body(): lax.ppermute(terms[k], 'src', [(i, peer(i, k, n)) for i in range(n)])  3.95 us
    ppermute x9, waiting for transfers between devices, body(): sums[i].append(lax.ppermute(terms[2 * j + r], ('src', 'rep'), perm))  3.3 us
    ppermute x3, starting transfers between devices, body(): codes.append(lax.ppermute(own, ('tgt', 'rep'), perm) if k + r else own)  3.12 us
    pallas_call x1, Pallas kernels, body(): pl.pallas_call(functools.partial(encode_kernel, n, fetched), out_shape=[s...  3.09 us
    ppermute x3, starting transfers between devices, body(): lax.ppermute(terms[k], 'src', [(i, peer(i, k, n)) for i in range(n)])  2.71 us
    ppermute x1, starting transfers between devices, body(): got.append(lax.ppermute(hold(parts[1], own), 'src', pair))  2.63 us
    pallas_call x2, Pallas kernels, add(): pl.pallas_call(functools.partial(add_kernel, n, [pieces[i] for i in some]...  1.57 us
  transfers between devices with their start and end apart: 18, of which 6 were waited for; matrix products, arithmetic and copies ran while one was open for 0% of the time, Pallas kernels for 5%

profile of v19, /device:TPU:9, one launch (start us, length us, event | category | flops | bytes accessed | tf_op | source)
XLA Modules:
  0.0 48.4 jit_solution(16098194881419107845)
XLA Ops:
  0.0 3.1 %encode.1 = (bf16[128,256]{1,0:T(8,128)(2,1)S(1)}, bf16[128,256]{1,0:T(8,128)(2,1)S(1)}, bf16[128,256]{1,0:T(8,128)(2,1)S(1)}, bf16[128,256]{1,0:T(8,128)(2,1)S(...) custom-call(bf16[2,2,64,1024]{3,2,1,0:T(8,128)(2,1)} %bitcast.3, bf16[1024,512]{1,0:T(8,128)(2,1)} %w_hbm.1, ...), custom_call_target="tpu_custom_call" | custom-call | tf_op jit(solution)/shard_map/encode/pallas_call | solution.py:218
  3.1 0.1 collective-permute-start
  3.2 2.5 %collective-permute-start.1 = (bf16[128,256]{1,0:T(8,128)(2,1)S(1)}, bf16[128,256]{1,0:T(8,128)(2,1)S(1)}, u32[]{:S(2)}, u32[]{:S(2)}) collective-permute-start(bf16[128,256]{1,0:T(8,128)(2,1)S(1)} %get-tuple-element.25), channel_id=1, source_target_pairs={{0,8},{4,12},{8,0},{12,4},{1,9},{5,13},{9,1},{13,5},{2,10},{6,14},... | collective-permute-start | bytes 196616 | tf_op jit(solution)/shard_map/ppermute | solution.py:237
  5.6 0.2 collective-permute-start.2
  5.8 1.1 %collective-permute-start.7 = (bf16[1,2,128,768]{3,2,1,0:T(8,128)(2,1)S(1)}, bf16[1,2,128,768]{3,2,1,0:T(8,128)(2,1)S(1)}, u32[]{:S(2)}, u32[]{:S(2)}) collective-permute-start(bf16[1,2,128,768]{3,2,1,0:T(8,128)(2,1)S(1)} %get-tuple-element.28), channel_id=1, source_target_pairs={{0,4},{4,0},{8,12},{12,8},{1,5},{5,1},{9,13},{13,9},{2,6},{6,2},{1... | collective-permute-start | bytes 1179656 | tf_op jit(solution)/shard_map/ppermute | solution.py:277
  6.9 0.0 collective-permute-done.refs_1_
  6.9 1.3 %collective-permute-done.1.refs_2_ = bf16[128,256]{1,0:T(8,128)(2,1)S(1)} collective-permute-done((bf16[128,256]{1,0:T(8,128)(2,1)S(1)}, bf16[128,256]{1,0:T(8,128)(2,1)S(1)}, u32[]{:S(2)}, u32[]{:S(2)}) %collective-permute-start.1) | collective-permute-done | bytes 65568 | tf_op jit(solution)/shard_map/ppermute | solution.py:237
  8.3 2.6 %collective-permute-done.2.refs_3_ = bf16[128,256]{1,0:T(8,128)(2,1)S(1)} collective-permute-done((bf16[128,256]{1,0:T(8,128)(2,1)S(1)}, bf16[128,256]{1,0:T(8,128)(2,1)S(1)}, u32[]{:S(2)}, u32[]{:S(2)}) %collective-permute-start.2) | collective-permute-done | bytes 65568 | tf_op jit(solution)/shard_map/ppermute | solution.py:237
  10.9 0.0 copy-done.4
  10.9 0.0 copy-done.3
  10.9 0.6 %codes.1.refs_0_.refs_1_ = bf16[2,64,256]{2,1,0:T(8,128)(2,1)S(1)} custom-call(s32[2,8]{1,0:T(2,128)S(1)} %copy-done.4, f32[4,128]{1,0:T(4,128)S(1)} %bitcast.2, bf16[128,256]{1,0:T(8,128)(2,1)S(1)} %get-tuple-element.23.refs_0_, bf16[128,256]{1,0:T(8,128)(2,1)S(1)} %collective-permute-done.refs_1_, bf16[128,256]{1,0:T(8,128)(2,1)S(1)} %collective-permute-done.1.refs_2_, ...), custom_call_target="tpu_custom_call" | custom-call | flops 20000000000 | tf_op jit(solution)/shard_map/codes/pallas_call | solution.py:238
  11.5 2.6 %collective-permute-start.5 = (bf16[2,64,256]{2,1,0:T(8,128)(2,1)S(1)}, bf16[2,64,256]{2,1,0:T(8,128)(2,1)S(1)}, u32[]{:S(2)}, u32[]{:S(2)}) collective-permute-start(bf16[2,64,256]{2,1,0:T(8,128)(2,1)S(1)} %codes.1.refs_0_.refs_1_), channel_id=1, source_target_pairs={{0,3},{1,2},{2,1},{3,0},{4,7},{5,6},{6,5},{7,4},{8,11},{9,10},{10,... | collective-permute-start | bytes 196616 | tf_op jit(solution)/shard_map/ppermute | solution.py:253
  14.2 0.3 collective-permute-start.4
  14.4 0.2 collective-permute-start.3
  14.6 2.6 %collective-permute-start.6 = (bf16[2,2,128,256]{3,2,1,0:T(8,128)(2,1)S(1)}, bf16[2,2,128,256]{3,2,1,0:T(8,128)(2,1)S(1)}, u32[]{:S(2)}, u32[]{:S(2)}) collective-permute-start(bf16[2,2,128,256]{3,2,1,0:T(8,128)(2,1)S(1)} %hold.1), channel_id=1, source_target_pairs={{0,4},{4,0},{8,12},{12,8},{1,5},{5,1},{9,13},{13,9},{2,6},{6,2},{1... | collective-permute-start | bytes 786440 | tf_op jit(solution)/shard_map/ppermute | solution.py:279
  17.3 0.8 %collective-permute-done.7.got_ref = bf16[1,2,128,768]{3,2,1,0:T(8,128)(2,1)S(1)} collective-permute-done((bf16[1,2,128,768]{3,2,1,0:T(8,128)(2,1)S(1)}, bf16[1,2,128,768]{3,2,1,0:T(8,128)(2,1)S(1)}, u32[]{:S(2)}, u32[]{:S(2)}) %collective-permute-start.7) | collective-permute-done | bytes 393248 | tf_op jit(solution)/shard_map/ppermute | solution.py:277
  18.0 1.2 %collective-permute-start.8 = (bf16[1,2,128,768]{3,2,1,0:T(8,128)(2,1)S(1)}, bf16[1,2,128,768]{3,2,1,0:T(8,128)(2,1)S(1)}, u32[]{:S(2)}, u32[]{:S(2)}) collective-permute-start(bf16[1,2,128,768]{3,2,1,0:T(8,128)(2,1)S(1)} %collective-permute-done.7.got_ref), channel_id=1, source_target_pairs={{0,16},{16,0},{1,17},{17,1},{2,18},{18,2},{3,19},{19,3},{4,20},{20... | collective-permute-start | bytes 1179656 | tf_op jit(solution)/shard_map/ppermute | solution.py:278
  19.3 0.0 collective-permute-done.5.refs_3_
  19.3 0.0 collective-permute-done.4.refs_2_
  19.3 0.0 collective-permute-done.3.refs_1_
  19.3 0.1 gather.1.lhs_ref
  19.4 0.4 decode.3
  19.8 2.5 %collective-permute-start.12 = (bf16[1,64,768]{2,1,0:T(8,128)(2,1)S(1)}, bf16[1,64,768]{2,1,0:T(8,128)(2,1)S(1)}, u32[]{:S(2)}, u32[]{:S(2)}) collective-permute-start(bf16[1,64,768]{2,1,0:T(8,128)(2,1)S(1)} %get-tuple-element.35), channel_id=1, source_target_pairs={{0,8},{1,9},{4,12},{5,13},{8,0},{9,1},{12,4},{13,5},{2,10},{3,11},... | collective-permute-start | bytes 294920 | tf_op jit(solution)/shard_map/ppermute | solution.py:318
  22.3 3.0 %collective-permute-start.13 = (bf16[1,64,768]{2,1,0:T(8,128)(2,1)S(1)}, bf16[1,64,768]{2,1,0:T(8,128)(2,1)S(1)}, u32[]{:S(2)}, u32[]{:S(2)}) collective-permute-start(bf16[1,64,768]{2,1,0:T(8,128)(2,1)S(1)} %get-tuple-element.36), channel_id=1, source_target_pairs={{0,9},{1,8},{4,13},{5,12},{8,1},{9,0},{12,5},{13,4},{2,11},{3,10},... | collective-permute-start | bytes 294920 | tf_op jit(solution)/shard_map/ppermute | solution.py:318
  25.3 0.1 collective-permute-start.14
  25.4 0.5 %collective-permute-done.8.got_ref = bf16[1,2,128,768]{3,2,1,0:T(8,128)(2,1)S(1)} collective-permute-done((bf16[1,2,128,768]{3,2,1,0:T(8,128)(2,1)S(1)}, bf16[1,2,128,768]{3,2,1,0:T(8,128)(2,1)S(1)}, u32[]{:S(2)}, u32[]{:S(2)}) %collective-permute-start.8) | collective-permute-done | bytes 393248 | tf_op jit(solution)/shard_map/ppermute | solution.py:278
  26.0 0.4 decode.4
  26.3 0.0 copy-start.1
  26.3 0.0 copy-start.2
  26.3 2.6 %collective-permute-start.15 = (bf16[1,64,768]{2,1,0:T(8,128)(2,1)S(1)}, bf16[1,64,768]{2,1,0:T(8,128)(2,1)S(1)}, u32[]{:S(2)}, u32[]{:S(2)}) collective-permute-start(bf16[1,64,768]{2,1,0:T(8,128)(2,1)S(1)} %get-tuple-element.38), channel_id=1, source_target_pairs={{0,8},{1,9},{4,12},{5,13},{8,0},{9,1},{12,4},{13,5},{2,10},{3,11},... | collective-permute-start | bytes 294920 | tf_op jit(solution)/shard_map/ppermute | solution.py:318
  28.9 0.0 collective-permute-done.6.got_ref
  28.9 3.6 %collective-permute-start.16 = (bf16[1,64,768]{2,1,0:T(8,128)(2,1)S(1)}, bf16[1,64,768]{2,1,0:T(8,128)(2,1)S(1)}, u32[]{:S(2)}, u32[]{:S(2)}) collective-permute-start(bf16[1,64,768]{2,1,0:T(8,128)(2,1)S(1)} %get-tuple-element.39), channel_id=1, source_target_pairs={{0,9},{1,8},{4,13},{5,12},{8,1},{9,0},{12,5},{13,4},{2,11},{3,10},... | collective-permute-start | bytes 294920 | tf_op jit(solution)/shard_map/ppermute | solution.py:318
  32.6 0.0 collective-permute-done.12.refs_0_
  32.6 0.3 collective-permute-start.17
  32.8 0.3 decode.5
  33.1 0.0 collective-permute-done.13.refs_1_
  33.2 9.9 %collective-permute-start.9 = (bf16[2,64,256]{2,1,0:T(8,128)(2,1)S(1)}, bf16[2,64,256]{2,1,0:T(8,128)(2,1)S(1)}, u32[]{:S(2)}, u32[]{:S(2)}) collective-permute-start(bf16[2,64,256]{2,1,0:T(8,128)(2,1)S(1)} %get-tuple-element.31), channel_id=1, source_target_pairs={{0,8},{1,9},{4,12},{5,13},{8,0},{9,1},{12,4},{13,5},{2,10},{3,11},... | collective-permute-start | bytes 196616 | tf_op jit(solution)/shard_map/ppermute | solution.py:318
  43.0 0.0 collective-permute-done.14.refs_2_
  43.0 0.0 collective-permute-start.10
  43.0 0.0 collective-permute-done.15.refs_4_
  43.1 0.4 collective-permute-start.11
  43.5 0.0 collective-permute-done.16.refs_5_
  43.5 0.0 collective-permute-done.17.refs_6_
  43.5 0.9 %add.2.refs_4_ = bf16[2,64,2048]{2,1,0:T(8,128)(2,1)} custom-call(f32[2,2048]{1,0:T(2,128)S(1)} %copy-done.2, bf16[2,64,2048]{2,1,0:T(8,128)(2,1)S(1)} %copy-done.1, bf16[1,64,768]{2,1,0:T(8,128)(2,1)S(1)} %collective-permute-done.12.refs_0_, bf16[1,64,768]{2,1,0:T(8,128)(2,1)S(1)} %collective-permute-done.13.refs_1_, ...), custom_call_target="tpu_custom_call" | custom-call | flops 20000000000 | tf_op jit(solution)/shard_map/add/pallas_call | solution.py:285
  44.4 1.2 %collective-permute-done.9.refs_0_ = bf16[2,64,256]{2,1,0:T(8,128)(2,1)S(1)} collective-permute-done((bf16[2,64,256]{2,1,0:T(8,128)(2,1)S(1)}, bf16[2,64,256]{2,1,0:T(8,128)(2,1)S(1)}, u32[]{:S(2)}, u32[]{:S(2)}) %collective-permute-start.9) | collective-permute-done | bytes 65568 | tf_op jit(solution)/shard_map/ppermute | solution.py:318
  45.6 2.1 %collective-permute-done.10.refs_1_ = bf16[2,64,256]{2,1,0:T(8,128)(2,1)S(1)} collective-permute-done((bf16[2,64,256]{2,1,0:T(8,128)(2,1)S(1)}, bf16[2,64,256]{2,1,0:T(8,128)(2,1)S(1)}, u32[]{:S(2)}, u32[]{:S(2)}) %collective-permute-start.10) | collective-permute-done | bytes 65568 | tf_op jit(solution)/shard_map/ppermute | solution.py:318
  47.6 0.0 collective-permute-done.11.refs_2_
  47.6 0.7 %add.3 = bf16[2,64,2048]{2,1,0:T(8,128)(2,1)} custom-call(f32[2,2048]{1,0:T(2,128)S(1)} %copy-done.2, bf16[2,64,2048]{2,1,0:T(8,128)(2,1)S(1)} %copy-done.1, bf16[2,64,256]{2,1,0:T(8,128)(2,1)S(1)} %collective-permute-done.9.refs_0_, bf16[2,64,256]{2,1,0:T(8,128)(2,1)S(1)} %collective-permute-done.10.refs_1_, ...), custom_call_target="tpu_custom_call", output_to_operand_aliasing={{}: (6, {})} | custom-call | tf_op jit(solution)/shard_map/add/pallas_call | solution.py:285
  (7 shorter events, 0.0 us)
Async XLA Ops:
  0.0 10.9 %copy-start.4 = (s32[2,8]{1,0:T(2,128)S(1)}, s32[2,8]{1,0:T(2,128)}, u32[]{:S(2)}) copy-start(s32[2,8]{1,0:T(2,128)} %active_ref.1) | copy-start | bytes 196
  0.0 10.9 %copy-start.3 = (f32[512]{0:T(512)S(1)}, f32[512]{0:T(512)}, u32[]{:S(2)}) copy-start(f32[512]{0:T(512)} %param.9) | copy-start | bytes 6148
  3.1 3.8 %collective-permute-start = (bf16[128,256]{1,0:T(8,128)(2,1)S(1)}, bf16[128,256]{1,0:T(8,128)(2,1)S(1)}, u32[]{:S(2)}, u32[]{:S(2)}) collective-permute-start(bf16[128,256]{1,0:T(8,128)(2,1)S(1)} %get-tuple-element.24), channel_id=1, source_target_pairs={{0,4},{4,0},{8,12},{12,8},{1,5},{5,1},{9,13},{13,9},{2,6},{6,2},{1... | collective-permute-start | bytes 196616 | tf_op jit(solution)/shard_map/ppermute | solution.py:237
  3.2 5.1 %collective-permute-start.1 = (bf16[128,256]{1,0:T(8,128)(2,1)S(1)}, bf16[128,256]{1,0:T(8,128)(2,1)S(1)}, u32[]{:S(2)}, u32[]{:S(2)}) collective-permute-start(bf16[128,256]{1,0:T(8,128)(2,1)S(1)} %get-tuple-element.25), channel_id=1, source_target_pairs={{0,8},{4,12},{8,0},{12,4},{1,9},{5,13},{9,1},{13,5},{2,10},{6,14},... | collective-permute-start | bytes 196616 | tf_op jit(solution)/shard_map/ppermute | solution.py:237
  5.6 5.2 %collective-permute-start.2 = (bf16[128,256]{1,0:T(8,128)(2,1)S(1)}, bf16[128,256]{1,0:T(8,128)(2,1)S(1)}, u32[]{:S(2)}, u32[]{:S(2)}) collective-permute-start(bf16[128,256]{1,0:T(8,128)(2,1)S(1)} %get-tuple-element.26), channel_id=1, source_target_pairs={{0,12},{4,8},{8,4},{12,0},{1,13},{5,9},{9,5},{13,1},{2,14},{6,10},... | collective-permute-start | bytes 196616 | tf_op jit(solution)/shard_map/ppermute | solution.py:237
  5.8 12.2 %collective-permute-start.7 = (bf16[1,2,128,768]{3,2,1,0:T(8,128)(2,1)S(1)}, bf16[1,2,128,768]{3,2,1,0:T(8,128)(2,1)S(1)}, u32[]{:S(2)}, u32[]{:S(2)}) collective-permute-start(bf16[1,2,128,768]{3,2,1,0:T(8,128)(2,1)S(1)} %get-tuple-element.28), channel_id=1, source_target_pairs={{0,4},{4,0},{8,12},{12,8},{1,5},{5,1},{9,13},{13,9},{2,6},{6,2},{1... | collective-permute-start | bytes 1179656 | tf_op jit(solution)/shard_map/ppermute | solution.py:277
  11.5 7.8 %collective-permute-start.5 = (bf16[2,64,256]{2,1,0:T(8,128)(2,1)S(1)}, bf16[2,64,256]{2,1,0:T(8,128)(2,1)S(1)}, u32[]{:S(2)}, u32[]{:S(2)}) collective-permute-start(bf16[2,64,256]{2,1,0:T(8,128)(2,1)S(1)} %codes.1.refs_0_.refs_1_), channel_id=1, source_target_pairs={{0,3},{1,2},{2,1},{3,0},{4,7},{5,6},{6,5},{7,4},{8,11},{9,10},{10,... | collective-permute-start | bytes 196616 | tf_op jit(solution)/shard_map/ppermute | solution.py:253
  14.2 5.1 %collective-permute-start.4 = (bf16[2,64,256]{2,1,0:T(8,128)(2,1)S(1)}, bf16[2,64,256]{2,1,0:T(8,128)(2,1)S(1)}, u32[]{:S(2)}, u32[]{:S(2)}) collective-permute-start(bf16[2,64,256]{2,1,0:T(8,128)(2,1)S(1)} %codes.1.refs_0_.refs_1_), channel_id=1, source_target_pairs={{0,2},{1,3},{2,0},{3,1},{4,6},{5,7},{6,4},{7,5},{8,10},{9,11},{10,... | collective-permute-start | bytes 196616 | tf_op jit(solution)/shard_map/ppermute | solution.py:253
  14.4 4.9 %collective-permute-start.3 = (bf16[2,64,256]{2,1,0:T(8,128)(2,1)S(1)}, bf16[2,64,256]{2,1,0:T(8,128)(2,1)S(1)}, u32[]{:S(2)}, u32[]{:S(2)}) collective-permute-start(bf16[2,64,256]{2,1,0:T(8,128)(2,1)S(1)} %codes.1.refs_0_.refs_1_), channel_id=1, source_target_pairs={{0,1},{1,0},{2,3},{3,2},{4,5},{5,4},{6,7},{7,6},{8,9},{9,8},{10,11... | collective-permute-start | bytes 196616 | tf_op jit(solution)/shard_map/ppermute | solution.py:253
  14.6 4.7 %copy-start = (bf16[2,2,128,2048]{3,2,1,0:T(8,128)(2,1)S(1)}, bf16[2,2,128,2048]{3,2,1,0:T(8,128)(2,1)}, u32[]{:S(2)}) copy-start(bf16[2,2,128,2048]{3,2,1,0:T(8,128)(2,1)} %dec_ref.5) | copy-start | bytes 6291460
  14.6 14.3 %collective-permute-start.6 = (bf16[2,2,128,256]{3,2,1,0:T(8,128)(2,1)S(1)}, bf16[2,2,128,256]{3,2,1,0:T(8,128)(2,1)S(1)}, u32[]{:S(2)}, u32[]{:S(2)}) collective-permute-start(bf16[2,2,128,256]{3,2,1,0:T(8,128)(2,1)S(1)} %hold.1), channel_id=1, source_target_pairs={{0,4},{4,0},{8,12},{12,8},{1,5},{5,1},{9,13},{13,9},{2,6},{6,2},{1... | collective-permute-start | bytes 786440 | tf_op jit(solution)/shard_map/ppermute | solution.py:279
  18.0 7.9 %collective-permute-start.8 = (bf16[1,2,128,768]{3,2,1,0:T(8,128)(2,1)S(1)}, bf16[1,2,128,768]{3,2,1,0:T(8,128)(2,1)S(1)}, u32[]{:S(2)}, u32[]{:S(2)}) collective-permute-start(bf16[1,2,128,768]{3,2,1,0:T(8,128)(2,1)S(1)} %collective-permute-done.7.got_ref), channel_id=1, source_target_pairs={{0,16},{16,0},{1,17},{17,1},{2,18},{18,2},{3,19},{19,3},{4,20},{20... | collective-permute-start | bytes 1179656 | tf_op jit(solution)/shard_map/ppermute | solution.py:278
  19.8 12.8 %collective-permute-start.12 = (bf16[1,64,768]{2,1,0:T(8,128)(2,1)S(1)}, bf16[1,64,768]{2,1,0:T(8,128)(2,1)S(1)}, u32[]{:S(2)}, u32[]{:S(2)}) collective-permute-start(bf16[1,64,768]{2,1,0:T(8,128)(2,1)S(1)} %get-tuple-element.35), channel_id=1, source_target_pairs={{0,8},{1,9},{4,12},{5,13},{8,0},{9,1},{12,4},{13,5},{2,10},{3,11},... | collective-permute-start | bytes 294920 | tf_op jit(solution)/shard_map/ppermute | solution.py:318
  22.3 10.9 %collective-permute-start.13 = (bf16[1,64,768]{2,1,0:T(8,128)(2,1)S(1)}, bf16[1,64,768]{2,1,0:T(8,128)(2,1)S(1)}, u32[]{:S(2)}, u32[]{:S(2)}) collective-permute-start(bf16[1,64,768]{2,1,0:T(8,128)(2,1)S(1)} %get-tuple-element.36), channel_id=1, source_target_pairs={{0,9},{1,8},{4,13},{5,12},{8,1},{9,0},{12,5},{13,4},{2,11},{3,10},... | collective-permute-start | bytes 294920 | tf_op jit(solution)/shard_map/ppermute | solution.py:318
  25.3 17.7 %collective-permute-start.14 = (bf16[1,64,768]{2,1,0:T(8,128)(2,1)S(1)}, bf16[1,64,768]{2,1,0:T(8,128)(2,1)S(1)}, u32[]{:S(2)}, u32[]{:S(2)}) collective-permute-start(bf16[1,64,768]{2,1,0:T(8,128)(2,1)S(1)} %get-tuple-element.37), channel_id=1, source_target_pairs={{0,1},{1,0},{4,5},{5,4},{8,9},{9,8},{12,13},{13,12},{2,3},{3,2},{6... | collective-permute-start | bytes 294920 | tf_op jit(solution)/shard_map/ppermute | solution.py:318
  26.3 17.2 %copy-start.1 = (bf16[2,64,2048]{2,1,0:T(8,128)(2,1)S(1)}, bf16[2,64,2048]{2,1,0:T(8,128)(2,1)}, u32[]{:S(2)}) copy-start(bf16[2,64,2048]{2,1,0:T(8,128)(2,1)} %target_ref.3) | copy-start | bytes 1572868
  26.3 17.2 %copy-start.2 = (f32[2,2048]{1,0:T(2,128)S(1)}, f32[2,2048]{1,0:T(2,128)}, u32[]{:S(2)}) copy-start(f32[2,2048]{1,0:T(2,128)} %bias_ref.3) | copy-start | bytes 49156
  26.3 16.7 %collective-permute-start.15 = (bf16[1,64,768]{2,1,0:T(8,128)(2,1)S(1)}, bf16[1,64,768]{2,1,0:T(8,128)(2,1)S(1)}, u32[]{:S(2)}, u32[]{:S(2)}) collective-permute-start(bf16[1,64,768]{2,1,0:T(8,128)(2,1)S(1)} %get-tuple-element.38), channel_id=1, source_target_pairs={{0,8},{1,9},{4,12},{5,13},{8,0},{9,1},{12,4},{13,5},{2,10},{3,11},... | collective-permute-start | bytes 294920 | tf_op jit(solution)/shard_map/ppermute | solution.py:318
  28.9 14.5 %collective-permute-start.16 = (bf16[1,64,768]{2,1,0:T(8,128)(2,1)S(1)}, bf16[1,64,768]{2,1,0:T(8,128)(2,1)S(1)}, u32[]{:S(2)}, u32[]{:S(2)}) collective-permute-start(bf16[1,64,768]{2,1,0:T(8,128)(2,1)S(1)} %get-tuple-element.39), channel_id=1, source_target_pairs={{0,9},{1,8},{4,13},{5,12},{8,1},{9,0},{12,5},{13,4},{2,11},{3,10},... | collective-permute-start | bytes 294920 | tf_op jit(solution)/shard_map/ppermute | solution.py:318
  32.6 10.9 %collective-permute-start.17 = (bf16[1,64,768]{2,1,0:T(8,128)(2,1)S(1)}, bf16[1,64,768]{2,1,0:T(8,128)(2,1)S(1)}, u32[]{:S(2)}, u32[]{:S(2)}) collective-permute-start(bf16[1,64,768]{2,1,0:T(8,128)(2,1)S(1)} %get-tuple-element.40), channel_id=1, source_target_pairs={{0,1},{1,0},{4,5},{5,4},{8,9},{9,8},{12,13},{13,12},{2,3},{3,2},{6... | collective-permute-start | bytes 294920 | tf_op jit(solution)/shard_map/ppermute | solution.py:318
  33.2 12.4 %collective-permute-start.9 = (bf16[2,64,256]{2,1,0:T(8,128)(2,1)S(1)}, bf16[2,64,256]{2,1,0:T(8,128)(2,1)S(1)}, u32[]{:S(2)}, u32[]{:S(2)}) collective-permute-start(bf16[2,64,256]{2,1,0:T(8,128)(2,1)S(1)} %get-tuple-element.31), channel_id=1, source_target_pairs={{0,8},{1,9},{4,12},{5,13},{8,0},{9,1},{12,4},{13,5},{2,10},{3,11},... | collective-permute-start | bytes 196616 | tf_op jit(solution)/shard_map/ppermute | solution.py:318
  43.0 4.6 %collective-permute-start.10 = (bf16[2,64,256]{2,1,0:T(8,128)(2,1)S(1)}, bf16[2,64,256]{2,1,0:T(8,128)(2,1)S(1)}, u32[]{:S(2)}, u32[]{:S(2)}) collective-permute-start(bf16[2,64,256]{2,1,0:T(8,128)(2,1)S(1)} %get-tuple-element.32), channel_id=1, source_target_pairs={{0,9},{1,8},{4,13},{5,12},{8,1},{9,0},{12,5},{13,4},{2,11},{3,10},... | collective-permute-start | bytes 196616 | tf_op jit(solution)/shard_map/ppermute | solution.py:318
  43.1 4.6 %collective-permute-start.11 = (bf16[2,64,256]{2,1,0:T(8,128)(2,1)S(1)}, bf16[2,64,256]{2,1,0:T(8,128)(2,1)S(1)}, u32[]{:S(2)}, u32[]{:S(2)}) collective-permute-start(bf16[2,64,256]{2,1,0:T(8,128)(2,1)S(1)} %get-tuple-element.33), channel_id=1, source_target_pairs={{0,1},{1,0},{4,5},{5,4},{8,9},{9,8},{12,13},{13,12},{2,3},{3,2},{6... | collective-permute-start | bytes 196616 | tf_op jit(solution)/shard_map/ppermute | solution.py:318

commit v20 on v19

--- a/solution.py
+++ b/solution.py
@@ -9,7 +9,7 @@
 
 VMEM_BYTES = 32 * 1024 * 1024
 LANES = 128
-FIRST = 6
+FIRST = 7
 PIECES = (((0,), 0, False), ((1,), 0, True), ((0, 1), 1, False))
 
 

time: 48.5 us -> 50.9 us (1.049)
  the two profiles are of different devices: /device:TPU:9 before, /device:TPU:0 now
where the time goes in v20:
time: 50.9 us; the launch traced here: 50.5 us
  waiting for transfers between devices  22.3 us (44%)
  starting transfers between devices  21.6 us (42%)
  Pallas kernels  6.46 us (13%)
    ppermute x9, starting transfers between devices, body(): sums[i].append(lax.ppermute(terms[2 * j + r], ('src', 'rep'), perm))  11.5 us
    ppermute x9, waiting for transfers between devices, body(): sums[i].append(lax.ppermute(terms[2 * j + r], ('src', 'rep'), perm))  6.03 us
    ppermute x3, waiting for transfers between devices, body(): lax.ppermute(terms[k], 'src', [(i, peer(i, k, n)) for i in range(n)])  5.92 us
    ppermute x1, waiting for transfers between devices, body(): got = [lax.ppermute(parts[0], 'src', pair)]  5.72 us
    ppermute x3, starting transfers between devices, body(): lax.ppermute(terms[k], 'src', [(i, peer(i, k, n)) for i in range(n)])  5.68 us
    ppermute x1, waiting for transfers between devices, body(): got.append(lax.ppermute(got[0], 'parts', [(0, 1), (1, 0)]))  4.65 us
    pallas_call x1, Pallas kernels, body(): pl.pallas_call(functools.partial(encode_kernel, n, fetched), out_shape=[s...  3.03 us
    ppermute x3, starting transfers between devices, body(): codes.append(lax.ppermute(own, ('tgt', 'rep'), perm) if k + r else own)  1.92 us
  transfers between devices with their start and end apart: 18, of which 9 were waited for; matrix products, arithmetic and copies ran while one was open for 0% of the time, Pallas kernels for 5%

profile of v20, /device:TPU:0, one launch (start us, length us, event | category | flops | bytes accessed | tf_op | source)
XLA Modules:
  0.0 50.5 jit_solution(3098429086309169801)
XLA Ops:
  0.0 3.0 %encode.1 = (bf16[128,256]{1,0:T(8,128)(2,1)S(1)}, bf16[128,256]{1,0:T(8,128)(2,1)S(1)}, bf16[128,256]{1,0:T(8,128)(2,1)S(1)}, bf16[128,256]{1,0:T(8,128)(2,1)S(...) custom-call(bf16[2,2,64,1024]{3,2,1,0:T(8,128)(2,1)} %bitcast.3, bf16[1024,512]{1,0:T(8,128)(2,1)} %w_hbm.1, ...), custom_call_target="tpu_custom_call" | custom-call | tf_op jit(solution)/shard_map/encode/pallas_call | solution.py:218
  3.0 3.1 %collective-permute-start = (bf16[128,256]{1,0:T(8,128)(2,1)S(1)}, bf16[128,256]{1,0:T(8,128)(2,1)S(1)}, u32[]{:S(2)}, u32[]{:S(2)}) collective-permute-start(bf16[128,256]{1,0:T(8,128)(2,1)S(1)} %get-tuple-element.24), channel_id=1, source_target_pairs={{0,4},{4,0},{8,12},{12,8},{1,5},{5,1},{9,13},{13,9},{2,6},{6,2},{1... | collective-permute-start | bytes 196616 | tf_op jit(solution)/shard_map/ppermute | solution.py:237
  6.1 2.6 %collective-permute-start.1 = (bf16[128,256]{1,0:T(8,128)(2,1)S(1)}, bf16[128,256]{1,0:T(8,128)(2,1)S(1)}, u32[]{:S(2)}, u32[]{:S(2)}) collective-permute-start(bf16[128,256]{1,0:T(8,128)(2,1)S(1)} %get-tuple-element.25), channel_id=1, source_target_pairs={{0,8},{4,12},{8,0},{12,4},{1,9},{5,13},{9,1},{13,5},{2,10},{6,14},... | collective-permute-start | bytes 196616 | tf_op jit(solution)/shard_map/ppermute | solution.py:237
  8.7 0.0 collective-permute-start.2
  8.7 0.9 %collective-permute-start.7 = (bf16[1,2,128,896]{3,2,1,0:T(8,128)(2,1)S(1)}, bf16[1,2,128,896]{3,2,1,0:T(8,128)(2,1)S(1)}, u32[]{:S(2)}, u32[]{:S(2)}) collective-permute-start(bf16[1,2,128,896]{3,2,1,0:T(8,128)(2,1)S(1)} %get-tuple-element.28), channel_id=1, source_target_pairs={{0,4},{4,0},{8,12},{12,8},{1,5},{5,1},{9,13},{13,9},{2,6},{6,2},{1... | collective-permute-start | bytes 1376264 | tf_op jit(solution)/shard_map/ppermute | solution.py:277
  9.6 0.0 collective-permute-done.refs_1_
  9.6 3.8 %collective-permute-done.1.refs_2_ = bf16[128,256]{1,0:T(8,128)(2,1)S(1)} collective-permute-done((bf16[128,256]{1,0:T(8,128)(2,1)S(1)}, bf16[128,256]{1,0:T(8,128)(2,1)S(1)}, u32[]{:S(2)}, u32[]{:S(2)}) %collective-permute-start.1) | collective-permute-done | bytes 65568 | tf_op jit(solution)/shard_map/ppermute | solution.py:237
  13.4 2.1 %collective-permute-done.2.refs_3_ = bf16[128,256]{1,0:T(8,128)(2,1)S(1)} collective-permute-done((bf16[128,256]{1,0:T(8,128)(2,1)S(1)}, bf16[128,256]{1,0:T(8,128)(2,1)S(1)}, u32[]{:S(2)}, u32[]{:S(2)}) %collective-permute-start.2) | collective-permute-done | bytes 65568 | tf_op jit(solution)/shard_map/ppermute | solution.py:237
  15.5 0.0 copy-done.4
  15.6 0.6 %codes.1.refs_0_.refs_1_ = bf16[2,64,256]{2,1,0:T(8,128)(2,1)S(1)} custom-call(s32[2,8]{1,0:T(2,128)S(1)} %copy-done.4, f32[4,128]{1,0:T(4,128)S(1)} %bitcast.2, bf16[128,256]{1,0:T(8,128)(2,1)S(1)} %get-tuple-element.23.refs_0_, bf16[128,256]{1,0:T(8,128)(2,1)S(1)} %collective-permute-done.refs_1_, bf16[128,256]{1,0:T(8,128)(2,1)S(1)} %collective-permute-done.1.refs_2_, ...), custom_call_target="tpu_custom_call" | custom-call | flops 20000000000 | tf_op jit(solution)/shard_map/codes/pallas_call | solution.py:238
  16.2 0.1 collective-permute-start.5
  16.3 1.6 %collective-permute-start.4 = (bf16[2,64,256]{2,1,0:T(8,128)(2,1)S(1)}, bf16[2,64,256]{2,1,0:T(8,128)(2,1)S(1)}, u32[]{:S(2)}, u32[]{:S(2)}) collective-permute-start(bf16[2,64,256]{2,1,0:T(8,128)(2,1)S(1)} %codes.1.refs_0_.refs_1_), channel_id=1, source_target_pairs={{0,2},{1,3},{2,0},{3,1},{4,6},{5,7},{6,4},{7,5},{8,10},{9,11},{10,... | collective-permute-start | bytes 196616 | tf_op jit(solution)/shard_map/ppermute | solution.py:253
  17.8 0.3 collective-permute-start.3
  18.1 0.0 collective-permute-start.6
  18.1 5.7 %collective-permute-done.7.got_ref = bf16[1,2,128,896]{3,2,1,0:T(8,128)(2,1)S(1)} collective-permute-done((bf16[1,2,128,896]{3,2,1,0:T(8,128)(2,1)S(1)}, bf16[1,2,128,896]{3,2,1,0:T(8,128)(2,1)S(1)}, u32[]{:S(2)}, u32[]{:S(2)}) %collective-permute-start.7) | collective-permute-done | bytes 458784 | tf_op jit(solution)/shard_map/ppermute | solution.py:277
  23.8 1.6 %collective-permute-start.8 = (bf16[1,2,128,896]{3,2,1,0:T(8,128)(2,1)S(1)}, bf16[1,2,128,896]{3,2,1,0:T(8,128)(2,1)S(1)}, u32[]{:S(2)}, u32[]{:S(2)}) collective-permute-start(bf16[1,2,128,896]{3,2,1,0:T(8,128)(2,1)S(1)} %collective-permute-done.7.got_ref), channel_id=1, source_target_pairs={{0,16},{16,0},{1,17},{17,1},{2,18},{18,2},{3,19},{19,3},{4,20},{20... | collective-permute-start | bytes 1376264 | tf_op jit(solution)/shard_map/ppermute | solution.py:278
  25.4 0.0 collective-permute-done.5.refs_3_
  25.5 0.0 collective-permute-done.4.refs_2_
  25.5 0.0 collective-permute-done.3.refs_1_
  25.5 0.1 gather.1.lhs_ref
  25.5 0.4 decode.3
  26.0 1.7 %collective-permute-start.12 = (bf16[1,64,896]{2,1,0:T(8,128)(2,1)S(1)}, bf16[1,64,896]{2,1,0:T(8,128)(2,1)S(1)}, u32[]{:S(2)}, u32[]{:S(2)}) collective-permute-start(bf16[1,64,896]{2,1,0:T(8,128)(2,1)S(1)} %get-tuple-element.35), channel_id=1, source_target_pairs={{0,8},{1,9},{4,12},{5,13},{8,0},{9,1},{12,4},{13,5},{2,10},{3,11},... | collective-permute-start | bytes 344072 | tf_op jit(solution)/shard_map/ppermute | solution.py:318
  27.7 0.0 collective-permute-start.13
  27.7 1.4 %collective-permute-start.14 = (bf16[1,64,896]{2,1,0:T(8,128)(2,1)S(1)}, bf16[1,64,896]{2,1,0:T(8,128)(2,1)S(1)}, u32[]{:S(2)}, u32[]{:S(2)}) collective-permute-start(bf16[1,64,896]{2,1,0:T(8,128)(2,1)S(1)} %get-tuple-element.37), channel_id=1, source_target_pairs={{0,1},{1,0},{4,5},{5,4},{8,9},{9,8},{12,13},{13,12},{2,3},{3,2},{6... | collective-permute-start | bytes 344072 | tf_op jit(solution)/shard_map/ppermute | solution.py:318
  29.1 4.6 %collective-permute-done.8.got_ref = bf16[1,2,128,896]{3,2,1,0:T(8,128)(2,1)S(1)} collective-permute-done((bf16[1,2,128,896]{3,2,1,0:T(8,128)(2,1)S(1)}, bf16[1,2,128,896]{3,2,1,0:T(8,128)(2,1)S(1)}, u32[]{:S(2)}, u32[]{:S(2)}) %collective-permute-start.8) | collective-permute-done | bytes 458784 | tf_op jit(solution)/shard_map/ppermute | solution.py:278
  33.7 0.4 decode.4
  34.2 0.0 copy-start.1
  34.2 0.0 copy-start.2
  34.2 1.3 %collective-permute-start.15 = (bf16[1,64,896]{2,1,0:T(8,128)(2,1)S(1)}, bf16[1,64,896]{2,1,0:T(8,128)(2,1)S(1)}, u32[]{:S(2)}, u32[]{:S(2)}) collective-permute-start(bf16[1,64,896]{2,1,0:T(8,128)(2,1)S(1)} %get-tuple-element.38), channel_id=1, source_target_pairs={{0,8},{1,9},{4,12},{5,13},{8,0},{9,1},{12,4},{13,5},{2,10},{3,11},... | collective-permute-start | bytes 344072 | tf_op jit(solution)/shard_map/ppermute | solution.py:318
  35.5 0.0 collective-permute-done.6.got_ref
  35.5 0.0 collective-permute-start.16
  35.5 1.8 %collective-permute-done.12.refs_0_ = bf16[1,64,896]{2,1,0:T(8,128)(2,1)S(1)} collective-permute-done((bf16[1,64,896]{2,1,0:T(8,128)(2,1)S(1)}, bf16[1,64,896]{2,1,0:T(8,128)(2,1)S(1)}, u32[]{:S(2)}, u32[]{:S(2)}) %collective-permute-start.12) | collective-permute-done | bytes 114720 | tf_op jit(solution)/shard_map/ppermute | solution.py:318
  37.3 0.0 collective-permute-start.17
  37.3 0.3 decode.5
  37.6 0.8 %collective-permute-done.13.refs_1_ = bf16[1,64,896]{2,1,0:T(8,128)(2,1)S(1)} collective-permute-done((bf16[1,64,896]{2,1,0:T(8,128)(2,1)S(1)}, bf16[1,64,896]{2,1,0:T(8,128)(2,1)S(1)}, u32[]{:S(2)}, u32[]{:S(2)}) %collective-permute-start.13) | collective-permute-done | bytes 114720 | tf_op jit(solution)/shard_map/ppermute | solution.py:318
  38.5 4.4 %collective-permute-start.9 = (bf16[2,64,128]{2,1,0:T(8,128)(2,1)S(1)}, bf16[2,64,128]{2,1,0:T(8,128)(2,1)S(1)}, u32[]{:S(2)}, u32[]{:S(2)}) collective-permute-start(bf16[2,64,128]{2,1,0:T(8,128)(2,1)S(1)} %get-tuple-element.31), channel_id=1, source_target_pairs={{0,8},{1,9},{4,12},{5,13},{8,0},{9,1},{12,4},{13,5},{2,10},{3,11},... | collective-permute-start | bytes 98312 | tf_op jit(solution)/shard_map/ppermute | solution.py:318
  42.9 0.0 collective-permute-done.14.refs_2_
  42.9 2.7 %collective-permute-start.10 = (bf16[2,64,128]{2,1,0:T(8,128)(2,1)S(1)}, bf16[2,64,128]{2,1,0:T(8,128)(2,1)S(1)}, u32[]{:S(2)}, u32[]{:S(2)}) collective-permute-start(bf16[2,64,128]{2,1,0:T(8,128)(2,1)S(1)} %get-tuple-element.32), channel_id=1, source_target_pairs={{0,9},{1,8},{4,13},{5,12},{8,1},{9,0},{12,5},{13,4},{2,11},{3,10},... | collective-permute-start | bytes 98312 | tf_op jit(solution)/shard_map/ppermute | solution.py:318
  45.6 0.4 collective-permute-done.15.refs_4_
  45.9 0.0 collective-permute-start.11
  45.9 1.1 %collective-permute-done.16.refs_5_ = bf16[1,64,896]{2,1,0:T(8,128)(2,1)S(1)} collective-permute-done((bf16[1,64,896]{2,1,0:T(8,128)(2,1)S(1)}, bf16[1,64,896]{2,1,0:T(8,128)(2,1)S(1)}, u32[]{:S(2)}, u32[]{:S(2)}) %collective-permute-start.16) | collective-permute-done | bytes 114720 | tf_op jit(solution)/shard_map/ppermute | solution.py:318
  47.1 0.0 collective-permute-done.17.refs_6_
  47.1 0.0 copy-done.1
  47.1 0.9 %add.2.refs_4_ = bf16[2,64,2048]{2,1,0:T(8,128)(2,1)} custom-call(f32[2,2048]{1,0:T(2,128)S(1)} %copy-done.2, bf16[2,64,2048]{2,1,0:T(8,128)(2,1)S(1)} %copy-done.1, bf16[1,64,896]{2,1,0:T(8,128)(2,1)S(1)} %collective-permute-done.12.refs_0_, bf16[1,64,896]{2,1,0:T(8,128)(2,1)S(1)} %collective-permute-done.13.refs_1_, ...), custom_call_target="tpu_custom_call" | custom-call | flops 20000000000 | tf_op jit(solution)/shard_map/add/pallas_call | solution.py:285
  48.0 1.9 %collective-permute-done.9.refs_0_ = bf16[2,64,128]{2,1,0:T(8,128)(2,1)S(1)} collective-permute-done((bf16[2,64,128]{2,1,0:T(8,128)(2,1)S(1)}, bf16[2,64,128]{2,1,0:T(8,128)(2,1)S(1)}, u32[]{:S(2)}, u32[]{:S(2)}) %collective-permute-start.9) | collective-permute-done | bytes 32800 | tf_op jit(solution)/shard_map/ppermute | solution.py:318
  49.8 0.0 collective-permute-done.10.refs_1_
  49.8 0.0 collective-permute-done.11.refs_2_
  49.8 0.7 %add.3 = bf16[2,64,2048]{2,1,0:T(8,128)(2,1)} custom-call(f32[2,2048]{1,0:T(2,128)S(1)} %copy-done.2, bf16[2,64,2048]{2,1,0:T(8,128)(2,1)S(1)} %copy-done.1, bf16[2,64,128]{2,1,0:T(8,128)(2,1)S(1)} %collective-permute-done.9.refs_0_, bf16[2,64,128]{2,1,0:T(8,128)(2,1)S(1)} %collective-permute-done.10.refs_1_, ...), custom_call_target="tpu_custom_call", output_to_operand_aliasing={{}: (6, {})} | custom-call | tf_op jit(solution)/shard_map/add/pallas_call | solution.py:285
  (7 shorter events, 0.0 us)
Async XLA Ops:
  0.0 15.5 %copy-start.4 = (s32[2,8]{1,0:T(2,128)S(1)}, s32[2,8]{1,0:T(2,128)}, u32[]{:S(2)}) copy-start(s32[2,8]{1,0:T(2,128)} %active_ref.1) | copy-start | bytes 196
  0.0 15.5 %copy-start.3 = (f32[512]{0:T(512)S(1)}, f32[512]{0:T(512)}, u32[]{:S(2)}) copy-start(f32[512]{0:T(512)} %param.9) | copy-start | bytes 6148
  3.0 6.6 %collective-permute-start = (bf16[128,256]{1,0:T(8,128)(2,1)S(1)}, bf16[128,256]{1,0:T(8,128)(2,1)S(1)}, u32[]{:S(2)}, u32[]{:S(2)}) collective-permute-start(bf16[128,256]{1,0:T(8,128)(2,1)S(1)} %get-tuple-element.24), channel_id=1, source_target_pairs={{0,4},{4,0},{8,12},{12,8},{1,5},{5,1},{9,13},{13,9},{2,6},{6,2},{1... | collective-permute-start | bytes 196616 | tf_op jit(solution)/shard_map/ppermute | solution.py:237
  6.1 7.3 %collective-permute-start.1 = (bf16[128,256]{1,0:T(8,128)(2,1)S(1)}, bf16[128,256]{1,0:T(8,128)(2,1)S(1)}, u32[]{:S(2)}, u32[]{:S(2)}) collective-permute-start(bf16[128,256]{1,0:T(8,128)(2,1)S(1)} %get-tuple-element.25), channel_id=1, source_target_pairs={{0,8},{4,12},{8,0},{12,4},{1,9},{5,13},{9,1},{13,5},{2,10},{6,14},... | collective-permute-start | bytes 196616 | tf_op jit(solution)/shard_map/ppermute | solution.py:237
  8.7 6.8 %collective-permute-start.2 = (bf16[128,256]{1,0:T(8,128)(2,1)S(1)}, bf16[128,256]{1,0:T(8,128)(2,1)S(1)}, u32[]{:S(2)}, u32[]{:S(2)}) collective-permute-start(bf16[128,256]{1,0:T(8,128)(2,1)S(1)} %get-tuple-element.26), channel_id=1, source_target_pairs={{0,12},{4,8},{8,4},{12,0},{1,13},{5,9},{9,5},{13,1},{2,14},{6,10},... | collective-permute-start | bytes 196616 | tf_op jit(solution)/shard_map/ppermute | solution.py:237
  8.7 15.1 %collective-permute-start.7 = (bf16[1,2,128,896]{3,2,1,0:T(8,128)(2,1)S(1)}, bf16[1,2,128,896]{3,2,1,0:T(8,128)(2,1)S(1)}, u32[]{:S(2)}, u32[]{:S(2)}) collective-permute-start(bf16[1,2,128,896]{3,2,1,0:T(8,128)(2,1)S(1)} %get-tuple-element.28), channel_id=1, source_target_pairs={{0,4},{4,0},{8,12},{12,8},{1,5},{5,1},{9,13},{13,9},{2,6},{6,2},{1... | collective-permute-start | bytes 1376264 | tf_op jit(solution)/shard_map/ppermute | solution.py:277
  16.2 9.3 %collective-permute-start.5 = (bf16[2,64,256]{2,1,0:T(8,128)(2,1)S(1)}, bf16[2,64,256]{2,1,0:T(8,128)(2,1)S(1)}, u32[]{:S(2)}, u32[]{:S(2)}) collective-permute-start(bf16[2,64,256]{2,1,0:T(8,128)(2,1)S(1)} %codes.1.refs_0_.refs_1_), channel_id=1, source_target_pairs={{0,3},{1,2},{2,1},{3,0},{4,7},{5,6},{6,5},{7,4},{8,11},{9,10},{10,... | collective-permute-start | bytes 196616 | tf_op jit(solution)/shard_map/ppermute | solution.py:253
  16.3 9.2 %collective-permute-start.4 = (bf16[2,64,256]{2,1,0:T(8,128)(2,1)S(1)}, bf16[2,64,256]{2,1,0:T(8,128)(2,1)S(1)}, u32[]{:S(2)}, u32[]{:S(2)}) collective-permute-start(bf16[2,64,256]{2,1,0:T(8,128)(2,1)S(1)} %codes.1.refs_0_.refs_1_), channel_id=1, source_target_pairs={{0,2},{1,3},{2,0},{3,1},{4,6},{5,7},{6,4},{7,5},{8,10},{9,11},{10,... | collective-permute-start | bytes 196616 | tf_op jit(solution)/shard_map/ppermute | solution.py:253
  17.8 7.6 %collective-permute-start.3 = (bf16[2,64,256]{2,1,0:T(8,128)(2,1)S(1)}, bf16[2,64,256]{2,1,0:T(8,128)(2,1)S(1)}, u32[]{:S(2)}, u32[]{:S(2)}) collective-permute-start(bf16[2,64,256]{2,1,0:T(8,128)(2,1)S(1)} %codes.1.refs_0_.refs_1_), channel_id=1, source_target_pairs={{0,1},{1,0},{2,3},{3,2},{4,5},{5,4},{6,7},{7,6},{8,9},{9,8},{10,11... | collective-permute-start | bytes 196616 | tf_op jit(solution)/shard_map/ppermute | solution.py:253
  18.1 7.4 %copy-start = (bf16[2,2,128,2048]{3,2,1,0:T(8,128)(2,1)S(1)}, bf16[2,2,128,2048]{3,2,1,0:T(8,128)(2,1)}, u32[]{:S(2)}) copy-start(bf16[2,2,128,2048]{3,2,1,0:T(8,128)(2,1)} %dec_ref.5) | copy-start | bytes 6291460
  18.1 17.4 %collective-permute-start.6 = (bf16[2,2,128,128]{3,2,1,0:T(8,128)(2,1)S(1)}, bf16[2,2,128,128]{3,2,1,0:T(8,128)(2,1)S(1)}, u32[]{:S(2)}, u32[]{:S(2)}) collective-permute-start(bf16[2,2,128,128]{3,2,1,0:T(8,128)(2,1)S(1)} %hold.1), channel_id=1, source_target_pairs={{0,4},{4,0},{8,12},{12,8},{1,5},{5,1},{9,13},{13,9},{2,6},{6,2},{1... | collective-permute-start | bytes 393224 | tf_op jit(solution)/shard_map/ppermute | solution.py:279
  23.8 9.9 %collective-permute-start.8 = (bf16[1,2,128,896]{3,2,1,0:T(8,128)(2,1)S(1)}, bf16[1,2,128,896]{3,2,1,0:T(8,128)(2,1)S(1)}, u32[]{:S(2)}, u32[]{:S(2)}) collective-permute-start(bf16[1,2,128,896]{3,2,1,0:T(8,128)(2,1)S(1)} %collective-permute-done.7.got_ref), channel_id=1, source_target_pairs={{0,16},{16,0},{1,17},{17,1},{2,18},{18,2},{3,19},{19,3},{4,20},{20... | collective-permute-start | bytes 1376264 | tf_op jit(solution)/shard_map/ppermute | solution.py:278
  26.0 11.3 %collective-permute-start.12 = (bf16[1,64,896]{2,1,0:T(8,128)(2,1)S(1)}, bf16[1,64,896]{2,1,0:T(8,128)(2,1)S(1)}, u32[]{:S(2)}, u32[]{:S(2)}) collective-permute-start(bf16[1,64,896]{2,1,0:T(8,128)(2,1)S(1)} %get-tuple-element.35), channel_id=1, source_target_pairs={{0,8},{1,9},{4,12},{5,13},{8,0},{9,1},{12,4},{13,5},{2,10},{3,11},... | collective-permute-start | bytes 344072 | tf_op jit(solution)/shard_map/ppermute | solution.py:318
  27.7 10.7 %collective-permute-start.13 = (bf16[1,64,896]{2,1,0:T(8,128)(2,1)S(1)}, bf16[1,64,896]{2,1,0:T(8,128)(2,1)S(1)}, u32[]{:S(2)}, u32[]{:S(2)}) collective-permute-start(bf16[1,64,896]{2,1,0:T(8,128)(2,1)S(1)} %get-tuple-element.36), channel_id=1, source_target_pairs={{0,9},{1,8},{4,13},{5,12},{8,1},{9,0},{12,5},{13,4},{2,11},{3,10},... | collective-permute-start | bytes 344072 | tf_op jit(solution)/shard_map/ppermute | solution.py:318
  27.7 15.2 %collective-permute-start.14 = (bf16[1,64,896]{2,1,0:T(8,128)(2,1)S(1)}, bf16[1,64,896]{2,1,0:T(8,128)(2,1)S(1)}, u32[]{:S(2)}, u32[]{:S(2)}) collective-permute-start(bf16[1,64,896]{2,1,0:T(8,128)(2,1)S(1)} %get-tuple-element.37), channel_id=1, source_target_pairs={{0,1},{1,0},{4,5},{5,4},{8,9},{9,8},{12,13},{13,12},{2,3},{3,2},{6... | collective-permute-start | bytes 344072 | tf_op jit(solution)/shard_map/ppermute | solution.py:318
  34.2 12.9 %copy-start.1 = (bf16[2,64,2048]{2,1,0:T(8,128)(2,1)S(1)}, bf16[2,64,2048]{2,1,0:T(8,128)(2,1)}, u32[]{:S(2)}) copy-start(bf16[2,64,2048]{2,1,0:T(8,128)(2,1)} %target_ref.3) | copy-start | bytes 1572868
  34.2 12.9 %copy-start.2 = (f32[2,2048]{1,0:T(2,128)S(1)}, f32[2,2048]{1,0:T(2,128)}, u32[]{:S(2)}) copy-start(f32[2,2048]{1,0:T(2,128)} %bias_ref.3) | copy-start | bytes 49156
  34.2 11.7 %collective-permute-start.15 = (bf16[1,64,896]{2,1,0:T(8,128)(2,1)S(1)}, bf16[1,64,896]{2,1,0:T(8,128)(2,1)S(1)}, u32[]{:S(2)}, u32[]{:S(2)}) collective-permute-start(bf16[1,64,896]{2,1,0:T(8,128)(2,1)S(1)} %get-tuple-element.38), channel_id=1, source_target_pairs={{0,8},{1,9},{4,12},{5,13},{8,0},{9,1},{12,4},{13,5},{2,10},{3,11},... | collective-permute-start | bytes 344072 | tf_op jit(solution)/shard_map/ppermute | solution.py:318
  35.5 11.6 %collective-permute-start.16 = (bf16[1,64,896]{2,1,0:T(8,128)(2,1)S(1)}, bf16[1,64,896]{2,1,0:T(8,128)(2,1)S(1)}, u32[]{:S(2)}, u32[]{:S(2)}) collective-permute-start(bf16[1,64,896]{2,1,0:T(8,128)(2,1)S(1)} %get-tuple-element.39), channel_id=1, source_target_pairs={{0,9},{1,8},{4,13},{5,12},{8,1},{9,0},{12,5},{13,4},{2,11},{3,10},... | collective-permute-start | bytes 344072 | tf_op jit(solution)/shard_map/ppermute | solution.py:318
  37.3 9.7 %collective-permute-start.17 = (bf16[1,64,896]{2,1,0:T(8,128)(2,1)S(1)}, bf16[1,64,896]{2,1,0:T(8,128)(2,1)S(1)}, u32[]{:S(2)}, u32[]{:S(2)}) collective-permute-start(bf16[1,64,896]{2,1,0:T(8,128)(2,1)S(1)} %get-tuple-element.40), channel_id=1, source_target_pairs={{0,1},{1,0},{4,5},{5,4},{8,9},{9,8},{12,13},{13,12},{2,3},{3,2},{6... | collective-permute-start | bytes 344072 | tf_op jit(solution)/shard_map/ppermute | solution.py:318
  38.5 11.4 %collective-permute-start.9 = (bf16[2,64,128]{2,1,0:T(8,128)(2,1)S(1)}, bf16[2,64,128]{2,1,0:T(8,128)(2,1)S(1)}, u32[]{:S(2)}, u32[]{:S(2)}) collective-permute-start(bf16[2,64,128]{2,1,0:T(8,128)(2,1)S(1)} %get-tuple-element.31), channel_id=1, source_target_pairs={{0,8},{1,9},{4,12},{5,13},{8,0},{9,1},{12,4},{13,5},{2,10},{3,11},... | collective-permute-start | bytes 98312 | tf_op jit(solution)/shard_map/ppermute | solution.py:318
  42.9 7.0 %collective-permute-start.10 = (bf16[2,64,128]{2,1,0:T(8,128)(2,1)S(1)}, bf16[2,64,128]{2,1,0:T(8,128)(2,1)S(1)}, u32[]{:S(2)}, u32[]{:S(2)}) collective-permute-start(bf16[2,64,128]{2,1,0:T(8,128)(2,1)S(1)} %get-tuple-element.32), channel_id=1, source_target_pairs={{0,9},{1,8},{4,13},{5,12},{8,1},{9,0},{12,5},{13,4},{2,11},{3,10},... | collective-permute-start | bytes 98312 | tf_op jit(solution)/shard_map/ppermute | solution.py:318
  45.9 3.9 %collective-permute-start.11 = (bf16[2,64,128]{2,1,0:T(8,128)(2,1)S(1)}, bf16[2,64,128]{2,1,0:T(8,128)(2,1)S(1)}, u32[]{:S(2)}, u32[]{:S(2)}) collective-permute-start(bf16[2,64,128]{2,1,0:T(8,128)(2,1)S(1)} %get-tuple-element.33), channel_id=1, source_target_pairs={{0,1},{1,0},{4,5},{5,4},{8,9},{9,8},{12,13},{13,12},{2,3},{3,2},{6... | collective-permute-start | bytes 98312 | tf_op jit(solution)/shard_map/ppermute | solution.py:318

commit v21 on v16

--- a/solution.py
+++ b/solution.py
@@ -9,7 +9,7 @@
 
 VMEM_BYTES = 32 * 1024 * 1024
 LANES = 128
-FIRST = 5
+FIRST = 6
 PIECES = (((0,), 0, False), ((1,), 0, True), ((0, 1), 1, False))
 
 
@@ -240,7 +240,7 @@
     terms, parts = list(results[:n]), list(results[n:])
     for k in range(1, n):
         terms[k] = lax.ppermute(terms[k], "src", [(i, peer(i, k, n)) for i in range(n)])
-    order = [0, half, *(k for k in range(1, n) if k != half)]
+    order = range(n)
     own = pl.pallas_call(
         functools.partial(codes_kernel, n, share, tile_rows),
         out_shape=shape(half, share, 2 * block),

time: 50.2 us -> 48.1 us (0.958)
  the two profiles are of different devices: /device:TPU:0 before, /device:TPU:9 now
where the time goes in v21:
time: 48.1 us; the launch traced here: 47.9 us
  starting transfers between devices  30.7 us (64%)
  waiting for transfers between devices  9.76 us (20%)
  Pallas kernels  7.25 us (15%)
    ppermute x9, starting transfers between devices, body(): sums[i].append(lax.ppermute(terms[2 * j + r], ('src', 'rep'), perm))  19.9 us
    ppermute x3, waiting for transfers between devices, body(): lax.ppermute(terms[k], 'src', [(i, peer(i, k, n)) for i in range(n)])  3.95 us
    ppermute x9, waiting for transfers between devices, body(): sums[i].append(lax.ppermute(terms[2 * j + r], ('src', 'rep'), perm))  3.3 us
    ppermute x3, starting transfers between devices, body(): codes.append(lax.ppermute(own, ('tgt', 'rep'), perm) if k + r else own)  3.12 us
    pallas_call x1, Pallas kernels, body(): pl.pallas_call(functools.partial(encode_kernel, n, fetched[:1]), out_shap...  2.97 us
    ppermute x3, starting transfers between devices, body(): lax.ppermute(terms[k], 'src', [(i, peer(i, k, n)) for i in range(n)])  2.71 us
    ppermute x1, starting transfers between devices, body(): got.append(lax.ppermute(part, 'src', pair))  2.69 us
    ppermute x1, waiting for transfers between devices, body(): got.append(lax.ppermute(got[0], 'parts', [(0, 1), (1, 0)]))  2.51 us
  transfers between devices with their start and end apart: 18, of which 5 were waited for; matrix products, arithmetic and copies ran while one was open for 0% of the time, Pallas kernels for 7%

profile of v21, /device:TPU:9, one launch (start us, length us, event | category | flops | bytes accessed | tf_op | source)
XLA Modules:
  0.0 47.9 jit_solution(1031030364037281054)
XLA Ops:
  0.0 3.0 %encode.1 = (bf16[128,256]{1,0:T(8,128)(2,1)S(1)}, bf16[128,256]{1,0:T(8,128)(2,1)S(1)}, bf16[128,256]{1,0:T(8,128)(2,1)S(1)}, bf16[128,256]{1,0:T(8,128)(2,1)S(1)}, bf16[1,2,128,768]{3,2,1,0:T(8,128)(2,1)S(1)}) custom-call(bf16[2,2,64,1024]{3,2,1,0:T(8,128)(2,1)} %bitcast.3, bf16[1024,512]{1,0:T(8,128)(2,1)} %w_hbm.1, bf16[2,2,128,2048]{3,2,1,0:T(8,128)(2,1)} %dec_ref.5), custom_call_target="tpu_custom_call" | custom-call | tf_op jit(solution)/shard_map/encode/pallas_call | solution.py:223
  3.0 0.1 collective-permute-start
  3.1 2.5 %collective-permute-start.1 = (bf16[128,256]{1,0:T(8,128)(2,1)S(1)}, bf16[128,256]{1,0:T(8,128)(2,1)S(1)}, u32[]{:S(2)}, u32[]{:S(2)}) collective-permute-start(bf16[128,256]{1,0:T(8,128)(2,1)S(1)} %get-tuple-element.24), channel_id=1, source_target_pairs={{0,8},{4,12},{8,0},{12,4},{1,9},{5,13},{9,1},{13,5},{2,10},{6,14},... | collective-permute-start | bytes 196616 | tf_op jit(solution)/shard_map/ppermute | solution.py:242
  5.5 0.2 collective-permute-start.2
  5.7 1.1 %collective-permute-start.7 = (bf16[1,2,128,768]{3,2,1,0:T(8,128)(2,1)S(1)}, bf16[1,2,128,768]{3,2,1,0:T(8,128)(2,1)S(1)}, u32[]{:S(2)}, u32[]{:S(2)}) collective-permute-start(bf16[1,2,128,768]{3,2,1,0:T(8,128)(2,1)S(1)} %get-tuple-element.26.before_ref), channel_id=1, source_target_pairs={{0,4},{4,0},{8,12},{12,8},{1,5},{5,1},{9,13},{13,9},{2,6},{6,2},{1... | collective-permute-start | bytes 1179656 | tf_op jit(solution)/shard_map/ppermute | solution.py:282
  6.8 0.0 collective-permute-done.refs_1_
  6.8 1.3 %collective-permute-done.1.refs_2_ = bf16[128,256]{1,0:T(8,128)(2,1)S(1)} collective-permute-done((bf16[128,256]{1,0:T(8,128)(2,1)S(1)}, bf16[128,256]{1,0:T(8,128)(2,1)S(1)}, u32[]{:S(2)}, u32[]{:S(2)}) %collective-permute-start.1) | collective-permute-done | bytes 65568 | tf_op jit(solution)/shard_map/ppermute | solution.py:242
  8.1 2.6 %collective-permute-done.2.refs_3_ = bf16[128,256]{1,0:T(8,128)(2,1)S(1)} collective-permute-done((bf16[128,256]{1,0:T(8,128)(2,1)S(1)}, bf16[128,256]{1,0:T(8,128)(2,1)S(1)}, u32[]{:S(2)}, u32[]{:S(2)}) %collective-permute-start.2) | collective-permute-done | bytes 65568 | tf_op jit(solution)/shard_map/ppermute | solution.py:242
  10.8 0.6 %codes.1.refs_0_.after_ref = bf16[2,64,256]{2,1,0:T(8,128)(2,1)S(1)} custom-call(s32[2,8]{1,0:T(2,128)S(1)} %copy-done.4, f32[4,128]{1,0:T(4,128)S(1)} %bitcast.2, bf16[128,256]{1,0:T(8,128)(2,1)S(1)} %get-tuple-element.22.refs_0_, bf16[128,256]{1,0:T(8,128)(2,1)S(1)} %collective-permute-done.refs_1_, bf16[128,256]{1,0:T(8,128)(2,1)S(1)} %collective-permute-done.1.refs_2_, ...), custom_call_target="tpu_custom_call" | custom-call | flops 20000000000 | tf_op jit(solution)/shard_map/codes/pallas_call | solution.py:244
  11.4 2.6 %collective-permute-start.5 = (bf16[2,64,256]{2,1,0:T(8,128)(2,1)S(1)}, bf16[2,64,256]{2,1,0:T(8,128)(2,1)S(1)}, u32[]{:S(2)}, u32[]{:S(2)}) collective-permute-start(bf16[2,64,256]{2,1,0:T(8,128)(2,1)S(1)} %codes.1.refs_0_.after_ref), channel_id=1, source_target_pairs={{0,3},{1,2},{2,1},{3,0},{4,7},{5,6},{6,5},{7,4},{8,11},{9,10},{10,... | collective-permute-start | bytes 196616 | tf_op jit(solution)/shard_map/ppermute | solution.py:259
  14.0 0.3 collective-permute-start.4
  14.3 0.2 collective-permute-start.3
  14.5 1.0 %part.1 = bf16[2,2,128,256]{3,2,1,0:T(8,128)(2,1)S(1)} custom-call(bf16[1,2,128,768]{3,2,1,0:T(8,128)(2,1)S(1)} %get-tuple-element.26.before_ref, bf16[2,2,128,2048]{3,2,1,0:T(8,128)(2,1)} %dec_ref.5, bf16[2,64,256]{2,1,0:T(8,128)(2,1)S(1)} %codes.1.refs_0_.after_ref), custom_call_target="tpu_custom_call" | custom-call | tf_op jit(solution)/shard_map/part/pallas_call | solution.py:271
  15.5 0.0 copy-start
  15.5 2.7 %collective-permute-start.6 = (bf16[2,2,128,256]{3,2,1,0:T(8,128)(2,1)S(1)}, bf16[2,2,128,256]{3,2,1,0:T(8,128)(2,1)S(1)}, u32[]{:S(2)}, u32[]{:S(2)}) collective-permute-start(bf16[2,2,128,256]{3,2,1,0:T(8,128)(2,1)S(1)} %part.1), channel_id=1, source_target_pairs={{0,4},{4,0},{8,12},{12,8},{1,5},{5,1},{9,13},{13,9},{2,6},{6,2},{1... | collective-permute-start | bytes 786440 | tf_op jit(solution)/shard_map/ppermute | solution.py:284
  18.2 0.0 collective-permute-done.7.got_ref
  18.2 1.2 %collective-permute-start.8 = (bf16[1,2,128,768]{3,2,1,0:T(8,128)(2,1)S(1)}, bf16[1,2,128,768]{3,2,1,0:T(8,128)(2,1)S(1)}, u32[]{:S(2)}, u32[]{:S(2)}) collective-permute-start(bf16[1,2,128,768]{3,2,1,0:T(8,128)(2,1)S(1)} %collective-permute-done.7.got_ref), channel_id=1, source_target_pairs={{0,16},{16,0},{1,17},{17,1},{2,18},{18,2},{3,19},{19,3},{4,20},{20... | collective-permute-start | bytes 1179656 | tf_op jit(solution)/shard_map/ppermute | solution.py:283
  19.4 0.0 collective-permute-done.5.refs_3_
  19.4 0.0 collective-permute-done.4.refs_2_
  19.4 0.0 collective-permute-done.3.refs_1_
  19.5 0.1 gather.1.lhs_ref
  19.5 0.4 decode.3
  19.9 2.2 %collective-permute-start.12 = (bf16[1,64,768]{2,1,0:T(8,128)(2,1)S(1)}, bf16[1,64,768]{2,1,0:T(8,128)(2,1)S(1)}, u32[]{:S(2)}, u32[]{:S(2)}) collective-permute-start(bf16[1,64,768]{2,1,0:T(8,128)(2,1)S(1)} %get-tuple-element.33), channel_id=1, source_target_pairs={{0,8},{1,9},{4,12},{5,13},{8,0},{9,1},{12,4},{13,5},{2,10},{3,11},... | collective-permute-start | bytes 294920 | tf_op jit(solution)/shard_map/ppermute | solution.py:323
  22.1 2.3 %collective-permute-start.13 = (bf16[1,64,768]{2,1,0:T(8,128)(2,1)S(1)}, bf16[1,64,768]{2,1,0:T(8,128)(2,1)S(1)}, u32[]{:S(2)}, u32[]{:S(2)}) collective-permute-start(bf16[1,64,768]{2,1,0:T(8,128)(2,1)S(1)} %get-tuple-element.34), channel_id=1, source_target_pairs={{0,9},{1,8},{4,13},{5,12},{8,1},{9,0},{12,5},{13,4},{2,11},{3,10},... | collective-permute-start | bytes 294920 | tf_op jit(solution)/shard_map/ppermute | solution.py:323
  24.5 0.3 collective-permute-start.14
  24.8 2.5 %collective-permute-done.8.got_ref = bf16[1,2,128,768]{3,2,1,0:T(8,128)(2,1)S(1)} collective-permute-done((bf16[1,2,128,768]{3,2,1,0:T(8,128)(2,1)S(1)}, bf16[1,2,128,768]{3,2,1,0:T(8,128)(2,1)S(1)}, u32[]{:S(2)}, u32[]{:S(2)}) %collective-permute-start.8) | collective-permute-done | bytes 393248 | tf_op jit(solution)/shard_map/ppermute | solution.py:283
  27.3 0.4 decode.4
  27.7 0.0 copy-start.1
  27.7 0.0 copy-start.2
  27.7 1.7 %collective-permute-start.15 = (bf16[1,64,768]{2,1,0:T(8,128)(2,1)S(1)}, bf16[1,64,768]{2,1,0:T(8,128)(2,1)S(1)}, u32[]{:S(2)}, u32[]{:S(2)}) collective-permute-start(bf16[1,64,768]{2,1,0:T(8,128)(2,1)S(1)} %get-tuple-element.36), channel_id=1, source_target_pairs={{0,8},{1,9},{4,12},{5,13},{8,0},{9,1},{12,4},{13,5},{2,10},{3,11},... | collective-permute-start | bytes 294920 | tf_op jit(solution)/shard_map/ppermute | solution.py:323
  29.4 0.0 collective-permute-done.6.got_ref
  29.4 3.4 %collective-permute-start.16 = (bf16[1,64,768]{2,1,0:T(8,128)(2,1)S(1)}, bf16[1,64,768]{2,1,0:T(8,128)(2,1)S(1)}, u32[]{:S(2)}, u32[]{:S(2)}) collective-permute-start(bf16[1,64,768]{2,1,0:T(8,128)(2,1)S(1)} %get-tuple-element.37), channel_id=1, source_target_pairs={{0,9},{1,8},{4,13},{5,12},{8,1},{9,0},{12,5},{13,4},{2,11},{3,10},... | collective-permute-start | bytes 294920 | tf_op jit(solution)/shard_map/ppermute | solution.py:323
  32.7 0.0 collective-permute-done.12.refs_0_
  32.7 0.0 collective-permute-start.17
  32.7 0.3 decode.5
  33.1 0.0 collective-permute-done.13.refs_1_
  33.1 9.5 %collective-permute-start.9 = (bf16[2,64,256]{2,1,0:T(8,128)(2,1)S(1)}, bf16[2,64,256]{2,1,0:T(8,128)(2,1)S(1)}, u32[]{:S(2)}, u32[]{:S(2)}) collective-permute-start(bf16[2,64,256]{2,1,0:T(8,128)(2,1)S(1)} %get-tuple-element.29), channel_id=1, source_target_pairs={{0,8},{1,9},{4,12},{5,13},{8,0},{9,1},{12,4},{13,5},{2,10},{3,11},... | collective-permute-start | bytes 196616 | tf_op jit(solution)/shard_map/ppermute | solution.py:323
  42.6 0.0 collective-permute-done.14.refs_2_
  42.6 0.0 collective-permute-start.10
  42.6 0.0 collective-permute-done.15.refs_4_
  42.6 0.4 collective-permute-start.11
  43.0 0.0 collective-permute-done.16.refs_5_
  43.0 0.0 collective-permute-done.17.refs_6_
  43.1 0.9 %add.2.refs_4_ = bf16[2,64,2048]{2,1,0:T(8,128)(2,1)} custom-call(f32[2,2048]{1,0:T(2,128)S(1)} %copy-done.2, bf16[2,64,2048]{2,1,0:T(8,128)(2,1)S(1)} %copy-done.1, bf16[1,64,768]{2,1,0:T(8,128)(2,1)S(1)} %collective-permute-done.12.refs_0_, bf16[1,64,768]{2,1,0:T(8,128)(2,1)S(1)} %collective-permute-done.13.refs_1_, ...), custom_call_target="tpu_custom_call" | custom-call | flops 20000000000 | tf_op jit(solution)/shard_map/add/pallas_call | solution.py:290
  43.9 1.3 %collective-permute-done.9.refs_0_ = bf16[2,64,256]{2,1,0:T(8,128)(2,1)S(1)} collective-permute-done((bf16[2,64,256]{2,1,0:T(8,128)(2,1)S(1)}, bf16[2,64,256]{2,1,0:T(8,128)(2,1)S(1)}, u32[]{:S(2)}, u32[]{:S(2)}) %collective-permute-start.9) | collective-permute-done | bytes 65568 | tf_op jit(solution)/shard_map/ppermute | solution.py:323
  45.2 2.0 %collective-permute-done.10.refs_1_ = bf16[2,64,256]{2,1,0:T(8,128)(2,1)S(1)} collective-permute-done((bf16[2,64,256]{2,1,0:T(8,128)(2,1)S(1)}, bf16[2,64,256]{2,1,0:T(8,128)(2,1)S(1)}, u32[]{:S(2)}, u32[]{:S(2)}) %collective-permute-start.10) | collective-permute-done | bytes 65568 | tf_op jit(solution)/shard_map/ppermute | solution.py:323
  47.2 0.0 collective-permute-done.11.refs_2_
  47.2 0.7 %add.3 = bf16[2,64,2048]{2,1,0:T(8,128)(2,1)} custom-call(f32[2,2048]{1,0:T(2,128)S(1)} %copy-done.2, bf16[2,64,2048]{2,1,0:T(8,128)(2,1)S(1)} %copy-done.1, bf16[2,64,256]{2,1,0:T(8,128)(2,1)S(1)} %collective-permute-done.9.refs_0_, bf16[2,64,256]{2,1,0:T(8,128)(2,1)S(1)} %collective-permute-done.10.refs_1_, ...), custom_call_target="tpu_custom_call", output_to_operand_aliasing={{}: (6, {})} | custom-call | tf_op jit(solution)/shard_map/add/pallas_call | solution.py:290
  (7 shorter events, 0.0 us)
Async XLA Ops:
  0.0 10.8 %copy-start.4 = (s32[2,8]{1,0:T(2,128)S(1)}, s32[2,8]{1,0:T(2,128)}, u32[]{:S(2)}) copy-start(s32[2,8]{1,0:T(2,128)} %active_ref.1) | copy-start | bytes 196
  0.0 10.8 %copy-start.3 = (f32[512]{0:T(512)S(1)}, f32[512]{0:T(512)}, u32[]{:S(2)}) copy-start(f32[512]{0:T(512)} %param.9) | copy-start | bytes 6148
  3.0 3.8 %collective-permute-start = (bf16[128,256]{1,0:T(8,128)(2,1)S(1)}, bf16[128,256]{1,0:T(8,128)(2,1)S(1)}, u32[]{:S(2)}, u32[]{:S(2)}) collective-permute-start(bf16[128,256]{1,0:T(8,128)(2,1)S(1)} %get-tuple-element.23), channel_id=1, source_target_pairs={{0,4},{4,0},{8,12},{12,8},{1,5},{5,1},{9,13},{13,9},{2,6},{6,2},{1... | collective-permute-start | bytes 196616 | tf_op jit(solution)/shard_map/ppermute | solution.py:242
  3.1 5.1 %collective-permute-start.1 = (bf16[128,256]{1,0:T(8,128)(2,1)S(1)}, bf16[128,256]{1,0:T(8,128)(2,1)S(1)}, u32[]{:S(2)}, u32[]{:S(2)}) collective-permute-start(bf16[128,256]{1,0:T(8,128)(2,1)S(1)} %get-tuple-element.24), channel_id=1, source_target_pairs={{0,8},{4,12},{8,0},{12,4},{1,9},{5,13},{9,1},{13,5},{2,10},{6,14},... | collective-permute-start | bytes 196616 | tf_op jit(solution)/shard_map/ppermute | solution.py:242
  5.5 5.2 %collective-permute-start.2 = (bf16[128,256]{1,0:T(8,128)(2,1)S(1)}, bf16[128,256]{1,0:T(8,128)(2,1)S(1)}, u32[]{:S(2)}, u32[]{:S(2)}) collective-permute-start(bf16[128,256]{1,0:T(8,128)(2,1)S(1)} %get-tuple-element.25), channel_id=1, source_target_pairs={{0,12},{4,8},{8,4},{12,0},{1,13},{5,9},{9,5},{13,1},{2,14},{6,10},... | collective-permute-start | bytes 196616 | tf_op jit(solution)/shard_map/ppermute | solution.py:242
  5.7 12.5 %collective-permute-start.7 = (bf16[1,2,128,768]{3,2,1,0:T(8,128)(2,1)S(1)}, bf16[1,2,128,768]{3,2,1,0:T(8,128)(2,1)S(1)}, u32[]{:S(2)}, u32[]{:S(2)}) collective-permute-start(bf16[1,2,128,768]{3,2,1,0:T(8,128)(2,1)S(1)} %get-tuple-element.26.before_ref), channel_id=1, source_target_pairs={{0,4},{4,0},{8,12},{12,8},{1,5},{5,1},{9,13},{13,9},{2,6},{6,2},{1... | collective-permute-start | bytes 1179656 | tf_op jit(solution)/shard_map/ppermute | solution.py:282
  11.4 8.0 %collective-permute-start.5 = (bf16[2,64,256]{2,1,0:T(8,128)(2,1)S(1)}, bf16[2,64,256]{2,1,0:T(8,128)(2,1)S(1)}, u32[]{:S(2)}, u32[]{:S(2)}) collective-permute-start(bf16[2,64,256]{2,1,0:T(8,128)(2,1)S(1)} %codes.1.refs_0_.after_ref), channel_id=1, source_target_pairs={{0,3},{1,2},{2,1},{3,0},{4,7},{5,6},{6,5},{7,4},{8,11},{9,10},{10,... | collective-permute-start | bytes 196616 | tf_op jit(solution)/shard_map/ppermute | solution.py:259
  14.0 5.4 %collective-permute-start.4 = (bf16[2,64,256]{2,1,0:T(8,128)(2,1)S(1)}, bf16[2,64,256]{2,1,0:T(8,128)(2,1)S(1)}, u32[]{:S(2)}, u32[]{:S(2)}) collective-permute-start(bf16[2,64,256]{2,1,0:T(8,128)(2,1)S(1)} %codes.1.refs_0_.after_ref), channel_id=1, source_target_pairs={{0,2},{1,3},{2,0},{3,1},{4,6},{5,7},{6,4},{7,5},{8,10},{9,11},{10,... | collective-permute-start | bytes 196616 | tf_op jit(solution)/shard_map/ppermute | solution.py:259
  14.3 5.1 %collective-permute-start.3 = (bf16[2,64,256]{2,1,0:T(8,128)(2,1)S(1)}, bf16[2,64,256]{2,1,0:T(8,128)(2,1)S(1)}, u32[]{:S(2)}, u32[]{:S(2)}) collective-permute-start(bf16[2,64,256]{2,1,0:T(8,128)(2,1)S(1)} %codes.1.refs_0_.after_ref), channel_id=1, source_target_pairs={{0,1},{1,0},{2,3},{3,2},{4,5},{5,4},{6,7},{7,6},{8,9},{9,8},{10,11... | collective-permute-start | bytes 196616 | tf_op jit(solution)/shard_map/ppermute | solution.py:259
  15.5 4.0 %copy-start = (bf16[2,2,128,2048]{3,2,1,0:T(8,128)(2,1)S(1)}, bf16[2,2,128,2048]{3,2,1,0:T(8,128)(2,1)}, u32[]{:S(2)}) copy-start(bf16[2,2,128,2048]{3,2,1,0:T(8,128)(2,1)} %dec_ref.5) | copy-start | bytes 6291460
  15.5 13.8 %collective-permute-start.6 = (bf16[2,2,128,256]{3,2,1,0:T(8,128)(2,1)S(1)}, bf16[2,2,128,256]{3,2,1,0:T(8,128)(2,1)S(1)}, u32[]{:S(2)}, u32[]{:S(2)}) collective-permute-start(bf16[2,2,128,256]{3,2,1,0:T(8,128)(2,1)S(1)} %part.1), channel_id=1, source_target_pairs={{0,4},{4,0},{8,12},{12,8},{1,5},{5,1},{9,13},{13,9},{2,6},{6,2},{1... | collective-permute-start | bytes 786440 | tf_op jit(solution)/shard_map/ppermute | solution.py:284
  18.2 9.1 %collective-permute-start.8 = (bf16[1,2,128,768]{3,2,1,0:T(8,128)(2,1)S(1)}, bf16[1,2,128,768]{3,2,1,0:T(8,128)(2,1)S(1)}, u32[]{:S(2)}, u32[]{:S(2)}) collective-permute-start(bf16[1,2,128,768]{3,2,1,0:T(8,128)(2,1)S(1)} %collective-permute-done.7.got_ref), channel_id=1, source_target_pairs={{0,16},{16,0},{1,17},{17,1},{2,18},{18,2},{3,19},{19,3},{4,20},{20... | collective-permute-start | bytes 1179656 | tf_op jit(solution)/shard_map/ppermute | solution.py:283
  19.9 12.8 %collective-permute-start.12 = (bf16[1,64,768]{2,1,0:T(8,128)(2,1)S(1)}, bf16[1,64,768]{2,1,0:T(8,128)(2,1)S(1)}, u32[]{:S(2)}, u32[]{:S(2)}) collective-permute-start(bf16[1,64,768]{2,1,0:T(8,128)(2,1)S(1)} %get-tuple-element.33), channel_id=1, source_target_pairs={{0,8},{1,9},{4,12},{5,13},{8,0},{9,1},{12,4},{13,5},{2,10},{3,11},... | collective-permute-start | bytes 294920 | tf_op jit(solution)/shard_map/ppermute | solution.py:323
  22.1 10.9 %collective-permute-start.13 = (bf16[1,64,768]{2,1,0:T(8,128)(2,1)S(1)}, bf16[1,64,768]{2,1,0:T(8,128)(2,1)S(1)}, u32[]{:S(2)}, u32[]{:S(2)}) collective-permute-start(bf16[1,64,768]{2,1,0:T(8,128)(2,1)S(1)} %get-tuple-element.34), channel_id=1, source_target_pairs={{0,9},{1,8},{4,13},{5,12},{8,1},{9,0},{12,5},{13,4},{2,11},{3,10},... | collective-permute-start | bytes 294920 | tf_op jit(solution)/shard_map/ppermute | solution.py:323
  24.5 18.1 %collective-permute-start.14 = (bf16[1,64,768]{2,1,0:T(8,128)(2,1)S(1)}, bf16[1,64,768]{2,1,0:T(8,128)(2,1)S(1)}, u32[]{:S(2)}, u32[]{:S(2)}) collective-permute-start(bf16[1,64,768]{2,1,0:T(8,128)(2,1)S(1)} %get-tuple-element.35), channel_id=1, source_target_pairs={{0,1},{1,0},{4,5},{5,4},{8,9},{9,8},{12,13},{13,12},{2,3},{3,2},{6... | collective-permute-start | bytes 294920 | tf_op jit(solution)/shard_map/ppermute | solution.py:323
  27.7 15.4 %copy-start.1 = (bf16[2,64,2048]{2,1,0:T(8,128)(2,1)S(1)}, bf16[2,64,2048]{2,1,0:T(8,128)(2,1)}, u32[]{:S(2)}) copy-start(bf16[2,64,2048]{2,1,0:T(8,128)(2,1)} %target_ref.3) | copy-start | bytes 1572868
  27.7 15.4 %copy-start.2 = (f32[2,2048]{1,0:T(2,128)S(1)}, f32[2,2048]{1,0:T(2,128)}, u32[]{:S(2)}) copy-start(f32[2,2048]{1,0:T(2,128)} %bias_ref.3) | copy-start | bytes 49156
  27.7 14.9 %collective-permute-start.15 = (bf16[1,64,768]{2,1,0:T(8,128)(2,1)S(1)}, bf16[1,64,768]{2,1,0:T(8,128)(2,1)S(1)}, u32[]{:S(2)}, u32[]{:S(2)}) collective-permute-start(bf16[1,64,768]{2,1,0:T(8,128)(2,1)S(1)} %get-tuple-element.36), channel_id=1, source_target_pairs={{0,8},{1,9},{4,12},{5,13},{8,0},{9,1},{12,4},{13,5},{2,10},{3,11},... | collective-permute-start | bytes 294920 | tf_op jit(solution)/shard_map/ppermute | solution.py:323
  29.4 13.7 %collective-permute-start.16 = (bf16[1,64,768]{2,1,0:T(8,128)(2,1)S(1)}, bf16[1,64,768]{2,1,0:T(8,128)(2,1)S(1)}, u32[]{:S(2)}, u32[]{:S(2)}) collective-permute-start(bf16[1,64,768]{2,1,0:T(8,128)(2,1)S(1)} %get-tuple-element.37), channel_id=1, source_target_pairs={{0,9},{1,8},{4,13},{5,12},{8,1},{9,0},{12,5},{13,4},{2,11},{3,10},... | collective-permute-start | bytes 294920 | tf_op jit(solution)/shard_map/ppermute | solution.py:323
  32.7 10.3 %collective-permute-start.17 = (bf16[1,64,768]{2,1,0:T(8,128)(2,1)S(1)}, bf16[1,64,768]{2,1,0:T(8,128)(2,1)S(1)}, u32[]{:S(2)}, u32[]{:S(2)}) collective-permute-start(bf16[1,64,768]{2,1,0:T(8,128)(2,1)S(1)} %get-tuple-element.38), channel_id=1, source_target_pairs={{0,1},{1,0},{4,5},{5,4},{8,9},{9,8},{12,13},{13,12},{2,3},{3,2},{6... | collective-permute-start | bytes 294920 | tf_op jit(solution)/shard_map/ppermute | solution.py:323
  33.1 12.1 %collective-permute-start.9 = (bf16[2,64,256]{2,1,0:T(8,128)(2,1)S(1)}, bf16[2,64,256]{2,1,0:T(8,128)(2,1)S(1)}, u32[]{:S(2)}, u32[]{:S(2)}) collective-permute-start(bf16[2,64,256]{2,1,0:T(8,128)(2,1)S(1)} %get-tuple-element.29), channel_id=1, source_target_pairs={{0,8},{1,9},{4,12},{5,13},{8,0},{9,1},{12,4},{13,5},{2,10},{3,11},... | collective-permute-start | bytes 196616 | tf_op jit(solution)/shard_map/ppermute | solution.py:323
  42.6 4.6 %collective-permute-start.10 = (bf16[2,64,256]{2,1,0:T(8,128)(2,1)S(1)}, bf16[2,64,256]{2,1,0:T(8,128)(2,1)S(1)}, u32[]{:S(2)}, u32[]{:S(2)}) collective-permute-start(bf16[2,64,256]{2,1,0:T(8,128)(2,1)S(1)} %get-tuple-element.30), channel_id=1, source_target_pairs={{0,9},{1,8},{4,13},{5,12},{8,1},{9,0},{12,5},{13,4},{2,11},{3,10},... | collective-permute-start | bytes 196616 | tf_op jit(solution)/shard_map/ppermute | solution.py:323
  42.6 4.6 %collective-permute-start.11 = (bf16[2,64,256]{2,1,0:T(8,128)(2,1)S(1)}, bf16[2,64,256]{2,1,0:T(8,128)(2,1)S(1)}, u32[]{:S(2)}, u32[]{:S(2)}) collective-permute-start(bf16[2,64,256]{2,1,0:T(8,128)(2,1)S(1)} %get-tuple-element.31), channel_id=1, source_target_pairs={{0,1},{1,0},{4,5},{5,4},{8,9},{9,8},{12,13},{13,12},{2,3},{3,2},{6... | collective-permute-start | bytes 196616 | tf_op jit(solution)/shard_map/ppermute | solution.py:323

commit v22 on v21

--- a/solution.py
+++ b/solution.py
@@ -63,11 +63,11 @@
         copies.append(pltpu.make_async_copy(w_hbm.at[rows], w_ref.at[rows], w_sems.at[i]))
     for copy in copies:
         copy.start()
-    for copy in copies:
-        copy.wait()
     copies_part = []
     for i, piece in enumerate(pieces):
         copies_part += part_copies(piece, dec_hbm, part_refs[i], part_sems.at[i])
+    for copy in copies:
+        copy.wait()
     src = lax.axis_index("src")
     for k in range(n):
         dest = peer(src, k, n)

time: 48.1 us -> 47.3 us (0.983)
  Pallas kernels: 7.25 us -> 6.35 us
    pallas_call x1, Pallas kernels: 2.97 us -> 2.07 us  [body(): pl.pallas_call(functools.partial(encode_kernel, n, fetched[:1]), out_shap...]
  transfers between devices with their start and end apart: 18 -> 18, of which waited for: 5 -> 5; matrix products, arithmetic and copies ran while one was open for 0% -> 0% of each run, Pallas kernels for 7% -> 8%
where the time goes in v22:
time: 47.3 us; the launch traced here: 47.1 us
  starting transfers between devices  30.8 us (65%)
  waiting for transfers between devices  9.79 us (21%)
  Pallas kernels  6.35 us (13%)
    ppermute x9, starting transfers between devices, body(): sums[i].append(lax.ppermute(terms[2 * j + r], ('src', 'rep'), perm))  19.9 us
    ppermute x3, waiting for transfers between devices, body(): lax.ppermute(terms[k], 'src', [(i, peer(i, k, n)) for i in range(n)])  3.94 us
    ppermute x9, waiting for transfers between devices, body(): sums[i].append(lax.ppermute(terms[2 * j + r], ('src', 'rep'), perm))  3.3 us
    ppermute x3, starting transfers between devices, body(): codes.append(lax.ppermute(own, ('tgt', 'rep'), perm) if k + r else own)  3.13 us
    ppermute x3, starting transfers between devices, body(): lax.ppermute(terms[k], 'src', [(i, peer(i, k, n)) for i in range(n)])  2.71 us
    ppermute x1, starting transfers between devices, body(): got.append(lax.ppermute(part, 'src', pair))  2.7 us
    ppermute x1, waiting for transfers between devices, body(): got.append(lax.ppermute(got[0], 'parts', [(0, 1), (1, 0)]))  2.54 us
    pallas_call x1, Pallas kernels, body(): pl.pallas_call(functools.partial(encode_kernel, n, fetched[:1]), out_shap...  2.07 us
  transfers between devices with their start and end apart: 18, of which 5 were waited for; matrix products, arithmetic and copies ran while one was open for 0% of the time, Pallas kernels for 8%

profile of v22, /device:TPU:9, one launch (start us, length us, event | category | flops | bytes accessed | tf_op | source)
XLA Modules:
  0.0 47.1 jit_solution(3600057176589107276)
XLA Ops:
  0.0 2.1 %encode.1 = (bf16[128,256]{1,0:T(8,128)(2,1)S(1)}, bf16[128,256]{1,0:T(8,128)(2,1)S(1)}, bf16[128,256]{1,0:T(8,128)(2,1)S(1)}, bf16[128,256]{1,0:T(8,128)(2,1)S(1)}, bf16[1,2,128,768]{3,2,1,0:T(8,128)(2,1)S(1)}) custom-call(bf16[2,2,64,1024]{3,2,1,0:T(8,128)(2,1)} %bitcast.3, bf16[1024,512]{1,0:T(8,128)(2,1)} %w_hbm.1, bf16[2,2,128,2048]{3,2,1,0:T(8,128)(2,1)} %dec_ref.5), custom_call_target="tpu_custom_call" | custom-call | tf_op jit(solution)/shard_map/encode/pallas_call | solution.py:223
  2.1 0.1 collective-permute-start
  2.2 2.5 %collective-permute-start.1 = (bf16[128,256]{1,0:T(8,128)(2,1)S(1)}, bf16[128,256]{1,0:T(8,128)(2,1)S(1)}, u32[]{:S(2)}, u32[]{:S(2)}) collective-permute-start(bf16[128,256]{1,0:T(8,128)(2,1)S(1)} %get-tuple-element.24), channel_id=1, source_target_pairs={{0,8},{4,12},{8,0},{12,4},{1,9},{5,13},{9,1},{13,5},{2,10},{6,14},... | collective-permute-start | bytes 196616 | tf_op jit(solution)/shard_map/ppermute | solution.py:242
  4.6 0.2 collective-permute-start.2
  4.8 1.1 %collective-permute-start.7 = (bf16[1,2,128,768]{3,2,1,0:T(8,128)(2,1)S(1)}, bf16[1,2,128,768]{3,2,1,0:T(8,128)(2,1)S(1)}, u32[]{:S(2)}, u32[]{:S(2)}) collective-permute-start(bf16[1,2,128,768]{3,2,1,0:T(8,128)(2,1)S(1)} %get-tuple-element.26.before_ref), channel_id=1, source_target_pairs={{0,4},{4,0},{8,12},{12,8},{1,5},{5,1},{9,13},{13,9},{2,6},{6,2},{1... | collective-permute-start | bytes 1179656 | tf_op jit(solution)/shard_map/ppermute | solution.py:282
  5.9 0.0 collective-permute-done.refs_1_
  5.9 1.3 %collective-permute-done.1.refs_2_ = bf16[128,256]{1,0:T(8,128)(2,1)S(1)} collective-permute-done((bf16[128,256]{1,0:T(8,128)(2,1)S(1)}, bf16[128,256]{1,0:T(8,128)(2,1)S(1)}, u32[]{:S(2)}, u32[]{:S(2)}) %collective-permute-start.1) | collective-permute-done | bytes 65568 | tf_op jit(solution)/shard_map/ppermute | solution.py:242
  7.2 2.6 %collective-permute-done.2.refs_3_ = bf16[128,256]{1,0:T(8,128)(2,1)S(1)} collective-permute-done((bf16[128,256]{1,0:T(8,128)(2,1)S(1)}, bf16[128,256]{1,0:T(8,128)(2,1)S(1)}, u32[]{:S(2)}, u32[]{:S(2)}) %collective-permute-start.2) | collective-permute-done | bytes 65568 | tf_op jit(solution)/shard_map/ppermute | solution.py:242
  9.9 0.6 %codes.1.refs_0_.after_ref = bf16[2,64,256]{2,1,0:T(8,128)(2,1)S(1)} custom-call(s32[2,8]{1,0:T(2,128)S(1)} %copy-done.4, f32[4,128]{1,0:T(4,128)S(1)} %bitcast.2, bf16[128,256]{1,0:T(8,128)(2,1)S(1)} %get-tuple-element.22.refs_0_, bf16[128,256]{1,0:T(8,128)(2,1)S(1)} %collective-permute-done.refs_1_, bf16[128,256]{1,0:T(8,128)(2,1)S(1)} %collective-permute-done.1.refs_2_, ...), custom_call_target="tpu_custom_call" | custom-call | flops 20000000000 | tf_op jit(solution)/shard_map/codes/pallas_call | solution.py:244
  10.5 2.7 %collective-permute-start.5 = (bf16[2,64,256]{2,1,0:T(8,128)(2,1)S(1)}, bf16[2,64,256]{2,1,0:T(8,128)(2,1)S(1)}, u32[]{:S(2)}, u32[]{:S(2)}) collective-permute-start(bf16[2,64,256]{2,1,0:T(8,128)(2,1)S(1)} %codes.1.refs_0_.after_ref), channel_id=1, source_target_pairs={{0,3},{1,2},{2,1},{3,0},{4,7},{5,6},{6,5},{7,4},{8,11},{9,10},{10,... | collective-permute-start | bytes 196616 | tf_op jit(solution)/shard_map/ppermute | solution.py:259
  13.2 0.3 collective-permute-start.4
  13.4 0.2 collective-permute-start.3
  13.6 1.0 %part.1 = bf16[2,2,128,256]{3,2,1,0:T(8,128)(2,1)S(1)} custom-call(bf16[1,2,128,768]{3,2,1,0:T(8,128)(2,1)S(1)} %get-tuple-element.26.before_ref, bf16[2,2,128,2048]{3,2,1,0:T(8,128)(2,1)} %dec_ref.5, bf16[2,64,256]{2,1,0:T(8,128)(2,1)S(1)} %codes.1.refs_0_.after_ref), custom_call_target="tpu_custom_call" | custom-call | tf_op jit(solution)/shard_map/part/pallas_call | solution.py:271
  14.6 0.0 copy-start
  14.6 2.7 %collective-permute-start.6 = (bf16[2,2,128,256]{3,2,1,0:T(8,128)(2,1)S(1)}, bf16[2,2,128,256]{3,2,1,0:T(8,128)(2,1)S(1)}, u32[]{:S(2)}, u32[]{:S(2)}) collective-permute-start(bf16[2,2,128,256]{3,2,1,0:T(8,128)(2,1)S(1)} %part.1), channel_id=1, source_target_pairs={{0,4},{4,0},{8,12},{12,8},{1,5},{5,1},{9,13},{13,9},{2,6},{6,2},{1... | collective-permute-start | bytes 786440 | tf_op jit(solution)/shard_map/ppermute | solution.py:284
  17.3 0.0 collective-permute-done.7.got_ref
  17.3 1.2 %collective-permute-start.8 = (bf16[1,2,128,768]{3,2,1,0:T(8,128)(2,1)S(1)}, bf16[1,2,128,768]{3,2,1,0:T(8,128)(2,1)S(1)}, u32[]{:S(2)}, u32[]{:S(2)}) collective-permute-start(bf16[1,2,128,768]{3,2,1,0:T(8,128)(2,1)S(1)} %collective-permute-done.7.got_ref), channel_id=1, source_target_pairs={{0,16},{16,0},{1,17},{17,1},{2,18},{18,2},{3,19},{19,3},{4,20},{20... | collective-permute-start | bytes 1179656 | tf_op jit(solution)/shard_map/ppermute | solution.py:283
  18.6 0.0 collective-permute-done.5.refs_3_
  18.6 0.0 collective-permute-done.4.refs_2_
  18.6 0.0 collective-permute-done.3.refs_1_
  18.6 0.1 gather.1.lhs_ref
  18.7 0.4 decode.3
  19.0 2.2 %collective-permute-start.12 = (bf16[1,64,768]{2,1,0:T(8,128)(2,1)S(1)}, bf16[1,64,768]{2,1,0:T(8,128)(2,1)S(1)}, u32[]{:S(2)}, u32[]{:S(2)}) collective-permute-start(bf16[1,64,768]{2,1,0:T(8,128)(2,1)S(1)} %get-tuple-element.33), channel_id=1, source_target_pairs={{0,8},{1,9},{4,12},{5,13},{8,0},{9,1},{12,4},{13,5},{2,10},{3,11},... | collective-permute-start | bytes 294920 | tf_op jit(solution)/shard_map/ppermute | solution.py:323
  21.2 2.3 %collective-permute-start.13 = (bf16[1,64,768]{2,1,0:T(8,128)(2,1)S(1)}, bf16[1,64,768]{2,1,0:T(8,128)(2,1)S(1)}, u32[]{:S(2)}, u32[]{:S(2)}) collective-permute-start(bf16[1,64,768]{2,1,0:T(8,128)(2,1)S(1)} %get-tuple-element.34), channel_id=1, source_target_pairs={{0,9},{1,8},{4,13},{5,12},{8,1},{9,0},{12,5},{13,4},{2,11},{3,10},... | collective-permute-start | bytes 294920 | tf_op jit(solution)/shard_map/ppermute | solution.py:323
  23.5 0.3 collective-permute-start.14
  23.9 2.5 %collective-permute-done.8.got_ref = bf16[1,2,128,768]{3,2,1,0:T(8,128)(2,1)S(1)} collective-permute-done((bf16[1,2,128,768]{3,2,1,0:T(8,128)(2,1)S(1)}, bf16[1,2,128,768]{3,2,1,0:T(8,128)(2,1)S(1)}, u32[]{:S(2)}, u32[]{:S(2)}) %collective-permute-start.8) | collective-permute-done | bytes 393248 | tf_op jit(solution)/shard_map/ppermute | solution.py:283
  26.4 0.4 decode.4
  26.8 0.0 copy-start.1
  26.8 0.0 copy-start.2
  26.8 1.7 %collective-permute-start.15 = (bf16[1,64,768]{2,1,0:T(8,128)(2,1)S(1)}, bf16[1,64,768]{2,1,0:T(8,128)(2,1)S(1)}, u32[]{:S(2)}, u32[]{:S(2)}) collective-permute-start(bf16[1,64,768]{2,1,0:T(8,128)(2,1)S(1)} %get-tuple-element.36), channel_id=1, source_target_pairs={{0,8},{1,9},{4,12},{5,13},{8,0},{9,1},{12,4},{13,5},{2,10},{3,11},... | collective-permute-start | bytes 294920 | tf_op jit(solution)/shard_map/ppermute | solution.py:323
  28.5 0.0 collective-permute-done.6.got_ref
  28.5 3.4 %collective-permute-start.16 = (bf16[1,64,768]{2,1,0:T(8,128)(2,1)S(1)}, bf16[1,64,768]{2,1,0:T(8,128)(2,1)S(1)}, u32[]{:S(2)}, u32[]{:S(2)}) collective-permute-start(bf16[1,64,768]{2,1,0:T(8,128)(2,1)S(1)} %get-tuple-element.37), channel_id=1, source_target_pairs={{0,9},{1,8},{4,13},{5,12},{8,1},{9,0},{12,5},{13,4},{2,11},{3,10},... | collective-permute-start | bytes 294920 | tf_op jit(solution)/shard_map/ppermute | solution.py:323
  31.8 0.0 collective-permute-done.12.refs_0_
  31.8 0.0 collective-permute-start.17
  31.9 0.3 decode.5
  32.2 0.0 collective-permute-done.13.refs_1_
  32.2 9.6 %collective-permute-start.9 = (bf16[2,64,256]{2,1,0:T(8,128)(2,1)S(1)}, bf16[2,64,256]{2,1,0:T(8,128)(2,1)S(1)}, u32[]{:S(2)}, u32[]{:S(2)}) collective-permute-start(bf16[2,64,256]{2,1,0:T(8,128)(2,1)S(1)} %get-tuple-element.29), channel_id=1, source_target_pairs={{0,8},{1,9},{4,12},{5,13},{8,0},{9,1},{12,4},{13,5},{2,10},{3,11},... | collective-permute-start | bytes 196616 | tf_op jit(solution)/shard_map/ppermute | solution.py:323
  41.7 0.0 collective-permute-done.14.refs_2_
  41.8 0.0 collective-permute-start.10
  41.8 0.0 collective-permute-done.15.refs_4_
  41.8 0.4 collective-permute-start.11
  42.2 0.0 collective-permute-done.16.refs_5_
  42.2 0.0 collective-permute-done.17.refs_6_
  42.2 0.9 %add.2.refs_4_ = bf16[2,64,2048]{2,1,0:T(8,128)(2,1)} custom-call(f32[2,2048]{1,0:T(2,128)S(1)} %copy-done.2, bf16[2,64,2048]{2,1,0:T(8,128)(2,1)S(1)} %copy-done.1, bf16[1,64,768]{2,1,0:T(8,128)(2,1)S(1)} %collective-permute-done.12.refs_0_, bf16[1,64,768]{2,1,0:T(8,128)(2,1)S(1)} %collective-permute-done.13.refs_1_, ...), custom_call_target="tpu_custom_call" | custom-call | flops 20000000000 | tf_op jit(solution)/shard_map/add/pallas_call | solution.py:290
  43.1 1.3 %collective-permute-done.9.refs_0_ = bf16[2,64,256]{2,1,0:T(8,128)(2,1)S(1)} collective-permute-done((bf16[2,64,256]{2,1,0:T(8,128)(2,1)S(1)}, bf16[2,64,256]{2,1,0:T(8,128)(2,1)S(1)}, u32[]{:S(2)}, u32[]{:S(2)}) %collective-permute-start.9) | collective-permute-done | bytes 65568 | tf_op jit(solution)/shard_map/ppermute | solution.py:323
  44.3 2.0 %collective-permute-done.10.refs_1_ = bf16[2,64,256]{2,1,0:T(8,128)(2,1)S(1)} collective-permute-done((bf16[2,64,256]{2,1,0:T(8,128)(2,1)S(1)}, bf16[2,64,256]{2,1,0:T(8,128)(2,1)S(1)}, u32[]{:S(2)}, u32[]{:S(2)}) %collective-permute-start.10) | collective-permute-done | bytes 65568 | tf_op jit(solution)/shard_map/ppermute | solution.py:323
  46.3 0.0 collective-permute-done.11.refs_2_
  46.3 0.7 %add.3 = bf16[2,64,2048]{2,1,0:T(8,128)(2,1)} custom-call(f32[2,2048]{1,0:T(2,128)S(1)} %copy-done.2, bf16[2,64,2048]{2,1,0:T(8,128)(2,1)S(1)} %copy-done.1, bf16[2,64,256]{2,1,0:T(8,128)(2,1)S(1)} %collective-permute-done.9.refs_0_, bf16[2,64,256]{2,1,0:T(8,128)(2,1)S(1)} %collective-permute-done.10.refs_1_, ...), custom_call_target="tpu_custom_call", output_to_operand_aliasing={{}: (6, {})} | custom-call | tf_op jit(solution)/shard_map/add/pallas_call | solution.py:290
  (7 shorter events, 0.0 us)
Async XLA Ops:
  0.0 9.9 %copy-start.4 = (s32[2,8]{1,0:T(2,128)S(1)}, s32[2,8]{1,0:T(2,128)}, u32[]{:S(2)}) copy-start(s32[2,8]{1,0:T(2,128)} %active_ref.1) | copy-start | bytes 196
  0.0 9.9 %copy-start.3 = (f32[512]{0:T(512)S(1)}, f32[512]{0:T(512)}, u32[]{:S(2)}) copy-start(f32[512]{0:T(512)} %param.9) | copy-start | bytes 6148
  2.1 3.8 %collective-permute-start = (bf16[128,256]{1,0:T(8,128)(2,1)S(1)}, bf16[128,256]{1,0:T(8,128)(2,1)S(1)}, u32[]{:S(2)}, u32[]{:S(2)}) collective-permute-start(bf16[128,256]{1,0:T(8,128)(2,1)S(1)} %get-tuple-element.23), channel_id=1, source_target_pairs={{0,4},{4,0},{8,12},{12,8},{1,5},{5,1},{9,13},{13,9},{2,6},{6,2},{1... | collective-permute-start | bytes 196616 | tf_op jit(solution)/shard_map/ppermute | solution.py:242
  2.2 5.1 %collective-permute-start.1 = (bf16[128,256]{1,0:T(8,128)(2,1)S(1)}, bf16[128,256]{1,0:T(8,128)(2,1)S(1)}, u32[]{:S(2)}, u32[]{:S(2)}) collective-permute-start(bf16[128,256]{1,0:T(8,128)(2,1)S(1)} %get-tuple-element.24), channel_id=1, source_target_pairs={{0,8},{4,12},{8,0},{12,4},{1,9},{5,13},{9,1},{13,5},{2,10},{6,14},... | collective-permute-start | bytes 196616 | tf_op jit(solution)/shard_map/ppermute | solution.py:242
  4.6 5.2 %collective-permute-start.2 = (bf16[128,256]{1,0:T(8,128)(2,1)S(1)}, bf16[128,256]{1,0:T(8,128)(2,1)S(1)}, u32[]{:S(2)}, u32[]{:S(2)}) collective-permute-start(bf16[128,256]{1,0:T(8,128)(2,1)S(1)} %get-tuple-element.25), channel_id=1, source_target_pairs={{0,12},{4,8},{8,4},{12,0},{1,13},{5,9},{9,5},{13,1},{2,14},{6,10},... | collective-permute-start | bytes 196616 | tf_op jit(solution)/shard_map/ppermute | solution.py:242
  4.8 12.5 %collective-permute-start.7 = (bf16[1,2,128,768]{3,2,1,0:T(8,128)(2,1)S(1)}, bf16[1,2,128,768]{3,2,1,0:T(8,128)(2,1)S(1)}, u32[]{:S(2)}, u32[]{:S(2)}) collective-permute-start(bf16[1,2,128,768]{3,2,1,0:T(8,128)(2,1)S(1)} %get-tuple-element.26.before_ref), channel_id=1, source_target_pairs={{0,4},{4,0},{8,12},{12,8},{1,5},{5,1},{9,13},{13,9},{2,6},{6,2},{1... | collective-permute-start | bytes 1179656 | tf_op jit(solution)/shard_map/ppermute | solution.py:282
  10.5 8.1 %collective-permute-start.5 = (bf16[2,64,256]{2,1,0:T(8,128)(2,1)S(1)}, bf16[2,64,256]{2,1,0:T(8,128)(2,1)S(1)}, u32[]{:S(2)}, u32[]{:S(2)}) collective-permute-start(bf16[2,64,256]{2,1,0:T(8,128)(2,1)S(1)} %codes.1.refs_0_.after_ref), channel_id=1, source_target_pairs={{0,3},{1,2},{2,1},{3,0},{4,7},{5,6},{6,5},{7,4},{8,11},{9,10},{10,... | collective-permute-start | bytes 196616 | tf_op jit(solution)/shard_map/ppermute | solution.py:259
  13.2 5.4 %collective-permute-start.4 = (bf16[2,64,256]{2,1,0:T(8,128)(2,1)S(1)}, bf16[2,64,256]{2,1,0:T(8,128)(2,1)S(1)}, u32[]{:S(2)}, u32[]{:S(2)}) collective-permute-start(bf16[2,64,256]{2,1,0:T(8,128)(2,1)S(1)} %codes.1.refs_0_.after_ref), channel_id=1, source_target_pairs={{0,2},{1,3},{2,0},{3,1},{4,6},{5,7},{6,4},{7,5},{8,10},{9,11},{10,... | collective-permute-start | bytes 196616 | tf_op jit(solution)/shard_map/ppermute | solution.py:259
  13.4 5.2 %collective-permute-start.3 = (bf16[2,64,256]{2,1,0:T(8,128)(2,1)S(1)}, bf16[2,64,256]{2,1,0:T(8,128)(2,1)S(1)}, u32[]{:S(2)}, u32[]{:S(2)}) collective-permute-start(bf16[2,64,256]{2,1,0:T(8,128)(2,1)S(1)} %codes.1.refs_0_.after_ref), channel_id=1, source_target_pairs={{0,1},{1,0},{2,3},{3,2},{4,5},{5,4},{6,7},{7,6},{8,9},{9,8},{10,11... | collective-permute-start | bytes 196616 | tf_op jit(solution)/shard_map/ppermute | solution.py:259
  14.6 4.0 %copy-start = (bf16[2,2,128,2048]{3,2,1,0:T(8,128)(2,1)S(1)}, bf16[2,2,128,2048]{3,2,1,0:T(8,128)(2,1)}, u32[]{:S(2)}) copy-start(bf16[2,2,128,2048]{3,2,1,0:T(8,128)(2,1)} %dec_ref.5) | copy-start | bytes 6291460
  14.6 13.9 %collective-permute-start.6 = (bf16[2,2,128,256]{3,2,1,0:T(8,128)(2,1)S(1)}, bf16[2,2,128,256]{3,2,1,0:T(8,128)(2,1)S(1)}, u32[]{:S(2)}, u32[]{:S(2)}) collective-permute-start(bf16[2,2,128,256]{3,2,1,0:T(8,128)(2,1)S(1)} %part.1), channel_id=1, source_target_pairs={{0,4},{4,0},{8,12},{12,8},{1,5},{5,1},{9,13},{13,9},{2,6},{6,2},{1... | collective-permute-start | bytes 786440 | tf_op jit(solution)/shard_map/ppermute | solution.py:284
  17.3 9.1 %collective-permute-start.8 = (bf16[1,2,128,768]{3,2,1,0:T(8,128)(2,1)S(1)}, bf16[1,2,128,768]{3,2,1,0:T(8,128)(2,1)S(1)}, u32[]{:S(2)}, u32[]{:S(2)}) collective-permute-start(bf16[1,2,128,768]{3,2,1,0:T(8,128)(2,1)S(1)} %collective-permute-done.7.got_ref), channel_id=1, source_target_pairs={{0,16},{16,0},{1,17},{17,1},{2,18},{18,2},{3,19},{19,3},{4,20},{20... | collective-permute-start | bytes 1179656 | tf_op jit(solution)/shard_map/ppermute | solution.py:283
  19.0 12.8 %collective-permute-start.12 = (bf16[1,64,768]{2,1,0:T(8,128)(2,1)S(1)}, bf16[1,64,768]{2,1,0:T(8,128)(2,1)S(1)}, u32[]{:S(2)}, u32[]{:S(2)}) collective-permute-start(bf16[1,64,768]{2,1,0:T(8,128)(2,1)S(1)} %get-tuple-element.33), channel_id=1, source_target_pairs={{0,8},{1,9},{4,12},{5,13},{8,0},{9,1},{12,4},{13,5},{2,10},{3,11},... | collective-permute-start | bytes 294920 | tf_op jit(solution)/shard_map/ppermute | solution.py:323
  21.2 10.9 %collective-permute-start.13 = (bf16[1,64,768]{2,1,0:T(8,128)(2,1)S(1)}, bf16[1,64,768]{2,1,0:T(8,128)(2,1)S(1)}, u32[]{:S(2)}, u32[]{:S(2)}) collective-permute-start(bf16[1,64,768]{2,1,0:T(8,128)(2,1)S(1)} %get-tuple-element.34), channel_id=1, source_target_pairs={{0,9},{1,8},{4,13},{5,12},{8,1},{9,0},{12,5},{13,4},{2,11},{3,10},... | collective-permute-start | bytes 294920 | tf_op jit(solution)/shard_map/ppermute | solution.py:323
  23.5 18.2 %collective-permute-start.14 = (bf16[1,64,768]{2,1,0:T(8,128)(2,1)S(1)}, bf16[1,64,768]{2,1,0:T(8,128)(2,1)S(1)}, u32[]{:S(2)}, u32[]{:S(2)}) collective-permute-start(bf16[1,64,768]{2,1,0:T(8,128)(2,1)S(1)} %get-tuple-element.35), channel_id=1, source_target_pairs={{0,1},{1,0},{4,5},{5,4},{8,9},{9,8},{12,13},{13,12},{2,3},{3,2},{6... | collective-permute-start | bytes 294920 | tf_op jit(solution)/shard_map/ppermute | solution.py:323
  26.8 15.4 %copy-start.1 = (bf16[2,64,2048]{2,1,0:T(8,128)(2,1)S(1)}, bf16[2,64,2048]{2,1,0:T(8,128)(2,1)}, u32[]{:S(2)}) copy-start(bf16[2,64,2048]{2,1,0:T(8,128)(2,1)} %target_ref.3) | copy-start | bytes 1572868
  26.8 15.4 %copy-start.2 = (f32[2,2048]{1,0:T(2,128)S(1)}, f32[2,2048]{1,0:T(2,128)}, u32[]{:S(2)}) copy-start(f32[2,2048]{1,0:T(2,128)} %bias_ref.3) | copy-start | bytes 49156
  26.8 15.0 %collective-permute-start.15 = (bf16[1,64,768]{2,1,0:T(8,128)(2,1)S(1)}, bf16[1,64,768]{2,1,0:T(8,128)(2,1)S(1)}, u32[]{:S(2)}, u32[]{:S(2)}) collective-permute-start(bf16[1,64,768]{2,1,0:T(8,128)(2,1)S(1)} %get-tuple-element.36), channel_id=1, source_target_pairs={{0,8},{1,9},{4,12},{5,13},{8,0},{9,1},{12,4},{13,5},{2,10},{3,11},... | collective-permute-start | bytes 294920 | tf_op jit(solution)/shard_map/ppermute | solution.py:323
  28.5 13.7 %collective-permute-start.16 = (bf16[1,64,768]{2,1,0:T(8,128)(2,1)S(1)}, bf16[1,64,768]{2,1,0:T(8,128)(2,1)S(1)}, u32[]{:S(2)}, u32[]{:S(2)}) collective-permute-start(bf16[1,64,768]{2,1,0:T(8,128)(2,1)S(1)} %get-tuple-element.37), channel_id=1, source_target_pairs={{0,9},{1,8},{4,13},{5,12},{8,1},{9,0},{12,5},{13,4},{2,11},{3,10},... | collective-permute-start | bytes 294920 | tf_op jit(solution)/shard_map/ppermute | solution.py:323
  31.8 10.3 %collective-permute-start.17 = (bf16[1,64,768]{2,1,0:T(8,128)(2,1)S(1)}, bf16[1,64,768]{2,1,0:T(8,128)(2,1)S(1)}, u32[]{:S(2)}, u32[]{:S(2)}) collective-permute-start(bf16[1,64,768]{2,1,0:T(8,128)(2,1)S(1)} %get-tuple-element.38), channel_id=1, source_target_pairs={{0,1},{1,0},{4,5},{5,4},{8,9},{9,8},{12,13},{13,12},{2,3},{3,2},{6... | collective-permute-start | bytes 294920 | tf_op jit(solution)/shard_map/ppermute | solution.py:323
  32.2 12.2 %collective-permute-start.9 = (bf16[2,64,256]{2,1,0:T(8,128)(2,1)S(1)}, bf16[2,64,256]{2,1,0:T(8,128)(2,1)S(1)}, u32[]{:S(2)}, u32[]{:S(2)}) collective-permute-start(bf16[2,64,256]{2,1,0:T(8,128)(2,1)S(1)} %get-tuple-element.29), channel_id=1, source_target_pairs={{0,8},{1,9},{4,12},{5,13},{8,0},{9,1},{12,4},{13,5},{2,10},{3,11},... | collective-permute-start | bytes 196616 | tf_op jit(solution)/shard_map/ppermute | solution.py:323
  41.8 4.6 %collective-permute-start.10 = (bf16[2,64,256]{2,1,0:T(8,128)(2,1)S(1)}, bf16[2,64,256]{2,1,0:T(8,128)(2,1)S(1)}, u32[]{:S(2)}, u32[]{:S(2)}) collective-permute-start(bf16[2,64,256]{2,1,0:T(8,128)(2,1)S(1)} %get-tuple-element.30), channel_id=1, source_target_pairs={{0,9},{1,8},{4,13},{5,12},{8,1},{9,0},{12,5},{13,4},{2,11},{3,10},... | collective-permute-start | bytes 196616 | tf_op jit(solution)/shard_map/ppermute | solution.py:323
  41.8 4.6 %collective-permute-start.11 = (bf16[2,64,256]{2,1,0:T(8,128)(2,1)S(1)}, bf16[2,64,256]{2,1,0:T(8,128)(2,1)S(1)}, u32[]{:S(2)}, u32[]{:S(2)}) collective-permute-start(bf16[2,64,256]{2,1,0:T(8,128)(2,1)S(1)} %get-tuple-element.31), channel_id=1, source_target_pairs={{0,1},{1,0},{4,5},{5,4},{8,9},{9,8},{12,13},{13,12},{2,3},{3,2},{6... | collective-permute-start | bytes 196616 | tf_op jit(solution)/shard_map/ppermute | solution.py:323

commit v23 on v22

--- a/solution.py
+++ b/solution.py
@@ -66,17 +66,26 @@
     copies_part = []
     for i, piece in enumerate(pieces):
         copies_part += part_copies(piece, dec_hbm, part_refs[i], part_sems.at[i])
-    for copy in copies:
+    for copy in copies[: 2 * half]:
         copy.wait()
     src = lax.axis_index("src")
-    for k in range(n):
-        dest = peer(src, k, n)
-        rows = acts_ref[lax.rem(dest, 2)]
-        rows = rows.reshape(rows.shape[0] * rows.shape[1], rows.shape[2])
-        columns = pl.ds(pl.multiple_of((dest // 2) * width, width), width)
-        term_refs[k][...] = jnp.dot(
-            rows, w_ref[:, columns], preferred_element_type=jnp.float32
-        ).astype(jnp.bfloat16)
+    features = w_ref.shape[0]
+    steps = max(1, min(4, features // 256))
+    totals = [0.0] * n
+    for step in range(steps):
+        for copy in copies[2 * half + step * 8 // steps : 2 * half + (step + 1) * 8 // steps]:
+            copy.wait()
+        depths = slice(step * features // steps, (step + 1) * features // steps)
+        for k in range(n):
+            dest = peer(src, k, n)
+            rows = acts_ref[lax.rem(dest, 2), :, :, depths]
+            rows = rows.reshape(rows.shape[0] * rows.shape[1], rows.shape[2])
+            columns = pl.ds(pl.multiple_of((dest // 2) * width, width), width)
+            totals[k] += jnp.dot(
+                rows, w_ref[depths, columns], preferred_element_type=jnp.float32
+            )
+            if step == steps - 1:
+                term_refs[k][...] = totals[k].astype(jnp.bfloat16)
     for copy in copies_part:
         copy.wait()
 

time: 47.3 us -> 47.4 us (level)
  no operation moved by 1% of the time
where the time goes in v23:
time: 47.4 us; the launch traced here: 47.2 us
  starting transfers between devices  30.7 us (65%)
  waiting for transfers between devices  9.8 us (21%)
  Pallas kernels  6.5 us (14%)
    ppermute x9, starting transfers between devices, body(): sums[i].append(lax.ppermute(terms[2 * j + r], ('src', 'rep'), perm))  19.9 us
    ppermute x3, waiting for transfers between devices, body(): lax.ppermute(terms[k], 'src', [(i, peer(i, k, n)) for i in range(n)])  3.96 us
    ppermute x9, waiting for transfers between devices, body(): sums[i].append(lax.ppermute(terms[2 * j + r], ('src', 'rep'), perm))  3.3 us
    ppermute x3, starting transfers between devices, body(): codes.append(lax.ppermute(own, ('tgt', 'rep'), perm) if k + r else own)  3.11 us
    ppermute x3, starting transfers between devices, body(): lax.ppermute(terms[k], 'src', [(i, peer(i, k, n)) for i in range(n)])  2.71 us
    ppermute x1, starting transfers between devices, body(): got.append(lax.ppermute(part, 'src', pair))  2.69 us
    ppermute x1, waiting for transfers between devices, body(): got.append(lax.ppermute(got[0], 'parts', [(0, 1), (1, 0)]))  2.53 us
    pallas_call x1, Pallas kernels, body(): pl.pallas_call(functools.partial(encode_kernel, n, fetched[:1]), out_shap...  2.22 us
  transfers between devices with their start and end apart: 18, of which 5 were waited for; matrix products, arithmetic and copies ran while one was open for 0% of the time, Pallas kernels for 8%

profile of v23, /device:TPU:9, one launch (start us, length us, event | category | flops | bytes accessed | tf_op | source)
XLA Modules:
  0.0 47.2 jit_solution(2609299848743488488)
XLA Ops:
  0.0 2.2 %encode.1 = (bf16[128,256]{1,0:T(8,128)(2,1)S(1)}, bf16[128,256]{1,0:T(8,128)(2,1)S(1)}, bf16[128,256]{1,0:T(8,128)(2,1)S(1)}, bf16[128,256]{1,0:T(8,128)(2,1)S(1)}, bf16[1,2,128,768]{3,2,1,0:T(8,128)(2,1)S(1)}) custom-call(bf16[2,2,64,1024]{3,2,1,0:T(8,128)(2,1)} %bitcast.3, bf16[1024,512]{1,0:T(8,128)(2,1)} %w_hbm.1, bf16[2,2,128,2048]{3,2,1,0:T(8,128)(2,1)} %dec_ref.5), custom_call_target="tpu_custom_call" | custom-call | tf_op jit(solution)/shard_map/encode/pallas_call | solution.py:232
  2.2 0.1 collective-permute-start
  2.3 2.4 %collective-permute-start.1 = (bf16[128,256]{1,0:T(8,128)(2,1)S(1)}, bf16[128,256]{1,0:T(8,128)(2,1)S(1)}, u32[]{:S(2)}, u32[]{:S(2)}) collective-permute-start(bf16[128,256]{1,0:T(8,128)(2,1)S(1)} %get-tuple-element.24), channel_id=1, source_target_pairs={{0,8},{4,12},{8,0},{12,4},{1,9},{5,13},{9,1},{13,5},{2,10},{6,14},... | collective-permute-start | bytes 196616 | tf_op jit(solution)/shard_map/ppermute | solution.py:251
  4.8 0.2 collective-permute-start.2
  4.9 1.1 %collective-permute-start.7 = (bf16[1,2,128,768]{3,2,1,0:T(8,128)(2,1)S(1)}, bf16[1,2,128,768]{3,2,1,0:T(8,128)(2,1)S(1)}, u32[]{:S(2)}, u32[]{:S(2)}) collective-permute-start(bf16[1,2,128,768]{3,2,1,0:T(8,128)(2,1)S(1)} %get-tuple-element.26.before_ref), channel_id=1, source_target_pairs={{0,4},{4,0},{8,12},{12,8},{1,5},{5,1},{9,13},{13,9},{2,6},{6,2},{1... | collective-permute-start | bytes 1179656 | tf_op jit(solution)/shard_map/ppermute | solution.py:291
  6.1 0.0 collective-permute-done.refs_1_
  6.1 1.3 %collective-permute-done.1.refs_2_ = bf16[128,256]{1,0:T(8,128)(2,1)S(1)} collective-permute-done((bf16[128,256]{1,0:T(8,128)(2,1)S(1)}, bf16[128,256]{1,0:T(8,128)(2,1)S(1)}, u32[]{:S(2)}, u32[]{:S(2)}) %collective-permute-start.1) | collective-permute-done | bytes 65568 | tf_op jit(solution)/shard_map/ppermute | solution.py:251
  7.4 2.7 %collective-permute-done.2.refs_3_ = bf16[128,256]{1,0:T(8,128)(2,1)S(1)} collective-permute-done((bf16[128,256]{1,0:T(8,128)(2,1)S(1)}, bf16[128,256]{1,0:T(8,128)(2,1)S(1)}, u32[]{:S(2)}, u32[]{:S(2)}) %collective-permute-start.2) | collective-permute-done | bytes 65568 | tf_op jit(solution)/shard_map/ppermute | solution.py:251
  10.0 0.6 %codes.1.refs_0_.after_ref = bf16[2,64,256]{2,1,0:T(8,128)(2,1)S(1)} custom-call(s32[2,8]{1,0:T(2,128)S(1)} %copy-done.4, f32[4,128]{1,0:T(4,128)S(1)} %bitcast.2, bf16[128,256]{1,0:T(8,128)(2,1)S(1)} %get-tuple-element.22.refs_0_, bf16[128,256]{1,0:T(8,128)(2,1)S(1)} %collective-permute-done.refs_1_, bf16[128,256]{1,0:T(8,128)(2,1)S(1)} %collective-permute-done.1.refs_2_, ...), custom_call_target="tpu_custom_call" | custom-call | flops 20000000000 | tf_op jit(solution)/shard_map/codes/pallas_call | solution.py:253
  10.7 2.6 %collective-permute-start.5 = (bf16[2,64,256]{2,1,0:T(8,128)(2,1)S(1)}, bf16[2,64,256]{2,1,0:T(8,128)(2,1)S(1)}, u32[]{:S(2)}, u32[]{:S(2)}) collective-permute-start(bf16[2,64,256]{2,1,0:T(8,128)(2,1)S(1)} %codes.1.refs_0_.after_ref), channel_id=1, source_target_pairs={{0,3},{1,2},{2,1},{3,0},{4,7},{5,6},{6,5},{7,4},{8,11},{9,10},{10,... | collective-permute-start | bytes 196616 | tf_op jit(solution)/shard_map/ppermute | solution.py:268
  13.3 0.3 collective-permute-start.4
  13.6 0.2 collective-permute-start.3
  13.8 1.0 %part.1 = bf16[2,2,128,256]{3,2,1,0:T(8,128)(2,1)S(1)} custom-call(bf16[1,2,128,768]{3,2,1,0:T(8,128)(2,1)S(1)} %get-tuple-element.26.before_ref, bf16[2,2,128,2048]{3,2,1,0:T(8,128)(2,1)} %dec_ref.5, bf16[2,64,256]{2,1,0:T(8,128)(2,1)S(1)} %codes.1.refs_0_.after_ref), custom_call_target="tpu_custom_call" | custom-call | tf_op jit(solution)/shard_map/part/pallas_call | solution.py:280
  14.7 0.0 copy-start
  14.8 2.7 %collective-permute-start.6 = (bf16[2,2,128,256]{3,2,1,0:T(8,128)(2,1)S(1)}, bf16[2,2,128,256]{3,2,1,0:T(8,128)(2,1)S(1)}, u32[]{:S(2)}, u32[]{:S(2)}) collective-permute-start(bf16[2,2,128,256]{3,2,1,0:T(8,128)(2,1)S(1)} %part.1), channel_id=1, source_target_pairs={{0,4},{4,0},{8,12},{12,8},{1,5},{5,1},{9,13},{13,9},{2,6},{6,2},{1... | collective-permute-start | bytes 786440 | tf_op jit(solution)/shard_map/ppermute | solution.py:293
  17.5 0.0 collective-permute-done.7.got_ref
  17.5 1.2 %collective-permute-start.8 = (bf16[1,2,128,768]{3,2,1,0:T(8,128)(2,1)S(1)}, bf16[1,2,128,768]{3,2,1,0:T(8,128)(2,1)S(1)}, u32[]{:S(2)}, u32[]{:S(2)}) collective-permute-start(bf16[1,2,128,768]{3,2,1,0:T(8,128)(2,1)S(1)} %collective-permute-done.7.got_ref), channel_id=1, source_target_pairs={{0,16},{16,0},{1,17},{17,1},{2,18},{18,2},{3,19},{19,3},{4,20},{20... | collective-permute-start | bytes 1179656 | tf_op jit(solution)/shard_map/ppermute | solution.py:292
  18.7 0.0 collective-permute-done.5.refs_3_
  18.7 0.0 collective-permute-done.4.refs_2_
  18.7 0.0 collective-permute-done.3.refs_1_
  18.7 0.1 gather.1.lhs_ref
  18.8 0.4 decode.3
  19.2 2.2 %collective-permute-start.12 = (bf16[1,64,768]{2,1,0:T(8,128)(2,1)S(1)}, bf16[1,64,768]{2,1,0:T(8,128)(2,1)S(1)}, u32[]{:S(2)}, u32[]{:S(2)}) collective-permute-start(bf16[1,64,768]{2,1,0:T(8,128)(2,1)S(1)} %get-tuple-element.33), channel_id=1, source_target_pairs={{0,8},{1,9},{4,12},{5,13},{8,0},{9,1},{12,4},{13,5},{2,10},{3,11},... | collective-permute-start | bytes 294920 | tf_op jit(solution)/shard_map/ppermute | solution.py:332
  21.4 2.3 %collective-permute-start.13 = (bf16[1,64,768]{2,1,0:T(8,128)(2,1)S(1)}, bf16[1,64,768]{2,1,0:T(8,128)(2,1)S(1)}, u32[]{:S(2)}, u32[]{:S(2)}) collective-permute-start(bf16[1,64,768]{2,1,0:T(8,128)(2,1)S(1)} %get-tuple-element.34), channel_id=1, source_target_pairs={{0,9},{1,8},{4,13},{5,12},{8,1},{9,0},{12,5},{13,4},{2,11},{3,10},... | collective-permute-start | bytes 294920 | tf_op jit(solution)/shard_map/ppermute | solution.py:332
  23.7 0.3 collective-permute-start.14
  24.0 2.5 %collective-permute-done.8.got_ref = bf16[1,2,128,768]{3,2,1,0:T(8,128)(2,1)S(1)} collective-permute-done((bf16[1,2,128,768]{3,2,1,0:T(8,128)(2,1)S(1)}, bf16[1,2,128,768]{3,2,1,0:T(8,128)(2,1)S(1)}, u32[]{:S(2)}, u32[]{:S(2)}) %collective-permute-start.8) | collective-permute-done | bytes 393248 | tf_op jit(solution)/shard_map/ppermute | solution.py:292
  26.5 0.4 decode.4
  26.9 0.0 copy-start.1
  26.9 0.0 copy-start.2
  26.9 1.7 %collective-permute-start.15 = (bf16[1,64,768]{2,1,0:T(8,128)(2,1)S(1)}, bf16[1,64,768]{2,1,0:T(8,128)(2,1)S(1)}, u32[]{:S(2)}, u32[]{:S(2)}) collective-permute-start(bf16[1,64,768]{2,1,0:T(8,128)(2,1)S(1)} %get-tuple-element.36), channel_id=1, source_target_pairs={{0,8},{1,9},{4,12},{5,13},{8,0},{9,1},{12,4},{13,5},{2,10},{3,11},... | collective-permute-start | bytes 294920 | tf_op jit(solution)/shard_map/ppermute | solution.py:332
  28.6 0.0 collective-permute-done.6.got_ref
  28.6 3.4 %collective-permute-start.16 = (bf16[1,64,768]{2,1,0:T(8,128)(2,1)S(1)}, bf16[1,64,768]{2,1,0:T(8,128)(2,1)S(1)}, u32[]{:S(2)}, u32[]{:S(2)}) collective-permute-start(bf16[1,64,768]{2,1,0:T(8,128)(2,1)S(1)} %get-tuple-element.37), channel_id=1, source_target_pairs={{0,9},{1,8},{4,13},{5,12},{8,1},{9,0},{12,5},{13,4},{2,11},{3,10},... | collective-permute-start | bytes 294920 | tf_op jit(solution)/shard_map/ppermute | solution.py:332
  32.0 0.0 collective-permute-done.12.refs_0_
  32.0 0.0 collective-permute-start.17
  32.0 0.3 decode.5
  32.3 0.0 collective-permute-done.13.refs_1_
  32.3 9.6 %collective-permute-start.9 = (bf16[2,64,256]{2,1,0:T(8,128)(2,1)S(1)}, bf16[2,64,256]{2,1,0:T(8,128)(2,1)S(1)}, u32[]{:S(2)}, u32[]{:S(2)}) collective-permute-start(bf16[2,64,256]{2,1,0:T(8,128)(2,1)S(1)} %get-tuple-element.29), channel_id=1, source_target_pairs={{0,8},{1,9},{4,12},{5,13},{8,0},{9,1},{12,4},{13,5},{2,10},{3,11},... | collective-permute-start | bytes 196616 | tf_op jit(solution)/shard_map/ppermute | solution.py:332
  41.9 0.0 collective-permute-done.14.refs_2_
  41.9 0.0 collective-permute-start.10
  41.9 0.0 collective-permute-done.15.refs_4_
  41.9 0.4 collective-permute-start.11
  42.3 0.0 collective-permute-done.16.refs_5_
  42.3 0.0 collective-permute-done.17.refs_6_
  42.3 0.9 %add.2.refs_4_ = bf16[2,64,2048]{2,1,0:T(8,128)(2,1)} custom-call(f32[2,2048]{1,0:T(2,128)S(1)} %copy-done.2, bf16[2,64,2048]{2,1,0:T(8,128)(2,1)S(1)} %copy-done.1, bf16[1,64,768]{2,1,0:T(8,128)(2,1)S(1)} %collective-permute-done.12.refs_0_, bf16[1,64,768]{2,1,0:T(8,128)(2,1)S(1)} %collective-permute-done.13.refs_1_, ...), custom_call_target="tpu_custom_call" | custom-call | flops 20000000000 | tf_op jit(solution)/shard_map/add/pallas_call | solution.py:299
  43.2 1.3 %collective-permute-done.9.refs_0_ = bf16[2,64,256]{2,1,0:T(8,128)(2,1)S(1)} collective-permute-done((bf16[2,64,256]{2,1,0:T(8,128)(2,1)S(1)}, bf16[2,64,256]{2,1,0:T(8,128)(2,1)S(1)}, u32[]{:S(2)}, u32[]{:S(2)}) %collective-permute-start.9) | collective-permute-done | bytes 65568 | tf_op jit(solution)/shard_map/ppermute | solution.py:332
  44.5 2.0 %collective-permute-done.10.refs_1_ = bf16[2,64,256]{2,1,0:T(8,128)(2,1)S(1)} collective-permute-done((bf16[2,64,256]{2,1,0:T(8,128)(2,1)S(1)}, bf16[2,64,256]{2,1,0:T(8,128)(2,1)S(1)}, u32[]{:S(2)}, u32[]{:S(2)}) %collective-permute-start.10) | collective-permute-done | bytes 65568 | tf_op jit(solution)/shard_map/ppermute | solution.py:332
  46.5 0.0 collective-permute-done.11.refs_2_
  46.5 0.7 %add.3 = bf16[2,64,2048]{2,1,0:T(8,128)(2,1)} custom-call(f32[2,2048]{1,0:T(2,128)S(1)} %copy-done.2, bf16[2,64,2048]{2,1,0:T(8,128)(2,1)S(1)} %copy-done.1, bf16[2,64,256]{2,1,0:T(8,128)(2,1)S(1)} %collective-permute-done.9.refs_0_, bf16[2,64,256]{2,1,0:T(8,128)(2,1)S(1)} %collective-permute-done.10.refs_1_, ...), custom_call_target="tpu_custom_call", output_to_operand_aliasing={{}: (6, {})} | custom-call | tf_op jit(solution)/shard_map/add/pallas_call | solution.py:299
  (7 shorter events, 0.0 us)
Async XLA Ops:
  0.0 10.0 %copy-start.4 = (s32[2,8]{1,0:T(2,128)S(1)}, s32[2,8]{1,0:T(2,128)}, u32[]{:S(2)}) copy-start(s32[2,8]{1,0:T(2,128)} %active_ref.1) | copy-start | bytes 196
  0.0 10.0 %copy-start.3 = (f32[512]{0:T(512)S(1)}, f32[512]{0:T(512)}, u32[]{:S(2)}) copy-start(f32[512]{0:T(512)} %param.9) | copy-start | bytes 6148
  2.2 3.8 %collective-permute-start = (bf16[128,256]{1,0:T(8,128)(2,1)S(1)}, bf16[128,256]{1,0:T(8,128)(2,1)S(1)}, u32[]{:S(2)}, u32[]{:S(2)}) collective-permute-start(bf16[128,256]{1,0:T(8,128)(2,1)S(1)} %get-tuple-element.23), channel_id=1, source_target_pairs={{0,4},{4,0},{8,12},{12,8},{1,5},{5,1},{9,13},{13,9},{2,6},{6,2},{1... | collective-permute-start | bytes 196616 | tf_op jit(solution)/shard_map/ppermute | solution.py:251
  2.3 5.1 %collective-permute-start.1 = (bf16[128,256]{1,0:T(8,128)(2,1)S(1)}, bf16[128,256]{1,0:T(8,128)(2,1)S(1)}, u32[]{:S(2)}, u32[]{:S(2)}) collective-permute-start(bf16[128,256]{1,0:T(8,128)(2,1)S(1)} %get-tuple-element.24), channel_id=1, source_target_pairs={{0,8},{4,12},{8,0},{12,4},{1,9},{5,13},{9,1},{13,5},{2,10},{6,14},... | collective-permute-start | bytes 196616 | tf_op jit(solution)/shard_map/ppermute | solution.py:251
  4.8 5.3 %collective-permute-start.2 = (bf16[128,256]{1,0:T(8,128)(2,1)S(1)}, bf16[128,256]{1,0:T(8,128)(2,1)S(1)}, u32[]{:S(2)}, u32[]{:S(2)}) collective-permute-start(bf16[128,256]{1,0:T(8,128)(2,1)S(1)} %get-tuple-element.25), channel_id=1, source_target_pairs={{0,12},{4,8},{8,4},{12,0},{1,13},{5,9},{9,5},{13,1},{2,14},{6,10},... | collective-permute-start | bytes 196616 | tf_op jit(solution)/shard_map/ppermute | solution.py:251
  4.9 12.5 %collective-permute-start.7 = (bf16[1,2,128,768]{3,2,1,0:T(8,128)(2,1)S(1)}, bf16[1,2,128,768]{3,2,1,0:T(8,128)(2,1)S(1)}, u32[]{:S(2)}, u32[]{:S(2)}) collective-permute-start(bf16[1,2,128,768]{3,2,1,0:T(8,128)(2,1)S(1)} %get-tuple-element.26.before_ref), channel_id=1, source_target_pairs={{0,4},{4,0},{8,12},{12,8},{1,5},{5,1},{9,13},{13,9},{2,6},{6,2},{1... | collective-permute-start | bytes 1179656 | tf_op jit(solution)/shard_map/ppermute | solution.py:291
  10.7 8.0 %collective-permute-start.5 = (bf16[2,64,256]{2,1,0:T(8,128)(2,1)S(1)}, bf16[2,64,256]{2,1,0:T(8,128)(2,1)S(1)}, u32[]{:S(2)}, u32[]{:S(2)}) collective-permute-start(bf16[2,64,256]{2,1,0:T(8,128)(2,1)S(1)} %codes.1.refs_0_.after_ref), channel_id=1, source_target_pairs={{0,3},{1,2},{2,1},{3,0},{4,7},{5,6},{6,5},{7,4},{8,11},{9,10},{10,... | collective-permute-start | bytes 196616 | tf_op jit(solution)/shard_map/ppermute | solution.py:268
  13.3 5.4 %collective-permute-start.4 = (bf16[2,64,256]{2,1,0:T(8,128)(2,1)S(1)}, bf16[2,64,256]{2,1,0:T(8,128)(2,1)S(1)}, u32[]{:S(2)}, u32[]{:S(2)}) collective-permute-start(bf16[2,64,256]{2,1,0:T(8,128)(2,1)S(1)} %codes.1.refs_0_.after_ref), channel_id=1, source_target_pairs={{0,2},{1,3},{2,0},{3,1},{4,6},{5,7},{6,4},{7,5},{8,10},{9,11},{10,... | collective-permute-start | bytes 196616 | tf_op jit(solution)/shard_map/ppermute | solution.py:268
  13.6 5.1 %collective-permute-start.3 = (bf16[2,64,256]{2,1,0:T(8,128)(2,1)S(1)}, bf16[2,64,256]{2,1,0:T(8,128)(2,1)S(1)}, u32[]{:S(2)}, u32[]{:S(2)}) collective-permute-start(bf16[2,64,256]{2,1,0:T(8,128)(2,1)S(1)} %codes.1.refs_0_.after_ref), channel_id=1, source_target_pairs={{0,1},{1,0},{2,3},{3,2},{4,5},{5,4},{6,7},{7,6},{8,9},{9,8},{10,11... | collective-permute-start | bytes 196616 | tf_op jit(solution)/shard_map/ppermute | solution.py:268
  14.7 4.0 %copy-start = (bf16[2,2,128,2048]{3,2,1,0:T(8,128)(2,1)S(1)}, bf16[2,2,128,2048]{3,2,1,0:T(8,128)(2,1)}, u32[]{:S(2)}) copy-start(bf16[2,2,128,2048]{3,2,1,0:T(8,128)(2,1)} %dec_ref.5) | copy-start | bytes 6291460
  14.8 13.8 %collective-permute-start.6 = (bf16[2,2,128,256]{3,2,1,0:T(8,128)(2,1)S(1)}, bf16[2,2,128,256]{3,2,1,0:T(8,128)(2,1)S(1)}, u32[]{:S(2)}, u32[]{:S(2)}) collective-permute-start(bf16[2,2,128,256]{3,2,1,0:T(8,128)(2,1)S(1)} %part.1), channel_id=1, source_target_pairs={{0,4},{4,0},{8,12},{12,8},{1,5},{5,1},{9,13},{13,9},{2,6},{6,2},{1... | collective-permute-start | bytes 786440 | tf_op jit(solution)/shard_map/ppermute | solution.py:293
  17.5 9.1 %collective-permute-start.8 = (bf16[1,2,128,768]{3,2,1,0:T(8,128)(2,1)S(1)}, bf16[1,2,128,768]{3,2,1,0:T(8,128)(2,1)S(1)}, u32[]{:S(2)}, u32[]{:S(2)}) collective-permute-start(bf16[1,2,128,768]{3,2,1,0:T(8,128)(2,1)S(1)} %collective-permute-done.7.got_ref), channel_id=1, source_target_pairs={{0,16},{16,0},{1,17},{17,1},{2,18},{18,2},{3,19},{19,3},{4,20},{20... | collective-permute-start | bytes 1179656 | tf_op jit(solution)/shard_map/ppermute | solution.py:292
  19.2 12.8 %collective-permute-start.12 = (bf16[1,64,768]{2,1,0:T(8,128)(2,1)S(1)}, bf16[1,64,768]{2,1,0:T(8,128)(2,1)S(1)}, u32[]{:S(2)}, u32[]{:S(2)}) collective-permute-start(bf16[1,64,768]{2,1,0:T(8,128)(2,1)S(1)} %get-tuple-element.33), channel_id=1, source_target_pairs={{0,8},{1,9},{4,12},{5,13},{8,0},{9,1},{12,4},{13,5},{2,10},{3,11},... | collective-permute-start | bytes 294920 | tf_op jit(solution)/shard_map/ppermute | solution.py:332
  21.4 10.9 %collective-permute-start.13 = (bf16[1,64,768]{2,1,0:T(8,128)(2,1)S(1)}, bf16[1,64,768]{2,1,0:T(8,128)(2,1)S(1)}, u32[]{:S(2)}, u32[]{:S(2)}) collective-permute-start(bf16[1,64,768]{2,1,0:T(8,128)(2,1)S(1)} %get-tuple-element.34), channel_id=1, source_target_pairs={{0,9},{1,8},{4,13},{5,12},{8,1},{9,0},{12,5},{13,4},{2,11},{3,10},... | collective-permute-start | bytes 294920 | tf_op jit(solution)/shard_map/ppermute | solution.py:332
  23.7 18.2 %collective-permute-start.14 = (bf16[1,64,768]{2,1,0:T(8,128)(2,1)S(1)}, bf16[1,64,768]{2,1,0:T(8,128)(2,1)S(1)}, u32[]{:S(2)}, u32[]{:S(2)}) collective-permute-start(bf16[1,64,768]{2,1,0:T(8,128)(2,1)S(1)} %get-tuple-element.35), channel_id=1, source_target_pairs={{0,1},{1,0},{4,5},{5,4},{8,9},{9,8},{12,13},{13,12},{2,3},{3,2},{6... | collective-permute-start | bytes 294920 | tf_op jit(solution)/shard_map/ppermute | solution.py:332
  26.9 15.4 %copy-start.1 = (bf16[2,64,2048]{2,1,0:T(8,128)(2,1)S(1)}, bf16[2,64,2048]{2,1,0:T(8,128)(2,1)}, u32[]{:S(2)}) copy-start(bf16[2,64,2048]{2,1,0:T(8,128)(2,1)} %target_ref.3) | copy-start | bytes 1572868
  26.9 15.4 %copy-start.2 = (f32[2,2048]{1,0:T(2,128)S(1)}, f32[2,2048]{1,0:T(2,128)}, u32[]{:S(2)}) copy-start(f32[2,2048]{1,0:T(2,128)} %bias_ref.3) | copy-start | bytes 49156
  26.9 15.0 %collective-permute-start.15 = (bf16[1,64,768]{2,1,0:T(8,128)(2,1)S(1)}, bf16[1,64,768]{2,1,0:T(8,128)(2,1)S(1)}, u32[]{:S(2)}, u32[]{:S(2)}) collective-permute-start(bf16[1,64,768]{2,1,0:T(8,128)(2,1)S(1)} %get-tuple-element.36), channel_id=1, source_target_pairs={{0,8},{1,9},{4,12},{5,13},{8,0},{9,1},{12,4},{13,5},{2,10},{3,11},... | collective-permute-start | bytes 294920 | tf_op jit(solution)/shard_map/ppermute | solution.py:332
  28.6 13.7 %collective-permute-start.16 = (bf16[1,64,768]{2,1,0:T(8,128)(2,1)S(1)}, bf16[1,64,768]{2,1,0:T(8,128)(2,1)S(1)}, u32[]{:S(2)}, u32[]{:S(2)}) collective-permute-start(bf16[1,64,768]{2,1,0:T(8,128)(2,1)S(1)} %get-tuple-element.37), channel_id=1, source_target_pairs={{0,9},{1,8},{4,13},{5,12},{8,1},{9,0},{12,5},{13,4},{2,11},{3,10},... | collective-permute-start | bytes 294920 | tf_op jit(solution)/shard_map/ppermute | solution.py:332
  32.0 10.3 %collective-permute-start.17 = (bf16[1,64,768]{2,1,0:T(8,128)(2,1)S(1)}, bf16[1,64,768]{2,1,0:T(8,128)(2,1)S(1)}, u32[]{:S(2)}, u32[]{:S(2)}) collective-permute-start(bf16[1,64,768]{2,1,0:T(8,128)(2,1)S(1)} %get-tuple-element.38), channel_id=1, source_target_pairs={{0,1},{1,0},{4,5},{5,4},{8,9},{9,8},{12,13},{13,12},{2,3},{3,2},{6... | collective-permute-start | bytes 294920 | tf_op jit(solution)/shard_map/ppermute | solution.py:332
  32.3 12.2 %collective-permute-start.9 = (bf16[2,64,256]{2,1,0:T(8,128)(2,1)S(1)}, bf16[2,64,256]{2,1,0:T(8,128)(2,1)S(1)}, u32[]{:S(2)}, u32[]{:S(2)}) collective-permute-start(bf16[2,64,256]{2,1,0:T(8,128)(2,1)S(1)} %get-tuple-element.29), channel_id=1, source_target_pairs={{0,8},{1,9},{4,12},{5,13},{8,0},{9,1},{12,4},{13,5},{2,10},{3,11},... | collective-permute-start | bytes 196616 | tf_op jit(solution)/shard_map/ppermute | solution.py:332
  41.9 4.6 %collective-permute-start.10 = (bf16[2,64,256]{2,1,0:T(8,128)(2,1)S(1)}, bf16[2,64,256]{2,1,0:T(8,128)(2,1)S(1)}, u32[]{:S(2)}, u32[]{:S(2)}) collective-permute-start(bf16[2,64,256]{2,1,0:T(8,128)(2,1)S(1)} %get-tuple-element.30), channel_id=1, source_target_pairs={{0,9},{1,8},{4,13},{5,12},{8,1},{9,0},{12,5},{13,4},{2,11},{3,10},... | collective-permute-start | bytes 196616 | tf_op jit(solution)/shard_map/ppermute | solution.py:332
  41.9 4.6 %collective-permute-start.11 = (bf16[2,64,256]{2,1,0:T(8,128)(2,1)S(1)}, bf16[2,64,256]{2,1,0:T(8,128)(2,1)S(1)}, u32[]{:S(2)}, u32[]{:S(2)}) collective-permute-start(bf16[2,64,256]{2,1,0:T(8,128)(2,1)S(1)} %get-tuple-element.31), channel_id=1, source_target_pairs={{0,1},{1,0},{4,5},{5,4},{8,9},{9,8},{12,13},{13,12},{2,3},{3,2},{6... | collective-permute-start | bytes 196616 | tf_op jit(solution)/shard_map/ppermute | solution.py:332

commit v24 on v22

--- a/solution.py
+++ b/solution.py
@@ -142,20 +142,23 @@
                     out_ref[rows, columns] = code_refs[2 * k + r][group, :, latents]
 
 
-def decode_kernel(n, piece, dec_ref, lhs_ref, got_ref, *refs):
-    offsets, first, width, _ = piece
+def decode_kernel(n, piece, splits, dec_ref, lhs_ref, *refs):
+    offsets, first, width = piece[:3]
     layers, groups, block, cols = dec_ref.shape
-    out_refs = refs[-2 * (n // 2) :]
-    depth = groups * block
+    got_refs, out_refs = refs[:splits], refs[-2 * (n // 2) :]
+    depth, part = groups * block, width // splits
     share = lhs_ref.shape[0] // len(out_refs)
-    start = pl.multiple_of(lax.axis_index("rep") * (cols // 2) + first, LANES)
     for i, offset in enumerate(offsets):
-        own = dec_ref[layer_of(offset, layers), :, :, pl.ds(start, width)].reshape(depth, width)
-        got = got_ref[i].reshape(depth, width)
-        total = jnp.dot(lhs_ref[:, :depth], own, preferred_element_type=jnp.float32)
-        total += jnp.dot(lhs_ref[:, depth:], got, preferred_element_type=jnp.float32)
-        for j, ref in enumerate(out_refs):
-            ref[i] = total[j * share : (j + 1) * share].astype(ref.dtype)
+        for c, ref in enumerate(got_refs):
+            start = lax.axis_index("rep") * (cols // 2) + first + c * part
+            columns = pl.ds(pl.multiple_of(start, LANES), part)
+            own = dec_ref[layer_of(offset, layers), :, :, columns].reshape(depth, part)
+            got = ref[i].reshape(depth, part)
+            total = jnp.dot(lhs_ref[:, :depth], own, preferred_element_type=jnp.float32)
+            total += jnp.dot(lhs_ref[:, depth:], got, preferred_element_type=jnp.float32)
+            for j, out_ref in enumerate(out_refs):
+                value = total[j * share : (j + 1) * share].astype(out_ref.dtype)
+                out_ref[i, :, c * part : (c + 1) * part] = value
 
 
 def add_kernel(n, pieces, bias_ref, target_ref, *refs):
@@ -197,7 +200,10 @@
     share = rows // n
     half = n // 2
     pieces = cut_pieces(cols // 2)
-    fetched = [piece for piece in pieces if not piece[3]]
+    offsets, first, width, _ = pieces[0]
+    splits = 2 if width % (2 * LANES) == 0 else 1
+    width //= splits
+    fetched = [(offsets, first + c * width, width, False) for c in range(splits)] + [pieces[2]]
     tile_rows = rows // active.shape[0]
     pair = [(i, i ^ 1) for i in range(n)]
     params = pltpu.CompilerParams(vmem_limit_bytes=VMEM_BYTES)
@@ -221,15 +227,15 @@
         return jax.ShapeDtypeStruct(extent, kind)
 
     results = pl.pallas_call(
-        functools.partial(encode_kernel, n, fetched[:1]),
+        functools.partial(encode_kernel, n, fetched[:-1]),
         out_shape=[shape(half * share, 2 * block)] * n
-        + [shape(len(offsets), groups, block, width) for offsets, _, width, _ in fetched[:1]],
+        + [shape(len(offsets), groups, block, width) for offsets, _, width, _ in fetched[:-1]],
         in_specs=[anywhere] * 3,
-        out_specs=[vmem] * (n + 1),
+        out_specs=[vmem] * (n + splits),
         scratch_shapes=[
             pltpu.VMEM((2, half, share, features), jnp.bfloat16),
             pltpu.VMEM(enc_w.shape, jnp.bfloat16),
-            pltpu.SemaphoreType.DMA((1, layers * groups)),
+            pltpu.SemaphoreType.DMA((splits, layers * groups)),
             pltpu.SemaphoreType.DMA((2 * half,)),
             pltpu.SemaphoreType.DMA((8,)),
         ],
@@ -269,8 +275,8 @@
     )(*codes)
 
     part = pl.pallas_call(
-        functools.partial(part_kernel, fetched[1]),
-        out_shape=shape(len(fetched[1][0]), groups, block, fetched[1][2]),
+        functools.partial(part_kernel, fetched[-1]),
+        out_shape=shape(len(fetched[-1][0]), groups, block, fetched[-1][2]),
         in_specs=[anywhere] * 3,
         out_specs=vmem,
         scratch_shapes=[pltpu.SemaphoreType.DMA((layers * groups,))],
@@ -279,9 +285,9 @@
         name="part",
     )(parts[0], dec_w, own)
 
-    got = [lax.ppermute(parts[0], "src", pair)]
-    got.append(lax.ppermute(got[0], "parts", [(0, 1), (1, 0)]))
-    got.append(lax.ppermute(part, "src", pair))
+    got = [[lax.ppermute(value, "src", pair) for value in parts]]
+    got.append([lax.ppermute(value, "parts", [(0, 1), (1, 0)]) for value in got[0]])
+    got.append([lax.ppermute(part, "src", pair)])
 
     def add(some, begun, billions):
         operands = [value for i in some for value in sums[i]]
@@ -308,14 +314,14 @@
         shapes = [shape(len(offsets), share, width)] * (2 * half)
         shapes[0] = shape(len(offsets), share, width, kind=jnp.float32)
         terms = pl.pallas_call(
-            functools.partial(decode_kernel, n, piece),
+            functools.partial(decode_kernel, n, piece, len(got[i])),
             out_shape=shapes,
-            in_specs=[vmem] * 3 + [anywhere] * len(after),
+            in_specs=[vmem] * (2 + len(got[i])) + [anywhere] * len(after),
             out_specs=[vmem] * len(shapes),
             compiler_params=params,
             cost_estimate=weight(0),
             name="decode",
-        )(dec_rows, lhs, got[i], *after)
+        )(dec_rows, lhs, *got[i], *after)
         after = [terms[0]]
         sums.append([])
         for r, j in [(r, j) for r in range(2) for j in range(1, half)] + [(1, 0)]:

time: 47.3 us -> 48.9 us (1.034)
  the two profiles are of different devices: /device:TPU:9 before, /device:TPU:0 now
where the time goes in v24:
time: 48.9 us; the launch traced here: 48.7 us
  waiting for transfers between devices  22.9 us (47%)
  starting transfers between devices  19.1 us (39%)
  Pallas kernels  6.58 us (13%)
    ppermute x9, waiting for transfers between devices, body(): sums[i].append(lax.ppermute(terms[2 * j + r], ('src', 'rep'), perm))  9.91 us
    ppermute x9, starting transfers between devices, body(): sums[i].append(lax.ppermute(terms[2 * j + r], ('src', 'rep'), perm))  7.44 us
    ppermute x2, waiting for transfers between devices, body(): lax.ppermute(value, 'parts', [(0, 1), (1, 0)])  6.68 us
    ppermute x3, starting transfers between devices, body(): lax.ppermute(terms[k], 'src', [(i, peer(i, k, n)) for i in range(n)])  5.67 us
    ppermute x3, waiting for transfers between devices, body(): lax.ppermute(terms[k], 'src', [(i, peer(i, k, n)) for i in range(n)])  4.8 us
    pallas_call x1, Pallas kernels, body(): pl.pallas_call(functools.partial(encode_kernel, n, fetched[:-1]), out_sha...  2.2 us
    ppermute x2, starting transfers between devices, body(): lax.ppermute(value, 'parts', [(0, 1), (1, 0)])  2.03 us
    ppermute x2, starting transfers between devices, body(): got = [[lax.ppermute(value, 'src', pair) for value in parts]]  2.03 us
  transfers between devices with their start and end apart: 20, of which 9 were waited for; matrix products, arithmetic and copies ran while one was open for 0% of the time, Pallas kernels for 8%

profile of v24, /device:TPU:0, one launch (start us, length us, event | category | flops | bytes accessed | tf_op | source)
XLA Modules:
  0.0 48.7 jit_solution(8167380123493808346)
XLA Ops:
  0.0 2.2 %encode.1 = (bf16[128,256]{1,0:T(8,128)(2,1)S(1)}, bf16[128,256]{1,0:T(8,128)(2,1)S(1)}, bf16[128,256]{1,0:T(8,128)(2,1)S(1)}, bf16[128,256]{1,0:T(8,128)(2,1)S(...) custom-call(bf16[2,2,64,1024]{3,2,1,0:T(8,128)(2,1)} %bitcast.3, bf16[1024,512]{1,0:T(8,128)(2,1)} %w_hbm.1, ...), custom_call_target="tpu_custom_call" | custom-call | tf_op jit(solution)/shard_map/encode/pallas_call | solution.py:229
  2.2 3.1 %collective-permute-start = (bf16[128,256]{1,0:T(8,128)(2,1)S(1)}, bf16[128,256]{1,0:T(8,128)(2,1)S(1)}, u32[]{:S(2)}, u32[]{:S(2)}) collective-permute-start(bf16[128,256]{1,0:T(8,128)(2,1)S(1)} %get-tuple-element.24), channel_id=1, source_target_pairs={{0,4},{4,0},{8,12},{12,8},{1,5},{5,1},{9,13},{13,9},{2,6},{6,2},{1... | collective-permute-start | bytes 196616 | tf_op jit(solution)/shard_map/ppermute | solution.py:248
  5.3 2.6 %collective-permute-start.1 = (bf16[128,256]{1,0:T(8,128)(2,1)S(1)}, bf16[128,256]{1,0:T(8,128)(2,1)S(1)}, u32[]{:S(2)}, u32[]{:S(2)}) collective-permute-start(bf16[128,256]{1,0:T(8,128)(2,1)S(1)} %get-tuple-element.25), channel_id=1, source_target_pairs={{0,8},{4,12},{8,0},{12,4},{1,9},{5,13},{9,1},{13,5},{2,10},{6,14},... | collective-permute-start | bytes 196616 | tf_op jit(solution)/shard_map/ppermute | solution.py:248
  7.9 0.0 collective-permute-start.2
  7.9 0.9 %collective-permute-start.9 = (bf16[1,2,128,384]{3,2,1,0:T(8,128)(2,1)S(1)}, bf16[1,2,128,384]{3,2,1,0:T(8,128)(2,1)S(1)}, u32[]{:S(2)}, u32[]{:S(2)}) collective-permute-start(bf16[1,2,128,384]{3,2,1,0:T(8,128)(2,1)S(1)} %get-tuple-element.28), channel_id=1, source_target_pairs={{0,4},{4,0},{8,12},{12,8},{1,5},{5,1},{9,13},{13,9},{2,6},{6,2},{1... | collective-permute-start | bytes 589832 | tf_op jit(solution)/shard_map/ppermute | solution.py:288
  8.8 1.1 %collective-permute-start.7 = (bf16[1,2,128,384]{3,2,1,0:T(8,128)(2,1)S(1)}, bf16[1,2,128,384]{3,2,1,0:T(8,128)(2,1)S(1)}, u32[]{:S(2)}, u32[]{:S(2)}) collective-permute-start(bf16[1,2,128,384]{3,2,1,0:T(8,128)(2,1)S(1)} %get-tuple-element.27.before_ref), channel_id=1, source_target_pairs={{0,4},{4,0},{8,12},{12,8},{1,5},{5,1},{9,13},{13,9},{2,6},{6,2},{1... | collective-permute-start | bytes 589832 | tf_op jit(solution)/shard_map/ppermute | solution.py:288
  9.9 0.0 collective-permute-done.refs_1_
  9.9 2.7 %collective-permute-done.1.refs_2_ = bf16[128,256]{1,0:T(8,128)(2,1)S(1)} collective-permute-done((bf16[128,256]{1,0:T(8,128)(2,1)S(1)}, bf16[128,256]{1,0:T(8,128)(2,1)S(1)}, u32[]{:S(2)}, u32[]{:S(2)}) %collective-permute-start.1) | collective-permute-done | bytes 65568 | tf_op jit(solution)/shard_map/ppermute | solution.py:248
  12.6 2.1 %collective-permute-done.2.refs_3_ = bf16[128,256]{1,0:T(8,128)(2,1)S(1)} collective-permute-done((bf16[128,256]{1,0:T(8,128)(2,1)S(1)}, bf16[128,256]{1,0:T(8,128)(2,1)S(1)}, u32[]{:S(2)}, u32[]{:S(2)}) %collective-permute-start.2) | collective-permute-done | bytes 65568 | tf_op jit(solution)/shard_map/ppermute | solution.py:248
  14.7 0.6 %codes.1.refs_0_.after_ref = bf16[2,64,256]{2,1,0:T(8,128)(2,1)S(1)} custom-call(s32[2,8]{1,0:T(2,128)S(1)} %copy-done.4, f32[4,128]{1,0:T(4,128)S(1)} %bitcast.2, bf16[128,256]{1,0:T(8,128)(2,1)S(1)} %get-tuple-element.23.refs_0_, bf16[128,256]{1,0:T(8,128)(2,1)S(1)} %collective-permute-done.refs_1_, bf16[128,256]{1,0:T(8,128)(2,1)S(1)} %collective-permute-done.1.refs_2_, ...), custom_call_target="tpu_custom_call" | custom-call | flops 20000000000 | tf_op jit(solution)/shard_map/codes/pallas_call | solution.py:250
  15.4 0.1 collective-permute-start.5
  15.4 1.6 %collective-permute-start.4 = (bf16[2,64,256]{2,1,0:T(8,128)(2,1)S(1)}, bf16[2,64,256]{2,1,0:T(8,128)(2,1)S(1)}, u32[]{:S(2)}, u32[]{:S(2)}) collective-permute-start(bf16[2,64,256]{2,1,0:T(8,128)(2,1)S(1)} %codes.1.refs_0_.after_ref), channel_id=1, source_target_pairs={{0,2},{1,3},{2,0},{3,1},{4,6},{5,7},{6,4},{7,5},{8,10},{9,11},{10,... | collective-permute-start | bytes 196616 | tf_op jit(solution)/shard_map/ppermute | solution.py:265
  17.0 0.3 collective-permute-start.3
  17.3 1.0 %part.1 = bf16[2,2,128,256]{3,2,1,0:T(8,128)(2,1)S(1)} custom-call(bf16[1,2,128,384]{3,2,1,0:T(8,128)(2,1)S(1)} %get-tuple-element.27.before_ref, bf16[2,2,128,2048]{3,2,1,0:T(8,128)(2,1)} %dec_ref.5, bf16[2,64,256]{2,1,0:T(8,128)(2,1)S(1)} %codes.1.refs_0_.after_ref), custom_call_target="tpu_custom_call" | custom-call | tf_op jit(solution)/shard_map/part/pallas_call | solution.py:277
  18.3 0.0 copy-start
  18.3 1.5 %collective-permute-done.5.refs_3_ = bf16[2,64,256]{2,1,0:T(8,128)(2,1)S(1)} collective-permute-done((bf16[2,64,256]{2,1,0:T(8,128)(2,1)S(1)}, bf16[2,64,256]{2,1,0:T(8,128)(2,1)S(1)}, u32[]{:S(2)}, u32[]{:S(2)}) %collective-permute-start.5) | collective-permute-done | bytes 65568 | tf_op jit(solution)/shard_map/ppermute | solution.py:265
  19.8 0.0 collective-permute-start.6
  19.8 0.0 collective-permute-done.9.refs_1_
  19.8 1.5 %collective-permute-start.10 = (bf16[1,2,128,384]{3,2,1,0:T(8,128)(2,1)S(1)}, bf16[1,2,128,384]{3,2,1,0:T(8,128)(2,1)S(1)}, u32[]{:S(2)}, u32[]{:S(2)}) collective-permute-start(bf16[1,2,128,384]{3,2,1,0:T(8,128)(2,1)S(1)} %collective-permute-done.9.refs_1_), channel_id=1, source_target_pairs={{0,16},{16,0},{1,17},{17,1},{2,18},{18,2},{3,19},{19,3},{4,20},{20... | collective-permute-start | bytes 589832 | tf_op jit(solution)/shard_map/ppermute | solution.py:289
  21.3 0.0 collective-permute-done.7.refs_0_
  21.3 0.5 %collective-permute-start.8 = (bf16[1,2,128,384]{3,2,1,0:T(8,128)(2,1)S(1)}, bf16[1,2,128,384]{3,2,1,0:T(8,128)(2,1)S(1)}, u32[]{:S(2)}, u32[]{:S(2)}) collective-permute-start(bf16[1,2,128,384]{3,2,1,0:T(8,128)(2,1)S(1)} %collective-permute-done.7.refs_0_), channel_id=1, source_target_pairs={{0,16},{16,0},{1,17},{17,1},{2,18},{18,2},{3,19},{19,3},{4,20},{20... | collective-permute-start | bytes 589832 | tf_op jit(solution)/shard_map/ppermute | solution.py:289
  21.8 0.0 collective-permute-done.4.refs_2_
  21.8 0.0 collective-permute-done.3.refs_1_
  21.9 0.4 decode.3
  22.3 2.0 %collective-permute-start.14 = (bf16[1,64,768]{2,1,0:T(8,128)(2,1)S(1)}, bf16[1,64,768]{2,1,0:T(8,128)(2,1)S(1)}, u32[]{:S(2)}, u32[]{:S(2)}) collective-permute-start(bf16[1,64,768]{2,1,0:T(8,128)(2,1)S(1)} %get-tuple-element.35), channel_id=1, source_target_pairs={{0,8},{1,9},{4,12},{5,13},{8,0},{9,1},{12,4},{13,5},{2,10},{3,11},... | collective-permute-start | bytes 294920 | tf_op jit(solution)/shard_map/ppermute | solution.py:329
  24.3 0.0 collective-permute-start.15
  24.3 3.2 %collective-permute-done.10.refs_1_ = bf16[1,2,128,384]{3,2,1,0:T(8,128)(2,1)S(1)} collective-permute-done((bf16[1,2,128,384]{3,2,1,0:T(8,128)(2,1)S(1)}, bf16[1,2,128,384]{3,2,1,0:T(8,128)(2,1)S(1)}, u32[]{:S(2)}, u32[]{:S(2)}) %collective-permute-start.10) | collective-permute-done | bytes 196640 | tf_op jit(solution)/shard_map/ppermute | solution.py:289
  27.5 0.0 collective-permute-start.16
  27.5 3.5 %collective-permute-done.8.refs_0_ = bf16[1,2,128,384]{3,2,1,0:T(8,128)(2,1)S(1)} collective-permute-done((bf16[1,2,128,384]{3,2,1,0:T(8,128)(2,1)S(1)}, bf16[1,2,128,384]{3,2,1,0:T(8,128)(2,1)S(1)}, u32[]{:S(2)}, u32[]{:S(2)}) %collective-permute-start.8) | collective-permute-done | bytes 196640 | tf_op jit(solution)/shard_map/ppermute | solution.py:289
  31.0 0.4 decode.4
  31.4 0.0 copy-start.1
  31.4 0.0 copy-start.2
  31.5 1.7 %collective-permute-start.17 = (bf16[1,64,768]{2,1,0:T(8,128)(2,1)S(1)}, bf16[1,64,768]{2,1,0:T(8,128)(2,1)S(1)}, u32[]{:S(2)}, u32[]{:S(2)}) collective-permute-start(bf16[1,64,768]{2,1,0:T(8,128)(2,1)S(1)} %get-tuple-element.38), channel_id=1, source_target_pairs={{0,8},{1,9},{4,12},{5,13},{8,0},{9,1},{12,4},{13,5},{2,10},{3,11},... | collective-permute-start | bytes 294920 | tf_op jit(solution)/shard_map/ppermute | solution.py:329
  33.2 0.0 collective-permute-done.14.refs_0_
  33.2 0.0 collective-permute-start.18
  33.2 0.0 collective-permute-done.6.refs_0_
  33.2 1.4 %collective-permute-start.19 = (bf16[1,64,768]{2,1,0:T(8,128)(2,1)S(1)}, bf16[1,64,768]{2,1,0:T(8,128)(2,1)S(1)}, u32[]{:S(2)}, u32[]{:S(2)}) collective-permute-start(bf16[1,64,768]{2,1,0:T(8,128)(2,1)S(1)} %get-tuple-element.40), channel_id=1, source_target_pairs={{0,1},{1,0},{4,5},{5,4},{8,9},{9,8},{12,13},{13,12},{2,3},{3,2},{6... | collective-permute-start | bytes 294920 | tf_op jit(solution)/shard_map/ppermute | solution.py:329
  34.6 0.3 decode.5
  34.9 1.7 %collective-permute-start.11 = (bf16[2,64,256]{2,1,0:T(8,128)(2,1)S(1)}, bf16[2,64,256]{2,1,0:T(8,128)(2,1)S(1)}, u32[]{:S(2)}, u32[]{:S(2)}) collective-permute-start(bf16[2,64,256]{2,1,0:T(8,128)(2,1)S(1)} %get-tuple-element.31), channel_id=1, source_target_pairs={{0,8},{1,9},{4,12},{5,13},{8,0},{9,1},{12,4},{13,5},{2,10},{3,11},... | collective-permute-start | bytes 196616 | tf_op jit(solution)/shard_map/ppermute | solution.py:329
  36.6 0.6 %collective-permute-start.12 = (bf16[2,64,256]{2,1,0:T(8,128)(2,1)S(1)}, bf16[2,64,256]{2,1,0:T(8,128)(2,1)S(1)}, u32[]{:S(2)}, u32[]{:S(2)}) collective-permute-start(bf16[2,64,256]{2,1,0:T(8,128)(2,1)S(1)} %get-tuple-element.32), channel_id=1, source_target_pairs={{0,9},{1,8},{4,13},{5,12},{8,1},{9,0},{12,5},{13,4},{2,11},{3,10},... | collective-permute-start | bytes 196616 | tf_op jit(solution)/shard_map/ppermute | solution.py:329
  37.2 6.8 %collective-permute-done.17.refs_4_ = bf16[1,64,768]{2,1,0:T(8,128)(2,1)S(1)} collective-permute-done((bf16[1,64,768]{2,1,0:T(8,128)(2,1)S(1)}, bf16[1,64,768]{2,1,0:T(8,128)(2,1)S(1)}, u32[]{:S(2)}, u32[]{:S(2)}) %collective-permute-start.17) | collective-permute-done | bytes 98336 | tf_op jit(solution)/shard_map/ppermute | solution.py:329
  44.0 0.0 collective-permute-start.13
  44.0 1.2 %collective-permute-done.18.refs_5_ = bf16[1,64,768]{2,1,0:T(8,128)(2,1)S(1)} collective-permute-done((bf16[1,64,768]{2,1,0:T(8,128)(2,1)S(1)}, bf16[1,64,768]{2,1,0:T(8,128)(2,1)S(1)}, u32[]{:S(2)}, u32[]{:S(2)}) %collective-permute-start.18) | collective-permute-done | bytes 98336 | tf_op jit(solution)/shard_map/ppermute | solution.py:329
  45.2 0.0 collective-permute-done.19.refs_6_
  45.2 0.9 %add.2.refs_4_ = bf16[2,64,2048]{2,1,0:T(8,128)(2,1)} custom-call(f32[2,2048]{1,0:T(2,128)S(1)} %copy-done.2, bf16[2,64,2048]{2,1,0:T(8,128)(2,1)S(1)} %copy-done.1, bf16[1,64,768]{2,1,0:T(8,128)(2,1)S(1)} %collective-permute-done.14.refs_0_, bf16[1,64,768]{2,1,0:T(8,128)(2,1)S(1)} %collective-permute-done.15.refs_1_, ...), custom_call_target="tpu_custom_call" | custom-call | flops 20000000000 | tf_op jit(solution)/shard_map/add/pallas_call | solution.py:296
  46.1 1.4 %collective-permute-done.11.refs_0_ = bf16[2,64,256]{2,1,0:T(8,128)(2,1)S(1)} collective-permute-done((bf16[2,64,256]{2,1,0:T(8,128)(2,1)S(1)}, bf16[2,64,256]{2,1,0:T(8,128)(2,1)S(1)}, u32[]{:S(2)}, u32[]{:S(2)}) %collective-permute-start.11) | collective-permute-done | bytes 65568 | tf_op jit(solution)/shard_map/ppermute | solution.py:329
  47.5 0.5 %collective-permute-done.12.refs_1_ = bf16[2,64,256]{2,1,0:T(8,128)(2,1)S(1)} collective-permute-done((bf16[2,64,256]{2,1,0:T(8,128)(2,1)S(1)}, bf16[2,64,256]{2,1,0:T(8,128)(2,1)S(1)}, u32[]{:S(2)}, u32[]{:S(2)}) %collective-permute-start.12) | collective-permute-done | bytes 65568 | tf_op jit(solution)/shard_map/ppermute | solution.py:329
  48.0 0.7 %add.3 = bf16[2,64,2048]{2,1,0:T(8,128)(2,1)} custom-call(f32[2,2048]{1,0:T(2,128)S(1)} %copy-done.2, bf16[2,64,2048]{2,1,0:T(8,128)(2,1)S(1)} %copy-done.1, bf16[2,64,256]{2,1,0:T(8,128)(2,1)S(1)} %collective-permute-done.11.refs_0_, bf16[2,64,256]{2,1,0:T(8,128)(2,1)S(1)} %collective-permute-done.12.refs_1_, ...), custom_call_target="tpu_custom_call", output_to_operand_aliasing={{}: (6, {})} | custom-call | tf_op jit(solution)/shard_map/add/pallas_call | solution.py:296
  (11 shorter events, 0.1 us)
Async XLA Ops:
  0.0 14.7 %copy-start.4 = (s32[2,8]{1,0:T(2,128)S(1)}, s32[2,8]{1,0:T(2,128)}, u32[]{:S(2)}) copy-start(s32[2,8]{1,0:T(2,128)} %active_ref.1) | copy-start | bytes 196
  0.0 14.7 %copy-start.3 = (f32[512]{0:T(512)S(1)}, f32[512]{0:T(512)}, u32[]{:S(2)}) copy-start(f32[512]{0:T(512)} %param.9) | copy-start | bytes 6148
  2.2 7.7 %collective-permute-start = (bf16[128,256]{1,0:T(8,128)(2,1)S(1)}, bf16[128,256]{1,0:T(8,128)(2,1)S(1)}, u32[]{:S(2)}, u32[]{:S(2)}) collective-permute-start(bf16[128,256]{1,0:T(8,128)(2,1)S(1)} %get-tuple-element.24), channel_id=1, source_target_pairs={{0,4},{4,0},{8,12},{12,8},{1,5},{5,1},{9,13},{13,9},{2,6},{6,2},{1... | collective-permute-start | bytes 196616 | tf_op jit(solution)/shard_map/ppermute | solution.py:248
  5.3 7.3 %collective-permute-start.1 = (bf16[128,256]{1,0:T(8,128)(2,1)S(1)}, bf16[128,256]{1,0:T(8,128)(2,1)S(1)}, u32[]{:S(2)}, u32[]{:S(2)}) collective-permute-start(bf16[128,256]{1,0:T(8,128)(2,1)S(1)} %get-tuple-element.25), channel_id=1, source_target_pairs={{0,8},{4,12},{8,0},{12,4},{1,9},{5,13},{9,1},{13,5},{2,10},{6,14},... | collective-permute-start | bytes 196616 | tf_op jit(solution)/shard_map/ppermute | solution.py:248
  7.9 6.8 %collective-permute-start.2 = (bf16[128,256]{1,0:T(8,128)(2,1)S(1)}, bf16[128,256]{1,0:T(8,128)(2,1)S(1)}, u32[]{:S(2)}, u32[]{:S(2)}) collective-permute-start(bf16[128,256]{1,0:T(8,128)(2,1)S(1)} %get-tuple-element.26), channel_id=1, source_target_pairs={{0,12},{4,8},{8,4},{12,0},{1,13},{5,9},{9,5},{13,1},{2,14},{6,10},... | collective-permute-start | bytes 196616 | tf_op jit(solution)/shard_map/ppermute | solution.py:248
  7.9 11.9 %collective-permute-start.9 = (bf16[1,2,128,384]{3,2,1,0:T(8,128)(2,1)S(1)}, bf16[1,2,128,384]{3,2,1,0:T(8,128)(2,1)S(1)}, u32[]{:S(2)}, u32[]{:S(2)}) collective-permute-start(bf16[1,2,128,384]{3,2,1,0:T(8,128)(2,1)S(1)} %get-tuple-element.28), channel_id=1, source_target_pairs={{0,4},{4,0},{8,12},{12,8},{1,5},{5,1},{9,13},{13,9},{2,6},{6,2},{1... | collective-permute-start | bytes 589832 | tf_op jit(solution)/shard_map/ppermute | solution.py:288
  8.8 12.5 %collective-permute-start.7 = (bf16[1,2,128,384]{3,2,1,0:T(8,128)(2,1)S(1)}, bf16[1,2,128,384]{3,2,1,0:T(8,128)(2,1)S(1)}, u32[]{:S(2)}, u32[]{:S(2)}) collective-permute-start(bf16[1,2,128,384]{3,2,1,0:T(8,128)(2,1)S(1)} %get-tuple-element.27.before_ref), channel_id=1, source_target_pairs={{0,4},{4,0},{8,12},{12,8},{1,5},{5,1},{9,13},{13,9},{2,6},{6,2},{1... | collective-permute-start | bytes 589832 | tf_op jit(solution)/shard_map/ppermute | solution.py:288
  15.4 4.4 %collective-permute-start.5 = (bf16[2,64,256]{2,1,0:T(8,128)(2,1)S(1)}, bf16[2,64,256]{2,1,0:T(8,128)(2,1)S(1)}, u32[]{:S(2)}, u32[]{:S(2)}) collective-permute-start(bf16[2,64,256]{2,1,0:T(8,128)(2,1)S(1)} %codes.1.refs_0_.after_ref), channel_id=1, source_target_pairs={{0,3},{1,2},{2,1},{3,0},{4,7},{5,6},{6,5},{7,4},{8,11},{9,10},{10,... | collective-permute-start | bytes 196616 | tf_op jit(solution)/shard_map/ppermute | solution.py:265
  15.4 6.4 %collective-permute-start.4 = (bf16[2,64,256]{2,1,0:T(8,128)(2,1)S(1)}, bf16[2,64,256]{2,1,0:T(8,128)(2,1)S(1)}, u32[]{:S(2)}, u32[]{:S(2)}) collective-permute-start(bf16[2,64,256]{2,1,0:T(8,128)(2,1)S(1)} %codes.1.refs_0_.after_ref), channel_id=1, source_target_pairs={{0,2},{1,3},{2,0},{3,1},{4,6},{5,7},{6,4},{7,5},{8,10},{9,11},{10,... | collective-permute-start | bytes 196616 | tf_op jit(solution)/shard_map/ppermute | solution.py:265
  17.0 4.8 %collective-permute-start.3 = (bf16[2,64,256]{2,1,0:T(8,128)(2,1)S(1)}, bf16[2,64,256]{2,1,0:T(8,128)(2,1)S(1)}, u32[]{:S(2)}, u32[]{:S(2)}) collective-permute-start(bf16[2,64,256]{2,1,0:T(8,128)(2,1)S(1)} %codes.1.refs_0_.after_ref), channel_id=1, source_target_pairs={{0,1},{1,0},{2,3},{3,2},{4,5},{5,4},{6,7},{7,6},{8,9},{9,8},{10,11... | collective-permute-start | bytes 196616 | tf_op jit(solution)/shard_map/ppermute | solution.py:265
  18.3 3.6 %copy-start = (bf16[2,2,128,2048]{3,2,1,0:T(8,128)(2,1)S(1)}, bf16[2,2,128,2048]{3,2,1,0:T(8,128)(2,1)}, u32[]{:S(2)}) copy-start(bf16[2,2,128,2048]{3,2,1,0:T(8,128)(2,1)} %dec_ref.5) | copy-start | bytes 6291460
  19.8 13.5 %collective-permute-start.6 = (bf16[2,2,128,256]{3,2,1,0:T(8,128)(2,1)S(1)}, bf16[2,2,128,256]{3,2,1,0:T(8,128)(2,1)S(1)}, u32[]{:S(2)}, u32[]{:S(2)}) collective-permute-start(bf16[2,2,128,256]{3,2,1,0:T(8,128)(2,1)S(1)} %part.1), channel_id=1, source_target_pairs={{0,4},{4,0},{8,12},{12,8},{1,5},{5,1},{9,13},{13,9},{2,6},{6,2},{1... | collective-permute-start | bytes 786440 | tf_op jit(solution)/shard_map/ppermute | solution.py:290
  19.8 7.7 %collective-permute-start.10 = (bf16[1,2,128,384]{3,2,1,0:T(8,128)(2,1)S(1)}, bf16[1,2,128,384]{3,2,1,0:T(8,128)(2,1)S(1)}, u32[]{:S(2)}, u32[]{:S(2)}) collective-permute-start(bf16[1,2,128,384]{3,2,1,0:T(8,128)(2,1)S(1)} %collective-permute-done.9.refs_1_), channel_id=1, source_target_pairs={{0,16},{16,0},{1,17},{17,1},{2,18},{18,2},{3,19},{19,3},{4,20},{20... | collective-permute-start | bytes 589832 | tf_op jit(solution)/shard_map/ppermute | solution.py:289
  21.3 9.7 %collective-permute-start.8 = (bf16[1,2,128,384]{3,2,1,0:T(8,128)(2,1)S(1)}, bf16[1,2,128,384]{3,2,1,0:T(8,128)(2,1)S(1)}, u32[]{:S(2)}, u32[]{:S(2)}) collective-permute-start(bf16[1,2,128,384]{3,2,1,0:T(8,128)(2,1)S(1)} %collective-permute-done.7.refs_0_), channel_id=1, source_target_pairs={{0,16},{16,0},{1,17},{17,1},{2,18},{18,2},{3,19},{19,3},{4,20},{20... | collective-permute-start | bytes 589832 | tf_op jit(solution)/shard_map/ppermute | solution.py:289
  22.3 10.9 %collective-permute-start.14 = (bf16[1,64,768]{2,1,0:T(8,128)(2,1)S(1)}, bf16[1,64,768]{2,1,0:T(8,128)(2,1)S(1)}, u32[]{:S(2)}, u32[]{:S(2)}) collective-permute-start(bf16[1,64,768]{2,1,0:T(8,128)(2,1)S(1)} %get-tuple-element.35), channel_id=1, source_target_pairs={{0,8},{1,9},{4,12},{5,13},{8,0},{9,1},{12,4},{13,5},{2,10},{3,11},... | collective-permute-start | bytes 294920 | tf_op jit(solution)/shard_map/ppermute | solution.py:329
  24.3 10.6 %collective-permute-start.15 = (bf16[1,64,768]{2,1,0:T(8,128)(2,1)S(1)}, bf16[1,64,768]{2,1,0:T(8,128)(2,1)S(1)}, u32[]{:S(2)}, u32[]{:S(2)}) collective-permute-start(bf16[1,64,768]{2,1,0:T(8,128)(2,1)S(1)} %get-tuple-element.36), channel_id=1, source_target_pairs={{0,9},{1,8},{4,13},{5,12},{8,1},{9,0},{12,5},{13,4},{2,11},{3,10},... | collective-permute-start | bytes 294920 | tf_op jit(solution)/shard_map/ppermute | solution.py:329
  27.5 9.1 %collective-permute-start.16 = (bf16[1,64,768]{2,1,0:T(8,128)(2,1)S(1)}, bf16[1,64,768]{2,1,0:T(8,128)(2,1)S(1)}, u32[]{:S(2)}, u32[]{:S(2)}) collective-permute-start(bf16[1,64,768]{2,1,0:T(8,128)(2,1)S(1)} %get-tuple-element.37), channel_id=1, source_target_pairs={{0,1},{1,0},{4,5},{5,4},{8,9},{9,8},{12,13},{13,12},{2,3},{3,2},{6... | collective-permute-start | bytes 294920 | tf_op jit(solution)/shard_map/ppermute | solution.py:329
  31.4 13.8 %copy-start.1 = (bf16[2,64,2048]{2,1,0:T(8,128)(2,1)S(1)}, bf16[2,64,2048]{2,1,0:T(8,128)(2,1)}, u32[]{:S(2)}) copy-start(bf16[2,64,2048]{2,1,0:T(8,128)(2,1)} %target_ref.3) | copy-start | bytes 1572868
  31.4 13.7 %copy-start.2 = (f32[2,2048]{1,0:T(2,128)S(1)}, f32[2,2048]{1,0:T(2,128)}, u32[]{:S(2)}) copy-start(f32[2,2048]{1,0:T(2,128)} %bias_ref.3) | copy-start | bytes 49156
  31.5 12.5 %collective-permute-start.17 = (bf16[1,64,768]{2,1,0:T(8,128)(2,1)S(1)}, bf16[1,64,768]{2,1,0:T(8,128)(2,1)S(1)}, u32[]{:S(2)}, u32[]{:S(2)}) collective-permute-start(bf16[1,64,768]{2,1,0:T(8,128)(2,1)S(1)} %get-tuple-element.38), channel_id=1, source_target_pairs={{0,8},{1,9},{4,12},{5,13},{8,0},{9,1},{12,4},{13,5},{2,10},{3,11},... | collective-permute-start | bytes 294920 | tf_op jit(solution)/shard_map/ppermute | solution.py:329
  33.2 12.0 %collective-permute-start.18 = (bf16[1,64,768]{2,1,0:T(8,128)(2,1)S(1)}, bf16[1,64,768]{2,1,0:T(8,128)(2,1)S(1)}, u32[]{:S(2)}, u32[]{:S(2)}) collective-permute-start(bf16[1,64,768]{2,1,0:T(8,128)(2,1)S(1)} %get-tuple-element.39), channel_id=1, source_target_pairs={{0,9},{1,8},{4,13},{5,12},{8,1},{9,0},{12,5},{13,4},{2,11},{3,10},... | collective-permute-start | bytes 294920 | tf_op jit(solution)/shard_map/ppermute | solution.py:329
  33.2 12.0 %collective-permute-start.19 = (bf16[1,64,768]{2,1,0:T(8,128)(2,1)S(1)}, bf16[1,64,768]{2,1,0:T(8,128)(2,1)S(1)}, u32[]{:S(2)}, u32[]{:S(2)}) collective-permute-start(bf16[1,64,768]{2,1,0:T(8,128)(2,1)S(1)} %get-tuple-element.40), channel_id=1, source_target_pairs={{0,1},{1,0},{4,5},{5,4},{8,9},{9,8},{12,13},{13,12},{2,3},{3,2},{6... | collective-permute-start | bytes 294920 | tf_op jit(solution)/shard_map/ppermute | solution.py:329
  34.9 12.6 %collective-permute-start.11 = (bf16[2,64,256]{2,1,0:T(8,128)(2,1)S(1)}, bf16[2,64,256]{2,1,0:T(8,128)(2,1)S(1)}, u32[]{:S(2)}, u32[]{:S(2)}) collective-permute-start(bf16[2,64,256]{2,1,0:T(8,128)(2,1)S(1)} %get-tuple-element.31), channel_id=1, source_target_pairs={{0,8},{1,9},{4,12},{5,13},{8,0},{9,1},{12,4},{13,5},{2,10},{3,11},... | collective-permute-start | bytes 196616 | tf_op jit(solution)/shard_map/ppermute | solution.py:329
  36.6 11.3 %collective-permute-start.12 = (bf16[2,64,256]{2,1,0:T(8,128)(2,1)S(1)}, bf16[2,64,256]{2,1,0:T(8,128)(2,1)S(1)}, u32[]{:S(2)}, u32[]{:S(2)}) collective-permute-start(bf16[2,64,256]{2,1,0:T(8,128)(2,1)S(1)} %get-tuple-element.32), channel_id=1, source_target_pairs={{0,9},{1,8},{4,13},{5,12},{8,1},{9,0},{12,5},{13,4},{2,11},{3,10},... | collective-permute-start | bytes 196616 | tf_op jit(solution)/shard_map/ppermute | solution.py:329
  44.0 4.0 %collective-permute-start.13 = (bf16[2,64,256]{2,1,0:T(8,128)(2,1)S(1)}, bf16[2,64,256]{2,1,0:T(8,128)(2,1)S(1)}, u32[]{:S(2)}, u32[]{:S(2)}) collective-permute-start(bf16[2,64,256]{2,1,0:T(8,128)(2,1)S(1)} %get-tuple-element.33), channel_id=1, source_target_pairs={{0,1},{1,0},{4,5},{5,4},{8,9},{9,8},{12,13},{13,12},{2,3},{3,2},{6... | collective-permute-start | bytes 196616 | tf_op jit(solution)/shard_map/ppermute | solution.py:329

commit v25 on v22

--- a/solution.py
+++ b/solution.py
@@ -9,7 +9,7 @@
 
 VMEM_BYTES = 32 * 1024 * 1024
 LANES = 128
-FIRST = 6
+FIRST = 5
 PIECES = (((0,), 0, False), ((1,), 0, True), ((0, 1), 1, False))
 
 

time: 47.3 us -> 49.6 us (1.049)
  the two profiles are of different devices: /device:TPU:9 before, /device:TPU:0 now
where the time goes in v25:
time: 49.6 us; the launch traced here: 49.4 us
  waiting for transfers between devices  23.5 us (47%)
  starting transfers between devices  19.2 us (39%)
  Pallas kernels  6.56 us (13%)
    ppermute x9, waiting for transfers between devices, body(): sums[i].append(lax.ppermute(terms[2 * j + r], ('src', 'rep'), perm))  11.4 us
    ppermute x9, starting transfers between devices, body(): sums[i].append(lax.ppermute(terms[2 * j + r], ('src', 'rep'), perm))  9.11 us
    ppermute x3, waiting for transfers between devices, body(): lax.ppermute(terms[k], 'src', [(i, peer(i, k, n)) for i in range(n)])  5.92 us
    ppermute x3, starting transfers between devices, body(): lax.ppermute(terms[k], 'src', [(i, peer(i, k, n)) for i in range(n)])  5.66 us
    ppermute x1, waiting for transfers between devices, body(): got.append(lax.ppermute(got[0], 'parts', [(0, 1), (1, 0)]))  3.6 us
    pallas_call x1, Pallas kernels, body(): pl.pallas_call(functools.partial(encode_kernel, n, fetched[:1]), out_shap...  2.08 us
    ppermute x3, starting transfers between devices, body(): codes.append(lax.ppermute(own, ('tgt', 'rep'), perm) if k + r else own)  1.92 us
    pallas_call x2, Pallas kernels, add(): pl.pallas_call(functools.partial(add_kernel, n, [pieces[i] for i in some]...  1.58 us
  transfers between devices with their start and end apart: 18, of which 10 were waited for; matrix products, arithmetic and copies ran while one was open for 0% of the time, Pallas kernels for 8%

profile of v25, /device:TPU:0, one launch (start us, length us, event | category | flops | bytes accessed | tf_op | source)
XLA Modules:
  0.0 49.4 jit_solution(52174170381327457)
XLA Ops:
  0.0 2.1 %encode.1 = (bf16[128,256]{1,0:T(8,128)(2,1)S(1)}, bf16[128,256]{1,0:T(8,128)(2,1)S(1)}, bf16[128,256]{1,0:T(8,128)(2,1)S(1)}, bf16[128,256]{1,0:T(8,128)(2,1)S(1)}, bf16[1,2,128,640]{3,2,1,0:T(8,128)(2,1)S(1)}) custom-call(bf16[2,2,64,1024]{3,2,1,0:T(8,128)(2,1)} %bitcast.3, bf16[1024,512]{1,0:T(8,128)(2,1)} %w_hbm.1, bf16[2,2,128,2048]{3,2,1,0:T(8,128)(2,1)} %dec_ref.5), custom_call_target="tpu_custom_call" | custom-call | tf_op jit(solution)/shard_map/encode/pallas_call | solution.py:223
  2.1 3.1 %collective-permute-start = (bf16[128,256]{1,0:T(8,128)(2,1)S(1)}, bf16[128,256]{1,0:T(8,128)(2,1)S(1)}, u32[]{:S(2)}, u32[]{:S(2)}) collective-permute-start(bf16[128,256]{1,0:T(8,128)(2,1)S(1)} %get-tuple-element.23), channel_id=1, source_target_pairs={{0,4},{4,0},{8,12},{12,8},{1,5},{5,1},{9,13},{13,9},{2,6},{6,2},{1... | collective-permute-start | bytes 196616 | tf_op jit(solution)/shard_map/ppermute | solution.py:242
  5.2 2.6 %collective-permute-start.1 = (bf16[128,256]{1,0:T(8,128)(2,1)S(1)}, bf16[128,256]{1,0:T(8,128)(2,1)S(1)}, u32[]{:S(2)}, u32[]{:S(2)}) collective-permute-start(bf16[128,256]{1,0:T(8,128)(2,1)S(1)} %get-tuple-element.24), channel_id=1, source_target_pairs={{0,8},{4,12},{8,0},{12,4},{1,9},{5,13},{9,1},{13,5},{2,10},{6,14},... | collective-permute-start | bytes 196616 | tf_op jit(solution)/shard_map/ppermute | solution.py:242
  7.7 0.0 collective-permute-start.2
  7.8 0.9 %collective-permute-start.7 = (bf16[1,2,128,640]{3,2,1,0:T(8,128)(2,1)S(1)}, bf16[1,2,128,640]{3,2,1,0:T(8,128)(2,1)S(1)}, u32[]{:S(2)}, u32[]{:S(2)}) collective-permute-start(bf16[1,2,128,640]{3,2,1,0:T(8,128)(2,1)S(1)} %get-tuple-element.26.before_ref), channel_id=1, source_target_pairs={{0,4},{4,0},{8,12},{12,8},{1,5},{5,1},{9,13},{13,9},{2,6},{6,2},{1... | collective-permute-start | bytes 983048 | tf_op jit(solution)/shard_map/ppermute | solution.py:282
  8.7 0.0 collective-permute-done.refs_1_
  8.7 3.8 %collective-permute-done.1.refs_2_ = bf16[128,256]{1,0:T(8,128)(2,1)S(1)} collective-permute-done((bf16[128,256]{1,0:T(8,128)(2,1)S(1)}, bf16[128,256]{1,0:T(8,128)(2,1)S(1)}, u32[]{:S(2)}, u32[]{:S(2)}) %collective-permute-start.1) | collective-permute-done | bytes 65568 | tf_op jit(solution)/shard_map/ppermute | solution.py:242
  12.5 2.1 %collective-permute-done.2.refs_3_ = bf16[128,256]{1,0:T(8,128)(2,1)S(1)} collective-permute-done((bf16[128,256]{1,0:T(8,128)(2,1)S(1)}, bf16[128,256]{1,0:T(8,128)(2,1)S(1)}, u32[]{:S(2)}, u32[]{:S(2)}) %collective-permute-start.2) | collective-permute-done | bytes 65568 | tf_op jit(solution)/shard_map/ppermute | solution.py:242
  14.6 0.6 %codes.1.refs_0_.after_ref = bf16[2,64,256]{2,1,0:T(8,128)(2,1)S(1)} custom-call(s32[2,8]{1,0:T(2,128)S(1)} %copy-done.4, f32[4,128]{1,0:T(4,128)S(1)} %bitcast.2, bf16[128,256]{1,0:T(8,128)(2,1)S(1)} %get-tuple-element.22.refs_0_, bf16[128,256]{1,0:T(8,128)(2,1)S(1)} %collective-permute-done.refs_1_, bf16[128,256]{1,0:T(8,128)(2,1)S(1)} %collective-permute-done.1.refs_2_, ...), custom_call_target="tpu_custom_call" | custom-call | flops 20000000000 | tf_op jit(solution)/shard_map/codes/pallas_call | solution.py:244
  15.2 0.1 collective-permute-start.5
  15.3 1.6 %collective-permute-start.4 = (bf16[2,64,256]{2,1,0:T(8,128)(2,1)S(1)}, bf16[2,64,256]{2,1,0:T(8,128)(2,1)S(1)}, u32[]{:S(2)}, u32[]{:S(2)}) collective-permute-start(bf16[2,64,256]{2,1,0:T(8,128)(2,1)S(1)} %codes.1.refs_0_.after_ref), channel_id=1, source_target_pairs={{0,2},{1,3},{2,0},{3,1},{4,6},{5,7},{6,4},{7,5},{8,10},{9,11},{10,... | collective-permute-start | bytes 196616 | tf_op jit(solution)/shard_map/ppermute | solution.py:259
  16.9 0.3 collective-permute-start.3
  17.1 1.1 %part.1 = bf16[2,2,128,384]{3,2,1,0:T(8,128)(2,1)S(1)} custom-call(bf16[1,2,128,640]{3,2,1,0:T(8,128)(2,1)S(1)} %get-tuple-element.26.before_ref, bf16[2,2,128,2048]{3,2,1,0:T(8,128)(2,1)} %dec_ref.5, bf16[2,64,256]{2,1,0:T(8,128)(2,1)S(1)} %codes.1.refs_0_.after_ref), custom_call_target="tpu_custom_call" | custom-call | tf_op jit(solution)/shard_map/part/pallas_call | solution.py:271
  18.2 0.0 copy-start
  18.2 0.1 collective-permute-start.6
  18.3 0.4 collective-permute-done.7.got_ref
  18.8 1.5 %collective-permute-start.8 = (bf16[1,2,128,640]{3,2,1,0:T(8,128)(2,1)S(1)}, bf16[1,2,128,640]{3,2,1,0:T(8,128)(2,1)S(1)}, u32[]{:S(2)}, u32[]{:S(2)}) collective-permute-start(bf16[1,2,128,640]{3,2,1,0:T(8,128)(2,1)S(1)} %collective-permute-done.7.got_ref), channel_id=1, source_target_pairs={{0,16},{16,0},{1,17},{17,1},{2,18},{18,2},{3,19},{19,3},{4,20},{20... | collective-permute-start | bytes 983048 | tf_op jit(solution)/shard_map/ppermute | solution.py:283
  20.3 0.0 collective-permute-done.5.refs_3_
  20.3 0.8 %collective-permute-done.4.refs_2_ = bf16[2,64,256]{2,1,0:T(8,128)(2,1)S(1)} collective-permute-done((bf16[2,64,256]{2,1,0:T(8,128)(2,1)S(1)}, bf16[2,64,256]{2,1,0:T(8,128)(2,1)S(1)}, u32[]{:S(2)}, u32[]{:S(2)}) %collective-permute-start.4) | collective-permute-done | bytes 65568 | tf_op jit(solution)/shard_map/ppermute | solution.py:259
  21.1 0.0 collective-permute-done.3.refs_1_
  21.1 0.0 copy-done
  21.1 0.4 decode.3
  21.5 0.9 %collective-permute-start.12 = (bf16[1,64,640]{2,1,0:T(8,128)(2,1)S(1)}, bf16[1,64,640]{2,1,0:T(8,128)(2,1)S(1)}, u32[]{:S(2)}, u32[]{:S(2)}) collective-permute-start(bf16[1,64,640]{2,1,0:T(8,128)(2,1)S(1)} %get-tuple-element.33), channel_id=1, source_target_pairs={{0,8},{1,9},{4,12},{5,13},{8,0},{9,1},{12,4},{13,5},{2,10},{3,11},... | collective-permute-start | bytes 245768 | tf_op jit(solution)/shard_map/ppermute | solution.py:323
  22.5 1.4 %collective-permute-start.13 = (bf16[1,64,640]{2,1,0:T(8,128)(2,1)S(1)}, bf16[1,64,640]{2,1,0:T(8,128)(2,1)S(1)}, u32[]{:S(2)}, u32[]{:S(2)}) collective-permute-start(bf16[1,64,640]{2,1,0:T(8,128)(2,1)S(1)} %get-tuple-element.34), channel_id=1, source_target_pairs={{0,9},{1,8},{4,13},{5,12},{8,1},{9,0},{12,5},{13,4},{2,11},{3,10},... | collective-permute-start | bytes 245768 | tf_op jit(solution)/shard_map/ppermute | solution.py:323
  23.9 0.7 %collective-permute-start.14 = (bf16[1,64,640]{2,1,0:T(8,128)(2,1)S(1)}, bf16[1,64,640]{2,1,0:T(8,128)(2,1)S(1)}, u32[]{:S(2)}, u32[]{:S(2)}) collective-permute-start(bf16[1,64,640]{2,1,0:T(8,128)(2,1)S(1)} %get-tuple-element.35), channel_id=1, source_target_pairs={{0,1},{1,0},{4,5},{5,4},{8,9},{9,8},{12,13},{13,12},{2,3},{3,2},{6... | collective-permute-start | bytes 245768 | tf_op jit(solution)/shard_map/ppermute | solution.py:323
  24.6 3.6 %collective-permute-done.8.got_ref = bf16[1,2,128,640]{3,2,1,0:T(8,128)(2,1)S(1)} collective-permute-done((bf16[1,2,128,640]{3,2,1,0:T(8,128)(2,1)S(1)}, bf16[1,2,128,640]{3,2,1,0:T(8,128)(2,1)S(1)}, u32[]{:S(2)}, u32[]{:S(2)}) %collective-permute-start.8) | collective-permute-done | bytes 327712 | tf_op jit(solution)/shard_map/ppermute | solution.py:283
  28.2 0.4 decode.4
  28.6 0.0 copy-start.1
  28.6 0.0 copy-start.2
  28.6 1.7 %collective-permute-start.15 = (bf16[1,64,640]{2,1,0:T(8,128)(2,1)S(1)}, bf16[1,64,640]{2,1,0:T(8,128)(2,1)S(1)}, u32[]{:S(2)}, u32[]{:S(2)}) collective-permute-start(bf16[1,64,640]{2,1,0:T(8,128)(2,1)S(1)} %get-tuple-element.36), channel_id=1, source_target_pairs={{0,8},{1,9},{4,12},{5,13},{8,0},{9,1},{12,4},{13,5},{2,10},{3,11},... | collective-permute-start | bytes 245768 | tf_op jit(solution)/shard_map/ppermute | solution.py:323
  30.3 0.0 collective-permute-done.12.refs_0_
  30.3 1.5 %collective-permute-start.16 = (bf16[1,64,640]{2,1,0:T(8,128)(2,1)S(1)}, bf16[1,64,640]{2,1,0:T(8,128)(2,1)S(1)}, u32[]{:S(2)}, u32[]{:S(2)}) collective-permute-start(bf16[1,64,640]{2,1,0:T(8,128)(2,1)S(1)} %get-tuple-element.37), channel_id=1, source_target_pairs={{0,9},{1,8},{4,13},{5,12},{8,1},{9,0},{12,5},{13,4},{2,11},{3,10},... | collective-permute-start | bytes 245768 | tf_op jit(solution)/shard_map/ppermute | solution.py:323
  31.8 1.3 %collective-permute-done.6.got_ref = bf16[2,2,128,384]{3,2,1,0:T(8,128)(2,1)S(1)} collective-permute-done((bf16[2,2,128,384]{3,2,1,0:T(8,128)(2,1)S(1)}, bf16[2,2,128,384]{3,2,1,0:T(8,128)(2,1)S(1)}, u32[]{:S(2)}, u32[]{:S(2)}) %collective-permute-start.6) | collective-permute-done | bytes 393248 | tf_op jit(solution)/shard_map/ppermute | solution.py:284
  33.2 0.0 collective-permute-start.17
  33.2 0.4 decode.5
  33.6 0.0 collective-permute-done.13.refs_1_
  33.6 0.3 collective-permute-start.9
  33.9 0.0 collective-permute-done.14.refs_2_
  33.9 2.5 %collective-permute-start.10 = (bf16[2,64,384]{2,1,0:T(8,128)(2,1)S(1)}, bf16[2,64,384]{2,1,0:T(8,128)(2,1)S(1)}, u32[]{:S(2)}, u32[]{:S(2)}) collective-permute-start(bf16[2,64,384]{2,1,0:T(8,128)(2,1)S(1)} %get-tuple-element.30), channel_id=1, source_target_pairs={{0,9},{1,8},{4,13},{5,12},{8,1},{9,0},{12,5},{13,4},{2,11},{3,10},... | collective-permute-start | bytes 294920 | tf_op jit(solution)/shard_map/ppermute | solution.py:323
  36.4 6.5 %collective-permute-done.15.refs_4_ = bf16[1,64,640]{2,1,0:T(8,128)(2,1)S(1)} collective-permute-done((bf16[1,64,640]{2,1,0:T(8,128)(2,1)S(1)}, bf16[1,64,640]{2,1,0:T(8,128)(2,1)S(1)}, u32[]{:S(2)}, u32[]{:S(2)}) %collective-permute-start.15) | collective-permute-done | bytes 81952 | tf_op jit(solution)/shard_map/ppermute | solution.py:323
  42.9 0.0 collective-permute-start.11
  42.9 1.6 %collective-permute-done.16.refs_5_ = bf16[1,64,640]{2,1,0:T(8,128)(2,1)S(1)} collective-permute-done((bf16[1,64,640]{2,1,0:T(8,128)(2,1)S(1)}, bf16[1,64,640]{2,1,0:T(8,128)(2,1)S(1)}, u32[]{:S(2)}, u32[]{:S(2)}) %collective-permute-start.16) | collective-permute-done | bytes 81952 | tf_op jit(solution)/shard_map/ppermute | solution.py:323
  44.4 0.0 collective-permute-done.17.refs_6_
  44.5 0.8 %add.2.refs_4_ = bf16[2,64,2048]{2,1,0:T(8,128)(2,1)} custom-call(f32[2,2048]{1,0:T(2,128)S(1)} %copy-done.2, bf16[2,64,2048]{2,1,0:T(8,128)(2,1)S(1)} %copy-done.1, bf16[1,64,640]{2,1,0:T(8,128)(2,1)S(1)} %collective-permute-done.12.refs_0_, bf16[1,64,640]{2,1,0:T(8,128)(2,1)S(1)} %collective-permute-done.13.refs_1_, ...), custom_call_target="tpu_custom_call" | custom-call | flops 20000000000 | tf_op jit(solution)/shard_map/add/pallas_call | solution.py:290
  45.3 1.5 %collective-permute-done.9.refs_0_ = bf16[2,64,384]{2,1,0:T(8,128)(2,1)S(1)} collective-permute-done((bf16[2,64,384]{2,1,0:T(8,128)(2,1)S(1)}, bf16[2,64,384]{2,1,0:T(8,128)(2,1)S(1)}, u32[]{:S(2)}, u32[]{:S(2)}) %collective-permute-start.9) | collective-permute-done | bytes 98336 | tf_op jit(solution)/shard_map/ppermute | solution.py:323
  46.7 1.9 %collective-permute-done.10.refs_1_ = bf16[2,64,384]{2,1,0:T(8,128)(2,1)S(1)} collective-permute-done((bf16[2,64,384]{2,1,0:T(8,128)(2,1)S(1)}, bf16[2,64,384]{2,1,0:T(8,128)(2,1)S(1)}, u32[]{:S(2)}, u32[]{:S(2)}) %collective-permute-start.10) | collective-permute-done | bytes 98336 | tf_op jit(solution)/shard_map/ppermute | solution.py:323
  48.7 0.0 collective-permute-done.11.refs_2_
  48.7 0.8 %add.3 = bf16[2,64,2048]{2,1,0:T(8,128)(2,1)} custom-call(f32[2,2048]{1,0:T(2,128)S(1)} %copy-done.2, bf16[2,64,2048]{2,1,0:T(8,128)(2,1)S(1)} %copy-done.1, bf16[2,64,384]{2,1,0:T(8,128)(2,1)S(1)} %collective-permute-done.9.refs_0_, bf16[2,64,384]{2,1,0:T(8,128)(2,1)S(1)} %collective-permute-done.10.refs_1_, ...), custom_call_target="tpu_custom_call", output_to_operand_aliasing={{}: (6, {})} | custom-call | tf_op jit(solution)/shard_map/add/pallas_call | solution.py:290
  (7 shorter events, 0.1 us)
Async XLA Ops:
  0.0 14.6 %copy-start.4 = (s32[2,8]{1,0:T(2,128)S(1)}, s32[2,8]{1,0:T(2,128)}, u32[]{:S(2)}) copy-start(s32[2,8]{1,0:T(2,128)} %active_ref.1) | copy-start | bytes 196
  0.0 14.6 %copy-start.3 = (f32[512]{0:T(512)S(1)}, f32[512]{0:T(512)}, u32[]{:S(2)}) copy-start(f32[512]{0:T(512)} %param.9) | copy-start | bytes 6148
  2.1 6.6 %collective-permute-start = (bf16[128,256]{1,0:T(8,128)(2,1)S(1)}, bf16[128,256]{1,0:T(8,128)(2,1)S(1)}, u32[]{:S(2)}, u32[]{:S(2)}) collective-permute-start(bf16[128,256]{1,0:T(8,128)(2,1)S(1)} %get-tuple-element.23), channel_id=1, source_target_pairs={{0,4},{4,0},{8,12},{12,8},{1,5},{5,1},{9,13},{13,9},{2,6},{6,2},{1... | collective-permute-start | bytes 196616 | tf_op jit(solution)/shard_map/ppermute | solution.py:242
  5.2 7.3 %collective-permute-start.1 = (bf16[128,256]{1,0:T(8,128)(2,1)S(1)}, bf16[128,256]{1,0:T(8,128)(2,1)S(1)}, u32[]{:S(2)}, u32[]{:S(2)}) collective-permute-start(bf16[128,256]{1,0:T(8,128)(2,1)S(1)} %get-tuple-element.24), channel_id=1, source_target_pairs={{0,8},{4,12},{8,0},{12,4},{1,9},{5,13},{9,1},{13,5},{2,10},{6,14},... | collective-permute-start | bytes 196616 | tf_op jit(solution)/shard_map/ppermute | solution.py:242
  7.7 6.8 %collective-permute-start.2 = (bf16[128,256]{1,0:T(8,128)(2,1)S(1)}, bf16[128,256]{1,0:T(8,128)(2,1)S(1)}, u32[]{:S(2)}, u32[]{:S(2)}) collective-permute-start(bf16[128,256]{1,0:T(8,128)(2,1)S(1)} %get-tuple-element.25), channel_id=1, source_target_pairs={{0,12},{4,8},{8,4},{12,0},{1,13},{5,9},{9,5},{13,1},{2,14},{6,10},... | collective-permute-start | bytes 196616 | tf_op jit(solution)/shard_map/ppermute | solution.py:242
  7.8 11.0 %collective-permute-start.7 = (bf16[1,2,128,640]{3,2,1,0:T(8,128)(2,1)S(1)}, bf16[1,2,128,640]{3,2,1,0:T(8,128)(2,1)S(1)}, u32[]{:S(2)}, u32[]{:S(2)}) collective-permute-start(bf16[1,2,128,640]{3,2,1,0:T(8,128)(2,1)S(1)} %get-tuple-element.26.before_ref), channel_id=1, source_target_pairs={{0,4},{4,0},{8,12},{12,8},{1,5},{5,1},{9,13},{13,9},{2,6},{6,2},{1... | collective-permute-start | bytes 983048 | tf_op jit(solution)/shard_map/ppermute | solution.py:282
  15.2 5.1 %collective-permute-start.5 = (bf16[2,64,256]{2,1,0:T(8,128)(2,1)S(1)}, bf16[2,64,256]{2,1,0:T(8,128)(2,1)S(1)}, u32[]{:S(2)}, u32[]{:S(2)}) collective-permute-start(bf16[2,64,256]{2,1,0:T(8,128)(2,1)S(1)} %codes.1.refs_0_.after_ref), channel_id=1, source_target_pairs={{0,3},{1,2},{2,1},{3,0},{4,7},{5,6},{6,5},{7,4},{8,11},{9,10},{10,... | collective-permute-start | bytes 196616 | tf_op jit(solution)/shard_map/ppermute | solution.py:259
  15.3 5.8 %collective-permute-start.4 = (bf16[2,64,256]{2,1,0:T(8,128)(2,1)S(1)}, bf16[2,64,256]{2,1,0:T(8,128)(2,1)S(1)}, u32[]{:S(2)}, u32[]{:S(2)}) collective-permute-start(bf16[2,64,256]{2,1,0:T(8,128)(2,1)S(1)} %codes.1.refs_0_.after_ref), channel_id=1, source_target_pairs={{0,2},{1,3},{2,0},{3,1},{4,6},{5,7},{6,4},{7,5},{8,10},{9,11},{10,... | collective-permute-start | bytes 196616 | tf_op jit(solution)/shard_map/ppermute | solution.py:259
  16.9 4.2 %collective-permute-start.3 = (bf16[2,64,256]{2,1,0:T(8,128)(2,1)S(1)}, bf16[2,64,256]{2,1,0:T(8,128)(2,1)S(1)}, u32[]{:S(2)}, u32[]{:S(2)}) collective-permute-start(bf16[2,64,256]{2,1,0:T(8,128)(2,1)S(1)} %codes.1.refs_0_.after_ref), channel_id=1, source_target_pairs={{0,1},{1,0},{2,3},{3,2},{4,5},{5,4},{6,7},{7,6},{8,9},{9,8},{10,11... | collective-permute-start | bytes 196616 | tf_op jit(solution)/shard_map/ppermute | solution.py:259
  18.2 2.9 %copy-start = (bf16[2,2,128,2048]{3,2,1,0:T(8,128)(2,1)S(1)}, bf16[2,2,128,2048]{3,2,1,0:T(8,128)(2,1)}, u32[]{:S(2)}) copy-start(bf16[2,2,128,2048]{3,2,1,0:T(8,128)(2,1)} %dec_ref.5) | copy-start | bytes 6291460
  18.2 14.9 %collective-permute-start.6 = (bf16[2,2,128,384]{3,2,1,0:T(8,128)(2,1)S(1)}, bf16[2,2,128,384]{3,2,1,0:T(8,128)(2,1)S(1)}, u32[]{:S(2)}, u32[]{:S(2)}) collective-permute-start(bf16[2,2,128,384]{3,2,1,0:T(8,128)(2,1)S(1)} %part.1), channel_id=1, source_target_pairs={{0,4},{4,0},{8,12},{12,8},{1,5},{5,1},{9,13},{13,9},{2,6},{6,2},{1... | collective-permute-start | bytes 1179656 | tf_op jit(solution)/shard_map/ppermute | solution.py:284
  18.8 9.5 %collective-permute-start.8 = (bf16[1,2,128,640]{3,2,1,0:T(8,128)(2,1)S(1)}, bf16[1,2,128,640]{3,2,1,0:T(8,128)(2,1)S(1)}, u32[]{:S(2)}, u32[]{:S(2)}) collective-permute-start(bf16[1,2,128,640]{3,2,1,0:T(8,128)(2,1)S(1)} %collective-permute-done.7.got_ref), channel_id=1, source_target_pairs={{0,16},{16,0},{1,17},{17,1},{2,18},{18,2},{3,19},{19,3},{4,20},{20... | collective-permute-start | bytes 983048 | tf_op jit(solution)/shard_map/ppermute | solution.py:283
  21.5 8.8 %collective-permute-start.12 = (bf16[1,64,640]{2,1,0:T(8,128)(2,1)S(1)}, bf16[1,64,640]{2,1,0:T(8,128)(2,1)S(1)}, u32[]{:S(2)}, u32[]{:S(2)}) collective-permute-start(bf16[1,64,640]{2,1,0:T(8,128)(2,1)S(1)} %get-tuple-element.33), channel_id=1, source_target_pairs={{0,8},{1,9},{4,12},{5,13},{8,0},{9,1},{12,4},{13,5},{2,10},{3,11},... | collective-permute-start | bytes 245768 | tf_op jit(solution)/shard_map/ppermute | solution.py:323
  22.5 11.1 %collective-permute-start.13 = (bf16[1,64,640]{2,1,0:T(8,128)(2,1)S(1)}, bf16[1,64,640]{2,1,0:T(8,128)(2,1)S(1)}, u32[]{:S(2)}, u32[]{:S(2)}) collective-permute-start(bf16[1,64,640]{2,1,0:T(8,128)(2,1)S(1)} %get-tuple-element.34), channel_id=1, source_target_pairs={{0,9},{1,8},{4,13},{5,12},{8,1},{9,0},{12,5},{13,4},{2,11},{3,10},... | collective-permute-start | bytes 245768 | tf_op jit(solution)/shard_map/ppermute | solution.py:323
  23.9 10.0 %collective-permute-start.14 = (bf16[1,64,640]{2,1,0:T(8,128)(2,1)S(1)}, bf16[1,64,640]{2,1,0:T(8,128)(2,1)S(1)}, u32[]{:S(2)}, u32[]{:S(2)}) collective-permute-start(bf16[1,64,640]{2,1,0:T(8,128)(2,1)S(1)} %get-tuple-element.35), channel_id=1, source_target_pairs={{0,1},{1,0},{4,5},{5,4},{8,9},{9,8},{12,13},{13,12},{2,3},{3,2},{6... | collective-permute-start | bytes 245768 | tf_op jit(solution)/shard_map/ppermute | solution.py:323
  28.6 15.8 %copy-start.1 = (bf16[2,64,2048]{2,1,0:T(8,128)(2,1)S(1)}, bf16[2,64,2048]{2,1,0:T(8,128)(2,1)}, u32[]{:S(2)}) copy-start(bf16[2,64,2048]{2,1,0:T(8,128)(2,1)} %target_ref.3) | copy-start | bytes 1572868
  28.6 15.8 %copy-start.2 = (f32[2,2048]{1,0:T(2,128)S(1)}, f32[2,2048]{1,0:T(2,128)}, u32[]{:S(2)}) copy-start(f32[2,2048]{1,0:T(2,128)} %bias_ref.3) | copy-start | bytes 49156
  28.6 14.3 %collective-permute-start.15 = (bf16[1,64,640]{2,1,0:T(8,128)(2,1)S(1)}, bf16[1,64,640]{2,1,0:T(8,128)(2,1)S(1)}, u32[]{:S(2)}, u32[]{:S(2)}) collective-permute-start(bf16[1,64,640]{2,1,0:T(8,128)(2,1)S(1)} %get-tuple-element.36), channel_id=1, source_target_pairs={{0,8},{1,9},{4,12},{5,13},{8,0},{9,1},{12,4},{13,5},{2,10},{3,11},... | collective-permute-start | bytes 245768 | tf_op jit(solution)/shard_map/ppermute | solution.py:323
  30.3 14.2 %collective-permute-start.16 = (bf16[1,64,640]{2,1,0:T(8,128)(2,1)S(1)}, bf16[1,64,640]{2,1,0:T(8,128)(2,1)S(1)}, u32[]{:S(2)}, u32[]{:S(2)}) collective-permute-start(bf16[1,64,640]{2,1,0:T(8,128)(2,1)S(1)} %get-tuple-element.37), channel_id=1, source_target_pairs={{0,9},{1,8},{4,13},{5,12},{8,1},{9,0},{12,5},{13,4},{2,11},{3,10},... | collective-permute-start | bytes 245768 | tf_op jit(solution)/shard_map/ppermute | solution.py:323
  33.2 11.3 %collective-permute-start.17 = (bf16[1,64,640]{2,1,0:T(8,128)(2,1)S(1)}, bf16[1,64,640]{2,1,0:T(8,128)(2,1)S(1)}, u32[]{:S(2)}, u32[]{:S(2)}) collective-permute-start(bf16[1,64,640]{2,1,0:T(8,128)(2,1)S(1)} %get-tuple-element.38), channel_id=1, source_target_pairs={{0,1},{1,0},{4,5},{5,4},{8,9},{9,8},{12,13},{13,12},{2,3},{3,2},{6... | collective-permute-start | bytes 245768 | tf_op jit(solution)/shard_map/ppermute | solution.py:323
  33.6 13.1 %collective-permute-start.9 = (bf16[2,64,384]{2,1,0:T(8,128)(2,1)S(1)}, bf16[2,64,384]{2,1,0:T(8,128)(2,1)S(1)}, u32[]{:S(2)}, u32[]{:S(2)}) collective-permute-start(bf16[2,64,384]{2,1,0:T(8,128)(2,1)S(1)} %get-tuple-element.29), channel_id=1, source_target_pairs={{0,8},{1,9},{4,12},{5,13},{8,0},{9,1},{12,4},{13,5},{2,10},{3,11},... | collective-permute-start | bytes 294920 | tf_op jit(solution)/shard_map/ppermute | solution.py:323
  33.9 14.7 %collective-permute-start.10 = (bf16[2,64,384]{2,1,0:T(8,128)(2,1)S(1)}, bf16[2,64,384]{2,1,0:T(8,128)(2,1)S(1)}, u32[]{:S(2)}, u32[]{:S(2)}) collective-permute-start(bf16[2,64,384]{2,1,0:T(8,128)(2,1)S(1)} %get-tuple-element.30), channel_id=1, source_target_pairs={{0,9},{1,8},{4,13},{5,12},{8,1},{9,0},{12,5},{13,4},{2,11},{3,10},... | collective-permute-start | bytes 294920 | tf_op jit(solution)/shard_map/ppermute | solution.py:323
  42.9 5.8 %collective-permute-start.11 = (bf16[2,64,384]{2,1,0:T(8,128)(2,1)S(1)}, bf16[2,64,384]{2,1,0:T(8,128)(2,1)S(1)}, u32[]{:S(2)}, u32[]{:S(2)}) collective-permute-start(bf16[2,64,384]{2,1,0:T(8,128)(2,1)S(1)} %get-tuple-element.31), channel_id=1, source_target_pairs={{0,1},{1,0},{4,5},{5,4},{8,9},{9,8},{12,13},{13,12},{2,3},{3,2},{6... | collective-permute-start | bytes 294920 | tf_op jit(solution)/shard_map/ppermute | solution.py:323

commit v26 on v22

--- a/solution.py
+++ b/solution.py
@@ -95,28 +95,18 @@
     pre = term_refs[0][...].astype(jnp.float32)
     for ref in term_refs[1:]:
         pre = pre + ref[...].astype(jnp.float32)
-    tiles, slots = active_ref.shape
+    tiles = active_ref.shape[0]
     for piece in range(2):
         columns = slice(piece * block, (piece + 1) * block)
         bias = bias_ref[pl.ds(half * 2 + piece, 1), :]
         wanted = tgt * n + half * 2 + piece
-        flags = []
-        for tile in range(tiles):
-            flags.append(
-                lax.fori_loop(
-                    0,
-                    slots,
-                    lambda i, total: total + (active_ref[tile, i] == wanted).astype(jnp.int32),
-                    jnp.int32(0),
-                    unroll=slots <= 16,
-                )
-            )
+        found = jnp.where(active_ref[...] == wanted, 1.0, 0.0).astype(jnp.float32)
+        flags = jnp.max(found, axis=1, keepdims=True)
         for group in range(n // 2):
             tile = ((group * 2 + parity) * share) // tile_rows
-            flag = flags[0]
+            live = flags[0:1]
             for i in range(1, tiles):
-                flag = jnp.where(tile == i, flags[i], flag)
-            live = jnp.where(flag > 0, 1.0, 0.0).astype(jnp.float32)
+                live = jnp.where(tile == i, flags[i : i + 1], live)
             rows = slice(group * share, (group + 1) * share)
             value = live * jnp.maximum(pre[rows, columns] + bias, 0.0)
             out_ref[group, :, columns] = value.astype(jnp.bfloat16)
@@ -202,7 +192,6 @@
     pair = [(i, i ^ 1) for i in range(n)]
     params = pltpu.CompilerParams(vmem_limit_bytes=VMEM_BYTES)
     vmem = pl.BlockSpec(memory_space=pltpu.VMEM)
-    smem = pl.BlockSpec(memory_space=pltpu.SMEM)
     anywhere = pl.BlockSpec(memory_space=pl.ANY)
     def weight(billions):
         return pl.CostEstimate(
@@ -244,7 +233,7 @@
     own = pl.pallas_call(
         functools.partial(codes_kernel, n, share, tile_rows),
         out_shape=shape(half, share, 2 * block),
-        in_specs=[smem] + [vmem] * (1 + n),
+        in_specs=[vmem] * (2 + n),
         out_specs=vmem,
         compiler_params=params,
         cost_estimate=weight(20),

time: 47.3 us -> 48.7 us (1.030)
  the two profiles are of different devices: /device:TPU:9 before, /device:TPU:0 now
where the time goes in v26:
time: 48.7 us; the launch traced here: 48.5 us
  waiting for transfers between devices  21.6 us (44%)
  starting transfers between devices  20.9 us (43%)
  Pallas kernels  5.87 us (12%)
    ppermute x9, starting transfers between devices, body(): sums[i].append(lax.ppermute(terms[2 * j + r], ('src', 'rep'), perm))  10.8 us
    ppermute x9, waiting for transfers between devices, body(): sums[i].append(lax.ppermute(terms[2 * j + r], ('src', 'rep'), perm))  8.48 us
    ppermute x3, waiting for transfers between devices, body(): lax.ppermute(terms[k], 'src', [(i, peer(i, k, n)) for i in range(n)])  5.92 us
    ppermute x3, starting transfers between devices, body(): lax.ppermute(terms[k], 'src', [(i, peer(i, k, n)) for i in range(n)])  5.66 us
    ppermute x1, waiting for transfers between devices, body(): got.append(lax.ppermute(got[0], 'parts', [(0, 1), (1, 0)]))  4.72 us
    ppermute x1, waiting for transfers between devices, body(): got = [lax.ppermute(parts[0], 'src', pair)]  2.42 us
    pallas_call x1, Pallas kernels, body(): pl.pallas_call(functools.partial(encode_kernel, n, fetched[:1]), out_shap...  2.08 us
    ppermute x3, starting transfers between devices, body(): codes.append(lax.ppermute(own, ('tgt', 'rep'), perm) if k + r else own)  1.92 us
  transfers between devices with their start and end apart: 18, of which 9 were waited for; matrix products, arithmetic and copies ran while one was open for 0% of the time, Pallas kernels for 6%

profile of v26, /device:TPU:0, one launch (start us, length us, event | category | flops | bytes accessed | tf_op | source)
XLA Modules:
  0.0 48.5 jit_solution(10071122581323411414)
XLA Ops:
  0.0 2.1 %encode.1 = (bf16[128,256]{1,0:T(8,128)(2,1)S(1)}, bf16[128,256]{1,0:T(8,128)(2,1)S(1)}, bf16[128,256]{1,0:T(8,128)(2,1)S(1)}, bf16[128,256]{1,0:T(8,128)(2,1)S(1)}, bf16[1,2,128,768]{3,2,1,0:T(8,128)(2,1)S(1)}) custom-call(bf16[2,2,64,1024]{3,2,1,0:T(8,128)(2,1)} %bitcast.3, bf16[1024,512]{1,0:T(8,128)(2,1)} %w_hbm.1, bf16[2,2,128,2048]{3,2,1,0:T(8,128)(2,1)} %dec_ref.5), custom_call_target="tpu_custom_call" | custom-call | tf_op jit(solution)/shard_map/encode/pallas_call | solution.py:212
  2.1 3.1 %collective-permute-start = (bf16[128,256]{1,0:T(8,128)(2,1)S(1)}, bf16[128,256]{1,0:T(8,128)(2,1)S(1)}, u32[]{:S(2)}, u32[]{:S(2)}) collective-permute-start(bf16[128,256]{1,0:T(8,128)(2,1)S(1)} %get-tuple-element.23), channel_id=1, source_target_pairs={{0,4},{4,0},{8,12},{12,8},{1,5},{5,1},{9,13},{13,9},{2,6},{6,2},{1... | collective-permute-start | bytes 196616 | tf_op jit(solution)/shard_map/ppermute | solution.py:231
  5.2 2.6 %collective-permute-start.1 = (bf16[128,256]{1,0:T(8,128)(2,1)S(1)}, bf16[128,256]{1,0:T(8,128)(2,1)S(1)}, u32[]{:S(2)}, u32[]{:S(2)}) collective-permute-start(bf16[128,256]{1,0:T(8,128)(2,1)S(1)} %get-tuple-element.24), channel_id=1, source_target_pairs={{0,8},{4,12},{8,0},{12,4},{1,9},{5,13},{9,1},{13,5},{2,10},{6,14},... | collective-permute-start | bytes 196616 | tf_op jit(solution)/shard_map/ppermute | solution.py:231
  7.7 0.0 collective-permute-start.2
  7.8 0.9 %collective-permute-start.7 = (bf16[1,2,128,768]{3,2,1,0:T(8,128)(2,1)S(1)}, bf16[1,2,128,768]{3,2,1,0:T(8,128)(2,1)S(1)}, u32[]{:S(2)}, u32[]{:S(2)}) collective-permute-start(bf16[1,2,128,768]{3,2,1,0:T(8,128)(2,1)S(1)} %get-tuple-element.26.before_ref), channel_id=1, source_target_pairs={{0,4},{4,0},{8,12},{12,8},{1,5},{5,1},{9,13},{13,9},{2,6},{6,2},{1... | collective-permute-start | bytes 1179656 | tf_op jit(solution)/shard_map/ppermute | solution.py:271
  8.7 0.0 collective-permute-done.refs_1_
  8.7 3.8 %collective-permute-done.1.refs_2_ = bf16[128,256]{1,0:T(8,128)(2,1)S(1)} collective-permute-done((bf16[128,256]{1,0:T(8,128)(2,1)S(1)}, bf16[128,256]{1,0:T(8,128)(2,1)S(1)}, u32[]{:S(2)}, u32[]{:S(2)}) %collective-permute-start.1) | collective-permute-done | bytes 65568 | tf_op jit(solution)/shard_map/ppermute | solution.py:231
  12.5 2.1 %collective-permute-done.2.refs_3_ = bf16[128,256]{1,0:T(8,128)(2,1)S(1)} collective-permute-done((bf16[128,256]{1,0:T(8,128)(2,1)S(1)}, bf16[128,256]{1,0:T(8,128)(2,1)S(1)}, u32[]{:S(2)}, u32[]{:S(2)}) %collective-permute-start.2) | collective-permute-done | bytes 65568 | tf_op jit(solution)/shard_map/ppermute | solution.py:231
  14.6 0.1 codes.1.refs_0_.after_ref
  14.7 0.1 collective-permute-start.5
  14.8 1.6 %collective-permute-start.4 = (bf16[2,64,256]{2,1,0:T(8,128)(2,1)S(1)}, bf16[2,64,256]{2,1,0:T(8,128)(2,1)S(1)}, u32[]{:S(2)}, u32[]{:S(2)}) collective-permute-start(bf16[2,64,256]{2,1,0:T(8,128)(2,1)S(1)} %codes.1.refs_0_.after_ref), channel_id=1, source_target_pairs={{0,2},{1,3},{2,0},{3,1},{4,6},{5,7},{6,4},{7,5},{8,10},{9,11},{10,... | collective-permute-start | bytes 196616 | tf_op jit(solution)/shard_map/ppermute | solution.py:248
  16.4 0.3 collective-permute-start.3
  16.7 1.0 %part.1 = bf16[2,2,128,256]{3,2,1,0:T(8,128)(2,1)S(1)} custom-call(bf16[1,2,128,768]{3,2,1,0:T(8,128)(2,1)S(1)} %get-tuple-element.26.before_ref, bf16[2,2,128,2048]{3,2,1,0:T(8,128)(2,1)} %dec_ref.5, bf16[2,64,256]{2,1,0:T(8,128)(2,1)S(1)} %codes.1.refs_0_.after_ref), custom_call_target="tpu_custom_call" | custom-call | tf_op jit(solution)/shard_map/part/pallas_call | solution.py:260
  17.6 0.0 copy-start
  17.7 0.1 collective-permute-start.6
  17.7 2.4 %collective-permute-done.7.got_ref = bf16[1,2,128,768]{3,2,1,0:T(8,128)(2,1)S(1)} collective-permute-done((bf16[1,2,128,768]{3,2,1,0:T(8,128)(2,1)S(1)}, bf16[1,2,128,768]{3,2,1,0:T(8,128)(2,1)S(1)}, u32[]{:S(2)}, u32[]{:S(2)}) %collective-permute-start.7) | collective-permute-done | bytes 393248 | tf_op jit(solution)/shard_map/ppermute | solution.py:271
  20.2 1.5 %collective-permute-start.8 = (bf16[1,2,128,768]{3,2,1,0:T(8,128)(2,1)S(1)}, bf16[1,2,128,768]{3,2,1,0:T(8,128)(2,1)S(1)}, u32[]{:S(2)}, u32[]{:S(2)}) collective-permute-start(bf16[1,2,128,768]{3,2,1,0:T(8,128)(2,1)S(1)} %collective-permute-done.7.got_ref), channel_id=1, source_target_pairs={{0,16},{16,0},{1,17},{17,1},{2,18},{18,2},{3,19},{19,3},{4,20},{20... | collective-permute-start | bytes 1179656 | tf_op jit(solution)/shard_map/ppermute | solution.py:272
  21.7 0.0 collective-permute-done.5.refs_3_
  21.7 0.0 collective-permute-done.4.refs_2_
  21.7 0.0 collective-permute-done.3.refs_1_
  21.7 0.1 gather.1.lhs_ref
  21.8 0.4 decode.3
  22.2 2.1 %collective-permute-start.12 = (bf16[1,64,768]{2,1,0:T(8,128)(2,1)S(1)}, bf16[1,64,768]{2,1,0:T(8,128)(2,1)S(1)}, u32[]{:S(2)}, u32[]{:S(2)}) collective-permute-start(bf16[1,64,768]{2,1,0:T(8,128)(2,1)S(1)} %get-tuple-element.33), channel_id=1, source_target_pairs={{0,8},{1,9},{4,12},{5,13},{8,0},{9,1},{12,4},{13,5},{2,10},{3,11},... | collective-permute-start | bytes 294920 | tf_op jit(solution)/shard_map/ppermute | solution.py:312
  24.3 0.0 collective-permute-start.13
  24.3 1.0 %collective-permute-start.14 = (bf16[1,64,768]{2,1,0:T(8,128)(2,1)S(1)}, bf16[1,64,768]{2,1,0:T(8,128)(2,1)S(1)}, u32[]{:S(2)}, u32[]{:S(2)}) collective-permute-start(bf16[1,64,768]{2,1,0:T(8,128)(2,1)S(1)} %get-tuple-element.35), channel_id=1, source_target_pairs={{0,1},{1,0},{4,5},{5,4},{8,9},{9,8},{12,13},{13,12},{2,3},{3,2},{6... | collective-permute-start | bytes 294920 | tf_op jit(solution)/shard_map/ppermute | solution.py:312
  25.3 4.7 %collective-permute-done.8.got_ref = bf16[1,2,128,768]{3,2,1,0:T(8,128)(2,1)S(1)} collective-permute-done((bf16[1,2,128,768]{3,2,1,0:T(8,128)(2,1)S(1)}, bf16[1,2,128,768]{3,2,1,0:T(8,128)(2,1)S(1)}, u32[]{:S(2)}, u32[]{:S(2)}) %collective-permute-start.8) | collective-permute-done | bytes 393248 | tf_op jit(solution)/shard_map/ppermute | solution.py:272
  30.0 0.4 decode.4
  30.4 0.0 copy-start.1
  30.4 0.0 copy-start.2
  30.4 1.3 %collective-permute-start.15 = (bf16[1,64,768]{2,1,0:T(8,128)(2,1)S(1)}, bf16[1,64,768]{2,1,0:T(8,128)(2,1)S(1)}, u32[]{:S(2)}, u32[]{:S(2)}) collective-permute-start(bf16[1,64,768]{2,1,0:T(8,128)(2,1)S(1)} %get-tuple-element.36), channel_id=1, source_target_pairs={{0,8},{1,9},{4,12},{5,13},{8,0},{9,1},{12,4},{13,5},{2,10},{3,11},... | collective-permute-start | bytes 294920 | tf_op jit(solution)/shard_map/ppermute | solution.py:312
  31.7 0.0 collective-permute-done.6.got_ref
  31.7 0.0 collective-permute-start.16
  31.7 1.8 %collective-permute-done.12.refs_0_ = bf16[1,64,768]{2,1,0:T(8,128)(2,1)S(1)} collective-permute-done((bf16[1,64,768]{2,1,0:T(8,128)(2,1)S(1)}, bf16[1,64,768]{2,1,0:T(8,128)(2,1)S(1)}, u32[]{:S(2)}, u32[]{:S(2)}) %collective-permute-start.12) | collective-permute-done | bytes 98336 | tf_op jit(solution)/shard_map/ppermute | solution.py:312
  33.5 0.0 collective-permute-start.17
  33.5 0.3 decode.5
  33.8 0.6 %collective-permute-done.13.refs_1_ = bf16[1,64,768]{2,1,0:T(8,128)(2,1)S(1)} collective-permute-done((bf16[1,64,768]{2,1,0:T(8,128)(2,1)S(1)}, bf16[1,64,768]{2,1,0:T(8,128)(2,1)S(1)}, u32[]{:S(2)}, u32[]{:S(2)}) %collective-permute-start.13) | collective-permute-done | bytes 98336 | tf_op jit(solution)/shard_map/ppermute | solution.py:312
  34.4 0.7 %collective-permute-start.9 = (bf16[2,64,256]{2,1,0:T(8,128)(2,1)S(1)}, bf16[2,64,256]{2,1,0:T(8,128)(2,1)S(1)}, u32[]{:S(2)}, u32[]{:S(2)}) collective-permute-start(bf16[2,64,256]{2,1,0:T(8,128)(2,1)S(1)} %get-tuple-element.29), channel_id=1, source_target_pairs={{0,8},{1,9},{4,12},{5,13},{8,0},{9,1},{12,4},{13,5},{2,10},{3,11},... | collective-permute-start | bytes 196616 | tf_op jit(solution)/shard_map/ppermute | solution.py:312
  35.1 0.0 collective-permute-done.14.refs_2_
  35.1 5.7 %collective-permute-start.10 = (bf16[2,64,256]{2,1,0:T(8,128)(2,1)S(1)}, bf16[2,64,256]{2,1,0:T(8,128)(2,1)S(1)}, u32[]{:S(2)}, u32[]{:S(2)}) collective-permute-start(bf16[2,64,256]{2,1,0:T(8,128)(2,1)S(1)} %get-tuple-element.30), channel_id=1, source_target_pairs={{0,9},{1,8},{4,13},{5,12},{8,1},{9,0},{12,5},{13,4},{2,11},{3,10},... | collective-permute-start | bytes 196616 | tf_op jit(solution)/shard_map/ppermute | solution.py:312
  40.8 0.0 collective-permute-done.15.refs_4_
  40.9 0.0 collective-permute-start.11
  40.9 0.9 %collective-permute-done.16.refs_5_ = bf16[1,64,768]{2,1,0:T(8,128)(2,1)S(1)} collective-permute-done((bf16[1,64,768]{2,1,0:T(8,128)(2,1)S(1)}, bf16[1,64,768]{2,1,0:T(8,128)(2,1)S(1)}, u32[]{:S(2)}, u32[]{:S(2)}) %collective-permute-start.16) | collective-permute-done | bytes 98336 | tf_op jit(solution)/shard_map/ppermute | solution.py:312
  41.8 0.0 collective-permute-done.17.refs_6_
  41.8 0.9 %add.2.refs_4_ = bf16[2,64,2048]{2,1,0:T(8,128)(2,1)} custom-call(f32[2,2048]{1,0:T(2,128)S(1)} %copy-done.2, bf16[2,64,2048]{2,1,0:T(8,128)(2,1)S(1)} %copy-done.1, bf16[1,64,768]{2,1,0:T(8,128)(2,1)S(1)} %collective-permute-done.12.refs_0_, bf16[1,64,768]{2,1,0:T(8,128)(2,1)S(1)} %collective-permute-done.13.refs_1_, ...), custom_call_target="tpu_custom_call" | custom-call | flops 20000000000 | tf_op jit(solution)/shard_map/add/pallas_call | solution.py:279
  42.6 4.2 %collective-permute-done.9.refs_0_ = bf16[2,64,256]{2,1,0:T(8,128)(2,1)S(1)} collective-permute-done((bf16[2,64,256]{2,1,0:T(8,128)(2,1)S(1)}, bf16[2,64,256]{2,1,0:T(8,128)(2,1)S(1)}, u32[]{:S(2)}, u32[]{:S(2)}) %collective-permute-start.9) | collective-permute-done | bytes 65568 | tf_op jit(solution)/shard_map/ppermute | solution.py:312
  46.8 0.9 %collective-permute-done.10.refs_1_ = bf16[2,64,256]{2,1,0:T(8,128)(2,1)S(1)} collective-permute-done((bf16[2,64,256]{2,1,0:T(8,128)(2,1)S(1)}, bf16[2,64,256]{2,1,0:T(8,128)(2,1)S(1)}, u32[]{:S(2)}, u32[]{:S(2)}) %collective-permute-start.10) | collective-permute-done | bytes 65568 | tf_op jit(solution)/shard_map/ppermute | solution.py:312
  47.8 0.0 collective-permute-done.11.refs_2_
  47.8 0.7 %add.3 = bf16[2,64,2048]{2,1,0:T(8,128)(2,1)} custom-call(f32[2,2048]{1,0:T(2,128)S(1)} %copy-done.2, bf16[2,64,2048]{2,1,0:T(8,128)(2,1)S(1)} %copy-done.1, bf16[2,64,256]{2,1,0:T(8,128)(2,1)S(1)} %collective-permute-done.9.refs_0_, bf16[2,64,256]{2,1,0:T(8,128)(2,1)S(1)} %collective-permute-done.10.refs_1_, ...), custom_call_target="tpu_custom_call", output_to_operand_aliasing={{}: (6, {})} | custom-call | tf_op jit(solution)/shard_map/add/pallas_call | solution.py:279
  (7 shorter events, 0.0 us)
Async XLA Ops:
  0.0 14.6 %copy-start.4 = (s32[2,8]{1,0:T(2,128)S(1)}, s32[2,8]{1,0:T(2,128)}, u32[]{:S(2)}) copy-start(s32[2,8]{1,0:T(2,128)} %active_ref.1) | copy-start | bytes 196
  0.0 14.6 %copy-start.3 = (f32[512]{0:T(512)S(1)}, f32[512]{0:T(512)}, u32[]{:S(2)}) copy-start(f32[512]{0:T(512)} %param.9) | copy-start | bytes 6148
  2.1 6.6 %collective-permute-start = (bf16[128,256]{1,0:T(8,128)(2,1)S(1)}, bf16[128,256]{1,0:T(8,128)(2,1)S(1)}, u32[]{:S(2)}, u32[]{:S(2)}) collective-permute-start(bf16[128,256]{1,0:T(8,128)(2,1)S(1)} %get-tuple-element.23), channel_id=1, source_target_pairs={{0,4},{4,0},{8,12},{12,8},{1,5},{5,1},{9,13},{13,9},{2,6},{6,2},{1... | collective-permute-start | bytes 196616 | tf_op jit(solution)/shard_map/ppermute | solution.py:231
  5.2 7.3 %collective-permute-start.1 = (bf16[128,256]{1,0:T(8,128)(2,1)S(1)}, bf16[128,256]{1,0:T(8,128)(2,1)S(1)}, u32[]{:S(2)}, u32[]{:S(2)}) collective-permute-start(bf16[128,256]{1,0:T(8,128)(2,1)S(1)} %get-tuple-element.24), channel_id=1, source_target_pairs={{0,8},{4,12},{8,0},{12,4},{1,9},{5,13},{9,1},{13,5},{2,10},{6,14},... | collective-permute-start | bytes 196616 | tf_op jit(solution)/shard_map/ppermute | solution.py:231
  7.7 6.8 %collective-permute-start.2 = (bf16[128,256]{1,0:T(8,128)(2,1)S(1)}, bf16[128,256]{1,0:T(8,128)(2,1)S(1)}, u32[]{:S(2)}, u32[]{:S(2)}) collective-permute-start(bf16[128,256]{1,0:T(8,128)(2,1)S(1)} %get-tuple-element.25), channel_id=1, source_target_pairs={{0,12},{4,8},{8,4},{12,0},{1,13},{5,9},{9,5},{13,1},{2,14},{6,10},... | collective-permute-start | bytes 196616 | tf_op jit(solution)/shard_map/ppermute | solution.py:231
  7.8 12.4 %collective-permute-start.7 = (bf16[1,2,128,768]{3,2,1,0:T(8,128)(2,1)S(1)}, bf16[1,2,128,768]{3,2,1,0:T(8,128)(2,1)S(1)}, u32[]{:S(2)}, u32[]{:S(2)}) collective-permute-start(bf16[1,2,128,768]{3,2,1,0:T(8,128)(2,1)S(1)} %get-tuple-element.26.before_ref), channel_id=1, source_target_pairs={{0,4},{4,0},{8,12},{12,8},{1,5},{5,1},{9,13},{13,9},{2,6},{6,2},{1... | collective-permute-start | bytes 1179656 | tf_op jit(solution)/shard_map/ppermute | solution.py:271
  14.7 6.9 %collective-permute-start.5 = (bf16[2,64,256]{2,1,0:T(8,128)(2,1)S(1)}, bf16[2,64,256]{2,1,0:T(8,128)(2,1)S(1)}, u32[]{:S(2)}, u32[]{:S(2)}) collective-permute-start(bf16[2,64,256]{2,1,0:T(8,128)(2,1)S(1)} %codes.1.refs_0_.after_ref), channel_id=1, source_target_pairs={{0,3},{1,2},{2,1},{3,0},{4,7},{5,6},{6,5},{7,4},{8,11},{9,10},{10,... | collective-permute-start | bytes 196616 | tf_op jit(solution)/shard_map/ppermute | solution.py:248
  14.8 6.9 %collective-permute-start.4 = (bf16[2,64,256]{2,1,0:T(8,128)(2,1)S(1)}, bf16[2,64,256]{2,1,0:T(8,128)(2,1)S(1)}, u32[]{:S(2)}, u32[]{:S(2)}) collective-permute-start(bf16[2,64,256]{2,1,0:T(8,128)(2,1)S(1)} %codes.1.refs_0_.after_ref), channel_id=1, source_target_pairs={{0,2},{1,3},{2,0},{3,1},{4,6},{5,7},{6,4},{7,5},{8,10},{9,11},{10,... | collective-permute-start | bytes 196616 | tf_op jit(solution)/shard_map/ppermute | solution.py:248
  16.4 5.3 %collective-permute-start.3 = (bf16[2,64,256]{2,1,0:T(8,128)(2,1)S(1)}, bf16[2,64,256]{2,1,0:T(8,128)(2,1)S(1)}, u32[]{:S(2)}, u32[]{:S(2)}) collective-permute-start(bf16[2,64,256]{2,1,0:T(8,128)(2,1)S(1)} %codes.1.refs_0_.after_ref), channel_id=1, source_target_pairs={{0,1},{1,0},{2,3},{3,2},{4,5},{5,4},{6,7},{7,6},{8,9},{9,8},{10,11... | collective-permute-start | bytes 196616 | tf_op jit(solution)/shard_map/ppermute | solution.py:248
  17.6 4.1 %copy-start = (bf16[2,2,128,2048]{3,2,1,0:T(8,128)(2,1)S(1)}, bf16[2,2,128,2048]{3,2,1,0:T(8,128)(2,1)}, u32[]{:S(2)}) copy-start(bf16[2,2,128,2048]{3,2,1,0:T(8,128)(2,1)} %dec_ref.5) | copy-start | bytes 6291460
  17.7 14.0 %collective-permute-start.6 = (bf16[2,2,128,256]{3,2,1,0:T(8,128)(2,1)S(1)}, bf16[2,2,128,256]{3,2,1,0:T(8,128)(2,1)S(1)}, u32[]{:S(2)}, u32[]{:S(2)}) collective-permute-start(bf16[2,2,128,256]{3,2,1,0:T(8,128)(2,1)S(1)} %part.1), channel_id=1, source_target_pairs={{0,4},{4,0},{8,12},{12,8},{1,5},{5,1},{9,13},{13,9},{2,6},{6,2},{1... | collective-permute-start | bytes 786440 | tf_op jit(solution)/shard_map/ppermute | solution.py:273
  20.2 9.8 %collective-permute-start.8 = (bf16[1,2,128,768]{3,2,1,0:T(8,128)(2,1)S(1)}, bf16[1,2,128,768]{3,2,1,0:T(8,128)(2,1)S(1)}, u32[]{:S(2)}, u32[]{:S(2)}) collective-permute-start(bf16[1,2,128,768]{3,2,1,0:T(8,128)(2,1)S(1)} %collective-permute-done.7.got_ref), channel_id=1, source_target_pairs={{0,16},{16,0},{1,17},{17,1},{2,18},{18,2},{3,19},{19,3},{4,20},{20... | collective-permute-start | bytes 1179656 | tf_op jit(solution)/shard_map/ppermute | solution.py:272
  22.2 11.3 %collective-permute-start.12 = (bf16[1,64,768]{2,1,0:T(8,128)(2,1)S(1)}, bf16[1,64,768]{2,1,0:T(8,128)(2,1)S(1)}, u32[]{:S(2)}, u32[]{:S(2)}) collective-permute-start(bf16[1,64,768]{2,1,0:T(8,128)(2,1)S(1)} %get-tuple-element.33), channel_id=1, source_target_pairs={{0,8},{1,9},{4,12},{5,13},{8,0},{9,1},{12,4},{13,5},{2,10},{3,11},... | collective-permute-start | bytes 294920 | tf_op jit(solution)/shard_map/ppermute | solution.py:312
  24.3 10.1 %collective-permute-start.13 = (bf16[1,64,768]{2,1,0:T(8,128)(2,1)S(1)}, bf16[1,64,768]{2,1,0:T(8,128)(2,1)S(1)}, u32[]{:S(2)}, u32[]{:S(2)}) collective-permute-start(bf16[1,64,768]{2,1,0:T(8,128)(2,1)S(1)} %get-tuple-element.34), channel_id=1, source_target_pairs={{0,9},{1,8},{4,13},{5,12},{8,1},{9,0},{12,5},{13,4},{2,11},{3,10},... | collective-permute-start | bytes 294920 | tf_op jit(solution)/shard_map/ppermute | solution.py:312
  24.3 10.8 %collective-permute-start.14 = (bf16[1,64,768]{2,1,0:T(8,128)(2,1)S(1)}, bf16[1,64,768]{2,1,0:T(8,128)(2,1)S(1)}, u32[]{:S(2)}, u32[]{:S(2)}) collective-permute-start(bf16[1,64,768]{2,1,0:T(8,128)(2,1)S(1)} %get-tuple-element.35), channel_id=1, source_target_pairs={{0,1},{1,0},{4,5},{5,4},{8,9},{9,8},{12,13},{13,12},{2,3},{3,2},{6... | collective-permute-start | bytes 294920 | tf_op jit(solution)/shard_map/ppermute | solution.py:312
  30.4 11.4 %copy-start.1 = (bf16[2,64,2048]{2,1,0:T(8,128)(2,1)S(1)}, bf16[2,64,2048]{2,1,0:T(8,128)(2,1)}, u32[]{:S(2)}) copy-start(bf16[2,64,2048]{2,1,0:T(8,128)(2,1)} %target_ref.3) | copy-start | bytes 1572868
  30.4 11.4 %copy-start.2 = (f32[2,2048]{1,0:T(2,128)S(1)}, f32[2,2048]{1,0:T(2,128)}, u32[]{:S(2)}) copy-start(f32[2,2048]{1,0:T(2,128)} %bias_ref.3) | copy-start | bytes 49156
  30.4 10.5 %collective-permute-start.15 = (bf16[1,64,768]{2,1,0:T(8,128)(2,1)S(1)}, bf16[1,64,768]{2,1,0:T(8,128)(2,1)S(1)}, u32[]{:S(2)}, u32[]{:S(2)}) collective-permute-start(bf16[1,64,768]{2,1,0:T(8,128)(2,1)S(1)} %get-tuple-element.36), channel_id=1, source_target_pairs={{0,8},{1,9},{4,12},{5,13},{8,0},{9,1},{12,4},{13,5},{2,10},{3,11},... | collective-permute-start | bytes 294920 | tf_op jit(solution)/shard_map/ppermute | solution.py:312
  31.7 10.1 %collective-permute-start.16 = (bf16[1,64,768]{2,1,0:T(8,128)(2,1)S(1)}, bf16[1,64,768]{2,1,0:T(8,128)(2,1)S(1)}, u32[]{:S(2)}, u32[]{:S(2)}) collective-permute-start(bf16[1,64,768]{2,1,0:T(8,128)(2,1)S(1)} %get-tuple-element.37), channel_id=1, source_target_pairs={{0,9},{1,8},{4,13},{5,12},{8,1},{9,0},{12,5},{13,4},{2,11},{3,10},... | collective-permute-start | bytes 294920 | tf_op jit(solution)/shard_map/ppermute | solution.py:312
  33.5 8.3 %collective-permute-start.17 = (bf16[1,64,768]{2,1,0:T(8,128)(2,1)S(1)}, bf16[1,64,768]{2,1,0:T(8,128)(2,1)S(1)}, u32[]{:S(2)}, u32[]{:S(2)}) collective-permute-start(bf16[1,64,768]{2,1,0:T(8,128)(2,1)S(1)} %get-tuple-element.38), channel_id=1, source_target_pairs={{0,1},{1,0},{4,5},{5,4},{8,9},{9,8},{12,13},{13,12},{2,3},{3,2},{6... | collective-permute-start | bytes 294920 | tf_op jit(solution)/shard_map/ppermute | solution.py:312
  34.4 12.4 %collective-permute-start.9 = (bf16[2,64,256]{2,1,0:T(8,128)(2,1)S(1)}, bf16[2,64,256]{2,1,0:T(8,128)(2,1)S(1)}, u32[]{:S(2)}, u32[]{:S(2)}) collective-permute-start(bf16[2,64,256]{2,1,0:T(8,128)(2,1)S(1)} %get-tuple-element.29), channel_id=1, source_target_pairs={{0,8},{1,9},{4,12},{5,13},{8,0},{9,1},{12,4},{13,5},{2,10},{3,11},... | collective-permute-start | bytes 196616 | tf_op jit(solution)/shard_map/ppermute | solution.py:312
  35.1 12.7 %collective-permute-start.10 = (bf16[2,64,256]{2,1,0:T(8,128)(2,1)S(1)}, bf16[2,64,256]{2,1,0:T(8,128)(2,1)S(1)}, u32[]{:S(2)}, u32[]{:S(2)}) collective-permute-start(bf16[2,64,256]{2,1,0:T(8,128)(2,1)S(1)} %get-tuple-element.30), channel_id=1, source_target_pairs={{0,9},{1,8},{4,13},{5,12},{8,1},{9,0},{12,5},{13,4},{2,11},{3,10},... | collective-permute-start | bytes 196616 | tf_op jit(solution)/shard_map/ppermute | solution.py:312
  40.9 6.9 %collective-permute-start.11 = (bf16[2,64,256]{2,1,0:T(8,128)(2,1)S(1)}, bf16[2,64,256]{2,1,0:T(8,128)(2,1)S(1)}, u32[]{:S(2)}, u32[]{:S(2)}) collective-permute-start(bf16[2,64,256]{2,1,0:T(8,128)(2,1)S(1)} %get-tuple-element.31), channel_id=1, source_target_pairs={{0,1},{1,0},{4,5},{5,4},{8,9},{9,8},{12,13},{13,12},{2,3},{3,2},{6... | collective-permute-start | bytes 196616 | tf_op jit(solution)/shard_map/ppermute | solution.py:312
